TPU v7x, 32 devices: a whole 2x2x4 slice. The times are simulated.
32 devices in a mesh: frames: 8 (over z, y), heads: 4 (over x, core).
Axes of the slice: x: 2, y: 2, z: 4, core: 2. Of those that a mesh axis runs over, the one named last changes fastest.
Arguments:
- queries: bfloat16 [768, 2560], P('frames', 'heads'), may hold values from -40 to 40
- keys_values: bfloat16 [2, 768, 2560], P(None, 'frames', 'heads'), may hold values from -40 to 40
- out_weight: bfloat16 [2560, 5120], P('heads', 'frames'), may hold values from -0.5 to 0.5
Outputs:
- projected: bfloat16 [768, 5120], P('frames', 'heads')
All inputs are finite; a program needn't handle non-finite values.
Results may differ from a plain program's by a relative error of at most 0.015.
Values may be sent and summed in bfloat16 or wider, within the bound.
No kernel may reach another device: no remote copies, remote signals or barrier semaphores. Data moves between devices by JAX's collectives and lax.ppermute only.
A program may use at most 64 MiB of HBM per device.

v0:
```python
import jax
import jax.numpy as jnp
from jax import lax
from jax.sharding import PartitionSpec as P

HD = 128
TPF = 32
FR_DEV = 3


reach_cap = 32


def from_behind(x, axis, by):
    devices = lax.axis_size(axis)
    return lax.ppermute(x, axis, [(i, (i + by) % devices) for i in range(devices)])


def on_device(queries, keys_values, out_weight):
    total_frames = lax.axis_size("frames") * FR_DEV
    reach = min(reach_cap, (total_frames - 1) // 2)
    steps = (reach + FR_DEV - 1) // FR_DEV
    width = keys_values.shape[2]
    span = FR_DEV + 2 * reach
    stacked = keys_values.reshape(2, FR_DEV, TPF, width)
    pieces = []
    for offset in range(-steps, steps + 1):
        if offset == 0:
            pieces.append(stacked)
        else:
            pieces.append(from_behind(stacked, "frames", -offset))
    window = jnp.concatenate(pieces, axis=1)
    lower_frame = steps * FR_DEV - reach
    extended = window[:, lower_frame : lower_frame + span]
    keys_ext = extended[0].reshape(span * TPF, width)
    values_ext = extended[1].reshape(span * TPF, width)
    row_frame = jnp.arange(FR_DEV * TPF, dtype=jnp.int32) // TPF
    col_frame = jnp.arange(span * TPF, dtype=jnp.int32) // TPF
    allowed = (col_frame[None, :] >= row_frame[:, None]) & (
        col_frame[None, :] <= row_frame[:, None] + 2 * reach
    )
    results = []
    for head in range(width // HD):
        lower = head * HD
        query_cols = queries[:, lower : lower + HD]
        key_cols = keys_ext[:, lower : lower + HD]
        scores = lax.dot_general(
            query_cols, key_cols, (((1,), (1,)), ((), ())), preferred_element_type=jnp.float32
        )
        scores = scores * HD ** (-0.5)
        top = jnp.max(jnp.where(allowed, scores, -1e30), axis=1, keepdims=True)
        weights = jnp.where(allowed, jnp.exp(scores - top), 0.0)
        probs = (weights / jnp.sum(weights, axis=1, keepdims=True)).astype(jnp.bfloat16)
        results.append(
            jnp.dot(
                probs, values_ext[:, lower : lower + HD], preferred_element_type=jnp.float32
            ).astype(jnp.bfloat16)
        )
    attended = jnp.concatenate(results, axis=1)
    partial_rows = jnp.dot(
        attended,
        lax.all_gather(out_weight, "frames", axis=1, tiled=True),
        preferred_element_type=jnp.float32,
    )
    return lax.psum_scatter(
        partial_rows.astype(jnp.bfloat16), "heads", scatter_dimension=1, tiled=True
    )


def solution(mesh):
    in_specs = (P("frames", "heads"), P(None, "frames", "heads"), P("heads", "frames"))
    out_specs = P("frames", "heads")
    return jax.shard_map(
        on_device, mesh=mesh, in_specs=in_specs, out_specs=out_specs, check_vma=False
    )
```

profile of v0, /device:TPU:3, one launch (start us, length us, event | category | flops | bytes accessed | tf_op | source)
XLA Modules:
  0.0 175.3 jit_solution(12018315020478273384)
XLA Ops:
  6.5 0.7 all-gather.2.cloned.1.call-update
  7.3 2.4 %collective-permute-start = (bf16[2,3,32,640]{3,2,1,0:T(8,128)(2,1)}, bf16[2,3,32,640]{3,2,1,0:T(8,128)(2,1)S(1)}, u32[]{:S(2)}, u32[]{:S(2)}) collective-permute-start(bf16[2,3,32,640]{3,2,1,0:T(8,128)(2,1)} %bitcast.25), channel_id=1, source_target_pairs={{0,16},{4,20},{8,24},{12,28},{16,0},{20,4},{24,8},{28,12},{1,17},{... | collective-permute-start | bytes 737288 | tf_op jit(solution)/shard_map/ppermute | solution.py:16
  9.7 2.3 %collective-permute-start.1 = (bf16[2,3,32,640]{3,2,1,0:T(8,128)(2,1)}, bf16[2,3,32,640]{3,2,1,0:T(8,128)(2,1)S(1)}, u32[]{:S(2)}, u32[]{:S(2)}) collective-permute-start(bf16[2,3,32,640]{3,2,1,0:T(8,128)(2,1)} %bitcast.26), channel_id=1, source_target_pairs={{0,12},{4,16},{8,20},{12,24},{16,28},{20,0},{24,4},{28,8},{1,13},{... | collective-permute-start | bytes 737288 | tf_op jit(solution)/shard_map/ppermute | solution.py:16
  11.9 0.3 collective-permute-start.3
  12.2 3.9 %collective-permute-start.4 = (bf16[2,3,32,640]{3,2,1,0:T(8,128)(2,1)}, bf16[2,3,32,640]{3,2,1,0:T(8,128)(2,1)S(1)}, u32[]{:S(2)}, u32[]{:S(2)}) collective-permute-start(bf16[2,3,32,640]{3,2,1,0:T(8,128)(2,1)} %bitcast.29), channel_id=1, source_target_pairs={{0,28},{4,0},{8,4},{12,8},{16,12},{20,16},{24,20},{28,24},{1,29},{... | collective-permute-start | bytes 737288 | tf_op jit(solution)/shard_map/ppermute | solution.py:16
  16.1 21.6 %collective-permute-done = bf16[2,3,32,640]{3,2,1,0:T(8,128)(2,1)S(1)} collective-permute-done((bf16[2,3,32,640]{3,2,1,0:T(8,128)(2,1)}, bf16[2,3,32,640]{3,2,1,0:T(8,128)(2,1)S(1)}, u32[]{:S(2)}, u32[]{:S(2)}) %collective-permute-start) | collective-permute-done | bytes 245792 | tf_op jit(solution)/shard_map/ppermute | solution.py:16
  37.8 24.5 %collective-permute-done.1 = bf16[2,3,32,640]{3,2,1,0:T(8,128)(2,1)S(1)} collective-permute-done((bf16[2,3,32,640]{3,2,1,0:T(8,128)(2,1)}, bf16[2,3,32,640]{3,2,1,0:T(8,128)(2,1)S(1)}, u32[]{:S(2)}, u32[]{:S(2)}) %collective-permute-start.1) | collective-permute-done | bytes 245792 | tf_op jit(solution)/shard_map/ppermute | solution.py:16
  62.5 16.4 %collective-permute-done.6 = bf16[2,3,32,640]{3,2,1,0:T(8,128)(2,1)S(1)} collective-permute-done((bf16[2,3,32,640]{3,2,1,0:T(8,128)(2,1)}, bf16[2,3,32,640]{3,2,1,0:T(8,128)(2,1)S(1)}, u32[]{:S(2)}, u32[]{:S(2)}) %collective-permute-start.6) | collective-permute-done | bytes 245792 | tf_op jit(solution)/shard_map/ppermute | solution.py:16
  79.0 0.2 fusion.38
  79.2 0.7 copy-done.1
  79.9 0.2 fusion.4
  80.1 0.2 fusion.1
  80.3 0.2 fusion.2
  80.5 0.3 select_reduce_fusion
  80.8 0.5 fusion.14
  81.3 0.4 fusion.13
  81.7 0.3 fusion.9
  82.1 0.3 fusion.8
  82.4 0.3 fusion.7
  82.7 0.3 fusion.6
  83.0 0.3 fusion.5
  83.3 57.4 %all-gather.2.cloned.1.call-done = bf16[640,5120]{1,0:T(8,128)(2,1)} async-done(((bf16[640,640]{1,0:T(8,128)(2,1)}), bf16[640,5120]{1,0:T(8,128)(2,1)}) %all-gather.2.cloned.1.call-update) | async-done | bytes 6553616 | tf_op jit(solution)/shard_map/all_gather | solution.py:62
  140.7 5.1 %convolution_convert_fusion = bf16[96,5120]{1,0:T(8,128)(2,1)} fusion(bf16[96,640]{1,0:T(8,128)(2,1)S(1)} %fusion.5, bf16[640,5120]{1,0:T(8,128)(2,1)} %all-gather.2.cloned.1.call-done), kind=kOutput, calls=%fused_computation | convolution fusion | flops 629637120 | bytes 7659520 | tf_op jit(solution)/shard_map/dot_general | solution.py:60
  145.8 22.6 %reduce-scatter.2.cloned.1.call-done = bf16[96,1280]{1,0:T(8,128)(2,1)} async-done(((bf16[96,5120]{1,0:T(8,128)(2,1)}), bf16[96,1280]{1,0:T(8,128)(2,1)}) %reduce-scatter.2.cloned.1.call-update) | async-done | bytes 245776 | tf_op jit(solution)/shard_map/reduce_scatter | solution.py:65
  (24 shorter events, 0.4 us)
Async XLA Ops:
  6.5 55.9 %copy-start = (bf16[2,96,640]{2,1,0:T(8,128)(2,1)S(1)}, bf16[2,96,640]{2,1,0:T(8,128)(2,1)}, u32[]{:S(2)}) copy-start(bf16[2,96,640]{2,1,0:T(8,128)(2,1)} %param.4) | copy-start | bytes 737284
  6.5 134.1 %all-gather.2.cloned.1.call-start = ((), (), s32[]{:S(2)}) async-start(), calls=%async_computation.1 | async-start | bytes 7372800 | tf_op jit(solution)/shard_map/all_gather | solution.py:62
  7.3 161.2 %reduce-scatter.2.cloned.1.call-start = ((), (), s32[]{:S(2)}) async-start(), calls=%async_computation.2 | async-start | bytes 1228800 | tf_op jit(solution)/shard_map/reduce_scatter | solution.py:65
  7.3 30.4 %collective-permute-start = (bf16[2,3,32,640]{3,2,1,0:T(8,128)(2,1)}, bf16[2,3,32,640]{3,2,1,0:T(8,128)(2,1)S(1)}, u32[]{:S(2)}, u32[]{:S(2)}) collective-permute-start(bf16[2,3,32,640]{3,2,1,0:T(8,128)(2,1)} %bitcast.25), channel_id=1, source_target_pairs={{0,16},{4,20},{8,24},{12,28},{16,0},{20,4},{24,8},{28,12},{1,17},{... | collective-permute-start | bytes 737288 | tf_op jit(solution)/shard_map/ppermute | solution.py:16
  9.7 52.6 %collective-permute-start.1 = (bf16[2,3,32,640]{3,2,1,0:T(8,128)(2,1)}, bf16[2,3,32,640]{3,2,1,0:T(8,128)(2,1)S(1)}, u32[]{:S(2)}, u32[]{:S(2)}) collective-permute-start(bf16[2,3,32,640]{3,2,1,0:T(8,128)(2,1)} %bitcast.26), channel_id=1, source_target_pairs={{0,12},{4,16},{8,20},{12,24},{16,28},{20,0},{24,4},{28,8},{1,13},{... | collective-permute-start | bytes 737288 | tf_op jit(solution)/shard_map/ppermute | solution.py:16
  11.9 50.4 %collective-permute-start.2 = (bf16[2,3,32,640]{3,2,1,0:T(8,128)(2,1)}, bf16[2,3,32,640]{3,2,1,0:T(8,128)(2,1)S(1)}, u32[]{:S(2)}, u32[]{:S(2)}) collective-permute-start(bf16[2,3,32,640]{3,2,1,0:T(8,128)(2,1)} %bitcast.27), channel_id=1, source_target_pairs={{0,8},{4,12},{8,16},{12,20},{16,24},{20,28},{24,0},{28,4},{1,9},{5... | collective-permute-start | bytes 737288 | tf_op jit(solution)/shard_map/ppermute | solution.py:16
  11.9 50.4 %collective-permute-start.3 = (bf16[2,3,32,640]{3,2,1,0:T(8,128)(2,1)}, bf16[2,3,32,640]{3,2,1,0:T(8,128)(2,1)S(1)}, u32[]{:S(2)}, u32[]{:S(2)}) collective-permute-start(bf16[2,3,32,640]{3,2,1,0:T(8,128)(2,1)} %bitcast.28), channel_id=1, source_target_pairs={{0,4},{4,8},{8,12},{12,16},{16,20},{20,24},{24,28},{28,0},{1,5},{5... | collective-permute-start | bytes 737288 | tf_op jit(solution)/shard_map/ppermute | solution.py:16
  12.2 50.2 %collective-permute-start.4 = (bf16[2,3,32,640]{3,2,1,0:T(8,128)(2,1)}, bf16[2,3,32,640]{3,2,1,0:T(8,128)(2,1)S(1)}, u32[]{:S(2)}, u32[]{:S(2)}) collective-permute-start(bf16[2,3,32,640]{3,2,1,0:T(8,128)(2,1)} %bitcast.29), channel_id=1, source_target_pairs={{0,28},{4,0},{8,4},{12,8},{16,12},{20,16},{24,20},{28,24},{1,29},{... | collective-permute-start | bytes 737288 | tf_op jit(solution)/shard_map/ppermute | solution.py:16
  37.7 24.8 %collective-permute-start.5 = (bf16[2,3,32,640]{3,2,1,0:T(8,128)(2,1)}, bf16[2,3,32,640]{3,2,1,0:T(8,128)(2,1)S(1)}, u32[]{:S(2)}, u32[]{:S(2)}) collective-permute-start(bf16[2,3,32,640]{3,2,1,0:T(8,128)(2,1)} %bitcast.30), channel_id=1, source_target_pairs={{0,24},{4,28},{8,0},{12,4},{16,8},{20,12},{24,16},{28,20},{1,25},{... | collective-permute-start | bytes 737288 | tf_op jit(solution)/shard_map/ppermute | solution.py:16
  62.3 16.7 %collective-permute-start.6 = (bf16[2,3,32,640]{3,2,1,0:T(8,128)(2,1)}, bf16[2,3,32,640]{3,2,1,0:T(8,128)(2,1)S(1)}, u32[]{:S(2)}, u32[]{:S(2)}) collective-permute-start(bf16[2,3,32,640]{3,2,1,0:T(8,128)(2,1)} %bitcast.31), channel_id=1, source_target_pairs={{0,20},{4,24},{8,28},{12,0},{16,4},{20,8},{24,12},{28,16},{1,21},{... | collective-permute-start | bytes 737288 | tf_op jit(solution)/shard_map/ppermute | solution.py:16
  79.0 0.9 copy-start.1
Sparse Core Ops, SparseCore 0:
  9.6 131.0 all-gather.1
  145.9 22.4 reduce-scatter.1
where the time goes:
time: 178 us; the launch traced here: 175 us
  waiting for transfers between devices  143 us (80%)
  between operations  13.6 us (8%)
  starting transfers between devices  8.84 us (5%)
  matrix products  8.09 us (5%)
    ppermute x7, waiting for transfers between devices, from_behind(): lax.ppermute(x, axis, [(i, (i + by) % devices) for i in range(devices)])  62.5 us
    all_gather x1, waiting for transfers between devices, on_device(): lax.all_gather(out_weight, 'frames', axis=1, tiled=True)  57.4 us
    reduce_scatter x1, waiting for transfers between devices, on_device(): lax.psum_scatter(partial_rows.astype(jnp.bfloat16), 'heads', scatter_dime...  22.6 us
    ppermute x7, starting transfers between devices, from_behind(): lax.ppermute(x, axis, [(i, (i + by) % devices) for i in range(devices)])  8.8 us
    dot_general x1, matrix products, on_device(): jnp.dot(attended, lax.all_gather(out_weight, 'frames', axis=1, tiled=True...  5.09 us
  transfers between devices with their start and end apart: 9, of which 5 were waited for; matrix products, arithmetic and copies ran while one was open for 2% of the time, Pallas kernels for 0%

commit v1 on v0

--- a/solution.py
+++ b/solution.py
@@ -1,11 +1,17 @@
+import functools
+import math
+
 import jax
 import jax.numpy as jnp
 from jax import lax
+from jax.experimental import pallas as pl
+from jax.experimental.pallas import tpu as pltpu
 from jax.sharding import PartitionSpec as P
 
 HD = 128
 TPF = 32
 FR_DEV = 3
+ROWS = FR_DEV * TPF
 
 
 reach_cap = 32
@@ -16,7 +22,7 @@
     return lax.ppermute(x, axis, [(i, (i + by) % devices) for i in range(devices)])
 
 
-def on_device(queries, keys_values, out_weight):
+def on_device_band(queries, keys_values, out_weight):
     total_frames = lax.axis_size("frames") * FR_DEV
     reach = min(reach_cap, (total_frames - 1) // 2)
     steps = (reach + FR_DEV - 1) // FR_DEV
@@ -67,9 +73,131 @@
     )
 
 
+def ring_order(n):
+    return list(range(0, n, 2)) + list(range(n - 1, 0, -2))
+
+
+def hop(x, n, by):
+    order = ring_order(n)
+    return lax.ppermute(x, "frames", [(order[i], order[(i + by) % n]) for i in range(n)])
+
+
+def gather_ring(parts, n):
+    order = jnp.array(ring_order(n), jnp.int32)
+    me = lax.axis_index("frames")
+    place = jnp.argmax(order == me).astype(jnp.int32)
+    stacks = [
+        lax.dynamic_update_slice_in_dim(jnp.zeros((n,) + p.shape, p.dtype), p[None], me, 0) for p in parts
+    ]
+    ups, downs = list(parts), list(parts)
+    for step in range(1, n // 2 + 1):
+        last = step == n // 2
+        for j in range(len(parts)):
+            for by, held in ((1, ups), (-1, downs)):
+                if last and (j % 2 == 0) == (by > 0):
+                    continue
+                held[j] = hop(held[j], n, by)
+                owner = order[(place - by * step) % n]
+                stacks[j] = lax.dynamic_update_slice_in_dim(stacks[j], held[j][None], owner, 0)
+    return stacks
+
+
+def attend_kernel(heads, total_frames, reach, count, first_ref, q_ref, kv_ref, w_ref, out_ref):
+    first = first_ref[0]
+    tokens = kv_ref.shape[0] * ROWS
+    scale = HD ** (-0.5) * math.log2(math.e)
+
+    def block(i, carry):
+        owner = 2 * i + first
+        row_frame = owner * FR_DEV + lax.broadcasted_iota(jnp.int32, (ROWS, tokens), 0) // TPF
+        col_frame = lax.broadcasted_iota(jnp.int32, (ROWS, tokens), 1) // TPF
+        apart = jnp.abs(row_frame - col_frame)
+        bias = jnp.where(jnp.minimum(apart, total_frames - apart) <= reach, 0.0, -1e30)
+        attended = []
+        for head in range(heads):
+            cols = slice(head * HD, (head + 1) * HD)
+            keys = kv_ref[:, 0, :, cols].reshape(tokens, HD)
+            values = kv_ref[:, 1, :, cols].reshape(tokens, HD)
+            scores = lax.dot_general(
+                q_ref[owner, :, cols], keys, (((1,), (1,)), ((), ())), preferred_element_type=jnp.float32
+            )
+            scores = scores * scale + bias
+            weights = jnp.exp2(scores - jnp.max(scores, axis=1, keepdims=True))
+            total = jnp.sum(weights, axis=1, keepdims=True)
+            mixed = jnp.dot(weights.astype(jnp.bfloat16), values, preferred_element_type=jnp.float32)
+            attended.append((mixed / total).astype(jnp.bfloat16))
+        rows = jnp.concatenate(attended, axis=1)
+        out_ref[i] = jnp.dot(rows, w_ref[...], preferred_element_type=jnp.float32).astype(out_ref.dtype)
+        return carry
+
+    lax.fori_loop(0, count, block, 0)
+
+
+def attend(first, q_all, kv_all, out_weight, out_dtype):
+    n, rows, width = q_all.shape
+    count = n // 2
+    total_frames = n * FR_DEV
+    reach = min(reach_cap, (total_frames - 1) // 2)
+    cols = out_weight.shape[1]
+    vmem = pl.BlockSpec(memory_space=pltpu.VMEM)
+    return pl.pallas_call(
+        functools.partial(attend_kernel, width // HD, total_frames, reach, count),
+        out_shape=jax.ShapeDtypeStruct((count, rows, cols), out_dtype),
+        in_specs=[pl.BlockSpec(memory_space=pltpu.SMEM), vmem, vmem, vmem],
+        out_specs=vmem,
+        compiler_params=pltpu.CompilerParams(vmem_limit_bytes=32 * 1024 * 1024),
+        cost_estimate=pl.CostEstimate(
+            flops=count * rows * width * (4 * n * rows + 2 * cols),
+            bytes_accessed=2 * (3 * q_all.size + out_weight.size),
+            transcendentals=count * rows * n * rows * (width // HD),
+        ),
+    )(first.reshape(1), q_all, kv_all, out_weight)
+
+
+def on_device_ring(queries, keys_values, out_weight):
+    n = lax.axis_size("frames")
+    cores = 2
+    frame, head = lax.axis_index("frames"), lax.axis_index("heads")
+    wide = lax.axis_size("heads") // cores
+    x, core = head // cores, head % cores
+    kv_all, q_all = gather_ring([keys_values, queries], n)
+    given = attend(1 - core, q_all, kv_all, out_weight, jnp.bfloat16)
+    taken = lax.ppermute(
+        given, "heads", [(h, h // cores * cores + (h + 1) % cores) for h in range(wide * cores)]
+    )
+    kept = attend(core, q_all, kv_all, out_weight, jnp.float32)
+    sources = 2 * wide
+    source = frame % 2 * wide + x
+    arrived = []
+    for slot in range(sources):
+        pairs = []
+        for f in range(n):
+            for h in range(wide * cores):
+                block = slot ^ (f % 2 * wide + h // cores)
+                pairs.append((f * wide * cores + h, (2 * block + h % cores) * wide * cores + f // 2))
+        which = slot ^ source
+        total = kept[which] + taken[which].astype(jnp.float32)
+        arrived.append(lax.ppermute(total.astype(jnp.bfloat16), ("frames", "heads"), pairs))
+    stack = jnp.stack(arrived)
+    mine = frame // 2
+    halves = []
+    for y in range(2):
+        total = sum(stack[mine ^ (y * wide + other)].astype(jnp.float32) for other in range(wide))
+        halves.append(total.astype(jnp.bfloat16))
+    return jnp.concatenate(halves, axis=1)
+
+
 def solution(mesh):
     in_specs = (P("frames", "heads"), P(None, "frames", "heads"), P("heads", "frames"))
     out_specs = P("frames", "heads")
+    n, heads = mesh.shape["frames"], mesh.shape["heads"]
+    total_frames = n * FR_DEV
+    reach = min(reach_cap, (total_frames - 1) // 2)
+    every = total_frames - (2 * reach + 1) < FR_DEV and heads == 4 and n == 2 * heads
     return jax.shard_map(
-        on_device, mesh=mesh, in_specs=in_specs, out_specs=out_specs, check_vma=False
-    )
+        on_device_ring if every else on_device_band,
+        mesh=mesh,
+        in_specs=in_specs,
+        out_specs=out_specs,
+        check_vma=False,
+    )

time: 178 us -> 99.8 us (0.56)
  the two profiles are of different devices: /device:TPU:3 before, /device:TPU:1 now
where the time goes in v1:
time: 99.8 us; the launch traced here: 99.2 us
  starting transfers between devices  29.5 us (30%)
  waiting for transfers between devices  23.3 us (23%)
  between operations  20.2 us (20%)
  Pallas kernels  15.6 us (16%)
  local copies, waits for them, and re-layouts  7.15 us (7%)
  other arithmetic  3.43 us (3%)
    pallas_call x2, Pallas kernels, attend(): pl.pallas_call(functools.partial(attend_kernel, width // HD, total_frames...  15.6 us
    ppermute x14, waiting for transfers between devices, hop(): lax.ppermute(x, 'frames', [(order[i], order[(i + by) % n]) for i in range...  15.4 us
    ppermute x4, starting transfers between devices, on_device_ring(): lax.ppermute(total.astype(jnp.bfloat16), ('frames', 'heads'), pairs)  12.9 us
    ppermute x14, starting transfers between devices, hop(): lax.ppermute(x, 'frames', [(order[i], order[(i + by) % n]) for i in range...  11.4 us
    ppermute x4, waiting for transfers between devices, on_device_ring(): lax.ppermute(total.astype(jnp.bfloat16), ('frames', 'heads'), pairs)  7.91 us
    ppermute x1, starting transfers between devices, on_device_ring(): lax.ppermute(given, 'heads', [(h, h // cores * cores + (h + 1) % cores) f...  5.21 us
    dynamic_update_slice x14, local copies, waits for them, and re-layouts, gather_ring(): lax.dynamic_update_slice_in_dim(stacks[j], held[j][None], owner, 0)  3.13 us
  transfers between devices with their start and end apart: 19, of which 7 were waited for; matrix products, arithmetic and copies ran while one was open for 7% of the time, Pallas kernels for 8%

profile of v1, /device:TPU:1, one launch (start us, length us, event | category | flops | bytes accessed | tf_op | source)
XLA Modules:
  0.0 99.2 jit_solution(7978848622979827445)
XLA Ops:
  0.0 2.1 %collective-permute-start.7 = (bf16[2,96,640]{2,1,0:T(8,128)(2,1)}, bf16[2,96,640]{2,1,0:T(8,128)(2,1)}, u32[]{:S(2)}, u32[]{:S(2)}) collective-permute-start(bf16[2,96,640]{2,1,0:T(8,128)(2,1)} %param.5), channel_id=1, source_target_pairs={{0,8},{8,16},{16,24},{24,28},{28,20},{20,12},{12,4},{4,0},{1,9},{9... | collective-permute-start | bytes 737288 | tf_op jit(solution)/shard_map/ppermute | solution.py:82
  2.1 1.5 %collective-permute-start = (bf16[96,640]{1,0:T(8,128)(2,1)}, bf16[96,640]{1,0:T(8,128)(2,1)}, u32[]{:S(2)}, u32[]{:S(2)}) collective-permute-start(bf16[96,640]{1,0:T(8,128)(2,1)} %param.4), channel_id=1, source_target_pairs={{0,8},{8,16},{16,24},{24,28},{28,20},{20,12},{12,4},{4,0},{1,9},{9... | collective-permute-start | bytes 368648 | tf_op jit(solution)/shard_map/ppermute | solution.py:82
  3.6 1.4 %compare_reduce_fusion = (pred[]{:T(512)}, s32[]{:T(128)}) fusion(s32[8]{0:T(128)} %constant.125.clone, s32[]{:T(128)S(6)} %axis_index.29), kind=kLoop, calls=%fused_computation.30 | loop fusion | flops 57 | bytes 41 | tf_op jit(solution)/shard_map/gather_ring/reduce | solution.py:88
  10.5 1.6 %fusion.6 = (s32[1]{0:T(128)}, s32[1]{0:T(128)}, s32[1]{0:T(128)}, s32[1]{0:T(128)}, s32[1]{0:T(128)}, /*index=5*/s32[1]{0:T(128)}, s32[1]{0:T(128)}, s32[1]{0:T(128)}) fusion(s32[8]{0:T(128)} %constant.125.clone, s32[]{:T(128)S(6)} %select_n.182, s32[]{:T(128)S(6)} %select_n.176, s32[]{:T(128)S(6)} %select_n.173, s32[]{:T(128)S(6)} %select_n.170, ...), kind=kLoop, calls=%fused_computation.31 | loop fusion | bytes 96 | tf_op jit(solution)/shard_map/dynamic_slice | solution.py:100
  27.8 1.5 %collective-permute-start.2 = (bf16[96,640]{1,0:T(8,128)(2,1)}, bf16[96,640]{1,0:T(8,128)(2,1)S(1)}, u32[]{:S(2)}, u32[]{:S(2)}) collective-permute-start(bf16[96,640]{1,0:T(8,128)(2,1)} %collective-permute-done), channel_id=1, source_target_pairs={{0,8},{8,16},{16,24},{24,28},{28,20},{20,12},{12,4},{4,0},{1,9},{9... | collective-permute-start | bytes 368648 | tf_op jit(solution)/shard_map/ppermute | solution.py:82
  31.2 1.5 %collective-permute-start.9 = (bf16[2,96,640]{2,1,0:T(8,128)(2,1)}, bf16[2,96,640]{2,1,0:T(8,128)(2,1)S(1)}, u32[]{:S(2)}, u32[]{:S(2)}) collective-permute-start(bf16[2,96,640]{2,1,0:T(8,128)(2,1)} %collective-permute-done.7), channel_id=1, source_target_pairs={{0,8},{8,16},{16,24},{24,28},{28,20},{20,12},{12,4},{4,0},{1,9},{9... | collective-permute-start | bytes 737288 | tf_op jit(solution)/shard_map/ppermute | solution.py:82
  32.8 1.0 bitcast_dynamic-update-slice_fusion.6
  33.8 1.5 %collective-permute-start.4 = (bf16[96,640]{1,0:T(8,128)(2,1)S(1)}, bf16[96,640]{1,0:T(8,128)(2,1)S(1)}, u32[]{:S(2)}, u32[]{:S(2)}) collective-permute-start(bf16[96,640]{1,0:T(8,128)(2,1)S(1)} %collective-permute-done.2), channel_id=1, source_target_pairs={{0,8},{8,16},{16,24},{24,28},{28,20},{20,12},{12,4},{4,0},{1,9},{9... | collective-permute-start | bytes 368648 | tf_op jit(solution)/shard_map/ppermute | solution.py:82
  35.4 4.1 %collective-permute-done.4 = bf16[96,640]{1,0:T(8,128)(2,1)S(1)} collective-permute-done((bf16[96,640]{1,0:T(8,128)(2,1)S(1)}, bf16[96,640]{1,0:T(8,128)(2,1)S(1)}, u32[]{:S(2)}, u32[]{:S(2)}) %collective-permute-start.4) | collective-permute-done | bytes 122912 | tf_op jit(solution)/shard_map/ppermute | solution.py:82
  39.5 1.5 %collective-permute-start.6 = (bf16[96,640]{1,0:T(8,128)(2,1)S(1)}, bf16[96,640]{1,0:T(8,128)(2,1)S(1)}, u32[]{:S(2)}, u32[]{:S(2)}) collective-permute-start(bf16[96,640]{1,0:T(8,128)(2,1)S(1)} %collective-permute-done.4), channel_id=1, source_target_pairs={{0,8},{8,16},{16,24},{24,28},{28,20},{20,12},{12,4},{4,0},{1,9},{9... | collective-permute-start | bytes 368648 | tf_op jit(solution)/shard_map/ppermute | solution.py:82
  41.6 1.3 %collective-permute-start.11 = (bf16[2,96,640]{2,1,0:T(8,128)(2,1)S(1)}, bf16[2,96,640]{2,1,0:T(8,128)(2,1)S(1)}, u32[]{:S(2)}, u32[]{:S(2)}) collective-permute-start(bf16[2,96,640]{2,1,0:T(8,128)(2,1)S(1)} %collective-permute-done.9), channel_id=1, source_target_pairs={{0,8},{8,16},{16,24},{24,28},{28,20},{20,12},{12,4},{4,0},{1,9},{9... | collective-permute-start | bytes 737288 | tf_op jit(solution)/shard_map/ppermute | solution.py:82
  43.6 4.7 %collective-permute-done.12 = bf16[2,96,640]{2,1,0:T(8,128)(2,1)S(1)} collective-permute-done((bf16[2,96,640]{2,1,0:T(8,128)(2,1)S(1)}, bf16[2,96,640]{2,1,0:T(8,128)(2,1)S(1)}, u32[]{:S(2)}, u32[]{:S(2)}) %collective-permute-start.12) | collective-permute-done | bytes 245792 | tf_op jit(solution)/shard_map/ppermute | solution.py:82
  48.5 5.7 %collective-permute-done.13 = bf16[2,96,640]{2,1,0:T(8,128)(2,1)S(1)} collective-permute-done((bf16[2,96,640]{2,1,0:T(8,128)(2,1)S(1)}, bf16[2,96,640]{2,1,0:T(8,128)(2,1)S(1)}, u32[]{:S(2)}, u32[]{:S(2)}) %collective-permute-start.13) | collective-permute-done | bytes 245792 | tf_op jit(solution)/shard_map/ppermute | solution.py:82
  54.3 7.8 %shard_map.47 = bf16[4,96,640]{2,1,0:T(8,128)(2,1)S(1)} custom-call(s32[1]{0:T(128)} %bitcast.25.first_ref, bf16[8,96,640]{2,1,0:T(8,128)(2,1)S(1)} %bitcast_dynamic-update-slice_fusion.8.q_ref, bf16[8,2,96,640]{3,2,1,0:T(8,128)(2,1)S(1)} %bitcast_dynamic-update-slice_fusion.kv_ref, bf16[640,640]{1,0:T(8,128)(2,1)S(1)} %copy-done), custom_call_target="tpu_custom_call" | custom-call | flops 1069547520 | bytes 3768320 | tf_op jit(solution)/shard_map/pallas_call | solution.py:143
  62.1 5.2 %collective-permute-start.14 = (bf16[4,96,640]{2,1,0:T(8,128)(2,1)S(1)}, bf16[4,96,640]{2,1,0:T(8,128)(2,1)}, u32[]{:S(2)}, u32[]{:S(2)}) collective-permute-start(bf16[4,96,640]{2,1,0:T(8,128)(2,1)S(1)} %shard_map.47), channel_id=1, source_target_pairs={{0,1},{1,0},{2,3},{3,2},{4,5},{5,4},{6,7},{7,6},{8,9},{9,8},{10,11... | collective-permute-start | bytes 1474568 | tf_op jit(solution)/shard_map/ppermute | solution.py:165
  67.3 1.1 %copy-done.1 = bf16[640,640]{1,0:T(8,128)(2,1)S(1)} copy-done((bf16[640,640]{1,0:T(8,128)(2,1)S(1)}, bf16[640,640]{1,0:T(8,128)(2,1)}, u32[]{:S(2)}) %copy-start.1) | copy-done | bytes 819224
  68.5 7.8 %shard_map.46 = f32[4,96,640]{2,1,0:T(8,128)S(1)} custom-call(s32[1]{0:T(128)} %bitcast.first_ref, bf16[8,96,640]{2,1,0:T(8,128)(2,1)S(1)} %bitcast_dynamic-update-slice_fusion.8.q_ref, bf16[8,2,96,640]{3,2,1,0:T(8,128)(2,1)S(1)} %bitcast_dynamic-update-slice_fusion.kv_ref, bf16[640,640]{1,0:T(8,128)(2,1)S(1)} %copy-done.1), custom_call_target="tpu_custom_call" | custom-call | flops 1069547520 | bytes 3768320 | tf_op jit(solution)/shard_map/pallas_call | solution.py:143
  76.3 1.2 %fusion = (bf16[96,640]{1,0:T(8,128)(2,1)S(1)}, bf16[96,640]{1,0:T(8,128)(2,1)S(1)}, bf16[96,640]{1,0:T(8,128)(2,1)S(1)}, bf16[96,640]{1,0:T(8,128)(2,1)S(1)}) fusion(f32[4,96,640]{2,1,0:T(8,128)S(1)} %shard_map.46, s32[]{:T(128)S(6)} %select_n.186, bf16[4,96,640]{2,1,0:T(8,128)(2,1)} %collective-permute-done.14, s32[]{:T(128)S(6)} %select_n.189, ...), kind=kLoop, calls=%fused_computation.16 | loop fusion | flops 737280 | bytes 1966096 | tf_op jit(solution)/shard_map/convert_element_type | solution.py:180
  77.5 2.0 %collective-permute-start.15 = (bf16[96,640]{1,0:T(8,128)(2,1)S(1)}, bf16[96,640]{1,0:T(8,128)(2,1)S(1)}, u32[]{:S(2)}, u32[]{:S(2)}) collective-permute-start(bf16[96,640]{1,0:T(8,128)(2,1)S(1)} %get-tuple-element.7), channel_id=1, source_target_pairs={{0,0},{1,4},{2,8},{3,12},{4,16},{5,20},{6,24},{7,28},{8,1},{9,5},{... | collective-permute-start | bytes 368648 | tf_op jit(solution)/shard_map/ppermute | solution.py:180
  79.5 3.7 %collective-permute-start.16 = (bf16[96,640]{1,0:T(8,128)(2,1)S(1)}, bf16[96,640]{1,0:T(8,128)(2,1)S(1)}, u32[]{:S(2)}, u32[]{:S(2)}) collective-permute-start(bf16[96,640]{1,0:T(8,128)(2,1)S(1)} %get-tuple-element.10), channel_id=1, source_target_pairs={{0,8},{1,12},{2,0},{3,4},{4,24},{5,28},{6,16},{7,20},{8,9},{9,13},... | collective-permute-start | bytes 368648 | tf_op jit(solution)/shard_map/ppermute | solution.py:180
  83.2 2.3 %collective-permute-start.17 = (bf16[96,640]{1,0:T(8,128)(2,1)S(1)}, bf16[96,640]{1,0:T(8,128)(2,1)S(1)}, u32[]{:S(2)}, u32[]{:S(2)}) collective-permute-start(bf16[96,640]{1,0:T(8,128)(2,1)S(1)} %get-tuple-element.9), channel_id=1, source_target_pairs={{0,16},{1,20},{2,24},{3,28},{4,0},{5,4},{6,8},{7,12},{8,17},{9,21}... | collective-permute-start | bytes 368648 | tf_op jit(solution)/shard_map/ppermute | solution.py:180
  85.5 4.9 %collective-permute-start.18 = (bf16[96,640]{1,0:T(8,128)(2,1)S(1)}, bf16[96,640]{1,0:T(8,128)(2,1)S(1)}, u32[]{:S(2)}, u32[]{:S(2)}) collective-permute-start(bf16[96,640]{1,0:T(8,128)(2,1)S(1)} %get-tuple-element.8), channel_id=1, source_target_pairs={{0,24},{1,28},{2,16},{3,20},{4,8},{5,12},{6,0},{7,4},{8,25},{9,29}... | collective-permute-start | bytes 368648 | tf_op jit(solution)/shard_map/ppermute | solution.py:180
  90.4 3.8 %collective-permute-done.17 = bf16[96,640]{1,0:T(8,128)(2,1)S(1)} collective-permute-done((bf16[96,640]{1,0:T(8,128)(2,1)S(1)}, bf16[96,640]{1,0:T(8,128)(2,1)S(1)}, u32[]{:S(2)}, u32[]{:S(2)}) %collective-permute-start.17) | collective-permute-done | bytes 122912 | tf_op jit(solution)/shard_map/ppermute | solution.py:180
  94.2 4.1 %collective-permute-done.18 = bf16[96,640]{1,0:T(8,128)(2,1)S(1)} collective-permute-done((bf16[96,640]{1,0:T(8,128)(2,1)S(1)}, bf16[96,640]{1,0:T(8,128)(2,1)S(1)}, u32[]{:S(2)}, u32[]{:S(2)}) %collective-permute-start.18) | collective-permute-done | bytes 122912 | tf_op jit(solution)/shard_map/ppermute | solution.py:180
  (46 shorter events, 5.7 us)
Async XLA Ops:
  0.0 22.6 %copy-start.2 = (bf16[2,96,640]{2,1,0:T(8,128)(2,1)S(1)}, bf16[2,96,640]{2,1,0:T(8,128)(2,1)}, u32[]{:S(2)}) copy-start(bf16[2,96,640]{2,1,0:T(8,128)(2,1)} %param.5) | copy-start | bytes 737284
  0.0 31.2 %collective-permute-start.7 = (bf16[2,96,640]{2,1,0:T(8,128)(2,1)}, bf16[2,96,640]{2,1,0:T(8,128)(2,1)}, u32[]{:S(2)}, u32[]{:S(2)}) collective-permute-start(bf16[2,96,640]{2,1,0:T(8,128)(2,1)} %param.5), channel_id=1, source_target_pairs={{0,8},{8,16},{16,24},{24,28},{28,20},{20,12},{12,4},{4,0},{1,9},{9... | collective-permute-start | bytes 737288 | tf_op jit(solution)/shard_map/ppermute | solution.py:82
  2.1 30.6 %collective-permute-start.8 = (bf16[2,96,640]{2,1,0:T(8,128)(2,1)}, bf16[2,96,640]{2,1,0:T(8,128)(2,1)S(1)}, u32[]{:S(2)}, u32[]{:S(2)}) collective-permute-start(bf16[2,96,640]{2,1,0:T(8,128)(2,1)} %param.5), channel_id=1, source_target_pairs={{0,4},{8,0},{16,8},{24,16},{28,24},{20,28},{12,20},{4,12},{1,5},{9... | collective-permute-start | bytes 737288 | tf_op jit(solution)/shard_map/ppermute | solution.py:82
  2.1 25.7 %collective-permute-start = (bf16[96,640]{1,0:T(8,128)(2,1)}, bf16[96,640]{1,0:T(8,128)(2,1)}, u32[]{:S(2)}, u32[]{:S(2)}) collective-permute-start(bf16[96,640]{1,0:T(8,128)(2,1)} %param.4), channel_id=1, source_target_pairs={{0,8},{8,16},{16,24},{24,28},{28,20},{20,12},{12,4},{4,0},{1,9},{9... | collective-permute-start | bytes 368648 | tf_op jit(solution)/shard_map/ppermute | solution.py:82
  3.6 25.8 %collective-permute-start.1 = (bf16[96,640]{1,0:T(8,128)(2,1)}, bf16[96,640]{1,0:T(8,128)(2,1)}, u32[]{:S(2)}, u32[]{:S(2)}) collective-permute-start(bf16[96,640]{1,0:T(8,128)(2,1)} %param.4), channel_id=1, source_target_pairs={{0,4},{8,0},{16,8},{24,16},{28,24},{20,28},{12,20},{4,12},{1,5},{9... | collective-permute-start | bytes 368648 | tf_op jit(solution)/shard_map/ppermute | solution.py:82
  27.8 5.9 %collective-permute-start.2 = (bf16[96,640]{1,0:T(8,128)(2,1)}, bf16[96,640]{1,0:T(8,128)(2,1)S(1)}, u32[]{:S(2)}, u32[]{:S(2)}) collective-permute-start(bf16[96,640]{1,0:T(8,128)(2,1)} %collective-permute-done), channel_id=1, source_target_pairs={{0,8},{8,16},{16,24},{24,28},{28,20},{20,12},{12,4},{4,0},{1,9},{9... | collective-permute-start | bytes 368648 | tf_op jit(solution)/shard_map/ppermute | solution.py:82
  29.4 5.9 %collective-permute-start.3 = (bf16[96,640]{1,0:T(8,128)(2,1)}, bf16[96,640]{1,0:T(8,128)(2,1)S(1)}, u32[]{:S(2)}, u32[]{:S(2)}) collective-permute-start(bf16[96,640]{1,0:T(8,128)(2,1)} %collective-permute-done.1), channel_id=1, source_target_pairs={{0,4},{8,0},{16,8},{24,16},{28,24},{20,28},{12,20},{4,12},{1,5},{9... | collective-permute-start | bytes 368648 | tf_op jit(solution)/shard_map/ppermute | solution.py:82
  31.2 10.3 %collective-permute-start.9 = (bf16[2,96,640]{2,1,0:T(8,128)(2,1)}, bf16[2,96,640]{2,1,0:T(8,128)(2,1)S(1)}, u32[]{:S(2)}, u32[]{:S(2)}) collective-permute-start(bf16[2,96,640]{2,1,0:T(8,128)(2,1)} %collective-permute-done.7), channel_id=1, source_target_pairs={{0,8},{8,16},{16,24},{24,28},{28,20},{20,12},{12,4},{4,0},{1,9},{9... | collective-permute-start | bytes 737288 | tf_op jit(solution)/shard_map/ppermute | solution.py:82
  32.7 10.2 %collective-permute-start.10 = (bf16[2,96,640]{2,1,0:T(8,128)(2,1)S(1)}, bf16[2,96,640]{2,1,0:T(8,128)(2,1)S(1)}, u32[]{:S(2)}, u32[]{:S(2)}) collective-permute-start(bf16[2,96,640]{2,1,0:T(8,128)(2,1)S(1)} %collective-permute-done.8), channel_id=1, source_target_pairs={{0,4},{8,0},{16,8},{24,16},{28,24},{20,28},{12,20},{4,12},{1,5},{9... | collective-permute-start | bytes 737288 | tf_op jit(solution)/shard_map/ppermute | solution.py:82
  33.8 5.8 %collective-permute-start.4 = (bf16[96,640]{1,0:T(8,128)(2,1)S(1)}, bf16[96,640]{1,0:T(8,128)(2,1)S(1)}, u32[]{:S(2)}, u32[]{:S(2)}) collective-permute-start(bf16[96,640]{1,0:T(8,128)(2,1)S(1)} %collective-permute-done.2), channel_id=1, source_target_pairs={{0,8},{8,16},{16,24},{24,28},{28,20},{20,12},{12,4},{4,0},{1,9},{9... | collective-permute-start | bytes 368648 | tf_op jit(solution)/shard_map/ppermute | solution.py:82
  35.3 19.0 %copy-start = (bf16[640,640]{1,0:T(8,128)(2,1)S(1)}, bf16[640,640]{1,0:T(8,128)(2,1)}, u32[]{:S(2)}) copy-start(bf16[640,640]{1,0:T(8,128)(2,1)} %w_ref.3) | copy-start | bytes 2457604
  35.3 6.2 %collective-permute-start.5 = (bf16[96,640]{1,0:T(8,128)(2,1)S(1)}, bf16[96,640]{1,0:T(8,128)(2,1)S(1)}, u32[]{:S(2)}, u32[]{:S(2)}) collective-permute-start(bf16[96,640]{1,0:T(8,128)(2,1)S(1)} %collective-permute-done.3), channel_id=1, source_target_pairs={{0,4},{8,0},{16,8},{24,16},{28,24},{20,28},{12,20},{4,12},{1,5},{9... | collective-permute-start | bytes 368648 | tf_op jit(solution)/shard_map/ppermute | solution.py:82
  39.5 4.0 %collective-permute-start.6 = (bf16[96,640]{1,0:T(8,128)(2,1)S(1)}, bf16[96,640]{1,0:T(8,128)(2,1)S(1)}, u32[]{:S(2)}, u32[]{:S(2)}) collective-permute-start(bf16[96,640]{1,0:T(8,128)(2,1)S(1)} %collective-permute-done.4), channel_id=1, source_target_pairs={{0,8},{8,16},{16,24},{24,28},{28,20},{20,12},{12,4},{4,0},{1,9},{9... | collective-permute-start | bytes 368648 | tf_op jit(solution)/shard_map/ppermute | solution.py:82
  41.6 6.9 %collective-permute-start.11 = (bf16[2,96,640]{2,1,0:T(8,128)(2,1)S(1)}, bf16[2,96,640]{2,1,0:T(8,128)(2,1)S(1)}, u32[]{:S(2)}, u32[]{:S(2)}) collective-permute-start(bf16[2,96,640]{2,1,0:T(8,128)(2,1)S(1)} %collective-permute-done.9), channel_id=1, source_target_pairs={{0,8},{8,16},{16,24},{24,28},{28,20},{20,12},{12,4},{4,0},{1,9},{9... | collective-permute-start | bytes 737288 | tf_op jit(solution)/shard_map/ppermute | solution.py:82
  42.9 5.3 %collective-permute-start.12 = (bf16[2,96,640]{2,1,0:T(8,128)(2,1)S(1)}, bf16[2,96,640]{2,1,0:T(8,128)(2,1)S(1)}, u32[]{:S(2)}, u32[]{:S(2)}) collective-permute-start(bf16[2,96,640]{2,1,0:T(8,128)(2,1)S(1)} %collective-permute-done.10), channel_id=1, source_target_pairs={{0,4},{8,0},{16,8},{24,16},{28,24},{20,28},{12,20},{4,12},{1,5},{9... | collective-permute-start | bytes 737288 | tf_op jit(solution)/shard_map/ppermute | solution.py:82
  48.3 6.0 %collective-permute-start.13 = (bf16[2,96,640]{2,1,0:T(8,128)(2,1)S(1)}, bf16[2,96,640]{2,1,0:T(8,128)(2,1)S(1)}, u32[]{:S(2)}, u32[]{:S(2)}) collective-permute-start(bf16[2,96,640]{2,1,0:T(8,128)(2,1)S(1)} %collective-permute-done.12), channel_id=1, source_target_pairs={{0,4},{8,0},{16,8},{24,16},{28,24},{20,28},{12,20},{4,12},{1,5},{9... | collective-permute-start | bytes 737288 | tf_op jit(solution)/shard_map/ppermute | solution.py:82
  62.1 14.2 %collective-permute-start.14 = (bf16[4,96,640]{2,1,0:T(8,128)(2,1)S(1)}, bf16[4,96,640]{2,1,0:T(8,128)(2,1)}, u32[]{:S(2)}, u32[]{:S(2)}) collective-permute-start(bf16[4,96,640]{2,1,0:T(8,128)(2,1)S(1)} %shard_map.47), channel_id=1, source_target_pairs={{0,1},{1,0},{2,3},{3,2},{4,5},{5,4},{6,7},{7,6},{8,9},{9,8},{10,11... | collective-permute-start | bytes 1474568 | tf_op jit(solution)/shard_map/ppermute | solution.py:165
  67.3 1.1 %copy-start.1 = (bf16[640,640]{1,0:T(8,128)(2,1)S(1)}, bf16[640,640]{1,0:T(8,128)(2,1)}, u32[]{:S(2)}) copy-start(bf16[640,640]{1,0:T(8,128)(2,1)} %w_ref.3) | copy-start | bytes 2457604
  77.5 12.9 %collective-permute-start.15 = (bf16[96,640]{1,0:T(8,128)(2,1)S(1)}, bf16[96,640]{1,0:T(8,128)(2,1)S(1)}, u32[]{:S(2)}, u32[]{:S(2)}) collective-permute-start(bf16[96,640]{1,0:T(8,128)(2,1)S(1)} %get-tuple-element.7), channel_id=1, source_target_pairs={{0,0},{1,4},{2,8},{3,12},{4,16},{5,20},{6,24},{7,28},{8,1},{9,5},{... | collective-permute-start | bytes 368648 | tf_op jit(solution)/shard_map/ppermute | solution.py:180
  79.5 10.9 %collective-permute-start.16 = (bf16[96,640]{1,0:T(8,128)(2,1)S(1)}, bf16[96,640]{1,0:T(8,128)(2,1)S(1)}, u32[]{:S(2)}, u32[]{:S(2)}) collective-permute-start(bf16[96,640]{1,0:T(8,128)(2,1)S(1)} %get-tuple-element.10), channel_id=1, source_target_pairs={{0,8},{1,12},{2,0},{3,4},{4,24},{5,28},{6,16},{7,20},{8,9},{9,13},... | collective-permute-start | bytes 368648 | tf_op jit(solution)/shard_map/ppermute | solution.py:180
  83.2 11.0 %collective-permute-start.17 = (bf16[96,640]{1,0:T(8,128)(2,1)S(1)}, bf16[96,640]{1,0:T(8,128)(2,1)S(1)}, u32[]{:S(2)}, u32[]{:S(2)}) collective-permute-start(bf16[96,640]{1,0:T(8,128)(2,1)S(1)} %get-tuple-element.9), channel_id=1, source_target_pairs={{0,16},{1,20},{2,24},{3,28},{4,0},{5,4},{6,8},{7,12},{8,17},{9,21}... | collective-permute-start | bytes 368648 | tf_op jit(solution)/shard_map/ppermute | solution.py:180
  85.5 12.8 %collective-permute-start.18 = (bf16[96,640]{1,0:T(8,128)(2,1)S(1)}, bf16[96,640]{1,0:T(8,128)(2,1)S(1)}, u32[]{:S(2)}, u32[]{:S(2)}) collective-permute-start(bf16[96,640]{1,0:T(8,128)(2,1)S(1)} %get-tuple-element.8), channel_id=1, source_target_pairs={{0,24},{1,28},{2,16},{3,20},{4,8},{5,12},{6,0},{7,4},{8,25},{9,29}... | collective-permute-start | bytes 368648 | tf_op jit(solution)/shard_map/ppermute | solution.py:180

commit v2 on v1

--- a/solution.py
+++ b/solution.py
@@ -77,71 +77,73 @@
     return list(range(0, n, 2)) + list(range(n - 1, 0, -2))
 
 
+def ring_place(f, n):
+    return f // 2 + f % 2 * (n - 1 - f // 2 * 2)
+
+
 def hop(x, n, by):
     order = ring_order(n)
     return lax.ppermute(x, "frames", [(order[i], order[(i + by) % n]) for i in range(n)])
 
 
 def gather_ring(parts, n):
-    order = jnp.array(ring_order(n), jnp.int32)
-    me = lax.axis_index("frames")
-    place = jnp.argmax(order == me).astype(jnp.int32)
-    stacks = [
-        lax.dynamic_update_slice_in_dim(jnp.zeros((n,) + p.shape, p.dtype), p[None], me, 0) for p in parts
-    ]
-    ups, downs = list(parts), list(parts)
+    found = [[p] + [None] * (n - 1) for p in parts]
     for step in range(1, n // 2 + 1):
         last = step == n // 2
         for j in range(len(parts)):
-            for by, held in ((1, ups), (-1, downs)):
+            for by in (1, -1):
                 if last and (j % 2 == 0) == (by > 0):
                     continue
-                held[j] = hop(held[j], n, by)
-                owner = order[(place - by * step) % n]
-                stacks[j] = lax.dynamic_update_slice_in_dim(stacks[j], held[j][None], owner, 0)
-    return stacks
-
-
-def attend_kernel(heads, total_frames, reach, count, first_ref, q_ref, kv_ref, w_ref, out_ref):
-    first = first_ref[0]
-    tokens = kv_ref.shape[0] * ROWS
+                found[j][by * step % n] = hop(found[j][by * (step - 1) % n], n, by)
+    return [jnp.stack(pieces) for pieces in found]
+
+
+def attend_kernel(heads, n, at_ref, q_ref, kv_ref, w_ref, out_ref):
+    place, first = at_ref[0], at_ref[1]
+    count = n // 2
     scale = HD ** (-0.5) * math.log2(math.e)
 
-    def block(i, carry):
-        owner = 2 * i + first
-        row_frame = owner * FR_DEV + lax.broadcasted_iota(jnp.int32, (ROWS, tokens), 0) // TPF
-        col_frame = lax.broadcasted_iota(jnp.int32, (ROWS, tokens), 1) // TPF
-        apart = jnp.abs(row_frame - col_frame)
-        bias = jnp.where(jnp.minimum(apart, total_frames - apart) <= reach, 0.0, -1e30)
-        attended = []
-        for head in range(heads):
-            cols = slice(head * HD, (head + 1) * HD)
-            keys = kv_ref[:, 0, :, cols].reshape(tokens, HD)
-            values = kv_ref[:, 1, :, cols].reshape(tokens, HD)
-            scores = lax.dot_general(
-                q_ref[owner, :, cols], keys, (((1,), (1,)), ((), ())), preferred_element_type=jnp.float32
+    def slots(parity):
+        return [(place - (i + parity * (n - 1 - 2 * i)) + n) % n for i in range(count)]
+
+    mine = slots(first)
+    order = mine + slots(1 - first)
+    ones = jnp.ones((n * ROWS, HD), jnp.bfloat16)
+    attended = []
+    for head in range(heads):
+        cols = slice(head * HD, (head + 1) * HD)
+        rows = jnp.concatenate([q_ref[o, :, cols] for o in mine], axis=0)
+        keys = jnp.concatenate([kv_ref[o, 0, :, cols] for o in order], axis=0)
+        values = jnp.concatenate([kv_ref[o, 1, :, cols] for o in order], axis=0)
+        scores = lax.dot_general(rows, keys, (((1,), (1,)), ((), ())), preferred_element_type=jnp.float32)
+        groups = []
+        for g in range(count * FR_DEV):
+            tall = slice(g * TPF, (g + 1) * TPF)
+            parts = [scores[tall, c : c + HD] for c in range(0, n * ROWS, HD)]
+            away = (g + count // 2 * FR_DEV) % (count * FR_DEV) * TPF
+            lane = lax.broadcasted_iota(jnp.int32, (TPF, HD), 1)
+            out_of_band = (lane >= away % HD) & (lane < away % HD + TPF)
+            parts[away // HD] = jnp.where(out_of_band, -1e30, parts[away // HD])
+            top = jnp.max(functools.reduce(jnp.maximum, parts), axis=1, keepdims=True)
+            groups.append(
+                jnp.concatenate([jnp.exp2((p - top) * scale).astype(jnp.bfloat16) for p in parts], axis=1)
             )
-            scores = scores * scale + bias
-            weights = jnp.exp2(scores - jnp.max(scores, axis=1, keepdims=True))
-            total = jnp.sum(weights, axis=1, keepdims=True)
-            mixed = jnp.dot(weights.astype(jnp.bfloat16), values, preferred_element_type=jnp.float32)
-            attended.append((mixed / total).astype(jnp.bfloat16))
-        rows = jnp.concatenate(attended, axis=1)
-        out_ref[i] = jnp.dot(rows, w_ref[...], preferred_element_type=jnp.float32).astype(out_ref.dtype)
-        return carry
-
-    lax.fori_loop(0, count, block, 0)
+        weights = jnp.concatenate(groups, axis=0)
+        mixed = jnp.dot(weights, jnp.concatenate([values, ones], axis=1), preferred_element_type=jnp.float32)
+        attended.append((mixed[:, :HD] / mixed[:, HD:]).astype(jnp.bfloat16))
+    result = jnp.dot(jnp.concatenate(attended, axis=1), w_ref[...], preferred_element_type=jnp.float32)
+    for i in range(count):
+        out_ref[i] = result[i * ROWS : (i + 1) * ROWS].astype(out_ref.dtype)
 
 
 def attend(first, q_all, kv_all, out_weight, out_dtype):
     n, rows, width = q_all.shape
     count = n // 2
-    total_frames = n * FR_DEV
-    reach = min(reach_cap, (total_frames - 1) // 2)
     cols = out_weight.shape[1]
+    place = ring_place(lax.axis_index("frames"), n)
     vmem = pl.BlockSpec(memory_space=pltpu.VMEM)
     return pl.pallas_call(
-        functools.partial(attend_kernel, width // HD, total_frames, reach, count),
+        functools.partial(attend_kernel, width // HD, n),
         out_shape=jax.ShapeDtypeStruct((count, rows, cols), out_dtype),
         in_specs=[pl.BlockSpec(memory_space=pltpu.SMEM), vmem, vmem, vmem],
         out_specs=vmem,
@@ -151,7 +153,7 @@
             bytes_accessed=2 * (3 * q_all.size + out_weight.size),
             transcendentals=count * rows * n * rows * (width // HD),
         ),
-    )(first.reshape(1), q_all, kv_all, out_weight)
+    )(jnp.stack([place, first]).astype(jnp.int32), q_all, kv_all, out_weight)
 
 
 def on_device_ring(queries, keys_values, out_weight):
@@ -193,7 +195,7 @@
     n, heads = mesh.shape["frames"], mesh.shape["heads"]
     total_frames = n * FR_DEV
     reach = min(reach_cap, (total_frames - 1) // 2)
-    every = total_frames - (2 * reach + 1) < FR_DEV and heads == 4 and n == 2 * heads
+    every = total_frames == 2 * reach + 2 and heads == 4 and n == 2 * heads
     return jax.shard_map(
         on_device_ring if every else on_device_band,
         mesh=mesh,

time: 99.8 us -> 71.9 us (0.72)
  between operations: 20.2 us -> 0.26 us
  Pallas kernels: 15.6 us -> 6.23 us
  waiting for transfers between devices: 23.3 us -> 29.2 us
  local copies, waits for them, and re-layouts: 7.15 us -> 5.19 us
  other arithmetic: 3.43 us -> 2.23 us
  starting transfers between devices: 29.5 us -> 28.5 us
    pallas_call x2, Pallas kernels: 15.6 us -> 6.23 us  [attend(): pl.pallas_call(functools.partial(attend_kernel, width // HD, n), out_shap...]
    ppermute x14, waiting for transfers between devices: 15.4 us -> 21.2 us  [hop(): lax.ppermute(x, 'frames', [(order[i], order[(i + by) % n]) for i in range...]
    dynamic_update_slice x16 -> x0, local copies, waits for them, and re-layouts: 4.09 us -> none  [the longest x14 3.13 us: gather_ring(): lax.dynamic_update_slice_in_dim(stacks[j], held[j][None], owner, 0)]
    unnamed x6 -> x18, local copies, waits for them, and re-layouts: 1.15 us -> 4.24 us
    dynamic_slice x1 -> x0, local copies, waits for them, and re-layouts: 1.64 us -> none  [gather_ring(): owner = order[(place - by * step) % n]]
    another operation x1 -> x2, other arithmetic: 1.37 us -> 0.15 us  [attend(): jnp.stack([place, first]).astype(jnp.int32)]
  transfers between devices with their start and end apart: 19 -> 19, of which waited for: 7 -> 8; matrix products, arithmetic and copies ran while one was open for 7% -> 6% of each run, Pallas kernels for 8% -> 4%
where the time goes in v2:
time: 71.9 us; the launch traced here: 71.6 us
  waiting for transfers between devices  29.2 us (41%)
  starting transfers between devices  28.5 us (40%)
  Pallas kernels  6.23 us (9%)
  local copies, waits for them, and re-layouts  5.19 us (7%)
  other arithmetic  2.23 us (3%)
    ppermute x14, waiting for transfers between devices, hop(): lax.ppermute(x, 'frames', [(order[i], order[(i + by) % n]) for i in range...  21.2 us
    ppermute x4, starting transfers between devices, on_device_ring(): lax.ppermute(total.astype(jnp.bfloat16), ('frames', 'heads'), pairs)  12.9 us
    ppermute x14, starting transfers between devices, hop(): lax.ppermute(x, 'frames', [(order[i], order[(i + by) % n]) for i in range...  11.2 us
    ppermute x4, waiting for transfers between devices, on_device_ring(): lax.ppermute(total.astype(jnp.bfloat16), ('frames', 'heads'), pairs)  7.91 us
    pallas_call x2, Pallas kernels, attend(): pl.pallas_call(functools.partial(attend_kernel, width // HD, n), out_shap...  6.23 us
    ppermute x1, starting transfers between devices, on_device_ring(): lax.ppermute(given, 'heads', [(h, h // cores * cores + (h + 1) % cores) f...  4.51 us
    unnamed x18, local copies, waits for them, and re-layouts  4.24 us
  transfers between devices with their start and end apart: 19, of which 8 were waited for; matrix products, arithmetic and copies ran while one was open for 6% of the time, Pallas kernels for 4%

profile of v2, /device:TPU:1, one launch (start us, length us, event | category | flops | bytes accessed | tf_op | source)
XLA Modules:
  0.0 71.6 jit_solution(11442181463991411345)
XLA Ops:
  0.0 2.1 %collective-permute-start.7 = (bf16[2,96,640]{2,1,0:T(8,128)(2,1)}, bf16[2,96,640]{2,1,0:T(8,128)(2,1)S(1)}, u32[]{:S(2)}, u32[]{:S(2)}) collective-permute-start(bf16[2,96,640]{2,1,0:T(8,128)(2,1)} %param.4), channel_id=1, source_target_pairs={{0,8},{8,16},{16,24},{24,28},{28,20},{20,12},{12,4},{4,0},{1,9},{9... | collective-permute-start | bytes 737288 | tf_op jit(solution)/shard_map/ppermute | solution.py:86
  2.1 1.5 %collective-permute-start = (bf16[96,640]{1,0:T(8,128)(2,1)}, bf16[96,640]{1,0:T(8,128)(2,1)}, u32[]{:S(2)}, u32[]{:S(2)}) collective-permute-start(bf16[96,640]{1,0:T(8,128)(2,1)} %param.3), channel_id=1, source_target_pairs={{0,8},{8,16},{16,24},{24,28},{28,20},{20,12},{12,4},{4,0},{1,9},{9... | collective-permute-start | bytes 368648 | tf_op jit(solution)/shard_map/ppermute | solution.py:86
  3.6 1.0 %bitcast_dynamic-update-slice_fusion.7 = bf16[8,2,96,640]{3,2,1,0:T(8,128)(2,1)S(1)} fusion(bf16[2,96,640]{2,1,0:T(8,128)(2,1)} %param.4), kind=kLoop, calls=%fused_computation.9 | loop fusion | bytes 491520
  5.6 5.1 %collective-permute-done = bf16[96,640]{1,0:T(8,128)(2,1)} collective-permute-done((bf16[96,640]{1,0:T(8,128)(2,1)}, bf16[96,640]{1,0:T(8,128)(2,1)}, u32[]{:S(2)}, u32[]{:S(2)}) %collective-permute-start) | collective-permute-done | bytes 122912 | tf_op jit(solution)/shard_map/ppermute | solution.py:86
  10.7 1.2 %collective-permute-start.1 = (bf16[96,640]{1,0:T(8,128)(2,1)}, bf16[96,640]{1,0:T(8,128)(2,1)S(1)}, u32[]{:S(2)}, u32[]{:S(2)}) collective-permute-start(bf16[96,640]{1,0:T(8,128)(2,1)} %collective-permute-done), channel_id=1, source_target_pairs={{0,8},{8,16},{16,24},{24,28},{28,20},{20,12},{12,4},{4,0},{1,9},{9... | collective-permute-start | bytes 368648 | tf_op jit(solution)/shard_map/ppermute | solution.py:86
  12.2 0.9 %bitcast_dynamic-update-slice_fusion.14 = bf16[8,96,640]{2,1,0:T(8,128)(2,1)S(1)} fusion(bf16[8,96,640]{2,1,0:T(8,128)(2,1)S(1)} %bitcast_dynamic-update-slice_fusion.15, bf16[96,640]{1,0:T(8,128)(2,1)} %collective-permute-done), kind=kLoop, calls=%fused_computation.28 | loop fusion | bytes 245760
  13.1 1.3 %collective-permute-start.8 = (bf16[2,96,640]{2,1,0:T(8,128)(2,1)S(1)}, bf16[2,96,640]{2,1,0:T(8,128)(2,1)S(1)}, u32[]{:S(2)}, u32[]{:S(2)}) collective-permute-start(bf16[2,96,640]{2,1,0:T(8,128)(2,1)S(1)} %collective-permute-done.7), channel_id=1, source_target_pairs={{0,8},{8,16},{16,24},{24,28},{28,20},{20,12},{12,4},{4,0},{1,9},{9... | collective-permute-start | bytes 737288 | tf_op jit(solution)/shard_map/ppermute | solution.py:86
  14.7 1.3 %collective-permute-start.2 = (bf16[96,640]{1,0:T(8,128)(2,1)S(1)}, bf16[96,640]{1,0:T(8,128)(2,1)S(1)}, u32[]{:S(2)}, u32[]{:S(2)}) collective-permute-start(bf16[96,640]{1,0:T(8,128)(2,1)S(1)} %collective-permute-done.1), channel_id=1, source_target_pairs={{0,8},{8,16},{16,24},{24,28},{28,20},{20,12},{12,4},{4,0},{1,9},{9... | collective-permute-start | bytes 368648 | tf_op jit(solution)/shard_map/ppermute | solution.py:86
  16.3 6.7 %collective-permute-done.2 = bf16[96,640]{1,0:T(8,128)(2,1)S(1)} collective-permute-done((bf16[96,640]{1,0:T(8,128)(2,1)S(1)}, bf16[96,640]{1,0:T(8,128)(2,1)S(1)}, u32[]{:S(2)}, u32[]{:S(2)}) %collective-permute-start.2) | collective-permute-done | bytes 122912 | tf_op jit(solution)/shard_map/ppermute | solution.py:86
  23.0 1.5 %collective-permute-start.3 = (bf16[96,640]{1,0:T(8,128)(2,1)S(1)}, bf16[96,640]{1,0:T(8,128)(2,1)S(1)}, u32[]{:S(2)}, u32[]{:S(2)}) collective-permute-start(bf16[96,640]{1,0:T(8,128)(2,1)S(1)} %collective-permute-done.2), channel_id=1, source_target_pairs={{0,8},{8,16},{16,24},{24,28},{28,20},{20,12},{12,4},{4,0},{1,9},{9... | collective-permute-start | bytes 368648 | tf_op jit(solution)/shard_map/ppermute | solution.py:86
  24.5 1.3 %collective-permute-start.9 = (bf16[2,96,640]{2,1,0:T(8,128)(2,1)S(1)}, bf16[2,96,640]{2,1,0:T(8,128)(2,1)S(1)}, u32[]{:S(2)}, u32[]{:S(2)}) collective-permute-start(bf16[2,96,640]{2,1,0:T(8,128)(2,1)S(1)} %collective-permute-done.8), channel_id=1, source_target_pairs={{0,8},{8,16},{16,24},{24,28},{28,20},{20,12},{12,4},{4,0},{1,9},{9... | collective-permute-start | bytes 737288 | tf_op jit(solution)/shard_map/ppermute | solution.py:86
  26.8 4.4 %collective-permute-done.12 = bf16[2,96,640]{2,1,0:T(8,128)(2,1)S(1)} collective-permute-done((bf16[2,96,640]{2,1,0:T(8,128)(2,1)S(1)}, bf16[2,96,640]{2,1,0:T(8,128)(2,1)S(1)}, u32[]{:S(2)}, u32[]{:S(2)}) %collective-permute-start.12) | collective-permute-done | bytes 245792 | tf_op jit(solution)/shard_map/ppermute | solution.py:86
  32.4 4.2 %collective-permute-done.13 = bf16[2,96,640]{2,1,0:T(8,128)(2,1)S(1)} collective-permute-done((bf16[2,96,640]{2,1,0:T(8,128)(2,1)S(1)}, bf16[2,96,640]{2,1,0:T(8,128)(2,1)S(1)}, u32[]{:S(2)}, u32[]{:S(2)}) %collective-permute-start.13) | collective-permute-done | bytes 245792 | tf_op jit(solution)/shard_map/ppermute | solution.py:86
  36.7 3.1 %shard_map.38 = bf16[4,96,640]{2,1,0:T(8,128)(2,1)S(1)} custom-call(s32[2]{0:T(128)S(1)} %pad_add_fusion.1.at_ref, bf16[8,96,640]{2,1,0:T(8,128)(2,1)S(1)} %bitcast_dynamic-update-slice_fusion.8.q_ref, bf16[8,2,96,640]{3,2,1,0:T(8,128)(2,1)S(1)} %bitcast_dynamic-update-slice_fusion.kv_ref, bf16[640,640]{1,0:T(8,128)(2,1)S(1)} %copy-done), custom_call_target="tpu_custom_call" | custom-call | flops 1069547520 | bytes 3768320 | tf_op jit(solution)/shard_map/pallas_call | solution.py:145
  39.8 4.5 %collective-permute-start.14 = (bf16[4,96,640]{2,1,0:T(8,128)(2,1)S(1)}, bf16[4,96,640]{2,1,0:T(8,128)(2,1)}, u32[]{:S(2)}, u32[]{:S(2)}) collective-permute-start(bf16[4,96,640]{2,1,0:T(8,128)(2,1)S(1)} %shard_map.38), channel_id=1, source_target_pairs={{0,1},{1,0},{2,3},{3,2},{4,5},{5,4},{6,7},{7,6},{8,9},{9,8},{10,11... | collective-permute-start | bytes 1474568 | tf_op jit(solution)/shard_map/ppermute | solution.py:167
  44.4 1.1 %copy-done.1 = bf16[640,640]{1,0:T(8,128)(2,1)S(1)} copy-done((bf16[640,640]{1,0:T(8,128)(2,1)S(1)}, bf16[640,640]{1,0:T(8,128)(2,1)}, u32[]{:S(2)}) %copy-start.1) | copy-done | bytes 819224
  45.5 3.1 %shard_map.37 = f32[4,96,640]{2,1,0:T(8,128)S(1)} custom-call(s32[2]{0:T(128)S(1)} %pad_add_fusion.at_ref, bf16[8,96,640]{2,1,0:T(8,128)(2,1)S(1)} %bitcast_dynamic-update-slice_fusion.8.q_ref, bf16[8,2,96,640]{3,2,1,0:T(8,128)(2,1)S(1)} %bitcast_dynamic-update-slice_fusion.kv_ref, bf16[640,640]{1,0:T(8,128)(2,1)S(1)} %copy-done.1), custom_call_target="tpu_custom_call" | custom-call | flops 1069547520 | bytes 3768320 | tf_op jit(solution)/shard_map/pallas_call | solution.py:145
  48.7 1.2 %fusion = (bf16[96,640]{1,0:T(8,128)(2,1)S(1)}, bf16[96,640]{1,0:T(8,128)(2,1)S(1)}, bf16[96,640]{1,0:T(8,128)(2,1)S(1)}, bf16[96,640]{1,0:T(8,128)(2,1)S(1)}) fusion(f32[4,96,640]{2,1,0:T(8,128)S(1)} %shard_map.37, s32[]{:T(128)S(6)} %select_n.58, bf16[4,96,640]{2,1,0:T(8,128)(2,1)} %collective-permute-done.14, s32[]{:T(128)S(6)} %select_n.61, ...), kind=kLoop, calls=%fused_computation.16 | loop fusion | flops 737280 | bytes 1966096 | tf_op jit(solution)/shard_map/convert_element_type | solution.py:182
  49.9 2.0 %collective-permute-start.15 = (bf16[96,640]{1,0:T(8,128)(2,1)S(1)}, bf16[96,640]{1,0:T(8,128)(2,1)S(1)}, u32[]{:S(2)}, u32[]{:S(2)}) collective-permute-start(bf16[96,640]{1,0:T(8,128)(2,1)S(1)} %get-tuple-element.5), channel_id=1, source_target_pairs={{0,0},{1,4},{2,8},{3,12},{4,16},{5,20},{6,24},{7,28},{8,1},{9,5},{... | collective-permute-start | bytes 368648 | tf_op jit(solution)/shard_map/ppermute | solution.py:182
  51.9 3.7 %collective-permute-start.16 = (bf16[96,640]{1,0:T(8,128)(2,1)S(1)}, bf16[96,640]{1,0:T(8,128)(2,1)S(1)}, u32[]{:S(2)}, u32[]{:S(2)}) collective-permute-start(bf16[96,640]{1,0:T(8,128)(2,1)S(1)} %get-tuple-element.8), channel_id=1, source_target_pairs={{0,8},{1,12},{2,0},{3,4},{4,24},{5,28},{6,16},{7,20},{8,9},{9,13},... | collective-permute-start | bytes 368648 | tf_op jit(solution)/shard_map/ppermute | solution.py:182
  55.6 2.3 %collective-permute-start.17 = (bf16[96,640]{1,0:T(8,128)(2,1)S(1)}, bf16[96,640]{1,0:T(8,128)(2,1)S(1)}, u32[]{:S(2)}, u32[]{:S(2)}) collective-permute-start(bf16[96,640]{1,0:T(8,128)(2,1)S(1)} %get-tuple-element.7), channel_id=1, source_target_pairs={{0,16},{1,20},{2,24},{3,28},{4,0},{5,4},{6,8},{7,12},{8,17},{9,21}... | collective-permute-start | bytes 368648 | tf_op jit(solution)/shard_map/ppermute | solution.py:182
  57.9 4.8 %collective-permute-start.18 = (bf16[96,640]{1,0:T(8,128)(2,1)S(1)}, bf16[96,640]{1,0:T(8,128)(2,1)S(1)}, u32[]{:S(2)}, u32[]{:S(2)}) collective-permute-start(bf16[96,640]{1,0:T(8,128)(2,1)S(1)} %get-tuple-element.6), channel_id=1, source_target_pairs={{0,24},{1,28},{2,16},{3,20},{4,8},{5,12},{6,0},{7,4},{8,25},{9,29}... | collective-permute-start | bytes 368648 | tf_op jit(solution)/shard_map/ppermute | solution.py:182
  62.8 3.8 %collective-permute-done.17 = bf16[96,640]{1,0:T(8,128)(2,1)S(1)} collective-permute-done((bf16[96,640]{1,0:T(8,128)(2,1)S(1)}, bf16[96,640]{1,0:T(8,128)(2,1)S(1)}, u32[]{:S(2)}, u32[]{:S(2)}) %collective-permute-start.17) | collective-permute-done | bytes 122912 | tf_op jit(solution)/shard_map/ppermute | solution.py:182
  66.6 4.1 %collective-permute-done.18 = bf16[96,640]{1,0:T(8,128)(2,1)S(1)} collective-permute-done((bf16[96,640]{1,0:T(8,128)(2,1)S(1)}, bf16[96,640]{1,0:T(8,128)(2,1)S(1)}, u32[]{:S(2)}, u32[]{:S(2)}) %collective-permute-start.18) | collective-permute-done | bytes 122912 | tf_op jit(solution)/shard_map/ppermute | solution.py:182
  (42 shorter events, 5.0 us)
Async XLA Ops:
  0.0 13.1 %collective-permute-start.7 = (bf16[2,96,640]{2,1,0:T(8,128)(2,1)}, bf16[2,96,640]{2,1,0:T(8,128)(2,1)S(1)}, u32[]{:S(2)}, u32[]{:S(2)}) collective-permute-start(bf16[2,96,640]{2,1,0:T(8,128)(2,1)} %param.4), channel_id=1, source_target_pairs={{0,8},{8,16},{16,24},{24,28},{28,20},{20,12},{12,4},{4,0},{1,9},{9... | collective-permute-start | bytes 737288 | tf_op jit(solution)/shard_map/ppermute | solution.py:86
  2.1 12.2 %collective-permute-start.10 = (bf16[2,96,640]{2,1,0:T(8,128)(2,1)}, bf16[2,96,640]{2,1,0:T(8,128)(2,1)S(1)}, u32[]{:S(2)}, u32[]{:S(2)}) collective-permute-start(bf16[2,96,640]{2,1,0:T(8,128)(2,1)} %param.4), channel_id=1, source_target_pairs={{0,4},{8,0},{16,8},{24,16},{28,24},{20,28},{12,20},{4,12},{1,5},{9... | collective-permute-start | bytes 737288 | tf_op jit(solution)/shard_map/ppermute | solution.py:86
  2.1 8.6 %collective-permute-start = (bf16[96,640]{1,0:T(8,128)(2,1)}, bf16[96,640]{1,0:T(8,128)(2,1)}, u32[]{:S(2)}, u32[]{:S(2)}) collective-permute-start(bf16[96,640]{1,0:T(8,128)(2,1)} %param.3), channel_id=1, source_target_pairs={{0,8},{8,16},{16,24},{24,28},{28,20},{20,12},{12,4},{4,0},{1,9},{9... | collective-permute-start | bytes 368648 | tf_op jit(solution)/shard_map/ppermute | solution.py:86
  3.6 8.3 %collective-permute-start.4 = (bf16[96,640]{1,0:T(8,128)(2,1)}, bf16[96,640]{1,0:T(8,128)(2,1)}, u32[]{:S(2)}, u32[]{:S(2)}) collective-permute-start(bf16[96,640]{1,0:T(8,128)(2,1)} %param.3), channel_id=1, source_target_pairs={{0,4},{8,0},{16,8},{24,16},{28,24},{20,28},{12,20},{4,12},{1,5},{9... | collective-permute-start | bytes 368648 | tf_op jit(solution)/shard_map/ppermute | solution.py:86
  10.7 4.0 %collective-permute-start.1 = (bf16[96,640]{1,0:T(8,128)(2,1)}, bf16[96,640]{1,0:T(8,128)(2,1)S(1)}, u32[]{:S(2)}, u32[]{:S(2)}) collective-permute-start(bf16[96,640]{1,0:T(8,128)(2,1)} %collective-permute-done), channel_id=1, source_target_pairs={{0,8},{8,16},{16,24},{24,28},{28,20},{20,12},{12,4},{4,0},{1,9},{9... | collective-permute-start | bytes 368648 | tf_op jit(solution)/shard_map/ppermute | solution.py:86
  11.9 4.2 %collective-permute-start.5 = (bf16[96,640]{1,0:T(8,128)(2,1)}, bf16[96,640]{1,0:T(8,128)(2,1)S(1)}, u32[]{:S(2)}, u32[]{:S(2)}) collective-permute-start(bf16[96,640]{1,0:T(8,128)(2,1)} %collective-permute-done.4), channel_id=1, source_target_pairs={{0,4},{8,0},{16,8},{24,16},{28,24},{20,28},{12,20},{4,12},{1,5},{9... | collective-permute-start | bytes 368648 | tf_op jit(solution)/shard_map/ppermute | solution.py:86
  13.1 11.4 %collective-permute-start.8 = (bf16[2,96,640]{2,1,0:T(8,128)(2,1)S(1)}, bf16[2,96,640]{2,1,0:T(8,128)(2,1)S(1)}, u32[]{:S(2)}, u32[]{:S(2)}) collective-permute-start(bf16[2,96,640]{2,1,0:T(8,128)(2,1)S(1)} %collective-permute-done.7), channel_id=1, source_target_pairs={{0,8},{8,16},{16,24},{24,28},{28,20},{20,12},{12,4},{4,0},{1,9},{9... | collective-permute-start | bytes 737288 | tf_op jit(solution)/shard_map/ppermute | solution.py:86
  14.4 11.5 %collective-permute-start.11 = (bf16[2,96,640]{2,1,0:T(8,128)(2,1)S(1)}, bf16[2,96,640]{2,1,0:T(8,128)(2,1)S(1)}, u32[]{:S(2)}, u32[]{:S(2)}) collective-permute-start(bf16[2,96,640]{2,1,0:T(8,128)(2,1)S(1)} %collective-permute-done.10), channel_id=1, source_target_pairs={{0,4},{8,0},{16,8},{24,16},{28,24},{20,28},{12,20},{4,12},{1,5},{9... | collective-permute-start | bytes 737288 | tf_op jit(solution)/shard_map/ppermute | solution.py:86
  14.7 8.3 %collective-permute-start.2 = (bf16[96,640]{1,0:T(8,128)(2,1)S(1)}, bf16[96,640]{1,0:T(8,128)(2,1)S(1)}, u32[]{:S(2)}, u32[]{:S(2)}) collective-permute-start(bf16[96,640]{1,0:T(8,128)(2,1)S(1)} %collective-permute-done.1), channel_id=1, source_target_pairs={{0,8},{8,16},{16,24},{24,28},{28,20},{20,12},{12,4},{4,0},{1,9},{9... | collective-permute-start | bytes 368648 | tf_op jit(solution)/shard_map/ppermute | solution.py:86
  16.1 10.6 %collective-permute-start.6 = (bf16[96,640]{1,0:T(8,128)(2,1)S(1)}, bf16[96,640]{1,0:T(8,128)(2,1)S(1)}, u32[]{:S(2)}, u32[]{:S(2)}) collective-permute-start(bf16[96,640]{1,0:T(8,128)(2,1)S(1)} %collective-permute-done.5), channel_id=1, source_target_pairs={{0,4},{8,0},{16,8},{24,16},{28,24},{20,28},{12,20},{4,12},{1,5},{9... | collective-permute-start | bytes 368648 | tf_op jit(solution)/shard_map/ppermute | solution.py:86
  23.0 3.7 %collective-permute-start.3 = (bf16[96,640]{1,0:T(8,128)(2,1)S(1)}, bf16[96,640]{1,0:T(8,128)(2,1)S(1)}, u32[]{:S(2)}, u32[]{:S(2)}) collective-permute-start(bf16[96,640]{1,0:T(8,128)(2,1)S(1)} %collective-permute-done.2), channel_id=1, source_target_pairs={{0,8},{8,16},{16,24},{24,28},{28,20},{20,12},{12,4},{4,0},{1,9},{9... | collective-permute-start | bytes 368648 | tf_op jit(solution)/shard_map/ppermute | solution.py:86
  24.5 12.2 %copy-start = (bf16[640,640]{1,0:T(8,128)(2,1)S(1)}, bf16[640,640]{1,0:T(8,128)(2,1)}, u32[]{:S(2)}) copy-start(bf16[640,640]{1,0:T(8,128)(2,1)} %w_ref.3) | copy-start | bytes 2457604
  24.5 7.8 %collective-permute-start.9 = (bf16[2,96,640]{2,1,0:T(8,128)(2,1)S(1)}, bf16[2,96,640]{2,1,0:T(8,128)(2,1)S(1)}, u32[]{:S(2)}, u32[]{:S(2)}) collective-permute-start(bf16[2,96,640]{2,1,0:T(8,128)(2,1)S(1)} %collective-permute-done.8), channel_id=1, source_target_pairs={{0,8},{8,16},{16,24},{24,28},{28,20},{20,12},{12,4},{4,0},{1,9},{9... | collective-permute-start | bytes 737288 | tf_op jit(solution)/shard_map/ppermute | solution.py:86
  25.9 5.3 %collective-permute-start.12 = (bf16[2,96,640]{2,1,0:T(8,128)(2,1)S(1)}, bf16[2,96,640]{2,1,0:T(8,128)(2,1)S(1)}, u32[]{:S(2)}, u32[]{:S(2)}) collective-permute-start(bf16[2,96,640]{2,1,0:T(8,128)(2,1)S(1)} %collective-permute-done.11), channel_id=1, source_target_pairs={{0,4},{8,0},{16,8},{24,16},{28,24},{20,28},{12,20},{4,12},{1,5},{9... | collective-permute-start | bytes 737288 | tf_op jit(solution)/shard_map/ppermute | solution.py:86
  31.2 5.3 %collective-permute-start.13 = (bf16[2,96,640]{2,1,0:T(8,128)(2,1)S(1)}, bf16[2,96,640]{2,1,0:T(8,128)(2,1)S(1)}, u32[]{:S(2)}, u32[]{:S(2)}) collective-permute-start(bf16[2,96,640]{2,1,0:T(8,128)(2,1)S(1)} %collective-permute-done.12), channel_id=1, source_target_pairs={{0,4},{8,0},{16,8},{24,16},{28,24},{20,28},{12,20},{4,12},{1,5},{9... | collective-permute-start | bytes 737288 | tf_op jit(solution)/shard_map/ppermute | solution.py:86
  39.8 8.9 %collective-permute-start.14 = (bf16[4,96,640]{2,1,0:T(8,128)(2,1)S(1)}, bf16[4,96,640]{2,1,0:T(8,128)(2,1)}, u32[]{:S(2)}, u32[]{:S(2)}) collective-permute-start(bf16[4,96,640]{2,1,0:T(8,128)(2,1)S(1)} %shard_map.38), channel_id=1, source_target_pairs={{0,1},{1,0},{2,3},{3,2},{4,5},{5,4},{6,7},{7,6},{8,9},{9,8},{10,11... | collective-permute-start | bytes 1474568 | tf_op jit(solution)/shard_map/ppermute | solution.py:167
  44.4 1.1 %copy-start.1 = (bf16[640,640]{1,0:T(8,128)(2,1)S(1)}, bf16[640,640]{1,0:T(8,128)(2,1)}, u32[]{:S(2)}) copy-start(bf16[640,640]{1,0:T(8,128)(2,1)} %w_ref.3) | copy-start | bytes 2457604
  49.9 12.9 %collective-permute-start.15 = (bf16[96,640]{1,0:T(8,128)(2,1)S(1)}, bf16[96,640]{1,0:T(8,128)(2,1)S(1)}, u32[]{:S(2)}, u32[]{:S(2)}) collective-permute-start(bf16[96,640]{1,0:T(8,128)(2,1)S(1)} %get-tuple-element.5), channel_id=1, source_target_pairs={{0,0},{1,4},{2,8},{3,12},{4,16},{5,20},{6,24},{7,28},{8,1},{9,5},{... | collective-permute-start | bytes 368648 | tf_op jit(solution)/shard_map/ppermute | solution.py:182
  51.9 10.9 %collective-permute-start.16 = (bf16[96,640]{1,0:T(8,128)(2,1)S(1)}, bf16[96,640]{1,0:T(8,128)(2,1)S(1)}, u32[]{:S(2)}, u32[]{:S(2)}) collective-permute-start(bf16[96,640]{1,0:T(8,128)(2,1)S(1)} %get-tuple-element.8), channel_id=1, source_target_pairs={{0,8},{1,12},{2,0},{3,4},{4,24},{5,28},{6,16},{7,20},{8,9},{9,13},... | collective-permute-start | bytes 368648 | tf_op jit(solution)/shard_map/ppermute | solution.py:182
  55.6 11.0 %collective-permute-start.17 = (bf16[96,640]{1,0:T(8,128)(2,1)S(1)}, bf16[96,640]{1,0:T(8,128)(2,1)S(1)}, u32[]{:S(2)}, u32[]{:S(2)}) collective-permute-start(bf16[96,640]{1,0:T(8,128)(2,1)S(1)} %get-tuple-element.7), channel_id=1, source_target_pairs={{0,16},{1,20},{2,24},{3,28},{4,0},{5,4},{6,8},{7,12},{8,17},{9,21}... | collective-permute-start | bytes 368648 | tf_op jit(solution)/shard_map/ppermute | solution.py:182
  57.9 12.8 %collective-permute-start.18 = (bf16[96,640]{1,0:T(8,128)(2,1)S(1)}, bf16[96,640]{1,0:T(8,128)(2,1)S(1)}, u32[]{:S(2)}, u32[]{:S(2)}) collective-permute-start(bf16[96,640]{1,0:T(8,128)(2,1)S(1)} %get-tuple-element.6), channel_id=1, source_target_pairs={{0,24},{1,28},{2,16},{3,20},{4,8},{5,12},{6,0},{7,4},{8,25},{9,29}... | collective-permute-start | bytes 368648 | tf_op jit(solution)/shard_map/ppermute | solution.py:182

commit v3 on v0

--- a/solution.py
+++ b/solution.py
@@ -1,11 +1,17 @@
+import functools
+import math
+
 import jax
 import jax.numpy as jnp
 from jax import lax
+from jax.experimental import pallas as pl
+from jax.experimental.pallas import tpu as pltpu
 from jax.sharding import PartitionSpec as P
 
 HD = 128
 TPF = 32
 FR_DEV = 3
+ROWS = FR_DEV * TPF
 
 
 reach_cap = 32
@@ -16,7 +22,7 @@
     return lax.ppermute(x, axis, [(i, (i + by) % devices) for i in range(devices)])
 
 
-def on_device(queries, keys_values, out_weight):
+def on_device_band(queries, keys_values, out_weight):
     total_frames = lax.axis_size("frames") * FR_DEV
     reach = min(reach_cap, (total_frames - 1) // 2)
     steps = (reach + FR_DEV - 1) // FR_DEV
@@ -67,9 +73,153 @@
     )
 
 
+def ring_order(n):
+    return list(range(0, n, 2)) + list(range(n - 1, 0, -2))
+
+
+def ring_place(f, n):
+    return (f >> 1) + (f & 1) * (n - 1 - (f >> 1) * 2)
+
+
+def hop(x, n, by):
+    order = ring_order(n)
+    return lax.ppermute(x, "frames", [(order[i], order[(i + by) % n]) for i in range(n)])
+
+
+def gather_ring(streams, n):
+    found = [[block] + [None] * (n - 1) for block in streams]
+    for step in range(1, n // 2 + 1):
+        for j, blocks in enumerate(found):
+            for by in (1, -1):
+                if step < n // 2 or (j == 0) == (by == 1):
+                    blocks[by * step % n] = hop(blocks[by * (step - 1) % n], n, by)
+    return found
+
+
+def pick(options, index):
+    low = jnp.where(index & 1 == 0, options[0], options[1])
+    high = jnp.where(index & 1 == 0, options[2], options[3])
+    return jnp.where(index & 2 == 0, low, high)
+
+
+def attend_kernel(heads, n, flip, at_ref, *refs):
+    first, second, w_ref, out_ref = refs[:n], refs[n : 2 * n], refs[2 * n], refs[-1]
+    place, at = at_ref[0], at_ref[1] ^ flip
+    count = n // 4
+    half = ROWS // 2
+    scale = HD ** (-0.5) * math.log2(math.e)
+    two = jnp.where((place - at + n) & 2 == 0, n - 2, 2)
+    away = [FR_DEV * ((at + 4 * i + two) & (n - 1)) for i in range(count)]
+    lane_frame = lax.broadcasted_iota(jnp.int32, (TPF, HD), 1) // TPF
+    ones = jnp.ones((n * ROWS, HD), jnp.bfloat16)
+    attended = []
+    for head in range(heads):
+        cols = slice(head * HD, (head + 1) * HD)
+        rows = jnp.concatenate(
+            [
+                pick([half_ref[ROWS:, cols] for half_ref in part[4 * i : 4 * i + 4]], at)
+                for i in range(count)
+                for part in (first, second)
+            ],
+            axis=0,
+        )
+        keys = jnp.concatenate([ref[:ROWS, cols] for ref in first], axis=0)
+        values = jnp.concatenate([ref[:ROWS, cols] for ref in second], axis=0)
+        scores = lax.dot_general(rows, keys, (((1,), (1,)), ((), ())), preferred_element_type=jnp.float32)
+        groups = []
+        for g in range(count * FR_DEV):
+            out_frame = away[g // FR_DEV] + g % FR_DEV
+            parts = []
+            for c in range(0, n * ROWS, HD):
+                part = scores[g * TPF : (g + 1) * TPF, c : c + HD]
+                parts.append(jnp.where(lane_frame == out_frame - c // TPF, -1e30, part))
+            top = jnp.max(functools.reduce(jnp.maximum, parts), axis=1, keepdims=True)
+            groups.append(
+                jnp.concatenate([jnp.exp2((p - top) * scale).astype(jnp.bfloat16) for p in parts], axis=1)
+            )
+        weights = jnp.concatenate(groups, axis=0)
+        mixed = jnp.dot(weights, jnp.concatenate([values, ones], axis=1), preferred_element_type=jnp.float32)
+        attended.append((mixed[:, :HD] / mixed[:, HD:]).astype(jnp.bfloat16))
+    result = jnp.dot(jnp.concatenate(attended, axis=1), w_ref[...], preferred_element_type=jnp.float32)
+    for i in range(count):
+        out_ref[i] = result[i * ROWS : (i + 1) * ROWS].astype(out_ref.dtype)
+
+
+def attend(where, flip, found, out_weight, out_dtype, after=()):
+    n = len(found[0])
+    count = n // 4
+    width, cols = out_weight.shape
+    vmem = pl.BlockSpec(memory_space=pltpu.VMEM)
+    return pl.pallas_call(
+        functools.partial(attend_kernel, width // HD, n, flip),
+        out_shape=jax.ShapeDtypeStruct((count, ROWS, cols), out_dtype),
+        in_specs=[pl.BlockSpec(memory_space=pltpu.SMEM)]
+        + [vmem] * (2 * n + 1)
+        + [pl.BlockSpec(memory_space=pl.ANY)] * len(after),
+        out_specs=vmem,
+        compiler_params=pltpu.CompilerParams(vmem_limit_bytes=16 * 1024 * 1024),
+        cost_estimate=pl.CostEstimate(
+            flops=count * ROWS * width * (4 * n * ROWS + 2 * cols),
+            bytes_accessed=2 * (3 * n * ROWS * width + out_weight.size),
+            transcendentals=count * ROWS * n * ROWS * (width // HD),
+        ),
+    )(where, *found[0], *found[1], out_weight, *after)
+
+
+def on_device_ring(queries, keys_values, out_weight):
+    n = lax.axis_size("frames")
+    frame, head = lax.axis_index("frames"), lax.axis_index("heads")
+    where = jnp.stack([ring_place(frame, n), head]).astype(jnp.int32)
+    half = ROWS // 2
+    streams = [
+        jnp.concatenate([keys_values[0], queries[:half]], axis=0),
+        jnp.concatenate([keys_values[1], queries[half:]], axis=0),
+    ]
+    found = gather_ring(streams, n)
+    to_core = [(h, h ^ 1) for h in range(4)]
+    to_x = [(h, h ^ 2) for h in range(4)]
+    f32 = jnp.float32
+    from_core = lax.ppermute(attend(where, 3, found, out_weight, jnp.bfloat16), "heads", to_core)
+    given = attend(where, 2, found, out_weight, f32)
+    given = (given + from_core.astype(f32)).astype(jnp.bfloat16)
+    from_x = lax.ppermute(given, "heads", to_x)
+    last_given = attend(where, 1, found, out_weight, jnp.bfloat16, (given,))
+    from_core = lax.ppermute(last_given, "heads", to_core)
+    kept = attend(where, 0, found, out_weight, f32, (last_given,))
+    order = ring_order(n)
+    z, y = frame >> 1, frame & 1
+
+    def flip(z, y, head):
+        return y & (1 ^ ((head + 2 * z + 1) >> 2 & 1))
+
+    arrived = []
+    for slot in range(2):
+        pairs = []
+        for f in range(n):
+            for h in range(4):
+                distance = 4 * (slot ^ flip(f >> 1, f & 1, h)) + h
+                owner = order[(ring_place(f, n) - distance) % n]
+                pairs.append((f * 4 + h, owner * 4 + f // 2))
+        j = slot ^ flip(z, y, head)
+        total = kept[j] + from_core[j].astype(f32) + from_x[j].astype(f32)
+        arrived.append(lax.ppermute(total.astype(jnp.bfloat16), ("frames", "heads"), pairs))
+    straight = (head - where[0]) & 4 == 0
+    return jnp.concatenate(
+        [jnp.where(straight, arrived[0], arrived[1]), jnp.where(straight, arrived[1], arrived[0])], axis=1
+    )
+
+
 def solution(mesh):
     in_specs = (P("frames", "heads"), P(None, "frames", "heads"), P("heads", "frames"))
     out_specs = P("frames", "heads")
+    n, heads = mesh.shape["frames"], mesh.shape["heads"]
+    total_frames = n * FR_DEV
+    reach = min(reach_cap, (total_frames - 1) // 2)
+    every = total_frames == 2 * reach + 2 and heads == 4 and n == 2 * heads
     return jax.shard_map(
-        on_device, mesh=mesh, in_specs=in_specs, out_specs=out_specs, check_vma=False
-    )
+        on_device_ring if every else on_device_band,
+        mesh=mesh,
+        in_specs=in_specs,
+        out_specs=out_specs,
+        check_vma=False,
+    )

time: 178 us -> 67.4 us (0.38); the launches traced: 175 us -> 67.1 us
  waiting for transfers between devices: 143 us -> 32.3 us
  between operations: 13.6 us -> 0.11 us
  Pallas kernels: 0 us -> 11.2 us
  starting transfers between devices: 8.84 us -> 19.7 us
  matrix products: 8.09 us -> 0 us
  other arithmetic: 0.41 us -> 2.78 us
    all_gather x1 -> x0, waiting for transfers between devices: 57.4 us -> none  [on_device(): lax.all_gather(out_weight, 'frames', axis=1, tiled=True)]
    ppermute x7 -> x19, waiting for transfers between devices: 62.5 us -> 32.3 us  [the longest x14 19.9 us: hop(): lax.ppermute(x, 'frames', [(order[i], order[(i + by) % n]) for i in range...]
    reduce_scatter x1 -> x0, waiting for transfers between devices: 22.6 us -> none  [on_device(): lax.psum_scatter(partial_rows.astype(jnp.bfloat16), 'heads', scatter_dime...]
    pallas_call x0 -> x4, Pallas kernels: none -> 11.2 us  [attend(): pl.pallas_call(functools.partial(attend_kernel, width // HD, n, flip), ou...]
    ppermute x7 -> x19, starting transfers between devices: 8.8 us -> 19.7 us  [the longest x14 10.4 us: hop(): lax.ppermute(x, 'frames', [(order[i], order[(i + by) % n]) for i in range...]
    dot_general x11 -> x0, matrix products: 8.09 us -> none  [the longest x1 5.09 us: on_device(): jnp.dot(attended, lax.all_gather(out_weight, 'frames', axis=1, tiled=True...]
    convert_element_type x0 -> x2, other arithmetic: none -> 1.92 us  [the longest x1 1.17 us: on_device_ring(): total.astype(jnp.bfloat16)]
  transfers between devices with their start and end apart: 9 -> 19, of which waited for: 5 -> 11; matrix products, arithmetic and copies ran while one was open for 2% -> 0% of each run, Pallas kernels for 0% -> 8%
where the time goes in v3:
time: 67.4 us; the launch traced here: 67.1 us
  waiting for transfers between devices  32.3 us (48%)
  starting transfers between devices  19.7 us (29%)
  Pallas kernels  11.2 us (17%)
  other arithmetic  2.78 us (4%)
  local copies, waits for them, and re-layouts  1.02 us (2%)
    ppermute x14, waiting for transfers between devices, hop(): lax.ppermute(x, 'frames', [(order[i], order[(i + by) % n]) for i in range...  19.9 us
    pallas_call x4, Pallas kernels, attend(): pl.pallas_call(functools.partial(attend_kernel, width // HD, n, flip), ou...  11.2 us
    ppermute x14, starting transfers between devices, hop(): lax.ppermute(x, 'frames', [(order[i], order[(i + by) % n]) for i in range...  10.4 us
    ppermute x2, waiting for transfers between devices, on_device_ring(): lax.ppermute(total.astype(jnp.bfloat16), ('frames', 'heads'), pairs)  7.86 us
    ppermute x2, starting transfers between devices, on_device_ring(): lax.ppermute(total.astype(jnp.bfloat16), ('frames', 'heads'), pairs)  7.15 us
    ppermute x1, waiting for transfers between devices, on_device_ring(): from_x = lax.ppermute(given, 'heads', to_x)  4.47 us
    ppermute x1, starting transfers between devices, on_device_ring(): lax.ppermute(attend(where, 3, found, out_weight, jnp.bfloat16), 'heads',...  1.93 us
  transfers between devices with their start and end apart: 19, of which 11 were waited for; matrix products, arithmetic and copies ran while one was open for 0% of the time, Pallas kernels for 8%

profile of v3, /device:TPU:3, one launch (start us, length us, event | category | flops | bytes accessed | tf_op | source)
XLA Modules:
  0.0 67.1 jit_solution(15029774941692268046)
XLA Ops:
  1.1 1.3 %collective-permute-start = (bf16[144,640]{1,0:T(8,128)(2,1)S(1)}, bf16[144,640]{1,0:T(8,128)(2,1)S(1)}, u32[]{:S(2)}, u32[]{:S(2)}) collective-permute-start(bf16[144,640]{1,0:T(8,128)(2,1)S(1)} %pad_maximum_fusion.1.refs_0_), channel_id=1, source_target_pairs={{0,8},{8,16},{16,24},{24,28},{28,20},{20,12},{12,4},{4,0},{1,9},{9... | collective-permute-start | bytes 552968 | tf_op jit(solution)/shard_map/ppermute | solution.py:86
  2.6 1.2 %collective-permute-start.4 = (bf16[144,640]{1,0:T(8,128)(2,1)S(1)}, bf16[144,640]{1,0:T(8,128)(2,1)S(1)}, u32[]{:S(2)}, u32[]{:S(2)}) collective-permute-start(bf16[144,640]{1,0:T(8,128)(2,1)S(1)} %pad_maximum_fusion.1.refs_0_), channel_id=1, source_target_pairs={{0,4},{8,0},{16,8},{24,16},{28,24},{20,28},{12,20},{4,12},{1,5},{9... | collective-permute-start | bytes 552968 | tf_op jit(solution)/shard_map/ppermute | solution.py:86
  4.1 2.5 %collective-permute-done.refs_1_ = bf16[144,640]{1,0:T(8,128)(2,1)S(1)} collective-permute-done((bf16[144,640]{1,0:T(8,128)(2,1)S(1)}, bf16[144,640]{1,0:T(8,128)(2,1)S(1)}, u32[]{:S(2)}, u32[]{:S(2)}) %collective-permute-start) | collective-permute-done | bytes 184352 | tf_op jit(solution)/shard_map/ppermute | solution.py:86
  6.6 1.3 %collective-permute-start.1 = (bf16[144,640]{1,0:T(8,128)(2,1)S(1)}, bf16[144,640]{1,0:T(8,128)(2,1)S(1)}, u32[]{:S(2)}, u32[]{:S(2)}) collective-permute-start(bf16[144,640]{1,0:T(8,128)(2,1)S(1)} %collective-permute-done.refs_1_), channel_id=1, source_target_pairs={{0,8},{8,16},{16,24},{24,28},{28,20},{20,12},{12,4},{4,0},{1,9},{9... | collective-permute-start | bytes 552968 | tf_op jit(solution)/shard_map/ppermute | solution.py:86
  8.1 3.5 %collective-permute-done.4.refs_7_ = bf16[144,640]{1,0:T(8,128)(2,1)S(1)} collective-permute-done((bf16[144,640]{1,0:T(8,128)(2,1)S(1)}, bf16[144,640]{1,0:T(8,128)(2,1)S(1)}, u32[]{:S(2)}, u32[]{:S(2)}) %collective-permute-start.4) | collective-permute-done | bytes 184352 | tf_op jit(solution)/shard_map/ppermute | solution.py:86
  11.8 1.3 %collective-permute-start.8 = (bf16[144,640]{1,0:T(8,128)(2,1)S(1)}, bf16[144,640]{1,0:T(8,128)(2,1)S(1)}, u32[]{:S(2)}, u32[]{:S(2)}) collective-permute-start(bf16[144,640]{1,0:T(8,128)(2,1)S(1)} %collective-permute-done.7.refs_9_), channel_id=1, source_target_pairs={{0,8},{8,16},{16,24},{24,28},{28,20},{20,12},{12,4},{4,0},{1,9},{9... | collective-permute-start | bytes 552968 | tf_op jit(solution)/shard_map/ppermute | solution.py:86
  13.1 1.4 %collective-permute-done.1.refs_2_ = bf16[144,640]{1,0:T(8,128)(2,1)S(1)} collective-permute-done((bf16[144,640]{1,0:T(8,128)(2,1)S(1)}, bf16[144,640]{1,0:T(8,128)(2,1)S(1)}, u32[]{:S(2)}, u32[]{:S(2)}) %collective-permute-start.1) | collective-permute-done | bytes 184352 | tf_op jit(solution)/shard_map/ppermute | solution.py:86
  14.5 1.3 %collective-permute-start.2 = (bf16[144,640]{1,0:T(8,128)(2,1)S(1)}, bf16[144,640]{1,0:T(8,128)(2,1)S(1)}, u32[]{:S(2)}, u32[]{:S(2)}) collective-permute-start(bf16[144,640]{1,0:T(8,128)(2,1)S(1)} %collective-permute-done.1.refs_2_), channel_id=1, source_target_pairs={{0,8},{8,16},{16,24},{24,28},{28,20},{20,12},{12,4},{4,0},{1,9},{9... | collective-permute-start | bytes 552968 | tf_op jit(solution)/shard_map/ppermute | solution.py:86
  16.0 3.5 %collective-permute-done.5.refs_6_ = bf16[144,640]{1,0:T(8,128)(2,1)S(1)} collective-permute-done((bf16[144,640]{1,0:T(8,128)(2,1)S(1)}, bf16[144,640]{1,0:T(8,128)(2,1)S(1)}, u32[]{:S(2)}, u32[]{:S(2)}) %collective-permute-start.5) | collective-permute-done | bytes 184352 | tf_op jit(solution)/shard_map/ppermute | solution.py:86
  19.7 1.3 %collective-permute-start.9 = (bf16[144,640]{1,0:T(8,128)(2,1)S(1)}, bf16[144,640]{1,0:T(8,128)(2,1)S(1)}, u32[]{:S(2)}, u32[]{:S(2)}) collective-permute-start(bf16[144,640]{1,0:T(8,128)(2,1)S(1)} %collective-permute-done.8.refs_10_), channel_id=1, source_target_pairs={{0,8},{8,16},{16,24},{24,28},{28,20},{20,12},{12,4},{4,0},{1,9},{9... | collective-permute-start | bytes 552968 | tf_op jit(solution)/shard_map/ppermute | solution.py:86
  21.0 1.3 %collective-permute-start.3 = (bf16[144,640]{1,0:T(8,128)(2,1)S(1)}, bf16[144,640]{1,0:T(8,128)(2,1)}, u32[]{:S(2)}, u32[]{:S(2)}) collective-permute-start(bf16[144,640]{1,0:T(8,128)(2,1)S(1)} %collective-permute-done.2.refs_3_), channel_id=1, source_target_pairs={{0,8},{8,16},{16,24},{24,28},{28,20},{20,12},{12,4},{4,0},{1,9},{9... | collective-permute-start | bytes 552968 | tf_op jit(solution)/shard_map/ppermute | solution.py:86
  22.3 1.2 %collective-permute-done.12.refs_13_ = bf16[144,640]{1,0:T(8,128)(2,1)S(1)} collective-permute-done((bf16[144,640]{1,0:T(8,128)(2,1)S(1)}, bf16[144,640]{1,0:T(8,128)(2,1)S(1)}, u32[]{:S(2)}, u32[]{:S(2)}) %collective-permute-start.12) | collective-permute-done | bytes 184352 | tf_op jit(solution)/shard_map/ppermute | solution.py:86
  23.7 3.7 %collective-permute-done.6.refs_5_ = bf16[144,640]{1,0:T(8,128)(2,1)S(1)} collective-permute-done((bf16[144,640]{1,0:T(8,128)(2,1)S(1)}, bf16[144,640]{1,0:T(8,128)(2,1)S(1)}, u32[]{:S(2)}, u32[]{:S(2)}) %collective-permute-start.6) | collective-permute-done | bytes 184352 | tf_op jit(solution)/shard_map/ppermute | solution.py:86
  28.5 3.0 %collective-permute-done.13.refs_12_ = bf16[144,640]{1,0:T(8,128)(2,1)} collective-permute-done((bf16[144,640]{1,0:T(8,128)(2,1)S(1)}, bf16[144,640]{1,0:T(8,128)(2,1)}, u32[]{:S(2)}, u32[]{:S(2)}) %collective-permute-start.13) | collective-permute-done | bytes 184352 | tf_op jit(solution)/shard_map/ppermute | solution.py:86
  31.5 2.6 %shard_map.38 = bf16[2,96,640]{2,1,0:T(8,128)(2,1)S(1)} custom-call(s32[2]{0:T(128)S(1)} %pad_add_fusion.at_ref, bf16[144,640]{1,0:T(8,128)(2,1)S(1)} %pad_maximum_fusion.1.refs_0_, bf16[144,640]{1,0:T(8,128)(2,1)S(1)} %collective-permute-done.refs_1_, bf16[144,640]{1,0:T(8,128)(2,1)S(1)} %collective-permute-done.1.refs_2_, ...), custom_call_target="tpu_custom_call" | custom-call | flops 534773760 | bytes 3768320 | tf_op jit(solution)/shard_map/pallas_call | solution.py:153
  34.1 1.9 %collective-permute-start.14 = (bf16[2,96,640]{2,1,0:T(8,128)(2,1)S(1)}, bf16[2,96,640]{2,1,0:T(8,128)(2,1)S(1)}, u32[]{:S(2)}, u32[]{:S(2)}) collective-permute-start(bf16[2,96,640]{2,1,0:T(8,128)(2,1)S(1)} %shard_map.38), channel_id=1, source_target_pairs={{0,1},{1,0},{2,3},{3,2},{4,5},{5,4},{6,7},{7,6},{8,9},{9,8},{10,11... | collective-permute-start | bytes 737288 | tf_op jit(solution)/shard_map/ppermute | solution.py:182
  36.0 2.6 %shard_map.37 = f32[2,96,640]{2,1,0:T(8,128)S(1)} custom-call(s32[2]{0:T(128)S(1)} %pad_add_fusion.at_ref, bf16[144,640]{1,0:T(8,128)(2,1)S(1)} %pad_maximum_fusion.1.refs_0_, bf16[144,640]{1,0:T(8,128)(2,1)S(1)} %collective-permute-done.refs_1_, bf16[144,640]{1,0:T(8,128)(2,1)S(1)} %collective-permute-done.1.refs_2_, ...), custom_call_target="tpu_custom_call" | custom-call | flops 534773760 | bytes 3768320 | tf_op jit(solution)/shard_map/pallas_call | solution.py:153
  39.4 3.3 %shard_map.39.refs_17_ = bf16[2,96,640]{2,1,0:T(8,128)(2,1)} custom-call(s32[2]{0:T(128)S(1)} %pad_add_fusion.at_ref, bf16[144,640]{1,0:T(8,128)(2,1)S(1)} %pad_maximum_fusion.1.refs_0_, bf16[144,640]{1,0:T(8,128)(2,1)S(1)} %collective-permute-done.refs_1_, bf16[144,640]{1,0:T(8,128)(2,1)S(1)} %collective-permute-done.1.refs_2_, ...), custom_call_target="tpu_custom_call" | custom-call | flops 534773760 | bytes 3768320 | tf_op jit(solution)/shard_map/pallas_call | solution.py:153
  43.0 2.6 %shard_map.40 = f32[2,96,640]{2,1,0:T(8,128)S(1)} custom-call(s32[2]{0:T(128)S(1)} %pad_add_fusion.at_ref, bf16[144,640]{1,0:T(8,128)(2,1)S(1)} %pad_maximum_fusion.1.refs_0_, bf16[144,640]{1,0:T(8,128)(2,1)S(1)} %collective-permute-done.refs_1_, bf16[144,640]{1,0:T(8,128)(2,1)S(1)} %collective-permute-done.1.refs_2_, ...), custom_call_target="tpu_custom_call" | custom-call | flops 534773760 | bytes 3768320 | tf_op jit(solution)/shard_map/pallas_call | solution.py:153
  45.7 4.5 %collective-permute-done.16 = bf16[2,96,640]{2,1,0:T(8,128)(2,1)} collective-permute-done((bf16[2,96,640]{2,1,0:T(8,128)(2,1)}, bf16[2,96,640]{2,1,0:T(8,128)(2,1)}, u32[]{:S(2)}, u32[]{:S(2)}) %collective-permute-start.16) | collective-permute-done | bytes 245792 | tf_op jit(solution)/shard_map/ppermute | solution.py:185
  50.1 1.2 %fusion = (bf16[96,640]{1,0:T(8,128)(2,1)S(1)}, bf16[96,640]{1,0:T(8,128)(2,1)S(1)}) fusion(f32[2,96,640]{2,1,0:T(8,128)S(1)} %shard_map.40, s32[]{:T(128)S(6)} %select_n.23, bf16[2,96,640]{2,1,0:T(8,128)(2,1)} %collective-permute-done.16, bf16[2,96,640]{2,1,0:T(8,128)(2,1)} %collective-permute-done.15, s32[]{:T(128)S(6)} %select_n.24), kind=kLoop, calls=%fused_computation.6 | loop fusion | flops 614400 | bytes 1228808 | tf_op jit(solution)/shard_map/convert_element_type | solution.py:205
  51.3 5.2 %collective-permute-start.17 = (bf16[96,640]{1,0:T(8,128)(2,1)S(1)}, bf16[96,640]{1,0:T(8,128)(2,1)S(1)}, u32[]{:S(2)}, u32[]{:S(2)}) collective-permute-start(bf16[96,640]{1,0:T(8,128)(2,1)S(1)} %get-tuple-element.5), channel_id=1, source_target_pairs={{0,0},{1,4},{2,12},{3,20},{4,24},{5,16},{6,8},{7,28},{8,9},{9,1},{... | collective-permute-start | bytes 368648 | tf_op jit(solution)/shard_map/ppermute | solution.py:205
  56.6 1.9 %collective-permute-start.18 = (bf16[96,640]{1,0:T(8,128)(2,1)S(1)}, bf16[96,640]{1,0:T(8,128)(2,1)S(1)}, u32[]{:S(2)}, u32[]{:S(2)}) collective-permute-start(bf16[96,640]{1,0:T(8,128)(2,1)S(1)} %get-tuple-element.6), channel_id=1, source_target_pairs={{0,28},{1,24},{2,16},{3,8},{4,4},{5,12},{6,20},{7,0},{8,21},{9,29}... | collective-permute-start | bytes 368648 | tf_op jit(solution)/shard_map/ppermute | solution.py:205
  59.2 7.1 %collective-permute-done.18 = bf16[96,640]{1,0:T(8,128)(2,1)S(1)} collective-permute-done((bf16[96,640]{1,0:T(8,128)(2,1)S(1)}, bf16[96,640]{1,0:T(8,128)(2,1)S(1)}, u32[]{:S(2)}, u32[]{:S(2)}) %collective-permute-start.18) | collective-permute-done | bytes 122912 | tf_op jit(solution)/shard_map/ppermute | solution.py:205
  (31 shorter events, 6.1 us)
Async XLA Ops:
  0.0 1.0 %copy-start.1 = (bf16[2,96,640]{2,1,0:T(8,128)(2,1)S(1)}, bf16[2,96,640]{2,1,0:T(8,128)(2,1)}, u32[]{:S(2)}) copy-start(bf16[2,96,640]{2,1,0:T(8,128)(2,1)} %param.4) | copy-start | bytes 737284
  0.0 31.5 %copy-start = (bf16[640,640]{1,0:T(8,128)(2,1)S(1)}, bf16[640,640]{1,0:T(8,128)(2,1)}, u32[]{:S(2)}) copy-start(bf16[640,640]{1,0:T(8,128)(2,1)} %refs_16_.7) | copy-start | bytes 2457604
  1.1 5.6 %collective-permute-start = (bf16[144,640]{1,0:T(8,128)(2,1)S(1)}, bf16[144,640]{1,0:T(8,128)(2,1)S(1)}, u32[]{:S(2)}, u32[]{:S(2)}) collective-permute-start(bf16[144,640]{1,0:T(8,128)(2,1)S(1)} %pad_maximum_fusion.1.refs_0_), channel_id=1, source_target_pairs={{0,8},{8,16},{16,24},{24,28},{28,20},{20,12},{12,4},{4,0},{1,9},{9... | collective-permute-start | bytes 552968 | tf_op jit(solution)/shard_map/ppermute | solution.py:86
  2.4 5.5 %collective-permute-start.10 = (bf16[144,640]{1,0:T(8,128)(2,1)S(1)}, bf16[144,640]{1,0:T(8,128)(2,1)S(1)}, u32[]{:S(2)}, u32[]{:S(2)}) collective-permute-start(bf16[144,640]{1,0:T(8,128)(2,1)S(1)} %pad_maximum_fusion.2.refs_8_), channel_id=1, source_target_pairs={{0,4},{8,0},{16,8},{24,16},{28,24},{20,28},{12,20},{4,12},{1,5},{9... | collective-permute-start | bytes 552968 | tf_op jit(solution)/shard_map/ppermute | solution.py:86
  2.6 9.0 %collective-permute-start.4 = (bf16[144,640]{1,0:T(8,128)(2,1)S(1)}, bf16[144,640]{1,0:T(8,128)(2,1)S(1)}, u32[]{:S(2)}, u32[]{:S(2)}) collective-permute-start(bf16[144,640]{1,0:T(8,128)(2,1)S(1)} %pad_maximum_fusion.1.refs_0_), channel_id=1, source_target_pairs={{0,4},{8,0},{16,8},{24,16},{28,24},{20,28},{12,20},{4,12},{1,5},{9... | collective-permute-start | bytes 552968 | tf_op jit(solution)/shard_map/ppermute | solution.py:86
  3.9 7.9 %collective-permute-start.7 = (bf16[144,640]{1,0:T(8,128)(2,1)S(1)}, bf16[144,640]{1,0:T(8,128)(2,1)S(1)}, u32[]{:S(2)}, u32[]{:S(2)}) collective-permute-start(bf16[144,640]{1,0:T(8,128)(2,1)S(1)} %pad_maximum_fusion.2.refs_8_), channel_id=1, source_target_pairs={{0,8},{8,16},{16,24},{24,28},{28,20},{20,12},{12,4},{4,0},{1,9},{9... | collective-permute-start | bytes 552968 | tf_op jit(solution)/shard_map/ppermute | solution.py:86
  6.6 7.9 %collective-permute-start.1 = (bf16[144,640]{1,0:T(8,128)(2,1)S(1)}, bf16[144,640]{1,0:T(8,128)(2,1)S(1)}, u32[]{:S(2)}, u32[]{:S(2)}) collective-permute-start(bf16[144,640]{1,0:T(8,128)(2,1)S(1)} %collective-permute-done.refs_1_), channel_id=1, source_target_pairs={{0,8},{8,16},{16,24},{24,28},{28,20},{20,12},{12,4},{4,0},{1,9},{9... | collective-permute-start | bytes 552968 | tf_op jit(solution)/shard_map/ppermute | solution.py:86
  7.9 7.9 %collective-permute-start.11 = (bf16[144,640]{1,0:T(8,128)(2,1)S(1)}, bf16[144,640]{1,0:T(8,128)(2,1)S(1)}, u32[]{:S(2)}, u32[]{:S(2)}) collective-permute-start(bf16[144,640]{1,0:T(8,128)(2,1)S(1)} %collective-permute-done.10.refs_15_), channel_id=1, source_target_pairs={{0,4},{8,0},{16,8},{24,16},{28,24},{20,28},{12,20},{4,12},{1,5},{9... | collective-permute-start | bytes 552968 | tf_op jit(solution)/shard_map/ppermute | solution.py:86
  11.6 7.9 %collective-permute-start.5 = (bf16[144,640]{1,0:T(8,128)(2,1)S(1)}, bf16[144,640]{1,0:T(8,128)(2,1)S(1)}, u32[]{:S(2)}, u32[]{:S(2)}) collective-permute-start(bf16[144,640]{1,0:T(8,128)(2,1)S(1)} %collective-permute-done.4.refs_7_), channel_id=1, source_target_pairs={{0,4},{8,0},{16,8},{24,16},{28,24},{20,28},{12,20},{4,12},{1,5},{9... | collective-permute-start | bytes 552968 | tf_op jit(solution)/shard_map/ppermute | solution.py:86
  11.8 7.9 %collective-permute-start.8 = (bf16[144,640]{1,0:T(8,128)(2,1)S(1)}, bf16[144,640]{1,0:T(8,128)(2,1)S(1)}, u32[]{:S(2)}, u32[]{:S(2)}) collective-permute-start(bf16[144,640]{1,0:T(8,128)(2,1)S(1)} %collective-permute-done.7.refs_9_), channel_id=1, source_target_pairs={{0,8},{8,16},{16,24},{24,28},{28,20},{20,12},{12,4},{4,0},{1,9},{9... | collective-permute-start | bytes 552968 | tf_op jit(solution)/shard_map/ppermute | solution.py:86
  14.5 6.5 %collective-permute-start.2 = (bf16[144,640]{1,0:T(8,128)(2,1)S(1)}, bf16[144,640]{1,0:T(8,128)(2,1)S(1)}, u32[]{:S(2)}, u32[]{:S(2)}) collective-permute-start(bf16[144,640]{1,0:T(8,128)(2,1)S(1)} %collective-permute-done.1.refs_2_), channel_id=1, source_target_pairs={{0,8},{8,16},{16,24},{24,28},{28,20},{20,12},{12,4},{4,0},{1,9},{9... | collective-permute-start | bytes 552968 | tf_op jit(solution)/shard_map/ppermute | solution.py:86
  15.8 7.7 %collective-permute-start.12 = (bf16[144,640]{1,0:T(8,128)(2,1)S(1)}, bf16[144,640]{1,0:T(8,128)(2,1)S(1)}, u32[]{:S(2)}, u32[]{:S(2)}) collective-permute-start(bf16[144,640]{1,0:T(8,128)(2,1)S(1)} %collective-permute-done.11.refs_14_), channel_id=1, source_target_pairs={{0,4},{8,0},{16,8},{24,16},{28,24},{20,28},{12,20},{4,12},{1,5},{9... | collective-permute-start | bytes 552968 | tf_op jit(solution)/shard_map/ppermute | solution.py:86
  19.5 7.9 %collective-permute-start.6 = (bf16[144,640]{1,0:T(8,128)(2,1)S(1)}, bf16[144,640]{1,0:T(8,128)(2,1)S(1)}, u32[]{:S(2)}, u32[]{:S(2)}) collective-permute-start(bf16[144,640]{1,0:T(8,128)(2,1)S(1)} %collective-permute-done.5.refs_6_), channel_id=1, source_target_pairs={{0,4},{8,0},{16,8},{24,16},{28,24},{20,28},{12,20},{4,12},{1,5},{9... | collective-permute-start | bytes 552968 | tf_op jit(solution)/shard_map/ppermute | solution.py:86
  19.7 7.7 %collective-permute-start.9 = (bf16[144,640]{1,0:T(8,128)(2,1)S(1)}, bf16[144,640]{1,0:T(8,128)(2,1)S(1)}, u32[]{:S(2)}, u32[]{:S(2)}) collective-permute-start(bf16[144,640]{1,0:T(8,128)(2,1)S(1)} %collective-permute-done.8.refs_10_), channel_id=1, source_target_pairs={{0,8},{8,16},{16,24},{24,28},{28,20},{20,12},{12,4},{4,0},{1,9},{9... | collective-permute-start | bytes 552968 | tf_op jit(solution)/shard_map/ppermute | solution.py:86
  21.0 7.5 %collective-permute-start.3 = (bf16[144,640]{1,0:T(8,128)(2,1)S(1)}, bf16[144,640]{1,0:T(8,128)(2,1)}, u32[]{:S(2)}, u32[]{:S(2)}) collective-permute-start(bf16[144,640]{1,0:T(8,128)(2,1)S(1)} %collective-permute-done.2.refs_3_), channel_id=1, source_target_pairs={{0,8},{8,16},{16,24},{24,28},{28,20},{20,12},{12,4},{4,0},{1,9},{9... | collective-permute-start | bytes 552968 | tf_op jit(solution)/shard_map/ppermute | solution.py:86
  23.5 8.0 %collective-permute-start.13 = (bf16[144,640]{1,0:T(8,128)(2,1)S(1)}, bf16[144,640]{1,0:T(8,128)(2,1)}, u32[]{:S(2)}, u32[]{:S(2)}) collective-permute-start(bf16[144,640]{1,0:T(8,128)(2,1)S(1)} %collective-permute-done.12.refs_13_), channel_id=1, source_target_pairs={{0,4},{8,0},{16,8},{24,16},{28,24},{20,28},{12,20},{4,12},{1,5},{9... | collective-permute-start | bytes 552968 | tf_op jit(solution)/shard_map/ppermute | solution.py:86
  34.1 4.6 %collective-permute-start.14 = (bf16[2,96,640]{2,1,0:T(8,128)(2,1)S(1)}, bf16[2,96,640]{2,1,0:T(8,128)(2,1)S(1)}, u32[]{:S(2)}, u32[]{:S(2)}) collective-permute-start(bf16[2,96,640]{2,1,0:T(8,128)(2,1)S(1)} %shard_map.38), channel_id=1, source_target_pairs={{0,1},{1,0},{2,3},{3,2},{4,5},{5,4},{6,7},{7,6},{8,9},{9,8},{10,11... | collective-permute-start | bytes 737288 | tf_op jit(solution)/shard_map/ppermute | solution.py:182
  42.8 2.9 %collective-permute-start.15 = (bf16[2,96,640]{2,1,0:T(8,128)(2,1)}, bf16[2,96,640]{2,1,0:T(8,128)(2,1)}, u32[]{:S(2)}, u32[]{:S(2)}) collective-permute-start(bf16[2,96,640]{2,1,0:T(8,128)(2,1)} %shard_map.39.refs_17_), channel_id=1, source_target_pairs={{0,1},{1,0},{2,3},{3,2},{4,5},{5,4},{6,7},{7,6},{8,9},{9,8},{10,11... | collective-permute-start | bytes 737288 | tf_op jit(solution)/shard_map/ppermute | solution.py:187
  42.8 7.4 %collective-permute-start.16 = (bf16[2,96,640]{2,1,0:T(8,128)(2,1)}, bf16[2,96,640]{2,1,0:T(8,128)(2,1)}, u32[]{:S(2)}, u32[]{:S(2)}) collective-permute-start(bf16[2,96,640]{2,1,0:T(8,128)(2,1)} %add_convert_fusion.refs_17_), channel_id=1, source_target_pairs={{0,2},{1,3},{2,0},{3,1},{4,6},{5,7},{6,4},{7,5},{8,10},{9,11},{10,... | collective-permute-start | bytes 737288 | tf_op jit(solution)/shard_map/ppermute | solution.py:185
  51.3 7.9 %collective-permute-start.17 = (bf16[96,640]{1,0:T(8,128)(2,1)S(1)}, bf16[96,640]{1,0:T(8,128)(2,1)S(1)}, u32[]{:S(2)}, u32[]{:S(2)}) collective-permute-start(bf16[96,640]{1,0:T(8,128)(2,1)S(1)} %get-tuple-element.5), channel_id=1, source_target_pairs={{0,0},{1,4},{2,12},{3,20},{4,24},{5,16},{6,8},{7,28},{8,9},{9,1},{... | collective-permute-start | bytes 368648 | tf_op jit(solution)/shard_map/ppermute | solution.py:205
  56.6 9.8 %collective-permute-start.18 = (bf16[96,640]{1,0:T(8,128)(2,1)S(1)}, bf16[96,640]{1,0:T(8,128)(2,1)S(1)}, u32[]{:S(2)}, u32[]{:S(2)}) collective-permute-start(bf16[96,640]{1,0:T(8,128)(2,1)S(1)} %get-tuple-element.6), channel_id=1, source_target_pairs={{0,28},{1,24},{2,16},{3,8},{4,4},{5,12},{6,20},{7,0},{8,21},{9,29}... | collective-permute-start | bytes 368648 | tf_op jit(solution)/shard_map/ppermute | solution.py:205

commit v4 on v3

--- a/solution.py
+++ b/solution.py
@@ -97,37 +97,37 @@
 
 
 def pick(options, index):
-    low = jnp.where(index & 1 == 0, options[0], options[1])
-    high = jnp.where(index & 1 == 0, options[2], options[3])
-    return jnp.where(index & 2 == 0, low, high)
-
-
-def attend_kernel(heads, n, flip, at_ref, *refs):
+    while len(options) > 1:
+        pairs = zip(options[::2], options[1::2])
+        options = [jnp.where(index & 1 == 0, even, odd) for even, odd in pairs]
+        index = index >> 1
+    return options[0]
+
+
+def attend_kernel(heads, n, flips, at_ref, *refs):
     first, second, w_ref, out_ref = refs[:n], refs[n : 2 * n], refs[2 * n], refs[-1]
-    place, at = at_ref[0], at_ref[1] ^ flip
-    count = n // 4
+    place, x, y, core = (at_ref[i] for i in range(4))
     half = ROWS // 2
     scale = HD ** (-0.5) * math.log2(math.e)
-    two = jnp.where((place - at + n) & 2 == 0, n - 2, 2)
-    away = [FR_DEV * ((at + 4 * i + two) & (n - 1)) for i in range(count)]
+    blocks, away = [], []
+    for flip_x, flip_y, flip_core in flips:
+        z = 2 * (core ^ flip_core) + (x ^ flip_x)
+        owner = z + (y ^ flip_y) * (n - 1 - 2 * z)
+        blocks.append((place - owner) & (n - 1))
+        away.append(FR_DEV * ((place - (owner ^ 2)) & (n - 1)))
     lane_frame = lax.broadcasted_iota(jnp.int32, (TPF, HD), 1) // TPF
     ones = jnp.ones((n * ROWS, HD), jnp.bfloat16)
     attended = []
     for head in range(heads):
         cols = slice(head * HD, (head + 1) * HD)
         rows = jnp.concatenate(
-            [
-                pick([half_ref[ROWS:, cols] for half_ref in part[4 * i : 4 * i + 4]], at)
-                for i in range(count)
-                for part in (first, second)
-            ],
-            axis=0,
+            [pick([ref[ROWS:, cols] for ref in part], block) for block in blocks for part in (first, second)], axis=0
         )
         keys = jnp.concatenate([ref[:ROWS, cols] for ref in first], axis=0)
         values = jnp.concatenate([ref[:ROWS, cols] for ref in second], axis=0)
         scores = lax.dot_general(rows, keys, (((1,), (1,)), ((), ())), preferred_element_type=jnp.float32)
         groups = []
-        for g in range(count * FR_DEV):
+        for g in range(len(flips) * FR_DEV):
             out_frame = away[g // FR_DEV] + g % FR_DEV
             parts = []
             for c in range(0, n * ROWS, HD):
@@ -141,18 +141,17 @@
         mixed = jnp.dot(weights, jnp.concatenate([values, ones], axis=1), preferred_element_type=jnp.float32)
         attended.append((mixed[:, :HD] / mixed[:, HD:]).astype(jnp.bfloat16))
     result = jnp.dot(jnp.concatenate(attended, axis=1), w_ref[...], preferred_element_type=jnp.float32)
-    for i in range(count):
-        out_ref[i] = result[i * ROWS : (i + 1) * ROWS].astype(out_ref.dtype)
-
-
-def attend(where, flip, found, out_weight, out_dtype, after=()):
+    out_ref[...] = result.astype(out_ref.dtype)
+
+
+def attend(where, flips, found, out_weight, out_dtype, after=()):
     n = len(found[0])
-    count = n // 4
+    count = len(flips)
     width, cols = out_weight.shape
     vmem = pl.BlockSpec(memory_space=pltpu.VMEM)
     return pl.pallas_call(
-        functools.partial(attend_kernel, width // HD, n, flip),
-        out_shape=jax.ShapeDtypeStruct((count, ROWS, cols), out_dtype),
+        functools.partial(attend_kernel, width // HD, n, flips),
+        out_shape=jax.ShapeDtypeStruct((count * ROWS, cols), out_dtype),
         in_specs=[pl.BlockSpec(memory_space=pltpu.SMEM)]
         + [vmem] * (2 * n + 1)
         + [pl.BlockSpec(memory_space=pl.ANY)] * len(after),
@@ -169,44 +168,34 @@
 def on_device_ring(queries, keys_values, out_weight):
     n = lax.axis_size("frames")
     frame, head = lax.axis_index("frames"), lax.axis_index("heads")
-    where = jnp.stack([ring_place(frame, n), head]).astype(jnp.int32)
+    x, y, core = head >> 1, frame & 1, head & 1
+    where = jnp.stack([ring_place(frame, n), x, y, core]).astype(jnp.int32)
     half = ROWS // 2
     streams = [
         jnp.concatenate([keys_values[0], queries[:half]], axis=0),
         jnp.concatenate([keys_values[1], queries[half:]], axis=0),
     ]
     found = gather_ring(streams, n)
-    to_core = [(h, h ^ 1) for h in range(4)]
-    to_x = [(h, h ^ 2) for h in range(4)]
-    f32 = jnp.float32
-    from_core = lax.ppermute(attend(where, 3, found, out_weight, jnp.bfloat16), "heads", to_core)
-    given = attend(where, 2, found, out_weight, f32)
-    given = (given + from_core.astype(f32)).astype(jnp.bfloat16)
-    from_x = lax.ppermute(given, "heads", to_x)
-    last_given = attend(where, 1, found, out_weight, jnp.bfloat16, (given,))
-    from_core = lax.ppermute(last_given, "heads", to_core)
-    kept = attend(where, 0, found, out_weight, f32, (last_given,))
-    order = ring_order(n)
-    z, y = frame >> 1, frame & 1
-
-    def flip(z, y, head):
-        return y & (1 ^ ((head + 2 * z + 1) >> 2 & 1))
-
-    arrived = []
-    for slot in range(2):
-        pairs = []
-        for f in range(n):
-            for h in range(4):
-                distance = 4 * (slot ^ flip(f >> 1, f & 1, h)) + h
-                owner = order[(ring_place(f, n) - distance) % n]
-                pairs.append((f * 4 + h, owner * 4 + f // 2))
-        j = slot ^ flip(z, y, head)
-        total = kept[j] + from_core[j].astype(f32) + from_x[j].astype(f32)
-        arrived.append(lax.ppermute(total.astype(jnp.bfloat16), ("frames", "heads"), pairs))
-    straight = (head - where[0]) & 4 == 0
-    return jnp.concatenate(
-        [jnp.where(straight, arrived[0], arrived[1]), jnp.where(straight, arrived[1], arrived[0])], axis=1
-    )
+    devices = [(f, h) for f in range(n) for h in range(4)]
+    f32, bf16 = jnp.float32, jnp.bfloat16
+
+    def swap(block, flip_x, flip_y, flip_core):
+        pairs = [(4 * f + h, 4 * (f ^ flip_y) + (h ^ (2 * flip_x + flip_core))) for f, h in devices]
+        return lax.ppermute(block, ("frames", "heads"), pairs)
+
+    flips = [(1, 1), (1, 0), (0, 1)]
+    given = attend(where, [(*flip, 1) for flip in flips + [(0, 0)]], found, out_weight, bf16)
+    from_core = swap(given, 0, 0, 1).reshape(len(flips) + 1, ROWS, -1)
+    kept = attend(where, [(*flip, 0) for flip in flips], found, out_weight, f32, (given,))
+    kept = kept.reshape(len(flips), ROWS, -1)
+    sums = [(kept[i] + from_core[i].astype(f32)).astype(bf16) for i in range(len(flips))]
+    diagonal, beside, across = (swap(block, *flip, 0) for block, flip in zip(sums, flips))
+    kept = attend(where, [(0, 0, 0)], found, out_weight, f32, tuple(sums))
+    same = (kept + from_core[-1].astype(f32) + beside.astype(f32)).astype(bf16)
+    other = (across.astype(f32) + diagonal.astype(f32)).astype(bf16)
+    block = jnp.concatenate([jnp.where(y == 0, same, other), jnp.where(y == 0, other, same)], axis=1)
+    pairs = [(4 * f + h, 4 * (2 * (2 * (h & 1) + (h >> 1)) + (f & 1)) + (f >> 1)) for f, h in devices]
+    return lax.ppermute(block, ("frames", "heads"), pairs)
 
 
 def solution(mesh):

time: 67.4 us -> 67.9 us (level)
  the two profiles are of different devices: /device:TPU:3 before, /device:TPU:1 now
where the time goes in v4:
time: 67.9 us; the launch traced here: 67.6 us
  waiting for transfers between devices  31.8 us (47%)
  starting transfers between devices  21.1 us (31%)
  Pallas kernels  9.72 us (14%)
  other arithmetic  3.16 us (5%)
  local copies, waits for them, and re-layouts  1.72 us (3%)
    ppermute x14, waiting for transfers between devices, hop(): lax.ppermute(x, 'frames', [(order[i], order[(i + by) % n]) for i in range...  19.8 us
    ppermute x14, starting transfers between devices, hop(): lax.ppermute(x, 'frames', [(order[i], order[(i + by) % n]) for i in range...  11.3 us
    pallas_call x3, Pallas kernels, attend(): pl.pallas_call(functools.partial(attend_kernel, width // HD, n, flips), o...  9.72 us
    ppermute x1, waiting for transfers between devices, on_device_ring(): return lax.ppermute(block, ('frames', 'heads'), pairs)  8.12 us
    ppermute x1, starting transfers between devices, on_device_ring(): return lax.ppermute(block, ('frames', 'heads'), pairs)  5.24 us
    ppermute x4, starting transfers between devices, swap(): return lax.ppermute(block, ('frames', 'heads'), pairs)  4.58 us
    ppermute x4, waiting for transfers between devices, swap(): return lax.ppermute(block, ('frames', 'heads'), pairs)  3.85 us
  transfers between devices with their start and end apart: 19, of which 11 were waited for; matrix products, arithmetic and copies ran while one was open for 0% of the time, Pallas kernels for 8%

profile of v4, /device:TPU:1, one launch (start us, length us, event | category | flops | bytes accessed | tf_op | source)
XLA Modules:
  0.0 67.6 jit_solution(2692736144422962678)
XLA Ops:
  1.1 2.2 %collective-permute-start = (bf16[144,640]{1,0:T(8,128)(2,1)S(1)}, bf16[144,640]{1,0:T(8,128)(2,1)S(1)}, u32[]{:S(2)}, u32[]{:S(2)}) collective-permute-start(bf16[144,640]{1,0:T(8,128)(2,1)S(1)} %pad_maximum_fusion.1.refs_0_), channel_id=1, source_target_pairs={{0,8},{8,16},{16,24},{24,28},{28,20},{20,12},{12,4},{4,0},{1,9},{9... | collective-permute-start | bytes 552968 | tf_op jit(solution)/shard_map/ppermute | solution.py:86
  3.3 1.4 %collective-permute-start.4 = (bf16[144,640]{1,0:T(8,128)(2,1)S(1)}, bf16[144,640]{1,0:T(8,128)(2,1)S(1)}, u32[]{:S(2)}, u32[]{:S(2)}) collective-permute-start(bf16[144,640]{1,0:T(8,128)(2,1)S(1)} %pad_maximum_fusion.1.refs_0_), channel_id=1, source_target_pairs={{0,4},{8,0},{16,8},{24,16},{28,24},{20,28},{12,20},{4,12},{1,5},{9... | collective-permute-start | bytes 552968 | tf_op jit(solution)/shard_map/ppermute | solution.py:86
  4.8 2.7 %collective-permute-done.refs_1_ = bf16[144,640]{1,0:T(8,128)(2,1)S(1)} collective-permute-done((bf16[144,640]{1,0:T(8,128)(2,1)S(1)}, bf16[144,640]{1,0:T(8,128)(2,1)S(1)}, u32[]{:S(2)}, u32[]{:S(2)}) %collective-permute-start) | collective-permute-done | bytes 184352 | tf_op jit(solution)/shard_map/ppermute | solution.py:86
  7.5 1.2 %collective-permute-start.1 = (bf16[144,640]{1,0:T(8,128)(2,1)S(1)}, bf16[144,640]{1,0:T(8,128)(2,1)S(1)}, u32[]{:S(2)}, u32[]{:S(2)}) collective-permute-start(bf16[144,640]{1,0:T(8,128)(2,1)S(1)} %collective-permute-done.refs_1_), channel_id=1, source_target_pairs={{0,8},{8,16},{16,24},{24,28},{28,20},{20,12},{12,4},{4,0},{1,9},{9... | collective-permute-start | bytes 552968 | tf_op jit(solution)/shard_map/ppermute | solution.py:86
  9.0 3.4 %collective-permute-done.4.refs_7_ = bf16[144,640]{1,0:T(8,128)(2,1)S(1)} collective-permute-done((bf16[144,640]{1,0:T(8,128)(2,1)S(1)}, bf16[144,640]{1,0:T(8,128)(2,1)S(1)}, u32[]{:S(2)}, u32[]{:S(2)}) %collective-permute-start.4) | collective-permute-done | bytes 184352 | tf_op jit(solution)/shard_map/ppermute | solution.py:86
  12.8 1.1 %collective-permute-start.8 = (bf16[144,640]{1,0:T(8,128)(2,1)S(1)}, bf16[144,640]{1,0:T(8,128)(2,1)S(1)}, u32[]{:S(2)}, u32[]{:S(2)}) collective-permute-start(bf16[144,640]{1,0:T(8,128)(2,1)S(1)} %collective-permute-done.7.refs_9_), channel_id=1, source_target_pairs={{0,8},{8,16},{16,24},{24,28},{28,20},{20,12},{12,4},{4,0},{1,9},{9... | collective-permute-start | bytes 552968 | tf_op jit(solution)/shard_map/ppermute | solution.py:86
  13.9 1.3 %collective-permute-done.1.refs_2_ = bf16[144,640]{1,0:T(8,128)(2,1)S(1)} collective-permute-done((bf16[144,640]{1,0:T(8,128)(2,1)S(1)}, bf16[144,640]{1,0:T(8,128)(2,1)S(1)}, u32[]{:S(2)}, u32[]{:S(2)}) %collective-permute-start.1) | collective-permute-done | bytes 184352 | tf_op jit(solution)/shard_map/ppermute | solution.py:86
  15.2 1.5 %collective-permute-start.2 = (bf16[144,640]{1,0:T(8,128)(2,1)S(1)}, bf16[144,640]{1,0:T(8,128)(2,1)S(1)}, u32[]{:S(2)}, u32[]{:S(2)}) collective-permute-start(bf16[144,640]{1,0:T(8,128)(2,1)S(1)} %collective-permute-done.1.refs_2_), channel_id=1, source_target_pairs={{0,8},{8,16},{16,24},{24,28},{28,20},{20,12},{12,4},{4,0},{1,9},{9... | collective-permute-start | bytes 552968 | tf_op jit(solution)/shard_map/ppermute | solution.py:86
  16.7 3.6 %collective-permute-done.5.refs_6_ = bf16[144,640]{1,0:T(8,128)(2,1)S(1)} collective-permute-done((bf16[144,640]{1,0:T(8,128)(2,1)S(1)}, bf16[144,640]{1,0:T(8,128)(2,1)S(1)}, u32[]{:S(2)}, u32[]{:S(2)}) %collective-permute-start.5) | collective-permute-done | bytes 184352 | tf_op jit(solution)/shard_map/ppermute | solution.py:86
  20.7 1.1 %collective-permute-start.9 = (bf16[144,640]{1,0:T(8,128)(2,1)S(1)}, bf16[144,640]{1,0:T(8,128)(2,1)S(1)}, u32[]{:S(2)}, u32[]{:S(2)}) collective-permute-start(bf16[144,640]{1,0:T(8,128)(2,1)S(1)} %collective-permute-done.8.refs_10_), channel_id=1, source_target_pairs={{0,8},{8,16},{16,24},{24,28},{28,20},{20,12},{12,4},{4,0},{1,9},{9... | collective-permute-start | bytes 552968 | tf_op jit(solution)/shard_map/ppermute | solution.py:86
  21.8 1.3 %collective-permute-start.3 = (bf16[144,640]{1,0:T(8,128)(2,1)S(1)}, bf16[144,640]{1,0:T(8,128)(2,1)}, u32[]{:S(2)}, u32[]{:S(2)}) collective-permute-start(bf16[144,640]{1,0:T(8,128)(2,1)S(1)} %collective-permute-done.2.refs_3_), channel_id=1, source_target_pairs={{0,8},{8,16},{16,24},{24,28},{28,20},{20,12},{12,4},{4,0},{1,9},{9... | collective-permute-start | bytes 552968 | tf_op jit(solution)/shard_map/ppermute | solution.py:86
  23.1 1.2 %collective-permute-done.12.refs_13_ = bf16[144,640]{1,0:T(8,128)(2,1)S(1)} collective-permute-done((bf16[144,640]{1,0:T(8,128)(2,1)S(1)}, bf16[144,640]{1,0:T(8,128)(2,1)S(1)}, u32[]{:S(2)}, u32[]{:S(2)}) %collective-permute-start.12) | collective-permute-done | bytes 184352 | tf_op jit(solution)/shard_map/ppermute | solution.py:86
  24.7 3.5 %collective-permute-done.6.refs_5_ = bf16[144,640]{1,0:T(8,128)(2,1)S(1)} collective-permute-done((bf16[144,640]{1,0:T(8,128)(2,1)S(1)}, bf16[144,640]{1,0:T(8,128)(2,1)S(1)}, u32[]{:S(2)}, u32[]{:S(2)}) %collective-permute-start.6) | collective-permute-done | bytes 184352 | tf_op jit(solution)/shard_map/ppermute | solution.py:86
  29.3 3.0 %collective-permute-done.13.refs_12_ = bf16[144,640]{1,0:T(8,128)(2,1)} collective-permute-done((bf16[144,640]{1,0:T(8,128)(2,1)S(1)}, bf16[144,640]{1,0:T(8,128)(2,1)}, u32[]{:S(2)}, u32[]{:S(2)}) %collective-permute-start.13) | collective-permute-done | bytes 184352 | tf_op jit(solution)/shard_map/ppermute | solution.py:86
  32.3 4.1 %shard_map.37.refs_17_ = bf16[384,640]{1,0:T(8,128)(2,1)S(1)} custom-call(s32[4]{0:T(128)S(1)} %pad_add_fusion.at_ref, bf16[144,640]{1,0:T(8,128)(2,1)S(1)} %pad_maximum_fusion.1.refs_0_, bf16[144,640]{1,0:T(8,128)(2,1)S(1)} %collective-permute-done.refs_1_, bf16[144,640]{1,0:T(8,128)(2,1)S(1)} %collective-permute-done.1.refs_2_, ...), custom_call_target="tpu_custom_call" | custom-call | flops 1069547520 | bytes 3768320 | tf_op jit(solution)/shard_map/pallas_call | solution.py:152
  36.4 1.9 %collective-permute-start.14 = (bf16[384,640]{1,0:T(8,128)(2,1)S(1)}, bf16[384,640]{1,0:T(8,128)(2,1)S(1)}, u32[]{:S(2)}, u32[]{:S(2)}) collective-permute-start(bf16[384,640]{1,0:T(8,128)(2,1)S(1)} %shard_map.37.refs_17_), channel_id=1, source_target_pairs={{0,1},{1,0},{2,3},{3,2},{4,5},{5,4},{6,7},{7,6},{8,9},{9,8},{10,11... | collective-permute-start | bytes 1474568 | tf_op jit(solution)/shard_map/ppermute | solution.py:184
  38.4 3.4 %shard_map.38 = f32[288,640]{1,0:T(8,128)S(1)} custom-call(s32[4]{0:T(128)S(1)} %pad_add_fusion.at_ref, bf16[144,640]{1,0:T(8,128)(2,1)S(1)} %pad_maximum_fusion.1.refs_0_, bf16[144,640]{1,0:T(8,128)(2,1)S(1)} %collective-permute-done.refs_1_, bf16[144,640]{1,0:T(8,128)(2,1)S(1)} %collective-permute-done.1.refs_2_, ...), custom_call_target="tpu_custom_call" | custom-call | flops 802160640 | bytes 3768320 | tf_op jit(solution)/shard_map/pallas_call | solution.py:152
  42.6 1.2 %collective-permute-start.15 = (bf16[96,640]{1,0:T(8,128)(2,1)}, bf16[96,640]{1,0:T(8,128)(2,1)}, u32[]{:S(2)}, u32[]{:S(2)}) collective-permute-start(bf16[96,640]{1,0:T(8,128)(2,1)} %get-tuple-element.7.refs_18_), channel_id=1, source_target_pairs={{0,2},{1,3},{2,0},{3,1},{4,6},{5,7},{6,4},{7,5},{8,10},{9,11},{10,... | collective-permute-start | bytes 368648 | tf_op jit(solution)/shard_map/ppermute | solution.py:184
  44.0 1.3 %collective-permute-start.17 = (bf16[96,640]{1,0:T(8,128)(2,1)S(1)}, bf16[96,640]{1,0:T(8,128)(2,1)}, u32[]{:S(2)}, u32[]{:S(2)}) collective-permute-start(bf16[96,640]{1,0:T(8,128)(2,1)S(1)} %get-tuple-element.9.refs_17_), channel_id=1, source_target_pairs={{0,6},{1,7},{2,4},{3,5},{4,2},{5,3},{6,0},{7,1},{8,14},{9,15},{10,... | collective-permute-start | bytes 368648 | tf_op jit(solution)/shard_map/ppermute | solution.py:184
  45.2 2.3 %shard_map.39 = f32[96,640]{1,0:T(8,128)S(1)} custom-call(s32[4]{0:T(128)S(1)} %pad_add_fusion.at_ref, bf16[144,640]{1,0:T(8,128)(2,1)S(1)} %pad_maximum_fusion.1.refs_0_, bf16[144,640]{1,0:T(8,128)(2,1)S(1)} %collective-permute-done.refs_1_, bf16[144,640]{1,0:T(8,128)(2,1)S(1)} %collective-permute-done.1.refs_2_, ...), custom_call_target="tpu_custom_call" | custom-call | flops 267386880 | bytes 3768320 | tf_op jit(solution)/shard_map/pallas_call | solution.py:152
  47.8 3.5 %collective-permute-done.16 = bf16[96,640]{1,0:T(8,128)(2,1)} collective-permute-done((bf16[96,640]{1,0:T(8,128)(2,1)}, bf16[96,640]{1,0:T(8,128)(2,1)}, u32[]{:S(2)}, u32[]{:S(2)}) %collective-permute-start.16) | collective-permute-done | bytes 122912 | tf_op jit(solution)/shard_map/ppermute | solution.py:184
  51.3 1.2 %broadcast_select_fusion.1 = (bf16[96,640]{1,0:T(8,128)(2,1)S(1)}, bf16[96,640]{1,0:T(8,128)(2,1)S(1)}) fusion(pred[]{:T(512)S(6)} %eq.4, bf16[96,640]{1,0:T(8,128)(2,1)} %collective-permute-done.17, bf16[96,640]{1,0:T(8,128)(2,1)} %collective-permute-done.16, bf16[96,640]{1,0:T(8,128)(2,1)} %collective-permute-done.15, f32[96,640]{1,0:T(8,128)S(1)} %shard_map.39, ...), kind=kLoop, calls=%fused_computation.14 | loop fusion | flops 614400 | bytes 983041 | tf_op jit(solution)/shard_map/jit(_where)/select_n | solution.py:196
  53.6 5.2 %collective-permute-start.18 = (bf16[96,1280]{1,0:T(8,128)(2,1)S(1)}, bf16[96,1280]{1,0:T(8,128)(2,1)S(1)}, u32[]{:S(2)}, u32[]{:S(2)}) collective-permute-start(bf16[96,1280]{1,0:T(8,128)(2,1)S(1)} %pad_maximum_fusion), channel_id=1, source_target_pairs={{0,0},{1,16},{2,8},{3,24},{4,4},{5,20},{6,12},{7,28},{8,1},{9,17},... | collective-permute-start | bytes 737288 | tf_op jit(solution)/shard_map/ppermute | solution.py:198
  58.8 8.1 %collective-permute-done.18 = bf16[96,1280]{1,0:T(8,128)(2,1)S(1)} collective-permute-done((bf16[96,1280]{1,0:T(8,128)(2,1)S(1)}, bf16[96,1280]{1,0:T(8,128)(2,1)S(1)}, u32[]{:S(2)}, u32[]{:S(2)}) %collective-permute-start.18) | collective-permute-done | bytes 245792 | tf_op jit(solution)/shard_map/ppermute | solution.py:198
  (33 shorter events, 6.8 us)
Async XLA Ops:
  0.0 1.0 %copy-start.2 = (bf16[2,96,640]{2,1,0:T(8,128)(2,1)S(1)}, bf16[2,96,640]{2,1,0:T(8,128)(2,1)}, u32[]{:S(2)}) copy-start(bf16[2,96,640]{2,1,0:T(8,128)(2,1)} %param.4) | copy-start | bytes 737284
  0.0 32.3 %copy-start = (bf16[640,640]{1,0:T(8,128)(2,1)S(1)}, bf16[640,640]{1,0:T(8,128)(2,1)}, u32[]{:S(2)}) copy-start(bf16[640,640]{1,0:T(8,128)(2,1)} %refs_16_.5) | copy-start | bytes 2457604
  1.1 6.5 %collective-permute-start = (bf16[144,640]{1,0:T(8,128)(2,1)S(1)}, bf16[144,640]{1,0:T(8,128)(2,1)S(1)}, u32[]{:S(2)}, u32[]{:S(2)}) collective-permute-start(bf16[144,640]{1,0:T(8,128)(2,1)S(1)} %pad_maximum_fusion.1.refs_0_), channel_id=1, source_target_pairs={{0,8},{8,16},{16,24},{24,28},{28,20},{20,12},{12,4},{4,0},{1,9},{9... | collective-permute-start | bytes 552968 | tf_op jit(solution)/shard_map/ppermute | solution.py:86
  3.3 5.5 %collective-permute-start.10 = (bf16[144,640]{1,0:T(8,128)(2,1)S(1)}, bf16[144,640]{1,0:T(8,128)(2,1)S(1)}, u32[]{:S(2)}, u32[]{:S(2)}) collective-permute-start(bf16[144,640]{1,0:T(8,128)(2,1)S(1)} %pad_maximum_fusion.2.refs_8_), channel_id=1, source_target_pairs={{0,4},{8,0},{16,8},{24,16},{28,24},{20,28},{12,20},{4,12},{1,5},{9... | collective-permute-start | bytes 552968 | tf_op jit(solution)/shard_map/ppermute | solution.py:86
  3.3 9.1 %collective-permute-start.4 = (bf16[144,640]{1,0:T(8,128)(2,1)S(1)}, bf16[144,640]{1,0:T(8,128)(2,1)S(1)}, u32[]{:S(2)}, u32[]{:S(2)}) collective-permute-start(bf16[144,640]{1,0:T(8,128)(2,1)S(1)} %pad_maximum_fusion.1.refs_0_), channel_id=1, source_target_pairs={{0,4},{8,0},{16,8},{24,16},{28,24},{20,28},{12,20},{4,12},{1,5},{9... | collective-permute-start | bytes 552968 | tf_op jit(solution)/shard_map/ppermute | solution.py:86
  4.7 8.1 %collective-permute-start.7 = (bf16[144,640]{1,0:T(8,128)(2,1)S(1)}, bf16[144,640]{1,0:T(8,128)(2,1)S(1)}, u32[]{:S(2)}, u32[]{:S(2)}) collective-permute-start(bf16[144,640]{1,0:T(8,128)(2,1)S(1)} %pad_maximum_fusion.2.refs_8_), channel_id=1, source_target_pairs={{0,8},{8,16},{16,24},{24,28},{28,20},{20,12},{12,4},{4,0},{1,9},{9... | collective-permute-start | bytes 552968 | tf_op jit(solution)/shard_map/ppermute | solution.py:86
  7.5 7.6 %collective-permute-start.1 = (bf16[144,640]{1,0:T(8,128)(2,1)S(1)}, bf16[144,640]{1,0:T(8,128)(2,1)S(1)}, u32[]{:S(2)}, u32[]{:S(2)}) collective-permute-start(bf16[144,640]{1,0:T(8,128)(2,1)S(1)} %collective-permute-done.refs_1_), channel_id=1, source_target_pairs={{0,8},{8,16},{16,24},{24,28},{28,20},{20,12},{12,4},{4,0},{1,9},{9... | collective-permute-start | bytes 552968 | tf_op jit(solution)/shard_map/ppermute | solution.py:86
  8.7 7.9 %collective-permute-start.11 = (bf16[144,640]{1,0:T(8,128)(2,1)S(1)}, bf16[144,640]{1,0:T(8,128)(2,1)S(1)}, u32[]{:S(2)}, u32[]{:S(2)}) collective-permute-start(bf16[144,640]{1,0:T(8,128)(2,1)S(1)} %collective-permute-done.10.refs_15_), channel_id=1, source_target_pairs={{0,4},{8,0},{16,8},{24,16},{28,24},{20,28},{12,20},{4,12},{1,5},{9... | collective-permute-start | bytes 552968 | tf_op jit(solution)/shard_map/ppermute | solution.py:86
  12.4 7.9 %collective-permute-start.5 = (bf16[144,640]{1,0:T(8,128)(2,1)S(1)}, bf16[144,640]{1,0:T(8,128)(2,1)S(1)}, u32[]{:S(2)}, u32[]{:S(2)}) collective-permute-start(bf16[144,640]{1,0:T(8,128)(2,1)S(1)} %collective-permute-done.4.refs_7_), channel_id=1, source_target_pairs={{0,4},{8,0},{16,8},{24,16},{28,24},{20,28},{12,20},{4,12},{1,5},{9... | collective-permute-start | bytes 552968 | tf_op jit(solution)/shard_map/ppermute | solution.py:86
  12.8 7.9 %collective-permute-start.8 = (bf16[144,640]{1,0:T(8,128)(2,1)S(1)}, bf16[144,640]{1,0:T(8,128)(2,1)S(1)}, u32[]{:S(2)}, u32[]{:S(2)}) collective-permute-start(bf16[144,640]{1,0:T(8,128)(2,1)S(1)} %collective-permute-done.7.refs_9_), channel_id=1, source_target_pairs={{0,8},{8,16},{16,24},{24,28},{28,20},{20,12},{12,4},{4,0},{1,9},{9... | collective-permute-start | bytes 552968 | tf_op jit(solution)/shard_map/ppermute | solution.py:86
  15.2 6.6 %collective-permute-start.2 = (bf16[144,640]{1,0:T(8,128)(2,1)S(1)}, bf16[144,640]{1,0:T(8,128)(2,1)S(1)}, u32[]{:S(2)}, u32[]{:S(2)}) collective-permute-start(bf16[144,640]{1,0:T(8,128)(2,1)S(1)} %collective-permute-done.1.refs_2_), channel_id=1, source_target_pairs={{0,8},{8,16},{16,24},{24,28},{28,20},{20,12},{12,4},{4,0},{1,9},{9... | collective-permute-start | bytes 552968 | tf_op jit(solution)/shard_map/ppermute | solution.py:86
  16.6 7.7 %collective-permute-start.12 = (bf16[144,640]{1,0:T(8,128)(2,1)S(1)}, bf16[144,640]{1,0:T(8,128)(2,1)S(1)}, u32[]{:S(2)}, u32[]{:S(2)}) collective-permute-start(bf16[144,640]{1,0:T(8,128)(2,1)S(1)} %collective-permute-done.11.refs_14_), channel_id=1, source_target_pairs={{0,4},{8,0},{16,8},{24,16},{28,24},{20,28},{12,20},{4,12},{1,5},{9... | collective-permute-start | bytes 552968 | tf_op jit(solution)/shard_map/ppermute | solution.py:86
  20.3 7.9 %collective-permute-start.6 = (bf16[144,640]{1,0:T(8,128)(2,1)S(1)}, bf16[144,640]{1,0:T(8,128)(2,1)S(1)}, u32[]{:S(2)}, u32[]{:S(2)}) collective-permute-start(bf16[144,640]{1,0:T(8,128)(2,1)S(1)} %collective-permute-done.5.refs_6_), channel_id=1, source_target_pairs={{0,4},{8,0},{16,8},{24,16},{28,24},{20,28},{12,20},{4,12},{1,5},{9... | collective-permute-start | bytes 552968 | tf_op jit(solution)/shard_map/ppermute | solution.py:86
  20.7 7.6 %collective-permute-start.9 = (bf16[144,640]{1,0:T(8,128)(2,1)S(1)}, bf16[144,640]{1,0:T(8,128)(2,1)S(1)}, u32[]{:S(2)}, u32[]{:S(2)}) collective-permute-start(bf16[144,640]{1,0:T(8,128)(2,1)S(1)} %collective-permute-done.8.refs_10_), channel_id=1, source_target_pairs={{0,8},{8,16},{16,24},{24,28},{28,20},{20,12},{12,4},{4,0},{1,9},{9... | collective-permute-start | bytes 552968 | tf_op jit(solution)/shard_map/ppermute | solution.py:86
  21.8 7.5 %collective-permute-start.3 = (bf16[144,640]{1,0:T(8,128)(2,1)S(1)}, bf16[144,640]{1,0:T(8,128)(2,1)}, u32[]{:S(2)}, u32[]{:S(2)}) collective-permute-start(bf16[144,640]{1,0:T(8,128)(2,1)S(1)} %collective-permute-done.2.refs_3_), channel_id=1, source_target_pairs={{0,8},{8,16},{16,24},{24,28},{28,20},{20,12},{12,4},{4,0},{1,9},{9... | collective-permute-start | bytes 552968 | tf_op jit(solution)/shard_map/ppermute | solution.py:86
  24.3 8.0 %collective-permute-start.13 = (bf16[144,640]{1,0:T(8,128)(2,1)S(1)}, bf16[144,640]{1,0:T(8,128)(2,1)}, u32[]{:S(2)}, u32[]{:S(2)}) collective-permute-start(bf16[144,640]{1,0:T(8,128)(2,1)S(1)} %collective-permute-done.12.refs_13_), channel_id=1, source_target_pairs={{0,4},{8,0},{16,8},{24,16},{28,24},{20,28},{12,20},{4,12},{1,5},{9... | collective-permute-start | bytes 552968 | tf_op jit(solution)/shard_map/ppermute | solution.py:86
  36.4 5.3 %collective-permute-start.14 = (bf16[384,640]{1,0:T(8,128)(2,1)S(1)}, bf16[384,640]{1,0:T(8,128)(2,1)S(1)}, u32[]{:S(2)}, u32[]{:S(2)}) collective-permute-start(bf16[384,640]{1,0:T(8,128)(2,1)S(1)} %shard_map.37.refs_17_), channel_id=1, source_target_pairs={{0,1},{1,0},{2,3},{3,2},{4,5},{5,4},{6,7},{7,6},{8,9},{9,8},{10,11... | collective-permute-start | bytes 1474568 | tf_op jit(solution)/shard_map/ppermute | solution.py:184
  41.7 0.9 %copy-start.1 = (bf16[384,640]{1,0:T(8,128)(2,1)}, bf16[384,640]{1,0:T(8,128)(2,1)S(1)}, u32[]{:S(2)}) copy-start(bf16[384,640]{1,0:T(8,128)(2,1)S(1)} %collective-permute-done.14) | copy-start | bytes 1474564
  42.6 5.2 %collective-permute-start.15 = (bf16[96,640]{1,0:T(8,128)(2,1)}, bf16[96,640]{1,0:T(8,128)(2,1)}, u32[]{:S(2)}, u32[]{:S(2)}) collective-permute-start(bf16[96,640]{1,0:T(8,128)(2,1)} %get-tuple-element.7.refs_18_), channel_id=1, source_target_pairs={{0,2},{1,3},{2,0},{3,1},{4,6},{5,7},{6,4},{7,5},{8,10},{9,11},{10,... | collective-permute-start | bytes 368648 | tf_op jit(solution)/shard_map/ppermute | solution.py:184
  43.8 7.6 %collective-permute-start.16 = (bf16[96,640]{1,0:T(8,128)(2,1)}, bf16[96,640]{1,0:T(8,128)(2,1)}, u32[]{:S(2)}, u32[]{:S(2)}) collective-permute-start(bf16[96,640]{1,0:T(8,128)(2,1)} %get-tuple-element.8.refs_19_), channel_id=1, source_target_pairs={{0,4},{1,5},{2,6},{3,7},{4,0},{5,1},{6,2},{7,3},{8,12},{9,13},{10,... | collective-permute-start | bytes 368648 | tf_op jit(solution)/shard_map/ppermute | solution.py:184
  44.0 7.4 %collective-permute-start.17 = (bf16[96,640]{1,0:T(8,128)(2,1)S(1)}, bf16[96,640]{1,0:T(8,128)(2,1)}, u32[]{:S(2)}, u32[]{:S(2)}) collective-permute-start(bf16[96,640]{1,0:T(8,128)(2,1)S(1)} %get-tuple-element.9.refs_17_), channel_id=1, source_target_pairs={{0,6},{1,7},{2,4},{3,5},{4,2},{5,3},{6,0},{7,1},{8,14},{9,15},{10,... | collective-permute-start | bytes 368648 | tf_op jit(solution)/shard_map/ppermute | solution.py:184
  53.6 13.4 %collective-permute-start.18 = (bf16[96,1280]{1,0:T(8,128)(2,1)S(1)}, bf16[96,1280]{1,0:T(8,128)(2,1)S(1)}, u32[]{:S(2)}, u32[]{:S(2)}) collective-permute-start(bf16[96,1280]{1,0:T(8,128)(2,1)S(1)} %pad_maximum_fusion), channel_id=1, source_target_pairs={{0,0},{1,16},{2,8},{3,24},{4,4},{5,20},{6,12},{7,28},{8,1},{9,17},... | collective-permute-start | bytes 737288 | tf_op jit(solution)/shard_map/ppermute | solution.py:198

commit v5 on v0

--- a/solution.py
+++ b/solution.py
@@ -1,11 +1,18 @@
+import functools
+import math
+
 import jax
 import jax.numpy as jnp
 from jax import lax
+from jax.experimental import pallas as pl
+from jax.experimental.pallas import tpu as pltpu
 from jax.sharding import PartitionSpec as P
 
 HD = 128
 TPF = 32
 FR_DEV = 3
+ROWS = FR_DEV * TPF
+SCALE = HD ** (-0.5) * math.log2(math.e)
 
 
 reach_cap = 32
@@ -16,7 +23,7 @@
     return lax.ppermute(x, axis, [(i, (i + by) % devices) for i in range(devices)])
 
 
-def on_device(queries, keys_values, out_weight):
+def on_device_band(queries, keys_values, out_weight):
     total_frames = lax.axis_size("frames") * FR_DEV
     reach = min(reach_cap, (total_frames - 1) // 2)
     steps = (reach + FR_DEV - 1) // FR_DEV
@@ -67,9 +74,220 @@
     )
 
 
+def ring_order(n):
+    return list(range(0, n, 2)) + list(range(n - 1, 0, -2))
+
+
+def ring_place(f, n):
+    return (f >> 1) + (f & 1) * (n - 1 - (f >> 1) * 2)
+
+
+def hop(x, n, by):
+    order = ring_order(n)
+    return lax.ppermute(x, "frames", [(order[i], order[(i + by) % n]) for i in range(n)])
+
+
+def gather_ring(streams, n):
+    found = [[block] + [None] * (n - 1) for block in streams]
+    for step in range(1, n // 2 + 1):
+        for j, blocks in enumerate(found):
+            for by in (1, -1):
+                if step < n // 2 or (j == 0) == (by == 1):
+                    blocks[by * step % n] = hop(blocks[by * (step - 1) % n], n, by)
+    return found
+
+
+def left_out(place, block, n):
+    return FR_DEV * ((place - ((place - block) & (n - 1) ^ 2)) & (n - 1))
+
+
+def frame_marks(place, blocks, n):
+    lane = lax.broadcasted_iota(jnp.int32, (TPF, HD), 1)
+    marks = []
+    for block in blocks:
+        frame = left_out(place, block, n)
+        for g in range(FR_DEV):
+            marks.append((lane == frame + g) | (lane >= n * FR_DEV))
+    return jnp.concatenate([jnp.where(mark, 1.0, 0.0) for mark in marks], axis=0).astype(jnp.bfloat16)
+
+
+def key_marks(blocks, padding, n):
+    lane = lax.broadcasted_iota(jnp.int32, (TPF, HD), 1)
+    frames = [FR_DEV * block + g for block in blocks for g in range(FR_DEV)] + [n * FR_DEV] * (padding // TPF)
+    return jnp.concatenate([jnp.where(lane == frame, -1e30, 0.0) for frame in frames], axis=0).astype(jnp.bfloat16)
+
+
+def rows_of(refs, rows, cols, padding=0):
+    pieces = [ref[rows, cols] for ref in refs]
+    if padding:
+        pieces.append(jnp.zeros((padding, HD), jnp.bfloat16))
+    return jnp.concatenate(pieces, axis=0)
+
+
+def scores_of(queries, keys):
+    return lax.dot_general(queries, keys, (((1,), (1,)), ((), ())), preferred_element_type=jnp.float32)
+
+
+def soften(scores, floor=None):
+    weights, tops = [], []
+    for r in range(0, scores.shape[0], TPF):
+        parts = [scores[r : r + TPF, c : c + HD] for c in range(0, scores.shape[1], HD)]
+        top = jnp.max(functools.reduce(jnp.maximum, parts), axis=1, keepdims=True)
+        top = jnp.broadcast_to(top, (TPF, HD))
+        if floor is not None:
+            top = jnp.maximum(top, floor[r : r + TPF])
+        weights.append(jnp.concatenate([jnp.exp2((p - top) * SCALE).astype(jnp.bfloat16) for p in parts], axis=1))
+        tops.append(top)
+    return jnp.concatenate(weights, axis=0), jnp.concatenate(tops, axis=0)
+
+
+def mix(weights, values):
+    ones = jnp.ones(values.shape, values.dtype)
+    mixed = jnp.dot(weights, jnp.concatenate([values, ones], axis=1), preferred_element_type=jnp.float32)
+    return mixed[:, :HD], mixed[:, HD:]
+
+
+TOKEN_ROWS = slice(0, ROWS)
+QUERY_ROWS = slice(ROWS, ROWS + ROWS // 2)
+
+
+def queries_of(first, second, blocks, cols):
+    pieces = [part[block][QUERY_ROWS, cols] for block in blocks for part in (first, second)]
+    return jnp.concatenate(pieces, axis=0)
+
+
+def near_kernel(heads, n, at_ref, *refs):
+    near = [d for d in range(n) if d != n // 2]
+    refs, (mixed_ref, sum_ref, top_ref) = refs[:-3], refs[-3:]
+    first, second = dict(zip(near, refs[: n - 1])), dict(zip(near, refs[n - 1 :]))
+    marks = frame_marks(at_ref[0], near, n)
+    keys_marks = key_marks(near, ROWS, n)
+    for head in range(heads):
+        cols = slice(head * HD, (head + 1) * HD)
+        queries = jnp.concatenate([queries_of(first, second, near, cols), marks], axis=1)
+        keys = rows_of([first[d] for d in near], TOKEN_ROWS, cols, ROWS)
+        values = rows_of([second[d] for d in near], TOKEN_ROWS, cols, ROWS)
+        weights, top = soften(scores_of(queries, jnp.concatenate([keys, keys_marks], axis=1)))
+        mixed_ref[head], sum_ref[head] = mix(weights, values)
+        top_ref[head] = top
+
+
+def slot_block(at_ref, slot, flip_core, n):
+    place, z, y, x, core = (at_ref[i] for i in range(5))
+    z = z ^ slot ^ (2 * y + x)
+    owner = z + (core ^ flip_core) * (n - 1 - 2 * z)
+    return (place - owner) & (n - 1)
+
+
+def finish_kernel(heads, n, at_ref, *refs):
+    far = n // 2
+    near = [d for d in range(n) if d != far]
+    first, second = refs[:n], refs[n : 2 * n]
+    mixed_ref, sum_ref, top_ref, w_ref, given_ref, attended_ref = refs[2 * n :]
+    place = at_ref[0]
+    pad = TPF
+    marks, far_marks = frame_marks(place, near, n), frame_marks(place, [far], n)
+    far_keys_marks, all_marks = key_marks([far], pad, n), key_marks(range(n), 0, n)
+    for head in range(heads):
+        cols = slice(head * HD, (head + 1) * HD)
+        queries = jnp.concatenate([queries_of(first, second, near, cols), marks], axis=1)
+        keys = jnp.concatenate([rows_of([first[far]], TOKEN_ROWS, cols, pad), far_keys_marks], axis=1)
+        before = top_ref[head]
+        weights, top = soften(scores_of(queries, keys), before)
+        mixed, total = mix(weights, rows_of([second[far]], TOKEN_ROWS, cols, pad))
+        kept = jnp.exp2((before - top) * SCALE)
+        mixed = (mixed + mixed_ref[head] * kept) / (total + sum_ref[head] * kept)
+        for i, d in enumerate(near):
+            attended_ref[d, :, cols] = mixed[i * ROWS : (i + 1) * ROWS].astype(jnp.bfloat16)
+        queries = jnp.concatenate([queries_of(first, second, [far], cols), far_marks], axis=1)
+        keys = jnp.concatenate([rows_of(first, TOKEN_ROWS, cols), all_marks], axis=1)
+        weights, _ = soften(scores_of(queries, keys))
+        mixed, total = mix(weights, rows_of(second, TOKEN_ROWS, cols))
+        attended_ref[far, :, cols] = (mixed / total).astype(jnp.bfloat16)
+    rows = jnp.concatenate([attended_ref[slot_block(at_ref, slot, 1, n)] for slot in range(n // 2)], axis=0)
+    given_ref[...] = jnp.dot(rows, w_ref[...], preferred_element_type=jnp.float32).astype(given_ref.dtype)
+
+
+def own_kernel(n, at_ref, attended_ref, w_ref, kept_ref):
+    rows = jnp.concatenate([attended_ref[slot_block(at_ref, slot, 0, n)] for slot in range(n // 2)], axis=0)
+    kept_ref[...] = jnp.dot(rows, w_ref[...], preferred_element_type=jnp.float32)
+
+
+def call(kernel, where, operands, outs, flops):
+    vmem = pl.BlockSpec(memory_space=pltpu.VMEM)
+    return pl.pallas_call(
+        kernel,
+        out_shape=[jax.ShapeDtypeStruct(shape, dtype) for shape, dtype in outs],
+        in_specs=[pl.BlockSpec(memory_space=pltpu.SMEM)] + [vmem] * len(operands),
+        out_specs=[vmem] * len(outs),
+        compiler_params=pltpu.CompilerParams(vmem_limit_bytes=20 * 1024 * 1024),
+        cost_estimate=pl.CostEstimate(flops=flops, bytes_accessed=0, transcendentals=0),
+    )(where, *operands)
+
+
+def on_device_ring(queries, keys_values, out_weight):
+    n = lax.axis_size("frames")
+    frame, head = lax.axis_index("frames"), lax.axis_index("heads")
+    z, y, x, core = frame >> 1, frame & 1, head >> 1, head & 1
+    where = jnp.stack([ring_place(frame, n), z, y, x, core]).astype(jnp.int32)
+    half = ROWS // 2
+    width, cols = out_weight.shape
+    heads = width // HD
+    streams = [
+        jnp.concatenate([keys_values[0], queries[:half]], axis=0),
+        jnp.concatenate([keys_values[1], queries[half:]], axis=0),
+    ]
+    first, second = gather_ring(streams, n)
+    f32, bf16 = jnp.float32, jnp.bfloat16
+    near = [d for d in range(n) if d != n // 2]
+    state = call(
+        functools.partial(near_kernel, heads, n),
+        where,
+        [blocks[d] for blocks in (first, second) for d in near],
+        [((heads, (n - 1) * ROWS, HD), f32)] * 3,
+        4 * (n - 1) ** 2 * ROWS**2 * width,
+    )
+    given, attended = call(
+        functools.partial(finish_kernel, heads, n),
+        where,
+        [*first, *second, *state, out_weight],
+        [((n // 2 * ROWS, cols), bf16), ((n, ROWS, width), bf16)],
+        8 * n * ROWS**2 * width,
+    )
+    from_core = lax.ppermute(given, "heads", [(h, h ^ 1) for h in range(4)])
+    (kept,) = call(
+        functools.partial(own_kernel, n),
+        where,
+        [attended, out_weight],
+        [((n // 2 * ROWS, cols), f32)],
+        n * ROWS * width * cols,
+    )
+    arrived = []
+    for slot in range(n // 2):
+        rows = slice(slot * ROWS, (slot + 1) * ROWS)
+        pairs = []
+        for f in range(n):
+            for h in range(4):
+                to = (f >> 1) ^ slot ^ (2 * (f & 1) + (h >> 1))
+                pairs.append((4 * f + h, 4 * (2 * to + (h & 1)) + (f >> 1)))
+        total = (kept[rows] + from_core[rows].astype(f32)).astype(bf16)
+        arrived.append(lax.ppermute(total, ("frames", "heads"), pairs).astype(f32))
+    low, high = (arrived[0] + arrived[1]).astype(bf16), (arrived[2] + arrived[3]).astype(bf16)
+    straight = (z ^ head) & 2 == 0
+    return jnp.concatenate([jnp.where(straight, low, high), jnp.where(straight, high, low)], axis=1)
+
+
 def solution(mesh):
     in_specs = (P("frames", "heads"), P(None, "frames", "heads"), P("heads", "frames"))
     out_specs = P("frames", "heads")
+    n, heads = mesh.shape["frames"], mesh.shape["heads"]
+    total_frames = n * FR_DEV
+    reach = min(reach_cap, (total_frames - 1) // 2)
+    every = total_frames == 2 * reach + 2 and heads == 4 and n == 2 * heads
     return jax.shard_map(
-        on_device, mesh=mesh, in_specs=in_specs, out_specs=out_specs, check_vma=False
-    )
+        on_device_ring if every else on_device_band,
+        mesh=mesh,
+        in_specs=in_specs,
+        out_specs=out_specs,
+        check_vma=False,
+    )

time: 178 us -> 66.6 us (0.37)
  the two profiles are of different devices: /device:TPU:3 before, /device:TPU:2 now
where the time goes in v5:
time: 66.6 us; the launch traced here: 66.3 us
  starting transfers between devices  29.4 us (44%)
  waiting for transfers between devices  24.5 us (37%)
  Pallas kernels  9.43 us (14%)
  local copies, waits for them, and re-layouts  1.94 us (3%)
  other arithmetic  0.96 us (1%)
    ppermute x4, starting transfers between devices, on_device_ring(): arrived.append(lax.ppermute(total, ('frames', 'heads'), pairs).astype(f32))  15 us
    ppermute x14, waiting for transfers between devices, hop(): lax.ppermute(x, 'frames', [(order[i], order[(i + by) % n]) for i in range...  14.6 us
    ppermute x14, starting transfers between devices, hop(): lax.ppermute(x, 'frames', [(order[i], order[(i + by) % n]) for i in range...  14.3 us
    pallas_call x3, Pallas kernels, call(): pl.pallas_call(kernel, out_shape=[jax.ShapeDtypeStruct(shape, dtype) for...  9.43 us
    ppermute x4, waiting for transfers between devices, on_device_ring(): arrived.append(lax.ppermute(total, ('frames', 'heads'), pairs).astype(f32))  9.17 us
  transfers between devices with their start and end apart: 19, of which 13 were waited for; matrix products, arithmetic and copies ran while one was open for 0% of the time, Pallas kernels for 8%

profile of v5, /device:TPU:2, one launch (start us, length us, event | category | flops | bytes accessed | tf_op | source)
XLA Modules:
  0.0 66.3 jit_solution(4238298242419572227)
XLA Ops:
  0.0 0.9 %fusion.4 = (bf16[48,640]{1,0:T(8,128)(2,1)S(1)}, bf16[48,640]{1,0:T(8,128)(2,1)S(1)}) fusion(bf16[96,640]{1,0:T(8,128)(2,1)} %param.3), kind=kLoop, calls=%fused_computation.17 | loop fusion | bytes 245760 | tf_op jit(solution)/shard_map/slice | solution.py:238
  0.9 1.0 %slice_bitcast_fusion = (bf16[96,640]{1,0:T(8,128)(2,1)S(1)}, bf16[96,640]{1,0:T(8,128)(2,1)S(1)}) fusion(bf16[2,96,640]{2,1,0:T(8,128)(2,1)} %param.4), kind=kLoop, calls=%fused_computation.13 | loop fusion | bytes 491520 | tf_op jit(solution)/shard_map/squeeze | solution.py:238
  1.9 1.6 %collective-permute-start = (bf16[144,640]{1,0:T(8,128)(2,1)S(1)}, bf16[144,640]{1,0:T(8,128)(2,1)S(1)}, u32[]{:S(2)}, u32[]{:S(2)}) collective-permute-start(bf16[144,640]{1,0:T(8,128)(2,1)S(1)} %pad_maximum_fusion.1.refs_0_), channel_id=1, source_target_pairs={{0,8},{8,16},{16,24},{24,28},{28,20},{20,12},{12,4},{4,0},{1,9},{9... | collective-permute-start | bytes 552968 | tf_op jit(solution)/shard_map/ppermute | solution.py:87
  4.0 1.5 %collective-permute-start.4 = (bf16[144,640]{1,0:T(8,128)(2,1)S(1)}, bf16[144,640]{1,0:T(8,128)(2,1)S(1)}, u32[]{:S(2)}, u32[]{:S(2)}) collective-permute-start(bf16[144,640]{1,0:T(8,128)(2,1)S(1)} %pad_maximum_fusion.1.refs_0_), channel_id=1, source_target_pairs={{0,4},{8,0},{16,8},{24,16},{28,24},{20,28},{12,20},{4,12},{1,5},{9... | collective-permute-start | bytes 552968 | tf_op jit(solution)/shard_map/ppermute | solution.py:87
  6.1 3.4 %collective-permute-done.refs_1_ = bf16[144,640]{1,0:T(8,128)(2,1)S(1)} collective-permute-done((bf16[144,640]{1,0:T(8,128)(2,1)S(1)}, bf16[144,640]{1,0:T(8,128)(2,1)S(1)}, u32[]{:S(2)}, u32[]{:S(2)}) %collective-permute-start) | collective-permute-done | bytes 184352 | tf_op jit(solution)/shard_map/ppermute | solution.py:87
  9.5 1.6 %collective-permute-start.1 = (bf16[144,640]{1,0:T(8,128)(2,1)S(1)}, bf16[144,640]{1,0:T(8,128)(2,1)S(1)}, u32[]{:S(2)}, u32[]{:S(2)}) collective-permute-start(bf16[144,640]{1,0:T(8,128)(2,1)S(1)} %collective-permute-done.refs_1_), channel_id=1, source_target_pairs={{0,8},{8,16},{16,24},{24,28},{28,20},{20,12},{12,4},{4,0},{1,9},{9... | collective-permute-start | bytes 552968 | tf_op jit(solution)/shard_map/ppermute | solution.py:87
  11.6 3.5 %collective-permute-done.4.refs_6_.refs_7_ = bf16[144,640]{1,0:T(8,128)(2,1)S(1)} collective-permute-done((bf16[144,640]{1,0:T(8,128)(2,1)S(1)}, bf16[144,640]{1,0:T(8,128)(2,1)S(1)}, u32[]{:S(2)}, u32[]{:S(2)}) %collective-permute-start.4) | collective-permute-done | bytes 184352 | tf_op jit(solution)/shard_map/ppermute | solution.py:87
  15.6 1.6 %collective-permute-start.8 = (bf16[144,640]{1,0:T(8,128)(2,1)S(1)}, bf16[144,640]{1,0:T(8,128)(2,1)S(1)}, u32[]{:S(2)}, u32[]{:S(2)}) collective-permute-start(bf16[144,640]{1,0:T(8,128)(2,1)S(1)} %collective-permute-done.7.refs_8_.refs_9_), channel_id=1, source_target_pairs={{0,8},{8,16},{16,24},{24,28},{28,20},{20,12},{12,4},{4,0},{1,9},{9... | collective-permute-start | bytes 552968 | tf_op jit(solution)/shard_map/ppermute | solution.py:87
  17.4 1.6 %collective-permute-start.2 = (bf16[144,640]{1,0:T(8,128)(2,1)S(1)}, bf16[144,640]{1,0:T(8,128)(2,1)S(1)}, u32[]{:S(2)}, u32[]{:S(2)}) collective-permute-start(bf16[144,640]{1,0:T(8,128)(2,1)S(1)} %collective-permute-done.1.refs_2_), channel_id=1, source_target_pairs={{0,8},{8,16},{16,24},{24,28},{28,20},{20,12},{12,4},{4,0},{1,9},{9... | collective-permute-start | bytes 552968 | tf_op jit(solution)/shard_map/ppermute | solution.py:87
  19.5 3.5 %collective-permute-done.5.refs_5_.refs_6_ = bf16[144,640]{1,0:T(8,128)(2,1)S(1)} collective-permute-done((bf16[144,640]{1,0:T(8,128)(2,1)S(1)}, bf16[144,640]{1,0:T(8,128)(2,1)S(1)}, u32[]{:S(2)}, u32[]{:S(2)}) %collective-permute-start.5) | collective-permute-done | bytes 184352 | tf_op jit(solution)/shard_map/ppermute | solution.py:87
  23.5 1.6 %collective-permute-start.9 = (bf16[144,640]{1,0:T(8,128)(2,1)S(1)}, bf16[144,640]{1,0:T(8,128)(2,1)S(1)}, u32[]{:S(2)}, u32[]{:S(2)}) collective-permute-start(bf16[144,640]{1,0:T(8,128)(2,1)S(1)} %collective-permute-done.8.refs_9_.refs_10_), channel_id=1, source_target_pairs={{0,8},{8,16},{16,24},{24,28},{28,20},{20,12},{12,4},{4,0},{1,9},{9... | collective-permute-start | bytes 552968 | tf_op jit(solution)/shard_map/ppermute | solution.py:87
  25.2 1.6 %collective-permute-start.3 = (bf16[144,640]{1,0:T(8,128)(2,1)S(1)}, bf16[144,640]{1,0:T(8,128)(2,1)S(1)}, u32[]{:S(2)}, u32[]{:S(2)}) collective-permute-start(bf16[144,640]{1,0:T(8,128)(2,1)S(1)} %collective-permute-done.2.refs_3_), channel_id=1, source_target_pairs={{0,8},{8,16},{16,24},{24,28},{28,20},{20,12},{12,4},{4,0},{1,9},{9... | collective-permute-start | bytes 552968 | tf_op jit(solution)/shard_map/ppermute | solution.py:87
  27.5 3.4 %collective-permute-done.6.refs_4_.refs_5_ = bf16[144,640]{1,0:T(8,128)(2,1)S(1)} collective-permute-done((bf16[144,640]{1,0:T(8,128)(2,1)S(1)}, bf16[144,640]{1,0:T(8,128)(2,1)S(1)}, u32[]{:S(2)}, u32[]{:S(2)}) %collective-permute-start.6) | collective-permute-done | bytes 184352 | tf_op jit(solution)/shard_map/ppermute | solution.py:87
  30.9 4.3 %shard_map.37 = (f32[5,672,128]{2,1,0:T(8,128)S(1)}, f32[5,672,128]{2,1,0:T(8,128)S(1)}, f32[5,672,128]{2,1,0:T(8,128)S(1)}) custom-call(s32[5]{0:T(128)S(1)} %stack.23.at_ref, bf16[144,640]{1,0:T(8,128)(2,1)S(1)} %pad_maximum_fusion.1.refs_0_, bf16[144,640]{1,0:T(8,128)(2,1)S(1)} %collective-permute-done.refs_1_, ...), custom_call_target="tpu_custom_call" | custom-call | flops 1156055040 | tf_op jit(solution)/shard_map/pallas_call | solution.py:218
  35.2 4.0 %shard_map.38 = (bf16[384,640]{1,0:T(8,128)(2,1)S(1)}, bf16[8,96,640]{2,1,0:T(8,128)(2,1)S(1)}) custom-call(s32[5]{0:T(128)S(1)} %stack.23.at_ref, bf16[144,640]{1,0:T(8,128)(2,1)S(1)} %pad_maximum_fusion.1.refs_0_, bf16[144,640]{1,0:T(8,128)(2,1)S(1)} %collective-permute-done.refs_1_, bf16[144,640]{1,0:T(8,128)(2,1)S(1)} %collective-permute-done.1.refs_2_, ...), custom_call_target="tpu_custom_call" | custom-call | flops 377487360 | tf_op jit(solution)/shard_map/pallas_call | solution.py:218
  39.3 1.1 %shard_map.39 = f32[384,640]{1,0:T(8,128)S(1)} custom-call(s32[5]{0:T(128)S(1)} %stack.23.at_ref, bf16[8,96,640]{2,1,0:T(8,128)(2,1)S(1)} %get-tuple-element.13.attended_ref, bf16[640,640]{1,0:T(8,128)(2,1)S(1)} %copy-done), custom_call_target="tpu_custom_call" | custom-call | flops 314572800 | tf_op jit(solution)/shard_map/pallas_call | solution.py:218
  41.3 5.4 %collective-permute-start.17 = (bf16[96,640]{1,0:T(8,128)(2,1)S(1)}, bf16[96,640]{1,0:T(8,128)(2,1)S(1)}, u32[]{:S(2)}, u32[]{:S(2)}) collective-permute-start(bf16[96,640]{1,0:T(8,128)(2,1)S(1)} %get-tuple-element.15), channel_id=1, source_target_pairs={{0,16},{1,20},{2,24},{3,28},{4,0},{5,4},{6,8},{7,12},{8,25},{9,29}... | collective-permute-start | bytes 368648 | tf_op jit(solution)/shard_map/ppermute | solution.py:274
  46.7 2.2 %collective-permute-start.18 = (bf16[96,640]{1,0:T(8,128)(2,1)S(1)}, bf16[96,640]{1,0:T(8,128)(2,1)S(1)}, u32[]{:S(2)}, u32[]{:S(2)}) collective-permute-start(bf16[96,640]{1,0:T(8,128)(2,1)S(1)} %get-tuple-element.16), channel_id=1, source_target_pairs={{0,24},{1,28},{2,16},{3,20},{4,8},{5,12},{6,0},{7,4},{8,17},{9,21}... | collective-permute-start | bytes 368648 | tf_op jit(solution)/shard_map/ppermute | solution.py:274
  48.9 3.2 %collective-permute-start.16 = (bf16[96,640]{1,0:T(8,128)(2,1)S(1)}, bf16[96,640]{1,0:T(8,128)(2,1)S(1)}, u32[]{:S(2)}, u32[]{:S(2)}) collective-permute-start(bf16[96,640]{1,0:T(8,128)(2,1)S(1)} %get-tuple-element.17), channel_id=1, source_target_pairs={{0,8},{1,12},{2,0},{3,4},{4,24},{5,28},{6,16},{7,20},{8,1},{9,5},{... | collective-permute-start | bytes 368648 | tf_op jit(solution)/shard_map/ppermute | solution.py:274
  52.2 4.2 %collective-permute-start.15 = (bf16[96,640]{1,0:T(8,128)(2,1)S(1)}, bf16[96,640]{1,0:T(8,128)(2,1)S(1)}, u32[]{:S(2)}, u32[]{:S(2)}) collective-permute-start(bf16[96,640]{1,0:T(8,128)(2,1)S(1)} %get-tuple-element.18), channel_id=1, source_target_pairs={{0,0},{1,4},{2,8},{3,12},{4,16},{5,20},{6,24},{7,28},{8,9},{9,13},... | collective-permute-start | bytes 368648 | tf_op jit(solution)/shard_map/ppermute | solution.py:274
  56.4 1.4 %collective-permute-done.18 = bf16[96,640]{1,0:T(8,128)(2,1)S(1)} collective-permute-done((bf16[96,640]{1,0:T(8,128)(2,1)S(1)}, bf16[96,640]{1,0:T(8,128)(2,1)S(1)}, u32[]{:S(2)}, u32[]{:S(2)}) %collective-permute-start.18) | collective-permute-done | bytes 122912 | tf_op jit(solution)/shard_map/ppermute | solution.py:274
  57.8 1.4 %collective-permute-done.16 = bf16[96,640]{1,0:T(8,128)(2,1)S(1)} collective-permute-done((bf16[96,640]{1,0:T(8,128)(2,1)S(1)}, bf16[96,640]{1,0:T(8,128)(2,1)S(1)}, u32[]{:S(2)}, u32[]{:S(2)}) %collective-permute-start.16) | collective-permute-done | bytes 122912 | tf_op jit(solution)/shard_map/ppermute | solution.py:274
  59.2 6.4 %collective-permute-done.15 = bf16[96,640]{1,0:T(8,128)(2,1)S(1)} collective-permute-done((bf16[96,640]{1,0:T(8,128)(2,1)S(1)}, bf16[96,640]{1,0:T(8,128)(2,1)S(1)}, u32[]{:S(2)}, u32[]{:S(2)}) %collective-permute-start.15) | collective-permute-done | bytes 122912 | tf_op jit(solution)/shard_map/ppermute | solution.py:274
  65.6 0.7 %pad_maximum_fusion = bf16[96,1280]{1,0:T(8,128)(2,1)} fusion(bf16[96,640]{1,0:T(8,128)(2,1)S(1)} %get-tuple-element.20, bf16[96,640]{1,0:T(8,128)(2,1)S(1)} %get-tuple-element.19), kind=kLoop, calls=%fused_computation.8 | loop fusion | flops 491520 | bytes 491520 | tf_op jit(solution)/shard_map/concatenate | solution.py:277
  (27 shorter events, 5.2 us)
Async XLA Ops:
  1.9 7.6 %collective-permute-start = (bf16[144,640]{1,0:T(8,128)(2,1)S(1)}, bf16[144,640]{1,0:T(8,128)(2,1)S(1)}, u32[]{:S(2)}, u32[]{:S(2)}) collective-permute-start(bf16[144,640]{1,0:T(8,128)(2,1)S(1)} %pad_maximum_fusion.1.refs_0_), channel_id=1, source_target_pairs={{0,8},{8,16},{16,24},{24,28},{28,20},{20,12},{12,4},{4,0},{1,9},{9... | collective-permute-start | bytes 552968 | tf_op jit(solution)/shard_map/ppermute | solution.py:87
  3.5 7.6 %collective-permute-start.10 = (bf16[144,640]{1,0:T(8,128)(2,1)S(1)}, bf16[144,640]{1,0:T(8,128)(2,1)S(1)}, u32[]{:S(2)}, u32[]{:S(2)}) collective-permute-start(bf16[144,640]{1,0:T(8,128)(2,1)S(1)} %pad_maximum_fusion.2.refs_7_.refs_8_), channel_id=1, source_target_pairs={{0,4},{8,0},{16,8},{24,16},{28,24},{20,28},{12,20},{4,12},{1,5},{9... | collective-permute-start | bytes 552968 | tf_op jit(solution)/shard_map/ppermute | solution.py:87
  4.0 11.1 %collective-permute-start.4 = (bf16[144,640]{1,0:T(8,128)(2,1)S(1)}, bf16[144,640]{1,0:T(8,128)(2,1)S(1)}, u32[]{:S(2)}, u32[]{:S(2)}) collective-permute-start(bf16[144,640]{1,0:T(8,128)(2,1)S(1)} %pad_maximum_fusion.1.refs_0_), channel_id=1, source_target_pairs={{0,4},{8,0},{16,8},{24,16},{28,24},{20,28},{12,20},{4,12},{1,5},{9... | collective-permute-start | bytes 552968 | tf_op jit(solution)/shard_map/ppermute | solution.py:87
  5.6 10.0 %collective-permute-start.7 = (bf16[144,640]{1,0:T(8,128)(2,1)S(1)}, bf16[144,640]{1,0:T(8,128)(2,1)S(1)}, u32[]{:S(2)}, u32[]{:S(2)}) collective-permute-start(bf16[144,640]{1,0:T(8,128)(2,1)S(1)} %pad_maximum_fusion.2.refs_7_.refs_8_), channel_id=1, source_target_pairs={{0,8},{8,16},{16,24},{24,28},{28,20},{20,12},{12,4},{4,0},{1,9},{9... | collective-permute-start | bytes 552968 | tf_op jit(solution)/shard_map/ppermute | solution.py:87
  9.5 7.9 %collective-permute-start.1 = (bf16[144,640]{1,0:T(8,128)(2,1)S(1)}, bf16[144,640]{1,0:T(8,128)(2,1)S(1)}, u32[]{:S(2)}, u32[]{:S(2)}) collective-permute-start(bf16[144,640]{1,0:T(8,128)(2,1)S(1)} %collective-permute-done.refs_1_), channel_id=1, source_target_pairs={{0,8},{8,16},{16,24},{24,28},{28,20},{20,12},{12,4},{4,0},{1,9},{9... | collective-permute-start | bytes 552968 | tf_op jit(solution)/shard_map/ppermute | solution.py:87
  11.2 7.9 %collective-permute-start.11 = (bf16[144,640]{1,0:T(8,128)(2,1)S(1)}, bf16[144,640]{1,0:T(8,128)(2,1)S(1)}, u32[]{:S(2)}, u32[]{:S(2)}) collective-permute-start(bf16[144,640]{1,0:T(8,128)(2,1)S(1)} %collective-permute-done.10.refs_13_.refs_15_), channel_id=1, source_target_pairs={{0,4},{8,0},{16,8},{24,16},{28,24},{20,28},{12,20},{4,12},{1,5},{9... | collective-permute-start | bytes 552968 | tf_op jit(solution)/shard_map/ppermute | solution.py:87
  15.1 7.9 %collective-permute-start.5 = (bf16[144,640]{1,0:T(8,128)(2,1)S(1)}, bf16[144,640]{1,0:T(8,128)(2,1)S(1)}, u32[]{:S(2)}, u32[]{:S(2)}) collective-permute-start(bf16[144,640]{1,0:T(8,128)(2,1)S(1)} %collective-permute-done.4.refs_6_.refs_7_), channel_id=1, source_target_pairs={{0,4},{8,0},{16,8},{24,16},{28,24},{20,28},{12,20},{4,12},{1,5},{9... | collective-permute-start | bytes 552968 | tf_op jit(solution)/shard_map/ppermute | solution.py:87
  15.6 7.9 %collective-permute-start.8 = (bf16[144,640]{1,0:T(8,128)(2,1)S(1)}, bf16[144,640]{1,0:T(8,128)(2,1)S(1)}, u32[]{:S(2)}, u32[]{:S(2)}) collective-permute-start(bf16[144,640]{1,0:T(8,128)(2,1)S(1)} %collective-permute-done.7.refs_8_.refs_9_), channel_id=1, source_target_pairs={{0,8},{8,16},{16,24},{24,28},{28,20},{20,12},{12,4},{4,0},{1,9},{9... | collective-permute-start | bytes 552968 | tf_op jit(solution)/shard_map/ppermute | solution.py:87
  17.4 7.8 %collective-permute-start.2 = (bf16[144,640]{1,0:T(8,128)(2,1)S(1)}, bf16[144,640]{1,0:T(8,128)(2,1)S(1)}, u32[]{:S(2)}, u32[]{:S(2)}) collective-permute-start(bf16[144,640]{1,0:T(8,128)(2,1)S(1)} %collective-permute-done.1.refs_2_), channel_id=1, source_target_pairs={{0,8},{8,16},{16,24},{24,28},{28,20},{20,12},{12,4},{4,0},{1,9},{9... | collective-permute-start | bytes 552968 | tf_op jit(solution)/shard_map/ppermute | solution.py:87
  19.1 7.9 %collective-permute-start.12 = (bf16[144,640]{1,0:T(8,128)(2,1)S(1)}, bf16[144,640]{1,0:T(8,128)(2,1)S(1)}, u32[]{:S(2)}, u32[]{:S(2)}) collective-permute-start(bf16[144,640]{1,0:T(8,128)(2,1)S(1)} %collective-permute-done.11.refs_12_.refs_14_), channel_id=1, source_target_pairs={{0,4},{8,0},{16,8},{24,16},{28,24},{20,28},{12,20},{4,12},{1,5},{9... | collective-permute-start | bytes 552968 | tf_op jit(solution)/shard_map/ppermute | solution.py:87
  23.0 7.9 %collective-permute-start.6 = (bf16[144,640]{1,0:T(8,128)(2,1)S(1)}, bf16[144,640]{1,0:T(8,128)(2,1)S(1)}, u32[]{:S(2)}, u32[]{:S(2)}) collective-permute-start(bf16[144,640]{1,0:T(8,128)(2,1)S(1)} %collective-permute-done.5.refs_5_.refs_6_), channel_id=1, source_target_pairs={{0,4},{8,0},{16,8},{24,16},{28,24},{20,28},{12,20},{4,12},{1,5},{9... | collective-permute-start | bytes 552968 | tf_op jit(solution)/shard_map/ppermute | solution.py:87
  23.5 7.4 %collective-permute-start.9 = (bf16[144,640]{1,0:T(8,128)(2,1)S(1)}, bf16[144,640]{1,0:T(8,128)(2,1)S(1)}, u32[]{:S(2)}, u32[]{:S(2)}) collective-permute-start(bf16[144,640]{1,0:T(8,128)(2,1)S(1)} %collective-permute-done.8.refs_9_.refs_10_), channel_id=1, source_target_pairs={{0,8},{8,16},{16,24},{24,28},{28,20},{20,12},{12,4},{4,0},{1,9},{9... | collective-permute-start | bytes 552968 | tf_op jit(solution)/shard_map/ppermute | solution.py:87
  25.2 10.0 %collective-permute-start.3 = (bf16[144,640]{1,0:T(8,128)(2,1)S(1)}, bf16[144,640]{1,0:T(8,128)(2,1)S(1)}, u32[]{:S(2)}, u32[]{:S(2)}) collective-permute-start(bf16[144,640]{1,0:T(8,128)(2,1)S(1)} %collective-permute-done.2.refs_3_), channel_id=1, source_target_pairs={{0,8},{8,16},{16,24},{24,28},{28,20},{20,12},{12,4},{4,0},{1,9},{9... | collective-permute-start | bytes 552968 | tf_op jit(solution)/shard_map/ppermute | solution.py:87
  27.0 8.2 %collective-permute-start.13 = (bf16[144,640]{1,0:T(8,128)(2,1)S(1)}, bf16[144,640]{1,0:T(8,128)(2,1)S(1)}, u32[]{:S(2)}, u32[]{:S(2)}) collective-permute-start(bf16[144,640]{1,0:T(8,128)(2,1)S(1)} %collective-permute-done.12.refs_11_.refs_13_), channel_id=1, source_target_pairs={{0,4},{8,0},{16,8},{24,16},{28,24},{20,28},{12,20},{4,12},{1,5},{9... | collective-permute-start | bytes 552968 | tf_op jit(solution)/shard_map/ppermute | solution.py:87
  27.5 7.7 %copy-start = (bf16[640,640]{1,0:T(8,128)(2,1)S(1)}, bf16[640,640]{1,0:T(8,128)(2,1)}, u32[]{:S(2)}) copy-start(bf16[640,640]{1,0:T(8,128)(2,1)} %w_ref.1) | copy-start | bytes 2457604
  39.2 1.9 %collective-permute-start.14 = (bf16[384,640]{1,0:T(8,128)(2,1)S(1)}, bf16[384,640]{1,0:T(8,128)(2,1)S(1)}, u32[]{:S(2)}, u32[]{:S(2)}) collective-permute-start(bf16[384,640]{1,0:T(8,128)(2,1)S(1)} %get-tuple-element.14), channel_id=1, source_target_pairs={{0,1},{1,0},{2,3},{3,2},{4,5},{5,4},{6,7},{7,6},{8,9},{9,8},{10,11... | collective-permute-start | bytes 1474568 | tf_op jit(solution)/shard_map/ppermute | solution.py:257
  41.3 15.1 %collective-permute-start.17 = (bf16[96,640]{1,0:T(8,128)(2,1)S(1)}, bf16[96,640]{1,0:T(8,128)(2,1)S(1)}, u32[]{:S(2)}, u32[]{:S(2)}) collective-permute-start(bf16[96,640]{1,0:T(8,128)(2,1)S(1)} %get-tuple-element.15), channel_id=1, source_target_pairs={{0,16},{1,20},{2,24},{3,28},{4,0},{5,4},{6,8},{7,12},{8,25},{9,29}... | collective-permute-start | bytes 368648 | tf_op jit(solution)/shard_map/ppermute | solution.py:274
  46.7 11.1 %collective-permute-start.18 = (bf16[96,640]{1,0:T(8,128)(2,1)S(1)}, bf16[96,640]{1,0:T(8,128)(2,1)S(1)}, u32[]{:S(2)}, u32[]{:S(2)}) collective-permute-start(bf16[96,640]{1,0:T(8,128)(2,1)S(1)} %get-tuple-element.16), channel_id=1, source_target_pairs={{0,24},{1,28},{2,16},{3,20},{4,8},{5,12},{6,0},{7,4},{8,17},{9,21}... | collective-permute-start | bytes 368648 | tf_op jit(solution)/shard_map/ppermute | solution.py:274
  48.9 10.2 %collective-permute-start.16 = (bf16[96,640]{1,0:T(8,128)(2,1)S(1)}, bf16[96,640]{1,0:T(8,128)(2,1)S(1)}, u32[]{:S(2)}, u32[]{:S(2)}) collective-permute-start(bf16[96,640]{1,0:T(8,128)(2,1)S(1)} %get-tuple-element.17), channel_id=1, source_target_pairs={{0,8},{1,12},{2,0},{3,4},{4,24},{5,28},{6,16},{7,20},{8,1},{9,5},{... | collective-permute-start | bytes 368648 | tf_op jit(solution)/shard_map/ppermute | solution.py:274
  52.2 13.4 %collective-permute-start.15 = (bf16[96,640]{1,0:T(8,128)(2,1)S(1)}, bf16[96,640]{1,0:T(8,128)(2,1)S(1)}, u32[]{:S(2)}, u32[]{:S(2)}) collective-permute-start(bf16[96,640]{1,0:T(8,128)(2,1)S(1)} %get-tuple-element.18), channel_id=1, source_target_pairs={{0,0},{1,4},{2,8},{3,12},{4,16},{5,20},{6,24},{7,28},{8,9},{9,13},... | collective-permute-start | bytes 368648 | tf_op jit(solution)/shard_map/ppermute | solution.py:274

commit v6 on v5

--- a/solution.py
+++ b/solution.py
@@ -173,8 +173,8 @@
 
 
 def slot_block(at_ref, slot, flip_core, n):
-    place, z, y, x, core = (at_ref[i] for i in range(5))
-    z = z ^ slot ^ (2 * y + x)
+    place, y, x, core = (at_ref[i] for i in range(4))
+    z = slot ^ (2 * y + x)
     owner = z + (core ^ flip_core) * (n - 1 - 2 * z)
     return (place - owner) & (n - 1)
 
@@ -229,7 +229,7 @@
     n = lax.axis_size("frames")
     frame, head = lax.axis_index("frames"), lax.axis_index("heads")
     z, y, x, core = frame >> 1, frame & 1, head >> 1, head & 1
-    where = jnp.stack([ring_place(frame, n), z, y, x, core]).astype(jnp.int32)
+    where = jnp.stack([ring_place(frame, n), y, x, core]).astype(jnp.int32)
     half = ROWS // 2
     width, cols = out_weight.shape
     heads = width // HD
@@ -268,12 +268,12 @@
         pairs = []
         for f in range(n):
             for h in range(4):
-                to = (f >> 1) ^ slot ^ (2 * (f & 1) + (h >> 1))
+                to = slot ^ (2 * (f & 1) + (h >> 1))
                 pairs.append((4 * f + h, 4 * (2 * to + (h & 1)) + (f >> 1)))
         total = (kept[rows] + from_core[rows].astype(f32)).astype(bf16)
         arrived.append(lax.ppermute(total, ("frames", "heads"), pairs).astype(f32))
     low, high = (arrived[0] + arrived[1]).astype(bf16), (arrived[2] + arrived[3]).astype(bf16)
-    straight = (z ^ head) & 2 == 0
+    straight = z & 2 == 0
     return jnp.concatenate([jnp.where(straight, low, high), jnp.where(straight, high, low)], axis=1)
 
 

time: 66.6 us -> 63.3 us (0.950)
  the two profiles are of different devices: /device:TPU:2 before, /device:TPU:5 now
where the time goes in v6:
time: 63.3 us; the launch traced here: 63.1 us
  starting transfers between devices  25.7 us (41%)
  waiting for transfers between devices  24.9 us (39%)
  Pallas kernels  9.43 us (15%)
  local copies, waits for them, and re-layouts  1.86 us (3%)
  other arithmetic  1.04 us (2%)
    ppermute x14, waiting for transfers between devices, hop(): lax.ppermute(x, 'frames', [(order[i], order[(i + by) % n]) for i in range...  14.8 us
    ppermute x4, starting transfers between devices, on_device_ring(): arrived.append(lax.ppermute(total, ('frames', 'heads'), pairs).astype(f32))  11.7 us
    ppermute x14, starting transfers between devices, hop(): lax.ppermute(x, 'frames', [(order[i], order[(i + by) % n]) for i in range...  10.6 us
    ppermute x4, waiting for transfers between devices, on_device_ring(): arrived.append(lax.ppermute(total, ('frames', 'heads'), pairs).astype(f32))  9.83 us
    pallas_call x3, Pallas kernels, call(): pl.pallas_call(kernel, out_shape=[jax.ShapeDtypeStruct(shape, dtype) for...  9.43 us
    ppermute x1, starting transfers between devices, on_device_ring(): from_core = lax.ppermute(given, 'heads', [(h, h ^ 1) for h in range(4)])  3.44 us
  transfers between devices with their start and end apart: 19, of which 9 were waited for; matrix products, arithmetic and copies ran while one was open for 0% of the time, Pallas kernels for 9%

profile of v6, /device:TPU:5, one launch (start us, length us, event | category | flops | bytes accessed | tf_op | source)
XLA Modules:
  0.0 63.1 jit_solution(17840336355588902301)
XLA Ops:
  0.0 0.9 %fusion.4 = (bf16[48,640]{1,0:T(8,128)(2,1)S(1)}, bf16[48,640]{1,0:T(8,128)(2,1)S(1)}) fusion(bf16[96,640]{1,0:T(8,128)(2,1)} %param.3), kind=kLoop, calls=%fused_computation.18 | loop fusion | bytes 245760 | tf_op jit(solution)/shard_map/slice | solution.py:238
  0.9 1.0 %slice_bitcast_fusion = (bf16[96,640]{1,0:T(8,128)(2,1)S(1)}, bf16[96,640]{1,0:T(8,128)(2,1)S(1)}) fusion(bf16[2,96,640]{2,1,0:T(8,128)(2,1)} %param.4), kind=kLoop, calls=%fused_computation.13 | loop fusion | bytes 491520 | tf_op jit(solution)/shard_map/squeeze | solution.py:238
  2.0 1.5 %collective-permute-start.10 = (bf16[144,640]{1,0:T(8,128)(2,1)S(1)}, bf16[144,640]{1,0:T(8,128)(2,1)S(1)}, u32[]{:S(2)}, u32[]{:S(2)}) collective-permute-start(bf16[144,640]{1,0:T(8,128)(2,1)S(1)} %pad_maximum_fusion.2.refs_7_.refs_8_), channel_id=1, source_target_pairs={{0,4},{8,0},{16,8},{24,16},{28,24},{20,28},{12,20},{4,12},{1,5},{9... | collective-permute-start | bytes 552968 | tf_op jit(solution)/shard_map/ppermute | solution.py:87
  3.5 1.3 %collective-permute-start.4 = (bf16[144,640]{1,0:T(8,128)(2,1)S(1)}, bf16[144,640]{1,0:T(8,128)(2,1)S(1)}, u32[]{:S(2)}, u32[]{:S(2)}) collective-permute-start(bf16[144,640]{1,0:T(8,128)(2,1)S(1)} %pad_maximum_fusion.1.refs_0_), channel_id=1, source_target_pairs={{0,4},{8,0},{16,8},{24,16},{28,24},{20,28},{12,20},{4,12},{1,5},{9... | collective-permute-start | bytes 552968 | tf_op jit(solution)/shard_map/ppermute | solution.py:87
  4.9 2.5 %collective-permute-done.refs_1_ = bf16[144,640]{1,0:T(8,128)(2,1)S(1)} collective-permute-done((bf16[144,640]{1,0:T(8,128)(2,1)S(1)}, bf16[144,640]{1,0:T(8,128)(2,1)S(1)}, u32[]{:S(2)}, u32[]{:S(2)}) %collective-permute-start) | collective-permute-done | bytes 184352 | tf_op jit(solution)/shard_map/ppermute | solution.py:87
  7.8 1.1 %collective-permute-start.11 = (bf16[144,640]{1,0:T(8,128)(2,1)S(1)}, bf16[144,640]{1,0:T(8,128)(2,1)S(1)}, u32[]{:S(2)}, u32[]{:S(2)}) collective-permute-start(bf16[144,640]{1,0:T(8,128)(2,1)S(1)} %collective-permute-done.10.refs_13_.refs_15_), channel_id=1, source_target_pairs={{0,4},{8,0},{16,8},{24,16},{28,24},{20,28},{12,20},{4,12},{1,5},{9... | collective-permute-start | bytes 552968 | tf_op jit(solution)/shard_map/ppermute | solution.py:87
  8.9 2.6 %collective-permute-done.4.refs_6_.refs_7_ = bf16[144,640]{1,0:T(8,128)(2,1)S(1)} collective-permute-done((bf16[144,640]{1,0:T(8,128)(2,1)S(1)}, bf16[144,640]{1,0:T(8,128)(2,1)S(1)}, u32[]{:S(2)}, u32[]{:S(2)}) %collective-permute-start.4) | collective-permute-done | bytes 184352 | tf_op jit(solution)/shard_map/ppermute | solution.py:87
  11.5 1.1 %collective-permute-start.5 = (bf16[144,640]{1,0:T(8,128)(2,1)S(1)}, bf16[144,640]{1,0:T(8,128)(2,1)S(1)}, u32[]{:S(2)}, u32[]{:S(2)}) collective-permute-start(bf16[144,640]{1,0:T(8,128)(2,1)S(1)} %collective-permute-done.4.refs_6_.refs_7_), channel_id=1, source_target_pairs={{0,4},{8,0},{16,8},{24,16},{28,24},{20,28},{12,20},{4,12},{1,5},{9... | collective-permute-start | bytes 552968 | tf_op jit(solution)/shard_map/ppermute | solution.py:87
  13.0 2.4 %collective-permute-done.1.refs_2_ = bf16[144,640]{1,0:T(8,128)(2,1)S(1)} collective-permute-done((bf16[144,640]{1,0:T(8,128)(2,1)S(1)}, bf16[144,640]{1,0:T(8,128)(2,1)S(1)}, u32[]{:S(2)}, u32[]{:S(2)}) %collective-permute-start.1) | collective-permute-done | bytes 184352 | tf_op jit(solution)/shard_map/ppermute | solution.py:87
  15.5 1.4 %collective-permute-start.12 = (bf16[144,640]{1,0:T(8,128)(2,1)S(1)}, bf16[144,640]{1,0:T(8,128)(2,1)S(1)}, u32[]{:S(2)}, u32[]{:S(2)}) collective-permute-start(bf16[144,640]{1,0:T(8,128)(2,1)S(1)} %collective-permute-done.11.refs_12_.refs_14_), channel_id=1, source_target_pairs={{0,4},{8,0},{16,8},{24,16},{28,24},{20,28},{12,20},{4,12},{1,5},{9... | collective-permute-start | bytes 552968 | tf_op jit(solution)/shard_map/ppermute | solution.py:87
  16.9 2.5 %collective-permute-done.5.refs_5_.refs_6_ = bf16[144,640]{1,0:T(8,128)(2,1)S(1)} collective-permute-done((bf16[144,640]{1,0:T(8,128)(2,1)S(1)}, bf16[144,640]{1,0:T(8,128)(2,1)S(1)}, u32[]{:S(2)}, u32[]{:S(2)}) %collective-permute-start.5) | collective-permute-done | bytes 184352 | tf_op jit(solution)/shard_map/ppermute | solution.py:87
  19.4 1.1 %collective-permute-start.6 = (bf16[144,640]{1,0:T(8,128)(2,1)S(1)}, bf16[144,640]{1,0:T(8,128)(2,1)S(1)}, u32[]{:S(2)}, u32[]{:S(2)}) collective-permute-start(bf16[144,640]{1,0:T(8,128)(2,1)S(1)} %collective-permute-done.5.refs_5_.refs_6_), channel_id=1, source_target_pairs={{0,4},{8,0},{16,8},{24,16},{28,24},{20,28},{12,20},{4,12},{1,5},{9... | collective-permute-start | bytes 552968 | tf_op jit(solution)/shard_map/ppermute | solution.py:87
  22.1 1.3 %collective-permute-done.12.refs_11_.refs_13_ = bf16[144,640]{1,0:T(8,128)(2,1)S(1)} collective-permute-done((bf16[144,640]{1,0:T(8,128)(2,1)S(1)}, bf16[144,640]{1,0:T(8,128)(2,1)S(1)}, u32[]{:S(2)}, u32[]{:S(2)}) %collective-permute-start.12) | collective-permute-done | bytes 184352 | tf_op jit(solution)/shard_map/ppermute | solution.py:87
  23.4 1.1 %collective-permute-start.13 = (bf16[144,640]{1,0:T(8,128)(2,1)S(1)}, bf16[144,640]{1,0:T(8,128)(2,1)S(1)}, u32[]{:S(2)}, u32[]{:S(2)}) collective-permute-start(bf16[144,640]{1,0:T(8,128)(2,1)S(1)} %collective-permute-done.12.refs_11_.refs_13_), channel_id=1, source_target_pairs={{0,4},{8,0},{16,8},{24,16},{28,24},{20,28},{12,20},{4,12},{1,5},{9... | collective-permute-start | bytes 552968 | tf_op jit(solution)/shard_map/ppermute | solution.py:87
  24.5 2.8 %collective-permute-done.6.refs_4_.refs_5_ = bf16[144,640]{1,0:T(8,128)(2,1)S(1)} collective-permute-done((bf16[144,640]{1,0:T(8,128)(2,1)S(1)}, bf16[144,640]{1,0:T(8,128)(2,1)S(1)}, u32[]{:S(2)}, u32[]{:S(2)}) %collective-permute-start.6) | collective-permute-done | bytes 184352 | tf_op jit(solution)/shard_map/ppermute | solution.py:87
  27.3 4.3 %shard_map.37 = (f32[5,672,128]{2,1,0:T(8,128)S(1)}, f32[5,672,128]{2,1,0:T(8,128)S(1)}, f32[5,672,128]{2,1,0:T(8,128)S(1)}) custom-call(s32[4]{0:T(128)S(1)} %pad_add_fusion.at_ref, bf16[144,640]{1,0:T(8,128)(2,1)S(1)} %pad_maximum_fusion.1.refs_0_, bf16[144,640]{1,0:T(8,128)(2,1)S(1)} %collective-permute-done.refs_1_, ...), custom_call_target="tpu_custom_call" | custom-call | flops 1156055040 | tf_op jit(solution)/shard_map/pallas_call | solution.py:218
  31.6 4.0 %shard_map.38 = (bf16[384,640]{1,0:T(8,128)(2,1)S(1)}, bf16[8,96,640]{2,1,0:T(8,128)(2,1)S(1)}) custom-call(s32[4]{0:T(128)S(1)} %pad_add_fusion.at_ref, bf16[144,640]{1,0:T(8,128)(2,1)S(1)} %pad_maximum_fusion.1.refs_0_, bf16[144,640]{1,0:T(8,128)(2,1)S(1)} %collective-permute-done.refs_1_, bf16[144,640]{1,0:T(8,128)(2,1)S(1)} %collective-permute-done.1.refs_2_, ...), custom_call_target="tpu_custom_call" | custom-call | flops 377487360 | tf_op jit(solution)/shard_map/pallas_call | solution.py:218
  35.7 3.4 %collective-permute-start.14 = (bf16[384,640]{1,0:T(8,128)(2,1)S(1)}, bf16[384,640]{1,0:T(8,128)(2,1)S(1)}, u32[]{:S(2)}, u32[]{:S(2)}) collective-permute-start(bf16[384,640]{1,0:T(8,128)(2,1)S(1)} %get-tuple-element.14), channel_id=1, source_target_pairs={{0,1},{1,0},{2,3},{3,2},{4,5},{5,4},{6,7},{7,6},{8,9},{9,8},{10,11... | collective-permute-start | bytes 1474568 | tf_op jit(solution)/shard_map/ppermute | solution.py:257
  39.1 1.1 %shard_map.39 = f32[384,640]{1,0:T(8,128)S(1)} custom-call(s32[4]{0:T(128)S(1)} %pad_add_fusion.at_ref, bf16[8,96,640]{2,1,0:T(8,128)(2,1)S(1)} %get-tuple-element.13.attended_ref, bf16[640,640]{1,0:T(8,128)(2,1)S(1)} %copy-done), custom_call_target="tpu_custom_call" | custom-call | flops 314572800 | tf_op jit(solution)/shard_map/pallas_call | solution.py:218
  41.2 4.1 %collective-permute-start.18 = (bf16[96,640]{1,0:T(8,128)(2,1)S(1)}, bf16[96,640]{1,0:T(8,128)(2,1)S(1)}, u32[]{:S(2)}, u32[]{:S(2)}) collective-permute-start(bf16[96,640]{1,0:T(8,128)(2,1)S(1)} %get-tuple-element.16), channel_id=1, source_target_pairs={{0,24},{1,28},{2,16},{3,20},{4,8},{5,12},{6,0},{7,4},{8,25},{9,29}... | collective-permute-start | bytes 368648 | tf_op jit(solution)/shard_map/ppermute | solution.py:274
  45.2 5.3 %collective-permute-start.16 = (bf16[96,640]{1,0:T(8,128)(2,1)S(1)}, bf16[96,640]{1,0:T(8,128)(2,1)S(1)}, u32[]{:S(2)}, u32[]{:S(2)}) collective-permute-start(bf16[96,640]{1,0:T(8,128)(2,1)S(1)} %get-tuple-element.17), channel_id=1, source_target_pairs={{0,8},{1,12},{2,0},{3,4},{4,24},{5,28},{6,16},{7,20},{8,9},{9,13},... | collective-permute-start | bytes 368648 | tf_op jit(solution)/shard_map/ppermute | solution.py:274
  50.5 1.9 %collective-permute-start.15 = (bf16[96,640]{1,0:T(8,128)(2,1)S(1)}, bf16[96,640]{1,0:T(8,128)(2,1)S(1)}, u32[]{:S(2)}, u32[]{:S(2)}) collective-permute-start(bf16[96,640]{1,0:T(8,128)(2,1)S(1)} %get-tuple-element.18), channel_id=1, source_target_pairs={{0,0},{1,4},{2,8},{3,12},{4,16},{5,20},{6,24},{7,28},{8,1},{9,5},{... | collective-permute-start | bytes 368648 | tf_op jit(solution)/shard_map/ppermute | solution.py:274
  52.5 9.8 %collective-permute-done.15 = bf16[96,640]{1,0:T(8,128)(2,1)S(1)} collective-permute-done((bf16[96,640]{1,0:T(8,128)(2,1)S(1)}, bf16[96,640]{1,0:T(8,128)(2,1)S(1)}, u32[]{:S(2)}, u32[]{:S(2)}) %collective-permute-start.15) | collective-permute-done | bytes 122912 | tf_op jit(solution)/shard_map/ppermute | solution.py:274
  62.4 0.7 %pad_maximum_fusion = bf16[96,1280]{1,0:T(8,128)(2,1)} fusion(bf16[96,640]{1,0:T(8,128)(2,1)S(1)} %get-tuple-element.20, bf16[96,640]{1,0:T(8,128)(2,1)S(1)} %get-tuple-element.19), kind=kLoop, calls=%fused_computation.8 | loop fusion | flops 491520 | bytes 491520 | tf_op jit(solution)/shard_map/concatenate | solution.py:277
  (27 shorter events, 3.6 us)
Async XLA Ops:
  1.9 5.6 %collective-permute-start = (bf16[144,640]{1,0:T(8,128)(2,1)S(1)}, bf16[144,640]{1,0:T(8,128)(2,1)S(1)}, u32[]{:S(2)}, u32[]{:S(2)}) collective-permute-start(bf16[144,640]{1,0:T(8,128)(2,1)S(1)} %pad_maximum_fusion.1.refs_0_), channel_id=1, source_target_pairs={{0,8},{8,16},{16,24},{24,28},{28,20},{20,12},{12,4},{4,0},{1,9},{9... | collective-permute-start | bytes 552968 | tf_op jit(solution)/shard_map/ppermute | solution.py:87
  2.0 5.8 %collective-permute-start.10 = (bf16[144,640]{1,0:T(8,128)(2,1)S(1)}, bf16[144,640]{1,0:T(8,128)(2,1)S(1)}, u32[]{:S(2)}, u32[]{:S(2)}) collective-permute-start(bf16[144,640]{1,0:T(8,128)(2,1)S(1)} %pad_maximum_fusion.2.refs_7_.refs_8_), channel_id=1, source_target_pairs={{0,4},{8,0},{16,8},{24,16},{28,24},{20,28},{12,20},{4,12},{1,5},{9... | collective-permute-start | bytes 552968 | tf_op jit(solution)/shard_map/ppermute | solution.py:87
  3.5 8.1 %collective-permute-start.4 = (bf16[144,640]{1,0:T(8,128)(2,1)S(1)}, bf16[144,640]{1,0:T(8,128)(2,1)S(1)}, u32[]{:S(2)}, u32[]{:S(2)}) collective-permute-start(bf16[144,640]{1,0:T(8,128)(2,1)S(1)} %pad_maximum_fusion.1.refs_0_), channel_id=1, source_target_pairs={{0,4},{8,0},{16,8},{24,16},{28,24},{20,28},{12,20},{4,12},{1,5},{9... | collective-permute-start | bytes 552968 | tf_op jit(solution)/shard_map/ppermute | solution.py:87
  4.8 7.8 %collective-permute-start.7 = (bf16[144,640]{1,0:T(8,128)(2,1)S(1)}, bf16[144,640]{1,0:T(8,128)(2,1)S(1)}, u32[]{:S(2)}, u32[]{:S(2)}) collective-permute-start(bf16[144,640]{1,0:T(8,128)(2,1)S(1)} %pad_maximum_fusion.2.refs_7_.refs_8_), channel_id=1, source_target_pairs={{0,8},{8,16},{16,24},{24,28},{28,20},{20,12},{12,4},{4,0},{1,9},{9... | collective-permute-start | bytes 552968 | tf_op jit(solution)/shard_map/ppermute | solution.py:87
  7.4 8.0 %collective-permute-start.1 = (bf16[144,640]{1,0:T(8,128)(2,1)S(1)}, bf16[144,640]{1,0:T(8,128)(2,1)S(1)}, u32[]{:S(2)}, u32[]{:S(2)}) collective-permute-start(bf16[144,640]{1,0:T(8,128)(2,1)S(1)} %collective-permute-done.refs_1_), channel_id=1, source_target_pairs={{0,8},{8,16},{16,24},{24,28},{28,20},{20,12},{12,4},{4,0},{1,9},{9... | collective-permute-start | bytes 552968 | tf_op jit(solution)/shard_map/ppermute | solution.py:87
  7.8 7.7 %collective-permute-start.11 = (bf16[144,640]{1,0:T(8,128)(2,1)S(1)}, bf16[144,640]{1,0:T(8,128)(2,1)S(1)}, u32[]{:S(2)}, u32[]{:S(2)}) collective-permute-start(bf16[144,640]{1,0:T(8,128)(2,1)S(1)} %collective-permute-done.10.refs_13_.refs_15_), channel_id=1, source_target_pairs={{0,4},{8,0},{16,8},{24,16},{28,24},{20,28},{12,20},{4,12},{1,5},{9... | collective-permute-start | bytes 552968 | tf_op jit(solution)/shard_map/ppermute | solution.py:87
  11.5 7.9 %collective-permute-start.5 = (bf16[144,640]{1,0:T(8,128)(2,1)S(1)}, bf16[144,640]{1,0:T(8,128)(2,1)S(1)}, u32[]{:S(2)}, u32[]{:S(2)}) collective-permute-start(bf16[144,640]{1,0:T(8,128)(2,1)S(1)} %collective-permute-done.4.refs_6_.refs_7_), channel_id=1, source_target_pairs={{0,4},{8,0},{16,8},{24,16},{28,24},{20,28},{12,20},{4,12},{1,5},{9... | collective-permute-start | bytes 552968 | tf_op jit(solution)/shard_map/ppermute | solution.py:87
  12.6 7.9 %collective-permute-start.8 = (bf16[144,640]{1,0:T(8,128)(2,1)S(1)}, bf16[144,640]{1,0:T(8,128)(2,1)S(1)}, u32[]{:S(2)}, u32[]{:S(2)}) collective-permute-start(bf16[144,640]{1,0:T(8,128)(2,1)S(1)} %collective-permute-done.7.refs_8_.refs_9_), channel_id=1, source_target_pairs={{0,8},{8,16},{16,24},{24,28},{28,20},{20,12},{12,4},{4,0},{1,9},{9... | collective-permute-start | bytes 552968 | tf_op jit(solution)/shard_map/ppermute | solution.py:87
  15.5 6.0 %collective-permute-start.2 = (bf16[144,640]{1,0:T(8,128)(2,1)S(1)}, bf16[144,640]{1,0:T(8,128)(2,1)S(1)}, u32[]{:S(2)}, u32[]{:S(2)}) collective-permute-start(bf16[144,640]{1,0:T(8,128)(2,1)S(1)} %collective-permute-done.1.refs_2_), channel_id=1, source_target_pairs={{0,8},{8,16},{16,24},{24,28},{28,20},{20,12},{12,4},{4,0},{1,9},{9... | collective-permute-start | bytes 552968 | tf_op jit(solution)/shard_map/ppermute | solution.py:87
  15.5 7.9 %collective-permute-start.12 = (bf16[144,640]{1,0:T(8,128)(2,1)S(1)}, bf16[144,640]{1,0:T(8,128)(2,1)S(1)}, u32[]{:S(2)}, u32[]{:S(2)}) collective-permute-start(bf16[144,640]{1,0:T(8,128)(2,1)S(1)} %collective-permute-done.11.refs_12_.refs_14_), channel_id=1, source_target_pairs={{0,4},{8,0},{16,8},{24,16},{28,24},{20,28},{12,20},{4,12},{1,5},{9... | collective-permute-start | bytes 552968 | tf_op jit(solution)/shard_map/ppermute | solution.py:87
  19.4 7.9 %collective-permute-start.6 = (bf16[144,640]{1,0:T(8,128)(2,1)S(1)}, bf16[144,640]{1,0:T(8,128)(2,1)S(1)}, u32[]{:S(2)}, u32[]{:S(2)}) collective-permute-start(bf16[144,640]{1,0:T(8,128)(2,1)S(1)} %collective-permute-done.5.refs_5_.refs_6_), channel_id=1, source_target_pairs={{0,4},{8,0},{16,8},{24,16},{28,24},{20,28},{12,20},{4,12},{1,5},{9... | collective-permute-start | bytes 552968 | tf_op jit(solution)/shard_map/ppermute | solution.py:87
  20.5 6.8 %collective-permute-start.9 = (bf16[144,640]{1,0:T(8,128)(2,1)S(1)}, bf16[144,640]{1,0:T(8,128)(2,1)S(1)}, u32[]{:S(2)}, u32[]{:S(2)}) collective-permute-start(bf16[144,640]{1,0:T(8,128)(2,1)S(1)} %collective-permute-done.8.refs_9_.refs_10_), channel_id=1, source_target_pairs={{0,8},{8,16},{16,24},{24,28},{28,20},{20,12},{12,4},{4,0},{1,9},{9... | collective-permute-start | bytes 552968 | tf_op jit(solution)/shard_map/ppermute | solution.py:87
  21.4 10.2 %collective-permute-start.3 = (bf16[144,640]{1,0:T(8,128)(2,1)S(1)}, bf16[144,640]{1,0:T(8,128)(2,1)S(1)}, u32[]{:S(2)}, u32[]{:S(2)}) collective-permute-start(bf16[144,640]{1,0:T(8,128)(2,1)S(1)} %collective-permute-done.2.refs_3_), channel_id=1, source_target_pairs={{0,8},{8,16},{16,24},{24,28},{28,20},{20,12},{12,4},{4,0},{1,9},{9... | collective-permute-start | bytes 552968 | tf_op jit(solution)/shard_map/ppermute | solution.py:87
  23.4 8.2 %collective-permute-start.13 = (bf16[144,640]{1,0:T(8,128)(2,1)S(1)}, bf16[144,640]{1,0:T(8,128)(2,1)S(1)}, u32[]{:S(2)}, u32[]{:S(2)}) collective-permute-start(bf16[144,640]{1,0:T(8,128)(2,1)S(1)} %collective-permute-done.12.refs_11_.refs_13_), channel_id=1, source_target_pairs={{0,4},{8,0},{16,8},{24,16},{28,24},{20,28},{12,20},{4,12},{1,5},{9... | collective-permute-start | bytes 552968 | tf_op jit(solution)/shard_map/ppermute | solution.py:87
  24.5 7.1 %copy-start = (bf16[640,640]{1,0:T(8,128)(2,1)S(1)}, bf16[640,640]{1,0:T(8,128)(2,1)}, u32[]{:S(2)}) copy-start(bf16[640,640]{1,0:T(8,128)(2,1)} %w_ref.1) | copy-start | bytes 2457604
  35.7 4.9 %collective-permute-start.14 = (bf16[384,640]{1,0:T(8,128)(2,1)S(1)}, bf16[384,640]{1,0:T(8,128)(2,1)S(1)}, u32[]{:S(2)}, u32[]{:S(2)}) collective-permute-start(bf16[384,640]{1,0:T(8,128)(2,1)S(1)} %get-tuple-element.14), channel_id=1, source_target_pairs={{0,1},{1,0},{2,3},{3,2},{4,5},{5,4},{6,7},{7,6},{8,9},{9,8},{10,11... | collective-permute-start | bytes 1474568 | tf_op jit(solution)/shard_map/ppermute | solution.py:257
  40.7 11.7 %collective-permute-start.17 = (bf16[96,640]{1,0:T(8,128)(2,1)S(1)}, bf16[96,640]{1,0:T(8,128)(2,1)S(1)}, u32[]{:S(2)}, u32[]{:S(2)}) collective-permute-start(bf16[96,640]{1,0:T(8,128)(2,1)S(1)} %get-tuple-element.15), channel_id=1, source_target_pairs={{0,16},{1,20},{2,24},{3,28},{4,0},{5,4},{6,8},{7,12},{8,17},{9,21}... | collective-permute-start | bytes 368648 | tf_op jit(solution)/shard_map/ppermute | solution.py:274
  41.2 11.3 %collective-permute-start.18 = (bf16[96,640]{1,0:T(8,128)(2,1)S(1)}, bf16[96,640]{1,0:T(8,128)(2,1)S(1)}, u32[]{:S(2)}, u32[]{:S(2)}) collective-permute-start(bf16[96,640]{1,0:T(8,128)(2,1)S(1)} %get-tuple-element.16), channel_id=1, source_target_pairs={{0,24},{1,28},{2,16},{3,20},{4,8},{5,12},{6,0},{7,4},{8,25},{9,29}... | collective-permute-start | bytes 368648 | tf_op jit(solution)/shard_map/ppermute | solution.py:274
  45.2 7.2 %collective-permute-start.16 = (bf16[96,640]{1,0:T(8,128)(2,1)S(1)}, bf16[96,640]{1,0:T(8,128)(2,1)S(1)}, u32[]{:S(2)}, u32[]{:S(2)}) collective-permute-start(bf16[96,640]{1,0:T(8,128)(2,1)S(1)} %get-tuple-element.17), channel_id=1, source_target_pairs={{0,8},{1,12},{2,0},{3,4},{4,24},{5,28},{6,16},{7,20},{8,9},{9,13},... | collective-permute-start | bytes 368648 | tf_op jit(solution)/shard_map/ppermute | solution.py:274
  50.5 11.8 %collective-permute-start.15 = (bf16[96,640]{1,0:T(8,128)(2,1)S(1)}, bf16[96,640]{1,0:T(8,128)(2,1)S(1)}, u32[]{:S(2)}, u32[]{:S(2)}) collective-permute-start(bf16[96,640]{1,0:T(8,128)(2,1)S(1)} %get-tuple-element.18), channel_id=1, source_target_pairs={{0,0},{1,4},{2,8},{3,12},{4,16},{5,20},{6,24},{7,28},{8,1},{9,5},{... | collective-permute-start | bytes 368648 | tf_op jit(solution)/shard_map/ppermute | solution.py:274

commit v7 on v5

--- a/solution.py
+++ b/solution.py
@@ -118,7 +118,7 @@
 
 
 def rows_of(refs, rows, cols, padding=0):
-    pieces = [ref[rows, cols] for ref in refs]
+    pieces = [ref[rows, cols] if len(ref.shape) == 2 else ref[rows, :, cols] for ref in refs]
     if padding:
         pieces.append(jnp.zeros((padding, HD), jnp.bfloat16))
     return jnp.concatenate(pieces, axis=0)
@@ -147,70 +147,63 @@
     return mixed[:, :HD], mixed[:, HD:]
 
 
-TOKEN_ROWS = slice(0, ROWS)
-QUERY_ROWS = slice(ROWS, ROWS + ROWS // 2)
-
-
-def queries_of(first, second, blocks, cols):
-    pieces = [part[block][QUERY_ROWS, cols] for block in blocks for part in (first, second)]
-    return jnp.concatenate(pieces, axis=0)
+PATTERNS = ((2, 1, 2, 1), (0, 3, 0, 3), (3, 0, 1, 2), (1, 2, 3, 0))
+
+
+def look_up(table, index):
+    code = sum(entry << (2 * i) for i, entry in enumerate(table))
+    return (jnp.int32(code - (code >> 31 << 32)) >> (2 * index)) & 3
+
+
+def slot_blocks(at_ref, flip_core, n):
+    place, z, y, x, core = (at_ref[i] for i in range(5))
+    blocks = []
+    for slot in range(n // 2):
+        to = look_up(sum(PATTERNS, ()), 4 * (slot ^ (2 * y + x)) + z)
+        owner = to + (core ^ flip_core) * (n - 1 - 2 * to)
+        blocks.append((place - owner) & (n - 1))
+    return blocks
 
 
 def near_kernel(heads, n, at_ref, *refs):
     near = [d for d in range(n) if d != n // 2]
-    refs, (mixed_ref, sum_ref, top_ref) = refs[:-3], refs[-3:]
-    first, second = dict(zip(near, refs[: n - 1])), dict(zip(near, refs[n - 1 :]))
-    marks = frame_marks(at_ref[0], near, n)
+    query_refs, kv_refs, (rows_ref, mixed_ref, sum_ref, top_ref) = refs[:n], refs[n:-4], refs[-4:]
+    marks = frame_marks(at_ref[0], range(n), n)
     keys_marks = key_marks(near, ROWS, n)
+    for d in range(n):
+        rows_ref[d] = query_refs[d][...]
     for head in range(heads):
         cols = slice(head * HD, (head + 1) * HD)
-        queries = jnp.concatenate([queries_of(first, second, near, cols), marks], axis=1)
-        keys = rows_of([first[d] for d in near], TOKEN_ROWS, cols, ROWS)
-        values = rows_of([second[d] for d in near], TOKEN_ROWS, cols, ROWS)
-        weights, top = soften(scores_of(queries, jnp.concatenate([keys, keys_marks], axis=1)))
-        mixed_ref[head], sum_ref[head] = mix(weights, values)
-        top_ref[head] = top
-
-
-def slot_block(at_ref, slot, flip_core, n):
-    place, z, y, x, core = (at_ref[i] for i in range(5))
-    z = z ^ slot ^ (2 * y + x)
-    owner = z + (core ^ flip_core) * (n - 1 - 2 * z)
-    return (place - owner) & (n - 1)
-
-
-def finish_kernel(heads, n, at_ref, *refs):
-    far = n // 2
-    near = [d for d in range(n) if d != far]
-    first, second = refs[:n], refs[n : 2 * n]
-    mixed_ref, sum_ref, top_ref, w_ref, given_ref, attended_ref = refs[2 * n :]
-    place = at_ref[0]
-    pad = TPF
-    marks, far_marks = frame_marks(place, near, n), frame_marks(place, [far], n)
-    far_keys_marks, all_marks = key_marks([far], pad, n), key_marks(range(n), 0, n)
+        queries = jnp.concatenate([rows_of(query_refs, slice(0, ROWS), cols), marks], axis=1)
+        keys = jnp.concatenate([rows_of(kv_refs, 0, cols, ROWS), keys_marks], axis=1)
+        weights, top = soften(scores_of(queries, keys))
+        mixed, total = mix(weights, rows_of(kv_refs, 1, cols, ROWS))
+        for d in range(n):
+            rows = slice(d * ROWS, (d + 1) * ROWS)
+            mixed_ref[head, d], sum_ref[head, d], top_ref[head, d] = mixed[rows], total[rows], top[rows]
+
+
+def finish_kernel(heads, n, flip_core, at_ref, rows_ref, mixed_ref, sum_ref, top_ref, kv_ref, w_ref, out_ref):
+    blocks = slot_blocks(at_ref, flip_core, n)
+    marks = frame_marks(at_ref[0], blocks, n)
+    keys_marks = key_marks([n // 2], TPF, n)
+    attended = []
+
+    def of(ref, head):
+        return jnp.concatenate([ref[head, block] for block in blocks], axis=0)
+
     for head in range(heads):
         cols = slice(head * HD, (head + 1) * HD)
-        queries = jnp.concatenate([queries_of(first, second, near, cols), marks], axis=1)
-        keys = jnp.concatenate([rows_of([first[far]], TOKEN_ROWS, cols, pad), far_keys_marks], axis=1)
-        before = top_ref[head]
-        weights, top = soften(scores_of(queries, keys), before)
-        mixed, total = mix(weights, rows_of([second[far]], TOKEN_ROWS, cols, pad))
+        queries = jnp.concatenate([rows_ref[block, :, cols] for block in blocks], axis=0)
+        keys = jnp.concatenate([rows_of([kv_ref], 0, cols, TPF), keys_marks], axis=1)
+        before = of(top_ref, head)
+        weights, top = soften(scores_of(jnp.concatenate([queries, marks], axis=1), keys), before)
+        mixed, total = mix(weights, rows_of([kv_ref], 1, cols, TPF))
         kept = jnp.exp2((before - top) * SCALE)
-        mixed = (mixed + mixed_ref[head] * kept) / (total + sum_ref[head] * kept)
-        for i, d in enumerate(near):
-            attended_ref[d, :, cols] = mixed[i * ROWS : (i + 1) * ROWS].astype(jnp.bfloat16)
-        queries = jnp.concatenate([queries_of(first, second, [far], cols), far_marks], axis=1)
-        keys = jnp.concatenate([rows_of(first, TOKEN_ROWS, cols), all_marks], axis=1)
-        weights, _ = soften(scores_of(queries, keys))
-        mixed, total = mix(weights, rows_of(second, TOKEN_ROWS, cols))
-        attended_ref[far, :, cols] = (mixed / total).astype(jnp.bfloat16)
-    rows = jnp.concatenate([attended_ref[slot_block(at_ref, slot, 1, n)] for slot in range(n // 2)], axis=0)
-    given_ref[...] = jnp.dot(rows, w_ref[...], preferred_element_type=jnp.float32).astype(given_ref.dtype)
-
-
-def own_kernel(n, at_ref, attended_ref, w_ref, kept_ref):
-    rows = jnp.concatenate([attended_ref[slot_block(at_ref, slot, 0, n)] for slot in range(n // 2)], axis=0)
-    kept_ref[...] = jnp.dot(rows, w_ref[...], preferred_element_type=jnp.float32)
+        mixed, total = mixed + of(mixed_ref, head) * kept, total + of(sum_ref, head) * kept
+        attended.append((mixed / total).astype(jnp.bfloat16))
+    rows = jnp.concatenate(attended, axis=1)
+    out_ref[...] = jnp.dot(rows, w_ref[...], preferred_element_type=jnp.float32).astype(out_ref.dtype)
 
 
 def call(kernel, where, operands, outs, flops):
@@ -230,50 +223,43 @@
     frame, head = lax.axis_index("frames"), lax.axis_index("heads")
     z, y, x, core = frame >> 1, frame & 1, head >> 1, head & 1
     where = jnp.stack([ring_place(frame, n), z, y, x, core]).astype(jnp.int32)
-    half = ROWS // 2
     width, cols = out_weight.shape
     heads = width // HD
-    streams = [
-        jnp.concatenate([keys_values[0], queries[:half]], axis=0),
-        jnp.concatenate([keys_values[1], queries[half:]], axis=0),
-    ]
-    first, second = gather_ring(streams, n)
+    found_queries, found_kv = gather_ring([queries, keys_values], n)
     f32, bf16 = jnp.float32, jnp.bfloat16
-    near = [d for d in range(n) if d != n // 2]
     state = call(
         functools.partial(near_kernel, heads, n),
         where,
-        [blocks[d] for blocks in (first, second) for d in near],
-        [((heads, (n - 1) * ROWS, HD), f32)] * 3,
-        4 * (n - 1) ** 2 * ROWS**2 * width,
-    )
-    given, attended = call(
-        functools.partial(finish_kernel, heads, n),
-        where,
-        [*first, *second, *state, out_weight],
-        [((n // 2 * ROWS, cols), bf16), ((n, ROWS, width), bf16)],
-        8 * n * ROWS**2 * width,
-    )
-    from_core = lax.ppermute(given, "heads", [(h, h ^ 1) for h in range(4)])
-    (kept,) = call(
-        functools.partial(own_kernel, n),
-        where,
-        [attended, out_weight],
-        [((n // 2 * ROWS, cols), f32)],
-        n * ROWS * width * cols,
-    )
+        [*found_queries, *(found_kv[d] for d in range(n) if d != n // 2)],
+        [((n, ROWS, width), bf16)] + [((heads, n, ROWS, HD), f32)] * 3,
+        4 * n * (n - 1) * ROWS**2 * width,
+    )
+
+    def finish(flip_core, dtype):
+        (rows,) = call(
+            functools.partial(finish_kernel, heads, n, flip_core),
+            where,
+            [*state, found_kv[n // 2], out_weight],
+            [((n // 2 * ROWS, cols), dtype)],
+            n * ROWS * width * cols,
+        )
+        return rows
+
+    from_core = lax.ppermute(finish(1, bf16), "heads", [(h, h ^ 1) for h in range(4)])
+    kept = finish(0, f32)
     arrived = []
     for slot in range(n // 2):
         rows = slice(slot * ROWS, (slot + 1) * ROWS)
         pairs = []
         for f in range(n):
             for h in range(4):
-                to = (f >> 1) ^ slot ^ (2 * (f & 1) + (h >> 1))
+                to = PATTERNS[slot ^ (2 * (f & 1) + (h >> 1))][f >> 1]
                 pairs.append((4 * f + h, 4 * (2 * to + (h & 1)) + (f >> 1)))
         total = (kept[rows] + from_core[rows].astype(f32)).astype(bf16)
         arrived.append(lax.ppermute(total, ("frames", "heads"), pairs).astype(f32))
     low, high = (arrived[0] + arrived[1]).astype(bf16), (arrived[2] + arrived[3]).astype(bf16)
-    straight = (z ^ head) & 2 == 0
+    patterns = [[p[source] for p in PATTERNS].index(to) for source in range(4) for to in range(4)]
+    straight = look_up(patterns, 4 * head + z) & 2 == 0
     return jnp.concatenate([jnp.where(straight, low, high), jnp.where(straight, high, low)], axis=1)
 
 

time: 66.6 us -> 63.5 us (0.953)
  starting transfers between devices: 29.4 us -> 25.4 us
  waiting for transfers between devices: 24.5 us -> 26 us
    ppermute x4, starting transfers between devices: 15 us -> 10.1 us  [on_device_ring(): arrived.append(lax.ppermute(total, ('frames', 'heads'), pairs).astype(f32))]
    ppermute x14, waiting for transfers between devices: 14.6 us -> 17.2 us  [hop(): lax.ppermute(x, 'frames', [(order[i], order[(i + by) % n]) for i in range...]
    unnamed x2 -> x6, local copies, waits for them, and re-layouts: 0.01 us -> 1.85 us
    squeeze x1 -> x0, local copies, waits for them, and re-layouts: 0.99 us -> none  [on_device_ring(): keys_values[1]]
    ppermute x14, starting transfers between devices: 14.3 us -> 15.3 us  [hop(): lax.ppermute(x, 'frames', [(order[i], order[(i + by) % n]) for i in range...]
    slice x1 -> x0, local copies, waits for them, and re-layouts: 0.87 us -> none  [on_device_ring(): queries[half:]]
    ppermute x1, waiting for transfers between devices: 0.7 us -> 0.01 us  [on_device_ring(): lax.ppermute(finish(1, bf16), 'heads', [(h, h ^ 1) for h in range(4)])]
  transfers between devices with their start and end apart: 19 -> 19, of which waited for: 13 -> 11; matrix products, arithmetic and copies ran while one was open for 0% -> 0% of each run, Pallas kernels for 8% -> 11%
where the time goes in v7:
time: 63.5 us; the launch traced here: 63.3 us
  waiting for transfers between devices  26 us (41%)
  starting transfers between devices  25.4 us (40%)
  Pallas kernels  8.93 us (14%)
  local copies, waits for them, and re-layouts  1.93 us (3%)
  other arithmetic  0.93 us (1%)
    ppermute x14, waiting for transfers between devices, hop(): lax.ppermute(x, 'frames', [(order[i], order[(i + by) % n]) for i in range...  17.2 us
    ppermute x14, starting transfers between devices, hop(): lax.ppermute(x, 'frames', [(order[i], order[(i + by) % n]) for i in range...  15.3 us
    ppermute x4, starting transfers between devices, on_device_ring(): arrived.append(lax.ppermute(total, ('frames', 'heads'), pairs).astype(f32))  10.1 us
    pallas_call x3, Pallas kernels, call(): pl.pallas_call(kernel, out_shape=[jax.ShapeDtypeStruct(shape, dtype) for...  8.93 us
    ppermute x4, waiting for transfers between devices, on_device_ring(): arrived.append(lax.ppermute(total, ('frames', 'heads'), pairs).astype(f32))  8.72 us
    unnamed x6, local copies, waits for them, and re-layouts  1.85 us
  transfers between devices with their start and end apart: 19, of which 11 were waited for; matrix products, arithmetic and copies ran while one was open for 0% of the time, Pallas kernels for 11%

profile of v7, /device:TPU:2, one launch (start us, length us, event | category | flops | bytes accessed | tf_op | source)
XLA Modules:
  0.0 63.3 jit_solution(12194590489034253079)
XLA Ops:
  0.0 1.5 %collective-permute-start.10 = (bf16[2,96,640]{2,1,0:T(8,128)(2,1)}, bf16[2,96,640]{2,1,0:T(8,128)(2,1)S(1)}, u32[]{:S(2)}, u32[]{:S(2)}) collective-permute-start(bf16[2,96,640]{2,1,0:T(8,128)(2,1)} %refs_8_.1), channel_id=1, source_target_pairs={{0,4},{8,0},{16,8},{24,16},{28,24},{20,28},{12,20},{4,12},{1,5},{9... | collective-permute-start | bytes 737288 | tf_op jit(solution)/shard_map/ppermute | solution.py:87
  2.0 5.9 %collective-permute-done.10.refs_14_ = bf16[2,96,640]{2,1,0:T(8,128)(2,1)S(1)} collective-permute-done((bf16[2,96,640]{2,1,0:T(8,128)(2,1)}, bf16[2,96,640]{2,1,0:T(8,128)(2,1)S(1)}, u32[]{:S(2)}, u32[]{:S(2)}) %collective-permute-start.10) | collective-permute-done | bytes 245792 | tf_op jit(solution)/shard_map/ppermute | solution.py:87
  7.9 1.5 %collective-permute-start.11 = (bf16[2,96,640]{2,1,0:T(8,128)(2,1)S(1)}, bf16[2,96,640]{2,1,0:T(8,128)(2,1)S(1)}, u32[]{:S(2)}, u32[]{:S(2)}) collective-permute-start(bf16[2,96,640]{2,1,0:T(8,128)(2,1)S(1)} %collective-permute-done.10.refs_14_), channel_id=1, source_target_pairs={{0,4},{8,0},{16,8},{24,16},{28,24},{20,28},{12,20},{4,12},{1,5},{9... | collective-permute-start | bytes 737288 | tf_op jit(solution)/shard_map/ppermute | solution.py:87
  9.9 1.6 %collective-permute-start.8 = (bf16[2,96,640]{2,1,0:T(8,128)(2,1)S(1)}, bf16[2,96,640]{2,1,0:T(8,128)(2,1)S(1)}, u32[]{:S(2)}, u32[]{:S(2)}) collective-permute-start(bf16[2,96,640]{2,1,0:T(8,128)(2,1)S(1)} %collective-permute-done.7.refs_9_), channel_id=1, source_target_pairs={{0,8},{8,16},{16,24},{24,28},{28,20},{20,12},{12,4},{4,0},{1,9},{9... | collective-permute-start | bytes 737288 | tf_op jit(solution)/shard_map/ppermute | solution.py:87
  12.0 3.9 %collective-permute-done.refs_1_ = bf16[96,640]{1,0:T(8,128)(2,1)S(1)} collective-permute-done((bf16[96,640]{1,0:T(8,128)(2,1)}, bf16[96,640]{1,0:T(8,128)(2,1)S(1)}, u32[]{:S(2)}, u32[]{:S(2)}) %collective-permute-start) | collective-permute-done | bytes 122912 | tf_op jit(solution)/shard_map/ppermute | solution.py:87
  16.7 1.5 %collective-permute-start.12 = (bf16[2,96,640]{2,1,0:T(8,128)(2,1)S(1)}, bf16[2,96,640]{2,1,0:T(8,128)(2,1)S(1)}, u32[]{:S(2)}, u32[]{:S(2)}) collective-permute-start(bf16[2,96,640]{2,1,0:T(8,128)(2,1)S(1)} %collective-permute-done.11.refs_13_), channel_id=1, source_target_pairs={{0,4},{8,0},{16,8},{24,16},{28,24},{20,28},{12,20},{4,12},{1,5},{9... | collective-permute-start | bytes 737288 | tf_op jit(solution)/shard_map/ppermute | solution.py:87
  18.2 1.1 %collective-permute-done.4.refs_7_ = bf16[96,640]{1,0:T(8,128)(2,1)S(1)} collective-permute-done((bf16[96,640]{1,0:T(8,128)(2,1)}, bf16[96,640]{1,0:T(8,128)(2,1)S(1)}, u32[]{:S(2)}, u32[]{:S(2)}) %collective-permute-start.4) | collective-permute-done | bytes 122912 | tf_op jit(solution)/shard_map/ppermute | solution.py:87
  19.3 1.5 %collective-permute-start.5 = (bf16[96,640]{1,0:T(8,128)(2,1)S(1)}, bf16[96,640]{1,0:T(8,128)(2,1)S(1)}, u32[]{:S(2)}, u32[]{:S(2)}) collective-permute-start(bf16[96,640]{1,0:T(8,128)(2,1)S(1)} %collective-permute-done.4.refs_7_), channel_id=1, source_target_pairs={{0,4},{8,0},{16,8},{24,16},{28,24},{20,28},{12,20},{4,12},{1,5},{9... | collective-permute-start | bytes 368648 | tf_op jit(solution)/shard_map/ppermute | solution.py:87
  22.0 1.6 %collective-permute-start.9 = (bf16[2,96,640]{2,1,0:T(8,128)(2,1)S(1)}, bf16[2,96,640]{2,1,0:T(8,128)(2,1)S(1)}, u32[]{:S(2)}, u32[]{:S(2)}) collective-permute-start(bf16[2,96,640]{2,1,0:T(8,128)(2,1)S(1)} %collective-permute-done.8.refs_10_), channel_id=1, source_target_pairs={{0,8},{8,16},{16,24},{24,28},{28,20},{20,12},{12,4},{4,0},{1,9},{9... | collective-permute-start | bytes 737288 | tf_op jit(solution)/shard_map/ppermute | solution.py:87
  23.5 1.9 %collective-permute-done.5.refs_6_ = bf16[96,640]{1,0:T(8,128)(2,1)S(1)} collective-permute-done((bf16[96,640]{1,0:T(8,128)(2,1)S(1)}, bf16[96,640]{1,0:T(8,128)(2,1)S(1)}, u32[]{:S(2)}, u32[]{:S(2)}) %collective-permute-start.5) | collective-permute-done | bytes 122912 | tf_op jit(solution)/shard_map/ppermute | solution.py:87
  25.4 1.5 %collective-permute-start.6 = (bf16[96,640]{1,0:T(8,128)(2,1)S(1)}, bf16[96,640]{1,0:T(8,128)(2,1)S(1)}, u32[]{:S(2)}, u32[]{:S(2)}) collective-permute-start(bf16[96,640]{1,0:T(8,128)(2,1)S(1)} %collective-permute-done.5.refs_6_), channel_id=1, source_target_pairs={{0,4},{8,0},{16,8},{24,16},{28,24},{20,28},{12,20},{4,12},{1,5},{9... | collective-permute-start | bytes 368648 | tf_op jit(solution)/shard_map/ppermute | solution.py:87
  26.9 0.8 %collective-permute-done.2.refs_3_ = bf16[96,640]{1,0:T(8,128)(2,1)S(1)} collective-permute-done((bf16[96,640]{1,0:T(8,128)(2,1)S(1)}, bf16[96,640]{1,0:T(8,128)(2,1)S(1)}, u32[]{:S(2)}, u32[]{:S(2)}) %collective-permute-start.2) | collective-permute-done | bytes 122912 | tf_op jit(solution)/shard_map/ppermute | solution.py:87
  28.2 1.5 %collective-permute-start.13 = (bf16[2,96,640]{2,1,0:T(8,128)(2,1)S(1)}, bf16[2,96,640]{2,1,0:T(8,128)(2,1)S(1)}, u32[]{:S(2)}, u32[]{:S(2)}) collective-permute-start(bf16[2,96,640]{2,1,0:T(8,128)(2,1)S(1)} %collective-permute-done.12.refs_12_), channel_id=1, source_target_pairs={{0,4},{8,0},{16,8},{24,16},{28,24},{20,28},{12,20},{4,12},{1,5},{9... | collective-permute-start | bytes 737288 | tf_op jit(solution)/shard_map/ppermute | solution.py:87
  30.5 2.1 %collective-permute-done.3.refs_4_ = bf16[96,640]{1,0:T(8,128)(2,1)S(1)} collective-permute-done((bf16[96,640]{1,0:T(8,128)(2,1)S(1)}, bf16[96,640]{1,0:T(8,128)(2,1)S(1)}, u32[]{:S(2)}, u32[]{:S(2)}) %collective-permute-start.3) | collective-permute-done | bytes 122912 | tf_op jit(solution)/shard_map/ppermute | solution.py:87
  32.6 0.9 %copy-done.1 = bf16[2,96,640]{2,1,0:T(8,128)(2,1)S(1)} copy-done((bf16[2,96,640]{2,1,0:T(8,128)(2,1)S(1)}, bf16[2,96,640]{2,1,0:T(8,128)(2,1)}, u32[]{:S(2)}) %copy-start.1) | copy-done | bytes 245784
  33.5 0.9 %copy-done.2 = bf16[96,640]{1,0:T(8,128)(2,1)S(1)} copy-done((bf16[96,640]{1,0:T(8,128)(2,1)S(1)}, bf16[96,640]{1,0:T(8,128)(2,1)}, u32[]{:S(2)}) %copy-start.2) | copy-done | bytes 122904
  34.4 4.8 %shard_map.37 = (bf16[8,96,640]{2,1,0:T(8,128)(2,1)S(1)}, f32[5,8,96,128]{3,2,1,0:T(8,128)S(1)}, f32[5,8,96,128]{3,2,1,0:T(8,128)S(1)}, f32[5,8,96,128]{3,2,1,0:T(8,128)S(1)}) custom-call(s32[5]{0:T(128)S(1)} %stack.23.at_ref, bf16[96,640]{1,0:T(8,128)(2,1)S(1)} %copy-done.2, bf16[96,640]{1,0:T(8,128)(2,1)S(1)} %collective-permute-done.refs_1_, ...), custom_call_target="tpu_custom_call" | custom-call | flops 1321205760 | tf_op jit(solution)/shard_map/pallas_call | solution.py:211
  39.3 2.0 %shard_map.39 = bf16[384,640]{1,0:T(8,128)(2,1)S(1)} custom-call(s32[5]{0:T(128)S(1)} %stack.23.at_ref, bf16[8,96,640]{2,1,0:T(8,128)(2,1)S(1)} %get-tuple-element.9.rows_ref, f32[5,8,96,128]{3,2,1,0:T(8,128)S(1)} %get-tuple-element.10.mixed_ref, f32[5,8,96,128]{3,2,1,0:T(8,128)S(1)} %get-tuple-element.11.sum_ref, ...), custom_call_target="tpu_custom_call" | custom-call | flops 314572800 | tf_op jit(solution)/shard_map/pallas_call | solution.py:211
  41.4 2.0 %shard_map.38 = f32[384,640]{1,0:T(8,128)S(1)} custom-call(s32[5]{0:T(128)S(1)} %stack.23.at_ref, bf16[8,96,640]{2,1,0:T(8,128)(2,1)S(1)} %get-tuple-element.9.rows_ref, f32[5,8,96,128]{3,2,1,0:T(8,128)S(1)} %get-tuple-element.10.mixed_ref, f32[5,8,96,128]{3,2,1,0:T(8,128)S(1)} %get-tuple-element.11.sum_ref, ...), custom_call_target="tpu_custom_call" | custom-call | flops 314572800 | tf_op jit(solution)/shard_map/pallas_call | solution.py:211
  43.6 3.4 %collective-permute-start.16 = (bf16[96,640]{1,0:T(8,128)(2,1)S(1)}, bf16[96,640]{1,0:T(8,128)(2,1)S(1)}, u32[]{:S(2)}, u32[]{:S(2)}) collective-permute-start(bf16[96,640]{1,0:T(8,128)(2,1)S(1)} %get-tuple-element.15), channel_id=1, source_target_pairs={{0,0},{1,4},{2,16},{3,20},{4,8},{5,12},{6,24},{7,28},{8,25},{9,29}... | collective-permute-start | bytes 368648 | tf_op jit(solution)/shard_map/ppermute | solution.py:259
  47.1 4.7 %collective-permute-start.18 = (bf16[96,640]{1,0:T(8,128)(2,1)S(1)}, bf16[96,640]{1,0:T(8,128)(2,1)S(1)}, u32[]{:S(2)}, u32[]{:S(2)}) collective-permute-start(bf16[96,640]{1,0:T(8,128)(2,1)S(1)} %get-tuple-element.14), channel_id=1, source_target_pairs={{0,8},{1,12},{2,24},{3,28},{4,0},{5,4},{6,16},{7,20},{8,17},{9,21}... | collective-permute-start | bytes 368648 | tf_op jit(solution)/shard_map/ppermute | solution.py:259
  51.8 1.9 %collective-permute-start.17 = (bf16[96,640]{1,0:T(8,128)(2,1)S(1)}, bf16[96,640]{1,0:T(8,128)(2,1)S(1)}, u32[]{:S(2)}, u32[]{:S(2)}) collective-permute-start(bf16[96,640]{1,0:T(8,128)(2,1)S(1)} %get-tuple-element.13), channel_id=1, source_target_pairs={{0,24},{1,28},{2,8},{3,12},{4,16},{5,20},{6,0},{7,4},{8,1},{9,5},{... | collective-permute-start | bytes 368648 | tf_op jit(solution)/shard_map/ppermute | solution.py:259
  53.7 4.6 %collective-permute-done.16 = bf16[96,640]{1,0:T(8,128)(2,1)S(1)} collective-permute-done((bf16[96,640]{1,0:T(8,128)(2,1)S(1)}, bf16[96,640]{1,0:T(8,128)(2,1)S(1)}, u32[]{:S(2)}, u32[]{:S(2)}) %collective-permute-start.16) | collective-permute-done | bytes 122912 | tf_op jit(solution)/shard_map/ppermute | solution.py:259
  58.4 4.1 %collective-permute-done.18 = bf16[96,640]{1,0:T(8,128)(2,1)S(1)} collective-permute-done((bf16[96,640]{1,0:T(8,128)(2,1)S(1)}, bf16[96,640]{1,0:T(8,128)(2,1)S(1)}, u32[]{:S(2)}, u32[]{:S(2)}) %collective-permute-start.18) | collective-permute-done | bytes 122912 | tf_op jit(solution)/shard_map/ppermute | solution.py:259
  (27 shorter events, 5.8 us)
Async XLA Ops:
  0.0 7.9 %collective-permute-start.10 = (bf16[2,96,640]{2,1,0:T(8,128)(2,1)}, bf16[2,96,640]{2,1,0:T(8,128)(2,1)S(1)}, u32[]{:S(2)}, u32[]{:S(2)}) collective-permute-start(bf16[2,96,640]{2,1,0:T(8,128)(2,1)} %refs_8_.1), channel_id=1, source_target_pairs={{0,4},{8,0},{16,8},{24,16},{28,24},{20,28},{12,20},{4,12},{1,5},{9... | collective-permute-start | bytes 737288 | tf_op jit(solution)/shard_map/ppermute | solution.py:87
  1.5 8.4 %collective-permute-start.7 = (bf16[2,96,640]{2,1,0:T(8,128)(2,1)}, bf16[2,96,640]{2,1,0:T(8,128)(2,1)S(1)}, u32[]{:S(2)}, u32[]{:S(2)}) collective-permute-start(bf16[2,96,640]{2,1,0:T(8,128)(2,1)} %refs_8_.1), channel_id=1, source_target_pairs={{0,8},{8,16},{16,24},{24,28},{28,20},{20,12},{12,4},{4,0},{1,9},{9... | collective-permute-start | bytes 737288 | tf_op jit(solution)/shard_map/ppermute | solution.py:87
  7.9 8.8 %collective-permute-start.11 = (bf16[2,96,640]{2,1,0:T(8,128)(2,1)S(1)}, bf16[2,96,640]{2,1,0:T(8,128)(2,1)S(1)}, u32[]{:S(2)}, u32[]{:S(2)}) collective-permute-start(bf16[2,96,640]{2,1,0:T(8,128)(2,1)S(1)} %collective-permute-done.10.refs_14_), channel_id=1, source_target_pairs={{0,4},{8,0},{16,8},{24,16},{28,24},{20,28},{12,20},{4,12},{1,5},{9... | collective-permute-start | bytes 737288 | tf_op jit(solution)/shard_map/ppermute | solution.py:87
  9.4 6.5 %collective-permute-start = (bf16[96,640]{1,0:T(8,128)(2,1)}, bf16[96,640]{1,0:T(8,128)(2,1)S(1)}, u32[]{:S(2)}, u32[]{:S(2)}) collective-permute-start(bf16[96,640]{1,0:T(8,128)(2,1)} %refs_0_.1), channel_id=1, source_target_pairs={{0,8},{8,16},{16,24},{24,28},{28,20},{20,12},{12,4},{4,0},{1,9},{9... | collective-permute-start | bytes 368648 | tf_op jit(solution)/shard_map/ppermute | solution.py:87
  9.9 12.0 %collective-permute-start.8 = (bf16[2,96,640]{2,1,0:T(8,128)(2,1)S(1)}, bf16[2,96,640]{2,1,0:T(8,128)(2,1)S(1)}, u32[]{:S(2)}, u32[]{:S(2)}) collective-permute-start(bf16[2,96,640]{2,1,0:T(8,128)(2,1)S(1)} %collective-permute-done.7.refs_9_), channel_id=1, source_target_pairs={{0,8},{8,16},{16,24},{24,28},{28,20},{20,12},{12,4},{4,0},{1,9},{9... | collective-permute-start | bytes 737288 | tf_op jit(solution)/shard_map/ppermute | solution.py:87
  11.5 7.8 %collective-permute-start.4 = (bf16[96,640]{1,0:T(8,128)(2,1)}, bf16[96,640]{1,0:T(8,128)(2,1)S(1)}, u32[]{:S(2)}, u32[]{:S(2)}) collective-permute-start(bf16[96,640]{1,0:T(8,128)(2,1)} %refs_0_.1), channel_id=1, source_target_pairs={{0,4},{8,0},{16,8},{24,16},{28,24},{20,28},{12,20},{4,12},{1,5},{9... | collective-permute-start | bytes 368648 | tf_op jit(solution)/shard_map/ppermute | solution.py:87
  15.9 5.6 %collective-permute-start.1 = (bf16[96,640]{1,0:T(8,128)(2,1)S(1)}, bf16[96,640]{1,0:T(8,128)(2,1)S(1)}, u32[]{:S(2)}, u32[]{:S(2)}) collective-permute-start(bf16[96,640]{1,0:T(8,128)(2,1)S(1)} %collective-permute-done.refs_1_), channel_id=1, source_target_pairs={{0,8},{8,16},{16,24},{24,28},{28,20},{20,12},{12,4},{4,0},{1,9},{9... | collective-permute-start | bytes 368648 | tf_op jit(solution)/shard_map/ppermute | solution.py:87
  16.7 11.6 %collective-permute-start.12 = (bf16[2,96,640]{2,1,0:T(8,128)(2,1)S(1)}, bf16[2,96,640]{2,1,0:T(8,128)(2,1)S(1)}, u32[]{:S(2)}, u32[]{:S(2)}) collective-permute-start(bf16[2,96,640]{2,1,0:T(8,128)(2,1)S(1)} %collective-permute-done.11.refs_13_), channel_id=1, source_target_pairs={{0,4},{8,0},{16,8},{24,16},{28,24},{20,28},{12,20},{4,12},{1,5},{9... | collective-permute-start | bytes 737288 | tf_op jit(solution)/shard_map/ppermute | solution.py:87
  19.3 6.1 %collective-permute-start.5 = (bf16[96,640]{1,0:T(8,128)(2,1)S(1)}, bf16[96,640]{1,0:T(8,128)(2,1)S(1)}, u32[]{:S(2)}, u32[]{:S(2)}) collective-permute-start(bf16[96,640]{1,0:T(8,128)(2,1)S(1)} %collective-permute-done.4.refs_7_), channel_id=1, source_target_pairs={{0,4},{8,0},{16,8},{24,16},{28,24},{20,28},{12,20},{4,12},{1,5},{9... | collective-permute-start | bytes 368648 | tf_op jit(solution)/shard_map/ppermute | solution.py:87
  21.4 6.3 %collective-permute-start.2 = (bf16[96,640]{1,0:T(8,128)(2,1)S(1)}, bf16[96,640]{1,0:T(8,128)(2,1)S(1)}, u32[]{:S(2)}, u32[]{:S(2)}) collective-permute-start(bf16[96,640]{1,0:T(8,128)(2,1)S(1)} %collective-permute-done.1.refs_2_), channel_id=1, source_target_pairs={{0,8},{8,16},{16,24},{24,28},{28,20},{20,12},{12,4},{4,0},{1,9},{9... | collective-permute-start | bytes 368648 | tf_op jit(solution)/shard_map/ppermute | solution.py:87
  22.0 10.6 %collective-permute-start.9 = (bf16[2,96,640]{2,1,0:T(8,128)(2,1)S(1)}, bf16[2,96,640]{2,1,0:T(8,128)(2,1)S(1)}, u32[]{:S(2)}, u32[]{:S(2)}) collective-permute-start(bf16[2,96,640]{2,1,0:T(8,128)(2,1)S(1)} %collective-permute-done.8.refs_10_), channel_id=1, source_target_pairs={{0,8},{8,16},{16,24},{24,28},{28,20},{20,12},{12,4},{4,0},{1,9},{9... | collective-permute-start | bytes 737288 | tf_op jit(solution)/shard_map/ppermute | solution.py:87
  25.4 5.1 %collective-permute-start.6 = (bf16[96,640]{1,0:T(8,128)(2,1)S(1)}, bf16[96,640]{1,0:T(8,128)(2,1)S(1)}, u32[]{:S(2)}, u32[]{:S(2)}) collective-permute-start(bf16[96,640]{1,0:T(8,128)(2,1)S(1)} %collective-permute-done.5.refs_6_), channel_id=1, source_target_pairs={{0,4},{8,0},{16,8},{24,16},{28,24},{20,28},{12,20},{4,12},{1,5},{9... | collective-permute-start | bytes 368648 | tf_op jit(solution)/shard_map/ppermute | solution.py:87
  27.7 4.9 %collective-permute-start.3 = (bf16[96,640]{1,0:T(8,128)(2,1)S(1)}, bf16[96,640]{1,0:T(8,128)(2,1)S(1)}, u32[]{:S(2)}, u32[]{:S(2)}) collective-permute-start(bf16[96,640]{1,0:T(8,128)(2,1)S(1)} %collective-permute-done.2.refs_3_), channel_id=1, source_target_pairs={{0,8},{8,16},{16,24},{24,28},{28,20},{20,12},{12,4},{4,0},{1,9},{9... | collective-permute-start | bytes 368648 | tf_op jit(solution)/shard_map/ppermute | solution.py:87
  28.2 11.1 %collective-permute-start.13 = (bf16[2,96,640]{2,1,0:T(8,128)(2,1)S(1)}, bf16[2,96,640]{2,1,0:T(8,128)(2,1)S(1)}, u32[]{:S(2)}, u32[]{:S(2)}) collective-permute-start(bf16[2,96,640]{2,1,0:T(8,128)(2,1)S(1)} %collective-permute-done.12.refs_12_), channel_id=1, source_target_pairs={{0,4},{8,0},{16,8},{24,16},{28,24},{20,28},{12,20},{4,12},{1,5},{9... | collective-permute-start | bytes 737288 | tf_op jit(solution)/shard_map/ppermute | solution.py:87
  29.8 9.5 %copy-start = (bf16[640,640]{1,0:T(8,128)(2,1)S(1)}, bf16[640,640]{1,0:T(8,128)(2,1)}, u32[]{:S(2)}) copy-start(bf16[640,640]{1,0:T(8,128)(2,1)} %w_ref.3) | copy-start | bytes 2457604
  32.6 0.9 %copy-start.1 = (bf16[2,96,640]{2,1,0:T(8,128)(2,1)S(1)}, bf16[2,96,640]{2,1,0:T(8,128)(2,1)}, u32[]{:S(2)}) copy-start(bf16[2,96,640]{2,1,0:T(8,128)(2,1)} %refs_8_.1) | copy-start | bytes 737284
  33.5 0.9 %copy-start.2 = (bf16[96,640]{1,0:T(8,128)(2,1)S(1)}, bf16[96,640]{1,0:T(8,128)(2,1)}, u32[]{:S(2)}) copy-start(bf16[96,640]{1,0:T(8,128)(2,1)} %refs_0_.1) | copy-start | bytes 368644
  41.4 2.1 %collective-permute-start.14 = (bf16[384,640]{1,0:T(8,128)(2,1)S(1)}, bf16[384,640]{1,0:T(8,128)(2,1)S(1)}, u32[]{:S(2)}, u32[]{:S(2)}) collective-permute-start(bf16[384,640]{1,0:T(8,128)(2,1)S(1)} %shard_map.39), channel_id=1, source_target_pairs={{0,1},{1,0},{2,3},{3,2},{4,5},{5,4},{6,7},{7,6},{8,9},{9,8},{10,11... | collective-permute-start | bytes 1474568 | tf_op jit(solution)/shard_map/ppermute | solution.py:248
  43.6 14.7 %collective-permute-start.16 = (bf16[96,640]{1,0:T(8,128)(2,1)S(1)}, bf16[96,640]{1,0:T(8,128)(2,1)S(1)}, u32[]{:S(2)}, u32[]{:S(2)}) collective-permute-start(bf16[96,640]{1,0:T(8,128)(2,1)S(1)} %get-tuple-element.15), channel_id=1, source_target_pairs={{0,0},{1,4},{2,16},{3,20},{4,8},{5,12},{6,24},{7,28},{8,25},{9,29}... | collective-permute-start | bytes 368648 | tf_op jit(solution)/shard_map/ppermute | solution.py:259
  47.0 11.3 %collective-permute-start.15 = (bf16[96,640]{1,0:T(8,128)(2,1)S(1)}, bf16[96,640]{1,0:T(8,128)(2,1)S(1)}, u32[]{:S(2)}, u32[]{:S(2)}) collective-permute-start(bf16[96,640]{1,0:T(8,128)(2,1)S(1)} %get-tuple-element.16), channel_id=1, source_target_pairs={{0,16},{1,20},{2,0},{3,4},{4,24},{5,28},{6,8},{7,12},{8,9},{9,13},... | collective-permute-start | bytes 368648 | tf_op jit(solution)/shard_map/ppermute | solution.py:259
  47.1 15.3 %collective-permute-start.18 = (bf16[96,640]{1,0:T(8,128)(2,1)S(1)}, bf16[96,640]{1,0:T(8,128)(2,1)S(1)}, u32[]{:S(2)}, u32[]{:S(2)}) collective-permute-start(bf16[96,640]{1,0:T(8,128)(2,1)S(1)} %get-tuple-element.14), channel_id=1, source_target_pairs={{0,8},{1,12},{2,24},{3,28},{4,0},{5,4},{6,16},{7,20},{8,17},{9,21}... | collective-permute-start | bytes 368648 | tf_op jit(solution)/shard_map/ppermute | solution.py:259
  51.8 10.7 %collective-permute-start.17 = (bf16[96,640]{1,0:T(8,128)(2,1)S(1)}, bf16[96,640]{1,0:T(8,128)(2,1)S(1)}, u32[]{:S(2)}, u32[]{:S(2)}) collective-permute-start(bf16[96,640]{1,0:T(8,128)(2,1)S(1)} %get-tuple-element.13), channel_id=1, source_target_pairs={{0,24},{1,28},{2,8},{3,12},{4,16},{5,20},{6,0},{7,4},{8,1},{9,5},{... | collective-permute-start | bytes 368648 | tf_op jit(solution)/shard_map/ppermute | solution.py:259

commit v8 on v7

--- a/solution.py
+++ b/solution.py
@@ -165,28 +165,62 @@
     return blocks
 
 
+TOKEN_ROWS = slice(0, ROWS)
+QUERY_ROWS = slice(ROWS, ROWS + ROWS // 2)
+
+
+def streams_kernel(queries_ref, kv_ref, first_ref, second_ref, sems):
+    half = ROWS // 2
+    copies = []
+    for i, out_ref in enumerate((first_ref, second_ref)):
+        copies.append((kv_ref.at[i], out_ref.at[pl.ds(0, ROWS)]))
+        copies.append((queries_ref.at[pl.ds(i * half, half)], out_ref.at[pl.ds(ROWS, half)]))
+    copies = [pltpu.make_async_copy(src, dst, sems.at[i]) for i, (src, dst) in enumerate(copies)]
+    for copy in copies:
+        copy.start()
+    for copy in copies:
+        copy.wait()
+
+
+def attend_all(place, block, queries, first, second, cols, n):
+    queries = jnp.concatenate([queries, frame_marks(place, [block], n)], axis=1)
+    keys = jnp.concatenate([rows_of(first, TOKEN_ROWS, cols), key_marks(range(n), 0, n)], axis=1)
+    weights, _ = soften(scores_of(queries, keys))
+    mixed, total = mix(weights, rows_of(second, TOKEN_ROWS, cols))
+    return (mixed / total).astype(jnp.bfloat16)
+
+
 def near_kernel(heads, n, at_ref, *refs):
-    near = [d for d in range(n) if d != n // 2]
-    query_refs, kv_refs, (rows_ref, mixed_ref, sum_ref, top_ref) = refs[:n], refs[n:-4], refs[-4:]
-    marks = frame_marks(at_ref[0], range(n), n)
+    far = n // 2
+    near = [d for d in range(n) if d != far]
+    first, second, (rows_ref, mixed_ref, sum_ref, top_ref) = refs[: n - 1], refs[n - 1 : -4], refs[-4:]
+    marks = frame_marks(at_ref[0], near, n)
     keys_marks = key_marks(near, ROWS, n)
-    for d in range(n):
-        rows_ref[d] = query_refs[d][...]
+    half = ROWS // 2
+    for d, first_ref, second_ref in zip(near, first, second):
+        rows_ref[d, :half] = first_ref[QUERY_ROWS, :]
+        rows_ref[d, half:] = second_ref[QUERY_ROWS, :]
+    rows_ref[far] = jnp.zeros(rows_ref.shape[1:], rows_ref.dtype)
     for head in range(heads):
         cols = slice(head * HD, (head + 1) * HD)
-        queries = jnp.concatenate([rows_of(query_refs, slice(0, ROWS), cols), marks], axis=1)
-        keys = jnp.concatenate([rows_of(kv_refs, 0, cols, ROWS), keys_marks], axis=1)
-        weights, top = soften(scores_of(queries, keys))
-        mixed, total = mix(weights, rows_of(kv_refs, 1, cols, ROWS))
-        for d in range(n):
-            rows = slice(d * ROWS, (d + 1) * ROWS)
+        queries = [ref[QUERY_ROWS, cols] for pair in zip(first, second) for ref in pair]
+        keys = jnp.concatenate([rows_of(first, TOKEN_ROWS, cols, ROWS), keys_marks], axis=1)
+        weights, top = soften(scores_of(jnp.concatenate([jnp.concatenate(queries, axis=0), marks], axis=1), keys))
+        mixed, total = mix(weights, rows_of(second, TOKEN_ROWS, cols, ROWS))
+        for i, d in enumerate(near):
+            rows = slice(i * ROWS, (i + 1) * ROWS)
             mixed_ref[head, d], sum_ref[head, d], top_ref[head, d] = mixed[rows], total[rows], top[rows]
-
-
-def finish_kernel(heads, n, flip_core, at_ref, rows_ref, mixed_ref, sum_ref, top_ref, kv_ref, w_ref, out_ref):
+        mixed_ref[head, far] = jnp.zeros((ROWS, HD), jnp.float32)
+        sum_ref[head, far] = jnp.ones((ROWS, HD), jnp.float32)
+        top_ref[head, far] = jnp.zeros((ROWS, HD), jnp.float32)
+
+
+def finish(heads, n, flip_core, at_ref, state, far_keys_ref, far_values_ref, far_rows_ref, w_ref):
+    rows_ref, mixed_ref, sum_ref, top_ref = state
+    far = n // 2
     blocks = slot_blocks(at_ref, flip_core, n)
     marks = frame_marks(at_ref[0], blocks, n)
-    keys_marks = key_marks([n // 2], TPF, n)
+    keys_marks = key_marks([far], TPF, n)
     attended = []
 
     def of(ref, head):
@@ -195,15 +229,35 @@
     for head in range(heads):
         cols = slice(head * HD, (head + 1) * HD)
         queries = jnp.concatenate([rows_ref[block, :, cols] for block in blocks], axis=0)
-        keys = jnp.concatenate([rows_of([kv_ref], 0, cols, TPF), keys_marks], axis=1)
+        keys = jnp.concatenate([rows_of([far_keys_ref], TOKEN_ROWS, cols, TPF), keys_marks], axis=1)
         before = of(top_ref, head)
         weights, top = soften(scores_of(jnp.concatenate([queries, marks], axis=1), keys), before)
-        mixed, total = mix(weights, rows_of([kv_ref], 1, cols, TPF))
+        mixed, total = mix(weights, rows_of([far_values_ref], TOKEN_ROWS, cols, TPF))
         kept = jnp.exp2((before - top) * SCALE)
         mixed, total = mixed + of(mixed_ref, head) * kept, total + of(sum_ref, head) * kept
-        attended.append((mixed / total).astype(jnp.bfloat16))
-    rows = jnp.concatenate(attended, axis=1)
-    out_ref[...] = jnp.dot(rows, w_ref[...], preferred_element_type=jnp.float32).astype(out_ref.dtype)
+        result = (mixed / total).astype(jnp.bfloat16)
+        result = [
+            jnp.where(block == far, far_rows_ref[:, cols], result[i * ROWS : (i + 1) * ROWS])
+            for i, block in enumerate(blocks)
+        ]
+        attended.append(jnp.concatenate(result, axis=0))
+    return jnp.dot(jnp.concatenate(attended, axis=1), w_ref[...], preferred_element_type=jnp.float32)
+
+
+def given_kernel(heads, n, at_ref, *refs):
+    far = n // 2
+    first, second, state, (w_ref, out_ref, far_rows_ref) = refs[:n], refs[n : 2 * n], refs[2 * n : 2 * n + 4], refs[-3:]
+    for head in range(heads):
+        cols = slice(head * HD, (head + 1) * HD)
+        queries = jnp.concatenate([part[far][QUERY_ROWS, cols] for part in (first, second)], axis=0)
+        far_rows_ref[:, cols] = attend_all(at_ref[0], far, queries, first, second, cols, n)
+    result = finish(heads, n, 1, at_ref, state, first[far], second[far], far_rows_ref, w_ref)
+    out_ref[...] = result.astype(out_ref.dtype)
+
+
+def kept_kernel(heads, n, at_ref, *refs):
+    state, others, out_ref = refs[:4], refs[4:8], refs[-1]
+    out_ref[...] = finish(heads, n, 0, at_ref, state, *others)
 
 
 def call(kernel, where, operands, outs, flops):
@@ -225,28 +279,39 @@
     where = jnp.stack([ring_place(frame, n), z, y, x, core]).astype(jnp.int32)
     width, cols = out_weight.shape
     heads = width // HD
-    found_queries, found_kv = gather_ring([queries, keys_values], n)
     f32, bf16 = jnp.float32, jnp.bfloat16
+    hbm, vmem = pl.BlockSpec(memory_space=pltpu.HBM), pl.BlockSpec(memory_space=pltpu.VMEM)
+    streams = pl.pallas_call(
+        streams_kernel,
+        out_shape=[jax.ShapeDtypeStruct((ROWS + ROWS // 2, width), bf16)] * 2,
+        in_specs=[hbm] * 2,
+        out_specs=[vmem] * 2,
+        scratch_shapes=[pltpu.SemaphoreType.DMA((4,))],
+    )(queries, keys_values)
+    first, second = gather_ring(streams, n)
+    far = n // 2
     state = call(
         functools.partial(near_kernel, heads, n),
         where,
-        [*found_queries, *(found_kv[d] for d in range(n) if d != n // 2)],
+        [blocks[d] for blocks in (first, second) for d in range(n) if d != far],
         [((n, ROWS, width), bf16)] + [((heads, n, ROWS, HD), f32)] * 3,
-        4 * n * (n - 1) * ROWS**2 * width,
-    )
-
-    def finish(flip_core, dtype):
-        (rows,) = call(
-            functools.partial(finish_kernel, heads, n, flip_core),
-            where,
-            [*state, found_kv[n // 2], out_weight],
-            [((n // 2 * ROWS, cols), dtype)],
-            n * ROWS * width * cols,
-        )
-        return rows
-
-    from_core = lax.ppermute(finish(1, bf16), "heads", [(h, h ^ 1) for h in range(4)])
-    kept = finish(0, f32)
+        4 * (n - 1) ** 2 * ROWS**2 * width,
+    )
+    given, far_rows = call(
+        functools.partial(given_kernel, heads, n),
+        where,
+        [*first, *second, *state, out_weight],
+        [((n // 2 * ROWS, cols), bf16), ((ROWS, width), bf16)],
+        n * ROWS * width * cols,
+    )
+    from_core = lax.ppermute(given, "heads", [(h, h ^ 1) for h in range(4)])
+    (kept,) = call(
+        functools.partial(kept_kernel, heads, n),
+        where,
+        [*state, first[far], second[far], far_rows, out_weight],
+        [((n // 2 * ROWS, cols), f32)],
+        n * ROWS * width * cols,
+    )
     arrived = []
     for slot in range(n // 2):
         rows = slice(slot * ROWS, (slot + 1) * ROWS)

time: 63.5 us -> 63.6 us (level)
  the two profiles are of different devices: /device:TPU:2 before, /device:TPU:3 now
where the time goes in v8:
time: 63.6 us; the launch traced here: 63.1 us
  waiting for transfers between devices  24.6 us (39%)
  starting transfers between devices  23.5 us (37%)
  Pallas kernels  11.9 us (19%)
  local copies, waits for them, and re-layouts  1.93 us (3%)
  other arithmetic  0.9 us (1%)
    ppermute x14, waiting for transfers between devices, hop(): lax.ppermute(x, 'frames', [(order[i], order[(i + by) % n]) for i in range...  16.1 us
    ppermute x14, starting transfers between devices, hop(): lax.ppermute(x, 'frames', [(order[i], order[(i + by) % n]) for i in range...  10.3 us
    pallas_call x3, Pallas kernels, call(): pl.pallas_call(kernel, out_shape=[jax.ShapeDtypeStruct(shape, dtype) for...  10.2 us
    ppermute x4, starting transfers between devices, on_device_ring(): arrived.append(lax.ppermute(total, ('frames', 'heads'), pairs).astype(f32))  9.82 us
    ppermute x4, waiting for transfers between devices, on_device_ring(): arrived.append(lax.ppermute(total, ('frames', 'heads'), pairs).astype(f32))  8.54 us
    ppermute x1, starting transfers between devices, on_device_ring(): from_core = lax.ppermute(given, 'heads', [(h, h ^ 1) for h in range(4)])  3.4 us
    unnamed x6, local copies, waits for them, and re-layouts  1.85 us
    pallas_call x1, Pallas kernels, on_device_ring(): pl.pallas_call(streams_kernel, out_shape=[jax.ShapeDtypeStruct((ROWS + RO...  1.76 us
  transfers between devices with their start and end apart: 19, of which 8 were waited for; matrix products, arithmetic and copies ran while one was open for 0% of the time, Pallas kernels for 10%

profile of v8, /device:TPU:3, one launch (start us, length us, event | category | flops | bytes accessed | tf_op | source)
XLA Modules:
  0.0 63.1 jit_solution(17900041385275332420)
XLA Ops:
  0.0 1.8 %shard_map.37 = (bf16[144,640]{1,0:T(8,128)(2,1)}, bf16[144,640]{1,0:T(8,128)(2,1)}) custom-call(bf16[96,640]{1,0:T(8,128)(2,1)} %queries_ref.1, bf16[2,96,640]{2,1,0:T(8,128)(2,1)} %kv_ref.1), custom_call_target="tpu_custom_call" | custom-call | tf_op jit(solution)/shard_map/pallas_call | solution.py:284
  1.8 1.3 %collective-permute-start = (bf16[144,640]{1,0:T(8,128)(2,1)}, bf16[144,640]{1,0:T(8,128)(2,1)S(1)}, u32[]{:S(2)}, u32[]{:S(2)}) collective-permute-start(bf16[144,640]{1,0:T(8,128)(2,1)} %get-tuple-element.13.refs_0_), channel_id=1, source_target_pairs={{0,8},{8,16},{16,24},{24,28},{28,20},{20,12},{12,4},{4,0},{1,9},{9... | collective-permute-start | bytes 552968 | tf_op jit(solution)/shard_map/ppermute | solution.py:87
  3.3 1.2 %collective-permute-start.3 = (bf16[144,640]{1,0:T(8,128)(2,1)}, bf16[144,640]{1,0:T(8,128)(2,1)S(1)}, u32[]{:S(2)}, u32[]{:S(2)}) collective-permute-start(bf16[144,640]{1,0:T(8,128)(2,1)} %get-tuple-element.13.refs_0_), channel_id=1, source_target_pairs={{0,4},{8,0},{16,8},{24,16},{28,24},{20,28},{12,20},{4,12},{1,5},{9... | collective-permute-start | bytes 552968 | tf_op jit(solution)/shard_map/ppermute | solution.py:87
  4.8 2.8 %collective-permute-done.refs_1_ = bf16[144,640]{1,0:T(8,128)(2,1)S(1)} collective-permute-done((bf16[144,640]{1,0:T(8,128)(2,1)}, bf16[144,640]{1,0:T(8,128)(2,1)S(1)}, u32[]{:S(2)}, u32[]{:S(2)}) %collective-permute-start) | collective-permute-done | bytes 184352 | tf_op jit(solution)/shard_map/ppermute | solution.py:87
  7.5 1.3 %collective-permute-start.1 = (bf16[144,640]{1,0:T(8,128)(2,1)S(1)}, bf16[144,640]{1,0:T(8,128)(2,1)S(1)}, u32[]{:S(2)}, u32[]{:S(2)}) collective-permute-start(bf16[144,640]{1,0:T(8,128)(2,1)S(1)} %collective-permute-done.refs_1_), channel_id=1, source_target_pairs={{0,8},{8,16},{16,24},{24,28},{28,20},{20,12},{12,4},{4,0},{1,9},{9... | collective-permute-start | bytes 552968 | tf_op jit(solution)/shard_map/ppermute | solution.py:87
  9.0 3.5 %collective-permute-done.3.refs_6_.refs_7_ = bf16[144,640]{1,0:T(8,128)(2,1)S(1)} collective-permute-done((bf16[144,640]{1,0:T(8,128)(2,1)}, bf16[144,640]{1,0:T(8,128)(2,1)S(1)}, u32[]{:S(2)}, u32[]{:S(2)}) %collective-permute-start.3) | collective-permute-done | bytes 184352 | tf_op jit(solution)/shard_map/ppermute | solution.py:87
  12.6 1.3 %collective-permute-start.7 = (bf16[144,640]{1,0:T(8,128)(2,1)S(1)}, bf16[144,640]{1,0:T(8,128)(2,1)S(1)}, u32[]{:S(2)}, u32[]{:S(2)}) collective-permute-start(bf16[144,640]{1,0:T(8,128)(2,1)S(1)} %collective-permute-done.6.refs_8_.refs_9_), channel_id=1, source_target_pairs={{0,8},{8,16},{16,24},{24,28},{28,20},{20,12},{12,4},{4,0},{1,9},{9... | collective-permute-start | bytes 552968 | tf_op jit(solution)/shard_map/ppermute | solution.py:87
  13.9 1.5 %collective-permute-done.1.refs_2_ = bf16[144,640]{1,0:T(8,128)(2,1)S(1)} collective-permute-done((bf16[144,640]{1,0:T(8,128)(2,1)S(1)}, bf16[144,640]{1,0:T(8,128)(2,1)S(1)}, u32[]{:S(2)}, u32[]{:S(2)}) %collective-permute-start.1) | collective-permute-done | bytes 184352 | tf_op jit(solution)/shard_map/ppermute | solution.py:87
  15.4 1.3 %collective-permute-start.2 = (bf16[144,640]{1,0:T(8,128)(2,1)S(1)}, bf16[144,640]{1,0:T(8,128)(2,1)S(1)}, u32[]{:S(2)}, u32[]{:S(2)}) collective-permute-start(bf16[144,640]{1,0:T(8,128)(2,1)S(1)} %collective-permute-done.1.refs_2_), channel_id=1, source_target_pairs={{0,8},{8,16},{16,24},{24,28},{28,20},{20,12},{12,4},{4,0},{1,9},{9... | collective-permute-start | bytes 552968 | tf_op jit(solution)/shard_map/ppermute | solution.py:87
  16.9 3.5 %collective-permute-done.4.refs_5_.refs_6_ = bf16[144,640]{1,0:T(8,128)(2,1)S(1)} collective-permute-done((bf16[144,640]{1,0:T(8,128)(2,1)S(1)}, bf16[144,640]{1,0:T(8,128)(2,1)S(1)}, u32[]{:S(2)}, u32[]{:S(2)}) %collective-permute-start.4) | collective-permute-done | bytes 184352 | tf_op jit(solution)/shard_map/ppermute | solution.py:87
  20.5 1.3 %collective-permute-start.8 = (bf16[144,640]{1,0:T(8,128)(2,1)S(1)}, bf16[144,640]{1,0:T(8,128)(2,1)S(1)}, u32[]{:S(2)}, u32[]{:S(2)}) collective-permute-start(bf16[144,640]{1,0:T(8,128)(2,1)S(1)} %collective-permute-done.7.refs_9_.refs_10_), channel_id=1, source_target_pairs={{0,8},{8,16},{16,24},{24,28},{28,20},{20,12},{12,4},{4,0},{1,9},{9... | collective-permute-start | bytes 552968 | tf_op jit(solution)/shard_map/ppermute | solution.py:87
  21.8 1.3 %collective-permute-start.12 = (bf16[144,640]{1,0:T(8,128)(2,1)S(1)}, bf16[144,640]{1,0:T(8,128)(2,1)S(1)}, u32[]{:S(2)}, u32[]{:S(2)}) collective-permute-start(bf16[144,640]{1,0:T(8,128)(2,1)S(1)} %collective-permute-done.2.refs_3_), channel_id=1, source_target_pairs={{0,8},{8,16},{16,24},{24,28},{28,20},{20,12},{12,4},{4,0},{1,9},{9... | collective-permute-start | bytes 552968 | tf_op jit(solution)/shard_map/ppermute | solution.py:87
  23.1 1.2 %collective-permute-done.11.refs_11_.refs_13_ = bf16[144,640]{1,0:T(8,128)(2,1)S(1)} collective-permute-done((bf16[144,640]{1,0:T(8,128)(2,1)S(1)}, bf16[144,640]{1,0:T(8,128)(2,1)S(1)}, u32[]{:S(2)}, u32[]{:S(2)}) %collective-permute-start.11) | collective-permute-done | bytes 184352 | tf_op jit(solution)/shard_map/ppermute | solution.py:87
  24.6 3.7 %collective-permute-done.5.refs_4_.refs_5_ = bf16[144,640]{1,0:T(8,128)(2,1)S(1)} collective-permute-done((bf16[144,640]{1,0:T(8,128)(2,1)S(1)}, bf16[144,640]{1,0:T(8,128)(2,1)S(1)}, u32[]{:S(2)}, u32[]{:S(2)}) %collective-permute-start.5) | collective-permute-done | bytes 184352 | tf_op jit(solution)/shard_map/ppermute | solution.py:87
  28.3 0.9 %copy-done.1 = bf16[144,640]{1,0:T(8,128)(2,1)S(1)} copy-done((bf16[144,640]{1,0:T(8,128)(2,1)S(1)}, bf16[144,640]{1,0:T(8,128)(2,1)}, u32[]{:S(2)}) %copy-start.1) | copy-done | bytes 184344
  30.1 4.3 %shard_map.38 = (bf16[8,96,640]{2,1,0:T(8,128)(2,1)S(1)}, f32[5,8,96,128]{3,2,1,0:T(8,128)S(1)}, f32[5,8,96,128]{3,2,1,0:T(8,128)S(1)}, f32[5,8,96,128]{3,2,1,0:T(8,128)S(1)}) custom-call(s32[5]{0:T(128)S(1)} %stack.23.at_ref, bf16[144,640]{1,0:T(8,128)(2,1)S(1)} %copy-done.1, bf16[144,640]{1,0:T(8,128)(2,1)S(1)} %collective-permute-done.refs_1_, ...), custom_call_target="tpu_custom_call" | custom-call | flops 1156055040 | tf_op jit(solution)/shard_map/pallas_call | solution.py:265
  34.5 3.8 %shard_map.39 = (bf16[384,640]{1,0:T(8,128)(2,1)S(1)}, bf16[96,640]{1,0:T(8,128)(2,1)S(1)}) custom-call(s32[5]{0:T(128)S(1)} %stack.23.at_ref, bf16[144,640]{1,0:T(8,128)(2,1)S(1)} %copy-done.1, bf16[144,640]{1,0:T(8,128)(2,1)S(1)} %collective-permute-done.refs_1_, bf16[144,640]{1,0:T(8,128)(2,1)S(1)} %collective-permute-done.1.refs_2_, ...), custom_call_target="tpu_custom_call" | custom-call | flops 314572800 | tf_op jit(solution)/shard_map/pallas_call | solution.py:265
  38.3 3.4 %collective-permute-start.14 = (bf16[384,640]{1,0:T(8,128)(2,1)S(1)}, bf16[384,640]{1,0:T(8,128)(2,1)S(1)}, u32[]{:S(2)}, u32[]{:S(2)}) collective-permute-start(bf16[384,640]{1,0:T(8,128)(2,1)S(1)} %get-tuple-element.20), channel_id=1, source_target_pairs={{0,1},{1,0},{2,3},{3,2},{4,5},{5,4},{6,7},{7,6},{8,9},{9,8},{10,11... | collective-permute-start | bytes 1474568 | tf_op jit(solution)/shard_map/ppermute | solution.py:307
  41.7 2.1 %shard_map.40 = f32[384,640]{1,0:T(8,128)S(1)} custom-call(s32[5]{0:T(128)S(1)} %stack.23.at_ref, bf16[8,96,640]{2,1,0:T(8,128)(2,1)S(1)} %get-tuple-element.15.refs_16_.refs_0_, f32[5,8,96,128]{3,2,1,0:T(8,128)S(1)} %get-tuple-element.16.refs_17_.refs_1_, f32[5,8,96,128]{3,2,1,0:T(8,128)S(1)} %get-tuple-element.17.refs_18_.refs_2_, ...), custom_call_target="tpu_custom_call" | custom-call | flops 314572800 | tf_op jit(solution)/shard_map/pallas_call | solution.py:265
  43.9 3.2 %collective-permute-start.17 = (bf16[96,640]{1,0:T(8,128)(2,1)S(1)}, bf16[96,640]{1,0:T(8,128)(2,1)S(1)}, u32[]{:S(2)}, u32[]{:S(2)}) collective-permute-start(bf16[96,640]{1,0:T(8,128)(2,1)S(1)} %get-tuple-element.21), channel_id=1, source_target_pairs={{0,24},{1,28},{2,8},{3,12},{4,16},{5,20},{6,0},{7,4},{8,1},{9,5},{... | collective-permute-start | bytes 368648 | tf_op jit(solution)/shard_map/ppermute | solution.py:324
  47.1 4.2 %collective-permute-start.18 = (bf16[96,640]{1,0:T(8,128)(2,1)S(1)}, bf16[96,640]{1,0:T(8,128)(2,1)S(1)}, u32[]{:S(2)}, u32[]{:S(2)}) collective-permute-start(bf16[96,640]{1,0:T(8,128)(2,1)S(1)} %get-tuple-element.22), channel_id=1, source_target_pairs={{0,8},{1,12},{2,24},{3,28},{4,0},{5,4},{6,16},{7,20},{8,17},{9,21}... | collective-permute-start | bytes 368648 | tf_op jit(solution)/shard_map/ppermute | solution.py:324
  51.3 2.3 %collective-permute-start.16 = (bf16[96,640]{1,0:T(8,128)(2,1)S(1)}, bf16[96,640]{1,0:T(8,128)(2,1)S(1)}, u32[]{:S(2)}, u32[]{:S(2)}) collective-permute-start(bf16[96,640]{1,0:T(8,128)(2,1)S(1)} %get-tuple-element.23), channel_id=1, source_target_pairs={{0,0},{1,4},{2,16},{3,20},{4,8},{5,12},{6,24},{7,28},{8,25},{9,29}... | collective-permute-start | bytes 368648 | tf_op jit(solution)/shard_map/ppermute | solution.py:324
  53.7 3.0 %collective-permute-done.18 = bf16[96,640]{1,0:T(8,128)(2,1)S(1)} collective-permute-done((bf16[96,640]{1,0:T(8,128)(2,1)S(1)}, bf16[96,640]{1,0:T(8,128)(2,1)S(1)}, u32[]{:S(2)}, u32[]{:S(2)}) %collective-permute-start.18) | collective-permute-done | bytes 122912 | tf_op jit(solution)/shard_map/ppermute | solution.py:324
  56.7 5.6 %collective-permute-done.16 = bf16[96,640]{1,0:T(8,128)(2,1)S(1)} collective-permute-done((bf16[96,640]{1,0:T(8,128)(2,1)S(1)}, bf16[96,640]{1,0:T(8,128)(2,1)S(1)}, u32[]{:S(2)}, u32[]{:S(2)}) %collective-permute-start.16) | collective-permute-done | bytes 122912 | tf_op jit(solution)/shard_map/ppermute | solution.py:324
  (28 shorter events, 3.3 us)
Async XLA Ops:
  1.8 5.8 %collective-permute-start = (bf16[144,640]{1,0:T(8,128)(2,1)}, bf16[144,640]{1,0:T(8,128)(2,1)S(1)}, u32[]{:S(2)}, u32[]{:S(2)}) collective-permute-start(bf16[144,640]{1,0:T(8,128)(2,1)} %get-tuple-element.13.refs_0_), channel_id=1, source_target_pairs={{0,8},{8,16},{16,24},{24,28},{28,20},{20,12},{12,4},{4,0},{1,9},{9... | collective-permute-start | bytes 552968 | tf_op jit(solution)/shard_map/ppermute | solution.py:87
  3.1 5.7 %collective-permute-start.9 = (bf16[144,640]{1,0:T(8,128)(2,1)}, bf16[144,640]{1,0:T(8,128)(2,1)S(1)}, u32[]{:S(2)}, u32[]{:S(2)}) collective-permute-start(bf16[144,640]{1,0:T(8,128)(2,1)} %get-tuple-element.14.refs_7_.refs_8_), channel_id=1, source_target_pairs={{0,4},{8,0},{16,8},{24,16},{28,24},{20,28},{12,20},{4,12},{1,5},{9... | collective-permute-start | bytes 552968 | tf_op jit(solution)/shard_map/ppermute | solution.py:87
  3.3 9.2 %collective-permute-start.3 = (bf16[144,640]{1,0:T(8,128)(2,1)}, bf16[144,640]{1,0:T(8,128)(2,1)S(1)}, u32[]{:S(2)}, u32[]{:S(2)}) collective-permute-start(bf16[144,640]{1,0:T(8,128)(2,1)} %get-tuple-element.13.refs_0_), channel_id=1, source_target_pairs={{0,4},{8,0},{16,8},{24,16},{28,24},{20,28},{12,20},{4,12},{1,5},{9... | collective-permute-start | bytes 552968 | tf_op jit(solution)/shard_map/ppermute | solution.py:87
  4.5 8.1 %collective-permute-start.6 = (bf16[144,640]{1,0:T(8,128)(2,1)}, bf16[144,640]{1,0:T(8,128)(2,1)S(1)}, u32[]{:S(2)}, u32[]{:S(2)}) collective-permute-start(bf16[144,640]{1,0:T(8,128)(2,1)} %get-tuple-element.14.refs_7_.refs_8_), channel_id=1, source_target_pairs={{0,8},{8,16},{16,24},{24,28},{28,20},{20,12},{12,4},{4,0},{1,9},{9... | collective-permute-start | bytes 552968 | tf_op jit(solution)/shard_map/ppermute | solution.py:87
  7.5 7.9 %collective-permute-start.1 = (bf16[144,640]{1,0:T(8,128)(2,1)S(1)}, bf16[144,640]{1,0:T(8,128)(2,1)S(1)}, u32[]{:S(2)}, u32[]{:S(2)}) collective-permute-start(bf16[144,640]{1,0:T(8,128)(2,1)S(1)} %collective-permute-done.refs_1_), channel_id=1, source_target_pairs={{0,8},{8,16},{16,24},{24,28},{28,20},{20,12},{12,4},{4,0},{1,9},{9... | collective-permute-start | bytes 552968 | tf_op jit(solution)/shard_map/ppermute | solution.py:87
  8.8 7.9 %collective-permute-start.10 = (bf16[144,640]{1,0:T(8,128)(2,1)S(1)}, bf16[144,640]{1,0:T(8,128)(2,1)S(1)}, u32[]{:S(2)}, u32[]{:S(2)}) collective-permute-start(bf16[144,640]{1,0:T(8,128)(2,1)S(1)} %collective-permute-done.9.refs_13_.refs_15_), channel_id=1, source_target_pairs={{0,4},{8,0},{16,8},{24,16},{28,24},{20,28},{12,20},{4,12},{1,5},{9... | collective-permute-start | bytes 552968 | tf_op jit(solution)/shard_map/ppermute | solution.py:87
  12.5 7.9 %collective-permute-start.4 = (bf16[144,640]{1,0:T(8,128)(2,1)S(1)}, bf16[144,640]{1,0:T(8,128)(2,1)S(1)}, u32[]{:S(2)}, u32[]{:S(2)}) collective-permute-start(bf16[144,640]{1,0:T(8,128)(2,1)S(1)} %collective-permute-done.3.refs_6_.refs_7_), channel_id=1, source_target_pairs={{0,4},{8,0},{16,8},{24,16},{28,24},{20,28},{12,20},{4,12},{1,5},{9... | collective-permute-start | bytes 552968 | tf_op jit(solution)/shard_map/ppermute | solution.py:87
  12.6 7.9 %collective-permute-start.7 = (bf16[144,640]{1,0:T(8,128)(2,1)S(1)}, bf16[144,640]{1,0:T(8,128)(2,1)S(1)}, u32[]{:S(2)}, u32[]{:S(2)}) collective-permute-start(bf16[144,640]{1,0:T(8,128)(2,1)S(1)} %collective-permute-done.6.refs_8_.refs_9_), channel_id=1, source_target_pairs={{0,8},{8,16},{16,24},{24,28},{28,20},{20,12},{12,4},{4,0},{1,9},{9... | collective-permute-start | bytes 552968 | tf_op jit(solution)/shard_map/ppermute | solution.py:87
  15.4 6.4 %collective-permute-start.2 = (bf16[144,640]{1,0:T(8,128)(2,1)S(1)}, bf16[144,640]{1,0:T(8,128)(2,1)S(1)}, u32[]{:S(2)}, u32[]{:S(2)}) collective-permute-start(bf16[144,640]{1,0:T(8,128)(2,1)S(1)} %collective-permute-done.1.refs_2_), channel_id=1, source_target_pairs={{0,8},{8,16},{16,24},{24,28},{28,20},{20,12},{12,4},{4,0},{1,9},{9... | collective-permute-start | bytes 552968 | tf_op jit(solution)/shard_map/ppermute | solution.py:87
  16.7 7.6 %collective-permute-start.11 = (bf16[144,640]{1,0:T(8,128)(2,1)S(1)}, bf16[144,640]{1,0:T(8,128)(2,1)S(1)}, u32[]{:S(2)}, u32[]{:S(2)}) collective-permute-start(bf16[144,640]{1,0:T(8,128)(2,1)S(1)} %collective-permute-done.10.refs_12_.refs_14_), channel_id=1, source_target_pairs={{0,4},{8,0},{16,8},{24,16},{28,24},{20,28},{12,20},{4,12},{1,5},{9... | collective-permute-start | bytes 552968 | tf_op jit(solution)/shard_map/ppermute | solution.py:87
  20.4 7.9 %collective-permute-start.5 = (bf16[144,640]{1,0:T(8,128)(2,1)S(1)}, bf16[144,640]{1,0:T(8,128)(2,1)S(1)}, u32[]{:S(2)}, u32[]{:S(2)}) collective-permute-start(bf16[144,640]{1,0:T(8,128)(2,1)S(1)} %collective-permute-done.4.refs_5_.refs_6_), channel_id=1, source_target_pairs={{0,4},{8,0},{16,8},{24,16},{28,24},{20,28},{12,20},{4,12},{1,5},{9... | collective-permute-start | bytes 552968 | tf_op jit(solution)/shard_map/ppermute | solution.py:87
  20.5 7.7 %collective-permute-start.8 = (bf16[144,640]{1,0:T(8,128)(2,1)S(1)}, bf16[144,640]{1,0:T(8,128)(2,1)S(1)}, u32[]{:S(2)}, u32[]{:S(2)}) collective-permute-start(bf16[144,640]{1,0:T(8,128)(2,1)S(1)} %collective-permute-done.7.refs_9_.refs_10_), channel_id=1, source_target_pairs={{0,8},{8,16},{16,24},{24,28},{28,20},{20,12},{12,4},{4,0},{1,9},{9... | collective-permute-start | bytes 552968 | tf_op jit(solution)/shard_map/ppermute | solution.py:87
  21.8 12.6 %collective-permute-start.12 = (bf16[144,640]{1,0:T(8,128)(2,1)S(1)}, bf16[144,640]{1,0:T(8,128)(2,1)S(1)}, u32[]{:S(2)}, u32[]{:S(2)}) collective-permute-start(bf16[144,640]{1,0:T(8,128)(2,1)S(1)} %collective-permute-done.2.refs_3_), channel_id=1, source_target_pairs={{0,8},{8,16},{16,24},{24,28},{28,20},{20,12},{12,4},{4,0},{1,9},{9... | collective-permute-start | bytes 552968 | tf_op jit(solution)/shard_map/ppermute | solution.py:87
  24.3 10.2 %collective-permute-start.13 = (bf16[144,640]{1,0:T(8,128)(2,1)S(1)}, bf16[144,640]{1,0:T(8,128)(2,1)S(1)}, u32[]{:S(2)}, u32[]{:S(2)}) collective-permute-start(bf16[144,640]{1,0:T(8,128)(2,1)S(1)} %collective-permute-done.11.refs_11_.refs_13_), channel_id=1, source_target_pairs={{0,4},{8,0},{16,8},{24,16},{28,24},{20,28},{12,20},{4,12},{1,5},{9... | collective-permute-start | bytes 552968 | tf_op jit(solution)/shard_map/ppermute | solution.py:87
  24.6 9.9 %copy-start = (bf16[640,640]{1,0:T(8,128)(2,1)S(1)}, bf16[640,640]{1,0:T(8,128)(2,1)}, u32[]{:S(2)}) copy-start(bf16[640,640]{1,0:T(8,128)(2,1)} %refs_7_.1) | copy-start | bytes 2457604
  28.3 0.9 %copy-start.1 = (bf16[144,640]{1,0:T(8,128)(2,1)S(1)}, bf16[144,640]{1,0:T(8,128)(2,1)}, u32[]{:S(2)}) copy-start(bf16[144,640]{1,0:T(8,128)(2,1)} %get-tuple-element.13.refs_0_) | copy-start | bytes 552964
  29.2 0.9 %copy-start.2 = (bf16[144,640]{1,0:T(8,128)(2,1)S(1)}, bf16[144,640]{1,0:T(8,128)(2,1)}, u32[]{:S(2)}) copy-start(bf16[144,640]{1,0:T(8,128)(2,1)} %get-tuple-element.14.refs_7_.refs_8_) | copy-start | bytes 552964
  38.3 5.5 %collective-permute-start.14 = (bf16[384,640]{1,0:T(8,128)(2,1)S(1)}, bf16[384,640]{1,0:T(8,128)(2,1)S(1)}, u32[]{:S(2)}, u32[]{:S(2)}) collective-permute-start(bf16[384,640]{1,0:T(8,128)(2,1)S(1)} %get-tuple-element.20), channel_id=1, source_target_pairs={{0,1},{1,0},{2,3},{3,2},{4,5},{5,4},{6,7},{7,6},{8,9},{9,8},{10,11... | collective-permute-start | bytes 1474568 | tf_op jit(solution)/shard_map/ppermute | solution.py:307
  43.9 9.9 %collective-permute-start.17 = (bf16[96,640]{1,0:T(8,128)(2,1)S(1)}, bf16[96,640]{1,0:T(8,128)(2,1)S(1)}, u32[]{:S(2)}, u32[]{:S(2)}) collective-permute-start(bf16[96,640]{1,0:T(8,128)(2,1)S(1)} %get-tuple-element.21), channel_id=1, source_target_pairs={{0,24},{1,28},{2,8},{3,12},{4,16},{5,20},{6,0},{7,4},{8,1},{9,5},{... | collective-permute-start | bytes 368648 | tf_op jit(solution)/shard_map/ppermute | solution.py:324
  47.1 9.6 %collective-permute-start.18 = (bf16[96,640]{1,0:T(8,128)(2,1)S(1)}, bf16[96,640]{1,0:T(8,128)(2,1)S(1)}, u32[]{:S(2)}, u32[]{:S(2)}) collective-permute-start(bf16[96,640]{1,0:T(8,128)(2,1)S(1)} %get-tuple-element.22), channel_id=1, source_target_pairs={{0,8},{1,12},{2,24},{3,28},{4,0},{5,4},{6,16},{7,20},{8,17},{9,21}... | collective-permute-start | bytes 368648 | tf_op jit(solution)/shard_map/ppermute | solution.py:324
  51.3 11.0 %collective-permute-start.16 = (bf16[96,640]{1,0:T(8,128)(2,1)S(1)}, bf16[96,640]{1,0:T(8,128)(2,1)S(1)}, u32[]{:S(2)}, u32[]{:S(2)}) collective-permute-start(bf16[96,640]{1,0:T(8,128)(2,1)S(1)} %get-tuple-element.23), channel_id=1, source_target_pairs={{0,0},{1,4},{2,16},{3,20},{4,8},{5,12},{6,24},{7,28},{8,25},{9,29}... | collective-permute-start | bytes 368648 | tf_op jit(solution)/shard_map/ppermute | solution.py:324
  53.6 8.6 %collective-permute-start.15 = (bf16[96,640]{1,0:T(8,128)(2,1)S(1)}, bf16[96,640]{1,0:T(8,128)(2,1)S(1)}, u32[]{:S(2)}, u32[]{:S(2)}) collective-permute-start(bf16[96,640]{1,0:T(8,128)(2,1)S(1)} %get-tuple-element.24), channel_id=1, source_target_pairs={{0,16},{1,20},{2,0},{3,4},{4,24},{5,28},{6,8},{7,12},{8,9},{9,13},... | collective-permute-start | bytes 368648 | tf_op jit(solution)/shard_map/ppermute | solution.py:324

commit v9 on v7

--- a/solution.py
+++ b/solution.py
@@ -92,7 +92,7 @@
     for step in range(1, n // 2 + 1):
         for j, blocks in enumerate(found):
             for by in (1, -1):
-                if step < n // 2 or (j == 0) == (by == 1):
+                if step < n // 2 or (j % 2 == 0) == (by == 1):
                     blocks[by * step % n] = hop(blocks[by * (step - 1) % n], n, by)
     return found
 
@@ -117,8 +117,8 @@
     return jnp.concatenate([jnp.where(lane == frame, -1e30, 0.0) for frame in frames], axis=0).astype(jnp.bfloat16)
 
 
-def rows_of(refs, rows, cols, padding=0):
-    pieces = [ref[rows, cols] if len(ref.shape) == 2 else ref[rows, :, cols] for ref in refs]
+def rows_of(refs, cols, padding=0):
+    pieces = [ref[:, cols] for ref in refs]
     if padding:
         pieces.append(jnp.zeros((padding, HD), jnp.bfloat16))
     return jnp.concatenate(pieces, axis=0)
@@ -165,25 +165,33 @@
     return blocks
 
 
-def near_kernel(heads, n, at_ref, *refs):
+def split_kernel(kv_ref, keys_ref, values_ref):
+    keys_ref[...] = kv_ref[0]
+    values_ref[...] = kv_ref[1]
+
+
+def rows_kernel(n, *refs):
+    for d in range(n):
+        refs[n][d] = refs[d][...]
+
+
+def near_kernel(heads, n, at_ref, rows_ref, *refs):
     near = [d for d in range(n) if d != n // 2]
-    query_refs, kv_refs, (rows_ref, mixed_ref, sum_ref, top_ref) = refs[:n], refs[n:-4], refs[-4:]
+    key_refs, value_refs, (mixed_ref, sum_ref, top_ref) = refs[: n - 1], refs[n - 1 : -3], refs[-3:]
     marks = frame_marks(at_ref[0], range(n), n)
     keys_marks = key_marks(near, ROWS, n)
-    for d in range(n):
-        rows_ref[d] = query_refs[d][...]
     for head in range(heads):
         cols = slice(head * HD, (head + 1) * HD)
-        queries = jnp.concatenate([rows_of(query_refs, slice(0, ROWS), cols), marks], axis=1)
-        keys = jnp.concatenate([rows_of(kv_refs, 0, cols, ROWS), keys_marks], axis=1)
+        queries = jnp.concatenate([rows_ref[:, :, cols].reshape(n * ROWS, HD), marks], axis=1)
+        keys = jnp.concatenate([rows_of(key_refs, cols, ROWS), keys_marks], axis=1)
         weights, top = soften(scores_of(queries, keys))
-        mixed, total = mix(weights, rows_of(kv_refs, 1, cols, ROWS))
+        mixed, total = mix(weights, rows_of(value_refs, cols, ROWS))
         for d in range(n):
             rows = slice(d * ROWS, (d + 1) * ROWS)
             mixed_ref[head, d], sum_ref[head, d], top_ref[head, d] = mixed[rows], total[rows], top[rows]
 
 
-def finish_kernel(heads, n, flip_core, at_ref, rows_ref, mixed_ref, sum_ref, top_ref, kv_ref, w_ref, out_ref):
+def finish_kernel(heads, n, flip_core, at_ref, rows_ref, mixed_ref, sum_ref, top_ref, keys_ref, values_ref, w_ref, out_ref):
     blocks = slot_blocks(at_ref, flip_core, n)
     marks = frame_marks(at_ref[0], blocks, n)
     keys_marks = key_marks([n // 2], TPF, n)
@@ -195,10 +203,10 @@
     for head in range(heads):
         cols = slice(head * HD, (head + 1) * HD)
         queries = jnp.concatenate([rows_ref[block, :, cols] for block in blocks], axis=0)
-        keys = jnp.concatenate([rows_of([kv_ref], 0, cols, TPF), keys_marks], axis=1)
+        keys = jnp.concatenate([rows_of([keys_ref], cols, TPF), keys_marks], axis=1)
         before = of(top_ref, head)
         weights, top = soften(scores_of(jnp.concatenate([queries, marks], axis=1), keys), before)
-        mixed, total = mix(weights, rows_of([kv_ref], 1, cols, TPF))
+        mixed, total = mix(weights, rows_of([values_ref], cols, TPF))
         kept = jnp.exp2((before - top) * SCALE)
         mixed, total = mixed + of(mixed_ref, head) * kept, total + of(sum_ref, head) * kept
         attended.append((mixed / total).astype(jnp.bfloat16))
@@ -206,16 +214,16 @@
     out_ref[...] = jnp.dot(rows, w_ref[...], preferred_element_type=jnp.float32).astype(out_ref.dtype)
 
 
-def call(kernel, where, operands, outs, flops):
+def call(kernel, scalars, operands, outs, flops):
     vmem = pl.BlockSpec(memory_space=pltpu.VMEM)
     return pl.pallas_call(
         kernel,
         out_shape=[jax.ShapeDtypeStruct(shape, dtype) for shape, dtype in outs],
-        in_specs=[pl.BlockSpec(memory_space=pltpu.SMEM)] + [vmem] * len(operands),
+        in_specs=[pl.BlockSpec(memory_space=pltpu.SMEM)] * len(scalars) + [vmem] * len(operands),
         out_specs=[vmem] * len(outs),
         compiler_params=pltpu.CompilerParams(vmem_limit_bytes=20 * 1024 * 1024),
         cost_estimate=pl.CostEstimate(flops=flops, bytes_accessed=0, transcendentals=0),
-    )(where, *operands)
+    )(*scalars, *operands)
 
 
 def on_device_ring(queries, keys_values, out_weight):
@@ -225,25 +233,29 @@
     where = jnp.stack([ring_place(frame, n), z, y, x, core]).astype(jnp.int32)
     width, cols = out_weight.shape
     heads = width // HD
-    found_queries, found_kv = gather_ring([queries, keys_values], n)
     f32, bf16 = jnp.float32, jnp.bfloat16
+    block = (queries.shape, bf16)
+    own = call(split_kernel, (), [keys_values], [block, block], 0)
+    queries, keys, values = gather_ring([queries, *own], n)
+    (rows,) = call(functools.partial(rows_kernel, n), (), queries, [((n, ROWS, width), bf16)], 0)
+    far = n // 2
     state = call(
         functools.partial(near_kernel, heads, n),
-        where,
-        [*found_queries, *(found_kv[d] for d in range(n) if d != n // 2)],
-        [((n, ROWS, width), bf16)] + [((heads, n, ROWS, HD), f32)] * 3,
+        (where,),
+        [rows, *(blocks[d] for blocks in (keys, values) for d in range(n) if d != far)],
+        [((heads, n, ROWS, HD), f32)] * 3,
         4 * n * (n - 1) * ROWS**2 * width,
     )
 
     def finish(flip_core, dtype):
-        (rows,) = call(
+        (sums,) = call(
             functools.partial(finish_kernel, heads, n, flip_core),
-            where,
-            [*state, found_kv[n // 2], out_weight],
+            (where,),
+            [rows, *state, keys[far], values[far], out_weight],
             [((n // 2 * ROWS, cols), dtype)],
             n * ROWS * width * cols,
         )
-        return rows
+        return sums
 
     from_core = lax.ppermute(finish(1, bf16), "heads", [(h, h ^ 1) for h in range(4)])
     kept = finish(0, f32)

time: 63.5 us -> 60.2 us (0.948)
  the two profiles are of different devices: /device:TPU:2 before, /device:TPU:1 now
where the time goes in v9:
time: 60.2 us; the launch traced here: 60 us
  starting transfers between devices  36.8 us (61%)
  waiting for transfers between devices  11.3 us (19%)
  Pallas kernels  8.97 us (15%)
  local copies, waits for them, and re-layouts  1.94 us (3%)
  other arithmetic  0.89 us (1%)
    ppermute x21, starting transfers between devices, hop(): lax.ppermute(x, 'frames', [(order[i], order[(i + by) % n]) for i in range...  21.4 us
    ppermute x4, starting transfers between devices, on_device_ring(): arrived.append(lax.ppermute(total, ('frames', 'heads'), pairs).astype(f32))  10.9 us
    pallas_call x5, Pallas kernels, call(): pl.pallas_call(kernel, out_shape=[jax.ShapeDtypeStruct(shape, dtype) for...  8.97 us
    ppermute x4, waiting for transfers between devices, on_device_ring(): arrived.append(lax.ppermute(total, ('frames', 'heads'), pairs).astype(f32))  7.32 us
    ppermute x1, starting transfers between devices, on_device_ring(): lax.ppermute(finish(1, bf16), 'heads', [(h, h ^ 1) for h in range(4)])  4.43 us
    ppermute x21, waiting for transfers between devices, hop(): lax.ppermute(x, 'frames', [(order[i], order[(i + by) % n]) for i in range...  4.01 us
    unnamed x6, local copies, waits for them, and re-layouts  1.85 us
  transfers between devices with their start and end apart: 26, of which 8 were waited for; matrix products, arithmetic and copies ran while one was open for 0% of the time, Pallas kernels for 12%

profile of v9, /device:TPU:1, one launch (start us, length us, event | category | flops | bytes accessed | tf_op | source)
XLA Modules:
  0.0 60.0 jit_solution(13555193595777129470)
XLA Ops:
  0.0 2.1 %collective-permute-start = (bf16[96,640]{1,0:T(8,128)(2,1)}, bf16[96,640]{1,0:T(8,128)(2,1)S(1)}, u32[]{:S(2)}, u32[]{:S(2)}) collective-permute-start(bf16[96,640]{1,0:T(8,128)(2,1)} %refs_0_.1), channel_id=1, source_target_pairs={{0,8},{8,16},{16,24},{24,28},{28,20},{20,12},{12,4},{4,0},{1,9},{9... | collective-permute-start | bytes 368648 | tf_op jit(solution)/shard_map/ppermute | solution.py:87
  3.1 1.5 %collective-permute-start.7 = (bf16[96,640]{1,0:T(8,128)(2,1)S(1)}, bf16[96,640]{1,0:T(8,128)(2,1)S(1)}, u32[]{:S(2)}, u32[]{:S(2)}) collective-permute-start(bf16[96,640]{1,0:T(8,128)(2,1)S(1)} %get-tuple-element.10.refs_0_), channel_id=1, source_target_pairs={{0,8},{8,16},{16,24},{24,28},{28,20},{20,12},{12,4},{4,0},{1,9},{9... | collective-permute-start | bytes 368648 | tf_op jit(solution)/shard_map/ppermute | solution.py:87
  4.6 1.5 %collective-permute-start.13 = (bf16[96,640]{1,0:T(8,128)(2,1)S(1)}, bf16[96,640]{1,0:T(8,128)(2,1)S(1)}, u32[]{:S(2)}, u32[]{:S(2)}) collective-permute-start(bf16[96,640]{1,0:T(8,128)(2,1)S(1)} %get-tuple-element.11.refs_7_), channel_id=1, source_target_pairs={{0,8},{8,16},{16,24},{24,28},{28,20},{20,12},{12,4},{4,0},{1,9},{9... | collective-permute-start | bytes 368648 | tf_op jit(solution)/shard_map/ppermute | solution.py:87
  6.5 1.2 %collective-permute-start.1 = (bf16[96,640]{1,0:T(8,128)(2,1)S(1)}, bf16[96,640]{1,0:T(8,128)(2,1)S(1)}, u32[]{:S(2)}, u32[]{:S(2)}) collective-permute-start(bf16[96,640]{1,0:T(8,128)(2,1)S(1)} %collective-permute-done.refs_1_), channel_id=1, source_target_pairs={{0,8},{8,16},{16,24},{24,28},{28,20},{20,12},{12,4},{4,0},{1,9},{9... | collective-permute-start | bytes 368648 | tf_op jit(solution)/shard_map/ppermute | solution.py:87
  9.1 1.3 %collective-permute-start.8 = (bf16[96,640]{1,0:T(8,128)(2,1)S(1)}, bf16[96,640]{1,0:T(8,128)(2,1)S(1)}, u32[]{:S(2)}, u32[]{:S(2)}) collective-permute-start(bf16[96,640]{1,0:T(8,128)(2,1)S(1)} %collective-permute-done.7.refs_1_), channel_id=1, source_target_pairs={{0,8},{8,16},{16,24},{24,28},{28,20},{20,12},{12,4},{4,0},{1,9},{9... | collective-permute-start | bytes 368648 | tf_op jit(solution)/shard_map/ppermute | solution.py:87
  10.4 1.1 %collective-permute-start.11 = (bf16[96,640]{1,0:T(8,128)(2,1)S(1)}, bf16[96,640]{1,0:T(8,128)(2,1)S(1)}, u32[]{:S(2)}, u32[]{:S(2)}) collective-permute-start(bf16[96,640]{1,0:T(8,128)(2,1)S(1)} %collective-permute-done.10.refs_6_), channel_id=1, source_target_pairs={{0,4},{8,0},{16,8},{24,16},{28,24},{20,28},{12,20},{4,12},{1,5},{9... | collective-permute-start | bytes 368648 | tf_op jit(solution)/shard_map/ppermute | solution.py:87
  11.5 1.3 %collective-permute-start.14 = (bf16[96,640]{1,0:T(8,128)(2,1)S(1)}, bf16[96,640]{1,0:T(8,128)(2,1)S(1)}, u32[]{:S(2)}, u32[]{:S(2)}) collective-permute-start(bf16[96,640]{1,0:T(8,128)(2,1)S(1)} %collective-permute-done.13.refs_8_), channel_id=1, source_target_pairs={{0,8},{8,16},{16,24},{24,28},{28,20},{20,12},{12,4},{4,0},{1,9},{9... | collective-permute-start | bytes 368648 | tf_op jit(solution)/shard_map/ppermute | solution.py:87
  12.9 1.3 %collective-permute-start.2 = (bf16[96,640]{1,0:T(8,128)(2,1)S(1)}, bf16[96,640]{1,0:T(8,128)(2,1)S(1)}, u32[]{:S(2)}, u32[]{:S(2)}) collective-permute-start(bf16[96,640]{1,0:T(8,128)(2,1)S(1)} %collective-permute-done.1.refs_2_), channel_id=1, source_target_pairs={{0,8},{8,16},{16,24},{24,28},{28,20},{20,12},{12,4},{4,0},{1,9},{9... | collective-permute-start | bytes 368648 | tf_op jit(solution)/shard_map/ppermute | solution.py:87
  14.4 1.0 %collective-permute-done.8.refs_2_ = bf16[96,640]{1,0:T(8,128)(2,1)S(1)} collective-permute-done((bf16[96,640]{1,0:T(8,128)(2,1)S(1)}, bf16[96,640]{1,0:T(8,128)(2,1)S(1)}, u32[]{:S(2)}, u32[]{:S(2)}) %collective-permute-start.8) | collective-permute-done | bytes 122912 | tf_op jit(solution)/shard_map/ppermute | solution.py:87
  15.4 1.4 %collective-permute-start.6 = (bf16[96,640]{1,0:T(8,128)(2,1)S(1)}, bf16[96,640]{1,0:T(8,128)(2,1)S(1)}, u32[]{:S(2)}, u32[]{:S(2)}) collective-permute-start(bf16[96,640]{1,0:T(8,128)(2,1)S(1)} %collective-permute-done.5.refs_6_), channel_id=1, source_target_pairs={{0,4},{8,0},{16,8},{24,16},{28,24},{20,28},{12,20},{4,12},{1,5},{9... | collective-permute-start | bytes 368648 | tf_op jit(solution)/shard_map/ppermute | solution.py:87
  16.8 1.3 %collective-permute-start.12 = (bf16[96,640]{1,0:T(8,128)(2,1)S(1)}, bf16[96,640]{1,0:T(8,128)(2,1)S(1)}, u32[]{:S(2)}, u32[]{:S(2)}) collective-permute-start(bf16[96,640]{1,0:T(8,128)(2,1)S(1)} %collective-permute-done.11.refs_5_), channel_id=1, source_target_pairs={{0,4},{8,0},{16,8},{24,16},{28,24},{20,28},{12,20},{4,12},{1,5},{9... | collective-permute-start | bytes 368648 | tf_op jit(solution)/shard_map/ppermute | solution.py:87
  18.1 1.4 %collective-permute-start.15 = (bf16[96,640]{1,0:T(8,128)(2,1)S(1)}, bf16[96,640]{1,0:T(8,128)(2,1)S(1)}, u32[]{:S(2)}, u32[]{:S(2)}) collective-permute-start(bf16[96,640]{1,0:T(8,128)(2,1)S(1)} %collective-permute-done.14.refs_9_), channel_id=1, source_target_pairs={{0,8},{8,16},{16,24},{24,28},{28,20},{20,12},{12,4},{4,0},{1,9},{9... | collective-permute-start | bytes 368648 | tf_op jit(solution)/shard_map/ppermute | solution.py:87
  20.4 1.7 %collective-permute-start.3 = (bf16[96,640]{1,0:T(8,128)(2,1)S(1)}, bf16[96,640]{1,0:T(8,128)(2,1)S(1)}, u32[]{:S(2)}, u32[]{:S(2)}) collective-permute-start(bf16[96,640]{1,0:T(8,128)(2,1)S(1)} %collective-permute-done.2.refs_3_), channel_id=1, source_target_pairs={{0,8},{8,16},{16,24},{24,28},{28,20},{20,12},{12,4},{4,0},{1,9},{9... | collective-permute-start | bytes 368648 | tf_op jit(solution)/shard_map/ppermute | solution.py:87
  22.1 1.3 %collective-permute-start.9 = (bf16[96,640]{1,0:T(8,128)(2,1)S(1)}, bf16[96,640]{1,0:T(8,128)(2,1)S(1)}, u32[]{:S(2)}, u32[]{:S(2)}) collective-permute-start(bf16[96,640]{1,0:T(8,128)(2,1)S(1)} %collective-permute-done.8.refs_2_), channel_id=1, source_target_pairs={{0,8},{8,16},{16,24},{24,28},{28,20},{20,12},{12,4},{4,0},{1,9},{9... | collective-permute-start | bytes 368648 | tf_op jit(solution)/shard_map/ppermute | solution.py:87
  23.7 1.5 %collective-permute-start.20 = (bf16[96,640]{1,0:T(8,128)(2,1)S(1)}, bf16[96,640]{1,0:T(8,128)(2,1)S(1)}, u32[]{:S(2)}, u32[]{:S(2)}) collective-permute-start(bf16[96,640]{1,0:T(8,128)(2,1)S(1)} %collective-permute-done.15.refs_10_), channel_id=1, source_target_pairs={{0,8},{8,16},{16,24},{24,28},{28,20},{20,12},{12,4},{4,0},{1,9},{9... | collective-permute-start | bytes 368648 | tf_op jit(solution)/shard_map/ppermute | solution.py:87
  26.1 1.1 %collective-permute-done.9.refs_3_ = bf16[96,640]{1,0:T(8,128)(2,1)S(1)} collective-permute-done((bf16[96,640]{1,0:T(8,128)(2,1)S(1)}, bf16[96,640]{1,0:T(8,128)(2,1)S(1)}, u32[]{:S(2)}, u32[]{:S(2)}) %collective-permute-start.9) | collective-permute-done | bytes 122912 | tf_op jit(solution)/shard_map/ppermute | solution.py:87
  27.5 4.8 %shard_map.39 = (f32[5,8,96,128]{3,2,1,0:T(8,128)S(1)}, f32[5,8,96,128]{3,2,1,0:T(8,128)S(1)}, f32[5,8,96,128]{3,2,1,0:T(8,128)S(1)}) custom-call(s32[5]{0:T(128)S(1)} %stack.23.at_ref, bf16[8,96,640]{2,1,0:T(8,128)(2,1)S(1)} %shard_map.37.rows_ref, bf16[96,640]{1,0:T(8,128)(2,1)S(1)} %get-tuple-element.10.refs_0_, ...), custom_call_target="tpu_custom_call" | custom-call | flops 1321205760 | tf_op jit(solution)/shard_map/pallas_call | solution.py:219
  32.3 2.1 %shard_map.41 = bf16[384,640]{1,0:T(8,128)(2,1)S(1)} custom-call(s32[5]{0:T(128)S(1)} %stack.23.at_ref, bf16[8,96,640]{2,1,0:T(8,128)(2,1)S(1)} %shard_map.37.rows_ref, f32[5,8,96,128]{3,2,1,0:T(8,128)S(1)} %get-tuple-element.12.mixed_ref, f32[5,8,96,128]{3,2,1,0:T(8,128)S(1)} %get-tuple-element.13.sum_ref, f32[5,8,96,128]{3,2,1,0:T(8,128)S(1)} %get-tuple-element.14.top_ref, ...), custom_call_target="tpu_custom_call" | custom-call | flops 314572800 | tf_op jit(solution)/shard_map/pallas_call | solution.py:219
  34.4 4.4 %collective-permute-start.21 = (bf16[384,640]{1,0:T(8,128)(2,1)S(1)}, bf16[384,640]{1,0:T(8,128)(2,1)S(1)}, u32[]{:S(2)}, u32[]{:S(2)}) collective-permute-start(bf16[384,640]{1,0:T(8,128)(2,1)S(1)} %shard_map.41), channel_id=1, source_target_pairs={{0,1},{1,0},{2,3},{3,2},{4,5},{5,4},{6,7},{7,6},{8,9},{9,8},{10,11... | collective-permute-start | bytes 1474568 | tf_op jit(solution)/shard_map/ppermute | solution.py:260
  38.8 2.0 %shard_map.40 = f32[384,640]{1,0:T(8,128)S(1)} custom-call(s32[5]{0:T(128)S(1)} %stack.23.at_ref, bf16[8,96,640]{2,1,0:T(8,128)(2,1)S(1)} %shard_map.37.rows_ref, f32[5,8,96,128]{3,2,1,0:T(8,128)S(1)} %get-tuple-element.12.mixed_ref, f32[5,8,96,128]{3,2,1,0:T(8,128)S(1)} %get-tuple-element.13.sum_ref, f32[5,8,96,128]{3,2,1,0:T(8,128)S(1)} %get-tuple-element.14.top_ref, ...), custom_call_target="tpu_custom_call" | custom-call | flops 314572800 | tf_op jit(solution)/shard_map/pallas_call | solution.py:219
  41.0 3.0 %collective-permute-start.23 = (bf16[96,640]{1,0:T(8,128)(2,1)S(1)}, bf16[96,640]{1,0:T(8,128)(2,1)S(1)}, u32[]{:S(2)}, u32[]{:S(2)}) collective-permute-start(bf16[96,640]{1,0:T(8,128)(2,1)S(1)} %get-tuple-element.17), channel_id=1, source_target_pairs={{0,0},{1,4},{2,16},{3,20},{4,8},{5,12},{6,24},{7,28},{8,25},{9,29}... | collective-permute-start | bytes 368648 | tf_op jit(solution)/shard_map/ppermute | solution.py:271
  44.0 4.5 %collective-permute-start.22 = (bf16[96,640]{1,0:T(8,128)(2,1)S(1)}, bf16[96,640]{1,0:T(8,128)(2,1)S(1)}, u32[]{:S(2)}, u32[]{:S(2)}) collective-permute-start(bf16[96,640]{1,0:T(8,128)(2,1)S(1)} %get-tuple-element.18), channel_id=1, source_target_pairs={{0,16},{1,20},{2,0},{3,4},{4,24},{5,28},{6,8},{7,12},{8,9},{9,13},... | collective-permute-start | bytes 368648 | tf_op jit(solution)/shard_map/ppermute | solution.py:271
  48.5 3.4 %collective-permute-start.24 = (bf16[96,640]{1,0:T(8,128)(2,1)S(1)}, bf16[96,640]{1,0:T(8,128)(2,1)S(1)}, u32[]{:S(2)}, u32[]{:S(2)}) collective-permute-start(bf16[96,640]{1,0:T(8,128)(2,1)S(1)} %get-tuple-element.15), channel_id=1, source_target_pairs={{0,24},{1,28},{2,8},{3,12},{4,16},{5,20},{6,0},{7,4},{8,1},{9,5},{... | collective-permute-start | bytes 368648 | tf_op jit(solution)/shard_map/ppermute | solution.py:271
  52.7 6.5 %collective-permute-done.25 = bf16[96,640]{1,0:T(8,128)(2,1)S(1)} collective-permute-done((bf16[96,640]{1,0:T(8,128)(2,1)S(1)}, bf16[96,640]{1,0:T(8,128)(2,1)S(1)}, u32[]{:S(2)}, u32[]{:S(2)}) %collective-permute-start.25) | collective-permute-done | bytes 122912 | tf_op jit(solution)/shard_map/ppermute | solution.py:271
  (43 shorter events, 7.3 us)
Async XLA Ops:
  0.0 6.1 %collective-permute-start = (bf16[96,640]{1,0:T(8,128)(2,1)}, bf16[96,640]{1,0:T(8,128)(2,1)S(1)}, u32[]{:S(2)}, u32[]{:S(2)}) collective-permute-start(bf16[96,640]{1,0:T(8,128)(2,1)} %refs_0_.1), channel_id=1, source_target_pairs={{0,8},{8,16},{16,24},{24,28},{28,20},{20,12},{12,4},{4,0},{1,9},{9... | collective-permute-start | bytes 368648 | tf_op jit(solution)/shard_map/ppermute | solution.py:87
  3.1 4.6 %collective-permute-start.7 = (bf16[96,640]{1,0:T(8,128)(2,1)S(1)}, bf16[96,640]{1,0:T(8,128)(2,1)S(1)}, u32[]{:S(2)}, u32[]{:S(2)}) collective-permute-start(bf16[96,640]{1,0:T(8,128)(2,1)S(1)} %get-tuple-element.10.refs_0_), channel_id=1, source_target_pairs={{0,8},{8,16},{16,24},{24,28},{28,20},{20,12},{12,4},{4,0},{1,9},{9... | collective-permute-start | bytes 368648 | tf_op jit(solution)/shard_map/ppermute | solution.py:87
  4.6 4.5 %collective-permute-start.10 = (bf16[96,640]{1,0:T(8,128)(2,1)S(1)}, bf16[96,640]{1,0:T(8,128)(2,1)S(1)}, u32[]{:S(2)}, u32[]{:S(2)}) collective-permute-start(bf16[96,640]{1,0:T(8,128)(2,1)S(1)} %get-tuple-element.10.refs_0_), channel_id=1, source_target_pairs={{0,4},{8,0},{16,8},{24,16},{28,24},{20,28},{12,20},{4,12},{1,5},{9... | collective-permute-start | bytes 368648 | tf_op jit(solution)/shard_map/ppermute | solution.py:87
  4.6 5.8 %collective-permute-start.13 = (bf16[96,640]{1,0:T(8,128)(2,1)S(1)}, bf16[96,640]{1,0:T(8,128)(2,1)S(1)}, u32[]{:S(2)}, u32[]{:S(2)}) collective-permute-start(bf16[96,640]{1,0:T(8,128)(2,1)S(1)} %get-tuple-element.11.refs_7_), channel_id=1, source_target_pairs={{0,8},{8,16},{16,24},{24,28},{28,20},{20,12},{12,4},{4,0},{1,9},{9... | collective-permute-start | bytes 368648 | tf_op jit(solution)/shard_map/ppermute | solution.py:87
  6.1 5.4 %collective-permute-start.16 = (bf16[96,640]{1,0:T(8,128)(2,1)S(1)}, bf16[96,640]{1,0:T(8,128)(2,1)S(1)}, u32[]{:S(2)}, u32[]{:S(2)}) collective-permute-start(bf16[96,640]{1,0:T(8,128)(2,1)S(1)} %get-tuple-element.11.refs_7_), channel_id=1, source_target_pairs={{0,4},{8,0},{16,8},{24,16},{28,24},{20,28},{12,20},{4,12},{1,5},{9... | collective-permute-start | bytes 368648 | tf_op jit(solution)/shard_map/ppermute | solution.py:87
  6.5 6.4 %collective-permute-start.1 = (bf16[96,640]{1,0:T(8,128)(2,1)S(1)}, bf16[96,640]{1,0:T(8,128)(2,1)S(1)}, u32[]{:S(2)}, u32[]{:S(2)}) collective-permute-start(bf16[96,640]{1,0:T(8,128)(2,1)S(1)} %collective-permute-done.refs_1_), channel_id=1, source_target_pairs={{0,8},{8,16},{16,24},{24,28},{28,20},{20,12},{12,4},{4,0},{1,9},{9... | collective-permute-start | bytes 368648 | tf_op jit(solution)/shard_map/ppermute | solution.py:87
  7.7 6.5 %collective-permute-start.5 = (bf16[96,640]{1,0:T(8,128)(2,1)S(1)}, bf16[96,640]{1,0:T(8,128)(2,1)S(1)}, u32[]{:S(2)}, u32[]{:S(2)}) collective-permute-start(bf16[96,640]{1,0:T(8,128)(2,1)S(1)} %collective-permute-done.4.refs_7_), channel_id=1, source_target_pairs={{0,4},{8,0},{16,8},{24,16},{28,24},{20,28},{12,20},{4,12},{1,5},{9... | collective-permute-start | bytes 368648 | tf_op jit(solution)/shard_map/ppermute | solution.py:87
  9.1 6.3 %collective-permute-start.8 = (bf16[96,640]{1,0:T(8,128)(2,1)S(1)}, bf16[96,640]{1,0:T(8,128)(2,1)S(1)}, u32[]{:S(2)}, u32[]{:S(2)}) collective-permute-start(bf16[96,640]{1,0:T(8,128)(2,1)S(1)} %collective-permute-done.7.refs_1_), channel_id=1, source_target_pairs={{0,8},{8,16},{16,24},{24,28},{28,20},{20,12},{12,4},{4,0},{1,9},{9... | collective-permute-start | bytes 368648 | tf_op jit(solution)/shard_map/ppermute | solution.py:87
  10.4 6.4 %collective-permute-start.11 = (bf16[96,640]{1,0:T(8,128)(2,1)S(1)}, bf16[96,640]{1,0:T(8,128)(2,1)S(1)}, u32[]{:S(2)}, u32[]{:S(2)}) collective-permute-start(bf16[96,640]{1,0:T(8,128)(2,1)S(1)} %collective-permute-done.10.refs_6_), channel_id=1, source_target_pairs={{0,4},{8,0},{16,8},{24,16},{28,24},{20,28},{12,20},{4,12},{1,5},{9... | collective-permute-start | bytes 368648 | tf_op jit(solution)/shard_map/ppermute | solution.py:87
  11.5 6.6 %collective-permute-start.14 = (bf16[96,640]{1,0:T(8,128)(2,1)S(1)}, bf16[96,640]{1,0:T(8,128)(2,1)S(1)}, u32[]{:S(2)}, u32[]{:S(2)}) collective-permute-start(bf16[96,640]{1,0:T(8,128)(2,1)S(1)} %collective-permute-done.13.refs_8_), channel_id=1, source_target_pairs={{0,8},{8,16},{16,24},{24,28},{28,20},{20,12},{12,4},{4,0},{1,9},{9... | collective-permute-start | bytes 368648 | tf_op jit(solution)/shard_map/ppermute | solution.py:87
  12.9 7.5 %collective-permute-start.2 = (bf16[96,640]{1,0:T(8,128)(2,1)S(1)}, bf16[96,640]{1,0:T(8,128)(2,1)S(1)}, u32[]{:S(2)}, u32[]{:S(2)}) collective-permute-start(bf16[96,640]{1,0:T(8,128)(2,1)S(1)} %collective-permute-done.1.refs_2_), channel_id=1, source_target_pairs={{0,8},{8,16},{16,24},{24,28},{28,20},{20,12},{12,4},{4,0},{1,9},{9... | collective-permute-start | bytes 368648 | tf_op jit(solution)/shard_map/ppermute | solution.py:87
  14.2 7.9 %collective-permute-start.17 = (bf16[96,640]{1,0:T(8,128)(2,1)S(1)}, bf16[96,640]{1,0:T(8,128)(2,1)S(1)}, u32[]{:S(2)}, u32[]{:S(2)}) collective-permute-start(bf16[96,640]{1,0:T(8,128)(2,1)S(1)} %collective-permute-done.16.refs_13_), channel_id=1, source_target_pairs={{0,4},{8,0},{16,8},{24,16},{28,24},{20,28},{12,20},{4,12},{1,5},{9... | collective-permute-start | bytes 368648 | tf_op jit(solution)/shard_map/ppermute | solution.py:87
  15.4 8.0 %collective-permute-start.6 = (bf16[96,640]{1,0:T(8,128)(2,1)S(1)}, bf16[96,640]{1,0:T(8,128)(2,1)S(1)}, u32[]{:S(2)}, u32[]{:S(2)}) collective-permute-start(bf16[96,640]{1,0:T(8,128)(2,1)S(1)} %collective-permute-done.5.refs_6_), channel_id=1, source_target_pairs={{0,4},{8,0},{16,8},{24,16},{28,24},{20,28},{12,20},{4,12},{1,5},{9... | collective-permute-start | bytes 368648 | tf_op jit(solution)/shard_map/ppermute | solution.py:87
  16.8 6.9 %collective-permute-start.12 = (bf16[96,640]{1,0:T(8,128)(2,1)S(1)}, bf16[96,640]{1,0:T(8,128)(2,1)S(1)}, u32[]{:S(2)}, u32[]{:S(2)}) collective-permute-start(bf16[96,640]{1,0:T(8,128)(2,1)S(1)} %collective-permute-done.11.refs_5_), channel_id=1, source_target_pairs={{0,4},{8,0},{16,8},{24,16},{28,24},{20,28},{12,20},{4,12},{1,5},{9... | collective-permute-start | bytes 368648 | tf_op jit(solution)/shard_map/ppermute | solution.py:87
  18.1 5.6 %collective-permute-start.15 = (bf16[96,640]{1,0:T(8,128)(2,1)S(1)}, bf16[96,640]{1,0:T(8,128)(2,1)S(1)}, u32[]{:S(2)}, u32[]{:S(2)}) collective-permute-start(bf16[96,640]{1,0:T(8,128)(2,1)S(1)} %collective-permute-done.14.refs_9_), channel_id=1, source_target_pairs={{0,8},{8,16},{16,24},{24,28},{28,20},{20,12},{12,4},{4,0},{1,9},{9... | collective-permute-start | bytes 368648 | tf_op jit(solution)/shard_map/ppermute | solution.py:87
  20.4 4.7 %collective-permute-start.3 = (bf16[96,640]{1,0:T(8,128)(2,1)S(1)}, bf16[96,640]{1,0:T(8,128)(2,1)S(1)}, u32[]{:S(2)}, u32[]{:S(2)}) collective-permute-start(bf16[96,640]{1,0:T(8,128)(2,1)S(1)} %collective-permute-done.2.refs_3_), channel_id=1, source_target_pairs={{0,8},{8,16},{16,24},{24,28},{28,20},{20,12},{12,4},{4,0},{1,9},{9... | collective-permute-start | bytes 368648 | tf_op jit(solution)/shard_map/ppermute | solution.py:87
  22.1 5.1 %collective-permute-start.9 = (bf16[96,640]{1,0:T(8,128)(2,1)S(1)}, bf16[96,640]{1,0:T(8,128)(2,1)S(1)}, u32[]{:S(2)}, u32[]{:S(2)}) collective-permute-start(bf16[96,640]{1,0:T(8,128)(2,1)S(1)} %collective-permute-done.8.refs_2_), channel_id=1, source_target_pairs={{0,8},{8,16},{16,24},{24,28},{28,20},{20,12},{12,4},{4,0},{1,9},{9... | collective-permute-start | bytes 368648 | tf_op jit(solution)/shard_map/ppermute | solution.py:87
  23.6 8.7 %collective-permute-start.19 = (bf16[96,640]{1,0:T(8,128)(2,1)S(1)}, bf16[96,640]{1,0:T(8,128)(2,1)S(1)}, u32[]{:S(2)}, u32[]{:S(2)}) collective-permute-start(bf16[96,640]{1,0:T(8,128)(2,1)S(1)} %collective-permute-done.12.refs_4_), channel_id=1, source_target_pairs={{0,4},{8,0},{16,8},{24,16},{28,24},{20,28},{12,20},{4,12},{1,5},{9... | collective-permute-start | bytes 368648 | tf_op jit(solution)/shard_map/ppermute | solution.py:87
  23.7 8.7 %collective-permute-start.20 = (bf16[96,640]{1,0:T(8,128)(2,1)S(1)}, bf16[96,640]{1,0:T(8,128)(2,1)S(1)}, u32[]{:S(2)}, u32[]{:S(2)}) collective-permute-start(bf16[96,640]{1,0:T(8,128)(2,1)S(1)} %collective-permute-done.15.refs_10_), channel_id=1, source_target_pairs={{0,8},{8,16},{16,24},{24,28},{28,20},{20,12},{12,4},{4,0},{1,9},{9... | collective-permute-start | bytes 368648 | tf_op jit(solution)/shard_map/ppermute | solution.py:87
  34.4 6.5 %collective-permute-start.21 = (bf16[384,640]{1,0:T(8,128)(2,1)S(1)}, bf16[384,640]{1,0:T(8,128)(2,1)S(1)}, u32[]{:S(2)}, u32[]{:S(2)}) collective-permute-start(bf16[384,640]{1,0:T(8,128)(2,1)S(1)} %shard_map.41), channel_id=1, source_target_pairs={{0,1},{1,0},{2,3},{3,2},{4,5},{5,4},{6,7},{7,6},{8,9},{9,8},{10,11... | collective-permute-start | bytes 1474568 | tf_op jit(solution)/shard_map/ppermute | solution.py:260
  41.0 10.9 %collective-permute-start.23 = (bf16[96,640]{1,0:T(8,128)(2,1)S(1)}, bf16[96,640]{1,0:T(8,128)(2,1)S(1)}, u32[]{:S(2)}, u32[]{:S(2)}) collective-permute-start(bf16[96,640]{1,0:T(8,128)(2,1)S(1)} %get-tuple-element.17), channel_id=1, source_target_pairs={{0,0},{1,4},{2,16},{3,20},{4,8},{5,12},{6,24},{7,28},{8,25},{9,29}... | collective-permute-start | bytes 368648 | tf_op jit(solution)/shard_map/ppermute | solution.py:271
  44.0 8.7 %collective-permute-start.22 = (bf16[96,640]{1,0:T(8,128)(2,1)S(1)}, bf16[96,640]{1,0:T(8,128)(2,1)S(1)}, u32[]{:S(2)}, u32[]{:S(2)}) collective-permute-start(bf16[96,640]{1,0:T(8,128)(2,1)S(1)} %get-tuple-element.18), channel_id=1, source_target_pairs={{0,16},{1,20},{2,0},{3,4},{4,24},{5,28},{6,8},{7,12},{8,9},{9,13},... | collective-permute-start | bytes 368648 | tf_op jit(solution)/shard_map/ppermute | solution.py:271
  48.5 10.8 %collective-permute-start.25 = (bf16[96,640]{1,0:T(8,128)(2,1)S(1)}, bf16[96,640]{1,0:T(8,128)(2,1)S(1)}, u32[]{:S(2)}, u32[]{:S(2)}) collective-permute-start(bf16[96,640]{1,0:T(8,128)(2,1)S(1)} %get-tuple-element.16), channel_id=1, source_target_pairs={{0,8},{1,12},{2,24},{3,28},{4,0},{5,4},{6,16},{7,20},{8,17},{9,21}... | collective-permute-start | bytes 368648 | tf_op jit(solution)/shard_map/ppermute | solution.py:271
  48.5 10.8 %collective-permute-start.24 = (bf16[96,640]{1,0:T(8,128)(2,1)S(1)}, bf16[96,640]{1,0:T(8,128)(2,1)S(1)}, u32[]{:S(2)}, u32[]{:S(2)}) collective-permute-start(bf16[96,640]{1,0:T(8,128)(2,1)S(1)} %get-tuple-element.15), channel_id=1, source_target_pairs={{0,24},{1,28},{2,8},{3,12},{4,16},{5,20},{6,0},{7,4},{8,1},{9,5},{... | collective-permute-start | bytes 368648 | tf_op jit(solution)/shard_map/ppermute | solution.py:271
  (5 other events, 16.6 us)

commit v10 on v9

--- a/solution.py
+++ b/solution.py
@@ -84,7 +84,11 @@
 
 def hop(x, n, by):
     order = ring_order(n)
-    return lax.ppermute(x, "frames", [(order[i], order[(i + by) % n]) for i in range(n)])
+    pairs = []
+    for i in range(n):
+        for h in range(4):
+            pairs.append((4 * order[i] + h, 4 * order[(i + by * (1 - 2 * (h & 1))) % n] + h))
+    return lax.ppermute(x, ("frames", "heads"), pairs)
 
 
 def gather_ring(streams, n):
@@ -97,15 +101,18 @@
     return found
 
 
-def left_out(place, block, n):
-    return FR_DEV * ((place - ((place - block) & (n - 1) ^ 2)) & (n - 1))
-
-
-def frame_marks(place, blocks, n):
+def ring_distance(at_ref, owner, n):
+    place, core = at_ref[0], at_ref[4]
+    return (place - owner) * (1 - 2 * core) & (n - 1)
+
+
+def frame_marks(at_ref, blocks, n):
+    place, core = at_ref[0], at_ref[4]
     lane = lax.broadcasted_iota(jnp.int32, (TPF, HD), 1)
     marks = []
     for block in blocks:
-        frame = left_out(place, block, n)
+        owner = (place - block * (1 - 2 * core)) & (n - 1)
+        frame = FR_DEV * ring_distance(at_ref, owner ^ 2, n)
         for g in range(FR_DEV):
             marks.append((lane == frame + g) | (lane >= n * FR_DEV))
     return jnp.concatenate([jnp.where(mark, 1.0, 0.0) for mark in marks], axis=0).astype(jnp.bfloat16)
@@ -156,12 +163,12 @@
 
 
 def slot_blocks(at_ref, flip_core, n):
-    place, z, y, x, core = (at_ref[i] for i in range(5))
+    z, y, x, core = (at_ref[i] for i in range(1, 5))
     blocks = []
     for slot in range(n // 2):
         to = look_up(sum(PATTERNS, ()), 4 * (slot ^ (2 * y + x)) + z)
         owner = to + (core ^ flip_core) * (n - 1 - 2 * to)
-        blocks.append((place - owner) & (n - 1))
+        blocks.append(ring_distance(at_ref, owner, n))
     return blocks
 
 
@@ -178,7 +185,7 @@
 def near_kernel(heads, n, at_ref, rows_ref, *refs):
     near = [d for d in range(n) if d != n // 2]
     key_refs, value_refs, (mixed_ref, sum_ref, top_ref) = refs[: n - 1], refs[n - 1 : -3], refs[-3:]
-    marks = frame_marks(at_ref[0], range(n), n)
+    marks = frame_marks(at_ref, range(n), n)
     keys_marks = key_marks(near, ROWS, n)
     for head in range(heads):
         cols = slice(head * HD, (head + 1) * HD)
@@ -193,7 +200,7 @@
 
 def finish_kernel(heads, n, flip_core, at_ref, rows_ref, mixed_ref, sum_ref, top_ref, keys_ref, values_ref, w_ref, out_ref):
     blocks = slot_blocks(at_ref, flip_core, n)
-    marks = frame_marks(at_ref[0], blocks, n)
+    marks = frame_marks(at_ref, blocks, n)
     keys_marks = key_marks([n // 2], TPF, n)
     attended = []
 

time: 60.2 us -> 60.4 us (level)
  waiting for transfers between devices: 11.3 us -> 15 us
  starting transfers between devices: 36.8 us -> 33.3 us
    ppermute x21, waiting for transfers between devices: 4.01 us -> 7.34 us  [hop(): return lax.ppermute(x, ('frames', 'heads'), pairs)]
    ppermute x21, starting transfers between devices: 21.4 us -> 19.5 us  [hop(): return lax.ppermute(x, ('frames', 'heads'), pairs)]
    ppermute x4, starting transfers between devices: 10.9 us -> 9.9 us  [on_device_ring(): arrived.append(lax.ppermute(total, ('frames', 'heads'), pairs).astype(f32))]
  transfers between devices with their start and end apart: 26 -> 26, of which waited for: 8 -> 12; matrix products, arithmetic and copies ran while one was open for 0% -> 0% of each run, Pallas kernels for 12% -> 11%
where the time goes in v10:
time: 60.4 us; the launch traced here: 60.2 us
  starting transfers between devices  33.3 us (55%)
  waiting for transfers between devices  15 us (25%)
  Pallas kernels  8.97 us (15%)
  local copies, waits for them, and re-layouts  1.94 us (3%)
  other arithmetic  0.89 us (1%)
    ppermute x21, starting transfers between devices, hop(): return lax.ppermute(x, ('frames', 'heads'), pairs)  19.5 us
    ppermute x4, starting transfers between devices, on_device_ring(): arrived.append(lax.ppermute(total, ('frames', 'heads'), pairs).astype(f32))  9.9 us
    pallas_call x5, Pallas kernels, call(): pl.pallas_call(kernel, out_shape=[jax.ShapeDtypeStruct(shape, dtype) for...  8.97 us
    ppermute x4, waiting for transfers between devices, on_device_ring(): arrived.append(lax.ppermute(total, ('frames', 'heads'), pairs).astype(f32))  7.69 us
    ppermute x21, waiting for transfers between devices, hop(): return lax.ppermute(x, ('frames', 'heads'), pairs)  7.34 us
    ppermute x1, starting transfers between devices, on_device_ring(): lax.ppermute(finish(1, bf16), 'heads', [(h, h ^ 1) for h in range(4)])  3.9 us
    unnamed x6, local copies, waits for them, and re-layouts  1.85 us
  transfers between devices with their start and end apart: 26, of which 12 were waited for; matrix products, arithmetic and copies ran while one was open for 0% of the time, Pallas kernels for 11%

profile of v10, /device:TPU:1, one launch (start us, length us, event | category | flops | bytes accessed | tf_op | source)
XLA Modules:
  0.0 60.2 jit_solution(1385369855225666073)
XLA Ops:
  0.0 2.1 %collective-permute-start = (bf16[96,640]{1,0:T(8,128)(2,1)}, bf16[96,640]{1,0:T(8,128)(2,1)S(1)}, u32[]{:S(2)}, u32[]{:S(2)}) collective-permute-start(bf16[96,640]{1,0:T(8,128)(2,1)} %refs_0_.1), channel_id=1, source_target_pairs={{0,8},{1,5},{2,10},{3,7},{8,16},{9,1},{10,18},{11,3},{16,24},{17,9... | collective-permute-start | bytes 368648 | tf_op jit(solution)/shard_map/ppermute | solution.py:91
  2.1 0.9 %copy-done.1 = bf16[2,96,640]{2,1,0:T(8,128)(2,1)S(1)} copy-done((bf16[2,96,640]{2,1,0:T(8,128)(2,1)S(1)}, bf16[2,96,640]{2,1,0:T(8,128)(2,1)}, u32[]{:S(2)}) %copy-start.1) | copy-done | bytes 245784
  3.1 1.5 %collective-permute-start.7 = (bf16[96,640]{1,0:T(8,128)(2,1)S(1)}, bf16[96,640]{1,0:T(8,128)(2,1)S(1)}, u32[]{:S(2)}, u32[]{:S(2)}) collective-permute-start(bf16[96,640]{1,0:T(8,128)(2,1)S(1)} %get-tuple-element.10.refs_0_), channel_id=1, source_target_pairs={{0,8},{1,5},{2,10},{3,7},{8,16},{9,1},{10,18},{11,3},{16,24},{17,9... | collective-permute-start | bytes 368648 | tf_op jit(solution)/shard_map/ppermute | solution.py:91
  4.7 1.3 %collective-permute-start.13 = (bf16[96,640]{1,0:T(8,128)(2,1)S(1)}, bf16[96,640]{1,0:T(8,128)(2,1)S(1)}, u32[]{:S(2)}, u32[]{:S(2)}) collective-permute-start(bf16[96,640]{1,0:T(8,128)(2,1)S(1)} %get-tuple-element.11.refs_7_), channel_id=1, source_target_pairs={{0,8},{1,5},{2,10},{3,7},{8,16},{9,1},{10,18},{11,3},{16,24},{17,9... | collective-permute-start | bytes 368648 | tf_op jit(solution)/shard_map/ppermute | solution.py:91
  7.0 1.6 %collective-permute-start.1 = (bf16[96,640]{1,0:T(8,128)(2,1)S(1)}, bf16[96,640]{1,0:T(8,128)(2,1)S(1)}, u32[]{:S(2)}, u32[]{:S(2)}) collective-permute-start(bf16[96,640]{1,0:T(8,128)(2,1)S(1)} %collective-permute-done.refs_1_), channel_id=1, source_target_pairs={{0,8},{1,5},{2,10},{3,7},{8,16},{9,1},{10,18},{11,3},{16,24},{17,9... | collective-permute-start | bytes 368648 | tf_op jit(solution)/shard_map/ppermute | solution.py:91
  8.6 1.0 %collective-permute-start.5 = (bf16[96,640]{1,0:T(8,128)(2,1)S(1)}, bf16[96,640]{1,0:T(8,128)(2,1)S(1)}, u32[]{:S(2)}, u32[]{:S(2)}) collective-permute-start(bf16[96,640]{1,0:T(8,128)(2,1)S(1)} %collective-permute-done.4.refs_7_), channel_id=1, source_target_pairs={{0,4},{1,9},{2,6},{3,11},{8,0},{9,17},{10,2},{11,19},{16,8},{17,25... | collective-permute-start | bytes 368648 | tf_op jit(solution)/shard_map/ppermute | solution.py:91
  9.9 1.2 %collective-permute-start.8 = (bf16[96,640]{1,0:T(8,128)(2,1)S(1)}, bf16[96,640]{1,0:T(8,128)(2,1)S(1)}, u32[]{:S(2)}, u32[]{:S(2)}) collective-permute-start(bf16[96,640]{1,0:T(8,128)(2,1)S(1)} %collective-permute-done.7.refs_1_), channel_id=1, source_target_pairs={{0,8},{1,5},{2,10},{3,7},{8,16},{9,1},{10,18},{11,3},{16,24},{17,9... | collective-permute-start | bytes 368648 | tf_op jit(solution)/shard_map/ppermute | solution.py:91
  12.5 1.2 %collective-permute-start.14 = (bf16[96,640]{1,0:T(8,128)(2,1)S(1)}, bf16[96,640]{1,0:T(8,128)(2,1)S(1)}, u32[]{:S(2)}, u32[]{:S(2)}) collective-permute-start(bf16[96,640]{1,0:T(8,128)(2,1)S(1)} %collective-permute-done.13.refs_8_), channel_id=1, source_target_pairs={{0,8},{1,5},{2,10},{3,7},{8,16},{9,1},{10,18},{11,3},{16,24},{17,9... | collective-permute-start | bytes 368648 | tf_op jit(solution)/shard_map/ppermute | solution.py:91
  13.8 1.3 %collective-permute-start.2 = (bf16[96,640]{1,0:T(8,128)(2,1)S(1)}, bf16[96,640]{1,0:T(8,128)(2,1)S(1)}, u32[]{:S(2)}, u32[]{:S(2)}) collective-permute-start(bf16[96,640]{1,0:T(8,128)(2,1)S(1)} %collective-permute-done.1.refs_2_), channel_id=1, source_target_pairs={{0,8},{1,5},{2,10},{3,7},{8,16},{9,1},{10,18},{11,3},{16,24},{17,9... | collective-permute-start | bytes 368648 | tf_op jit(solution)/shard_map/ppermute | solution.py:91
  15.5 1.6 %collective-permute-start.6 = (bf16[96,640]{1,0:T(8,128)(2,1)S(1)}, bf16[96,640]{1,0:T(8,128)(2,1)S(1)}, u32[]{:S(2)}, u32[]{:S(2)}) collective-permute-start(bf16[96,640]{1,0:T(8,128)(2,1)S(1)} %collective-permute-done.5.refs_6_), channel_id=1, source_target_pairs={{0,4},{1,9},{2,6},{3,11},{8,0},{9,17},{10,2},{11,19},{16,8},{17,25... | collective-permute-start | bytes 368648 | tf_op jit(solution)/shard_map/ppermute | solution.py:91
  17.3 1.1 %collective-permute-start.12 = (bf16[96,640]{1,0:T(8,128)(2,1)S(1)}, bf16[96,640]{1,0:T(8,128)(2,1)S(1)}, u32[]{:S(2)}, u32[]{:S(2)}) collective-permute-start(bf16[96,640]{1,0:T(8,128)(2,1)S(1)} %collective-permute-done.11.refs_5_), channel_id=1, source_target_pairs={{0,4},{1,9},{2,6},{3,11},{8,0},{9,17},{10,2},{11,19},{16,8},{17,25... | collective-permute-start | bytes 368648 | tf_op jit(solution)/shard_map/ppermute | solution.py:91
  19.0 1.3 %collective-permute-done.2.refs_3_ = bf16[96,640]{1,0:T(8,128)(2,1)S(1)} collective-permute-done((bf16[96,640]{1,0:T(8,128)(2,1)S(1)}, bf16[96,640]{1,0:T(8,128)(2,1)S(1)}, u32[]{:S(2)}, u32[]{:S(2)}) %collective-permute-start.2) | collective-permute-done | bytes 122912 | tf_op jit(solution)/shard_map/ppermute | solution.py:91
  20.8 1.6 %collective-permute-start.9 = (bf16[96,640]{1,0:T(8,128)(2,1)S(1)}, bf16[96,640]{1,0:T(8,128)(2,1)S(1)}, u32[]{:S(2)}, u32[]{:S(2)}) collective-permute-start(bf16[96,640]{1,0:T(8,128)(2,1)S(1)} %collective-permute-done.8.refs_2_), channel_id=1, source_target_pairs={{0,8},{1,5},{2,10},{3,7},{8,16},{9,1},{10,18},{11,3},{16,24},{17,9... | collective-permute-start | bytes 368648 | tf_op jit(solution)/shard_map/ppermute | solution.py:91
  22.8 1.5 %collective-permute-done.12.refs_4_ = bf16[96,640]{1,0:T(8,128)(2,1)S(1)} collective-permute-done((bf16[96,640]{1,0:T(8,128)(2,1)S(1)}, bf16[96,640]{1,0:T(8,128)(2,1)S(1)}, u32[]{:S(2)}, u32[]{:S(2)}) %collective-permute-start.12) | collective-permute-done | bytes 122912 | tf_op jit(solution)/shard_map/ppermute | solution.py:91
  24.8 1.0 %collective-permute-start.20 = (bf16[96,640]{1,0:T(8,128)(2,1)S(1)}, bf16[96,640]{1,0:T(8,128)(2,1)S(1)}, u32[]{:S(2)}, u32[]{:S(2)}) collective-permute-start(bf16[96,640]{1,0:T(8,128)(2,1)S(1)} %collective-permute-done.15.refs_10_), channel_id=1, source_target_pairs={{0,8},{1,5},{2,10},{3,7},{8,16},{9,1},{10,18},{11,3},{16,24},{17,9... | collective-permute-start | bytes 368648 | tf_op jit(solution)/shard_map/ppermute | solution.py:91
  27.2 1.6 %collective-permute-done.9.refs_3_ = bf16[96,640]{1,0:T(8,128)(2,1)S(1)} collective-permute-done((bf16[96,640]{1,0:T(8,128)(2,1)S(1)}, bf16[96,640]{1,0:T(8,128)(2,1)S(1)}, u32[]{:S(2)}, u32[]{:S(2)}) %collective-permute-start.9) | collective-permute-done | bytes 122912 | tf_op jit(solution)/shard_map/ppermute | solution.py:91
  28.9 4.8 %shard_map.39 = (f32[5,8,96,128]{3,2,1,0:T(8,128)S(1)}, f32[5,8,96,128]{3,2,1,0:T(8,128)S(1)}, f32[5,8,96,128]{3,2,1,0:T(8,128)S(1)}) custom-call(s32[5]{0:T(128)S(1)} %stack.23.at_ref, bf16[8,96,640]{2,1,0:T(8,128)(2,1)S(1)} %shard_map.37.rows_ref, bf16[96,640]{1,0:T(8,128)(2,1)S(1)} %get-tuple-element.10.refs_0_, ...), custom_call_target="tpu_custom_call" | custom-call | flops 1321205760 | tf_op jit(solution)/shard_map/pallas_call | solution.py:226
  33.7 2.1 %shard_map.41 = bf16[384,640]{1,0:T(8,128)(2,1)S(1)} custom-call(s32[5]{0:T(128)S(1)} %stack.23.at_ref, bf16[8,96,640]{2,1,0:T(8,128)(2,1)S(1)} %shard_map.37.rows_ref, f32[5,8,96,128]{3,2,1,0:T(8,128)S(1)} %get-tuple-element.12.mixed_ref, f32[5,8,96,128]{3,2,1,0:T(8,128)S(1)} %get-tuple-element.13.sum_ref, f32[5,8,96,128]{3,2,1,0:T(8,128)S(1)} %get-tuple-element.14.top_ref, ...), custom_call_target="tpu_custom_call" | custom-call | flops 314572800 | tf_op jit(solution)/shard_map/pallas_call | solution.py:226
  35.7 3.9 %collective-permute-start.21 = (bf16[384,640]{1,0:T(8,128)(2,1)S(1)}, bf16[384,640]{1,0:T(8,128)(2,1)S(1)}, u32[]{:S(2)}, u32[]{:S(2)}) collective-permute-start(bf16[384,640]{1,0:T(8,128)(2,1)S(1)} %shard_map.41), channel_id=1, source_target_pairs={{0,1},{1,0},{2,3},{3,2},{4,5},{5,4},{6,7},{7,6},{8,9},{9,8},{10,11... | collective-permute-start | bytes 1474568 | tf_op jit(solution)/shard_map/ppermute | solution.py:267
  39.6 2.0 %shard_map.40 = f32[384,640]{1,0:T(8,128)S(1)} custom-call(s32[5]{0:T(128)S(1)} %stack.23.at_ref, bf16[8,96,640]{2,1,0:T(8,128)(2,1)S(1)} %shard_map.37.rows_ref, f32[5,8,96,128]{3,2,1,0:T(8,128)S(1)} %get-tuple-element.12.mixed_ref, f32[5,8,96,128]{3,2,1,0:T(8,128)S(1)} %get-tuple-element.13.sum_ref, f32[5,8,96,128]{3,2,1,0:T(8,128)S(1)} %get-tuple-element.14.top_ref, ...), custom_call_target="tpu_custom_call" | custom-call | flops 314572800 | tf_op jit(solution)/shard_map/pallas_call | solution.py:226
  41.8 2.4 %collective-permute-start.23 = (bf16[96,640]{1,0:T(8,128)(2,1)S(1)}, bf16[96,640]{1,0:T(8,128)(2,1)S(1)}, u32[]{:S(2)}, u32[]{:S(2)}) collective-permute-start(bf16[96,640]{1,0:T(8,128)(2,1)S(1)} %get-tuple-element.17), channel_id=1, source_target_pairs={{0,0},{1,4},{2,16},{3,20},{4,8},{5,12},{6,24},{7,28},{8,25},{9,29}... | collective-permute-start | bytes 368648 | tf_op jit(solution)/shard_map/ppermute | solution.py:278
  44.2 4.2 %collective-permute-start.22 = (bf16[96,640]{1,0:T(8,128)(2,1)S(1)}, bf16[96,640]{1,0:T(8,128)(2,1)S(1)}, u32[]{:S(2)}, u32[]{:S(2)}) collective-permute-start(bf16[96,640]{1,0:T(8,128)(2,1)S(1)} %get-tuple-element.18), channel_id=1, source_target_pairs={{0,16},{1,20},{2,0},{3,4},{4,24},{5,28},{6,8},{7,12},{8,9},{9,13},... | collective-permute-start | bytes 368648 | tf_op jit(solution)/shard_map/ppermute | solution.py:278
  48.4 3.3 %collective-permute-start.24 = (bf16[96,640]{1,0:T(8,128)(2,1)S(1)}, bf16[96,640]{1,0:T(8,128)(2,1)S(1)}, u32[]{:S(2)}, u32[]{:S(2)}) collective-permute-start(bf16[96,640]{1,0:T(8,128)(2,1)S(1)} %get-tuple-element.15), channel_id=1, source_target_pairs={{0,24},{1,28},{2,8},{3,12},{4,16},{5,20},{6,0},{7,4},{8,1},{9,5},{... | collective-permute-start | bytes 368648 | tf_op jit(solution)/shard_map/ppermute | solution.py:278
  52.3 7.2 %collective-permute-done.25 = bf16[96,640]{1,0:T(8,128)(2,1)S(1)} collective-permute-done((bf16[96,640]{1,0:T(8,128)(2,1)S(1)}, bf16[96,640]{1,0:T(8,128)(2,1)S(1)}, u32[]{:S(2)}, u32[]{:S(2)}) %collective-permute-start.25) | collective-permute-done | bytes 122912 | tf_op jit(solution)/shard_map/ppermute | solution.py:278
  (43 shorter events, 8.3 us)
Async XLA Ops:
  0.0 6.0 %collective-permute-start = (bf16[96,640]{1,0:T(8,128)(2,1)}, bf16[96,640]{1,0:T(8,128)(2,1)S(1)}, u32[]{:S(2)}, u32[]{:S(2)}) collective-permute-start(bf16[96,640]{1,0:T(8,128)(2,1)} %refs_0_.1), channel_id=1, source_target_pairs={{0,8},{1,5},{2,10},{3,7},{8,16},{9,1},{10,18},{11,3},{16,24},{17,9... | collective-permute-start | bytes 368648 | tf_op jit(solution)/shard_map/ppermute | solution.py:91
  3.1 5.5 %collective-permute-start.7 = (bf16[96,640]{1,0:T(8,128)(2,1)S(1)}, bf16[96,640]{1,0:T(8,128)(2,1)S(1)}, u32[]{:S(2)}, u32[]{:S(2)}) collective-permute-start(bf16[96,640]{1,0:T(8,128)(2,1)S(1)} %get-tuple-element.10.refs_0_), channel_id=1, source_target_pairs={{0,8},{1,5},{2,10},{3,7},{8,16},{9,1},{10,18},{11,3},{16,24},{17,9... | collective-permute-start | bytes 368648 | tf_op jit(solution)/shard_map/ppermute | solution.py:91
  4.7 6.4 %collective-permute-start.13 = (bf16[96,640]{1,0:T(8,128)(2,1)S(1)}, bf16[96,640]{1,0:T(8,128)(2,1)S(1)}, u32[]{:S(2)}, u32[]{:S(2)}) collective-permute-start(bf16[96,640]{1,0:T(8,128)(2,1)S(1)} %get-tuple-element.11.refs_7_), channel_id=1, source_target_pairs={{0,8},{1,5},{2,10},{3,7},{8,16},{9,1},{10,18},{11,3},{16,24},{17,9... | collective-permute-start | bytes 368648 | tf_op jit(solution)/shard_map/ppermute | solution.py:91
  6.0 6.5 %collective-permute-start.16 = (bf16[96,640]{1,0:T(8,128)(2,1)S(1)}, bf16[96,640]{1,0:T(8,128)(2,1)S(1)}, u32[]{:S(2)}, u32[]{:S(2)}) collective-permute-start(bf16[96,640]{1,0:T(8,128)(2,1)S(1)} %get-tuple-element.11.refs_7_), channel_id=1, source_target_pairs={{0,4},{1,9},{2,6},{3,11},{8,0},{9,17},{10,2},{11,19},{16,8},{17,25... | collective-permute-start | bytes 368648 | tf_op jit(solution)/shard_map/ppermute | solution.py:91
  7.0 6.7 %collective-permute-start.1 = (bf16[96,640]{1,0:T(8,128)(2,1)S(1)}, bf16[96,640]{1,0:T(8,128)(2,1)S(1)}, u32[]{:S(2)}, u32[]{:S(2)}) collective-permute-start(bf16[96,640]{1,0:T(8,128)(2,1)S(1)} %collective-permute-done.refs_1_), channel_id=1, source_target_pairs={{0,8},{1,5},{2,10},{3,7},{8,16},{9,1},{10,18},{11,3},{16,24},{17,9... | collective-permute-start | bytes 368648 | tf_op jit(solution)/shard_map/ppermute | solution.py:91
  8.6 6.5 %collective-permute-start.5 = (bf16[96,640]{1,0:T(8,128)(2,1)S(1)}, bf16[96,640]{1,0:T(8,128)(2,1)S(1)}, u32[]{:S(2)}, u32[]{:S(2)}) collective-permute-start(bf16[96,640]{1,0:T(8,128)(2,1)S(1)} %collective-permute-done.4.refs_7_), channel_id=1, source_target_pairs={{0,4},{1,9},{2,6},{3,11},{8,0},{9,17},{10,2},{11,19},{16,8},{17,25... | collective-permute-start | bytes 368648 | tf_op jit(solution)/shard_map/ppermute | solution.py:91
  9.9 5.6 %collective-permute-start.8 = (bf16[96,640]{1,0:T(8,128)(2,1)S(1)}, bf16[96,640]{1,0:T(8,128)(2,1)S(1)}, u32[]{:S(2)}, u32[]{:S(2)}) collective-permute-start(bf16[96,640]{1,0:T(8,128)(2,1)S(1)} %collective-permute-done.7.refs_1_), channel_id=1, source_target_pairs={{0,8},{1,5},{2,10},{3,7},{8,16},{9,1},{10,18},{11,3},{16,24},{17,9... | collective-permute-start | bytes 368648 | tf_op jit(solution)/shard_map/ppermute | solution.py:91
  11.1 6.2 %collective-permute-start.11 = (bf16[96,640]{1,0:T(8,128)(2,1)S(1)}, bf16[96,640]{1,0:T(8,128)(2,1)S(1)}, u32[]{:S(2)}, u32[]{:S(2)}) collective-permute-start(bf16[96,640]{1,0:T(8,128)(2,1)S(1)} %collective-permute-done.10.refs_6_), channel_id=1, source_target_pairs={{0,4},{1,9},{2,6},{3,11},{8,0},{9,17},{10,2},{11,19},{16,8},{17,25... | collective-permute-start | bytes 368648 | tf_op jit(solution)/shard_map/ppermute | solution.py:91
  12.5 5.9 %collective-permute-start.14 = (bf16[96,640]{1,0:T(8,128)(2,1)S(1)}, bf16[96,640]{1,0:T(8,128)(2,1)S(1)}, u32[]{:S(2)}, u32[]{:S(2)}) collective-permute-start(bf16[96,640]{1,0:T(8,128)(2,1)S(1)} %collective-permute-done.13.refs_8_), channel_id=1, source_target_pairs={{0,8},{1,5},{2,10},{3,7},{8,16},{9,1},{10,18},{11,3},{16,24},{17,9... | collective-permute-start | bytes 368648 | tf_op jit(solution)/shard_map/ppermute | solution.py:91
  13.8 6.6 %collective-permute-start.2 = (bf16[96,640]{1,0:T(8,128)(2,1)S(1)}, bf16[96,640]{1,0:T(8,128)(2,1)S(1)}, u32[]{:S(2)}, u32[]{:S(2)}) collective-permute-start(bf16[96,640]{1,0:T(8,128)(2,1)S(1)} %collective-permute-done.1.refs_2_), channel_id=1, source_target_pairs={{0,8},{1,5},{2,10},{3,7},{8,16},{9,1},{10,18},{11,3},{16,24},{17,9... | collective-permute-start | bytes 368648 | tf_op jit(solution)/shard_map/ppermute | solution.py:91
  15.1 5.7 %collective-permute-start.17 = (bf16[96,640]{1,0:T(8,128)(2,1)S(1)}, bf16[96,640]{1,0:T(8,128)(2,1)S(1)}, u32[]{:S(2)}, u32[]{:S(2)}) collective-permute-start(bf16[96,640]{1,0:T(8,128)(2,1)S(1)} %collective-permute-done.16.refs_13_), channel_id=1, source_target_pairs={{0,4},{1,9},{2,6},{3,11},{8,0},{9,17},{10,2},{11,19},{16,8},{17,25... | collective-permute-start | bytes 368648 | tf_op jit(solution)/shard_map/ppermute | solution.py:91
  15.5 7.2 %collective-permute-start.6 = (bf16[96,640]{1,0:T(8,128)(2,1)S(1)}, bf16[96,640]{1,0:T(8,128)(2,1)S(1)}, u32[]{:S(2)}, u32[]{:S(2)}) collective-permute-start(bf16[96,640]{1,0:T(8,128)(2,1)S(1)} %collective-permute-done.5.refs_6_), channel_id=1, source_target_pairs={{0,4},{1,9},{2,6},{3,11},{8,0},{9,17},{10,2},{11,19},{16,8},{17,25... | collective-permute-start | bytes 368648 | tf_op jit(solution)/shard_map/ppermute | solution.py:91
  17.3 7.0 %collective-permute-start.12 = (bf16[96,640]{1,0:T(8,128)(2,1)S(1)}, bf16[96,640]{1,0:T(8,128)(2,1)S(1)}, u32[]{:S(2)}, u32[]{:S(2)}) collective-permute-start(bf16[96,640]{1,0:T(8,128)(2,1)S(1)} %collective-permute-done.11.refs_5_), channel_id=1, source_target_pairs={{0,4},{1,9},{2,6},{3,11},{8,0},{9,17},{10,2},{11,19},{16,8},{17,25... | collective-permute-start | bytes 368648 | tf_op jit(solution)/shard_map/ppermute | solution.py:91
  18.5 6.4 %collective-permute-start.15 = (bf16[96,640]{1,0:T(8,128)(2,1)S(1)}, bf16[96,640]{1,0:T(8,128)(2,1)S(1)}, u32[]{:S(2)}, u32[]{:S(2)}) collective-permute-start(bf16[96,640]{1,0:T(8,128)(2,1)S(1)} %collective-permute-done.14.refs_9_), channel_id=1, source_target_pairs={{0,8},{1,5},{2,10},{3,7},{8,16},{9,1},{10,18},{11,3},{16,24},{17,9... | collective-permute-start | bytes 368648 | tf_op jit(solution)/shard_map/ppermute | solution.py:91
  20.3 5.9 %collective-permute-start.3 = (bf16[96,640]{1,0:T(8,128)(2,1)S(1)}, bf16[96,640]{1,0:T(8,128)(2,1)S(1)}, u32[]{:S(2)}, u32[]{:S(2)}) collective-permute-start(bf16[96,640]{1,0:T(8,128)(2,1)S(1)} %collective-permute-done.2.refs_3_), channel_id=1, source_target_pairs={{0,8},{1,5},{2,10},{3,7},{8,16},{9,1},{10,18},{11,3},{16,24},{17,9... | collective-permute-start | bytes 368648 | tf_op jit(solution)/shard_map/ppermute | solution.py:91
  20.8 8.1 %collective-permute-start.9 = (bf16[96,640]{1,0:T(8,128)(2,1)S(1)}, bf16[96,640]{1,0:T(8,128)(2,1)S(1)}, u32[]{:S(2)}, u32[]{:S(2)}) collective-permute-start(bf16[96,640]{1,0:T(8,128)(2,1)S(1)} %collective-permute-done.8.refs_2_), channel_id=1, source_target_pairs={{0,8},{1,5},{2,10},{3,7},{8,16},{9,1},{10,18},{11,3},{16,24},{17,9... | collective-permute-start | bytes 368648 | tf_op jit(solution)/shard_map/ppermute | solution.py:91
  22.8 6.1 %collective-permute-start.18 = (bf16[96,640]{1,0:T(8,128)(2,1)S(1)}, bf16[96,640]{1,0:T(8,128)(2,1)S(1)}, u32[]{:S(2)}, u32[]{:S(2)}) collective-permute-start(bf16[96,640]{1,0:T(8,128)(2,1)S(1)} %collective-permute-done.17.refs_12_), channel_id=1, source_target_pairs={{0,4},{1,9},{2,6},{3,11},{8,0},{9,17},{10,2},{11,19},{16,8},{17,25... | collective-permute-start | bytes 368648 | tf_op jit(solution)/shard_map/ppermute | solution.py:91
  24.4 9.3 %collective-permute-start.19 = (bf16[96,640]{1,0:T(8,128)(2,1)S(1)}, bf16[96,640]{1,0:T(8,128)(2,1)S(1)}, u32[]{:S(2)}, u32[]{:S(2)}) collective-permute-start(bf16[96,640]{1,0:T(8,128)(2,1)S(1)} %collective-permute-done.12.refs_4_), channel_id=1, source_target_pairs={{0,4},{1,9},{2,6},{3,11},{8,0},{9,17},{10,2},{11,19},{16,8},{17,25... | collective-permute-start | bytes 368648 | tf_op jit(solution)/shard_map/ppermute | solution.py:91
  24.8 8.8 %collective-permute-start.20 = (bf16[96,640]{1,0:T(8,128)(2,1)S(1)}, bf16[96,640]{1,0:T(8,128)(2,1)S(1)}, u32[]{:S(2)}, u32[]{:S(2)}) collective-permute-start(bf16[96,640]{1,0:T(8,128)(2,1)S(1)} %collective-permute-done.15.refs_10_), channel_id=1, source_target_pairs={{0,8},{1,5},{2,10},{3,7},{8,16},{9,1},{10,18},{11,3},{16,24},{17,9... | collective-permute-start | bytes 368648 | tf_op jit(solution)/shard_map/ppermute | solution.py:91
  35.7 6.0 %collective-permute-start.21 = (bf16[384,640]{1,0:T(8,128)(2,1)S(1)}, bf16[384,640]{1,0:T(8,128)(2,1)S(1)}, u32[]{:S(2)}, u32[]{:S(2)}) collective-permute-start(bf16[384,640]{1,0:T(8,128)(2,1)S(1)} %shard_map.41), channel_id=1, source_target_pairs={{0,1},{1,0},{2,3},{3,2},{4,5},{5,4},{6,7},{7,6},{8,9},{9,8},{10,11... | collective-permute-start | bytes 1474568 | tf_op jit(solution)/shard_map/ppermute | solution.py:267
  41.8 9.9 %collective-permute-start.23 = (bf16[96,640]{1,0:T(8,128)(2,1)S(1)}, bf16[96,640]{1,0:T(8,128)(2,1)S(1)}, u32[]{:S(2)}, u32[]{:S(2)}) collective-permute-start(bf16[96,640]{1,0:T(8,128)(2,1)S(1)} %get-tuple-element.17), channel_id=1, source_target_pairs={{0,0},{1,4},{2,16},{3,20},{4,8},{5,12},{6,24},{7,28},{8,25},{9,29}... | collective-permute-start | bytes 368648 | tf_op jit(solution)/shard_map/ppermute | solution.py:278
  44.2 8.1 %collective-permute-start.22 = (bf16[96,640]{1,0:T(8,128)(2,1)S(1)}, bf16[96,640]{1,0:T(8,128)(2,1)S(1)}, u32[]{:S(2)}, u32[]{:S(2)}) collective-permute-start(bf16[96,640]{1,0:T(8,128)(2,1)S(1)} %get-tuple-element.18), channel_id=1, source_target_pairs={{0,16},{1,20},{2,0},{3,4},{4,24},{5,28},{6,8},{7,12},{8,9},{9,13},... | collective-permute-start | bytes 368648 | tf_op jit(solution)/shard_map/ppermute | solution.py:278
  48.4 11.0 %collective-permute-start.25 = (bf16[96,640]{1,0:T(8,128)(2,1)S(1)}, bf16[96,640]{1,0:T(8,128)(2,1)S(1)}, u32[]{:S(2)}, u32[]{:S(2)}) collective-permute-start(bf16[96,640]{1,0:T(8,128)(2,1)S(1)} %get-tuple-element.16), channel_id=1, source_target_pairs={{0,8},{1,12},{2,24},{3,28},{4,0},{5,4},{6,16},{7,20},{8,17},{9,21}... | collective-permute-start | bytes 368648 | tf_op jit(solution)/shard_map/ppermute | solution.py:278
  48.4 11.0 %collective-permute-start.24 = (bf16[96,640]{1,0:T(8,128)(2,1)S(1)}, bf16[96,640]{1,0:T(8,128)(2,1)S(1)}, u32[]{:S(2)}, u32[]{:S(2)}) collective-permute-start(bf16[96,640]{1,0:T(8,128)(2,1)S(1)} %get-tuple-element.15), channel_id=1, source_target_pairs={{0,24},{1,28},{2,8},{3,12},{4,16},{5,20},{6,0},{7,4},{8,1},{9,5},{... | collective-permute-start | bytes 368648 | tf_op jit(solution)/shard_map/ppermute | solution.py:278
  (5 other events, 18.6 us)

commit v11 on v10

--- a/solution.py
+++ b/solution.py
@@ -162,11 +162,11 @@
     return (jnp.int32(code - (code >> 31 << 32)) >> (2 * index)) & 3
 
 
-def slot_blocks(at_ref, flip_core, n):
+def slot_blocks(at_ref, flip_x, flip_core, n):
     z, y, x, core = (at_ref[i] for i in range(1, 5))
     blocks = []
-    for slot in range(n // 2):
-        to = look_up(sum(PATTERNS, ()), 4 * (slot ^ (2 * y + x)) + z)
+    for slot in range(2):
+        to = look_up(sum(PATTERNS, ()), 4 * ((slot ^ y) + 2 * (x ^ flip_x)) + z)
         owner = to + (core ^ flip_core) * (n - 1 - 2 * to)
         blocks.append(ring_distance(at_ref, owner, n))
     return blocks
@@ -198,8 +198,8 @@
             mixed_ref[head, d], sum_ref[head, d], top_ref[head, d] = mixed[rows], total[rows], top[rows]
 
 
-def finish_kernel(heads, n, flip_core, at_ref, rows_ref, mixed_ref, sum_ref, top_ref, keys_ref, values_ref, w_ref, out_ref):
-    blocks = slot_blocks(at_ref, flip_core, n)
+def finish_kernel(heads, n, flips, at_ref, rows_ref, mixed_ref, sum_ref, top_ref, keys_ref, values_ref, w_ref, *refs):
+    blocks = [block for flip in flips for block in slot_blocks(at_ref, *flip, n)]
     marks = frame_marks(at_ref, blocks, n)
     keys_marks = key_marks([n // 2], TPF, n)
     attended = []
@@ -218,19 +218,21 @@
         mixed, total = mixed + of(mixed_ref, head) * kept, total + of(sum_ref, head) * kept
         attended.append((mixed / total).astype(jnp.bfloat16))
     rows = jnp.concatenate(attended, axis=1)
-    out_ref[...] = jnp.dot(rows, w_ref[...], preferred_element_type=jnp.float32).astype(out_ref.dtype)
-
-
-def call(kernel, scalars, operands, outs, flops):
+    refs[-1][...] = jnp.dot(rows, w_ref[...], preferred_element_type=jnp.float32).astype(refs[-1].dtype)
+
+
+def call(kernel, scalars, operands, outs, flops, after=()):
     vmem = pl.BlockSpec(memory_space=pltpu.VMEM)
     return pl.pallas_call(
         kernel,
         out_shape=[jax.ShapeDtypeStruct(shape, dtype) for shape, dtype in outs],
-        in_specs=[pl.BlockSpec(memory_space=pltpu.SMEM)] * len(scalars) + [vmem] * len(operands),
+        in_specs=[pl.BlockSpec(memory_space=pltpu.SMEM)] * len(scalars)
+        + [vmem] * len(operands)
+        + [pl.BlockSpec(memory_space=pl.ANY)] * len(after),
         out_specs=[vmem] * len(outs),
         compiler_params=pltpu.CompilerParams(vmem_limit_bytes=20 * 1024 * 1024),
         cost_estimate=pl.CostEstimate(flops=flops, bytes_accessed=0, transcendentals=0),
-    )(*scalars, *operands)
+    )(*scalars, *operands, *after)
 
 
 def on_device_ring(queries, keys_values, out_weight):
@@ -254,31 +256,35 @@
         4 * n * (n - 1) * ROWS**2 * width,
     )
 
-    def finish(flip_core, dtype):
+    def finish(flips, dtype, after=()):
         (sums,) = call(
-            functools.partial(finish_kernel, heads, n, flip_core),
+            functools.partial(finish_kernel, heads, n, flips),
             (where,),
             [rows, *state, keys[far], values[far], out_weight],
-            [((n // 2 * ROWS, cols), dtype)],
+            [((len(flips) * 2 * ROWS, cols), dtype)],
             n * ROWS * width * cols,
+            after,
         )
-        return sums
-
-    from_core = lax.ppermute(finish(1, bf16), "heads", [(h, h ^ 1) for h in range(4)])
-    kept = finish(0, f32)
+        return sums.reshape(len(flips), 2 * ROWS, cols)
+
+    given = finish([(1, 1), (0, 1)], bf16)
+    from_core = lax.ppermute(given, "heads", [(h, h ^ 1) for h in range(4)])
+    given = (finish([(1, 0)], f32, (given,))[0] + from_core[0].astype(f32)).astype(bf16)
+    from_x = lax.ppermute(given, "heads", [(h, h ^ 2) for h in range(4)])
+    kept = finish([(0, 0)], f32, (given,))[0]
     arrived = []
-    for slot in range(n // 2):
-        rows = slice(slot * ROWS, (slot + 1) * ROWS)
+    for slot in range(2):
+        part = slice(slot * ROWS, (slot + 1) * ROWS)
         pairs = []
         for f in range(n):
             for h in range(4):
-                to = PATTERNS[slot ^ (2 * (f & 1) + (h >> 1))][f >> 1]
+                to = PATTERNS[(slot ^ (f & 1)) + 2 * (h >> 1)][f >> 1]
                 pairs.append((4 * f + h, 4 * (2 * to + (h & 1)) + (f >> 1)))
-        total = (kept[rows] + from_core[rows].astype(f32)).astype(bf16)
-        arrived.append(lax.ppermute(total, ("frames", "heads"), pairs).astype(f32))
-    low, high = (arrived[0] + arrived[1]).astype(bf16), (arrived[2] + arrived[3]).astype(bf16)
+        total = kept[part] + from_core[1, part].astype(f32) + from_x[part].astype(f32)
+        arrived.append(lax.ppermute(total.astype(bf16), ("frames", "heads"), pairs))
     patterns = [[p[source] for p in PATTERNS].index(to) for source in range(4) for to in range(4)]
-    straight = look_up(patterns, 4 * head + z) & 2 == 0
+    straight = look_up(patterns, 4 * head + z) & 1 == 0
+    low, high = arrived
     return jnp.concatenate([jnp.where(straight, low, high), jnp.where(straight, high, low)], axis=1)
 
 

time: 60.4 us -> 61 us (level)
  the two profiles are of different devices: /device:TPU:1 before, /device:TPU:3 now
where the time goes in v11:
time: 61 us; the launch traced here: 60.5 us
  starting transfers between devices  28.1 us (46%)
  waiting for transfers between devices  19.3 us (32%)
  Pallas kernels  10.1 us (17%)
  local copies, waits for them, and re-layouts  1.94 us (3%)
  other arithmetic  0.87 us (1%)
    ppermute x21, starting transfers between devices, hop(): return lax.ppermute(x, ('frames', 'heads'), pairs)  17.9 us
    pallas_call x6, Pallas kernels, call(): pl.pallas_call(kernel, out_shape=[jax.ShapeDtypeStruct(shape, dtype) for...  10.1 us
    ppermute x21, waiting for transfers between devices, hop(): return lax.ppermute(x, ('frames', 'heads'), pairs)  8.01 us
    ppermute x2, starting transfers between devices, on_device_ring(): arrived.append(lax.ppermute(total.astype(bf16), ('frames', 'heads'), pairs))  6.65 us
    ppermute x2, waiting for transfers between devices, on_device_ring(): arrived.append(lax.ppermute(total.astype(bf16), ('frames', 'heads'), pairs))  5.84 us
    ppermute x1, waiting for transfers between devices, on_device_ring(): from_x = lax.ppermute(given, 'heads', [(h, h ^ 2) for h in range(4)])  5.45 us
    ppermute x1, starting transfers between devices, on_device_ring(): from_core = lax.ppermute(given, 'heads', [(h, h ^ 1) for h in range(4)])  3.17 us
    unnamed x6, local copies, waits for them, and re-layouts  1.85 us
  transfers between devices with their start and end apart: 25, of which 14 were waited for; matrix products, arithmetic and copies ran while one was open for 0% of the time, Pallas kernels for 13%

profile of v11, /device:TPU:3, one launch (start us, length us, event | category | flops | bytes accessed | tf_op | source)
XLA Modules:
  0.0 60.5 jit_solution(4811823356304759843)
XLA Ops:
  0.0 1.2 %collective-permute-start = (bf16[96,640]{1,0:T(8,128)(2,1)}, bf16[96,640]{1,0:T(8,128)(2,1)S(1)}, u32[]{:S(2)}, u32[]{:S(2)}) collective-permute-start(bf16[96,640]{1,0:T(8,128)(2,1)} %refs_0_.1), channel_id=1, source_target_pairs={{0,8},{1,5},{2,10},{3,7},{8,16},{9,1},{10,18},{11,3},{16,24},{17,9... | collective-permute-start | bytes 368648 | tf_op jit(solution)/shard_map/ppermute | solution.py:91
  2.4 1.3 %collective-permute-start.10 = (bf16[96,640]{1,0:T(8,128)(2,1)S(1)}, bf16[96,640]{1,0:T(8,128)(2,1)S(1)}, u32[]{:S(2)}, u32[]{:S(2)}) collective-permute-start(bf16[96,640]{1,0:T(8,128)(2,1)S(1)} %get-tuple-element.10.refs_0_), channel_id=1, source_target_pairs={{0,4},{1,9},{2,6},{3,11},{8,0},{9,17},{10,2},{11,19},{16,8},{17,25... | collective-permute-start | bytes 368648 | tf_op jit(solution)/shard_map/ppermute | solution.py:91
  4.0 1.3 %collective-permute-start.16 = (bf16[96,640]{1,0:T(8,128)(2,1)S(1)}, bf16[96,640]{1,0:T(8,128)(2,1)S(1)}, u32[]{:S(2)}, u32[]{:S(2)}) collective-permute-start(bf16[96,640]{1,0:T(8,128)(2,1)S(1)} %get-tuple-element.11.refs_7_), channel_id=1, source_target_pairs={{0,4},{1,9},{2,6},{3,11},{8,0},{9,17},{10,2},{11,19},{16,8},{17,25... | collective-permute-start | bytes 368648 | tf_op jit(solution)/shard_map/ppermute | solution.py:91
  5.5 1.2 %collective-permute-done.4.refs_7_ = bf16[96,640]{1,0:T(8,128)(2,1)S(1)} collective-permute-done((bf16[96,640]{1,0:T(8,128)(2,1)}, bf16[96,640]{1,0:T(8,128)(2,1)S(1)}, u32[]{:S(2)}, u32[]{:S(2)}) %collective-permute-start.4) | collective-permute-done | bytes 122912 | tf_op jit(solution)/shard_map/ppermute | solution.py:91
  9.1 1.3 %collective-permute-start.11 = (bf16[96,640]{1,0:T(8,128)(2,1)S(1)}, bf16[96,640]{1,0:T(8,128)(2,1)S(1)}, u32[]{:S(2)}, u32[]{:S(2)}) collective-permute-start(bf16[96,640]{1,0:T(8,128)(2,1)S(1)} %collective-permute-done.10.refs_6_), channel_id=1, source_target_pairs={{0,4},{1,9},{2,6},{3,11},{8,0},{9,17},{10,2},{11,19},{16,8},{17,25... | collective-permute-start | bytes 368648 | tf_op jit(solution)/shard_map/ppermute | solution.py:91
  11.7 1.3 %collective-permute-start.17 = (bf16[96,640]{1,0:T(8,128)(2,1)S(1)}, bf16[96,640]{1,0:T(8,128)(2,1)S(1)}, u32[]{:S(2)}, u32[]{:S(2)}) collective-permute-start(bf16[96,640]{1,0:T(8,128)(2,1)S(1)} %collective-permute-done.16.refs_13_), channel_id=1, source_target_pairs={{0,4},{1,9},{2,6},{3,11},{8,0},{9,17},{10,2},{11,19},{16,8},{17,25... | collective-permute-start | bytes 368648 | tf_op jit(solution)/shard_map/ppermute | solution.py:91
  13.7 1.2 %collective-permute-start.8 = (bf16[96,640]{1,0:T(8,128)(2,1)S(1)}, bf16[96,640]{1,0:T(8,128)(2,1)S(1)}, u32[]{:S(2)}, u32[]{:S(2)}) collective-permute-start(bf16[96,640]{1,0:T(8,128)(2,1)S(1)} %collective-permute-done.7.refs_1_), channel_id=1, source_target_pairs={{0,8},{1,5},{2,10},{3,7},{8,16},{9,1},{10,18},{11,3},{16,24},{17,9... | collective-permute-start | bytes 368648 | tf_op jit(solution)/shard_map/ppermute | solution.py:91
  16.3 1.3 %collective-permute-start.12 = (bf16[96,640]{1,0:T(8,128)(2,1)S(1)}, bf16[96,640]{1,0:T(8,128)(2,1)S(1)}, u32[]{:S(2)}, u32[]{:S(2)}) collective-permute-start(bf16[96,640]{1,0:T(8,128)(2,1)S(1)} %collective-permute-done.11.refs_5_), channel_id=1, source_target_pairs={{0,4},{1,9},{2,6},{3,11},{8,0},{9,17},{10,2},{11,19},{16,8},{17,25... | collective-permute-start | bytes 368648 | tf_op jit(solution)/shard_map/ppermute | solution.py:91
  18.1 1.2 %collective-permute-start.15 = (bf16[96,640]{1,0:T(8,128)(2,1)S(1)}, bf16[96,640]{1,0:T(8,128)(2,1)S(1)}, u32[]{:S(2)}, u32[]{:S(2)}) collective-permute-start(bf16[96,640]{1,0:T(8,128)(2,1)S(1)} %collective-permute-done.14.refs_9_), channel_id=1, source_target_pairs={{0,8},{1,5},{2,10},{3,7},{8,16},{9,1},{10,18},{11,3},{16,24},{17,9... | collective-permute-start | bytes 368648 | tf_op jit(solution)/shard_map/ppermute | solution.py:91
  19.3 1.3 %collective-permute-start.3 = (bf16[96,640]{1,0:T(8,128)(2,1)S(1)}, bf16[96,640]{1,0:T(8,128)(2,1)S(1)}, u32[]{:S(2)}, u32[]{:S(2)}) collective-permute-start(bf16[96,640]{1,0:T(8,128)(2,1)S(1)} %collective-permute-done.2.refs_3_), channel_id=1, source_target_pairs={{0,8},{1,5},{2,10},{3,7},{8,16},{9,1},{10,18},{11,3},{16,24},{17,9... | collective-permute-start | bytes 368648 | tf_op jit(solution)/shard_map/ppermute | solution.py:91
  21.4 1.3 %collective-permute-start.18 = (bf16[96,640]{1,0:T(8,128)(2,1)S(1)}, bf16[96,640]{1,0:T(8,128)(2,1)S(1)}, u32[]{:S(2)}, u32[]{:S(2)}) collective-permute-start(bf16[96,640]{1,0:T(8,128)(2,1)S(1)} %collective-permute-done.17.refs_12_), channel_id=1, source_target_pairs={{0,4},{1,9},{2,6},{3,11},{8,0},{9,17},{10,2},{11,19},{16,8},{17,25... | collective-permute-start | bytes 368648 | tf_op jit(solution)/shard_map/ppermute | solution.py:91
  23.2 1.1 %collective-permute-start.19 = (bf16[96,640]{1,0:T(8,128)(2,1)S(1)}, bf16[96,640]{1,0:T(8,128)(2,1)S(1)}, u32[]{:S(2)}, u32[]{:S(2)}) collective-permute-start(bf16[96,640]{1,0:T(8,128)(2,1)S(1)} %collective-permute-done.12.refs_4_), channel_id=1, source_target_pairs={{0,4},{1,9},{2,6},{3,11},{8,0},{9,17},{10,2},{11,19},{16,8},{17,25... | collective-permute-start | bytes 368648 | tf_op jit(solution)/shard_map/ppermute | solution.py:91
  24.7 1.2 %collective-permute-done.3.refs_4_ = bf16[96,640]{1,0:T(8,128)(2,1)S(1)} collective-permute-done((bf16[96,640]{1,0:T(8,128)(2,1)S(1)}, bf16[96,640]{1,0:T(8,128)(2,1)S(1)}, u32[]{:S(2)}, u32[]{:S(2)}) %collective-permute-start.3) | collective-permute-done | bytes 122912 | tf_op jit(solution)/shard_map/ppermute | solution.py:91
  26.8 1.2 %collective-permute-done.9.refs_3_ = bf16[96,640]{1,0:T(8,128)(2,1)S(1)} collective-permute-done((bf16[96,640]{1,0:T(8,128)(2,1)S(1)}, bf16[96,640]{1,0:T(8,128)(2,1)S(1)}, u32[]{:S(2)}, u32[]{:S(2)}) %collective-permute-start.9) | collective-permute-done | bytes 122912 | tf_op jit(solution)/shard_map/ppermute | solution.py:91
  28.0 4.8 %shard_map.39 = (f32[5,8,96,128]{3,2,1,0:T(8,128)S(1)}, f32[5,8,96,128]{3,2,1,0:T(8,128)S(1)}, f32[5,8,96,128]{3,2,1,0:T(8,128)S(1)}) custom-call(s32[5]{0:T(128)S(1)} %stack.23.at_ref, bf16[8,96,640]{2,1,0:T(8,128)(2,1)S(1)} %shard_map.37.rows_ref, bf16[96,640]{1,0:T(8,128)(2,1)S(1)} %get-tuple-element.10.refs_0_, ...), custom_call_target="tpu_custom_call" | custom-call | flops 1321205760 | tf_op jit(solution)/shard_map/pallas_call | solution.py:226
  32.8 2.1 %shard_map.40 = bf16[384,640]{1,0:T(8,128)(2,1)S(1)} custom-call(s32[5]{0:T(128)S(1)} %stack.23.at_ref, bf16[8,96,640]{2,1,0:T(8,128)(2,1)S(1)} %shard_map.37.rows_ref, f32[5,8,96,128]{3,2,1,0:T(8,128)S(1)} %get-tuple-element.12.mixed_ref, f32[5,8,96,128]{3,2,1,0:T(8,128)S(1)} %get-tuple-element.13.sum_ref, f32[5,8,96,128]{3,2,1,0:T(8,128)S(1)} %get-tuple-element.14.top_ref, ...), custom_call_target="tpu_custom_call" | custom-call | flops 314572800 | tf_op jit(solution)/shard_map/pallas_call | solution.py:226
  34.9 3.2 %collective-permute-start.21 = (bf16[2,192,640]{2,1,0:T(8,128)(2,1)S(1)}, bf16[2,192,640]{2,1,0:T(8,128)(2,1)S(1)}, u32[]{:S(2)}, u32[]{:S(2)}) collective-permute-start(bf16[2,192,640]{2,1,0:T(8,128)(2,1)S(1)} %bitcast.21), channel_id=1, source_target_pairs={{0,1},{1,0},{2,3},{3,2},{4,5},{5,4},{6,7},{7,6},{8,9},{9,8},{10,11... | collective-permute-start | bytes 1474568 | tf_op jit(solution)/shard_map/ppermute | solution.py:271
  38.1 1.6 %shard_map.41 = f32[192,640]{1,0:T(8,128)S(1)} custom-call(s32[5]{0:T(128)S(1)} %stack.23.at_ref, bf16[8,96,640]{2,1,0:T(8,128)(2,1)S(1)} %shard_map.37.rows_ref, f32[5,8,96,128]{3,2,1,0:T(8,128)S(1)} %get-tuple-element.12.mixed_ref, f32[5,8,96,128]{3,2,1,0:T(8,128)S(1)} %get-tuple-element.13.sum_ref, f32[5,8,96,128]{3,2,1,0:T(8,128)S(1)} %get-tuple-element.14.top_ref, ...), custom_call_target="tpu_custom_call" | custom-call | flops 314572800 | tf_op jit(solution)/shard_map/pallas_call | solution.py:226
  40.0 1.6 %shard_map.42 = f32[192,640]{1,0:T(8,128)S(1)} custom-call(s32[5]{0:T(128)S(1)} %stack.23.at_ref, bf16[8,96,640]{2,1,0:T(8,128)(2,1)S(1)} %shard_map.37.rows_ref, f32[5,8,96,128]{3,2,1,0:T(8,128)S(1)} %get-tuple-element.12.mixed_ref, f32[5,8,96,128]{3,2,1,0:T(8,128)S(1)} %get-tuple-element.13.sum_ref, f32[5,8,96,128]{3,2,1,0:T(8,128)S(1)} %get-tuple-element.14.top_ref, ...), custom_call_target="tpu_custom_call" | custom-call | flops 314572800 | tf_op jit(solution)/shard_map/pallas_call | solution.py:226
  41.6 5.5 %collective-permute-done.22 = bf16[192,640]{1,0:T(8,128)(2,1)S(1)} collective-permute-done((bf16[192,640]{1,0:T(8,128)(2,1)S(1)}, bf16[192,640]{1,0:T(8,128)(2,1)S(1)}, u32[]{:S(2)}, u32[]{:S(2)}) %collective-permute-start.22) | collective-permute-done | bytes 245792 | tf_op jit(solution)/shard_map/ppermute | solution.py:273
  47.2 4.1 %collective-permute-start.23 = (bf16[96,640]{1,0:T(8,128)(2,1)S(1)}, bf16[96,640]{1,0:T(8,128)(2,1)S(1)}, u32[]{:S(2)}, u32[]{:S(2)}) collective-permute-start(bf16[96,640]{1,0:T(8,128)(2,1)S(1)} %get-tuple-element.15), channel_id=1, source_target_pairs={{0,16},{1,20},{2,24},{3,28},{4,0},{5,4},{6,8},{7,12},{8,9},{9,13},... | collective-permute-start | bytes 368648 | tf_op jit(solution)/shard_map/ppermute | solution.py:284
  51.3 2.5 %collective-permute-start.24 = (bf16[96,640]{1,0:T(8,128)(2,1)S(1)}, bf16[96,640]{1,0:T(8,128)(2,1)S(1)}, u32[]{:S(2)}, u32[]{:S(2)}) collective-permute-start(bf16[96,640]{1,0:T(8,128)(2,1)S(1)} %get-tuple-element.16), channel_id=1, source_target_pairs={{0,0},{1,4},{2,8},{3,12},{4,16},{5,20},{6,24},{7,28},{8,25},{9,29}... | collective-permute-start | bytes 368648 | tf_op jit(solution)/shard_map/ppermute | solution.py:284
  53.9 1.8 %collective-permute-done.23 = bf16[96,640]{1,0:T(8,128)(2,1)S(1)} collective-permute-done((bf16[96,640]{1,0:T(8,128)(2,1)S(1)}, bf16[96,640]{1,0:T(8,128)(2,1)S(1)}, u32[]{:S(2)}, u32[]{:S(2)}) %collective-permute-start.23) | collective-permute-done | bytes 122912 | tf_op jit(solution)/shard_map/ppermute | solution.py:284
  55.6 4.1 %collective-permute-done.24 = bf16[96,640]{1,0:T(8,128)(2,1)S(1)} collective-permute-done((bf16[96,640]{1,0:T(8,128)(2,1)S(1)}, bf16[96,640]{1,0:T(8,128)(2,1)S(1)}, u32[]{:S(2)}, u32[]{:S(2)}) %collective-permute-start.24) | collective-permute-done | bytes 122912 | tf_op jit(solution)/shard_map/ppermute | solution.py:284
  (43 shorter events, 11.7 us)
Async XLA Ops:
  0.0 5.3 %collective-permute-start = (bf16[96,640]{1,0:T(8,128)(2,1)}, bf16[96,640]{1,0:T(8,128)(2,1)S(1)}, u32[]{:S(2)}, u32[]{:S(2)}) collective-permute-start(bf16[96,640]{1,0:T(8,128)(2,1)} %refs_0_.1), channel_id=1, source_target_pairs={{0,8},{1,5},{2,10},{3,7},{8,16},{9,1},{10,18},{11,3},{16,24},{17,9... | collective-permute-start | bytes 368648 | tf_op jit(solution)/shard_map/ppermute | solution.py:91
  1.2 5.4 %collective-permute-start.4 = (bf16[96,640]{1,0:T(8,128)(2,1)}, bf16[96,640]{1,0:T(8,128)(2,1)S(1)}, u32[]{:S(2)}, u32[]{:S(2)}) collective-permute-start(bf16[96,640]{1,0:T(8,128)(2,1)} %refs_0_.1), channel_id=1, source_target_pairs={{0,4},{1,9},{2,6},{3,11},{8,0},{9,17},{10,2},{11,19},{16,8},{17,25... | collective-permute-start | bytes 368648 | tf_op jit(solution)/shard_map/ppermute | solution.py:91
  2.4 5.6 %collective-permute-start.10 = (bf16[96,640]{1,0:T(8,128)(2,1)S(1)}, bf16[96,640]{1,0:T(8,128)(2,1)S(1)}, u32[]{:S(2)}, u32[]{:S(2)}) collective-permute-start(bf16[96,640]{1,0:T(8,128)(2,1)S(1)} %get-tuple-element.10.refs_0_), channel_id=1, source_target_pairs={{0,4},{1,9},{2,6},{3,11},{8,0},{9,17},{10,2},{11,19},{16,8},{17,25... | collective-permute-start | bytes 368648 | tf_op jit(solution)/shard_map/ppermute | solution.py:91
  3.8 5.3 %collective-permute-start.13 = (bf16[96,640]{1,0:T(8,128)(2,1)S(1)}, bf16[96,640]{1,0:T(8,128)(2,1)S(1)}, u32[]{:S(2)}, u32[]{:S(2)}) collective-permute-start(bf16[96,640]{1,0:T(8,128)(2,1)S(1)} %get-tuple-element.11.refs_7_), channel_id=1, source_target_pairs={{0,8},{1,5},{2,10},{3,7},{8,16},{9,1},{10,18},{11,3},{16,24},{17,9... | collective-permute-start | bytes 368648 | tf_op jit(solution)/shard_map/ppermute | solution.py:91
  4.0 6.5 %collective-permute-start.16 = (bf16[96,640]{1,0:T(8,128)(2,1)S(1)}, bf16[96,640]{1,0:T(8,128)(2,1)S(1)}, u32[]{:S(2)}, u32[]{:S(2)}) collective-permute-start(bf16[96,640]{1,0:T(8,128)(2,1)S(1)} %get-tuple-element.11.refs_7_), channel_id=1, source_target_pairs={{0,4},{1,9},{2,6},{3,11},{8,0},{9,17},{10,2},{11,19},{16,8},{17,25... | collective-permute-start | bytes 368648 | tf_op jit(solution)/shard_map/ppermute | solution.py:91
  5.3 6.5 %collective-permute-start.7 = (bf16[96,640]{1,0:T(8,128)(2,1)S(1)}, bf16[96,640]{1,0:T(8,128)(2,1)S(1)}, u32[]{:S(2)}, u32[]{:S(2)}) collective-permute-start(bf16[96,640]{1,0:T(8,128)(2,1)S(1)} %get-tuple-element.10.refs_0_), channel_id=1, source_target_pairs={{0,8},{1,5},{2,10},{3,7},{8,16},{9,1},{10,18},{11,3},{16,24},{17,9... | collective-permute-start | bytes 368648 | tf_op jit(solution)/shard_map/ppermute | solution.py:91
  6.7 6.8 %collective-permute-start.1 = (bf16[96,640]{1,0:T(8,128)(2,1)S(1)}, bf16[96,640]{1,0:T(8,128)(2,1)S(1)}, u32[]{:S(2)}, u32[]{:S(2)}) collective-permute-start(bf16[96,640]{1,0:T(8,128)(2,1)S(1)} %collective-permute-done.refs_1_), channel_id=1, source_target_pairs={{0,8},{1,5},{2,10},{3,7},{8,16},{9,1},{10,18},{11,3},{16,24},{17,9... | collective-permute-start | bytes 368648 | tf_op jit(solution)/shard_map/ppermute | solution.py:91
  8.0 5.7 %collective-permute-start.5 = (bf16[96,640]{1,0:T(8,128)(2,1)S(1)}, bf16[96,640]{1,0:T(8,128)(2,1)S(1)}, u32[]{:S(2)}, u32[]{:S(2)}) collective-permute-start(bf16[96,640]{1,0:T(8,128)(2,1)S(1)} %collective-permute-done.4.refs_7_), channel_id=1, source_target_pairs={{0,4},{1,9},{2,6},{3,11},{8,0},{9,17},{10,2},{11,19},{16,8},{17,25... | collective-permute-start | bytes 368648 | tf_op jit(solution)/shard_map/ppermute | solution.py:91
  9.1 6.8 %collective-permute-start.11 = (bf16[96,640]{1,0:T(8,128)(2,1)S(1)}, bf16[96,640]{1,0:T(8,128)(2,1)S(1)}, u32[]{:S(2)}, u32[]{:S(2)}) collective-permute-start(bf16[96,640]{1,0:T(8,128)(2,1)S(1)} %collective-permute-done.10.refs_6_), channel_id=1, source_target_pairs={{0,4},{1,9},{2,6},{3,11},{8,0},{9,17},{10,2},{11,19},{16,8},{17,25... | collective-permute-start | bytes 368648 | tf_op jit(solution)/shard_map/ppermute | solution.py:91
  10.4 5.9 %collective-permute-start.14 = (bf16[96,640]{1,0:T(8,128)(2,1)S(1)}, bf16[96,640]{1,0:T(8,128)(2,1)S(1)}, u32[]{:S(2)}, u32[]{:S(2)}) collective-permute-start(bf16[96,640]{1,0:T(8,128)(2,1)S(1)} %collective-permute-done.13.refs_8_), channel_id=1, source_target_pairs={{0,8},{1,5},{2,10},{3,7},{8,16},{9,1},{10,18},{11,3},{16,24},{17,9... | collective-permute-start | bytes 368648 | tf_op jit(solution)/shard_map/ppermute | solution.py:91
  11.7 6.4 %collective-permute-start.17 = (bf16[96,640]{1,0:T(8,128)(2,1)S(1)}, bf16[96,640]{1,0:T(8,128)(2,1)S(1)}, u32[]{:S(2)}, u32[]{:S(2)}) collective-permute-start(bf16[96,640]{1,0:T(8,128)(2,1)S(1)} %collective-permute-done.16.refs_13_), channel_id=1, source_target_pairs={{0,4},{1,9},{2,6},{3,11},{8,0},{9,17},{10,2},{11,19},{16,8},{17,25... | collective-permute-start | bytes 368648 | tf_op jit(solution)/shard_map/ppermute | solution.py:91
  13.5 5.8 %collective-permute-start.2 = (bf16[96,640]{1,0:T(8,128)(2,1)S(1)}, bf16[96,640]{1,0:T(8,128)(2,1)S(1)}, u32[]{:S(2)}, u32[]{:S(2)}) collective-permute-start(bf16[96,640]{1,0:T(8,128)(2,1)S(1)} %collective-permute-done.1.refs_2_), channel_id=1, source_target_pairs={{0,8},{1,5},{2,10},{3,7},{8,16},{9,1},{10,18},{11,3},{16,24},{17,9... | collective-permute-start | bytes 368648 | tf_op jit(solution)/shard_map/ppermute | solution.py:91
  13.7 7.7 %collective-permute-start.8 = (bf16[96,640]{1,0:T(8,128)(2,1)S(1)}, bf16[96,640]{1,0:T(8,128)(2,1)S(1)}, u32[]{:S(2)}, u32[]{:S(2)}) collective-permute-start(bf16[96,640]{1,0:T(8,128)(2,1)S(1)} %collective-permute-done.7.refs_1_), channel_id=1, source_target_pairs={{0,8},{1,5},{2,10},{3,7},{8,16},{9,1},{10,18},{11,3},{16,24},{17,9... | collective-permute-start | bytes 368648 | tf_op jit(solution)/shard_map/ppermute | solution.py:91
  15.9 6.8 %collective-permute-start.6 = (bf16[96,640]{1,0:T(8,128)(2,1)S(1)}, bf16[96,640]{1,0:T(8,128)(2,1)S(1)}, u32[]{:S(2)}, u32[]{:S(2)}) collective-permute-start(bf16[96,640]{1,0:T(8,128)(2,1)S(1)} %collective-permute-done.5.refs_6_), channel_id=1, source_target_pairs={{0,4},{1,9},{2,6},{3,11},{8,0},{9,17},{10,2},{11,19},{16,8},{17,25... | collective-permute-start | bytes 368648 | tf_op jit(solution)/shard_map/ppermute | solution.py:91
  16.3 6.9 %collective-permute-start.12 = (bf16[96,640]{1,0:T(8,128)(2,1)S(1)}, bf16[96,640]{1,0:T(8,128)(2,1)S(1)}, u32[]{:S(2)}, u32[]{:S(2)}) collective-permute-start(bf16[96,640]{1,0:T(8,128)(2,1)S(1)} %collective-permute-done.11.refs_5_), channel_id=1, source_target_pairs={{0,4},{1,9},{2,6},{3,11},{8,0},{9,17},{10,2},{11,19},{16,8},{17,25... | collective-permute-start | bytes 368648 | tf_op jit(solution)/shard_map/ppermute | solution.py:91
  18.1 6.2 %collective-permute-start.15 = (bf16[96,640]{1,0:T(8,128)(2,1)S(1)}, bf16[96,640]{1,0:T(8,128)(2,1)S(1)}, u32[]{:S(2)}, u32[]{:S(2)}) collective-permute-start(bf16[96,640]{1,0:T(8,128)(2,1)S(1)} %collective-permute-done.14.refs_9_), channel_id=1, source_target_pairs={{0,8},{1,5},{2,10},{3,7},{8,16},{9,1},{10,18},{11,3},{16,24},{17,9... | collective-permute-start | bytes 368648 | tf_op jit(solution)/shard_map/ppermute | solution.py:91
  19.3 6.5 %collective-permute-start.3 = (bf16[96,640]{1,0:T(8,128)(2,1)S(1)}, bf16[96,640]{1,0:T(8,128)(2,1)S(1)}, u32[]{:S(2)}, u32[]{:S(2)}) collective-permute-start(bf16[96,640]{1,0:T(8,128)(2,1)S(1)} %collective-permute-done.2.refs_3_), channel_id=1, source_target_pairs={{0,8},{1,5},{2,10},{3,7},{8,16},{9,1},{10,18},{11,3},{16,24},{17,9... | collective-permute-start | bytes 368648 | tf_op jit(solution)/shard_map/ppermute | solution.py:91
  21.4 5.4 %collective-permute-start.18 = (bf16[96,640]{1,0:T(8,128)(2,1)S(1)}, bf16[96,640]{1,0:T(8,128)(2,1)S(1)}, u32[]{:S(2)}, u32[]{:S(2)}) collective-permute-start(bf16[96,640]{1,0:T(8,128)(2,1)S(1)} %collective-permute-done.17.refs_12_), channel_id=1, source_target_pairs={{0,4},{1,9},{2,6},{3,11},{8,0},{9,17},{10,2},{11,19},{16,8},{17,25... | collective-permute-start | bytes 368648 | tf_op jit(solution)/shard_map/ppermute | solution.py:91
  22.7 5.3 %collective-permute-start.9 = (bf16[96,640]{1,0:T(8,128)(2,1)S(1)}, bf16[96,640]{1,0:T(8,128)(2,1)S(1)}, u32[]{:S(2)}, u32[]{:S(2)}) collective-permute-start(bf16[96,640]{1,0:T(8,128)(2,1)S(1)} %collective-permute-done.8.refs_2_), channel_id=1, source_target_pairs={{0,8},{1,5},{2,10},{3,7},{8,16},{9,1},{10,18},{11,3},{16,24},{17,9... | collective-permute-start | bytes 368648 | tf_op jit(solution)/shard_map/ppermute | solution.py:91
  23.2 9.6 %collective-permute-start.19 = (bf16[96,640]{1,0:T(8,128)(2,1)S(1)}, bf16[96,640]{1,0:T(8,128)(2,1)S(1)}, u32[]{:S(2)}, u32[]{:S(2)}) collective-permute-start(bf16[96,640]{1,0:T(8,128)(2,1)S(1)} %collective-permute-done.12.refs_4_), channel_id=1, source_target_pairs={{0,4},{1,9},{2,6},{3,11},{8,0},{9,17},{10,2},{11,19},{16,8},{17,25... | collective-permute-start | bytes 368648 | tf_op jit(solution)/shard_map/ppermute | solution.py:91
  24.3 8.5 %collective-permute-start.20 = (bf16[96,640]{1,0:T(8,128)(2,1)S(1)}, bf16[96,640]{1,0:T(8,128)(2,1)S(1)}, u32[]{:S(2)}, u32[]{:S(2)}) collective-permute-start(bf16[96,640]{1,0:T(8,128)(2,1)S(1)} %collective-permute-done.15.refs_10_), channel_id=1, source_target_pairs={{0,8},{1,5},{2,10},{3,7},{8,16},{9,1},{10,18},{11,3},{16,24},{17,9... | collective-permute-start | bytes 368648 | tf_op jit(solution)/shard_map/ppermute | solution.py:91
  39.7 7.4 %collective-permute-start.22 = (bf16[192,640]{1,0:T(8,128)(2,1)S(1)}, bf16[192,640]{1,0:T(8,128)(2,1)S(1)}, u32[]{:S(2)}, u32[]{:S(2)}) collective-permute-start(bf16[192,640]{1,0:T(8,128)(2,1)S(1)} %fusion.refs_0_), channel_id=1, source_target_pairs={{0,2},{1,3},{2,0},{3,1},{4,6},{5,7},{6,4},{7,5},{8,10},{9,11},{10,... | collective-permute-start | bytes 737288 | tf_op jit(solution)/shard_map/ppermute | solution.py:273
  47.2 8.4 %collective-permute-start.23 = (bf16[96,640]{1,0:T(8,128)(2,1)S(1)}, bf16[96,640]{1,0:T(8,128)(2,1)S(1)}, u32[]{:S(2)}, u32[]{:S(2)}) collective-permute-start(bf16[96,640]{1,0:T(8,128)(2,1)S(1)} %get-tuple-element.15), channel_id=1, source_target_pairs={{0,16},{1,20},{2,24},{3,28},{4,0},{5,4},{6,8},{7,12},{8,9},{9,13},... | collective-permute-start | bytes 368648 | tf_op jit(solution)/shard_map/ppermute | solution.py:284
  51.3 8.4 %collective-permute-start.24 = (bf16[96,640]{1,0:T(8,128)(2,1)S(1)}, bf16[96,640]{1,0:T(8,128)(2,1)S(1)}, u32[]{:S(2)}, u32[]{:S(2)}) collective-permute-start(bf16[96,640]{1,0:T(8,128)(2,1)S(1)} %get-tuple-element.16), channel_id=1, source_target_pairs={{0,0},{1,4},{2,8},{3,12},{4,16},{5,20},{6,24},{7,28},{8,25},{9,29}... | collective-permute-start | bytes 368648 | tf_op jit(solution)/shard_map/ppermute | solution.py:284
  (4 other events, 12.6 us)

commit v12 on v11

--- a/solution.py
+++ b/solution.py
@@ -269,18 +269,19 @@
 
     given = finish([(1, 1), (0, 1)], bf16)
     from_core = lax.ppermute(given, "heads", [(h, h ^ 1) for h in range(4)])
-    given = (finish([(1, 0)], f32, (given,))[0] + from_core[0].astype(f32)).astype(bf16)
-    from_x = lax.ppermute(given, "heads", [(h, h ^ 2) for h in range(4)])
-    kept = finish([(0, 0)], f32, (given,))[0]
+    sums = finish([(1, 0)], f32, (given,))[0]
+    parts = [slice(slot * ROWS, (slot + 1) * ROWS) for slot in range(2)]
+    given = [(sums[part] + from_core[0, part].astype(f32)).astype(bf16) for part in parts]
+    from_x = [lax.ppermute(block, "heads", [(h, h ^ 2) for h in range(4)]) for block in given]
+    kept = finish([(0, 0)], f32, given)[0]
     arrived = []
-    for slot in range(2):
-        part = slice(slot * ROWS, (slot + 1) * ROWS)
+    for slot, part in enumerate(parts):
         pairs = []
         for f in range(n):
             for h in range(4):
                 to = PATTERNS[(slot ^ (f & 1)) + 2 * (h >> 1)][f >> 1]
                 pairs.append((4 * f + h, 4 * (2 * to + (h & 1)) + (f >> 1)))
-        total = kept[part] + from_core[1, part].astype(f32) + from_x[part].astype(f32)
+        total = kept[part] + from_core[1, part].astype(f32) + from_x[slot].astype(f32)
         arrived.append(lax.ppermute(total.astype(bf16), ("frames", "heads"), pairs))
     patterns = [[p[source] for p in PATTERNS].index(to) for source in range(4) for to in range(4)]
     straight = look_up(patterns, 4 * head + z) & 1 == 0

time: 61 us -> 61 us (level)
  starting transfers between devices: 28.1 us -> 29.3 us
  waiting for transfers between devices: 19.3 us -> 18.1 us
    ppermute x1 -> x2, waiting for transfers between devices: 5.45 us -> 4.24 us  [on_device_ring(): lax.ppermute(block, 'heads', [(h, h ^ 2) for h in range(4)])]
    ppermute x1 -> x2, starting transfers between devices: 0.32 us -> 1.53 us  [on_device_ring(): lax.ppermute(block, 'heads', [(h, h ^ 2) for h in range(4)])]
  transfers between devices with their start and end apart: 25 -> 26, of which waited for: 14 -> 15; matrix products, arithmetic and copies ran while one was open for 0% -> 0% of each run, Pallas kernels for 13% -> 13%
where the time goes in v12:
time: 61 us; the launch traced here: 60.5 us
  starting transfers between devices  29.3 us (48%)
  waiting for transfers between devices  18.1 us (30%)
  Pallas kernels  10.1 us (17%)
  local copies, waits for them, and re-layouts  1.94 us (3%)
  other arithmetic  0.88 us (1%)
    ppermute x21, starting transfers between devices, hop(): return lax.ppermute(x, ('frames', 'heads'), pairs)  17.9 us
    pallas_call x6, Pallas kernels, call(): pl.pallas_call(kernel, out_shape=[jax.ShapeDtypeStruct(shape, dtype) for...  10.1 us
    ppermute x21, waiting for transfers between devices, hop(): return lax.ppermute(x, ('frames', 'heads'), pairs)  8.01 us
    ppermute x2, starting transfers between devices, on_device_ring(): arrived.append(lax.ppermute(total.astype(bf16), ('frames', 'heads'), pairs))  6.65 us
    ppermute x2, waiting for transfers between devices, on_device_ring(): arrived.append(lax.ppermute(total.astype(bf16), ('frames', 'heads'), pairs))  5.84 us
    ppermute x2, waiting for transfers between devices, on_device_ring(): lax.ppermute(block, 'heads', [(h, h ^ 2) for h in range(4)])  4.24 us
    ppermute x1, starting transfers between devices, on_device_ring(): from_core = lax.ppermute(given, 'heads', [(h, h ^ 1) for h in range(4)])  3.17 us
    unnamed x6, local copies, waits for them, and re-layouts  1.85 us
  transfers between devices with their start and end apart: 26, of which 15 were waited for; matrix products, arithmetic and copies ran while one was open for 0% of the time, Pallas kernels for 13%

profile of v12, /device:TPU:3, one launch (start us, length us, event | category | flops | bytes accessed | tf_op | source)
XLA Modules:
  0.0 60.5 jit_solution(11936040872621886267)
XLA Ops:
  0.0 1.2 %collective-permute-start = (bf16[96,640]{1,0:T(8,128)(2,1)}, bf16[96,640]{1,0:T(8,128)(2,1)S(1)}, u32[]{:S(2)}, u32[]{:S(2)}) collective-permute-start(bf16[96,640]{1,0:T(8,128)(2,1)} %refs_0_.1), channel_id=1, source_target_pairs={{0,8},{1,5},{2,10},{3,7},{8,16},{9,1},{10,18},{11,3},{16,24},{17,9... | collective-permute-start | bytes 368648 | tf_op jit(solution)/shard_map/ppermute | solution.py:91
  2.4 1.3 %collective-permute-start.10 = (bf16[96,640]{1,0:T(8,128)(2,1)S(1)}, bf16[96,640]{1,0:T(8,128)(2,1)S(1)}, u32[]{:S(2)}, u32[]{:S(2)}) collective-permute-start(bf16[96,640]{1,0:T(8,128)(2,1)S(1)} %get-tuple-element.10.refs_0_), channel_id=1, source_target_pairs={{0,4},{1,9},{2,6},{3,11},{8,0},{9,17},{10,2},{11,19},{16,8},{17,25... | collective-permute-start | bytes 368648 | tf_op jit(solution)/shard_map/ppermute | solution.py:91
  4.0 1.3 %collective-permute-start.16 = (bf16[96,640]{1,0:T(8,128)(2,1)S(1)}, bf16[96,640]{1,0:T(8,128)(2,1)S(1)}, u32[]{:S(2)}, u32[]{:S(2)}) collective-permute-start(bf16[96,640]{1,0:T(8,128)(2,1)S(1)} %get-tuple-element.11.refs_7_), channel_id=1, source_target_pairs={{0,4},{1,9},{2,6},{3,11},{8,0},{9,17},{10,2},{11,19},{16,8},{17,25... | collective-permute-start | bytes 368648 | tf_op jit(solution)/shard_map/ppermute | solution.py:91
  5.5 1.2 %collective-permute-done.4.refs_7_ = bf16[96,640]{1,0:T(8,128)(2,1)S(1)} collective-permute-done((bf16[96,640]{1,0:T(8,128)(2,1)}, bf16[96,640]{1,0:T(8,128)(2,1)S(1)}, u32[]{:S(2)}, u32[]{:S(2)}) %collective-permute-start.4) | collective-permute-done | bytes 122912 | tf_op jit(solution)/shard_map/ppermute | solution.py:91
  9.1 1.3 %collective-permute-start.11 = (bf16[96,640]{1,0:T(8,128)(2,1)S(1)}, bf16[96,640]{1,0:T(8,128)(2,1)S(1)}, u32[]{:S(2)}, u32[]{:S(2)}) collective-permute-start(bf16[96,640]{1,0:T(8,128)(2,1)S(1)} %collective-permute-done.10.refs_6_), channel_id=1, source_target_pairs={{0,4},{1,9},{2,6},{3,11},{8,0},{9,17},{10,2},{11,19},{16,8},{17,25... | collective-permute-start | bytes 368648 | tf_op jit(solution)/shard_map/ppermute | solution.py:91
  11.7 1.3 %collective-permute-start.17 = (bf16[96,640]{1,0:T(8,128)(2,1)S(1)}, bf16[96,640]{1,0:T(8,128)(2,1)S(1)}, u32[]{:S(2)}, u32[]{:S(2)}) collective-permute-start(bf16[96,640]{1,0:T(8,128)(2,1)S(1)} %collective-permute-done.16.refs_13_), channel_id=1, source_target_pairs={{0,4},{1,9},{2,6},{3,11},{8,0},{9,17},{10,2},{11,19},{16,8},{17,25... | collective-permute-start | bytes 368648 | tf_op jit(solution)/shard_map/ppermute | solution.py:91
  13.7 1.2 %collective-permute-start.8 = (bf16[96,640]{1,0:T(8,128)(2,1)S(1)}, bf16[96,640]{1,0:T(8,128)(2,1)S(1)}, u32[]{:S(2)}, u32[]{:S(2)}) collective-permute-start(bf16[96,640]{1,0:T(8,128)(2,1)S(1)} %collective-permute-done.7.refs_1_), channel_id=1, source_target_pairs={{0,8},{1,5},{2,10},{3,7},{8,16},{9,1},{10,18},{11,3},{16,24},{17,9... | collective-permute-start | bytes 368648 | tf_op jit(solution)/shard_map/ppermute | solution.py:91
  16.3 1.3 %collective-permute-start.12 = (bf16[96,640]{1,0:T(8,128)(2,1)S(1)}, bf16[96,640]{1,0:T(8,128)(2,1)S(1)}, u32[]{:S(2)}, u32[]{:S(2)}) collective-permute-start(bf16[96,640]{1,0:T(8,128)(2,1)S(1)} %collective-permute-done.11.refs_5_), channel_id=1, source_target_pairs={{0,4},{1,9},{2,6},{3,11},{8,0},{9,17},{10,2},{11,19},{16,8},{17,25... | collective-permute-start | bytes 368648 | tf_op jit(solution)/shard_map/ppermute | solution.py:91
  18.1 1.2 %collective-permute-start.15 = (bf16[96,640]{1,0:T(8,128)(2,1)S(1)}, bf16[96,640]{1,0:T(8,128)(2,1)S(1)}, u32[]{:S(2)}, u32[]{:S(2)}) collective-permute-start(bf16[96,640]{1,0:T(8,128)(2,1)S(1)} %collective-permute-done.14.refs_9_), channel_id=1, source_target_pairs={{0,8},{1,5},{2,10},{3,7},{8,16},{9,1},{10,18},{11,3},{16,24},{17,9... | collective-permute-start | bytes 368648 | tf_op jit(solution)/shard_map/ppermute | solution.py:91
  19.3 1.3 %collective-permute-start.3 = (bf16[96,640]{1,0:T(8,128)(2,1)S(1)}, bf16[96,640]{1,0:T(8,128)(2,1)S(1)}, u32[]{:S(2)}, u32[]{:S(2)}) collective-permute-start(bf16[96,640]{1,0:T(8,128)(2,1)S(1)} %collective-permute-done.2.refs_3_), channel_id=1, source_target_pairs={{0,8},{1,5},{2,10},{3,7},{8,16},{9,1},{10,18},{11,3},{16,24},{17,9... | collective-permute-start | bytes 368648 | tf_op jit(solution)/shard_map/ppermute | solution.py:91
  21.4 1.3 %collective-permute-start.18 = (bf16[96,640]{1,0:T(8,128)(2,1)S(1)}, bf16[96,640]{1,0:T(8,128)(2,1)S(1)}, u32[]{:S(2)}, u32[]{:S(2)}) collective-permute-start(bf16[96,640]{1,0:T(8,128)(2,1)S(1)} %collective-permute-done.17.refs_12_), channel_id=1, source_target_pairs={{0,4},{1,9},{2,6},{3,11},{8,0},{9,17},{10,2},{11,19},{16,8},{17,25... | collective-permute-start | bytes 368648 | tf_op jit(solution)/shard_map/ppermute | solution.py:91
  26.8 1.2 %collective-permute-done.9.refs_3_ = bf16[96,640]{1,0:T(8,128)(2,1)S(1)} collective-permute-done((bf16[96,640]{1,0:T(8,128)(2,1)S(1)}, bf16[96,640]{1,0:T(8,128)(2,1)S(1)}, u32[]{:S(2)}, u32[]{:S(2)}) %collective-permute-start.9) | collective-permute-done | bytes 122912 | tf_op jit(solution)/shard_map/ppermute | solution.py:91
  28.0 4.8 %shard_map.39 = (f32[5,8,96,128]{3,2,1,0:T(8,128)S(1)}, f32[5,8,96,128]{3,2,1,0:T(8,128)S(1)}, f32[5,8,96,128]{3,2,1,0:T(8,128)S(1)}) custom-call(s32[5]{0:T(128)S(1)} %stack.23.at_ref, bf16[8,96,640]{2,1,0:T(8,128)(2,1)S(1)} %shard_map.37.rows_ref, bf16[96,640]{1,0:T(8,128)(2,1)S(1)} %get-tuple-element.10.refs_0_, ...), custom_call_target="tpu_custom_call" | custom-call | flops 1321205760 | tf_op jit(solution)/shard_map/pallas_call | solution.py:226
  32.8 2.1 %shard_map.40 = bf16[384,640]{1,0:T(8,128)(2,1)S(1)} custom-call(s32[5]{0:T(128)S(1)} %stack.23.at_ref, bf16[8,96,640]{2,1,0:T(8,128)(2,1)S(1)} %shard_map.37.rows_ref, f32[5,8,96,128]{3,2,1,0:T(8,128)S(1)} %get-tuple-element.12.mixed_ref, f32[5,8,96,128]{3,2,1,0:T(8,128)S(1)} %get-tuple-element.13.sum_ref, f32[5,8,96,128]{3,2,1,0:T(8,128)S(1)} %get-tuple-element.14.top_ref, ...), custom_call_target="tpu_custom_call" | custom-call | flops 314572800 | tf_op jit(solution)/shard_map/pallas_call | solution.py:226
  34.9 3.2 %collective-permute-start.21 = (bf16[2,192,640]{2,1,0:T(8,128)(2,1)S(1)}, bf16[2,192,640]{2,1,0:T(8,128)(2,1)S(1)}, u32[]{:S(2)}, u32[]{:S(2)}) collective-permute-start(bf16[2,192,640]{2,1,0:T(8,128)(2,1)S(1)} %bitcast.26), channel_id=1, source_target_pairs={{0,1},{1,0},{2,3},{3,2},{4,5},{5,4},{6,7},{7,6},{8,9},{9,8},{10,11... | collective-permute-start | bytes 1474568 | tf_op jit(solution)/shard_map/ppermute | solution.py:271
  38.1 1.6 %shard_map.41 = f32[192,640]{1,0:T(8,128)S(1)} custom-call(s32[5]{0:T(128)S(1)} %stack.23.at_ref, bf16[8,96,640]{2,1,0:T(8,128)(2,1)S(1)} %shard_map.37.rows_ref, f32[5,8,96,128]{3,2,1,0:T(8,128)S(1)} %get-tuple-element.12.mixed_ref, f32[5,8,96,128]{3,2,1,0:T(8,128)S(1)} %get-tuple-element.13.sum_ref, f32[5,8,96,128]{3,2,1,0:T(8,128)S(1)} %get-tuple-element.14.top_ref, ...), custom_call_target="tpu_custom_call" | custom-call | flops 314572800 | tf_op jit(solution)/shard_map/pallas_call | solution.py:226
  40.0 1.2 %collective-permute-start.24 = (bf16[96,640]{1,0:T(8,128)(2,1)S(1)}, bf16[96,640]{1,0:T(8,128)(2,1)S(1)}, u32[]{:S(2)}, u32[]{:S(2)}) collective-permute-start(bf16[96,640]{1,0:T(8,128)(2,1)S(1)} %get-tuple-element.17.refs_1_), channel_id=1, source_target_pairs={{0,2},{1,3},{2,0},{3,1},{4,6},{5,7},{6,4},{7,5},{8,10},{9,11},{10,... | collective-permute-start | bytes 368648 | tf_op jit(solution)/shard_map/ppermute | solution.py:275
  41.3 1.6 %shard_map.42 = f32[192,640]{1,0:T(8,128)S(1)} custom-call(s32[5]{0:T(128)S(1)} %stack.23.at_ref, bf16[8,96,640]{2,1,0:T(8,128)(2,1)S(1)} %shard_map.37.rows_ref, f32[5,8,96,128]{3,2,1,0:T(8,128)S(1)} %get-tuple-element.12.mixed_ref, f32[5,8,96,128]{3,2,1,0:T(8,128)S(1)} %get-tuple-element.13.sum_ref, f32[5,8,96,128]{3,2,1,0:T(8,128)S(1)} %get-tuple-element.14.top_ref, ...), custom_call_target="tpu_custom_call" | custom-call | flops 314572800 | tf_op jit(solution)/shard_map/pallas_call | solution.py:226
  42.9 1.6 %collective-permute-done.22 = bf16[96,640]{1,0:T(8,128)(2,1)S(1)} collective-permute-done((bf16[96,640]{1,0:T(8,128)(2,1)S(1)}, bf16[96,640]{1,0:T(8,128)(2,1)S(1)}, u32[]{:S(2)}, u32[]{:S(2)}) %collective-permute-start.22) | collective-permute-done | bytes 122912 | tf_op jit(solution)/shard_map/ppermute | solution.py:275
  44.5 2.6 %collective-permute-done.24 = bf16[96,640]{1,0:T(8,128)(2,1)S(1)} collective-permute-done((bf16[96,640]{1,0:T(8,128)(2,1)S(1)}, bf16[96,640]{1,0:T(8,128)(2,1)S(1)}, u32[]{:S(2)}, u32[]{:S(2)}) %collective-permute-start.24) | collective-permute-done | bytes 122912 | tf_op jit(solution)/shard_map/ppermute | solution.py:275
  47.2 4.1 %collective-permute-start.23 = (bf16[96,640]{1,0:T(8,128)(2,1)S(1)}, bf16[96,640]{1,0:T(8,128)(2,1)S(1)}, u32[]{:S(2)}, u32[]{:S(2)}) collective-permute-start(bf16[96,640]{1,0:T(8,128)(2,1)S(1)} %get-tuple-element.15), channel_id=1, source_target_pairs={{0,16},{1,20},{2,24},{3,28},{4,0},{5,4},{6,8},{7,12},{8,9},{9,13},... | collective-permute-start | bytes 368648 | tf_op jit(solution)/shard_map/ppermute | solution.py:285
  51.3 2.5 %collective-permute-start.25 = (bf16[96,640]{1,0:T(8,128)(2,1)S(1)}, bf16[96,640]{1,0:T(8,128)(2,1)S(1)}, u32[]{:S(2)}, u32[]{:S(2)}) collective-permute-start(bf16[96,640]{1,0:T(8,128)(2,1)S(1)} %get-tuple-element.16), channel_id=1, source_target_pairs={{0,0},{1,4},{2,8},{3,12},{4,16},{5,20},{6,24},{7,28},{8,25},{9,29}... | collective-permute-start | bytes 368648 | tf_op jit(solution)/shard_map/ppermute | solution.py:285
  53.9 1.8 %collective-permute-done.23 = bf16[96,640]{1,0:T(8,128)(2,1)S(1)} collective-permute-done((bf16[96,640]{1,0:T(8,128)(2,1)S(1)}, bf16[96,640]{1,0:T(8,128)(2,1)S(1)}, u32[]{:S(2)}, u32[]{:S(2)}) %collective-permute-start.23) | collective-permute-done | bytes 122912 | tf_op jit(solution)/shard_map/ppermute | solution.py:285
  55.6 4.1 %collective-permute-done.25 = bf16[96,640]{1,0:T(8,128)(2,1)S(1)} collective-permute-done((bf16[96,640]{1,0:T(8,128)(2,1)S(1)}, bf16[96,640]{1,0:T(8,128)(2,1)S(1)}, u32[]{:S(2)}, u32[]{:S(2)}) %collective-permute-start.25) | collective-permute-done | bytes 122912 | tf_op jit(solution)/shard_map/ppermute | solution.py:285
  (45 shorter events, 14.0 us)
Async XLA Ops:
  0.0 5.3 %collective-permute-start = (bf16[96,640]{1,0:T(8,128)(2,1)}, bf16[96,640]{1,0:T(8,128)(2,1)S(1)}, u32[]{:S(2)}, u32[]{:S(2)}) collective-permute-start(bf16[96,640]{1,0:T(8,128)(2,1)} %refs_0_.1), channel_id=1, source_target_pairs={{0,8},{1,5},{2,10},{3,7},{8,16},{9,1},{10,18},{11,3},{16,24},{17,9... | collective-permute-start | bytes 368648 | tf_op jit(solution)/shard_map/ppermute | solution.py:91
  1.2 5.4 %collective-permute-start.4 = (bf16[96,640]{1,0:T(8,128)(2,1)}, bf16[96,640]{1,0:T(8,128)(2,1)S(1)}, u32[]{:S(2)}, u32[]{:S(2)}) collective-permute-start(bf16[96,640]{1,0:T(8,128)(2,1)} %refs_0_.1), channel_id=1, source_target_pairs={{0,4},{1,9},{2,6},{3,11},{8,0},{9,17},{10,2},{11,19},{16,8},{17,25... | collective-permute-start | bytes 368648 | tf_op jit(solution)/shard_map/ppermute | solution.py:91
  2.4 5.6 %collective-permute-start.10 = (bf16[96,640]{1,0:T(8,128)(2,1)S(1)}, bf16[96,640]{1,0:T(8,128)(2,1)S(1)}, u32[]{:S(2)}, u32[]{:S(2)}) collective-permute-start(bf16[96,640]{1,0:T(8,128)(2,1)S(1)} %get-tuple-element.10.refs_0_), channel_id=1, source_target_pairs={{0,4},{1,9},{2,6},{3,11},{8,0},{9,17},{10,2},{11,19},{16,8},{17,25... | collective-permute-start | bytes 368648 | tf_op jit(solution)/shard_map/ppermute | solution.py:91
  3.8 5.3 %collective-permute-start.13 = (bf16[96,640]{1,0:T(8,128)(2,1)S(1)}, bf16[96,640]{1,0:T(8,128)(2,1)S(1)}, u32[]{:S(2)}, u32[]{:S(2)}) collective-permute-start(bf16[96,640]{1,0:T(8,128)(2,1)S(1)} %get-tuple-element.11.refs_7_), channel_id=1, source_target_pairs={{0,8},{1,5},{2,10},{3,7},{8,16},{9,1},{10,18},{11,3},{16,24},{17,9... | collective-permute-start | bytes 368648 | tf_op jit(solution)/shard_map/ppermute | solution.py:91
  4.0 6.5 %collective-permute-start.16 = (bf16[96,640]{1,0:T(8,128)(2,1)S(1)}, bf16[96,640]{1,0:T(8,128)(2,1)S(1)}, u32[]{:S(2)}, u32[]{:S(2)}) collective-permute-start(bf16[96,640]{1,0:T(8,128)(2,1)S(1)} %get-tuple-element.11.refs_7_), channel_id=1, source_target_pairs={{0,4},{1,9},{2,6},{3,11},{8,0},{9,17},{10,2},{11,19},{16,8},{17,25... | collective-permute-start | bytes 368648 | tf_op jit(solution)/shard_map/ppermute | solution.py:91
  5.3 6.5 %collective-permute-start.7 = (bf16[96,640]{1,0:T(8,128)(2,1)S(1)}, bf16[96,640]{1,0:T(8,128)(2,1)S(1)}, u32[]{:S(2)}, u32[]{:S(2)}) collective-permute-start(bf16[96,640]{1,0:T(8,128)(2,1)S(1)} %get-tuple-element.10.refs_0_), channel_id=1, source_target_pairs={{0,8},{1,5},{2,10},{3,7},{8,16},{9,1},{10,18},{11,3},{16,24},{17,9... | collective-permute-start | bytes 368648 | tf_op jit(solution)/shard_map/ppermute | solution.py:91
  6.7 6.8 %collective-permute-start.1 = (bf16[96,640]{1,0:T(8,128)(2,1)S(1)}, bf16[96,640]{1,0:T(8,128)(2,1)S(1)}, u32[]{:S(2)}, u32[]{:S(2)}) collective-permute-start(bf16[96,640]{1,0:T(8,128)(2,1)S(1)} %collective-permute-done.refs_1_), channel_id=1, source_target_pairs={{0,8},{1,5},{2,10},{3,7},{8,16},{9,1},{10,18},{11,3},{16,24},{17,9... | collective-permute-start | bytes 368648 | tf_op jit(solution)/shard_map/ppermute | solution.py:91
  8.0 5.7 %collective-permute-start.5 = (bf16[96,640]{1,0:T(8,128)(2,1)S(1)}, bf16[96,640]{1,0:T(8,128)(2,1)S(1)}, u32[]{:S(2)}, u32[]{:S(2)}) collective-permute-start(bf16[96,640]{1,0:T(8,128)(2,1)S(1)} %collective-permute-done.4.refs_7_), channel_id=1, source_target_pairs={{0,4},{1,9},{2,6},{3,11},{8,0},{9,17},{10,2},{11,19},{16,8},{17,25... | collective-permute-start | bytes 368648 | tf_op jit(solution)/shard_map/ppermute | solution.py:91
  9.1 6.8 %collective-permute-start.11 = (bf16[96,640]{1,0:T(8,128)(2,1)S(1)}, bf16[96,640]{1,0:T(8,128)(2,1)S(1)}, u32[]{:S(2)}, u32[]{:S(2)}) collective-permute-start(bf16[96,640]{1,0:T(8,128)(2,1)S(1)} %collective-permute-done.10.refs_6_), channel_id=1, source_target_pairs={{0,4},{1,9},{2,6},{3,11},{8,0},{9,17},{10,2},{11,19},{16,8},{17,25... | collective-permute-start | bytes 368648 | tf_op jit(solution)/shard_map/ppermute | solution.py:91
  10.4 5.9 %collective-permute-start.14 = (bf16[96,640]{1,0:T(8,128)(2,1)S(1)}, bf16[96,640]{1,0:T(8,128)(2,1)S(1)}, u32[]{:S(2)}, u32[]{:S(2)}) collective-permute-start(bf16[96,640]{1,0:T(8,128)(2,1)S(1)} %collective-permute-done.13.refs_8_), channel_id=1, source_target_pairs={{0,8},{1,5},{2,10},{3,7},{8,16},{9,1},{10,18},{11,3},{16,24},{17,9... | collective-permute-start | bytes 368648 | tf_op jit(solution)/shard_map/ppermute | solution.py:91
  11.7 6.4 %collective-permute-start.17 = (bf16[96,640]{1,0:T(8,128)(2,1)S(1)}, bf16[96,640]{1,0:T(8,128)(2,1)S(1)}, u32[]{:S(2)}, u32[]{:S(2)}) collective-permute-start(bf16[96,640]{1,0:T(8,128)(2,1)S(1)} %collective-permute-done.16.refs_13_), channel_id=1, source_target_pairs={{0,4},{1,9},{2,6},{3,11},{8,0},{9,17},{10,2},{11,19},{16,8},{17,25... | collective-permute-start | bytes 368648 | tf_op jit(solution)/shard_map/ppermute | solution.py:91
  13.5 5.8 %collective-permute-start.2 = (bf16[96,640]{1,0:T(8,128)(2,1)S(1)}, bf16[96,640]{1,0:T(8,128)(2,1)S(1)}, u32[]{:S(2)}, u32[]{:S(2)}) collective-permute-start(bf16[96,640]{1,0:T(8,128)(2,1)S(1)} %collective-permute-done.1.refs_2_), channel_id=1, source_target_pairs={{0,8},{1,5},{2,10},{3,7},{8,16},{9,1},{10,18},{11,3},{16,24},{17,9... | collective-permute-start | bytes 368648 | tf_op jit(solution)/shard_map/ppermute | solution.py:91
  13.7 7.7 %collective-permute-start.8 = (bf16[96,640]{1,0:T(8,128)(2,1)S(1)}, bf16[96,640]{1,0:T(8,128)(2,1)S(1)}, u32[]{:S(2)}, u32[]{:S(2)}) collective-permute-start(bf16[96,640]{1,0:T(8,128)(2,1)S(1)} %collective-permute-done.7.refs_1_), channel_id=1, source_target_pairs={{0,8},{1,5},{2,10},{3,7},{8,16},{9,1},{10,18},{11,3},{16,24},{17,9... | collective-permute-start | bytes 368648 | tf_op jit(solution)/shard_map/ppermute | solution.py:91
  15.9 6.8 %collective-permute-start.6 = (bf16[96,640]{1,0:T(8,128)(2,1)S(1)}, bf16[96,640]{1,0:T(8,128)(2,1)S(1)}, u32[]{:S(2)}, u32[]{:S(2)}) collective-permute-start(bf16[96,640]{1,0:T(8,128)(2,1)S(1)} %collective-permute-done.5.refs_6_), channel_id=1, source_target_pairs={{0,4},{1,9},{2,6},{3,11},{8,0},{9,17},{10,2},{11,19},{16,8},{17,25... | collective-permute-start | bytes 368648 | tf_op jit(solution)/shard_map/ppermute | solution.py:91
  16.3 6.9 %collective-permute-start.12 = (bf16[96,640]{1,0:T(8,128)(2,1)S(1)}, bf16[96,640]{1,0:T(8,128)(2,1)S(1)}, u32[]{:S(2)}, u32[]{:S(2)}) collective-permute-start(bf16[96,640]{1,0:T(8,128)(2,1)S(1)} %collective-permute-done.11.refs_5_), channel_id=1, source_target_pairs={{0,4},{1,9},{2,6},{3,11},{8,0},{9,17},{10,2},{11,19},{16,8},{17,25... | collective-permute-start | bytes 368648 | tf_op jit(solution)/shard_map/ppermute | solution.py:91
  18.1 6.2 %collective-permute-start.15 = (bf16[96,640]{1,0:T(8,128)(2,1)S(1)}, bf16[96,640]{1,0:T(8,128)(2,1)S(1)}, u32[]{:S(2)}, u32[]{:S(2)}) collective-permute-start(bf16[96,640]{1,0:T(8,128)(2,1)S(1)} %collective-permute-done.14.refs_9_), channel_id=1, source_target_pairs={{0,8},{1,5},{2,10},{3,7},{8,16},{9,1},{10,18},{11,3},{16,24},{17,9... | collective-permute-start | bytes 368648 | tf_op jit(solution)/shard_map/ppermute | solution.py:91
  19.3 6.5 %collective-permute-start.3 = (bf16[96,640]{1,0:T(8,128)(2,1)S(1)}, bf16[96,640]{1,0:T(8,128)(2,1)S(1)}, u32[]{:S(2)}, u32[]{:S(2)}) collective-permute-start(bf16[96,640]{1,0:T(8,128)(2,1)S(1)} %collective-permute-done.2.refs_3_), channel_id=1, source_target_pairs={{0,8},{1,5},{2,10},{3,7},{8,16},{9,1},{10,18},{11,3},{16,24},{17,9... | collective-permute-start | bytes 368648 | tf_op jit(solution)/shard_map/ppermute | solution.py:91
  21.4 5.4 %collective-permute-start.18 = (bf16[96,640]{1,0:T(8,128)(2,1)S(1)}, bf16[96,640]{1,0:T(8,128)(2,1)S(1)}, u32[]{:S(2)}, u32[]{:S(2)}) collective-permute-start(bf16[96,640]{1,0:T(8,128)(2,1)S(1)} %collective-permute-done.17.refs_12_), channel_id=1, source_target_pairs={{0,4},{1,9},{2,6},{3,11},{8,0},{9,17},{10,2},{11,19},{16,8},{17,25... | collective-permute-start | bytes 368648 | tf_op jit(solution)/shard_map/ppermute | solution.py:91
  22.7 5.3 %collective-permute-start.9 = (bf16[96,640]{1,0:T(8,128)(2,1)S(1)}, bf16[96,640]{1,0:T(8,128)(2,1)S(1)}, u32[]{:S(2)}, u32[]{:S(2)}) collective-permute-start(bf16[96,640]{1,0:T(8,128)(2,1)S(1)} %collective-permute-done.8.refs_2_), channel_id=1, source_target_pairs={{0,8},{1,5},{2,10},{3,7},{8,16},{9,1},{10,18},{11,3},{16,24},{17,9... | collective-permute-start | bytes 368648 | tf_op jit(solution)/shard_map/ppermute | solution.py:91
  23.2 9.6 %collective-permute-start.19 = (bf16[96,640]{1,0:T(8,128)(2,1)S(1)}, bf16[96,640]{1,0:T(8,128)(2,1)S(1)}, u32[]{:S(2)}, u32[]{:S(2)}) collective-permute-start(bf16[96,640]{1,0:T(8,128)(2,1)S(1)} %collective-permute-done.12.refs_4_), channel_id=1, source_target_pairs={{0,4},{1,9},{2,6},{3,11},{8,0},{9,17},{10,2},{11,19},{16,8},{17,25... | collective-permute-start | bytes 368648 | tf_op jit(solution)/shard_map/ppermute | solution.py:91
  24.3 8.5 %collective-permute-start.20 = (bf16[96,640]{1,0:T(8,128)(2,1)S(1)}, bf16[96,640]{1,0:T(8,128)(2,1)S(1)}, u32[]{:S(2)}, u32[]{:S(2)}) collective-permute-start(bf16[96,640]{1,0:T(8,128)(2,1)S(1)} %collective-permute-done.15.refs_10_), channel_id=1, source_target_pairs={{0,8},{1,5},{2,10},{3,7},{8,16},{9,1},{10,18},{11,3},{16,24},{17,9... | collective-permute-start | bytes 368648 | tf_op jit(solution)/shard_map/ppermute | solution.py:91
  40.0 7.1 %collective-permute-start.24 = (bf16[96,640]{1,0:T(8,128)(2,1)S(1)}, bf16[96,640]{1,0:T(8,128)(2,1)S(1)}, u32[]{:S(2)}, u32[]{:S(2)}) collective-permute-start(bf16[96,640]{1,0:T(8,128)(2,1)S(1)} %get-tuple-element.17.refs_1_), channel_id=1, source_target_pairs={{0,2},{1,3},{2,0},{3,1},{4,6},{5,7},{6,4},{7,5},{8,10},{9,11},{10,... | collective-permute-start | bytes 368648 | tf_op jit(solution)/shard_map/ppermute | solution.py:275
  47.2 8.4 %collective-permute-start.23 = (bf16[96,640]{1,0:T(8,128)(2,1)S(1)}, bf16[96,640]{1,0:T(8,128)(2,1)S(1)}, u32[]{:S(2)}, u32[]{:S(2)}) collective-permute-start(bf16[96,640]{1,0:T(8,128)(2,1)S(1)} %get-tuple-element.15), channel_id=1, source_target_pairs={{0,16},{1,20},{2,24},{3,28},{4,0},{5,4},{6,8},{7,12},{8,9},{9,13},... | collective-permute-start | bytes 368648 | tf_op jit(solution)/shard_map/ppermute | solution.py:285
  51.3 8.4 %collective-permute-start.25 = (bf16[96,640]{1,0:T(8,128)(2,1)S(1)}, bf16[96,640]{1,0:T(8,128)(2,1)S(1)}, u32[]{:S(2)}, u32[]{:S(2)}) collective-permute-start(bf16[96,640]{1,0:T(8,128)(2,1)S(1)} %get-tuple-element.16), channel_id=1, source_target_pairs={{0,0},{1,4},{2,8},{3,12},{4,16},{5,20},{6,24},{7,28},{8,25},{9,29}... | collective-permute-start | bytes 368648 | tf_op jit(solution)/shard_map/ppermute | solution.py:285
  (5 other events, 17.4 us)

commit v13 on v12

--- a/solution.py
+++ b/solution.py
@@ -221,6 +221,11 @@
     refs[-1][...] = jnp.dot(rows, w_ref[...], preferred_element_type=jnp.float32).astype(refs[-1].dtype)
 
 
+def sum_kernel(rows, kept_ref, from_core_ref, from_x_ref, total_ref):
+    total = kept_ref[rows] + from_core_ref[1, rows].astype(jnp.float32) + from_x_ref[...].astype(jnp.float32)
+    total_ref[...] = total.astype(total_ref.dtype)
+
+
 def call(kernel, scalars, operands, outs, flops, after=()):
     vmem = pl.BlockSpec(memory_space=pltpu.VMEM)
     return pl.pallas_call(
@@ -281,8 +286,10 @@
             for h in range(4):
                 to = PATTERNS[(slot ^ (f & 1)) + 2 * (h >> 1)][f >> 1]
                 pairs.append((4 * f + h, 4 * (2 * to + (h & 1)) + (f >> 1)))
-        total = kept[part] + from_core[1, part].astype(f32) + from_x[slot].astype(f32)
-        arrived.append(lax.ppermute(total.astype(bf16), ("frames", "heads"), pairs))
+        (total,) = call(
+            functools.partial(sum_kernel, part), (), [kept, from_core, from_x[slot]], [((ROWS, cols), bf16)], 0
+        )
+        arrived.append(lax.ppermute(total, ("frames", "heads"), pairs))
     patterns = [[p[source] for p in PATTERNS].index(to) for source in range(4) for to in range(4)]
     straight = look_up(patterns, 4 * head + z) & 1 == 0
     low, high = arrived

time: 61 us -> 59.7 us (0.979)
  waiting for transfers between devices: 18.1 us -> 15.7 us
  starting transfers between devices: 29.3 us -> 30.1 us
    ppermute x2, waiting for transfers between devices: 4.24 us -> 1.61 us  [on_device_ring(): lax.ppermute(block, 'heads', [(h, h ^ 2) for h in range(4)])]
    ppermute x2, starting transfers between devices: 6.65 us -> 7.42 us  [on_device_ring(): arrived.append(lax.ppermute(total, ('frames', 'heads'), pairs))]
    pallas_call x6 -> x8, Pallas kernels: 10.1 us -> 10.2 us  [call(): pl.pallas_call(kernel, out_shape=[jax.ShapeDtypeStruct(shape, dtype) for...]
  transfers between devices with their start and end apart: 26 -> 26, of which waited for: 15 -> 14; matrix products, arithmetic and copies ran while one was open for 0% -> 0% of each run, Pallas kernels for 13% -> 14%
where the time goes in v13:
time: 59.7 us; the launch traced here: 58.9 us
  starting transfers between devices  30.1 us (50%)
  waiting for transfers between devices  15.7 us (26%)
  Pallas kernels  10.2 us (17%)
  local copies, waits for them, and re-layouts  1.94 us (3%)
  other arithmetic  0.79 us (1%)
    ppermute x21, starting transfers between devices, hop(): return lax.ppermute(x, ('frames', 'heads'), pairs)  17.9 us
    pallas_call x8, Pallas kernels, call(): pl.pallas_call(kernel, out_shape=[jax.ShapeDtypeStruct(shape, dtype) for...  10.2 us
    ppermute x21, waiting for transfers between devices, hop(): return lax.ppermute(x, ('frames', 'heads'), pairs)  8.01 us
    ppermute x2, starting transfers between devices, on_device_ring(): arrived.append(lax.ppermute(total, ('frames', 'heads'), pairs))  7.42 us
    ppermute x2, waiting for transfers between devices, on_device_ring(): arrived.append(lax.ppermute(total, ('frames', 'heads'), pairs))  6.13 us
    ppermute x1, starting transfers between devices, on_device_ring(): from_core = lax.ppermute(given, 'heads', [(h, h ^ 1) for h in range(4)])  3.17 us
    unnamed x6, local copies, waits for them, and re-layouts  1.85 us
    ppermute x2, waiting for transfers between devices, on_device_ring(): lax.ppermute(block, 'heads', [(h, h ^ 2) for h in range(4)])  1.61 us
  transfers between devices with their start and end apart: 26, of which 14 were waited for; matrix products, arithmetic and copies ran while one was open for 0% of the time, Pallas kernels for 14%

profile of v13, /device:TPU:3, one launch (start us, length us, event | category | flops | bytes accessed | tf_op | source)
XLA Modules:
  0.0 58.9 jit_solution(1903311417444841205)
XLA Ops:
  0.0 1.2 %collective-permute-start = (bf16[96,640]{1,0:T(8,128)(2,1)}, bf16[96,640]{1,0:T(8,128)(2,1)S(1)}, u32[]{:S(2)}, u32[]{:S(2)}) collective-permute-start(bf16[96,640]{1,0:T(8,128)(2,1)} %refs_0_.1), channel_id=1, source_target_pairs={{0,8},{1,5},{2,10},{3,7},{8,16},{9,1},{10,18},{11,3},{16,24},{17,9... | collective-permute-start | bytes 368648 | tf_op jit(solution)/shard_map/ppermute | solution.py:91
  2.4 1.3 %collective-permute-start.10 = (bf16[96,640]{1,0:T(8,128)(2,1)S(1)}, bf16[96,640]{1,0:T(8,128)(2,1)S(1)}, u32[]{:S(2)}, u32[]{:S(2)}) collective-permute-start(bf16[96,640]{1,0:T(8,128)(2,1)S(1)} %get-tuple-element.10.refs_0_), channel_id=1, source_target_pairs={{0,4},{1,9},{2,6},{3,11},{8,0},{9,17},{10,2},{11,19},{16,8},{17,25... | collective-permute-start | bytes 368648 | tf_op jit(solution)/shard_map/ppermute | solution.py:91
  4.0 1.3 %collective-permute-start.16 = (bf16[96,640]{1,0:T(8,128)(2,1)S(1)}, bf16[96,640]{1,0:T(8,128)(2,1)S(1)}, u32[]{:S(2)}, u32[]{:S(2)}) collective-permute-start(bf16[96,640]{1,0:T(8,128)(2,1)S(1)} %get-tuple-element.11.refs_7_), channel_id=1, source_target_pairs={{0,4},{1,9},{2,6},{3,11},{8,0},{9,17},{10,2},{11,19},{16,8},{17,25... | collective-permute-start | bytes 368648 | tf_op jit(solution)/shard_map/ppermute | solution.py:91
  5.5 1.2 %collective-permute-done.4.refs_7_ = bf16[96,640]{1,0:T(8,128)(2,1)S(1)} collective-permute-done((bf16[96,640]{1,0:T(8,128)(2,1)}, bf16[96,640]{1,0:T(8,128)(2,1)S(1)}, u32[]{:S(2)}, u32[]{:S(2)}) %collective-permute-start.4) | collective-permute-done | bytes 122912 | tf_op jit(solution)/shard_map/ppermute | solution.py:91
  9.1 1.3 %collective-permute-start.11 = (bf16[96,640]{1,0:T(8,128)(2,1)S(1)}, bf16[96,640]{1,0:T(8,128)(2,1)S(1)}, u32[]{:S(2)}, u32[]{:S(2)}) collective-permute-start(bf16[96,640]{1,0:T(8,128)(2,1)S(1)} %collective-permute-done.10.refs_6_), channel_id=1, source_target_pairs={{0,4},{1,9},{2,6},{3,11},{8,0},{9,17},{10,2},{11,19},{16,8},{17,25... | collective-permute-start | bytes 368648 | tf_op jit(solution)/shard_map/ppermute | solution.py:91
  11.7 1.3 %collective-permute-start.17 = (bf16[96,640]{1,0:T(8,128)(2,1)S(1)}, bf16[96,640]{1,0:T(8,128)(2,1)S(1)}, u32[]{:S(2)}, u32[]{:S(2)}) collective-permute-start(bf16[96,640]{1,0:T(8,128)(2,1)S(1)} %collective-permute-done.16.refs_13_), channel_id=1, source_target_pairs={{0,4},{1,9},{2,6},{3,11},{8,0},{9,17},{10,2},{11,19},{16,8},{17,25... | collective-permute-start | bytes 368648 | tf_op jit(solution)/shard_map/ppermute | solution.py:91
  13.7 1.2 %collective-permute-start.8 = (bf16[96,640]{1,0:T(8,128)(2,1)S(1)}, bf16[96,640]{1,0:T(8,128)(2,1)S(1)}, u32[]{:S(2)}, u32[]{:S(2)}) collective-permute-start(bf16[96,640]{1,0:T(8,128)(2,1)S(1)} %collective-permute-done.7.refs_1_), channel_id=1, source_target_pairs={{0,8},{1,5},{2,10},{3,7},{8,16},{9,1},{10,18},{11,3},{16,24},{17,9... | collective-permute-start | bytes 368648 | tf_op jit(solution)/shard_map/ppermute | solution.py:91
  16.3 1.3 %collective-permute-start.12 = (bf16[96,640]{1,0:T(8,128)(2,1)S(1)}, bf16[96,640]{1,0:T(8,128)(2,1)S(1)}, u32[]{:S(2)}, u32[]{:S(2)}) collective-permute-start(bf16[96,640]{1,0:T(8,128)(2,1)S(1)} %collective-permute-done.11.refs_5_), channel_id=1, source_target_pairs={{0,4},{1,9},{2,6},{3,11},{8,0},{9,17},{10,2},{11,19},{16,8},{17,25... | collective-permute-start | bytes 368648 | tf_op jit(solution)/shard_map/ppermute | solution.py:91
  18.1 1.2 %collective-permute-start.15 = (bf16[96,640]{1,0:T(8,128)(2,1)S(1)}, bf16[96,640]{1,0:T(8,128)(2,1)S(1)}, u32[]{:S(2)}, u32[]{:S(2)}) collective-permute-start(bf16[96,640]{1,0:T(8,128)(2,1)S(1)} %collective-permute-done.14.refs_9_), channel_id=1, source_target_pairs={{0,8},{1,5},{2,10},{3,7},{8,16},{9,1},{10,18},{11,3},{16,24},{17,9... | collective-permute-start | bytes 368648 | tf_op jit(solution)/shard_map/ppermute | solution.py:91
  19.3 1.3 %collective-permute-start.3 = (bf16[96,640]{1,0:T(8,128)(2,1)S(1)}, bf16[96,640]{1,0:T(8,128)(2,1)S(1)}, u32[]{:S(2)}, u32[]{:S(2)}) collective-permute-start(bf16[96,640]{1,0:T(8,128)(2,1)S(1)} %collective-permute-done.2.refs_3_), channel_id=1, source_target_pairs={{0,8},{1,5},{2,10},{3,7},{8,16},{9,1},{10,18},{11,3},{16,24},{17,9... | collective-permute-start | bytes 368648 | tf_op jit(solution)/shard_map/ppermute | solution.py:91
  21.4 1.3 %collective-permute-start.18 = (bf16[96,640]{1,0:T(8,128)(2,1)S(1)}, bf16[96,640]{1,0:T(8,128)(2,1)S(1)}, u32[]{:S(2)}, u32[]{:S(2)}) collective-permute-start(bf16[96,640]{1,0:T(8,128)(2,1)S(1)} %collective-permute-done.17.refs_12_), channel_id=1, source_target_pairs={{0,4},{1,9},{2,6},{3,11},{8,0},{9,17},{10,2},{11,19},{16,8},{17,25... | collective-permute-start | bytes 368648 | tf_op jit(solution)/shard_map/ppermute | solution.py:91
  24.7 1.2 %collective-permute-done.3.refs_4_ = bf16[96,640]{1,0:T(8,128)(2,1)S(1)} collective-permute-done((bf16[96,640]{1,0:T(8,128)(2,1)S(1)}, bf16[96,640]{1,0:T(8,128)(2,1)S(1)}, u32[]{:S(2)}, u32[]{:S(2)}) %collective-permute-start.3) | collective-permute-done | bytes 122912 | tf_op jit(solution)/shard_map/ppermute | solution.py:91
  26.8 1.2 %collective-permute-done.9.refs_3_ = bf16[96,640]{1,0:T(8,128)(2,1)S(1)} collective-permute-done((bf16[96,640]{1,0:T(8,128)(2,1)S(1)}, bf16[96,640]{1,0:T(8,128)(2,1)S(1)}, u32[]{:S(2)}, u32[]{:S(2)}) %collective-permute-start.9) | collective-permute-done | bytes 122912 | tf_op jit(solution)/shard_map/ppermute | solution.py:91
  28.0 4.8 %shard_map.39 = (f32[5,8,96,128]{3,2,1,0:T(8,128)S(1)}, f32[5,8,96,128]{3,2,1,0:T(8,128)S(1)}, f32[5,8,96,128]{3,2,1,0:T(8,128)S(1)}) custom-call(s32[5]{0:T(128)S(1)} %stack.23.at_ref, bf16[8,96,640]{2,1,0:T(8,128)(2,1)S(1)} %shard_map.37.rows_ref, bf16[96,640]{1,0:T(8,128)(2,1)S(1)} %get-tuple-element.10.refs_0_, ...), custom_call_target="tpu_custom_call" | custom-call | flops 1321205760 | tf_op jit(solution)/shard_map/pallas_call | solution.py:231
  32.8 2.1 %shard_map.40 = bf16[384,640]{1,0:T(8,128)(2,1)S(1)} custom-call(s32[5]{0:T(128)S(1)} %stack.23.at_ref, bf16[8,96,640]{2,1,0:T(8,128)(2,1)S(1)} %shard_map.37.rows_ref, f32[5,8,96,128]{3,2,1,0:T(8,128)S(1)} %get-tuple-element.12.mixed_ref, f32[5,8,96,128]{3,2,1,0:T(8,128)S(1)} %get-tuple-element.13.sum_ref, f32[5,8,96,128]{3,2,1,0:T(8,128)S(1)} %get-tuple-element.14.top_ref, ...), custom_call_target="tpu_custom_call" | custom-call | flops 314572800 | tf_op jit(solution)/shard_map/pallas_call | solution.py:231
  34.9 3.2 %collective-permute-start.21 = (bf16[2,192,640]{2,1,0:T(8,128)(2,1)S(1)}, bf16[2,192,640]{2,1,0:T(8,128)(2,1)S(1)}, u32[]{:S(2)}, u32[]{:S(2)}) collective-permute-start(bf16[2,192,640]{2,1,0:T(8,128)(2,1)S(1)} %bitcast.16), channel_id=1, source_target_pairs={{0,1},{1,0},{2,3},{3,2},{4,5},{5,4},{6,7},{7,6},{8,9},{9,8},{10,11... | collective-permute-start | bytes 1474568 | tf_op jit(solution)/shard_map/ppermute | solution.py:276
  38.1 1.6 %shard_map.41 = f32[192,640]{1,0:T(8,128)S(1)} custom-call(s32[5]{0:T(128)S(1)} %stack.23.at_ref, bf16[8,96,640]{2,1,0:T(8,128)(2,1)S(1)} %shard_map.37.rows_ref, f32[5,8,96,128]{3,2,1,0:T(8,128)S(1)} %get-tuple-element.12.mixed_ref, f32[5,8,96,128]{3,2,1,0:T(8,128)S(1)} %get-tuple-element.13.sum_ref, f32[5,8,96,128]{3,2,1,0:T(8,128)S(1)} %get-tuple-element.14.top_ref, ...), custom_call_target="tpu_custom_call" | custom-call | flops 314572800 | tf_op jit(solution)/shard_map/pallas_call | solution.py:231
  40.0 1.2 %collective-permute-start.22 = (bf16[96,640]{1,0:T(8,128)(2,1)S(1)}, bf16[96,640]{1,0:T(8,128)(2,1)S(1)}, u32[]{:S(2)}, u32[]{:S(2)}) collective-permute-start(bf16[96,640]{1,0:T(8,128)(2,1)S(1)} %get-tuple-element.16.refs_0_), channel_id=1, source_target_pairs={{0,2},{1,3},{2,0},{3,1},{4,6},{5,7},{6,4},{7,5},{8,10},{9,11},{10,... | collective-permute-start | bytes 368648 | tf_op jit(solution)/shard_map/ppermute | solution.py:280
  41.3 1.6 %shard_map.42.kept_ref = f32[192,640]{1,0:T(8,128)S(1)} custom-call(s32[5]{0:T(128)S(1)} %stack.23.at_ref, bf16[8,96,640]{2,1,0:T(8,128)(2,1)S(1)} %shard_map.37.rows_ref, f32[5,8,96,128]{3,2,1,0:T(8,128)S(1)} %get-tuple-element.12.mixed_ref, f32[5,8,96,128]{3,2,1,0:T(8,128)S(1)} %get-tuple-element.13.sum_ref, ...), custom_call_target="tpu_custom_call" | custom-call | flops 314572800 | tf_op jit(solution)/shard_map/pallas_call | solution.py:231
  42.9 1.6 %collective-permute-done.24.from_x_ref = bf16[96,640]{1,0:T(8,128)(2,1)S(1)} collective-permute-done((bf16[96,640]{1,0:T(8,128)(2,1)S(1)}, bf16[96,640]{1,0:T(8,128)(2,1)S(1)}, u32[]{:S(2)}, u32[]{:S(2)}) %collective-permute-start.24) | collective-permute-done | bytes 122912 | tf_op jit(solution)/shard_map/ppermute | solution.py:280
  44.5 6.0 %collective-permute-start.25 = (bf16[96,640]{1,0:T(8,128)(2,1)S(1)}, bf16[96,640]{1,0:T(8,128)(2,1)S(1)}, u32[]{:S(2)}, u32[]{:S(2)}) collective-permute-start(bf16[96,640]{1,0:T(8,128)(2,1)S(1)} %shard_map.44), channel_id=1, source_target_pairs={{0,0},{1,4},{2,8},{3,12},{4,16},{5,20},{6,24},{7,28},{8,25},{9,29}... | collective-permute-start | bytes 368648 | tf_op jit(solution)/shard_map/ppermute | solution.py:292
  50.6 1.4 %collective-permute-start.23 = (bf16[96,640]{1,0:T(8,128)(2,1)S(1)}, bf16[96,640]{1,0:T(8,128)(2,1)S(1)}, u32[]{:S(2)}, u32[]{:S(2)}) collective-permute-start(bf16[96,640]{1,0:T(8,128)(2,1)S(1)} %shard_map.43), channel_id=1, source_target_pairs={{0,16},{1,20},{2,24},{3,28},{4,0},{5,4},{6,8},{7,12},{8,9},{9,13},... | collective-permute-start | bytes 368648 | tf_op jit(solution)/shard_map/ppermute | solution.py:292
  52.0 3.2 %collective-permute-done.25 = bf16[96,640]{1,0:T(8,128)(2,1)S(1)} collective-permute-done((bf16[96,640]{1,0:T(8,128)(2,1)S(1)}, bf16[96,640]{1,0:T(8,128)(2,1)S(1)}, u32[]{:S(2)}, u32[]{:S(2)}) %collective-permute-start.25) | collective-permute-done | bytes 122912 | tf_op jit(solution)/shard_map/ppermute | solution.py:292
  55.2 2.9 %collective-permute-done.23 = bf16[96,640]{1,0:T(8,128)(2,1)S(1)} collective-permute-done((bf16[96,640]{1,0:T(8,128)(2,1)S(1)}, bf16[96,640]{1,0:T(8,128)(2,1)S(1)}, u32[]{:S(2)}, u32[]{:S(2)}) %collective-permute-start.23) | collective-permute-done | bytes 122912 | tf_op jit(solution)/shard_map/ppermute | solution.py:292
  (46 shorter events, 12.8 us)
Async XLA Ops:
  0.0 5.3 %collective-permute-start = (bf16[96,640]{1,0:T(8,128)(2,1)}, bf16[96,640]{1,0:T(8,128)(2,1)S(1)}, u32[]{:S(2)}, u32[]{:S(2)}) collective-permute-start(bf16[96,640]{1,0:T(8,128)(2,1)} %refs_0_.1), channel_id=1, source_target_pairs={{0,8},{1,5},{2,10},{3,7},{8,16},{9,1},{10,18},{11,3},{16,24},{17,9... | collective-permute-start | bytes 368648 | tf_op jit(solution)/shard_map/ppermute | solution.py:91
  1.2 5.4 %collective-permute-start.4 = (bf16[96,640]{1,0:T(8,128)(2,1)}, bf16[96,640]{1,0:T(8,128)(2,1)S(1)}, u32[]{:S(2)}, u32[]{:S(2)}) collective-permute-start(bf16[96,640]{1,0:T(8,128)(2,1)} %refs_0_.1), channel_id=1, source_target_pairs={{0,4},{1,9},{2,6},{3,11},{8,0},{9,17},{10,2},{11,19},{16,8},{17,25... | collective-permute-start | bytes 368648 | tf_op jit(solution)/shard_map/ppermute | solution.py:91
  2.4 5.6 %collective-permute-start.10 = (bf16[96,640]{1,0:T(8,128)(2,1)S(1)}, bf16[96,640]{1,0:T(8,128)(2,1)S(1)}, u32[]{:S(2)}, u32[]{:S(2)}) collective-permute-start(bf16[96,640]{1,0:T(8,128)(2,1)S(1)} %get-tuple-element.10.refs_0_), channel_id=1, source_target_pairs={{0,4},{1,9},{2,6},{3,11},{8,0},{9,17},{10,2},{11,19},{16,8},{17,25... | collective-permute-start | bytes 368648 | tf_op jit(solution)/shard_map/ppermute | solution.py:91
  3.8 5.3 %collective-permute-start.13 = (bf16[96,640]{1,0:T(8,128)(2,1)S(1)}, bf16[96,640]{1,0:T(8,128)(2,1)S(1)}, u32[]{:S(2)}, u32[]{:S(2)}) collective-permute-start(bf16[96,640]{1,0:T(8,128)(2,1)S(1)} %get-tuple-element.11.refs_7_), channel_id=1, source_target_pairs={{0,8},{1,5},{2,10},{3,7},{8,16},{9,1},{10,18},{11,3},{16,24},{17,9... | collective-permute-start | bytes 368648 | tf_op jit(solution)/shard_map/ppermute | solution.py:91
  4.0 6.5 %collective-permute-start.16 = (bf16[96,640]{1,0:T(8,128)(2,1)S(1)}, bf16[96,640]{1,0:T(8,128)(2,1)S(1)}, u32[]{:S(2)}, u32[]{:S(2)}) collective-permute-start(bf16[96,640]{1,0:T(8,128)(2,1)S(1)} %get-tuple-element.11.refs_7_), channel_id=1, source_target_pairs={{0,4},{1,9},{2,6},{3,11},{8,0},{9,17},{10,2},{11,19},{16,8},{17,25... | collective-permute-start | bytes 368648 | tf_op jit(solution)/shard_map/ppermute | solution.py:91
  5.3 6.5 %collective-permute-start.7 = (bf16[96,640]{1,0:T(8,128)(2,1)S(1)}, bf16[96,640]{1,0:T(8,128)(2,1)S(1)}, u32[]{:S(2)}, u32[]{:S(2)}) collective-permute-start(bf16[96,640]{1,0:T(8,128)(2,1)S(1)} %get-tuple-element.10.refs_0_), channel_id=1, source_target_pairs={{0,8},{1,5},{2,10},{3,7},{8,16},{9,1},{10,18},{11,3},{16,24},{17,9... | collective-permute-start | bytes 368648 | tf_op jit(solution)/shard_map/ppermute | solution.py:91
  6.7 6.8 %collective-permute-start.1 = (bf16[96,640]{1,0:T(8,128)(2,1)S(1)}, bf16[96,640]{1,0:T(8,128)(2,1)S(1)}, u32[]{:S(2)}, u32[]{:S(2)}) collective-permute-start(bf16[96,640]{1,0:T(8,128)(2,1)S(1)} %collective-permute-done.refs_1_), channel_id=1, source_target_pairs={{0,8},{1,5},{2,10},{3,7},{8,16},{9,1},{10,18},{11,3},{16,24},{17,9... | collective-permute-start | bytes 368648 | tf_op jit(solution)/shard_map/ppermute | solution.py:91
  8.0 5.7 %collective-permute-start.5 = (bf16[96,640]{1,0:T(8,128)(2,1)S(1)}, bf16[96,640]{1,0:T(8,128)(2,1)S(1)}, u32[]{:S(2)}, u32[]{:S(2)}) collective-permute-start(bf16[96,640]{1,0:T(8,128)(2,1)S(1)} %collective-permute-done.4.refs_7_), channel_id=1, source_target_pairs={{0,4},{1,9},{2,6},{3,11},{8,0},{9,17},{10,2},{11,19},{16,8},{17,25... | collective-permute-start | bytes 368648 | tf_op jit(solution)/shard_map/ppermute | solution.py:91
  9.1 6.8 %collective-permute-start.11 = (bf16[96,640]{1,0:T(8,128)(2,1)S(1)}, bf16[96,640]{1,0:T(8,128)(2,1)S(1)}, u32[]{:S(2)}, u32[]{:S(2)}) collective-permute-start(bf16[96,640]{1,0:T(8,128)(2,1)S(1)} %collective-permute-done.10.refs_6_), channel_id=1, source_target_pairs={{0,4},{1,9},{2,6},{3,11},{8,0},{9,17},{10,2},{11,19},{16,8},{17,25... | collective-permute-start | bytes 368648 | tf_op jit(solution)/shard_map/ppermute | solution.py:91
  10.4 5.9 %collective-permute-start.14 = (bf16[96,640]{1,0:T(8,128)(2,1)S(1)}, bf16[96,640]{1,0:T(8,128)(2,1)S(1)}, u32[]{:S(2)}, u32[]{:S(2)}) collective-permute-start(bf16[96,640]{1,0:T(8,128)(2,1)S(1)} %collective-permute-done.13.refs_8_), channel_id=1, source_target_pairs={{0,8},{1,5},{2,10},{3,7},{8,16},{9,1},{10,18},{11,3},{16,24},{17,9... | collective-permute-start | bytes 368648 | tf_op jit(solution)/shard_map/ppermute | solution.py:91
  11.7 6.4 %collective-permute-start.17 = (bf16[96,640]{1,0:T(8,128)(2,1)S(1)}, bf16[96,640]{1,0:T(8,128)(2,1)S(1)}, u32[]{:S(2)}, u32[]{:S(2)}) collective-permute-start(bf16[96,640]{1,0:T(8,128)(2,1)S(1)} %collective-permute-done.16.refs_13_), channel_id=1, source_target_pairs={{0,4},{1,9},{2,6},{3,11},{8,0},{9,17},{10,2},{11,19},{16,8},{17,25... | collective-permute-start | bytes 368648 | tf_op jit(solution)/shard_map/ppermute | solution.py:91
  13.5 5.8 %collective-permute-start.2 = (bf16[96,640]{1,0:T(8,128)(2,1)S(1)}, bf16[96,640]{1,0:T(8,128)(2,1)S(1)}, u32[]{:S(2)}, u32[]{:S(2)}) collective-permute-start(bf16[96,640]{1,0:T(8,128)(2,1)S(1)} %collective-permute-done.1.refs_2_), channel_id=1, source_target_pairs={{0,8},{1,5},{2,10},{3,7},{8,16},{9,1},{10,18},{11,3},{16,24},{17,9... | collective-permute-start | bytes 368648 | tf_op jit(solution)/shard_map/ppermute | solution.py:91
  13.7 7.7 %collective-permute-start.8 = (bf16[96,640]{1,0:T(8,128)(2,1)S(1)}, bf16[96,640]{1,0:T(8,128)(2,1)S(1)}, u32[]{:S(2)}, u32[]{:S(2)}) collective-permute-start(bf16[96,640]{1,0:T(8,128)(2,1)S(1)} %collective-permute-done.7.refs_1_), channel_id=1, source_target_pairs={{0,8},{1,5},{2,10},{3,7},{8,16},{9,1},{10,18},{11,3},{16,24},{17,9... | collective-permute-start | bytes 368648 | tf_op jit(solution)/shard_map/ppermute | solution.py:91
  15.9 6.8 %collective-permute-start.6 = (bf16[96,640]{1,0:T(8,128)(2,1)S(1)}, bf16[96,640]{1,0:T(8,128)(2,1)S(1)}, u32[]{:S(2)}, u32[]{:S(2)}) collective-permute-start(bf16[96,640]{1,0:T(8,128)(2,1)S(1)} %collective-permute-done.5.refs_6_), channel_id=1, source_target_pairs={{0,4},{1,9},{2,6},{3,11},{8,0},{9,17},{10,2},{11,19},{16,8},{17,25... | collective-permute-start | bytes 368648 | tf_op jit(solution)/shard_map/ppermute | solution.py:91
  16.3 6.9 %collective-permute-start.12 = (bf16[96,640]{1,0:T(8,128)(2,1)S(1)}, bf16[96,640]{1,0:T(8,128)(2,1)S(1)}, u32[]{:S(2)}, u32[]{:S(2)}) collective-permute-start(bf16[96,640]{1,0:T(8,128)(2,1)S(1)} %collective-permute-done.11.refs_5_), channel_id=1, source_target_pairs={{0,4},{1,9},{2,6},{3,11},{8,0},{9,17},{10,2},{11,19},{16,8},{17,25... | collective-permute-start | bytes 368648 | tf_op jit(solution)/shard_map/ppermute | solution.py:91
  18.1 6.2 %collective-permute-start.15 = (bf16[96,640]{1,0:T(8,128)(2,1)S(1)}, bf16[96,640]{1,0:T(8,128)(2,1)S(1)}, u32[]{:S(2)}, u32[]{:S(2)}) collective-permute-start(bf16[96,640]{1,0:T(8,128)(2,1)S(1)} %collective-permute-done.14.refs_9_), channel_id=1, source_target_pairs={{0,8},{1,5},{2,10},{3,7},{8,16},{9,1},{10,18},{11,3},{16,24},{17,9... | collective-permute-start | bytes 368648 | tf_op jit(solution)/shard_map/ppermute | solution.py:91
  19.3 6.5 %collective-permute-start.3 = (bf16[96,640]{1,0:T(8,128)(2,1)S(1)}, bf16[96,640]{1,0:T(8,128)(2,1)S(1)}, u32[]{:S(2)}, u32[]{:S(2)}) collective-permute-start(bf16[96,640]{1,0:T(8,128)(2,1)S(1)} %collective-permute-done.2.refs_3_), channel_id=1, source_target_pairs={{0,8},{1,5},{2,10},{3,7},{8,16},{9,1},{10,18},{11,3},{16,24},{17,9... | collective-permute-start | bytes 368648 | tf_op jit(solution)/shard_map/ppermute | solution.py:91
  21.4 5.4 %collective-permute-start.18 = (bf16[96,640]{1,0:T(8,128)(2,1)S(1)}, bf16[96,640]{1,0:T(8,128)(2,1)S(1)}, u32[]{:S(2)}, u32[]{:S(2)}) collective-permute-start(bf16[96,640]{1,0:T(8,128)(2,1)S(1)} %collective-permute-done.17.refs_12_), channel_id=1, source_target_pairs={{0,4},{1,9},{2,6},{3,11},{8,0},{9,17},{10,2},{11,19},{16,8},{17,25... | collective-permute-start | bytes 368648 | tf_op jit(solution)/shard_map/ppermute | solution.py:91
  22.7 5.3 %collective-permute-start.9 = (bf16[96,640]{1,0:T(8,128)(2,1)S(1)}, bf16[96,640]{1,0:T(8,128)(2,1)S(1)}, u32[]{:S(2)}, u32[]{:S(2)}) collective-permute-start(bf16[96,640]{1,0:T(8,128)(2,1)S(1)} %collective-permute-done.8.refs_2_), channel_id=1, source_target_pairs={{0,8},{1,5},{2,10},{3,7},{8,16},{9,1},{10,18},{11,3},{16,24},{17,9... | collective-permute-start | bytes 368648 | tf_op jit(solution)/shard_map/ppermute | solution.py:91
  23.2 9.6 %collective-permute-start.19 = (bf16[96,640]{1,0:T(8,128)(2,1)S(1)}, bf16[96,640]{1,0:T(8,128)(2,1)S(1)}, u32[]{:S(2)}, u32[]{:S(2)}) collective-permute-start(bf16[96,640]{1,0:T(8,128)(2,1)S(1)} %collective-permute-done.12.refs_4_), channel_id=1, source_target_pairs={{0,4},{1,9},{2,6},{3,11},{8,0},{9,17},{10,2},{11,19},{16,8},{17,25... | collective-permute-start | bytes 368648 | tf_op jit(solution)/shard_map/ppermute | solution.py:91
  24.3 8.5 %collective-permute-start.20 = (bf16[96,640]{1,0:T(8,128)(2,1)S(1)}, bf16[96,640]{1,0:T(8,128)(2,1)S(1)}, u32[]{:S(2)}, u32[]{:S(2)}) collective-permute-start(bf16[96,640]{1,0:T(8,128)(2,1)S(1)} %collective-permute-done.15.refs_10_), channel_id=1, source_target_pairs={{0,8},{1,5},{2,10},{3,7},{8,16},{9,1},{10,18},{11,3},{16,24},{17,9... | collective-permute-start | bytes 368648 | tf_op jit(solution)/shard_map/ppermute | solution.py:91
  40.0 10.5 %collective-permute-start.22 = (bf16[96,640]{1,0:T(8,128)(2,1)S(1)}, bf16[96,640]{1,0:T(8,128)(2,1)S(1)}, u32[]{:S(2)}, u32[]{:S(2)}) collective-permute-start(bf16[96,640]{1,0:T(8,128)(2,1)S(1)} %get-tuple-element.16.refs_0_), channel_id=1, source_target_pairs={{0,2},{1,3},{2,0},{3,1},{4,6},{5,7},{6,4},{7,5},{8,10},{9,11},{10,... | collective-permute-start | bytes 368648 | tf_op jit(solution)/shard_map/ppermute | solution.py:280
  44.5 10.7 %collective-permute-start.25 = (bf16[96,640]{1,0:T(8,128)(2,1)S(1)}, bf16[96,640]{1,0:T(8,128)(2,1)S(1)}, u32[]{:S(2)}, u32[]{:S(2)}) collective-permute-start(bf16[96,640]{1,0:T(8,128)(2,1)S(1)} %shard_map.44), channel_id=1, source_target_pairs={{0,0},{1,4},{2,8},{3,12},{4,16},{5,20},{6,24},{7,28},{8,25},{9,29}... | collective-permute-start | bytes 368648 | tf_op jit(solution)/shard_map/ppermute | solution.py:292
  50.6 7.5 %collective-permute-start.23 = (bf16[96,640]{1,0:T(8,128)(2,1)S(1)}, bf16[96,640]{1,0:T(8,128)(2,1)S(1)}, u32[]{:S(2)}, u32[]{:S(2)}) collective-permute-start(bf16[96,640]{1,0:T(8,128)(2,1)S(1)} %shard_map.43), channel_id=1, source_target_pairs={{0,16},{1,20},{2,24},{3,28},{4,0},{5,4},{6,8},{7,12},{8,9},{9,13},... | collective-permute-start | bytes 368648 | tf_op jit(solution)/shard_map/ppermute | solution.py:292
  (5 other events, 17.4 us)

commit v14 on v13

--- a/solution.py
+++ b/solution.py
@@ -172,6 +172,15 @@
     return blocks
 
 
+def ahead(scores, heads):
+    columns = [slice(head * HD, (head + 1) * HD) for head in range(heads)]
+    now = scores(columns[0])
+    for head, cols in enumerate(columns):
+        later = scores(columns[head + 1]) if head + 1 < heads else None
+        yield head, cols, now
+        now = later
+
+
 def split_kernel(kv_ref, keys_ref, values_ref):
     keys_ref[...] = kv_ref[0]
     values_ref[...] = kv_ref[1]
@@ -187,11 +196,13 @@
     key_refs, value_refs, (mixed_ref, sum_ref, top_ref) = refs[: n - 1], refs[n - 1 : -3], refs[-3:]
     marks = frame_marks(at_ref, range(n), n)
     keys_marks = key_marks(near, ROWS, n)
-    for head in range(heads):
-        cols = slice(head * HD, (head + 1) * HD)
+
+    def scores(cols):
         queries = jnp.concatenate([rows_ref[:, :, cols].reshape(n * ROWS, HD), marks], axis=1)
-        keys = jnp.concatenate([rows_of(key_refs, cols, ROWS), keys_marks], axis=1)
-        weights, top = soften(scores_of(queries, keys))
+        return scores_of(queries, jnp.concatenate([rows_of(key_refs, cols, ROWS), keys_marks], axis=1))
+
+    for head, cols, now in ahead(scores, heads):
+        weights, top = soften(now)
         mixed, total = mix(weights, rows_of(value_refs, cols, ROWS))
         for d in range(n):
             rows = slice(d * ROWS, (d + 1) * ROWS)
@@ -207,12 +218,14 @@
     def of(ref, head):
         return jnp.concatenate([ref[head, block] for block in blocks], axis=0)
 
-    for head in range(heads):
-        cols = slice(head * HD, (head + 1) * HD)
+    def scores(cols):
         queries = jnp.concatenate([rows_ref[block, :, cols] for block in blocks], axis=0)
         keys = jnp.concatenate([rows_of([keys_ref], cols, TPF), keys_marks], axis=1)
+        return scores_of(jnp.concatenate([queries, marks], axis=1), keys)
+
+    for head, cols, now in ahead(scores, heads):
         before = of(top_ref, head)
-        weights, top = soften(scores_of(jnp.concatenate([queries, marks], axis=1), keys), before)
+        weights, top = soften(now, before)
         mixed, total = mix(weights, rows_of([values_ref], cols, TPF))
         kept = jnp.exp2((before - top) * SCALE)
         mixed, total = mixed + of(mixed_ref, head) * kept, total + of(sum_ref, head) * kept

time: 59.7 us -> 59.1 us (0.990)
  Pallas kernels: 10.2 us -> 9.51 us
    pallas_call x8, Pallas kernels: 10.2 us -> 9.51 us  [call(): pl.pallas_call(kernel, out_shape=[jax.ShapeDtypeStruct(shape, dtype) for...]
  transfers between devices with their start and end apart: 26 -> 26, of which waited for: 14 -> 15; matrix products, arithmetic and copies ran while one was open for 0% -> 0% of each run, Pallas kernels for 14% -> 13%
where the time goes in v14:
time: 59.1 us; the launch traced here: 58.6 us
  starting transfers between devices  30.1 us (51%)
  waiting for transfers between devices  16.1 us (27%)
  Pallas kernels  9.51 us (16%)
  local copies, waits for them, and re-layouts  1.94 us (3%)
  other arithmetic  0.79 us (1%)
    ppermute x21, starting transfers between devices, hop(): return lax.ppermute(x, ('frames', 'heads'), pairs)  17.9 us
    pallas_call x8, Pallas kernels, call(): pl.pallas_call(kernel, out_shape=[jax.ShapeDtypeStruct(shape, dtype) for...  9.51 us
    ppermute x21, waiting for transfers between devices, hop(): return lax.ppermute(x, ('frames', 'heads'), pairs)  8.01 us
    ppermute x2, starting transfers between devices, on_device_ring(): arrived.append(lax.ppermute(total, ('frames', 'heads'), pairs))  7.41 us
    ppermute x2, waiting for transfers between devices, on_device_ring(): arrived.append(lax.ppermute(total, ('frames', 'heads'), pairs))  6.45 us
    ppermute x1, starting transfers between devices, on_device_ring(): from_core = lax.ppermute(given, 'heads', [(h, h ^ 1) for h in range(4)])  3.17 us
    unnamed x6, local copies, waits for them, and re-layouts  1.85 us
    ppermute x2, waiting for transfers between devices, on_device_ring(): lax.ppermute(block, 'heads', [(h, h ^ 2) for h in range(4)])  1.62 us
  transfers between devices with their start and end apart: 26, of which 15 were waited for; matrix products, arithmetic and copies ran while one was open for 0% of the time, Pallas kernels for 13%

profile of v14, /device:TPU:3, one launch (start us, length us, event | category | flops | bytes accessed | tf_op | source)
XLA Modules:
  0.0 58.6 jit_solution(15112655450601285885)
XLA Ops:
  0.0 1.2 %collective-permute-start = (bf16[96,640]{1,0:T(8,128)(2,1)}, bf16[96,640]{1,0:T(8,128)(2,1)S(1)}, u32[]{:S(2)}, u32[]{:S(2)}) collective-permute-start(bf16[96,640]{1,0:T(8,128)(2,1)} %refs_0_.1), channel_id=1, source_target_pairs={{0,8},{1,5},{2,10},{3,7},{8,16},{9,1},{10,18},{11,3},{16,24},{17,9... | collective-permute-start | bytes 368648 | tf_op jit(solution)/shard_map/ppermute | solution.py:91
  2.4 1.3 %collective-permute-start.10 = (bf16[96,640]{1,0:T(8,128)(2,1)S(1)}, bf16[96,640]{1,0:T(8,128)(2,1)S(1)}, u32[]{:S(2)}, u32[]{:S(2)}) collective-permute-start(bf16[96,640]{1,0:T(8,128)(2,1)S(1)} %get-tuple-element.10.refs_0_), channel_id=1, source_target_pairs={{0,4},{1,9},{2,6},{3,11},{8,0},{9,17},{10,2},{11,19},{16,8},{17,25... | collective-permute-start | bytes 368648 | tf_op jit(solution)/shard_map/ppermute | solution.py:91
  4.0 1.3 %collective-permute-start.16 = (bf16[96,640]{1,0:T(8,128)(2,1)S(1)}, bf16[96,640]{1,0:T(8,128)(2,1)S(1)}, u32[]{:S(2)}, u32[]{:S(2)}) collective-permute-start(bf16[96,640]{1,0:T(8,128)(2,1)S(1)} %get-tuple-element.11.refs_7_), channel_id=1, source_target_pairs={{0,4},{1,9},{2,6},{3,11},{8,0},{9,17},{10,2},{11,19},{16,8},{17,25... | collective-permute-start | bytes 368648 | tf_op jit(solution)/shard_map/ppermute | solution.py:91
  5.5 1.2 %collective-permute-done.4.refs_7_ = bf16[96,640]{1,0:T(8,128)(2,1)S(1)} collective-permute-done((bf16[96,640]{1,0:T(8,128)(2,1)}, bf16[96,640]{1,0:T(8,128)(2,1)S(1)}, u32[]{:S(2)}, u32[]{:S(2)}) %collective-permute-start.4) | collective-permute-done | bytes 122912 | tf_op jit(solution)/shard_map/ppermute | solution.py:91
  9.1 1.3 %collective-permute-start.11 = (bf16[96,640]{1,0:T(8,128)(2,1)S(1)}, bf16[96,640]{1,0:T(8,128)(2,1)S(1)}, u32[]{:S(2)}, u32[]{:S(2)}) collective-permute-start(bf16[96,640]{1,0:T(8,128)(2,1)S(1)} %collective-permute-done.10.refs_6_), channel_id=1, source_target_pairs={{0,4},{1,9},{2,6},{3,11},{8,0},{9,17},{10,2},{11,19},{16,8},{17,25... | collective-permute-start | bytes 368648 | tf_op jit(solution)/shard_map/ppermute | solution.py:91
  11.7 1.3 %collective-permute-start.17 = (bf16[96,640]{1,0:T(8,128)(2,1)S(1)}, bf16[96,640]{1,0:T(8,128)(2,1)S(1)}, u32[]{:S(2)}, u32[]{:S(2)}) collective-permute-start(bf16[96,640]{1,0:T(8,128)(2,1)S(1)} %collective-permute-done.16.refs_13_), channel_id=1, source_target_pairs={{0,4},{1,9},{2,6},{3,11},{8,0},{9,17},{10,2},{11,19},{16,8},{17,25... | collective-permute-start | bytes 368648 | tf_op jit(solution)/shard_map/ppermute | solution.py:91
  13.7 1.2 %collective-permute-start.8 = (bf16[96,640]{1,0:T(8,128)(2,1)S(1)}, bf16[96,640]{1,0:T(8,128)(2,1)S(1)}, u32[]{:S(2)}, u32[]{:S(2)}) collective-permute-start(bf16[96,640]{1,0:T(8,128)(2,1)S(1)} %collective-permute-done.7.refs_1_), channel_id=1, source_target_pairs={{0,8},{1,5},{2,10},{3,7},{8,16},{9,1},{10,18},{11,3},{16,24},{17,9... | collective-permute-start | bytes 368648 | tf_op jit(solution)/shard_map/ppermute | solution.py:91
  16.3 1.3 %collective-permute-start.12 = (bf16[96,640]{1,0:T(8,128)(2,1)S(1)}, bf16[96,640]{1,0:T(8,128)(2,1)S(1)}, u32[]{:S(2)}, u32[]{:S(2)}) collective-permute-start(bf16[96,640]{1,0:T(8,128)(2,1)S(1)} %collective-permute-done.11.refs_5_), channel_id=1, source_target_pairs={{0,4},{1,9},{2,6},{3,11},{8,0},{9,17},{10,2},{11,19},{16,8},{17,25... | collective-permute-start | bytes 368648 | tf_op jit(solution)/shard_map/ppermute | solution.py:91
  18.1 1.2 %collective-permute-start.15 = (bf16[96,640]{1,0:T(8,128)(2,1)S(1)}, bf16[96,640]{1,0:T(8,128)(2,1)S(1)}, u32[]{:S(2)}, u32[]{:S(2)}) collective-permute-start(bf16[96,640]{1,0:T(8,128)(2,1)S(1)} %collective-permute-done.14.refs_9_), channel_id=1, source_target_pairs={{0,8},{1,5},{2,10},{3,7},{8,16},{9,1},{10,18},{11,3},{16,24},{17,9... | collective-permute-start | bytes 368648 | tf_op jit(solution)/shard_map/ppermute | solution.py:91
  19.3 1.3 %collective-permute-start.3 = (bf16[96,640]{1,0:T(8,128)(2,1)S(1)}, bf16[96,640]{1,0:T(8,128)(2,1)S(1)}, u32[]{:S(2)}, u32[]{:S(2)}) collective-permute-start(bf16[96,640]{1,0:T(8,128)(2,1)S(1)} %collective-permute-done.2.refs_3_), channel_id=1, source_target_pairs={{0,8},{1,5},{2,10},{3,7},{8,16},{9,1},{10,18},{11,3},{16,24},{17,9... | collective-permute-start | bytes 368648 | tf_op jit(solution)/shard_map/ppermute | solution.py:91
  21.4 1.3 %collective-permute-start.18 = (bf16[96,640]{1,0:T(8,128)(2,1)S(1)}, bf16[96,640]{1,0:T(8,128)(2,1)S(1)}, u32[]{:S(2)}, u32[]{:S(2)}) collective-permute-start(bf16[96,640]{1,0:T(8,128)(2,1)S(1)} %collective-permute-done.17.refs_12_), channel_id=1, source_target_pairs={{0,4},{1,9},{2,6},{3,11},{8,0},{9,17},{10,2},{11,19},{16,8},{17,25... | collective-permute-start | bytes 368648 | tf_op jit(solution)/shard_map/ppermute | solution.py:91
  24.7 1.2 %collective-permute-done.3.refs_4_ = bf16[96,640]{1,0:T(8,128)(2,1)S(1)} collective-permute-done((bf16[96,640]{1,0:T(8,128)(2,1)S(1)}, bf16[96,640]{1,0:T(8,128)(2,1)S(1)}, u32[]{:S(2)}, u32[]{:S(2)}) %collective-permute-start.3) | collective-permute-done | bytes 122912 | tf_op jit(solution)/shard_map/ppermute | solution.py:91
  26.8 1.2 %collective-permute-done.9.refs_3_ = bf16[96,640]{1,0:T(8,128)(2,1)S(1)} collective-permute-done((bf16[96,640]{1,0:T(8,128)(2,1)S(1)}, bf16[96,640]{1,0:T(8,128)(2,1)S(1)}, u32[]{:S(2)}, u32[]{:S(2)}) %collective-permute-start.9) | collective-permute-done | bytes 122912 | tf_op jit(solution)/shard_map/ppermute | solution.py:91
  28.0 4.6 %shard_map.39 = (f32[5,8,96,128]{3,2,1,0:T(8,128)S(1)}, f32[5,8,96,128]{3,2,1,0:T(8,128)S(1)}, f32[5,8,96,128]{3,2,1,0:T(8,128)S(1)}) custom-call(s32[5]{0:T(128)S(1)} %stack.23.at_ref, bf16[8,96,640]{2,1,0:T(8,128)(2,1)S(1)} %shard_map.37.rows_ref, bf16[96,640]{1,0:T(8,128)(2,1)S(1)} %get-tuple-element.10.refs_0_, ...), custom_call_target="tpu_custom_call" | custom-call | flops 1321205760 | tf_op jit(solution)/shard_map/pallas_call | solution.py:244
  32.6 1.9 %shard_map.40 = bf16[384,640]{1,0:T(8,128)(2,1)S(1)} custom-call(s32[5]{0:T(128)S(1)} %stack.23.at_ref, bf16[8,96,640]{2,1,0:T(8,128)(2,1)S(1)} %shard_map.37.rows_ref, f32[5,8,96,128]{3,2,1,0:T(8,128)S(1)} %get-tuple-element.12.mixed_ref, f32[5,8,96,128]{3,2,1,0:T(8,128)S(1)} %get-tuple-element.13.sum_ref, f32[5,8,96,128]{3,2,1,0:T(8,128)S(1)} %get-tuple-element.14.top_ref, ...), custom_call_target="tpu_custom_call" | custom-call | flops 314572800 | tf_op jit(solution)/shard_map/pallas_call | solution.py:244
  34.6 3.2 %collective-permute-start.21 = (bf16[2,192,640]{2,1,0:T(8,128)(2,1)S(1)}, bf16[2,192,640]{2,1,0:T(8,128)(2,1)S(1)}, u32[]{:S(2)}, u32[]{:S(2)}) collective-permute-start(bf16[2,192,640]{2,1,0:T(8,128)(2,1)S(1)} %bitcast.16), channel_id=1, source_target_pairs={{0,1},{1,0},{2,3},{3,2},{4,5},{5,4},{6,7},{7,6},{8,9},{9,8},{10,11... | collective-permute-start | bytes 1474568 | tf_op jit(solution)/shard_map/ppermute | solution.py:289
  37.7 1.4 %shard_map.41 = f32[192,640]{1,0:T(8,128)S(1)} custom-call(s32[5]{0:T(128)S(1)} %stack.23.at_ref, bf16[8,96,640]{2,1,0:T(8,128)(2,1)S(1)} %shard_map.37.rows_ref, f32[5,8,96,128]{3,2,1,0:T(8,128)S(1)} %get-tuple-element.12.mixed_ref, f32[5,8,96,128]{3,2,1,0:T(8,128)S(1)} %get-tuple-element.13.sum_ref, f32[5,8,96,128]{3,2,1,0:T(8,128)S(1)} %get-tuple-element.14.top_ref, ...), custom_call_target="tpu_custom_call" | custom-call | flops 314572800 | tf_op jit(solution)/shard_map/pallas_call | solution.py:244
  39.6 1.2 %collective-permute-start.22 = (bf16[96,640]{1,0:T(8,128)(2,1)S(1)}, bf16[96,640]{1,0:T(8,128)(2,1)S(1)}, u32[]{:S(2)}, u32[]{:S(2)}) collective-permute-start(bf16[96,640]{1,0:T(8,128)(2,1)S(1)} %get-tuple-element.16.refs_0_), channel_id=1, source_target_pairs={{0,2},{1,3},{2,0},{3,1},{4,6},{5,7},{6,4},{7,5},{8,10},{9,11},{10,... | collective-permute-start | bytes 368648 | tf_op jit(solution)/shard_map/ppermute | solution.py:293
  40.8 1.4 %shard_map.42.kept_ref = f32[192,640]{1,0:T(8,128)S(1)} custom-call(s32[5]{0:T(128)S(1)} %stack.23.at_ref, bf16[8,96,640]{2,1,0:T(8,128)(2,1)S(1)} %shard_map.37.rows_ref, f32[5,8,96,128]{3,2,1,0:T(8,128)S(1)} %get-tuple-element.12.mixed_ref, f32[5,8,96,128]{3,2,1,0:T(8,128)S(1)} %get-tuple-element.13.sum_ref, ...), custom_call_target="tpu_custom_call" | custom-call | flops 314572800 | tf_op jit(solution)/shard_map/pallas_call | solution.py:244
  42.2 1.6 %collective-permute-done.24.from_x_ref = bf16[96,640]{1,0:T(8,128)(2,1)S(1)} collective-permute-done((bf16[96,640]{1,0:T(8,128)(2,1)S(1)}, bf16[96,640]{1,0:T(8,128)(2,1)S(1)}, u32[]{:S(2)}, u32[]{:S(2)}) %collective-permute-start.24) | collective-permute-done | bytes 122912 | tf_op jit(solution)/shard_map/ppermute | solution.py:293
  43.9 6.3 %collective-permute-start.25 = (bf16[96,640]{1,0:T(8,128)(2,1)S(1)}, bf16[96,640]{1,0:T(8,128)(2,1)S(1)}, u32[]{:S(2)}, u32[]{:S(2)}) collective-permute-start(bf16[96,640]{1,0:T(8,128)(2,1)S(1)} %shard_map.44), channel_id=1, source_target_pairs={{0,0},{1,4},{2,8},{3,12},{4,16},{5,20},{6,24},{7,28},{8,25},{9,29}... | collective-permute-start | bytes 368648 | tf_op jit(solution)/shard_map/ppermute | solution.py:305
  50.3 1.1 %collective-permute-start.23 = (bf16[96,640]{1,0:T(8,128)(2,1)S(1)}, bf16[96,640]{1,0:T(8,128)(2,1)S(1)}, u32[]{:S(2)}, u32[]{:S(2)}) collective-permute-start(bf16[96,640]{1,0:T(8,128)(2,1)S(1)} %shard_map.43), channel_id=1, source_target_pairs={{0,16},{1,20},{2,24},{3,28},{4,0},{5,4},{6,8},{7,12},{8,9},{9,13},... | collective-permute-start | bytes 368648 | tf_op jit(solution)/shard_map/ppermute | solution.py:305
  51.4 2.9 %collective-permute-done.25 = bf16[96,640]{1,0:T(8,128)(2,1)S(1)} collective-permute-done((bf16[96,640]{1,0:T(8,128)(2,1)S(1)}, bf16[96,640]{1,0:T(8,128)(2,1)S(1)}, u32[]{:S(2)}, u32[]{:S(2)}) %collective-permute-start.25) | collective-permute-done | bytes 122912 | tf_op jit(solution)/shard_map/ppermute | solution.py:305
  54.3 3.5 %collective-permute-done.23 = bf16[96,640]{1,0:T(8,128)(2,1)S(1)} collective-permute-done((bf16[96,640]{1,0:T(8,128)(2,1)S(1)}, bf16[96,640]{1,0:T(8,128)(2,1)S(1)}, u32[]{:S(2)}, u32[]{:S(2)}) %collective-permute-start.23) | collective-permute-done | bytes 122912 | tf_op jit(solution)/shard_map/ppermute | solution.py:305
  (46 shorter events, 12.9 us)
Async XLA Ops:
  0.0 5.3 %collective-permute-start = (bf16[96,640]{1,0:T(8,128)(2,1)}, bf16[96,640]{1,0:T(8,128)(2,1)S(1)}, u32[]{:S(2)}, u32[]{:S(2)}) collective-permute-start(bf16[96,640]{1,0:T(8,128)(2,1)} %refs_0_.1), channel_id=1, source_target_pairs={{0,8},{1,5},{2,10},{3,7},{8,16},{9,1},{10,18},{11,3},{16,24},{17,9... | collective-permute-start | bytes 368648 | tf_op jit(solution)/shard_map/ppermute | solution.py:91
  1.2 5.4 %collective-permute-start.4 = (bf16[96,640]{1,0:T(8,128)(2,1)}, bf16[96,640]{1,0:T(8,128)(2,1)S(1)}, u32[]{:S(2)}, u32[]{:S(2)}) collective-permute-start(bf16[96,640]{1,0:T(8,128)(2,1)} %refs_0_.1), channel_id=1, source_target_pairs={{0,4},{1,9},{2,6},{3,11},{8,0},{9,17},{10,2},{11,19},{16,8},{17,25... | collective-permute-start | bytes 368648 | tf_op jit(solution)/shard_map/ppermute | solution.py:91
  2.4 5.6 %collective-permute-start.10 = (bf16[96,640]{1,0:T(8,128)(2,1)S(1)}, bf16[96,640]{1,0:T(8,128)(2,1)S(1)}, u32[]{:S(2)}, u32[]{:S(2)}) collective-permute-start(bf16[96,640]{1,0:T(8,128)(2,1)S(1)} %get-tuple-element.10.refs_0_), channel_id=1, source_target_pairs={{0,4},{1,9},{2,6},{3,11},{8,0},{9,17},{10,2},{11,19},{16,8},{17,25... | collective-permute-start | bytes 368648 | tf_op jit(solution)/shard_map/ppermute | solution.py:91
  3.8 5.3 %collective-permute-start.13 = (bf16[96,640]{1,0:T(8,128)(2,1)S(1)}, bf16[96,640]{1,0:T(8,128)(2,1)S(1)}, u32[]{:S(2)}, u32[]{:S(2)}) collective-permute-start(bf16[96,640]{1,0:T(8,128)(2,1)S(1)} %get-tuple-element.11.refs_7_), channel_id=1, source_target_pairs={{0,8},{1,5},{2,10},{3,7},{8,16},{9,1},{10,18},{11,3},{16,24},{17,9... | collective-permute-start | bytes 368648 | tf_op jit(solution)/shard_map/ppermute | solution.py:91
  4.0 6.5 %collective-permute-start.16 = (bf16[96,640]{1,0:T(8,128)(2,1)S(1)}, bf16[96,640]{1,0:T(8,128)(2,1)S(1)}, u32[]{:S(2)}, u32[]{:S(2)}) collective-permute-start(bf16[96,640]{1,0:T(8,128)(2,1)S(1)} %get-tuple-element.11.refs_7_), channel_id=1, source_target_pairs={{0,4},{1,9},{2,6},{3,11},{8,0},{9,17},{10,2},{11,19},{16,8},{17,25... | collective-permute-start | bytes 368648 | tf_op jit(solution)/shard_map/ppermute | solution.py:91
  5.3 6.5 %collective-permute-start.7 = (bf16[96,640]{1,0:T(8,128)(2,1)S(1)}, bf16[96,640]{1,0:T(8,128)(2,1)S(1)}, u32[]{:S(2)}, u32[]{:S(2)}) collective-permute-start(bf16[96,640]{1,0:T(8,128)(2,1)S(1)} %get-tuple-element.10.refs_0_), channel_id=1, source_target_pairs={{0,8},{1,5},{2,10},{3,7},{8,16},{9,1},{10,18},{11,3},{16,24},{17,9... | collective-permute-start | bytes 368648 | tf_op jit(solution)/shard_map/ppermute | solution.py:91
  6.7 6.8 %collective-permute-start.1 = (bf16[96,640]{1,0:T(8,128)(2,1)S(1)}, bf16[96,640]{1,0:T(8,128)(2,1)S(1)}, u32[]{:S(2)}, u32[]{:S(2)}) collective-permute-start(bf16[96,640]{1,0:T(8,128)(2,1)S(1)} %collective-permute-done.refs_1_), channel_id=1, source_target_pairs={{0,8},{1,5},{2,10},{3,7},{8,16},{9,1},{10,18},{11,3},{16,24},{17,9... | collective-permute-start | bytes 368648 | tf_op jit(solution)/shard_map/ppermute | solution.py:91
  8.0 5.7 %collective-permute-start.5 = (bf16[96,640]{1,0:T(8,128)(2,1)S(1)}, bf16[96,640]{1,0:T(8,128)(2,1)S(1)}, u32[]{:S(2)}, u32[]{:S(2)}) collective-permute-start(bf16[96,640]{1,0:T(8,128)(2,1)S(1)} %collective-permute-done.4.refs_7_), channel_id=1, source_target_pairs={{0,4},{1,9},{2,6},{3,11},{8,0},{9,17},{10,2},{11,19},{16,8},{17,25... | collective-permute-start | bytes 368648 | tf_op jit(solution)/shard_map/ppermute | solution.py:91
  9.1 6.8 %collective-permute-start.11 = (bf16[96,640]{1,0:T(8,128)(2,1)S(1)}, bf16[96,640]{1,0:T(8,128)(2,1)S(1)}, u32[]{:S(2)}, u32[]{:S(2)}) collective-permute-start(bf16[96,640]{1,0:T(8,128)(2,1)S(1)} %collective-permute-done.10.refs_6_), channel_id=1, source_target_pairs={{0,4},{1,9},{2,6},{3,11},{8,0},{9,17},{10,2},{11,19},{16,8},{17,25... | collective-permute-start | bytes 368648 | tf_op jit(solution)/shard_map/ppermute | solution.py:91
  10.4 5.9 %collective-permute-start.14 = (bf16[96,640]{1,0:T(8,128)(2,1)S(1)}, bf16[96,640]{1,0:T(8,128)(2,1)S(1)}, u32[]{:S(2)}, u32[]{:S(2)}) collective-permute-start(bf16[96,640]{1,0:T(8,128)(2,1)S(1)} %collective-permute-done.13.refs_8_), channel_id=1, source_target_pairs={{0,8},{1,5},{2,10},{3,7},{8,16},{9,1},{10,18},{11,3},{16,24},{17,9... | collective-permute-start | bytes 368648 | tf_op jit(solution)/shard_map/ppermute | solution.py:91
  11.7 6.4 %collective-permute-start.17 = (bf16[96,640]{1,0:T(8,128)(2,1)S(1)}, bf16[96,640]{1,0:T(8,128)(2,1)S(1)}, u32[]{:S(2)}, u32[]{:S(2)}) collective-permute-start(bf16[96,640]{1,0:T(8,128)(2,1)S(1)} %collective-permute-done.16.refs_13_), channel_id=1, source_target_pairs={{0,4},{1,9},{2,6},{3,11},{8,0},{9,17},{10,2},{11,19},{16,8},{17,25... | collective-permute-start | bytes 368648 | tf_op jit(solution)/shard_map/ppermute | solution.py:91
  13.5 5.8 %collective-permute-start.2 = (bf16[96,640]{1,0:T(8,128)(2,1)S(1)}, bf16[96,640]{1,0:T(8,128)(2,1)S(1)}, u32[]{:S(2)}, u32[]{:S(2)}) collective-permute-start(bf16[96,640]{1,0:T(8,128)(2,1)S(1)} %collective-permute-done.1.refs_2_), channel_id=1, source_target_pairs={{0,8},{1,5},{2,10},{3,7},{8,16},{9,1},{10,18},{11,3},{16,24},{17,9... | collective-permute-start | bytes 368648 | tf_op jit(solution)/shard_map/ppermute | solution.py:91
  13.7 7.7 %collective-permute-start.8 = (bf16[96,640]{1,0:T(8,128)(2,1)S(1)}, bf16[96,640]{1,0:T(8,128)(2,1)S(1)}, u32[]{:S(2)}, u32[]{:S(2)}) collective-permute-start(bf16[96,640]{1,0:T(8,128)(2,1)S(1)} %collective-permute-done.7.refs_1_), channel_id=1, source_target_pairs={{0,8},{1,5},{2,10},{3,7},{8,16},{9,1},{10,18},{11,3},{16,24},{17,9... | collective-permute-start | bytes 368648 | tf_op jit(solution)/shard_map/ppermute | solution.py:91
  15.9 6.8 %collective-permute-start.6 = (bf16[96,640]{1,0:T(8,128)(2,1)S(1)}, bf16[96,640]{1,0:T(8,128)(2,1)S(1)}, u32[]{:S(2)}, u32[]{:S(2)}) collective-permute-start(bf16[96,640]{1,0:T(8,128)(2,1)S(1)} %collective-permute-done.5.refs_6_), channel_id=1, source_target_pairs={{0,4},{1,9},{2,6},{3,11},{8,0},{9,17},{10,2},{11,19},{16,8},{17,25... | collective-permute-start | bytes 368648 | tf_op jit(solution)/shard_map/ppermute | solution.py:91
  16.3 6.9 %collective-permute-start.12 = (bf16[96,640]{1,0:T(8,128)(2,1)S(1)}, bf16[96,640]{1,0:T(8,128)(2,1)S(1)}, u32[]{:S(2)}, u32[]{:S(2)}) collective-permute-start(bf16[96,640]{1,0:T(8,128)(2,1)S(1)} %collective-permute-done.11.refs_5_), channel_id=1, source_target_pairs={{0,4},{1,9},{2,6},{3,11},{8,0},{9,17},{10,2},{11,19},{16,8},{17,25... | collective-permute-start | bytes 368648 | tf_op jit(solution)/shard_map/ppermute | solution.py:91
  18.1 6.2 %collective-permute-start.15 = (bf16[96,640]{1,0:T(8,128)(2,1)S(1)}, bf16[96,640]{1,0:T(8,128)(2,1)S(1)}, u32[]{:S(2)}, u32[]{:S(2)}) collective-permute-start(bf16[96,640]{1,0:T(8,128)(2,1)S(1)} %collective-permute-done.14.refs_9_), channel_id=1, source_target_pairs={{0,8},{1,5},{2,10},{3,7},{8,16},{9,1},{10,18},{11,3},{16,24},{17,9... | collective-permute-start | bytes 368648 | tf_op jit(solution)/shard_map/ppermute | solution.py:91
  19.3 6.5 %collective-permute-start.3 = (bf16[96,640]{1,0:T(8,128)(2,1)S(1)}, bf16[96,640]{1,0:T(8,128)(2,1)S(1)}, u32[]{:S(2)}, u32[]{:S(2)}) collective-permute-start(bf16[96,640]{1,0:T(8,128)(2,1)S(1)} %collective-permute-done.2.refs_3_), channel_id=1, source_target_pairs={{0,8},{1,5},{2,10},{3,7},{8,16},{9,1},{10,18},{11,3},{16,24},{17,9... | collective-permute-start | bytes 368648 | tf_op jit(solution)/shard_map/ppermute | solution.py:91
  21.4 5.4 %collective-permute-start.18 = (bf16[96,640]{1,0:T(8,128)(2,1)S(1)}, bf16[96,640]{1,0:T(8,128)(2,1)S(1)}, u32[]{:S(2)}, u32[]{:S(2)}) collective-permute-start(bf16[96,640]{1,0:T(8,128)(2,1)S(1)} %collective-permute-done.17.refs_12_), channel_id=1, source_target_pairs={{0,4},{1,9},{2,6},{3,11},{8,0},{9,17},{10,2},{11,19},{16,8},{17,25... | collective-permute-start | bytes 368648 | tf_op jit(solution)/shard_map/ppermute | solution.py:91
  22.7 5.3 %collective-permute-start.9 = (bf16[96,640]{1,0:T(8,128)(2,1)S(1)}, bf16[96,640]{1,0:T(8,128)(2,1)S(1)}, u32[]{:S(2)}, u32[]{:S(2)}) collective-permute-start(bf16[96,640]{1,0:T(8,128)(2,1)S(1)} %collective-permute-done.8.refs_2_), channel_id=1, source_target_pairs={{0,8},{1,5},{2,10},{3,7},{8,16},{9,1},{10,18},{11,3},{16,24},{17,9... | collective-permute-start | bytes 368648 | tf_op jit(solution)/shard_map/ppermute | solution.py:91
  23.2 9.4 %collective-permute-start.19 = (bf16[96,640]{1,0:T(8,128)(2,1)S(1)}, bf16[96,640]{1,0:T(8,128)(2,1)S(1)}, u32[]{:S(2)}, u32[]{:S(2)}) collective-permute-start(bf16[96,640]{1,0:T(8,128)(2,1)S(1)} %collective-permute-done.12.refs_4_), channel_id=1, source_target_pairs={{0,4},{1,9},{2,6},{3,11},{8,0},{9,17},{10,2},{11,19},{16,8},{17,25... | collective-permute-start | bytes 368648 | tf_op jit(solution)/shard_map/ppermute | solution.py:91
  24.3 8.3 %collective-permute-start.20 = (bf16[96,640]{1,0:T(8,128)(2,1)S(1)}, bf16[96,640]{1,0:T(8,128)(2,1)S(1)}, u32[]{:S(2)}, u32[]{:S(2)}) collective-permute-start(bf16[96,640]{1,0:T(8,128)(2,1)S(1)} %collective-permute-done.15.refs_10_), channel_id=1, source_target_pairs={{0,8},{1,5},{2,10},{3,7},{8,16},{9,1},{10,18},{11,3},{16,24},{17,9... | collective-permute-start | bytes 368648 | tf_op jit(solution)/shard_map/ppermute | solution.py:91
  39.6 10.6 %collective-permute-start.22 = (bf16[96,640]{1,0:T(8,128)(2,1)S(1)}, bf16[96,640]{1,0:T(8,128)(2,1)S(1)}, u32[]{:S(2)}, u32[]{:S(2)}) collective-permute-start(bf16[96,640]{1,0:T(8,128)(2,1)S(1)} %get-tuple-element.16.refs_0_), channel_id=1, source_target_pairs={{0,2},{1,3},{2,0},{3,1},{4,6},{5,7},{6,4},{7,5},{8,10},{9,11},{10,... | collective-permute-start | bytes 368648 | tf_op jit(solution)/shard_map/ppermute | solution.py:293
  43.9 10.4 %collective-permute-start.25 = (bf16[96,640]{1,0:T(8,128)(2,1)S(1)}, bf16[96,640]{1,0:T(8,128)(2,1)S(1)}, u32[]{:S(2)}, u32[]{:S(2)}) collective-permute-start(bf16[96,640]{1,0:T(8,128)(2,1)S(1)} %shard_map.44), channel_id=1, source_target_pairs={{0,0},{1,4},{2,8},{3,12},{4,16},{5,20},{6,24},{7,28},{8,25},{9,29}... | collective-permute-start | bytes 368648 | tf_op jit(solution)/shard_map/ppermute | solution.py:305
  50.3 7.5 %collective-permute-start.23 = (bf16[96,640]{1,0:T(8,128)(2,1)S(1)}, bf16[96,640]{1,0:T(8,128)(2,1)S(1)}, u32[]{:S(2)}, u32[]{:S(2)}) collective-permute-start(bf16[96,640]{1,0:T(8,128)(2,1)S(1)} %shard_map.43), channel_id=1, source_target_pairs={{0,16},{1,20},{2,24},{3,28},{4,0},{5,4},{6,8},{7,12},{8,9},{9,13},... | collective-permute-start | bytes 368648 | tf_op jit(solution)/shard_map/ppermute | solution.py:305
  (5 other events, 16.9 us)

commit v15 on v14

--- a/solution.py
+++ b/solution.py
@@ -172,6 +172,13 @@
     return blocks
 
 
+def add_keys(mixed, total, before, scores, values):
+    weights, top = soften(scores, before)
+    more, more_total = mix(weights, values)
+    kept = jnp.exp2((before - top) * SCALE)
+    return more + mixed * kept, more_total + total * kept, top
+
+
 def ahead(scores, heads):
     columns = [slice(head * HD, (head + 1) * HD) for head in range(heads)]
     now = scores(columns[0])
@@ -181,7 +188,8 @@
         now = later
 
 
-def split_kernel(kv_ref, keys_ref, values_ref):
+def split_kernel(queries_ref, kv_ref, copy_ref, keys_ref, values_ref):
+    copy_ref[...] = queries_ref[...]
     keys_ref[...] = kv_ref[0]
     values_ref[...] = kv_ref[1]
 
@@ -191,22 +199,27 @@
         refs[n][d] = refs[d][...]
 
 
-def near_kernel(heads, n, at_ref, rows_ref, *refs):
-    near = [d for d in range(n) if d != n // 2]
-    key_refs, value_refs, (mixed_ref, sum_ref, top_ref) = refs[: n - 1], refs[n - 1 : -3], refs[-3:]
+def near_kernel(heads, n, blocks, at_ref, rows_ref, *refs):
+    count = len(blocks)
+    key_refs, value_refs, state, outs = refs[:count], refs[count : 2 * count], refs[2 * count : -3], refs[-3:]
+    padding = -count * ROWS % (2 * HD)
     marks = frame_marks(at_ref, range(n), n)
-    keys_marks = key_marks(near, ROWS, n)
+    keys_marks = key_marks(blocks, padding, n)
 
     def scores(cols):
         queries = jnp.concatenate([rows_ref[:, :, cols].reshape(n * ROWS, HD), marks], axis=1)
-        return scores_of(queries, jnp.concatenate([rows_of(key_refs, cols, ROWS), keys_marks], axis=1))
+        return scores_of(queries, jnp.concatenate([rows_of(key_refs, cols, padding), keys_marks], axis=1))
 
     for head, cols, now in ahead(scores, heads):
-        weights, top = soften(now)
-        mixed, total = mix(weights, rows_of(value_refs, cols, ROWS))
-        for d in range(n):
-            rows = slice(d * ROWS, (d + 1) * ROWS)
-            mixed_ref[head, d], sum_ref[head, d], top_ref[head, d] = mixed[rows], total[rows], top[rows]
+        values = rows_of(value_refs, cols, padding)
+        if state:
+            mixed, total, before = (ref[head].reshape(n * ROWS, HD) for ref in state)
+            mixed, total, top = add_keys(mixed, total, before, now, values)
+        else:
+            weights, top = soften(now)
+            mixed, total = mix(weights, values)
+        for ref, result in zip(outs, (mixed, total, top)):
+            ref[head] = result.reshape(n, ROWS, HD)
 
 
 def finish_kernel(heads, n, flips, at_ref, rows_ref, mixed_ref, sum_ref, top_ref, keys_ref, values_ref, w_ref, *refs):
@@ -224,19 +237,18 @@
         return scores_of(jnp.concatenate([queries, marks], axis=1), keys)
 
     for head, cols, now in ahead(scores, heads):
-        before = of(top_ref, head)
-        weights, top = soften(now, before)
-        mixed, total = mix(weights, rows_of([values_ref], cols, TPF))
-        kept = jnp.exp2((before - top) * SCALE)
-        mixed, total = mixed + of(mixed_ref, head) * kept, total + of(sum_ref, head) * kept
+        values = rows_of([values_ref], cols, TPF)
+        mixed, total, _ = add_keys(of(mixed_ref, head), of(sum_ref, head), of(top_ref, head), now, values)
         attended.append((mixed / total).astype(jnp.bfloat16))
     rows = jnp.concatenate(attended, axis=1)
     refs[-1][...] = jnp.dot(rows, w_ref[...], preferred_element_type=jnp.float32).astype(refs[-1].dtype)
 
 
-def sum_kernel(rows, kept_ref, from_core_ref, from_x_ref, total_ref):
-    total = kept_ref[rows] + from_core_ref[1, rows].astype(jnp.float32) + from_x_ref[...].astype(jnp.float32)
-    total_ref[...] = total.astype(total_ref.dtype)
+def sum_kernel(half, rows, others, own_ref, from_core_ref, *refs):
+    total = own_ref[rows] + from_core_ref[half, rows].astype(jnp.float32)
+    for ref in refs[:others]:
+        total += ref[...].astype(jnp.float32)
+    refs[-1][...] = total.astype(refs[-1].dtype)
 
 
 def call(kernel, scalars, operands, outs, flops, after=()):
@@ -262,17 +274,19 @@
     heads = width // HD
     f32, bf16 = jnp.float32, jnp.bfloat16
     block = (queries.shape, bf16)
-    own = call(split_kernel, (), [keys_values], [block, block], 0)
+    own_queries, *own = call(split_kernel, (), [queries, keys_values], [block] * 3, 0)
     queries, keys, values = gather_ring([queries, *own], n)
-    (rows,) = call(functools.partial(rows_kernel, n), (), queries, [((n, ROWS, width), bf16)], 0)
+    (rows,) = call(functools.partial(rows_kernel, n), (), [own_queries, *queries[1:]], [((n, ROWS, width), bf16)], 0)
     far = n // 2
-    state = call(
-        functools.partial(near_kernel, heads, n),
-        (where,),
-        [rows, *(blocks[d] for blocks in (keys, values) for d in range(n) if d != far)],
-        [((heads, n, ROWS, HD), f32)] * 3,
-        4 * n * (n - 1) * ROWS**2 * width,
-    )
+    state = []
+    for blocks in ([0, 1, 2, n - 2, n - 1], list(range(3, far)) + list(range(far + 1, n - 2))):
+        state = call(
+            functools.partial(near_kernel, heads, n, blocks),
+            (where,),
+            [rows, *(keys[d] for d in blocks), *(values[d] for d in blocks), *state],
+            [((heads, n, ROWS, HD), f32)] * 3,
+            4 * n * len(blocks) * ROWS**2 * width,
+        )
 
     def finish(flips, dtype, after=()):
         (sums,) = call(
@@ -289,9 +303,16 @@
     from_core = lax.ppermute(given, "heads", [(h, h ^ 1) for h in range(4)])
     sums = finish([(1, 0)], f32, (given,))[0]
     parts = [slice(slot * ROWS, (slot + 1) * ROWS) for slot in range(2)]
-    given = [(sums[part] + from_core[0, part].astype(f32)).astype(bf16) for part in parts]
-    from_x = [lax.ppermute(block, "heads", [(h, h ^ 2) for h in range(4)]) for block in given]
-    kept = finish([(0, 0)], f32, given)[0]
+
+    def add(half, part, own, others=(), after=()):
+        kernel = functools.partial(sum_kernel, half, part, len(others))
+        return call(kernel, (), [own, from_core, *others], [((ROWS, cols), bf16)], 0, after)[0]
+
+    to_x = [(h, h ^ 2) for h in range(4)]
+    given = add(0, parts[0], sums)
+    from_x = [lax.ppermute(given, "heads", to_x)]
+    kept = finish([(0, 0)], f32, (given,))[0]
+    from_x.append(lax.ppermute(add(0, parts[1], sums, (), (kept,)), "heads", to_x))
     arrived = []
     for slot, part in enumerate(parts):
         pairs = []
@@ -299,9 +320,7 @@
             for h in range(4):
                 to = PATTERNS[(slot ^ (f & 1)) + 2 * (h >> 1)][f >> 1]
                 pairs.append((4 * f + h, 4 * (2 * to + (h & 1)) + (f >> 1)))
-        (total,) = call(
-            functools.partial(sum_kernel, part), (), [kept, from_core, from_x[slot]], [((ROWS, cols), bf16)], 0
-        )
+        total = add(1, part, kept, [from_x[slot]])
         arrived.append(lax.ppermute(total, ("frames", "heads"), pairs))
     patterns = [[p[source] for p in PATTERNS].index(to) for source in range(4) for to in range(4)]
     straight = look_up(patterns, 4 * head + z) & 1 == 0

time: 59.1 us -> 61.3 us (1.037)
  Pallas kernels: 9.51 us -> 10.7 us
  waiting for transfers between devices: 16.1 us -> 17 us
    ppermute x2, waiting for transfers between devices: 1.62 us -> 3.08 us  [the longest x1 3.07 us: on_device_ring(): lax.ppermute(add(0, parts[1], sums, (), (kept,)), 'heads', to_x)]
    ppermute x21, starting transfers between devices: 17.9 us -> 16.6 us  [hop(): return lax.ppermute(x, ('frames', 'heads'), pairs)]
    pallas_call x8 -> x11, Pallas kernels: 9.51 us -> 10.7 us  [call(): pl.pallas_call(kernel, out_shape=[jax.ShapeDtypeStruct(shape, dtype) for...]
    ppermute x1, starting transfers between devices: 3.17 us -> 4.18 us  [on_device_ring(): from_core = lax.ppermute(given, 'heads', [(h, h ^ 1) for h in range(4)])]
  transfers between devices with their start and end apart: 26 -> 26, of which waited for: 15 -> 13; matrix products, arithmetic and copies ran while one was open for 0% -> 0% of each run, Pallas kernels for 13% -> 12%
where the time goes in v15:
time: 61.3 us; the launch traced here: 60.3 us
  starting transfers between devices  29.7 us (48%)
  waiting for transfers between devices  17 us (28%)
  Pallas kernels  10.7 us (17%)
  local copies, waits for them, and re-layouts  1.93 us (3%)
  other arithmetic  0.74 us (1%)
    ppermute x21, starting transfers between devices, hop(): return lax.ppermute(x, ('frames', 'heads'), pairs)  16.6 us
    pallas_call x11, Pallas kernels, call(): pl.pallas_call(kernel, out_shape=[jax.ShapeDtypeStruct(shape, dtype) for...  10.7 us
    ppermute x21, waiting for transfers between devices, hop(): return lax.ppermute(x, ('frames', 'heads'), pairs)  7.76 us
    ppermute x2, starting transfers between devices, on_device_ring(): arrived.append(lax.ppermute(total, ('frames', 'heads'), pairs))  7.42 us
    ppermute x2, waiting for transfers between devices, on_device_ring(): arrived.append(lax.ppermute(total, ('frames', 'heads'), pairs))  6.08 us
    ppermute x1, starting transfers between devices, on_device_ring(): from_core = lax.ppermute(given, 'heads', [(h, h ^ 1) for h in range(4)])  4.18 us
    ppermute x1, waiting for transfers between devices, on_device_ring(): lax.ppermute(add(0, parts[1], sums, (), (kept,)), 'heads', to_x)  3.07 us
    unnamed x6, local copies, waits for them, and re-layouts  1.85 us
  transfers between devices with their start and end apart: 26, of which 13 were waited for; matrix products, arithmetic and copies ran while one was open for 0% of the time, Pallas kernels for 12%

profile of v15, /device:TPU:3, one launch (start us, length us, event | category | flops | bytes accessed | tf_op | source)
XLA Modules:
  0.0 60.3 jit_solution(4268780674943270495)
XLA Ops:
  0.0 1.2 %collective-permute-start = (bf16[96,640]{1,0:T(8,128)(2,1)}, bf16[96,640]{1,0:T(8,128)(2,1)S(1)}, u32[]{:S(2)}, u32[]{:S(2)}) collective-permute-start(bf16[96,640]{1,0:T(8,128)(2,1)} %queries_ref.1), channel_id=1, source_target_pairs={{0,8},{1,5},{2,10},{3,7},{8,16},{9,1},{10,18},{11,3},{16,24},{17,9... | collective-permute-start | bytes 368648 | tf_op jit(solution)/shard_map/ppermute | solution.py:91
  3.3 1.3 %collective-permute-start.10 = (bf16[96,640]{1,0:T(8,128)(2,1)S(1)}, bf16[96,640]{1,0:T(8,128)(2,1)S(1)}, u32[]{:S(2)}, u32[]{:S(2)}) collective-permute-start(bf16[96,640]{1,0:T(8,128)(2,1)S(1)} %get-tuple-element.15.refs_0_), channel_id=1, source_target_pairs={{0,4},{1,9},{2,6},{3,11},{8,0},{9,17},{10,2},{11,19},{16,8},{17,25... | collective-permute-start | bytes 368648 | tf_op jit(solution)/shard_map/ppermute | solution.py:91
  4.9 1.3 %collective-permute-start.16 = (bf16[96,640]{1,0:T(8,128)(2,1)S(1)}, bf16[96,640]{1,0:T(8,128)(2,1)S(1)}, u32[]{:S(2)}, u32[]{:S(2)}) collective-permute-start(bf16[96,640]{1,0:T(8,128)(2,1)S(1)} %get-tuple-element.16.refs_5_), channel_id=1, source_target_pairs={{0,4},{1,9},{2,6},{3,11},{8,0},{9,17},{10,2},{11,19},{16,8},{17,25... | collective-permute-start | bytes 368648 | tf_op jit(solution)/shard_map/ppermute | solution.py:91
  8.4 1.3 %collective-permute-done.13.refs_6_ = bf16[96,640]{1,0:T(8,128)(2,1)S(1)} collective-permute-done((bf16[96,640]{1,0:T(8,128)(2,1)S(1)}, bf16[96,640]{1,0:T(8,128)(2,1)S(1)}, u32[]{:S(2)}, u32[]{:S(2)}) %collective-permute-start.13) | collective-permute-done | bytes 122912 | tf_op jit(solution)/shard_map/ppermute | solution.py:91
  9.7 1.3 %collective-permute-start.11 = (bf16[96,640]{1,0:T(8,128)(2,1)S(1)}, bf16[96,640]{1,0:T(8,128)(2,1)S(1)}, u32[]{:S(2)}, u32[]{:S(2)}) collective-permute-start(bf16[96,640]{1,0:T(8,128)(2,1)S(1)} %collective-permute-done.10.refs_4_), channel_id=1, source_target_pairs={{0,4},{1,9},{2,6},{3,11},{8,0},{9,17},{10,2},{11,19},{16,8},{17,25... | collective-permute-start | bytes 368648 | tf_op jit(solution)/shard_map/ppermute | solution.py:91
  12.4 1.3 %collective-permute-start.17 = (bf16[96,640]{1,0:T(8,128)(2,1)S(1)}, bf16[96,640]{1,0:T(8,128)(2,1)S(1)}, u32[]{:S(2)}, u32[]{:S(2)}) collective-permute-start(bf16[96,640]{1,0:T(8,128)(2,1)S(1)} %collective-permute-done.16.refs_9_), channel_id=1, source_target_pairs={{0,4},{1,9},{2,6},{3,11},{8,0},{9,17},{10,2},{11,19},{16,8},{17,25... | collective-permute-start | bytes 368648 | tf_op jit(solution)/shard_map/ppermute | solution.py:91
  14.3 1.2 %collective-permute-start.8 = (bf16[96,640]{1,0:T(8,128)(2,1)S(1)}, bf16[96,640]{1,0:T(8,128)(2,1)S(1)}, u32[]{:S(2)}, u32[]{:S(2)}) collective-permute-start(bf16[96,640]{1,0:T(8,128)(2,1)S(1)} %collective-permute-done.7.refs_1_), channel_id=1, source_target_pairs={{0,8},{1,5},{2,10},{3,7},{8,16},{9,1},{10,18},{11,3},{16,24},{17,9... | collective-permute-start | bytes 368648 | tf_op jit(solution)/shard_map/ppermute | solution.py:91
  16.6 1.3 %collective-permute-start.12 = (bf16[96,640]{1,0:T(8,128)(2,1)S(1)}, bf16[96,640]{1,0:T(8,128)(2,1)S(1)}, u32[]{:S(2)}, u32[]{:S(2)}) collective-permute-start(bf16[96,640]{1,0:T(8,128)(2,1)S(1)} %collective-permute-done.11.refs_3_), channel_id=1, source_target_pairs={{0,4},{1,9},{2,6},{3,11},{8,0},{9,17},{10,2},{11,19},{16,8},{17,25... | collective-permute-start | bytes 368648 | tf_op jit(solution)/shard_map/ppermute | solution.py:91
  19.9 2.0 %collective-permute-done.8.refs_2_ = bf16[96,640]{1,0:T(8,128)(2,1)S(1)} collective-permute-done((bf16[96,640]{1,0:T(8,128)(2,1)S(1)}, bf16[96,640]{1,0:T(8,128)(2,1)S(1)}, u32[]{:S(2)}, u32[]{:S(2)}) %collective-permute-start.8) | collective-permute-done | bytes 122912 | tf_op jit(solution)/shard_map/ppermute | solution.py:91
  21.9 1.3 %collective-permute-start.18 = (bf16[96,640]{1,0:T(8,128)(2,1)S(1)}, bf16[96,640]{1,0:T(8,128)(2,1)S(1)}, u32[]{:S(2)}, u32[]{:S(2)}) collective-permute-start(bf16[96,640]{1,0:T(8,128)(2,1)S(1)} %collective-permute-done.17.refs_8_), channel_id=1, source_target_pairs={{0,4},{1,9},{2,6},{3,11},{8,0},{9,17},{10,2},{11,19},{16,8},{17,25... | collective-permute-start | bytes 368648 | tf_op jit(solution)/shard_map/ppermute | solution.py:91
  23.4 1.3 %collective-permute-start.19 = (bf16[96,640]{1,0:T(8,128)(2,1)S(1)}, bf16[96,640]{1,0:T(8,128)(2,1)S(1)}, u32[]{:S(2)}, u32[]{:S(2)}) collective-permute-start(bf16[96,640]{1,0:T(8,128)(2,1)S(1)} %collective-permute-done.12.refs_1_), channel_id=1, source_target_pairs={{0,4},{1,9},{2,6},{3,11},{8,0},{9,17},{10,2},{11,19},{16,8},{17,25... | collective-permute-start | bytes 368648 | tf_op jit(solution)/shard_map/ppermute | solution.py:91
  24.9 1.4 %collective-permute-done.3.refs_4_ = bf16[96,640]{1,0:T(8,128)(2,1)S(1)} collective-permute-done((bf16[96,640]{1,0:T(8,128)(2,1)S(1)}, bf16[96,640]{1,0:T(8,128)(2,1)S(1)}, u32[]{:S(2)}, u32[]{:S(2)}) %collective-permute-start.3) | collective-permute-done | bytes 122912 | tf_op jit(solution)/shard_map/ppermute | solution.py:91
  26.4 3.2 %shard_map.39 = (f32[5,8,96,128]{3,2,1,0:T(8,128)S(1)}, f32[5,8,96,128]{3,2,1,0:T(8,128)S(1)}, f32[5,8,96,128]{3,2,1,0:T(8,128)S(1)}) custom-call(s32[5]{0:T(128)S(1)} %stack.23.at_ref, bf16[8,96,640]{2,1,0:T(8,128)(2,1)S(1)} %shard_map.38.rows_ref, bf16[96,640]{1,0:T(8,128)(2,1)S(1)} %get-tuple-element.15.refs_0_, ...), custom_call_target="tpu_custom_call" | custom-call | flops 943718400 | tf_op jit(solution)/shard_map/pallas_call | solution.py:256
  29.6 2.5 %shard_map.40 = (f32[5,8,96,128]{3,2,1,0:T(8,128)S(1)}, f32[5,8,96,128]{3,2,1,0:T(8,128)S(1)}, f32[5,8,96,128]{3,2,1,0:T(8,128)S(1)}) custom-call(s32[5]{0:T(128)S(1)} %stack.23.at_ref, bf16[8,96,640]{2,1,0:T(8,128)(2,1)S(1)} %shard_map.38.rows_ref, bf16[96,640]{1,0:T(8,128)(2,1)S(1)} %collective-permute-done.9.refs_0_, ...), custom_call_target="tpu_custom_call" | custom-call | flops 377487360 | tf_op jit(solution)/shard_map/pallas_call | solution.py:256
  32.2 1.9 %shard_map.41 = bf16[384,640]{1,0:T(8,128)(2,1)S(1)} custom-call(s32[5]{0:T(128)S(1)} %stack.23.at_ref, bf16[8,96,640]{2,1,0:T(8,128)(2,1)S(1)} %shard_map.38.rows_ref, f32[5,8,96,128]{3,2,1,0:T(8,128)S(1)} %get-tuple-element.20.mixed_ref, f32[5,8,96,128]{3,2,1,0:T(8,128)S(1)} %get-tuple-element.21.sum_ref, f32[5,8,96,128]{3,2,1,0:T(8,128)S(1)} %get-tuple-element.22.top_ref, ...), custom_call_target="tpu_custom_call" | custom-call | flops 314572800 | tf_op jit(solution)/shard_map/pallas_call | solution.py:256
  34.1 4.2 %collective-permute-start.21 = (bf16[2,192,640]{2,1,0:T(8,128)(2,1)S(1)}, bf16[2,192,640]{2,1,0:T(8,128)(2,1)S(1)}, u32[]{:S(2)}, u32[]{:S(2)}) collective-permute-start(bf16[2,192,640]{2,1,0:T(8,128)(2,1)S(1)} %bitcast.6), channel_id=1, source_target_pairs={{0,1},{1,0},{2,3},{3,2},{4,5},{5,4},{6,7},{7,6},{8,9},{9,8},{10,11... | collective-permute-start | bytes 1474568 | tf_op jit(solution)/shard_map/ppermute | solution.py:303
  38.3 1.4 %shard_map.42.own_ref = f32[192,640]{1,0:T(8,128)S(1)} custom-call(s32[5]{0:T(128)S(1)} %stack.23.at_ref, bf16[8,96,640]{2,1,0:T(8,128)(2,1)S(1)} %shard_map.38.rows_ref, f32[5,8,96,128]{3,2,1,0:T(8,128)S(1)} %get-tuple-element.20.mixed_ref, f32[5,8,96,128]{3,2,1,0:T(8,128)S(1)} %get-tuple-element.21.sum_ref, ...), custom_call_target="tpu_custom_call" | custom-call | flops 314572800 | tf_op jit(solution)/shard_map/pallas_call | solution.py:256
  39.8 1.4 %shard_map.44.own_ref.refs_0_ = f32[192,640]{1,0:T(8,128)S(1)} custom-call(s32[5]{0:T(128)S(1)} %stack.23.at_ref, bf16[8,96,640]{2,1,0:T(8,128)(2,1)S(1)} %shard_map.38.rows_ref, f32[5,8,96,128]{3,2,1,0:T(8,128)S(1)} %get-tuple-element.20.mixed_ref, f32[5,8,96,128]{3,2,1,0:T(8,128)S(1)} %get-tuple-element.21.sum_ref, ...), custom_call_target="tpu_custom_call" | custom-call | flops 314572800 | tf_op jit(solution)/shard_map/pallas_call | solution.py:256
  41.4 1.4 %collective-permute-start.22 = (bf16[96,640]{1,0:T(8,128)(2,1)S(1)}, bf16[96,640]{1,0:T(8,128)(2,1)S(1)}, u32[]{:S(2)}, u32[]{:S(2)}) collective-permute-start(bf16[96,640]{1,0:T(8,128)(2,1)S(1)} %shard_map.43.refs_0_), channel_id=1, source_target_pairs={{0,2},{1,3},{2,0},{3,1},{4,6},{5,7},{6,4},{7,5},{8,10},{9,11},{10,... | collective-permute-start | bytes 368648 | tf_op jit(solution)/shard_map/ppermute | solution.py:313
  42.8 3.1 %collective-permute-done.24.refs_0_ = bf16[96,640]{1,0:T(8,128)(2,1)S(1)} collective-permute-done((bf16[96,640]{1,0:T(8,128)(2,1)S(1)}, bf16[96,640]{1,0:T(8,128)(2,1)S(1)}, u32[]{:S(2)}, u32[]{:S(2)}) %collective-permute-start.24) | collective-permute-done | bytes 122912 | tf_op jit(solution)/shard_map/ppermute | solution.py:315
  45.9 5.1 %collective-permute-start.25 = (bf16[96,640]{1,0:T(8,128)(2,1)S(1)}, bf16[96,640]{1,0:T(8,128)(2,1)S(1)}, u32[]{:S(2)}, u32[]{:S(2)}) collective-permute-start(bf16[96,640]{1,0:T(8,128)(2,1)S(1)} %shard_map.47), channel_id=1, source_target_pairs={{0,0},{1,4},{2,8},{3,12},{4,16},{5,20},{6,24},{7,28},{8,25},{9,29}... | collective-permute-start | bytes 368648 | tf_op jit(solution)/shard_map/ppermute | solution.py:324
  51.1 2.3 %collective-permute-start.23 = (bf16[96,640]{1,0:T(8,128)(2,1)S(1)}, bf16[96,640]{1,0:T(8,128)(2,1)S(1)}, u32[]{:S(2)}, u32[]{:S(2)}) collective-permute-start(bf16[96,640]{1,0:T(8,128)(2,1)S(1)} %shard_map.45), channel_id=1, source_target_pairs={{0,16},{1,20},{2,24},{3,28},{4,0},{5,4},{6,8},{7,12},{8,9},{9,13},... | collective-permute-start | bytes 368648 | tf_op jit(solution)/shard_map/ppermute | solution.py:324
  53.4 3.4 %collective-permute-done.25 = bf16[96,640]{1,0:T(8,128)(2,1)S(1)} collective-permute-done((bf16[96,640]{1,0:T(8,128)(2,1)S(1)}, bf16[96,640]{1,0:T(8,128)(2,1)S(1)}, u32[]{:S(2)}, u32[]{:S(2)}) %collective-permute-start.25) | collective-permute-done | bytes 122912 | tf_op jit(solution)/shard_map/ppermute | solution.py:324
  56.8 2.7 %collective-permute-done.23 = bf16[96,640]{1,0:T(8,128)(2,1)S(1)} collective-permute-done((bf16[96,640]{1,0:T(8,128)(2,1)S(1)}, bf16[96,640]{1,0:T(8,128)(2,1)S(1)}, u32[]{:S(2)}, u32[]{:S(2)}) %collective-permute-start.23) | collective-permute-done | bytes 122912 | tf_op jit(solution)/shard_map/ppermute | solution.py:324
  (48 shorter events, 11.3 us)
Async XLA Ops:
  0.0 6.2 %collective-permute-start = (bf16[96,640]{1,0:T(8,128)(2,1)}, bf16[96,640]{1,0:T(8,128)(2,1)S(1)}, u32[]{:S(2)}, u32[]{:S(2)}) collective-permute-start(bf16[96,640]{1,0:T(8,128)(2,1)} %queries_ref.1), channel_id=1, source_target_pairs={{0,8},{1,5},{2,10},{3,7},{8,16},{9,1},{10,18},{11,3},{16,24},{17,9... | collective-permute-start | bytes 368648 | tf_op jit(solution)/shard_map/ppermute | solution.py:91
  1.2 5.4 %collective-permute-start.4 = (bf16[96,640]{1,0:T(8,128)(2,1)}, bf16[96,640]{1,0:T(8,128)(2,1)S(1)}, u32[]{:S(2)}, u32[]{:S(2)}) collective-permute-start(bf16[96,640]{1,0:T(8,128)(2,1)} %queries_ref.1), channel_id=1, source_target_pairs={{0,4},{1,9},{2,6},{3,11},{8,0},{9,17},{10,2},{11,19},{16,8},{17,25... | collective-permute-start | bytes 368648 | tf_op jit(solution)/shard_map/ppermute | solution.py:91
  4.7 5.0 %collective-permute-start.13 = (bf16[96,640]{1,0:T(8,128)(2,1)S(1)}, bf16[96,640]{1,0:T(8,128)(2,1)S(1)}, u32[]{:S(2)}, u32[]{:S(2)}) collective-permute-start(bf16[96,640]{1,0:T(8,128)(2,1)S(1)} %get-tuple-element.16.refs_5_), channel_id=1, source_target_pairs={{0,8},{1,5},{2,10},{3,7},{8,16},{9,1},{10,18},{11,3},{16,24},{17,9... | collective-permute-start | bytes 368648 | tf_op jit(solution)/shard_map/ppermute | solution.py:91
  4.9 6.2 %collective-permute-start.16 = (bf16[96,640]{1,0:T(8,128)(2,1)S(1)}, bf16[96,640]{1,0:T(8,128)(2,1)S(1)}, u32[]{:S(2)}, u32[]{:S(2)}) collective-permute-start(bf16[96,640]{1,0:T(8,128)(2,1)S(1)} %get-tuple-element.16.refs_5_), channel_id=1, source_target_pairs={{0,4},{1,9},{2,6},{3,11},{8,0},{9,17},{10,2},{11,19},{16,8},{17,25... | collective-permute-start | bytes 368648 | tf_op jit(solution)/shard_map/ppermute | solution.py:91
  6.2 6.2 %collective-permute-start.7 = (bf16[96,640]{1,0:T(8,128)(2,1)S(1)}, bf16[96,640]{1,0:T(8,128)(2,1)S(1)}, u32[]{:S(2)}, u32[]{:S(2)}) collective-permute-start(bf16[96,640]{1,0:T(8,128)(2,1)S(1)} %get-tuple-element.15.refs_0_), channel_id=1, source_target_pairs={{0,8},{1,5},{2,10},{3,7},{8,16},{9,1},{10,18},{11,3},{16,24},{17,9... | collective-permute-start | bytes 368648 | tf_op jit(solution)/shard_map/ppermute | solution.py:91
  6.7 7.3 %collective-permute-start.1 = (bf16[96,640]{1,0:T(8,128)(2,1)S(1)}, bf16[96,640]{1,0:T(8,128)(2,1)S(1)}, u32[]{:S(2)}, u32[]{:S(2)}) collective-permute-start(bf16[96,640]{1,0:T(8,128)(2,1)S(1)} %collective-permute-done.refs_1_), channel_id=1, source_target_pairs={{0,8},{1,5},{2,10},{3,7},{8,16},{9,1},{10,18},{11,3},{16,24},{17,9... | collective-permute-start | bytes 368648 | tf_op jit(solution)/shard_map/ppermute | solution.py:91
  8.0 6.3 %collective-permute-start.5 = (bf16[96,640]{1,0:T(8,128)(2,1)S(1)}, bf16[96,640]{1,0:T(8,128)(2,1)S(1)}, u32[]{:S(2)}, u32[]{:S(2)}) collective-permute-start(bf16[96,640]{1,0:T(8,128)(2,1)S(1)} %collective-permute-done.4.refs_7_), channel_id=1, source_target_pairs={{0,4},{1,9},{2,6},{3,11},{8,0},{9,17},{10,2},{11,19},{16,8},{17,25... | collective-permute-start | bytes 368648 | tf_op jit(solution)/shard_map/ppermute | solution.py:91
  9.7 5.8 %collective-permute-start.11 = (bf16[96,640]{1,0:T(8,128)(2,1)S(1)}, bf16[96,640]{1,0:T(8,128)(2,1)S(1)}, u32[]{:S(2)}, u32[]{:S(2)}) collective-permute-start(bf16[96,640]{1,0:T(8,128)(2,1)S(1)} %collective-permute-done.10.refs_4_), channel_id=1, source_target_pairs={{0,4},{1,9},{2,6},{3,11},{8,0},{9,17},{10,2},{11,19},{16,8},{17,25... | collective-permute-start | bytes 368648 | tf_op jit(solution)/shard_map/ppermute | solution.py:91
  11.0 5.6 %collective-permute-start.14 = (bf16[96,640]{1,0:T(8,128)(2,1)S(1)}, bf16[96,640]{1,0:T(8,128)(2,1)S(1)}, u32[]{:S(2)}, u32[]{:S(2)}) collective-permute-start(bf16[96,640]{1,0:T(8,128)(2,1)S(1)} %collective-permute-done.13.refs_6_), channel_id=1, source_target_pairs={{0,8},{1,5},{2,10},{3,7},{8,16},{9,1},{10,18},{11,3},{16,24},{17,9... | collective-permute-start | bytes 368648 | tf_op jit(solution)/shard_map/ppermute | solution.py:91
  12.4 5.6 %collective-permute-start.17 = (bf16[96,640]{1,0:T(8,128)(2,1)S(1)}, bf16[96,640]{1,0:T(8,128)(2,1)S(1)}, u32[]{:S(2)}, u32[]{:S(2)}) collective-permute-start(bf16[96,640]{1,0:T(8,128)(2,1)S(1)} %collective-permute-done.16.refs_9_), channel_id=1, source_target_pairs={{0,4},{1,9},{2,6},{3,11},{8,0},{9,17},{10,2},{11,19},{16,8},{17,25... | collective-permute-start | bytes 368648 | tf_op jit(solution)/shard_map/ppermute | solution.py:91
  14.0 5.4 %collective-permute-start.2 = (bf16[96,640]{1,0:T(8,128)(2,1)S(1)}, bf16[96,640]{1,0:T(8,128)(2,1)S(1)}, u32[]{:S(2)}, u32[]{:S(2)}) collective-permute-start(bf16[96,640]{1,0:T(8,128)(2,1)S(1)} %collective-permute-done.1.refs_2_), channel_id=1, source_target_pairs={{0,8},{1,5},{2,10},{3,7},{8,16},{9,1},{10,18},{11,3},{16,24},{17,9... | collective-permute-start | bytes 368648 | tf_op jit(solution)/shard_map/ppermute | solution.py:91
  14.3 7.6 %collective-permute-start.8 = (bf16[96,640]{1,0:T(8,128)(2,1)S(1)}, bf16[96,640]{1,0:T(8,128)(2,1)S(1)}, u32[]{:S(2)}, u32[]{:S(2)}) collective-permute-start(bf16[96,640]{1,0:T(8,128)(2,1)S(1)} %collective-permute-done.7.refs_1_), channel_id=1, source_target_pairs={{0,8},{1,5},{2,10},{3,7},{8,16},{9,1},{10,18},{11,3},{16,24},{17,9... | collective-permute-start | bytes 368648 | tf_op jit(solution)/shard_map/ppermute | solution.py:91
  15.5 7.7 %collective-permute-start.6 = (bf16[96,640]{1,0:T(8,128)(2,1)S(1)}, bf16[96,640]{1,0:T(8,128)(2,1)S(1)}, u32[]{:S(2)}, u32[]{:S(2)}) collective-permute-start(bf16[96,640]{1,0:T(8,128)(2,1)S(1)} %collective-permute-done.5.refs_6_), channel_id=1, source_target_pairs={{0,4},{1,9},{2,6},{3,11},{8,0},{9,17},{10,2},{11,19},{16,8},{17,25... | collective-permute-start | bytes 368648 | tf_op jit(solution)/shard_map/ppermute | solution.py:91
  16.6 6.8 %collective-permute-start.12 = (bf16[96,640]{1,0:T(8,128)(2,1)S(1)}, bf16[96,640]{1,0:T(8,128)(2,1)S(1)}, u32[]{:S(2)}, u32[]{:S(2)}) collective-permute-start(bf16[96,640]{1,0:T(8,128)(2,1)S(1)} %collective-permute-done.11.refs_3_), channel_id=1, source_target_pairs={{0,4},{1,9},{2,6},{3,11},{8,0},{9,17},{10,2},{11,19},{16,8},{17,25... | collective-permute-start | bytes 368648 | tf_op jit(solution)/shard_map/ppermute | solution.py:91
  17.9 6.8 %collective-permute-start.15 = (bf16[96,640]{1,0:T(8,128)(2,1)S(1)}, bf16[96,640]{1,0:T(8,128)(2,1)S(1)}, u32[]{:S(2)}, u32[]{:S(2)}) collective-permute-start(bf16[96,640]{1,0:T(8,128)(2,1)S(1)} %collective-permute-done.14.refs_7_), channel_id=1, source_target_pairs={{0,8},{1,5},{2,10},{3,7},{8,16},{9,1},{10,18},{11,3},{16,24},{17,9... | collective-permute-start | bytes 368648 | tf_op jit(solution)/shard_map/ppermute | solution.py:91
  19.4 6.9 %collective-permute-start.3 = (bf16[96,640]{1,0:T(8,128)(2,1)S(1)}, bf16[96,640]{1,0:T(8,128)(2,1)S(1)}, u32[]{:S(2)}, u32[]{:S(2)}) collective-permute-start(bf16[96,640]{1,0:T(8,128)(2,1)S(1)} %collective-permute-done.2.refs_3_), channel_id=1, source_target_pairs={{0,8},{1,5},{2,10},{3,7},{8,16},{9,1},{10,18},{11,3},{16,24},{17,9... | collective-permute-start | bytes 368648 | tf_op jit(solution)/shard_map/ppermute | solution.py:91
  21.9 7.7 %collective-permute-start.18 = (bf16[96,640]{1,0:T(8,128)(2,1)S(1)}, bf16[96,640]{1,0:T(8,128)(2,1)S(1)}, u32[]{:S(2)}, u32[]{:S(2)}) collective-permute-start(bf16[96,640]{1,0:T(8,128)(2,1)S(1)} %collective-permute-done.17.refs_8_), channel_id=1, source_target_pairs={{0,4},{1,9},{2,6},{3,11},{8,0},{9,17},{10,2},{11,19},{16,8},{17,25... | collective-permute-start | bytes 368648 | tf_op jit(solution)/shard_map/ppermute | solution.py:91
  23.2 6.4 %collective-permute-start.9 = (bf16[96,640]{1,0:T(8,128)(2,1)S(1)}, bf16[96,640]{1,0:T(8,128)(2,1)S(1)}, u32[]{:S(2)}, u32[]{:S(2)}) collective-permute-start(bf16[96,640]{1,0:T(8,128)(2,1)S(1)} %collective-permute-done.8.refs_2_), channel_id=1, source_target_pairs={{0,8},{1,5},{2,10},{3,7},{8,16},{9,1},{10,18},{11,3},{16,24},{17,9... | collective-permute-start | bytes 368648 | tf_op jit(solution)/shard_map/ppermute | solution.py:91
  23.4 8.7 %collective-permute-start.19 = (bf16[96,640]{1,0:T(8,128)(2,1)S(1)}, bf16[96,640]{1,0:T(8,128)(2,1)S(1)}, u32[]{:S(2)}, u32[]{:S(2)}) collective-permute-start(bf16[96,640]{1,0:T(8,128)(2,1)S(1)} %collective-permute-done.12.refs_1_), channel_id=1, source_target_pairs={{0,4},{1,9},{2,6},{3,11},{8,0},{9,17},{10,2},{11,19},{16,8},{17,25... | collective-permute-start | bytes 368648 | tf_op jit(solution)/shard_map/ppermute | solution.py:91
  24.7 7.4 %collective-permute-start.20 = (bf16[96,640]{1,0:T(8,128)(2,1)S(1)}, bf16[96,640]{1,0:T(8,128)(2,1)S(1)}, u32[]{:S(2)}, u32[]{:S(2)}) collective-permute-start(bf16[96,640]{1,0:T(8,128)(2,1)S(1)} %collective-permute-done.15.refs_2_), channel_id=1, source_target_pairs={{0,8},{1,5},{2,10},{3,7},{8,16},{9,1},{10,18},{11,3},{16,24},{17,9... | collective-permute-start | bytes 368648 | tf_op jit(solution)/shard_map/ppermute | solution.py:91
  34.1 5.7 %collective-permute-start.21 = (bf16[2,192,640]{2,1,0:T(8,128)(2,1)S(1)}, bf16[2,192,640]{2,1,0:T(8,128)(2,1)S(1)}, u32[]{:S(2)}, u32[]{:S(2)}) collective-permute-start(bf16[2,192,640]{2,1,0:T(8,128)(2,1)S(1)} %bitcast.6), channel_id=1, source_target_pairs={{0,1},{1,0},{2,3},{3,2},{4,5},{5,4},{6,7},{7,6},{8,9},{9,8},{10,11... | collective-permute-start | bytes 1474568 | tf_op jit(solution)/shard_map/ppermute | solution.py:303
  41.4 9.6 %collective-permute-start.22 = (bf16[96,640]{1,0:T(8,128)(2,1)S(1)}, bf16[96,640]{1,0:T(8,128)(2,1)S(1)}, u32[]{:S(2)}, u32[]{:S(2)}) collective-permute-start(bf16[96,640]{1,0:T(8,128)(2,1)S(1)} %shard_map.43.refs_0_), channel_id=1, source_target_pairs={{0,2},{1,3},{2,0},{3,1},{4,6},{5,7},{6,4},{7,5},{8,10},{9,11},{10,... | collective-permute-start | bytes 368648 | tf_op jit(solution)/shard_map/ppermute | solution.py:313
  45.9 10.9 %collective-permute-start.25 = (bf16[96,640]{1,0:T(8,128)(2,1)S(1)}, bf16[96,640]{1,0:T(8,128)(2,1)S(1)}, u32[]{:S(2)}, u32[]{:S(2)}) collective-permute-start(bf16[96,640]{1,0:T(8,128)(2,1)S(1)} %shard_map.47), channel_id=1, source_target_pairs={{0,0},{1,4},{2,8},{3,12},{4,16},{5,20},{6,24},{7,28},{8,25},{9,29}... | collective-permute-start | bytes 368648 | tf_op jit(solution)/shard_map/ppermute | solution.py:324
  51.1 8.4 %collective-permute-start.23 = (bf16[96,640]{1,0:T(8,128)(2,1)S(1)}, bf16[96,640]{1,0:T(8,128)(2,1)S(1)}, u32[]{:S(2)}, u32[]{:S(2)}) collective-permute-start(bf16[96,640]{1,0:T(8,128)(2,1)S(1)} %shard_map.45), channel_id=1, source_target_pairs={{0,16},{1,20},{2,24},{3,28},{4,0},{5,4},{6,8},{7,12},{8,9},{9,13},... | collective-permute-start | bytes 368648 | tf_op jit(solution)/shard_map/ppermute | solution.py:324
  (5 other events, 13.6 us)

commit v16 on v14

--- a/solution.py
+++ b/solution.py
@@ -154,24 +154,6 @@
     return mixed[:, :HD], mixed[:, HD:]
 
 
-PATTERNS = ((2, 1, 2, 1), (0, 3, 0, 3), (3, 0, 1, 2), (1, 2, 3, 0))
-
-
-def look_up(table, index):
-    code = sum(entry << (2 * i) for i, entry in enumerate(table))
-    return (jnp.int32(code - (code >> 31 << 32)) >> (2 * index)) & 3
-
-
-def slot_blocks(at_ref, flip_x, flip_core, n):
-    z, y, x, core = (at_ref[i] for i in range(1, 5))
-    blocks = []
-    for slot in range(2):
-        to = look_up(sum(PATTERNS, ()), 4 * ((slot ^ y) + 2 * (x ^ flip_x)) + z)
-        owner = to + (core ^ flip_core) * (n - 1 - 2 * to)
-        blocks.append(ring_distance(at_ref, owner, n))
-    return blocks
-
-
 def ahead(scores, heads):
     columns = [slice(head * HD, (head + 1) * HD) for head in range(heads)]
     now = scores(columns[0])
@@ -186,57 +168,58 @@
     values_ref[...] = kv_ref[1]
 
 
-def rows_kernel(n, *refs):
-    for d in range(n):
-        refs[n][d] = refs[d][...]
-
-
-def near_kernel(heads, n, at_ref, rows_ref, *refs):
-    near = [d for d in range(n) if d != n // 2]
-    key_refs, value_refs, (mixed_ref, sum_ref, top_ref) = refs[: n - 1], refs[n - 1 : -3], refs[-3:]
-    marks = frame_marks(at_ref, range(n), n)
-    keys_marks = key_marks(near, ROWS, n)
+def blocks_for(at_ref, parity, flips):
+    x, core = at_ref[3], at_ref[4]
+    found = []
+    for flip_x, flip_core in flips:
+        m = 2 * (core ^ flip_core) + (x ^ flip_x)
+        found.append(jnp.where(core == 0, m, (-m - parity) & 3))
+    return found
+
+
+def attend_kernel(heads, n, blocks, before, flips, at_ref, *refs):
+    count = len(blocks)
+    query_refs, refs = refs[:count], refs[count:]
+    key_refs, value_refs, refs = refs[:n], refs[n : 2 * n], refs[2 * n :]
+    attended_ref = refs[-2] if flips else refs[-1]
+    marks = frame_marks(at_ref, blocks, n)
+    keys_marks = key_marks(range(n), 0, n)
+    places = list(range(count))
+    if before:
+        places = [2]
+        for source, place in enumerate((0, 1, 3)):
+            attended_ref[place] = refs[0][source]
 
     def scores(cols):
-        queries = jnp.concatenate([rows_ref[:, :, cols].reshape(n * ROWS, HD), marks], axis=1)
-        return scores_of(queries, jnp.concatenate([rows_of(key_refs, cols, ROWS), keys_marks], axis=1))
-
-    for head, cols, now in ahead(scores, heads):
-        weights, top = soften(now)
-        mixed, total = mix(weights, rows_of(value_refs, cols, ROWS))
-        for d in range(n):
-            rows = slice(d * ROWS, (d + 1) * ROWS)
-            mixed_ref[head, d], sum_ref[head, d], top_ref[head, d] = mixed[rows], total[rows], top[rows]
-
-
-def finish_kernel(heads, n, flips, at_ref, rows_ref, mixed_ref, sum_ref, top_ref, keys_ref, values_ref, w_ref, *refs):
-    blocks = [block for flip in flips for block in slot_blocks(at_ref, *flip, n)]
-    marks = frame_marks(at_ref, blocks, n)
-    keys_marks = key_marks([n // 2], TPF, n)
-    attended = []
-
-    def of(ref, head):
-        return jnp.concatenate([ref[head, block] for block in blocks], axis=0)
-
-    def scores(cols):
-        queries = jnp.concatenate([rows_ref[block, :, cols] for block in blocks], axis=0)
-        keys = jnp.concatenate([rows_of([keys_ref], cols, TPF), keys_marks], axis=1)
-        return scores_of(jnp.concatenate([queries, marks], axis=1), keys)
-
-    for head, cols, now in ahead(scores, heads):
-        before = of(top_ref, head)
-        weights, top = soften(now, before)
-        mixed, total = mix(weights, rows_of([values_ref], cols, TPF))
-        kept = jnp.exp2((before - top) * SCALE)
-        mixed, total = mixed + of(mixed_ref, head) * kept, total + of(sum_ref, head) * kept
-        attended.append((mixed / total).astype(jnp.bfloat16))
-    rows = jnp.concatenate(attended, axis=1)
-    refs[-1][...] = jnp.dot(rows, w_ref[...], preferred_element_type=jnp.float32).astype(refs[-1].dtype)
-
-
-def sum_kernel(rows, kept_ref, from_core_ref, from_x_ref, total_ref):
-    total = kept_ref[rows] + from_core_ref[1, rows].astype(jnp.float32) + from_x_ref[...].astype(jnp.float32)
-    total_ref[...] = total.astype(total_ref.dtype)
+        queries = jnp.concatenate([rows_of(query_refs, cols), marks], axis=1)
+        return scores_of(queries, jnp.concatenate([rows_of(key_refs, cols), keys_marks], axis=1))
+
+    for _, cols, now in ahead(scores, heads):
+        weights, _ = soften(now)
+        mixed, total = mix(weights, rows_of(value_refs, cols))
+        result = (mixed / total).astype(jnp.bfloat16)
+        for i, place in enumerate(places):
+            attended_ref[place, :, cols] = result[i * ROWS : (i + 1) * ROWS]
+    if flips:
+        w_ref, out_ref = refs[1 if before else 0], refs[-1]
+        out_ref[...] = times_w(at_ref, blocks[0] % 2, flips, attended_ref, w_ref).astype(out_ref.dtype)
+
+
+def times_w(at_ref, parity, flips, attended_ref, w_ref):
+    rows = jnp.concatenate([attended_ref[block] for block in blocks_for(at_ref, parity, flips)], axis=0)
+    return jnp.dot(rows, w_ref[...], preferred_element_type=jnp.float32)
+
+
+def kept_kernel(parity, at_ref, attended_ref, w_ref, out_ref):
+    out_ref[...] = times_w(at_ref, parity, [(1, 0), (0, 0)], attended_ref, w_ref)
+
+
+def sum_kernel(half, others, own_ref, from_core_ref, *refs):
+    rows = slice(half * ROWS, (half + 1) * ROWS)
+    total = own_ref[rows] + from_core_ref[rows].astype(jnp.float32)
+    for ref in refs[:others]:
+        total += ref[...].astype(jnp.float32)
+    refs[-1][...] = total.astype(refs[-1].dtype)
 
 
 def call(kernel, scalars, operands, outs, flops, after=()):
@@ -263,50 +246,55 @@
     f32, bf16 = jnp.float32, jnp.bfloat16
     block = (queries.shape, bf16)
     own = call(split_kernel, (), [keys_values], [block, block], 0)
-    queries, keys, values = gather_ring([queries, *own], n)
-    (rows,) = call(functools.partial(rows_kernel, n), (), queries, [((n, ROWS, width), bf16)], 0)
-    far = n // 2
-    state = call(
-        functools.partial(near_kernel, heads, n),
-        (where,),
-        [rows, *(blocks[d] for blocks in (keys, values) for d in range(n) if d != far)],
-        [((heads, n, ROWS, HD), f32)] * 3,
-        4 * n * (n - 1) * ROWS**2 * width,
-    )
-
-    def finish(flips, dtype, after=()):
-        (sums,) = call(
-            functools.partial(finish_kernel, heads, n, flips),
+    keys, values, queries = gather_ring([*own, queries], n)
+
+    def attend(blocks, before=(), flips=(), after=()):
+        outs = [((4 if before else len(blocks), ROWS, width), bf16)]
+        if flips:
+            outs.append(((len(flips) * ROWS, cols), bf16))
+        return call(
+            functools.partial(attend_kernel, heads, n, blocks, bool(before), flips),
             (where,),
-            [rows, *state, keys[far], values[far], out_weight],
-            [((len(flips) * 2 * ROWS, cols), dtype)],
-            n * ROWS * width * cols,
+            [*(queries[d] for d in blocks), *keys, *values, *before, *([out_weight] if flips else [])],
+            outs,
+            4 * len(blocks) * n * ROWS**2 * width,
             after,
         )
-        return sums.reshape(len(flips), 2 * ROWS, cols)
-
-    given = finish([(1, 1), (0, 1)], bf16)
-    from_core = lax.ppermute(given, "heads", [(h, h ^ 1) for h in range(4)])
-    sums = finish([(1, 0)], f32, (given,))[0]
-    parts = [slice(slot * ROWS, (slot + 1) * ROWS) for slot in range(2)]
-    given = [(sums[part] + from_core[0, part].astype(f32)).astype(bf16) for part in parts]
-    from_x = [lax.ppermute(block, "heads", [(h, h ^ 2) for h in range(4)]) for block in given]
-    kept = finish([(0, 0)], f32, given)[0]
-    arrived = []
-    for slot, part in enumerate(parts):
+
+    def add(half, own, from_core, *others):
+        kernel = functools.partial(sum_kernel, half, len(others))
+        return call(kernel, (), [own, from_core, *others], [((ROWS, cols), bf16)], 0)[0]
+
+    def sums(parity, attended, given, after=()):
+        from_core = lax.ppermute(given, "heads", [(h, h ^ 1) for h in range(4)])
+        (kept,) = call(
+            functools.partial(kept_kernel, parity),
+            (where,),
+            [attended, out_weight],
+            [((2 * ROWS, cols), f32)],
+            2 * ROWS * width * cols,
+            after,
+        )
+        from_x = lax.ppermute(add(0, kept, from_core), "heads", [(h, h ^ 2) for h in range(4)])
+        return add(1, kept, from_core, from_x)
+
+    def send(parity, total):
+        order = ring_order(n)
         pairs = []
         for f in range(n):
             for h in range(4):
-                to = PATTERNS[(slot ^ (f & 1)) + 2 * (h >> 1)][f >> 1]
-                pairs.append((4 * f + h, 4 * (2 * to + (h & 1)) + (f >> 1)))
-        (total,) = call(
-            functools.partial(sum_kernel, part), (), [kept, from_core, from_x[slot]], [((ROWS, cols), bf16)], 0
-        )
-        arrived.append(lax.ppermute(total, ("frames", "heads"), pairs))
-    patterns = [[p[source] for p in PATTERNS].index(to) for source in range(4) for to in range(4)]
-    straight = look_up(patterns, 4 * head + z) & 1 == 0
-    low, high = arrived
-    return jnp.concatenate([jnp.where(straight, low, high), jnp.where(straight, high, low)], axis=1)
+                distance = 2 * (2 * (h & 1) + (h >> 1)) + parity
+                pairs.append((4 * f + h, 4 * order[(ring_place(f, n) - distance) % n] + (f >> 1)))
+        return lax.ppermute(total, ("frames", "heads"), pairs)
+
+    others = [(1, 1), (0, 1)]
+    (some,) = attend([0, 2, n - 2])
+    attended, given = attend([1, 3, n - 3, n - 1], (), others, (some,))
+    odd = send(1, sums(1, attended, given))
+    attended, given = attend([n // 2], (some,), others, (attended,))
+    even = send(0, sums(0, attended, given))
+    straight = (head - where[0]) & 1 == 0
+    return jnp.concatenate([jnp.where(straight, even, odd), jnp.where(straight, odd, even)], axis=1)
 
 
 def solution(mesh):

time: 59.1 us -> 60.4 us (1.022)
  waiting for transfers between devices: 16.1 us -> 17.9 us
  local copies, waits for them, and re-layouts: 1.94 us -> 1.03 us
    ppermute x5 -> x6, waiting for transfers between devices: 8.13 us -> 9.33 us  [the longest x2 6.42 us: send(): return lax.ppermute(total, ('frames', 'heads'), pairs)]
    unnamed x6, local copies, waits for them, and re-layouts: 1.85 us -> 0.95 us
    ppermute x5 -> x6, starting transfers between devices: 12.1 us -> 12.4 us  [the longest x2 6.26 us: send(): return lax.ppermute(total, ('frames', 'heads'), pairs)]
    pallas_call x8 -> x10, Pallas kernels: 9.51 us -> 9.65 us  [call(): pl.pallas_call(kernel, out_shape=[jax.ShapeDtypeStruct(shape, dtype) for...]
  transfers between devices with their start and end apart: 26 -> 27, of which waited for: 15 -> 13; matrix products, arithmetic and copies ran while one was open for 0% -> 0% of each run, Pallas kernels for 13% -> 12%
where the time goes in v16:
time: 60.4 us; the launch traced here: 59.3 us
  starting transfers between devices  29.8 us (49%)
  waiting for transfers between devices  17.9 us (30%)
  Pallas kernels  9.65 us (16%)
  local copies, waits for them, and re-layouts  1.03 us (2%)
  other arithmetic  0.74 us (1%)
    ppermute x21, starting transfers between devices, hop(): return lax.ppermute(x, ('frames', 'heads'), pairs)  17.4 us
    pallas_call x10, Pallas kernels, call(): pl.pallas_call(kernel, out_shape=[jax.ShapeDtypeStruct(shape, dtype) for...  9.65 us
    ppermute x21, waiting for transfers between devices, hop(): return lax.ppermute(x, ('frames', 'heads'), pairs)  8.56 us
    ppermute x2, waiting for transfers between devices, send(): return lax.ppermute(total, ('frames', 'heads'), pairs)  6.42 us
    ppermute x2, starting transfers between devices, send(): return lax.ppermute(total, ('frames', 'heads'), pairs)  6.26 us
    ppermute x2, starting transfers between devices, sums(): from_core = lax.ppermute(given, 'heads', [(h, h ^ 1) for h in range(4)])  4.59 us
    ppermute x2, waiting for transfers between devices, sums(): lax.ppermute(add(0, kept, from_core), 'heads', [(h, h ^ 2) for h in range...  2.9 us
    ppermute x2, starting transfers between devices, sums(): lax.ppermute(add(0, kept, from_core), 'heads', [(h, h ^ 2) for h in range...  1.6 us
  transfers between devices with their start and end apart: 27, of which 13 were waited for; matrix products, arithmetic and copies ran while one was open for 0% of the time, Pallas kernels for 12%

profile of v16, /device:TPU:3, one launch (start us, length us, event | category | flops | bytes accessed | tf_op | source)
XLA Modules:
  0.0 59.3 jit_solution(4998662863841247275)
XLA Ops:
  0.0 1.2 %collective-permute-start = (bf16[96,640]{1,0:T(8,128)(2,1)}, bf16[96,640]{1,0:T(8,128)(2,1)S(1)}, u32[]{:S(2)}, u32[]{:S(2)}) collective-permute-start(bf16[96,640]{1,0:T(8,128)(2,1)} %refs_0_.1), channel_id=1, source_target_pairs={{0,8},{1,5},{2,10},{3,7},{8,16},{9,1},{10,18},{11,3},{16,24},{17,9... | collective-permute-start | bytes 368648 | tf_op jit(solution)/shard_map/ppermute | solution.py:91
  2.4 1.3 %collective-permute-start.4 = (bf16[96,640]{1,0:T(8,128)(2,1)S(1)}, bf16[96,640]{1,0:T(8,128)(2,1)S(1)}, u32[]{:S(2)}, u32[]{:S(2)}) collective-permute-start(bf16[96,640]{1,0:T(8,128)(2,1)S(1)} %get-tuple-element.11.refs_3_.refs_4_.refs_1_), channel_id=1, source_target_pairs={{0,8},{1,5},{2,10},{3,7},{8,16},{9,1},{10,18},{11,3},{16,24},{17,9... | collective-permute-start | bytes 368648 | tf_op jit(solution)/shard_map/ppermute | solution.py:91
  4.0 1.3 %collective-permute-start.8 = (bf16[96,640]{1,0:T(8,128)(2,1)S(1)}, bf16[96,640]{1,0:T(8,128)(2,1)S(1)}, u32[]{:S(2)}, u32[]{:S(2)}) collective-permute-start(bf16[96,640]{1,0:T(8,128)(2,1)S(1)} %get-tuple-element.11.refs_3_.refs_4_.refs_1_), channel_id=1, source_target_pairs={{0,4},{1,9},{2,6},{3,11},{8,0},{9,17},{10,2},{11,19},{16,8},{17,25... | collective-permute-start | bytes 368648 | tf_op jit(solution)/shard_map/ppermute | solution.py:91
  5.5 1.2 %collective-permute-done.18.refs_3_ = bf16[96,640]{1,0:T(8,128)(2,1)S(1)} collective-permute-done((bf16[96,640]{1,0:T(8,128)(2,1)}, bf16[96,640]{1,0:T(8,128)(2,1)S(1)}, u32[]{:S(2)}, u32[]{:S(2)}) %collective-permute-start.18) | collective-permute-done | bytes 122912 | tf_op jit(solution)/shard_map/ppermute | solution.py:91
  6.7 1.2 %collective-permute-start.1 = (bf16[96,640]{1,0:T(8,128)(2,1)S(1)}, bf16[96,640]{1,0:T(8,128)(2,1)S(1)}, u32[]{:S(2)}, u32[]{:S(2)}) collective-permute-start(bf16[96,640]{1,0:T(8,128)(2,1)S(1)} %collective-permute-done.refs_0_), channel_id=1, source_target_pairs={{0,8},{1,5},{2,10},{3,7},{8,16},{9,1},{10,18},{11,3},{16,24},{17,9... | collective-permute-start | bytes 368648 | tf_op jit(solution)/shard_map/ppermute | solution.py:91
  7.9 1.2 %collective-permute-start.5 = (bf16[96,640]{1,0:T(8,128)(2,1)S(1)}, bf16[96,640]{1,0:T(8,128)(2,1)S(1)}, u32[]{:S(2)}, u32[]{:S(2)}) collective-permute-start(bf16[96,640]{1,0:T(8,128)(2,1)S(1)} %collective-permute-done.4.refs_4_.refs_5_.refs_2_), channel_id=1, source_target_pairs={{0,8},{1,5},{2,10},{3,7},{8,16},{9,1},{10,18},{11,3},{16,24},{17,9... | collective-permute-start | bytes 368648 | tf_op jit(solution)/shard_map/ppermute | solution.py:91
  9.3 1.4 %collective-permute-done.8.refs_10_.refs_11_.refs_8_ = bf16[96,640]{1,0:T(8,128)(2,1)S(1)} collective-permute-done((bf16[96,640]{1,0:T(8,128)(2,1)S(1)}, bf16[96,640]{1,0:T(8,128)(2,1)S(1)}, u32[]{:S(2)}, u32[]{:S(2)}) %collective-permute-start.8) | collective-permute-done | bytes 122912 | tf_op jit(solution)/shard_map/ppermute | solution.py:91
  11.0 1.3 %collective-permute-start.9 = (bf16[96,640]{1,0:T(8,128)(2,1)S(1)}, bf16[96,640]{1,0:T(8,128)(2,1)S(1)}, u32[]{:S(2)}, u32[]{:S(2)}) collective-permute-start(bf16[96,640]{1,0:T(8,128)(2,1)S(1)} %collective-permute-done.8.refs_10_.refs_11_.refs_8_), channel_id=1, source_target_pairs={{0,4},{1,9},{2,6},{3,11},{8,0},{9,17},{10,2},{11,19},{16,8},{17,25... | collective-permute-start | bytes 368648 | tf_op jit(solution)/shard_map/ppermute | solution.py:91
  13.4 1.1 %collective-permute-done.5.refs_5_.refs_6_.refs_3_ = bf16[96,640]{1,0:T(8,128)(2,1)S(1)} collective-permute-done((bf16[96,640]{1,0:T(8,128)(2,1)S(1)}, bf16[96,640]{1,0:T(8,128)(2,1)S(1)}, u32[]{:S(2)}, u32[]{:S(2)}) %collective-permute-start.5) | collective-permute-done | bytes 122912 | tf_op jit(solution)/shard_map/ppermute | solution.py:91
  17.1 1.3 %collective-permute-start.2 = (bf16[96,640]{1,0:T(8,128)(2,1)S(1)}, bf16[96,640]{1,0:T(8,128)(2,1)S(1)}, u32[]{:S(2)}, u32[]{:S(2)}) collective-permute-start(bf16[96,640]{1,0:T(8,128)(2,1)S(1)} %collective-permute-done.1.refs_1_), channel_id=1, source_target_pairs={{0,8},{1,5},{2,10},{3,7},{8,16},{9,1},{10,18},{11,3},{16,24},{17,9... | collective-permute-start | bytes 368648 | tf_op jit(solution)/shard_map/ppermute | solution.py:91
  18.9 1.1 %collective-permute-start.13 = (bf16[96,640]{1,0:T(8,128)(2,1)S(1)}, bf16[96,640]{1,0:T(8,128)(2,1)S(1)}, u32[]{:S(2)}, u32[]{:S(2)}) collective-permute-start(bf16[96,640]{1,0:T(8,128)(2,1)S(1)} %collective-permute-done.12.refs_13_.refs_14_.refs_11_), channel_id=1, source_target_pairs={{0,8},{1,5},{2,10},{3,7},{8,16},{9,1},{10,18},{11,3},{16,24},{17,9... | collective-permute-start | bytes 368648 | tf_op jit(solution)/shard_map/ppermute | solution.py:91
  20.1 1.2 %collective-permute-start.7 = (bf16[96,640]{1,0:T(8,128)(2,1)S(1)}, bf16[96,640]{1,0:T(8,128)(2,1)S(1)}, u32[]{:S(2)}, u32[]{:S(2)}) collective-permute-start(bf16[96,640]{1,0:T(8,128)(2,1)S(1)} %collective-permute-done.6.refs_6_.refs_7_.refs_4_), channel_id=1, source_target_pairs={{0,8},{1,5},{2,10},{3,7},{8,16},{9,1},{10,18},{11,3},{16,24},{17,9... | collective-permute-start | bytes 368648 | tf_op jit(solution)/shard_map/ppermute | solution.py:91
  21.5 1.2 %collective-permute-done.2.refs_1_ = bf16[96,640]{1,0:T(8,128)(2,1)S(1)} collective-permute-done((bf16[96,640]{1,0:T(8,128)(2,1)S(1)}, bf16[96,640]{1,0:T(8,128)(2,1)S(1)}, u32[]{:S(2)}, u32[]{:S(2)}) %collective-permute-start.2) | collective-permute-done | bytes 122912 | tf_op jit(solution)/shard_map/ppermute | solution.py:91
  22.7 1.3 %collective-permute-start.20 = (bf16[96,640]{1,0:T(8,128)(2,1)S(1)}, bf16[96,640]{1,0:T(8,128)(2,1)S(1)}, u32[]{:S(2)}, u32[]{:S(2)}) collective-permute-start(bf16[96,640]{1,0:T(8,128)(2,1)S(1)} %collective-permute-done.19.refs_2_), channel_id=1, source_target_pairs={{0,4},{1,9},{2,6},{3,11},{8,0},{9,17},{10,2},{11,19},{16,8},{17,25... | collective-permute-start | bytes 368648 | tf_op jit(solution)/shard_map/ppermute | solution.py:91
  25.3 1.7 %collective-permute-done.7.refs_7_.refs_8_.refs_5_ = bf16[96,640]{1,0:T(8,128)(2,1)S(1)} collective-permute-done((bf16[96,640]{1,0:T(8,128)(2,1)S(1)}, bf16[96,640]{1,0:T(8,128)(2,1)S(1)}, u32[]{:S(2)}, u32[]{:S(2)}) %collective-permute-start.7) | collective-permute-done | bytes 122912 | tf_op jit(solution)/shard_map/ppermute | solution.py:91
  27.0 2.3 %shard_map.38.refs_21_.refs_17_ = bf16[3,96,640]{2,1,0:T(8,128)(2,1)S(1)} custom-call(s32[5]{0:T(128)S(1)} %stack.23.at_ref, bf16[96,640]{1,0:T(8,128)(2,1)S(1)} %copy-done.2, bf16[96,640]{1,0:T(8,128)(2,1)S(1)} %collective-permute-done.1.refs_1_, bf16[96,640]{1,0:T(8,128)(2,1)S(1)} %collective-permute-done.19.refs_2_, ...), custom_call_target="tpu_custom_call" | custom-call | flops 566231040 | tf_op jit(solution)/shard_map/pallas_call | solution.py:227
  29.3 3.0 %shard_map.39 = (bf16[4,96,640]{2,1,0:T(8,128)(2,1)S(1)}, bf16[192,640]{1,0:T(8,128)(2,1)S(1)}) custom-call(s32[5]{0:T(128)S(1)} %stack.23.at_ref, bf16[96,640]{1,0:T(8,128)(2,1)S(1)} %collective-permute-done.refs_0_, bf16[96,640]{1,0:T(8,128)(2,1)S(1)} %collective-permute-done.2.refs_1_, bf16[96,640]{1,0:T(8,128)(2,1)S(1)} %collective-permute-done.20.refs_2_, ...), custom_call_target="tpu_custom_call" | custom-call | flops 754974720 | tf_op jit(solution)/shard_map/pallas_call | solution.py:227
  32.4 2.3 %shard_map.40 = (bf16[4,96,640]{2,1,0:T(8,128)(2,1)S(1)}, bf16[192,640]{1,0:T(8,128)(2,1)S(1)}) custom-call(s32[5]{0:T(128)S(1)} %stack.23.at_ref, bf16[96,640]{1,0:T(8,128)(2,1)S(1)} %collective-permute-done.3.refs_0_, bf16[96,640]{1,0:T(8,128)(2,1)S(1)} %get-tuple-element.11.refs_3_.refs_4_.refs_1_, ...), custom_call_target="tpu_custom_call" | custom-call | flops 188743680 | tf_op jit(solution)/shard_map/pallas_call | solution.py:227
  34.7 4.5 %collective-permute-start.21 = (bf16[192,640]{1,0:T(8,128)(2,1)S(1)}, bf16[192,640]{1,0:T(8,128)(2,1)S(1)}, u32[]{:S(2)}, u32[]{:S(2)}) collective-permute-start(bf16[192,640]{1,0:T(8,128)(2,1)S(1)} %get-tuple-element.15), channel_id=1, source_target_pairs={{0,1},{1,0},{2,3},{3,2},{4,5},{5,4},{6,7},{7,6},{8,9},{9,8},{10,11... | collective-permute-start | bytes 737288 | tf_op jit(solution)/shard_map/ppermute | solution.py:269
  41.6 1.2 %collective-permute-start.25 = (bf16[96,640]{1,0:T(8,128)(2,1)S(1)}, bf16[96,640]{1,0:T(8,128)(2,1)S(1)}, u32[]{:S(2)}, u32[]{:S(2)}) collective-permute-start(bf16[96,640]{1,0:T(8,128)(2,1)S(1)} %shard_map.45), channel_id=1, source_target_pairs={{0,2},{1,3},{2,0},{3,1},{4,6},{5,7},{6,4},{7,5},{8,10},{9,11},{10,... | collective-permute-start | bytes 368648 | tf_op jit(solution)/shard_map/ppermute | solution.py:278
  42.8 2.9 %collective-permute-done.22.refs_0_ = bf16[96,640]{1,0:T(8,128)(2,1)S(1)} collective-permute-done((bf16[96,640]{1,0:T(8,128)(2,1)S(1)}, bf16[96,640]{1,0:T(8,128)(2,1)S(1)}, u32[]{:S(2)}, u32[]{:S(2)}) %collective-permute-start.22) | collective-permute-done | bytes 122912 | tf_op jit(solution)/shard_map/ppermute | solution.py:278
  45.8 6.2 %collective-permute-start.23 = (bf16[96,640]{1,0:T(8,128)(2,1)S(1)}, bf16[96,640]{1,0:T(8,128)(2,1)S(1)}, u32[]{:S(2)}, u32[]{:S(2)}) collective-permute-start(bf16[96,640]{1,0:T(8,128)(2,1)S(1)} %shard_map.43), channel_id=1, source_target_pairs={{0,0},{1,28},{2,12},{3,16},{4,4},{5,24},{6,20},{7,8},{8,9},{9,21},... | collective-permute-start | bytes 368648 | tf_op jit(solution)/shard_map/ppermute | solution.py:288
  52.1 3.0 %collective-permute-done.23 = bf16[96,640]{1,0:T(8,128)(2,1)S(1)} collective-permute-done((bf16[96,640]{1,0:T(8,128)(2,1)S(1)}, bf16[96,640]{1,0:T(8,128)(2,1)S(1)}, u32[]{:S(2)}, u32[]{:S(2)}) %collective-permute-start.23) | collective-permute-done | bytes 122912 | tf_op jit(solution)/shard_map/ppermute | solution.py:288
  55.1 3.4 %collective-permute-done.26 = bf16[96,640]{1,0:T(8,128)(2,1)S(1)} collective-permute-done((bf16[96,640]{1,0:T(8,128)(2,1)S(1)}, bf16[96,640]{1,0:T(8,128)(2,1)S(1)}, u32[]{:S(2)}, u32[]{:S(2)}) %collective-permute-start.26) | collective-permute-done | bytes 122912 | tf_op jit(solution)/shard_map/ppermute | solution.py:288
  (49 shorter events, 11.2 us)
Async XLA Ops:
  1.2 5.4 %collective-permute-start.18 = (bf16[96,640]{1,0:T(8,128)(2,1)}, bf16[96,640]{1,0:T(8,128)(2,1)S(1)}, u32[]{:S(2)}, u32[]{:S(2)}) collective-permute-start(bf16[96,640]{1,0:T(8,128)(2,1)} %refs_0_.1), channel_id=1, source_target_pairs={{0,4},{1,9},{2,6},{3,11},{8,0},{9,17},{10,2},{11,19},{16,8},{17,25... | collective-permute-start | bytes 368648 | tf_op jit(solution)/shard_map/ppermute | solution.py:91
  2.4 5.4 %collective-permute-start.4 = (bf16[96,640]{1,0:T(8,128)(2,1)S(1)}, bf16[96,640]{1,0:T(8,128)(2,1)S(1)}, u32[]{:S(2)}, u32[]{:S(2)}) collective-permute-start(bf16[96,640]{1,0:T(8,128)(2,1)S(1)} %get-tuple-element.11.refs_3_.refs_4_.refs_1_), channel_id=1, source_target_pairs={{0,8},{1,5},{2,10},{3,7},{8,16},{9,1},{10,18},{11,3},{16,24},{17,9... | collective-permute-start | bytes 368648 | tf_op jit(solution)/shard_map/ppermute | solution.py:91
  3.7 5.3 %collective-permute-start.14 = (bf16[96,640]{1,0:T(8,128)(2,1)S(1)}, bf16[96,640]{1,0:T(8,128)(2,1)S(1)}, u32[]{:S(2)}, u32[]{:S(2)}) collective-permute-start(bf16[96,640]{1,0:T(8,128)(2,1)S(1)} %get-tuple-element.12.refs_11_.refs_12_.refs_9_), channel_id=1, source_target_pairs={{0,4},{1,9},{2,6},{3,11},{8,0},{9,17},{10,2},{11,19},{16,8},{17,25... | collective-permute-start | bytes 368648 | tf_op jit(solution)/shard_map/ppermute | solution.py:91
  4.0 6.8 %collective-permute-start.8 = (bf16[96,640]{1,0:T(8,128)(2,1)S(1)}, bf16[96,640]{1,0:T(8,128)(2,1)S(1)}, u32[]{:S(2)}, u32[]{:S(2)}) collective-permute-start(bf16[96,640]{1,0:T(8,128)(2,1)S(1)} %get-tuple-element.11.refs_3_.refs_4_.refs_1_), channel_id=1, source_target_pairs={{0,4},{1,9},{2,6},{3,11},{8,0},{9,17},{10,2},{11,19},{16,8},{17,25... | collective-permute-start | bytes 368648 | tf_op jit(solution)/shard_map/ppermute | solution.py:91
  5.3 5.7 %collective-permute-start.11 = (bf16[96,640]{1,0:T(8,128)(2,1)S(1)}, bf16[96,640]{1,0:T(8,128)(2,1)S(1)}, u32[]{:S(2)}, u32[]{:S(2)}) collective-permute-start(bf16[96,640]{1,0:T(8,128)(2,1)S(1)} %get-tuple-element.12.refs_11_.refs_12_.refs_9_), channel_id=1, source_target_pairs={{0,8},{1,5},{2,10},{3,7},{8,16},{9,1},{10,18},{11,3},{16,24},{17,9... | collective-permute-start | bytes 368648 | tf_op jit(solution)/shard_map/ppermute | solution.py:91
  6.7 6.1 %collective-permute-start.1 = (bf16[96,640]{1,0:T(8,128)(2,1)S(1)}, bf16[96,640]{1,0:T(8,128)(2,1)S(1)}, u32[]{:S(2)}, u32[]{:S(2)}) collective-permute-start(bf16[96,640]{1,0:T(8,128)(2,1)S(1)} %collective-permute-done.refs_0_), channel_id=1, source_target_pairs={{0,8},{1,5},{2,10},{3,7},{8,16},{9,1},{10,18},{11,3},{16,24},{17,9... | collective-permute-start | bytes 368648 | tf_op jit(solution)/shard_map/ppermute | solution.py:91
  7.9 6.7 %collective-permute-start.5 = (bf16[96,640]{1,0:T(8,128)(2,1)S(1)}, bf16[96,640]{1,0:T(8,128)(2,1)S(1)}, u32[]{:S(2)}, u32[]{:S(2)}) collective-permute-start(bf16[96,640]{1,0:T(8,128)(2,1)S(1)} %collective-permute-done.4.refs_4_.refs_5_.refs_2_), channel_id=1, source_target_pairs={{0,8},{1,5},{2,10},{3,7},{8,16},{9,1},{10,18},{11,3},{16,24},{17,9... | collective-permute-start | bytes 368648 | tf_op jit(solution)/shard_map/ppermute | solution.py:91
  9.1 6.0 %collective-permute-start.15 = (bf16[96,640]{1,0:T(8,128)(2,1)S(1)}, bf16[96,640]{1,0:T(8,128)(2,1)S(1)}, u32[]{:S(2)}, u32[]{:S(2)}) collective-permute-start(bf16[96,640]{1,0:T(8,128)(2,1)S(1)} %collective-permute-done.14.refs_18_.refs_19_.refs_16_), channel_id=1, source_target_pairs={{0,4},{1,9},{2,6},{3,11},{8,0},{9,17},{10,2},{11,19},{16,8},{17,25... | collective-permute-start | bytes 368648 | tf_op jit(solution)/shard_map/ppermute | solution.py:91
  10.8 6.3 %collective-permute-start.19 = (bf16[96,640]{1,0:T(8,128)(2,1)S(1)}, bf16[96,640]{1,0:T(8,128)(2,1)S(1)}, u32[]{:S(2)}, u32[]{:S(2)}) collective-permute-start(bf16[96,640]{1,0:T(8,128)(2,1)S(1)} %collective-permute-done.18.refs_3_), channel_id=1, source_target_pairs={{0,4},{1,9},{2,6},{3,11},{8,0},{9,17},{10,2},{11,19},{16,8},{17,25... | collective-permute-start | bytes 368648 | tf_op jit(solution)/shard_map/ppermute | solution.py:91
  11.0 7.6 %collective-permute-start.9 = (bf16[96,640]{1,0:T(8,128)(2,1)S(1)}, bf16[96,640]{1,0:T(8,128)(2,1)S(1)}, u32[]{:S(2)}, u32[]{:S(2)}) collective-permute-start(bf16[96,640]{1,0:T(8,128)(2,1)S(1)} %collective-permute-done.8.refs_10_.refs_11_.refs_8_), channel_id=1, source_target_pairs={{0,4},{1,9},{2,6},{3,11},{8,0},{9,17},{10,2},{11,19},{16,8},{17,25... | collective-permute-start | bytes 368648 | tf_op jit(solution)/shard_map/ppermute | solution.py:91
  12.8 6.1 %collective-permute-start.12 = (bf16[96,640]{1,0:T(8,128)(2,1)S(1)}, bf16[96,640]{1,0:T(8,128)(2,1)S(1)}, u32[]{:S(2)}, u32[]{:S(2)}) collective-permute-start(bf16[96,640]{1,0:T(8,128)(2,1)S(1)} %collective-permute-done.11.refs_12_.refs_13_.refs_10_), channel_id=1, source_target_pairs={{0,8},{1,5},{2,10},{3,7},{8,16},{9,1},{10,18},{11,3},{16,24},{17,9... | collective-permute-start | bytes 368648 | tf_op jit(solution)/shard_map/ppermute | solution.py:91
  14.5 5.5 %collective-permute-start.6 = (bf16[96,640]{1,0:T(8,128)(2,1)S(1)}, bf16[96,640]{1,0:T(8,128)(2,1)S(1)}, u32[]{:S(2)}, u32[]{:S(2)}) collective-permute-start(bf16[96,640]{1,0:T(8,128)(2,1)S(1)} %collective-permute-done.5.refs_5_.refs_6_.refs_3_), channel_id=1, source_target_pairs={{0,8},{1,5},{2,10},{3,7},{8,16},{9,1},{10,18},{11,3},{16,24},{17,9... | collective-permute-start | bytes 368648 | tf_op jit(solution)/shard_map/ppermute | solution.py:91
  15.1 6.2 %collective-permute-start.16 = (bf16[96,640]{1,0:T(8,128)(2,1)S(1)}, bf16[96,640]{1,0:T(8,128)(2,1)S(1)}, u32[]{:S(2)}, u32[]{:S(2)}) collective-permute-start(bf16[96,640]{1,0:T(8,128)(2,1)S(1)} %collective-permute-done.15.refs_17_.refs_18_.refs_15_), channel_id=1, source_target_pairs={{0,4},{1,9},{2,6},{3,11},{8,0},{9,17},{10,2},{11,19},{16,8},{17,25... | collective-permute-start | bytes 368648 | tf_op jit(solution)/shard_map/ppermute | solution.py:91
  17.1 5.6 %collective-permute-start.2 = (bf16[96,640]{1,0:T(8,128)(2,1)S(1)}, bf16[96,640]{1,0:T(8,128)(2,1)S(1)}, u32[]{:S(2)}, u32[]{:S(2)}) collective-permute-start(bf16[96,640]{1,0:T(8,128)(2,1)S(1)} %collective-permute-done.1.refs_1_), channel_id=1, source_target_pairs={{0,8},{1,5},{2,10},{3,7},{8,16},{9,1},{10,18},{11,3},{16,24},{17,9... | collective-permute-start | bytes 368648 | tf_op jit(solution)/shard_map/ppermute | solution.py:91
  18.5 5.6 %collective-permute-start.10 = (bf16[96,640]{1,0:T(8,128)(2,1)S(1)}, bf16[96,640]{1,0:T(8,128)(2,1)S(1)}, u32[]{:S(2)}, u32[]{:S(2)}) collective-permute-start(bf16[96,640]{1,0:T(8,128)(2,1)S(1)} %collective-permute-done.9.refs_9_.refs_10_.refs_7_), channel_id=1, source_target_pairs={{0,4},{1,9},{2,6},{3,11},{8,0},{9,17},{10,2},{11,19},{16,8},{17,25... | collective-permute-start | bytes 368648 | tf_op jit(solution)/shard_map/ppermute | solution.py:91
  18.9 6.4 %collective-permute-start.13 = (bf16[96,640]{1,0:T(8,128)(2,1)S(1)}, bf16[96,640]{1,0:T(8,128)(2,1)S(1)}, u32[]{:S(2)}, u32[]{:S(2)}) collective-permute-start(bf16[96,640]{1,0:T(8,128)(2,1)S(1)} %collective-permute-done.12.refs_13_.refs_14_.refs_11_), channel_id=1, source_target_pairs={{0,8},{1,5},{2,10},{3,7},{8,16},{9,1},{10,18},{11,3},{16,24},{17,9... | collective-permute-start | bytes 368648 | tf_op jit(solution)/shard_map/ppermute | solution.py:91
  20.1 6.9 %collective-permute-start.7 = (bf16[96,640]{1,0:T(8,128)(2,1)S(1)}, bf16[96,640]{1,0:T(8,128)(2,1)S(1)}, u32[]{:S(2)}, u32[]{:S(2)}) collective-permute-start(bf16[96,640]{1,0:T(8,128)(2,1)S(1)} %collective-permute-done.6.refs_6_.refs_7_.refs_4_), channel_id=1, source_target_pairs={{0,8},{1,5},{2,10},{3,7},{8,16},{9,1},{10,18},{11,3},{16,24},{17,9... | collective-permute-start | bytes 368648 | tf_op jit(solution)/shard_map/ppermute | solution.py:91
  21.3 5.7 %collective-permute-start.17 = (bf16[96,640]{1,0:T(8,128)(2,1)S(1)}, bf16[96,640]{1,0:T(8,128)(2,1)S(1)}, u32[]{:S(2)}, u32[]{:S(2)}) collective-permute-start(bf16[96,640]{1,0:T(8,128)(2,1)S(1)} %collective-permute-done.16.refs_16_.refs_17_.refs_14_), channel_id=1, source_target_pairs={{0,4},{1,9},{2,6},{3,11},{8,0},{9,17},{10,2},{11,19},{16,8},{17,25... | collective-permute-start | bytes 368648 | tf_op jit(solution)/shard_map/ppermute | solution.py:91
  22.7 6.6 %collective-permute-start.20 = (bf16[96,640]{1,0:T(8,128)(2,1)S(1)}, bf16[96,640]{1,0:T(8,128)(2,1)S(1)}, u32[]{:S(2)}, u32[]{:S(2)}) collective-permute-start(bf16[96,640]{1,0:T(8,128)(2,1)S(1)} %collective-permute-done.19.refs_2_), channel_id=1, source_target_pairs={{0,4},{1,9},{2,6},{3,11},{8,0},{9,17},{10,2},{11,19},{16,8},{17,25... | collective-permute-start | bytes 368648 | tf_op jit(solution)/shard_map/ppermute | solution.py:91
  24.1 8.3 %collective-permute-start.3 = (bf16[96,640]{1,0:T(8,128)(2,1)S(1)}, bf16[96,640]{1,0:T(8,128)(2,1)S(1)}, u32[]{:S(2)}, u32[]{:S(2)}) collective-permute-start(bf16[96,640]{1,0:T(8,128)(2,1)S(1)} %collective-permute-done.2.refs_1_), channel_id=1, source_target_pairs={{0,8},{1,5},{2,10},{3,7},{8,16},{9,1},{10,18},{11,3},{16,24},{17,9... | collective-permute-start | bytes 368648 | tf_op jit(solution)/shard_map/ppermute | solution.py:91
  34.7 6.5 %collective-permute-start.21 = (bf16[192,640]{1,0:T(8,128)(2,1)S(1)}, bf16[192,640]{1,0:T(8,128)(2,1)S(1)}, u32[]{:S(2)}, u32[]{:S(2)}) collective-permute-start(bf16[192,640]{1,0:T(8,128)(2,1)S(1)} %get-tuple-element.15), channel_id=1, source_target_pairs={{0,1},{1,0},{2,3},{3,2},{4,5},{5,4},{6,7},{7,6},{8,9},{9,8},{10,11... | collective-permute-start | bytes 737288 | tf_op jit(solution)/shard_map/ppermute | solution.py:269
  41.6 10.4 %collective-permute-start.25 = (bf16[96,640]{1,0:T(8,128)(2,1)S(1)}, bf16[96,640]{1,0:T(8,128)(2,1)S(1)}, u32[]{:S(2)}, u32[]{:S(2)}) collective-permute-start(bf16[96,640]{1,0:T(8,128)(2,1)S(1)} %shard_map.45), channel_id=1, source_target_pairs={{0,2},{1,3},{2,0},{3,1},{4,6},{5,7},{6,4},{7,5},{8,10},{9,11},{10,... | collective-permute-start | bytes 368648 | tf_op jit(solution)/shard_map/ppermute | solution.py:278
  45.8 9.3 %collective-permute-start.23 = (bf16[96,640]{1,0:T(8,128)(2,1)S(1)}, bf16[96,640]{1,0:T(8,128)(2,1)S(1)}, u32[]{:S(2)}, u32[]{:S(2)}) collective-permute-start(bf16[96,640]{1,0:T(8,128)(2,1)S(1)} %shard_map.43), channel_id=1, source_target_pairs={{0,0},{1,28},{2,12},{3,16},{4,4},{5,24},{6,20},{7,8},{8,9},{9,21},... | collective-permute-start | bytes 368648 | tf_op jit(solution)/shard_map/ppermute | solution.py:288
  52.0 6.5 %collective-permute-start.26 = (bf16[96,640]{1,0:T(8,128)(2,1)S(1)}, bf16[96,640]{1,0:T(8,128)(2,1)S(1)}, u32[]{:S(2)}, u32[]{:S(2)}) collective-permute-start(bf16[96,640]{1,0:T(8,128)(2,1)S(1)} %shard_map.46), channel_id=1, source_target_pairs={{0,4},{1,24},{2,20},{3,8},{4,12},{5,16},{6,28},{7,0},{8,1},{9,29},... | collective-permute-start | bytes 368648 | tf_op jit(solution)/shard_map/ppermute | solution.py:288
  (6 other events, 42.8 us)

commit v17 on v16

--- a/solution.py
+++ b/solution.py
@@ -91,13 +91,22 @@
     return lax.ppermute(x, ("frames", "heads"), pairs)
 
 
-def gather_ring(streams, n):
-    found = [[block] + [None] * (n - 1) for block in streams]
-    for step in range(1, n // 2 + 1):
-        for j, blocks in enumerate(found):
+def held(block, after):
+    return call(copy_kernel, (), [block], [(block.shape, block.dtype)], 0, after)[0]
+
+
+def gather_ring(keys, values, queries, n):
+    found = [[block] + [None] * (n - 1) for block in (keys, values, queries)]
+    far = n // 2
+    for j, blocks in enumerate(found):
+        for step in range(1, far + 1):
             for by in (1, -1):
-                if step < n // 2 or (j % 2 == 0) == (by == 1):
-                    blocks[by * step % n] = hop(blocks[by * (step - 1) % n], n, by)
+                if step < far or by == (1, -1, None)[j]:
+                    block = blocks[by * (step - 1) % n]
+                    if j == 2 and step > 1:
+                        near = (far - 1, far + 1) if step == 2 else (far,)
+                        block = held(block, [found[i][d] for i in range(2) for d in near])
+                    blocks[by * step % n] = hop(block, n, by)
     return found
 
 
@@ -163,6 +172,10 @@
         now = later
 
 
+def copy_kernel(from_ref, *refs):
+    refs[-1][...] = from_ref[...]
+
+
 def split_kernel(kv_ref, keys_ref, values_ref):
     keys_ref[...] = kv_ref[0]
     values_ref[...] = kv_ref[1]
@@ -184,11 +197,10 @@
     attended_ref = refs[-2] if flips else refs[-1]
     marks = frame_marks(at_ref, blocks, n)
     keys_marks = key_marks(range(n), 0, n)
-    places = list(range(count))
-    if before:
-        places = [2]
-        for source, place in enumerate((0, 1, 3)):
-            attended_ref[place] = refs[0][source]
+    for source, place in before:
+        attended_ref[place] = refs[0][source]
+    taken = [place for _, place in before]
+    places = [place for place in range(attended_ref.shape[0]) if place not in taken]
 
     def scores(cols):
         queries = jnp.concatenate([rows_of(query_refs, cols), marks], axis=1)
@@ -246,16 +258,16 @@
     f32, bf16 = jnp.float32, jnp.bfloat16
     block = (queries.shape, bf16)
     own = call(split_kernel, (), [keys_values], [block, block], 0)
-    keys, values, queries = gather_ring([*own, queries], n)
-
-    def attend(blocks, before=(), flips=(), after=()):
-        outs = [((4 if before else len(blocks), ROWS, width), bf16)]
+    keys, values, queries = gather_ring(*own, queries, n)
+
+    def attend(blocks, results=(), before=(), flips=(), after=()):
+        outs = [((len(before) + len(blocks), ROWS, width), bf16)]
         if flips:
             outs.append(((len(flips) * ROWS, cols), bf16))
         return call(
-            functools.partial(attend_kernel, heads, n, blocks, bool(before), flips),
+            functools.partial(attend_kernel, heads, n, blocks, before, flips),
             (where,),
-            [*(queries[d] for d in blocks), *keys, *values, *before, *([out_weight] if flips else [])],
+            [*(queries[d] for d in blocks), *keys, *values, *results, *([out_weight] if flips else [])],
             outs,
             4 * len(blocks) * n * ROWS**2 * width,
             after,
@@ -288,10 +300,12 @@
         return lax.ppermute(total, ("frames", "heads"), pairs)
 
     others = [(1, 1), (0, 1)]
-    (some,) = attend([0, 2, n - 2])
-    attended, given = attend([1, 3, n - 3, n - 1], (), others, (some,))
+    near = attend([0, 1, n - 1])
+    queries[n // 2] = hop(held(queries[n // 2 - 1], near), n, 1)
+    attended, given = attend([3, n - 3], near, [(1, 0), (2, 3)], others)
     odd = send(1, sums(1, attended, given))
-    attended, given = attend([n // 2], (some,), others, (attended,))
+    even = attend([2, n - 2], near, [(0, 0)])
+    attended, given = attend([n // 2], even, [(0, 0), (1, 1), (2, 3)], others, (attended,))
     even = send(0, sums(0, attended, given))
     straight = (head - where[0]) & 1 == 0
     return jnp.concatenate([jnp.where(straight, even, odd), jnp.where(straight, odd, even)], axis=1)

time: 60.4 us -> 67.1 us (1.11)
  the two profiles are of different devices: /device:TPU:3 before, /device:TPU:1 now
where the time goes in v17:
time: 67.1 us; the launch traced here: 67 us
  starting transfers between devices  34.2 us (51%)
  waiting for transfers between devices  19.7 us (29%)
  Pallas kernels  11.2 us (17%)
  local copies, waits for them, and re-layouts  1.04 us (2%)
  other arithmetic  0.74 us (1%)
    ppermute x21, starting transfers between devices, hop(): return lax.ppermute(x, ('frames', 'heads'), pairs)  18.8 us
    ppermute x21, waiting for transfers between devices, hop(): return lax.ppermute(x, ('frames', 'heads'), pairs)  11.5 us
    pallas_call x16, Pallas kernels, call(): pl.pallas_call(kernel, out_shape=[jax.ShapeDtypeStruct(shape, dtype) for...  11.2 us
    ppermute x2, starting transfers between devices, send(): return lax.ppermute(total, ('frames', 'heads'), pairs)  9.42 us
    ppermute x2, waiting for transfers between devices, send(): return lax.ppermute(total, ('frames', 'heads'), pairs)  5.26 us
    ppermute x2, starting transfers between devices, sums(): from_core = lax.ppermute(given, 'heads', [(h, h ^ 1) for h in range(4)])  4.37 us
    ppermute x2, waiting for transfers between devices, sums(): lax.ppermute(add(0, kept, from_core), 'heads', [(h, h ^ 2) for h in range...  2.85 us
    ppermute x2, starting transfers between devices, sums(): lax.ppermute(add(0, kept, from_core), 'heads', [(h, h ^ 2) for h in range...  1.6 us
  transfers between devices with their start and end apart: 27, of which 14 were waited for; matrix products, arithmetic and copies ran while one was open for 0% of the time, Pallas kernels for 17%

profile of v17, /device:TPU:1, one launch (start us, length us, event | category | flops | bytes accessed | tf_op | source)
XLA Modules:
  0.0 67.0 jit_solution(2700364866462705804)
XLA Ops:
  1.0 2.1 %collective-permute-start.1 = (bf16[96,640]{1,0:T(8,128)(2,1)S(1)}, bf16[96,640]{1,0:T(8,128)(2,1)S(1)}, u32[]{:S(2)}, u32[]{:S(2)}) collective-permute-start(bf16[96,640]{1,0:T(8,128)(2,1)S(1)} %get-tuple-element.11.refs_3_.refs_2_.refs_1_), channel_id=1, source_target_pairs={{0,8},{1,5},{2,10},{3,7},{8,16},{9,1},{10,18},{11,3},{16,24},{17,9... | collective-permute-start | bytes 368648 | tf_op jit(solution)/shard_map/ppermute | solution.py:91
  3.2 1.4 %collective-permute-start.4 = (bf16[96,640]{1,0:T(8,128)(2,1)S(1)}, bf16[96,640]{1,0:T(8,128)(2,1)S(1)}, u32[]{:S(2)}, u32[]{:S(2)}) collective-permute-start(bf16[96,640]{1,0:T(8,128)(2,1)S(1)} %get-tuple-element.11.refs_3_.refs_2_.refs_1_), channel_id=1, source_target_pairs={{0,4},{1,9},{2,6},{3,11},{8,0},{9,17},{10,2},{11,19},{16,8},{17,25... | collective-permute-start | bytes 368648 | tf_op jit(solution)/shard_map/ppermute | solution.py:91
  5.7 1.5 %collective-permute-start.2 = (bf16[96,640]{1,0:T(8,128)(2,1)S(1)}, bf16[96,640]{1,0:T(8,128)(2,1)S(1)}, u32[]{:S(2)}, u32[]{:S(2)}) collective-permute-start(bf16[96,640]{1,0:T(8,128)(2,1)S(1)} %collective-permute-done.1.refs_4_.refs_3_.refs_2_), channel_id=1, source_target_pairs={{0,8},{1,5},{2,10},{3,7},{8,16},{9,1},{10,18},{11,3},{16,24},{17,9... | collective-permute-start | bytes 368648 | tf_op jit(solution)/shard_map/ppermute | solution.py:91
  7.8 1.3 %collective-permute-done.4.refs_10_.refs_9_.refs_8_ = bf16[96,640]{1,0:T(8,128)(2,1)S(1)} collective-permute-done((bf16[96,640]{1,0:T(8,128)(2,1)S(1)}, bf16[96,640]{1,0:T(8,128)(2,1)S(1)}, u32[]{:S(2)}, u32[]{:S(2)}) %collective-permute-start.4) | collective-permute-done | bytes 122912 | tf_op jit(solution)/shard_map/ppermute | solution.py:91
  11.2 1.5 %collective-permute-start = (bf16[96,640]{1,0:T(8,128)(2,1)S(1)}, bf16[96,640]{1,0:T(8,128)(2,1)S(1)}, u32[]{:S(2)}, u32[]{:S(2)}) collective-permute-start(bf16[96,640]{1,0:T(8,128)(2,1)S(1)} %copy-done.2), channel_id=1, source_target_pairs={{0,8},{1,5},{2,10},{3,7},{8,16},{9,1},{10,18},{11,3},{16,24},{17,9... | collective-permute-start | bytes 368648 | tf_op jit(solution)/shard_map/ppermute | solution.py:91
  12.6 1.3 %collective-permute-start.3 = (bf16[96,640]{1,0:T(8,128)(2,1)S(1)}, bf16[96,640]{1,0:T(8,128)(2,1)S(1)}, u32[]{:S(2)}, u32[]{:S(2)}) collective-permute-start(bf16[96,640]{1,0:T(8,128)(2,1)S(1)} %collective-permute-done.2.refs_5_.refs_4_.refs_3_), channel_id=1, source_target_pairs={{0,8},{1,5},{2,10},{3,7},{8,16},{9,1},{10,18},{11,3},{16,24},{17,9... | collective-permute-start | bytes 368648 | tf_op jit(solution)/shard_map/ppermute | solution.py:91
  16.2 1.3 %collective-permute-done.from_ref.refs_1_ = bf16[96,640]{1,0:T(8,128)(2,1)S(1)} collective-permute-done((bf16[96,640]{1,0:T(8,128)(2,1)S(1)}, bf16[96,640]{1,0:T(8,128)(2,1)S(1)}, u32[]{:S(2)}, u32[]{:S(2)}) %collective-permute-start) | collective-permute-done | bytes 122912 | tf_op jit(solution)/shard_map/ppermute | solution.py:91
  17.5 1.6 %collective-permute-start.17 = (bf16[96,640]{1,0:T(8,128)(2,1)S(1)}, bf16[96,640]{1,0:T(8,128)(2,1)S(1)}, u32[]{:S(2)}, u32[]{:S(2)}) collective-permute-start(bf16[96,640]{1,0:T(8,128)(2,1)S(1)} %copy-done.2), channel_id=1, source_target_pairs={{0,4},{1,9},{2,6},{3,11},{8,0},{9,17},{10,2},{11,19},{16,8},{17,25... | collective-permute-start | bytes 368648 | tf_op jit(solution)/shard_map/ppermute | solution.py:91
  19.8 1.1 %collective-permute-start.15 = (bf16[96,640]{1,0:T(8,128)(2,1)S(1)}, bf16[96,640]{1,0:T(8,128)(2,1)S(1)}, u32[]{:S(2)}, u32[]{:S(2)}) collective-permute-start(bf16[96,640]{1,0:T(8,128)(2,1)S(1)} %collective-permute-done.12.refs_3_.refs_16_.refs_15_.refs_14_), channel_id=1, source_target_pairs={{0,4},{1,9},{2,6},{3,11},{8,0},{9,17},{10,2},{11,19},{16,8},{17,25... | collective-permute-start | bytes 368648 | tf_op jit(solution)/shard_map/ppermute | solution.py:91
  21.9 1.4 %collective-permute-start.13 = (bf16[96,640]{1,0:T(8,128)(2,1)S(1)}, bf16[96,640]{1,0:T(8,128)(2,1)S(1)}, u32[]{:S(2)}, u32[]{:S(2)}) collective-permute-start(bf16[96,640]{1,0:T(8,128)(2,1)S(1)} %shard_map.38), channel_id=1, source_target_pairs={{0,8},{1,5},{2,10},{3,7},{8,16},{9,1},{10,18},{11,3},{16,24},{17,9... | collective-permute-start | bytes 368648 | tf_op jit(solution)/shard_map/ppermute | solution.py:91
  23.3 1.2 %collective-permute-done.17.refs_2_.from_ref = bf16[96,640]{1,0:T(8,128)(2,1)S(1)} collective-permute-done((bf16[96,640]{1,0:T(8,128)(2,1)S(1)}, bf16[96,640]{1,0:T(8,128)(2,1)S(1)}, u32[]{:S(2)}, u32[]{:S(2)}) %collective-permute-start.17) | collective-permute-done | bytes 122912 | tf_op jit(solution)/shard_map/ppermute | solution.py:91
  24.8 1.8 %collective-permute-done.15.refs_1_.refs_15_.refs_14_.refs_13_ = bf16[96,640]{1,0:T(8,128)(2,1)S(1)} collective-permute-done((bf16[96,640]{1,0:T(8,128)(2,1)S(1)}, bf16[96,640]{1,0:T(8,128)(2,1)S(1)}, u32[]{:S(2)}, u32[]{:S(2)}) %collective-permute-start.15) | collective-permute-done | bytes 122912 | tf_op jit(solution)/shard_map/ppermute | solution.py:91
  28.5 1.4 %collective-permute-done.19.refs_1_.from_ref = bf16[96,640]{1,0:T(8,128)(2,1)S(1)} collective-permute-done((bf16[96,640]{1,0:T(8,128)(2,1)S(1)}, bf16[96,640]{1,0:T(8,128)(2,1)S(1)}, u32[]{:S(2)}, u32[]{:S(2)}) %collective-permute-start.19) | collective-permute-done | bytes 122912 | tf_op jit(solution)/shard_map/ppermute | solution.py:91
  30.0 2.3 %shard_map.40.refs_0_.refs_18_ = bf16[3,96,640]{2,1,0:T(8,128)(2,1)S(1)} custom-call(s32[5]{0:T(128)S(1)} %stack.23.at_ref, bf16[96,640]{1,0:T(8,128)(2,1)S(1)} %copy-done.2, bf16[96,640]{1,0:T(8,128)(2,1)S(1)} %collective-permute-done.from_ref.refs_1_, bf16[96,640]{1,0:T(8,128)(2,1)S(1)} %collective-permute-done.17.refs_2_.from_ref, ...), custom_call_target="tpu_custom_call" | custom-call | flops 566231040 | tf_op jit(solution)/shard_map/pallas_call | solution.py:239
  32.3 1.5 %collective-permute-start.18 = (bf16[96,640]{1,0:T(8,128)(2,1)S(1)}, bf16[96,640]{1,0:T(8,128)(2,1)S(1)}, u32[]{:S(2)}, u32[]{:S(2)}) collective-permute-start(bf16[96,640]{1,0:T(8,128)(2,1)S(1)} %shard_map.41), channel_id=1, source_target_pairs={{0,8},{1,5},{2,10},{3,7},{8,16},{9,1},{10,18},{11,3},{16,24},{17,9... | collective-permute-start | bytes 368648 | tf_op jit(solution)/shard_map/ppermute | solution.py:91
  33.8 2.0 %shard_map.43.refs_17_ = bf16[3,96,640]{2,1,0:T(8,128)(2,1)S(1)} custom-call(s32[5]{0:T(128)S(1)} %stack.23.at_ref, bf16[96,640]{1,0:T(8,128)(2,1)S(1)} %collective-permute-done.13.from_ref.refs_0_, bf16[96,640]{1,0:T(8,128)(2,1)S(1)} %collective-permute-done.19.refs_1_.from_ref, bf16[96,640]{1,0:T(8,128)(2,1)S(1)} %get-tuple-element.11.refs_3_.refs_2_.refs_1_, ...), custom_call_target="tpu_custom_call" | custom-call | flops 377487360 | tf_op jit(solution)/shard_map/pallas_call | solution.py:239
  35.8 2.5 %shard_map.45 = (bf16[4,96,640]{2,1,0:T(8,128)(2,1)S(1)}, bf16[192,640]{1,0:T(8,128)(2,1)S(1)}) custom-call(s32[5]{0:T(128)S(1)} %stack.23.at_ref, bf16[96,640]{1,0:T(8,128)(2,1)S(1)} %collective-permute-done.16.from_ref.refs_0_, bf16[96,640]{1,0:T(8,128)(2,1)S(1)} %collective-permute-done.20.refs_1_, ...), custom_call_target="tpu_custom_call" | custom-call | flops 377487360 | tf_op jit(solution)/shard_map/pallas_call | solution.py:239
  38.3 4.3 %collective-permute-start.24 = (bf16[192,640]{1,0:T(8,128)(2,1)S(1)}, bf16[192,640]{1,0:T(8,128)(2,1)S(1)}, u32[]{:S(2)}, u32[]{:S(2)}) collective-permute-start(bf16[192,640]{1,0:T(8,128)(2,1)S(1)} %get-tuple-element.16), channel_id=1, source_target_pairs={{0,1},{1,0},{2,3},{3,2},{4,5},{5,4},{6,7},{7,6},{8,9},{9,8},{10,11... | collective-permute-start | bytes 737288 | tf_op jit(solution)/shard_map/ppermute | solution.py:281
  42.6 2.3 %shard_map.46 = (bf16[4,96,640]{2,1,0:T(8,128)(2,1)S(1)}, bf16[192,640]{1,0:T(8,128)(2,1)S(1)}) custom-call(s32[5]{0:T(128)S(1)} %stack.23.at_ref, bf16[96,640]{1,0:T(8,128)(2,1)S(1)} %collective-permute-done.18.refs_0_, bf16[96,640]{1,0:T(8,128)(2,1)S(1)} %get-tuple-element.11.refs_3_.refs_2_.refs_1_, ...), custom_call_target="tpu_custom_call" | custom-call | flops 188743680 | tf_op jit(solution)/shard_map/pallas_call | solution.py:239
  46.9 1.3 %collective-permute-start.25 = (bf16[96,640]{1,0:T(8,128)(2,1)S(1)}, bf16[96,640]{1,0:T(8,128)(2,1)S(1)}, u32[]{:S(2)}, u32[]{:S(2)}) collective-permute-start(bf16[96,640]{1,0:T(8,128)(2,1)S(1)} %shard_map.51), channel_id=1, source_target_pairs={{0,2},{1,3},{2,0},{3,1},{4,6},{5,7},{6,4},{7,5},{8,10},{9,11},{10,... | collective-permute-start | bytes 368648 | tf_op jit(solution)/shard_map/ppermute | solution.py:290
  48.6 2.8 %collective-permute-done.25.refs_0_ = bf16[96,640]{1,0:T(8,128)(2,1)S(1)} collective-permute-done((bf16[96,640]{1,0:T(8,128)(2,1)S(1)}, bf16[96,640]{1,0:T(8,128)(2,1)S(1)}, u32[]{:S(2)}, u32[]{:S(2)}) %collective-permute-start.25) | collective-permute-done | bytes 122912 | tf_op jit(solution)/shard_map/ppermute | solution.py:290
  51.5 6.0 %collective-permute-start.26 = (bf16[96,640]{1,0:T(8,128)(2,1)S(1)}, bf16[96,640]{1,0:T(8,128)(2,1)S(1)}, u32[]{:S(2)}, u32[]{:S(2)}) collective-permute-start(bf16[96,640]{1,0:T(8,128)(2,1)S(1)} %shard_map.52), channel_id=1, source_target_pairs={{0,4},{1,24},{2,20},{3,8},{4,12},{5,16},{6,28},{7,0},{8,1},{9,29},... | collective-permute-start | bytes 368648 | tf_op jit(solution)/shard_map/ppermute | solution.py:300
  57.5 3.5 %collective-permute-start.23 = (bf16[96,640]{1,0:T(8,128)(2,1)S(1)}, bf16[96,640]{1,0:T(8,128)(2,1)S(1)}, u32[]{:S(2)}, u32[]{:S(2)}) collective-permute-start(bf16[96,640]{1,0:T(8,128)(2,1)S(1)} %shard_map.49), channel_id=1, source_target_pairs={{0,0},{1,28},{2,12},{3,16},{4,4},{5,24},{6,20},{7,8},{8,9},{9,21},... | collective-permute-start | bytes 368648 | tf_op jit(solution)/shard_map/ppermute | solution.py:300
  61.0 5.3 %collective-permute-done.23 = bf16[96,640]{1,0:T(8,128)(2,1)S(1)} collective-permute-done((bf16[96,640]{1,0:T(8,128)(2,1)S(1)}, bf16[96,640]{1,0:T(8,128)(2,1)S(1)}, u32[]{:S(2)}, u32[]{:S(2)}) %collective-permute-start.23) | collective-permute-done | bytes 122912 | tf_op jit(solution)/shard_map/ppermute | solution.py:300
  (55 shorter events, 14.2 us)
Async XLA Ops:
  1.0 4.7 %collective-permute-start.1 = (bf16[96,640]{1,0:T(8,128)(2,1)S(1)}, bf16[96,640]{1,0:T(8,128)(2,1)S(1)}, u32[]{:S(2)}, u32[]{:S(2)}) collective-permute-start(bf16[96,640]{1,0:T(8,128)(2,1)S(1)} %get-tuple-element.11.refs_3_.refs_2_.refs_1_), channel_id=1, source_target_pairs={{0,8},{1,5},{2,10},{3,7},{8,16},{9,1},{10,18},{11,3},{16,24},{17,9... | collective-permute-start | bytes 368648 | tf_op jit(solution)/shard_map/ppermute | solution.py:91
  3.2 5.9 %collective-permute-start.4 = (bf16[96,640]{1,0:T(8,128)(2,1)S(1)}, bf16[96,640]{1,0:T(8,128)(2,1)S(1)}, u32[]{:S(2)}, u32[]{:S(2)}) collective-permute-start(bf16[96,640]{1,0:T(8,128)(2,1)S(1)} %get-tuple-element.11.refs_3_.refs_2_.refs_1_), channel_id=1, source_target_pairs={{0,4},{1,9},{2,6},{3,11},{8,0},{9,17},{10,2},{11,19},{16,8},{17,25... | collective-permute-start | bytes 368648 | tf_op jit(solution)/shard_map/ppermute | solution.py:91
  4.6 5.5 %collective-permute-start.7 = (bf16[96,640]{1,0:T(8,128)(2,1)S(1)}, bf16[96,640]{1,0:T(8,128)(2,1)S(1)}, u32[]{:S(2)}, u32[]{:S(2)}) collective-permute-start(bf16[96,640]{1,0:T(8,128)(2,1)S(1)} %get-tuple-element.12.refs_11_.refs_10_.refs_9_), channel_id=1, source_target_pairs={{0,8},{1,5},{2,10},{3,7},{8,16},{9,1},{10,18},{11,3},{16,24},{17,9... | collective-permute-start | bytes 368648 | tf_op jit(solution)/shard_map/ppermute | solution.py:91
  5.7 6.9 %collective-permute-start.2 = (bf16[96,640]{1,0:T(8,128)(2,1)S(1)}, bf16[96,640]{1,0:T(8,128)(2,1)S(1)}, u32[]{:S(2)}, u32[]{:S(2)}) collective-permute-start(bf16[96,640]{1,0:T(8,128)(2,1)S(1)} %collective-permute-done.1.refs_4_.refs_3_.refs_2_), channel_id=1, source_target_pairs={{0,8},{1,5},{2,10},{3,7},{8,16},{9,1},{10,18},{11,3},{16,24},{17,9... | collective-permute-start | bytes 368648 | tf_op jit(solution)/shard_map/ppermute | solution.py:91
  7.8 6.1 %collective-permute-start.11 = (bf16[96,640]{1,0:T(8,128)(2,1)S(1)}, bf16[96,640]{1,0:T(8,128)(2,1)S(1)}, u32[]{:S(2)}, u32[]{:S(2)}) collective-permute-start(bf16[96,640]{1,0:T(8,128)(2,1)S(1)} %collective-permute-done.10.refs_18_.refs_17_.refs_16_), channel_id=1, source_target_pairs={{0,4},{1,9},{2,6},{3,11},{8,0},{9,17},{10,2},{11,19},{16,8},{17,25... | collective-permute-start | bytes 368648 | tf_op jit(solution)/shard_map/ppermute | solution.py:91
  9.1 5.6 %collective-permute-start.5 = (bf16[96,640]{1,0:T(8,128)(2,1)S(1)}, bf16[96,640]{1,0:T(8,128)(2,1)S(1)}, u32[]{:S(2)}, u32[]{:S(2)}) collective-permute-start(bf16[96,640]{1,0:T(8,128)(2,1)S(1)} %collective-permute-done.4.refs_10_.refs_9_.refs_8_), channel_id=1, source_target_pairs={{0,4},{1,9},{2,6},{3,11},{8,0},{9,17},{10,2},{11,19},{16,8},{17,25... | collective-permute-start | bytes 368648 | tf_op jit(solution)/shard_map/ppermute | solution.py:91
  10.1 5.2 %collective-permute-start.8 = (bf16[96,640]{1,0:T(8,128)(2,1)S(1)}, bf16[96,640]{1,0:T(8,128)(2,1)S(1)}, u32[]{:S(2)}, u32[]{:S(2)}) collective-permute-start(bf16[96,640]{1,0:T(8,128)(2,1)S(1)} %collective-permute-done.7.refs_12_.refs_11_.refs_10_), channel_id=1, source_target_pairs={{0,8},{1,5},{2,10},{3,7},{8,16},{9,1},{10,18},{11,3},{16,24},{17,9... | collective-permute-start | bytes 368648 | tf_op jit(solution)/shard_map/ppermute | solution.py:91
  11.2 6.4 %collective-permute-start = (bf16[96,640]{1,0:T(8,128)(2,1)S(1)}, bf16[96,640]{1,0:T(8,128)(2,1)S(1)}, u32[]{:S(2)}, u32[]{:S(2)}) collective-permute-start(bf16[96,640]{1,0:T(8,128)(2,1)S(1)} %copy-done.2), channel_id=1, source_target_pairs={{0,8},{1,5},{2,10},{3,7},{8,16},{9,1},{10,18},{11,3},{16,24},{17,9... | collective-permute-start | bytes 368648 | tf_op jit(solution)/shard_map/ppermute | solution.py:91
  12.6 6.8 %collective-permute-start.3 = (bf16[96,640]{1,0:T(8,128)(2,1)S(1)}, bf16[96,640]{1,0:T(8,128)(2,1)S(1)}, u32[]{:S(2)}, u32[]{:S(2)}) collective-permute-start(bf16[96,640]{1,0:T(8,128)(2,1)S(1)} %collective-permute-done.2.refs_5_.refs_4_.refs_3_), channel_id=1, source_target_pairs={{0,8},{1,5},{2,10},{3,7},{8,16},{9,1},{10,18},{11,3},{16,24},{17,9... | collective-permute-start | bytes 368648 | tf_op jit(solution)/shard_map/ppermute | solution.py:91
  13.9 5.8 %collective-permute-start.12 = (bf16[96,640]{1,0:T(8,128)(2,1)S(1)}, bf16[96,640]{1,0:T(8,128)(2,1)S(1)}, u32[]{:S(2)}, u32[]{:S(2)}) collective-permute-start(bf16[96,640]{1,0:T(8,128)(2,1)S(1)} %collective-permute-done.11.refs_17_.refs_16_.refs_15_), channel_id=1, source_target_pairs={{0,4},{1,9},{2,6},{3,11},{8,0},{9,17},{10,2},{11,19},{16,8},{17,25... | collective-permute-start | bytes 368648 | tf_op jit(solution)/shard_map/ppermute | solution.py:91
  14.8 7.1 %collective-permute-start.6 = (bf16[96,640]{1,0:T(8,128)(2,1)S(1)}, bf16[96,640]{1,0:T(8,128)(2,1)S(1)}, u32[]{:S(2)}, u32[]{:S(2)}) collective-permute-start(bf16[96,640]{1,0:T(8,128)(2,1)S(1)} %collective-permute-done.5.refs_9_.refs_8_.refs_7_), channel_id=1, source_target_pairs={{0,4},{1,9},{2,6},{3,11},{8,0},{9,17},{10,2},{11,19},{16,8},{17,25... | collective-permute-start | bytes 368648 | tf_op jit(solution)/shard_map/ppermute | solution.py:91
  15.3 6.5 %collective-permute-start.9 = (bf16[96,640]{1,0:T(8,128)(2,1)S(1)}, bf16[96,640]{1,0:T(8,128)(2,1)S(1)}, u32[]{:S(2)}, u32[]{:S(2)}) collective-permute-start(bf16[96,640]{1,0:T(8,128)(2,1)S(1)} %collective-permute-done.8.refs_13_.refs_12_.refs_11_), channel_id=1, source_target_pairs={{0,8},{1,5},{2,10},{3,7},{8,16},{9,1},{10,18},{11,3},{16,24},{17,9... | collective-permute-start | bytes 368648 | tf_op jit(solution)/shard_map/ppermute | solution.py:91
  17.5 7.0 %collective-permute-start.17 = (bf16[96,640]{1,0:T(8,128)(2,1)S(1)}, bf16[96,640]{1,0:T(8,128)(2,1)S(1)}, u32[]{:S(2)}, u32[]{:S(2)}) collective-permute-start(bf16[96,640]{1,0:T(8,128)(2,1)S(1)} %copy-done.2), channel_id=1, source_target_pairs={{0,4},{1,9},{2,6},{3,11},{8,0},{9,17},{10,2},{11,19},{16,8},{17,25... | collective-permute-start | bytes 368648 | tf_op jit(solution)/shard_map/ppermute | solution.py:91
  19.5 5.3 %collective-permute-start.14 = (bf16[96,640]{1,0:T(8,128)(2,1)S(1)}, bf16[96,640]{1,0:T(8,128)(2,1)S(1)}, u32[]{:S(2)}, u32[]{:S(2)}) collective-permute-start(bf16[96,640]{1,0:T(8,128)(2,1)S(1)} %collective-permute-done.3.refs_0_.refs_6_.refs_5_.refs_4_), channel_id=1, source_target_pairs={{0,8},{1,5},{2,10},{3,7},{8,16},{9,1},{10,18},{11,3},{16,24},{17,9... | collective-permute-start | bytes 368648 | tf_op jit(solution)/shard_map/ppermute | solution.py:91
  19.8 6.8 %collective-permute-start.15 = (bf16[96,640]{1,0:T(8,128)(2,1)S(1)}, bf16[96,640]{1,0:T(8,128)(2,1)S(1)}, u32[]{:S(2)}, u32[]{:S(2)}) collective-permute-start(bf16[96,640]{1,0:T(8,128)(2,1)S(1)} %collective-permute-done.12.refs_3_.refs_16_.refs_15_.refs_14_), channel_id=1, source_target_pairs={{0,4},{1,9},{2,6},{3,11},{8,0},{9,17},{10,2},{11,19},{16,8},{17,25... | collective-permute-start | bytes 368648 | tf_op jit(solution)/shard_map/ppermute | solution.py:91
  21.9 5.5 %collective-permute-start.13 = (bf16[96,640]{1,0:T(8,128)(2,1)S(1)}, bf16[96,640]{1,0:T(8,128)(2,1)S(1)}, u32[]{:S(2)}, u32[]{:S(2)}) collective-permute-start(bf16[96,640]{1,0:T(8,128)(2,1)S(1)} %shard_map.38), channel_id=1, source_target_pairs={{0,8},{1,5},{2,10},{3,7},{8,16},{9,1},{10,18},{11,3},{16,24},{17,9... | collective-permute-start | bytes 368648 | tf_op jit(solution)/shard_map/ppermute | solution.py:91
  24.5 5.4 %collective-permute-start.19 = (bf16[96,640]{1,0:T(8,128)(2,1)S(1)}, bf16[96,640]{1,0:T(8,128)(2,1)S(1)}, u32[]{:S(2)}, u32[]{:S(2)}) collective-permute-start(bf16[96,640]{1,0:T(8,128)(2,1)S(1)} %shard_map.42), channel_id=1, source_target_pairs={{0,4},{1,9},{2,6},{3,11},{8,0},{9,17},{10,2},{11,19},{16,8},{17,25... | collective-permute-start | bytes 368648 | tf_op jit(solution)/shard_map/ppermute | solution.py:91
  27.4 4.8 %collective-permute-start.16 = (bf16[96,640]{1,0:T(8,128)(2,1)S(1)}, bf16[96,640]{1,0:T(8,128)(2,1)S(1)}, u32[]{:S(2)}, u32[]{:S(2)}) collective-permute-start(bf16[96,640]{1,0:T(8,128)(2,1)S(1)} %shard_map.39), channel_id=1, source_target_pairs={{0,8},{1,5},{2,10},{3,7},{8,16},{9,1},{10,18},{11,3},{16,24},{17,9... | collective-permute-start | bytes 368648 | tf_op jit(solution)/shard_map/ppermute | solution.py:91
  29.9 5.9 %collective-permute-start.20 = (bf16[96,640]{1,0:T(8,128)(2,1)S(1)}, bf16[96,640]{1,0:T(8,128)(2,1)S(1)}, u32[]{:S(2)}, u32[]{:S(2)}) collective-permute-start(bf16[96,640]{1,0:T(8,128)(2,1)S(1)} %shard_map.44), channel_id=1, source_target_pairs={{0,4},{1,9},{2,6},{3,11},{8,0},{9,17},{10,2},{11,19},{16,8},{17,25... | collective-permute-start | bytes 368648 | tf_op jit(solution)/shard_map/ppermute | solution.py:91
  32.3 10.3 %collective-permute-start.18 = (bf16[96,640]{1,0:T(8,128)(2,1)S(1)}, bf16[96,640]{1,0:T(8,128)(2,1)S(1)}, u32[]{:S(2)}, u32[]{:S(2)}) collective-permute-start(bf16[96,640]{1,0:T(8,128)(2,1)S(1)} %shard_map.41), channel_id=1, source_target_pairs={{0,8},{1,5},{2,10},{3,7},{8,16},{9,1},{10,18},{11,3},{16,24},{17,9... | collective-permute-start | bytes 368648 | tf_op jit(solution)/shard_map/ppermute | solution.py:91
  38.3 8.6 %collective-permute-start.24 = (bf16[192,640]{1,0:T(8,128)(2,1)S(1)}, bf16[192,640]{1,0:T(8,128)(2,1)S(1)}, u32[]{:S(2)}, u32[]{:S(2)}) collective-permute-start(bf16[192,640]{1,0:T(8,128)(2,1)S(1)} %get-tuple-element.16), channel_id=1, source_target_pairs={{0,1},{1,0},{2,3},{3,2},{4,5},{5,4},{6,7},{7,6},{8,9},{9,8},{10,11... | collective-permute-start | bytes 737288 | tf_op jit(solution)/shard_map/ppermute | solution.py:281
  48.2 9.2 %collective-permute-start.22 = (bf16[96,640]{1,0:T(8,128)(2,1)S(1)}, bf16[96,640]{1,0:T(8,128)(2,1)S(1)}, u32[]{:S(2)}, u32[]{:S(2)}) collective-permute-start(bf16[96,640]{1,0:T(8,128)(2,1)S(1)} %shard_map.48), channel_id=1, source_target_pairs={{0,2},{1,3},{2,0},{3,1},{4,6},{5,7},{6,4},{7,5},{8,10},{9,11},{10,... | collective-permute-start | bytes 368648 | tf_op jit(solution)/shard_map/ppermute | solution.py:290
  51.5 9.5 %collective-permute-start.26 = (bf16[96,640]{1,0:T(8,128)(2,1)S(1)}, bf16[96,640]{1,0:T(8,128)(2,1)S(1)}, u32[]{:S(2)}, u32[]{:S(2)}) collective-permute-start(bf16[96,640]{1,0:T(8,128)(2,1)S(1)} %shard_map.52), channel_id=1, source_target_pairs={{0,4},{1,24},{2,20},{3,8},{4,12},{5,16},{6,28},{7,0},{8,1},{9,29},... | collective-permute-start | bytes 368648 | tf_op jit(solution)/shard_map/ppermute | solution.py:300
  57.5 8.7 %collective-permute-start.23 = (bf16[96,640]{1,0:T(8,128)(2,1)S(1)}, bf16[96,640]{1,0:T(8,128)(2,1)S(1)}, u32[]{:S(2)}, u32[]{:S(2)}) collective-permute-start(bf16[96,640]{1,0:T(8,128)(2,1)S(1)} %shard_map.49), channel_id=1, source_target_pairs={{0,0},{1,28},{2,12},{3,16},{4,4},{5,24},{6,20},{7,8},{8,9},{9,21},... | collective-permute-start | bytes 368648 | tf_op jit(solution)/shard_map/ppermute | solution.py:300
  (6 other events, 27.2 us)

commit v18 on v14

--- a/solution.py
+++ b/solution.py
@@ -154,7 +154,7 @@
     return mixed[:, :HD], mixed[:, HD:]
 
 
-PATTERNS = ((2, 1, 2, 1), (0, 3, 0, 3), (3, 0, 1, 2), (1, 2, 3, 0))
+PATTERNS = ((3, 0, 2, 1), (1, 3, 1, 3), (2, 1, 3, 0), (0, 2, 0, 2))
 
 
 def look_up(table, index):
@@ -213,21 +213,20 @@
     blocks = [block for flip in flips for block in slot_blocks(at_ref, *flip, n)]
     marks = frame_marks(at_ref, blocks, n)
     keys_marks = key_marks([n // 2], TPF, n)
-    attended = []
 
     def of(ref, head):
         return jnp.concatenate([ref[head, block] for block in blocks], axis=0)
 
-    def scores(cols):
+    columns = [slice(head * HD, (head + 1) * HD) for head in range(heads)]
+    scores, attended = [], []
+    for cols in columns:
         queries = jnp.concatenate([rows_ref[block, :, cols] for block in blocks], axis=0)
         keys = jnp.concatenate([rows_of([keys_ref], cols, TPF), keys_marks], axis=1)
-        return scores_of(jnp.concatenate([queries, marks], axis=1), keys)
-
-    for head, cols, now in ahead(scores, heads):
-        before = of(top_ref, head)
-        weights, top = soften(now, before)
-        mixed, total = mix(weights, rows_of([values_ref], cols, TPF))
-        kept = jnp.exp2((before - top) * SCALE)
+        scores.append(scores_of(jnp.concatenate([queries, marks], axis=1), keys))
+    softened = [soften(now, of(top_ref, head)) for head, now in enumerate(scores)]
+    more = [mix(weights, rows_of([values_ref], cols, TPF)) for (weights, _), cols in zip(softened, columns)]
+    for head, ((_, top), (mixed, total)) in enumerate(zip(softened, more)):
+        kept = jnp.exp2((of(top_ref, head) - top) * SCALE)
         mixed, total = mixed + of(mixed_ref, head) * kept, total + of(sum_ref, head) * kept
         attended.append((mixed / total).astype(jnp.bfloat16))
     rows = jnp.concatenate(attended, axis=1)

time: 59.1 us -> 57 us (0.964)
  waiting for transfers between devices: 16.1 us -> 14.3 us
  starting transfers between devices: 30.1 us -> 29.4 us
    ppermute x2, waiting for transfers between devices: 6.45 us -> 4.52 us  [on_device_ring(): arrived.append(lax.ppermute(total, ('frames', 'heads'), pairs))]
    ppermute x2, starting transfers between devices: 7.41 us -> 6.79 us  [on_device_ring(): arrived.append(lax.ppermute(total, ('frames', 'heads'), pairs))]
where the time goes in v18:
time: 57 us; the launch traced here: 56 us
  starting transfers between devices  29.4 us (52%)
  waiting for transfers between devices  14.3 us (25%)
  Pallas kernels  9.43 us (17%)
  local copies, waits for them, and re-layouts  1.94 us (3%)
  other arithmetic  0.79 us (1%)
    ppermute x21, starting transfers between devices, hop(): return lax.ppermute(x, ('frames', 'heads'), pairs)  17.9 us
    pallas_call x8, Pallas kernels, call(): pl.pallas_call(kernel, out_shape=[jax.ShapeDtypeStruct(shape, dtype) for...  9.43 us
    ppermute x21, waiting for transfers between devices, hop(): return lax.ppermute(x, ('frames', 'heads'), pairs)  8.01 us
    ppermute x2, starting transfers between devices, on_device_ring(): arrived.append(lax.ppermute(total, ('frames', 'heads'), pairs))  6.79 us
    ppermute x2, waiting for transfers between devices, on_device_ring(): arrived.append(lax.ppermute(total, ('frames', 'heads'), pairs))  4.52 us
    ppermute x1, starting transfers between devices, on_device_ring(): from_core = lax.ppermute(given, 'heads', [(h, h ^ 1) for h in range(4)])  3.17 us
    unnamed x6, local copies, waits for them, and re-layouts  1.85 us
    ppermute x2, waiting for transfers between devices, on_device_ring(): lax.ppermute(block, 'heads', [(h, h ^ 2) for h in range(4)])  1.68 us
  transfers between devices with their start and end apart: 26, of which 15 were waited for; matrix products, arithmetic and copies ran while one was open for 0% of the time, Pallas kernels for 13%

profile of v18, /device:TPU:3, one launch (start us, length us, event | category | flops | bytes accessed | tf_op | source)
XLA Modules:
  0.0 56.0 jit_solution(16803456933706287048)
XLA Ops:
  0.0 1.2 %collective-permute-start = (bf16[96,640]{1,0:T(8,128)(2,1)}, bf16[96,640]{1,0:T(8,128)(2,1)S(1)}, u32[]{:S(2)}, u32[]{:S(2)}) collective-permute-start(bf16[96,640]{1,0:T(8,128)(2,1)} %refs_0_.1), channel_id=1, source_target_pairs={{0,8},{1,5},{2,10},{3,7},{8,16},{9,1},{10,18},{11,3},{16,24},{17,9... | collective-permute-start | bytes 368648 | tf_op jit(solution)/shard_map/ppermute | solution.py:91
  2.4 1.3 %collective-permute-start.10 = (bf16[96,640]{1,0:T(8,128)(2,1)S(1)}, bf16[96,640]{1,0:T(8,128)(2,1)S(1)}, u32[]{:S(2)}, u32[]{:S(2)}) collective-permute-start(bf16[96,640]{1,0:T(8,128)(2,1)S(1)} %get-tuple-element.10.refs_0_), channel_id=1, source_target_pairs={{0,4},{1,9},{2,6},{3,11},{8,0},{9,17},{10,2},{11,19},{16,8},{17,25... | collective-permute-start | bytes 368648 | tf_op jit(solution)/shard_map/ppermute | solution.py:91
  4.0 1.3 %collective-permute-start.16 = (bf16[96,640]{1,0:T(8,128)(2,1)S(1)}, bf16[96,640]{1,0:T(8,128)(2,1)S(1)}, u32[]{:S(2)}, u32[]{:S(2)}) collective-permute-start(bf16[96,640]{1,0:T(8,128)(2,1)S(1)} %get-tuple-element.11.refs_7_), channel_id=1, source_target_pairs={{0,4},{1,9},{2,6},{3,11},{8,0},{9,17},{10,2},{11,19},{16,8},{17,25... | collective-permute-start | bytes 368648 | tf_op jit(solution)/shard_map/ppermute | solution.py:91
  5.5 1.2 %collective-permute-done.4.refs_7_ = bf16[96,640]{1,0:T(8,128)(2,1)S(1)} collective-permute-done((bf16[96,640]{1,0:T(8,128)(2,1)}, bf16[96,640]{1,0:T(8,128)(2,1)S(1)}, u32[]{:S(2)}, u32[]{:S(2)}) %collective-permute-start.4) | collective-permute-done | bytes 122912 | tf_op jit(solution)/shard_map/ppermute | solution.py:91
  9.1 1.3 %collective-permute-start.11 = (bf16[96,640]{1,0:T(8,128)(2,1)S(1)}, bf16[96,640]{1,0:T(8,128)(2,1)S(1)}, u32[]{:S(2)}, u32[]{:S(2)}) collective-permute-start(bf16[96,640]{1,0:T(8,128)(2,1)S(1)} %collective-permute-done.10.refs_6_), channel_id=1, source_target_pairs={{0,4},{1,9},{2,6},{3,11},{8,0},{9,17},{10,2},{11,19},{16,8},{17,25... | collective-permute-start | bytes 368648 | tf_op jit(solution)/shard_map/ppermute | solution.py:91
  11.7 1.3 %collective-permute-start.17 = (bf16[96,640]{1,0:T(8,128)(2,1)S(1)}, bf16[96,640]{1,0:T(8,128)(2,1)S(1)}, u32[]{:S(2)}, u32[]{:S(2)}) collective-permute-start(bf16[96,640]{1,0:T(8,128)(2,1)S(1)} %collective-permute-done.16.refs_13_), channel_id=1, source_target_pairs={{0,4},{1,9},{2,6},{3,11},{8,0},{9,17},{10,2},{11,19},{16,8},{17,25... | collective-permute-start | bytes 368648 | tf_op jit(solution)/shard_map/ppermute | solution.py:91
  13.7 1.2 %collective-permute-start.8 = (bf16[96,640]{1,0:T(8,128)(2,1)S(1)}, bf16[96,640]{1,0:T(8,128)(2,1)S(1)}, u32[]{:S(2)}, u32[]{:S(2)}) collective-permute-start(bf16[96,640]{1,0:T(8,128)(2,1)S(1)} %collective-permute-done.7.refs_1_), channel_id=1, source_target_pairs={{0,8},{1,5},{2,10},{3,7},{8,16},{9,1},{10,18},{11,3},{16,24},{17,9... | collective-permute-start | bytes 368648 | tf_op jit(solution)/shard_map/ppermute | solution.py:91
  16.3 1.3 %collective-permute-start.12 = (bf16[96,640]{1,0:T(8,128)(2,1)S(1)}, bf16[96,640]{1,0:T(8,128)(2,1)S(1)}, u32[]{:S(2)}, u32[]{:S(2)}) collective-permute-start(bf16[96,640]{1,0:T(8,128)(2,1)S(1)} %collective-permute-done.11.refs_5_), channel_id=1, source_target_pairs={{0,4},{1,9},{2,6},{3,11},{8,0},{9,17},{10,2},{11,19},{16,8},{17,25... | collective-permute-start | bytes 368648 | tf_op jit(solution)/shard_map/ppermute | solution.py:91
  18.1 1.2 %collective-permute-start.15 = (bf16[96,640]{1,0:T(8,128)(2,1)S(1)}, bf16[96,640]{1,0:T(8,128)(2,1)S(1)}, u32[]{:S(2)}, u32[]{:S(2)}) collective-permute-start(bf16[96,640]{1,0:T(8,128)(2,1)S(1)} %collective-permute-done.14.refs_9_), channel_id=1, source_target_pairs={{0,8},{1,5},{2,10},{3,7},{8,16},{9,1},{10,18},{11,3},{16,24},{17,9... | collective-permute-start | bytes 368648 | tf_op jit(solution)/shard_map/ppermute | solution.py:91
  19.3 1.3 %collective-permute-start.3 = (bf16[96,640]{1,0:T(8,128)(2,1)S(1)}, bf16[96,640]{1,0:T(8,128)(2,1)S(1)}, u32[]{:S(2)}, u32[]{:S(2)}) collective-permute-start(bf16[96,640]{1,0:T(8,128)(2,1)S(1)} %collective-permute-done.2.refs_3_), channel_id=1, source_target_pairs={{0,8},{1,5},{2,10},{3,7},{8,16},{9,1},{10,18},{11,3},{16,24},{17,9... | collective-permute-start | bytes 368648 | tf_op jit(solution)/shard_map/ppermute | solution.py:91
  21.4 1.3 %collective-permute-start.18 = (bf16[96,640]{1,0:T(8,128)(2,1)S(1)}, bf16[96,640]{1,0:T(8,128)(2,1)S(1)}, u32[]{:S(2)}, u32[]{:S(2)}) collective-permute-start(bf16[96,640]{1,0:T(8,128)(2,1)S(1)} %collective-permute-done.17.refs_12_), channel_id=1, source_target_pairs={{0,4},{1,9},{2,6},{3,11},{8,0},{9,17},{10,2},{11,19},{16,8},{17,25... | collective-permute-start | bytes 368648 | tf_op jit(solution)/shard_map/ppermute | solution.py:91
  24.7 1.2 %collective-permute-done.3.refs_4_ = bf16[96,640]{1,0:T(8,128)(2,1)S(1)} collective-permute-done((bf16[96,640]{1,0:T(8,128)(2,1)S(1)}, bf16[96,640]{1,0:T(8,128)(2,1)S(1)}, u32[]{:S(2)}, u32[]{:S(2)}) %collective-permute-start.3) | collective-permute-done | bytes 122912 | tf_op jit(solution)/shard_map/ppermute | solution.py:91
  26.8 1.2 %collective-permute-done.9.refs_3_ = bf16[96,640]{1,0:T(8,128)(2,1)S(1)} collective-permute-done((bf16[96,640]{1,0:T(8,128)(2,1)S(1)}, bf16[96,640]{1,0:T(8,128)(2,1)S(1)}, u32[]{:S(2)}, u32[]{:S(2)}) %collective-permute-start.9) | collective-permute-done | bytes 122912 | tf_op jit(solution)/shard_map/ppermute | solution.py:91
  28.0 4.6 %shard_map.39 = (f32[5,8,96,128]{3,2,1,0:T(8,128)S(1)}, f32[5,8,96,128]{3,2,1,0:T(8,128)S(1)}, f32[5,8,96,128]{3,2,1,0:T(8,128)S(1)}) custom-call(s32[5]{0:T(128)S(1)} %stack.23.at_ref, bf16[8,96,640]{2,1,0:T(8,128)(2,1)S(1)} %shard_map.37.rows_ref, bf16[96,640]{1,0:T(8,128)(2,1)S(1)} %get-tuple-element.10.refs_0_, ...), custom_call_target="tpu_custom_call" | custom-call | flops 1321205760 | tf_op jit(solution)/shard_map/pallas_call | solution.py:243
  32.6 2.0 %shard_map.40 = bf16[384,640]{1,0:T(8,128)(2,1)S(1)} custom-call(s32[5]{0:T(128)S(1)} %stack.23.at_ref, bf16[8,96,640]{2,1,0:T(8,128)(2,1)S(1)} %shard_map.37.rows_ref, f32[5,8,96,128]{3,2,1,0:T(8,128)S(1)} %get-tuple-element.12.mixed_ref, f32[5,8,96,128]{3,2,1,0:T(8,128)S(1)} %get-tuple-element.13.sum_ref, f32[5,8,96,128]{3,2,1,0:T(8,128)S(1)} %get-tuple-element.14.top_ref, ...), custom_call_target="tpu_custom_call" | custom-call | flops 314572800 | tf_op jit(solution)/shard_map/pallas_call | solution.py:243
  34.6 3.2 %collective-permute-start.21 = (bf16[2,192,640]{2,1,0:T(8,128)(2,1)S(1)}, bf16[2,192,640]{2,1,0:T(8,128)(2,1)S(1)}, u32[]{:S(2)}, u32[]{:S(2)}) collective-permute-start(bf16[2,192,640]{2,1,0:T(8,128)(2,1)S(1)} %bitcast.16), channel_id=1, source_target_pairs={{0,1},{1,0},{2,3},{3,2},{4,5},{5,4},{6,7},{7,6},{8,9},{9,8},{10,11... | collective-permute-start | bytes 1474568 | tf_op jit(solution)/shard_map/ppermute | solution.py:288
  37.8 1.3 %shard_map.41 = f32[192,640]{1,0:T(8,128)S(1)} custom-call(s32[5]{0:T(128)S(1)} %stack.23.at_ref, bf16[8,96,640]{2,1,0:T(8,128)(2,1)S(1)} %shard_map.37.rows_ref, f32[5,8,96,128]{3,2,1,0:T(8,128)S(1)} %get-tuple-element.12.mixed_ref, f32[5,8,96,128]{3,2,1,0:T(8,128)S(1)} %get-tuple-element.13.sum_ref, f32[5,8,96,128]{3,2,1,0:T(8,128)S(1)} %get-tuple-element.14.top_ref, ...), custom_call_target="tpu_custom_call" | custom-call | flops 314572800 | tf_op jit(solution)/shard_map/pallas_call | solution.py:243
  39.6 1.2 %collective-permute-start.22 = (bf16[96,640]{1,0:T(8,128)(2,1)S(1)}, bf16[96,640]{1,0:T(8,128)(2,1)S(1)}, u32[]{:S(2)}, u32[]{:S(2)}) collective-permute-start(bf16[96,640]{1,0:T(8,128)(2,1)S(1)} %get-tuple-element.16.refs_0_), channel_id=1, source_target_pairs={{0,2},{1,3},{2,0},{3,1},{4,6},{5,7},{6,4},{7,5},{8,10},{9,11},{10,... | collective-permute-start | bytes 368648 | tf_op jit(solution)/shard_map/ppermute | solution.py:292
  40.8 1.4 %shard_map.42.kept_ref = f32[192,640]{1,0:T(8,128)S(1)} custom-call(s32[5]{0:T(128)S(1)} %stack.23.at_ref, bf16[8,96,640]{2,1,0:T(8,128)(2,1)S(1)} %shard_map.37.rows_ref, f32[5,8,96,128]{3,2,1,0:T(8,128)S(1)} %get-tuple-element.12.mixed_ref, f32[5,8,96,128]{3,2,1,0:T(8,128)S(1)} %get-tuple-element.13.sum_ref, ...), custom_call_target="tpu_custom_call" | custom-call | flops 314572800 | tf_op jit(solution)/shard_map/pallas_call | solution.py:243
  42.2 1.7 %collective-permute-done.24.from_x_ref = bf16[96,640]{1,0:T(8,128)(2,1)S(1)} collective-permute-done((bf16[96,640]{1,0:T(8,128)(2,1)S(1)}, bf16[96,640]{1,0:T(8,128)(2,1)S(1)}, u32[]{:S(2)}, u32[]{:S(2)}) %collective-permute-start.24) | collective-permute-done | bytes 122912 | tf_op jit(solution)/shard_map/ppermute | solution.py:292
  43.9 3.5 %collective-permute-start.25 = (bf16[96,640]{1,0:T(8,128)(2,1)S(1)}, bf16[96,640]{1,0:T(8,128)(2,1)S(1)}, u32[]{:S(2)}, u32[]{:S(2)}) collective-permute-start(bf16[96,640]{1,0:T(8,128)(2,1)S(1)} %shard_map.44), channel_id=1, source_target_pairs={{0,8},{1,12},{2,0},{3,4},{4,24},{5,28},{6,16},{7,20},{8,25},{9,29}... | collective-permute-start | bytes 368648 | tf_op jit(solution)/shard_map/ppermute | solution.py:304
  47.4 3.3 %collective-permute-start.23 = (bf16[96,640]{1,0:T(8,128)(2,1)S(1)}, bf16[96,640]{1,0:T(8,128)(2,1)S(1)}, u32[]{:S(2)}, u32[]{:S(2)}) collective-permute-start(bf16[96,640]{1,0:T(8,128)(2,1)S(1)} %shard_map.43), channel_id=1, source_target_pairs={{0,24},{1,28},{2,16},{3,20},{4,8},{5,12},{6,0},{7,4},{8,1},{9,5},{... | collective-permute-start | bytes 368648 | tf_op jit(solution)/shard_map/ppermute | solution.py:304
  50.8 1.5 %collective-permute-done.25 = bf16[96,640]{1,0:T(8,128)(2,1)S(1)} collective-permute-done((bf16[96,640]{1,0:T(8,128)(2,1)S(1)}, bf16[96,640]{1,0:T(8,128)(2,1)S(1)}, u32[]{:S(2)}, u32[]{:S(2)}) %collective-permute-start.25) | collective-permute-done | bytes 122912 | tf_op jit(solution)/shard_map/ppermute | solution.py:304
  52.3 3.0 %collective-permute-done.23 = bf16[96,640]{1,0:T(8,128)(2,1)S(1)} collective-permute-done((bf16[96,640]{1,0:T(8,128)(2,1)S(1)}, bf16[96,640]{1,0:T(8,128)(2,1)S(1)}, u32[]{:S(2)}, u32[]{:S(2)}) %collective-permute-start.23) | collective-permute-done | bytes 122912 | tf_op jit(solution)/shard_map/ppermute | solution.py:304
  (46 shorter events, 13.0 us)
Async XLA Ops:
  0.0 5.3 %collective-permute-start = (bf16[96,640]{1,0:T(8,128)(2,1)}, bf16[96,640]{1,0:T(8,128)(2,1)S(1)}, u32[]{:S(2)}, u32[]{:S(2)}) collective-permute-start(bf16[96,640]{1,0:T(8,128)(2,1)} %refs_0_.1), channel_id=1, source_target_pairs={{0,8},{1,5},{2,10},{3,7},{8,16},{9,1},{10,18},{11,3},{16,24},{17,9... | collective-permute-start | bytes 368648 | tf_op jit(solution)/shard_map/ppermute | solution.py:91
  1.2 5.4 %collective-permute-start.4 = (bf16[96,640]{1,0:T(8,128)(2,1)}, bf16[96,640]{1,0:T(8,128)(2,1)S(1)}, u32[]{:S(2)}, u32[]{:S(2)}) collective-permute-start(bf16[96,640]{1,0:T(8,128)(2,1)} %refs_0_.1), channel_id=1, source_target_pairs={{0,4},{1,9},{2,6},{3,11},{8,0},{9,17},{10,2},{11,19},{16,8},{17,25... | collective-permute-start | bytes 368648 | tf_op jit(solution)/shard_map/ppermute | solution.py:91
  2.4 5.6 %collective-permute-start.10 = (bf16[96,640]{1,0:T(8,128)(2,1)S(1)}, bf16[96,640]{1,0:T(8,128)(2,1)S(1)}, u32[]{:S(2)}, u32[]{:S(2)}) collective-permute-start(bf16[96,640]{1,0:T(8,128)(2,1)S(1)} %get-tuple-element.10.refs_0_), channel_id=1, source_target_pairs={{0,4},{1,9},{2,6},{3,11},{8,0},{9,17},{10,2},{11,19},{16,8},{17,25... | collective-permute-start | bytes 368648 | tf_op jit(solution)/shard_map/ppermute | solution.py:91
  3.8 5.3 %collective-permute-start.13 = (bf16[96,640]{1,0:T(8,128)(2,1)S(1)}, bf16[96,640]{1,0:T(8,128)(2,1)S(1)}, u32[]{:S(2)}, u32[]{:S(2)}) collective-permute-start(bf16[96,640]{1,0:T(8,128)(2,1)S(1)} %get-tuple-element.11.refs_7_), channel_id=1, source_target_pairs={{0,8},{1,5},{2,10},{3,7},{8,16},{9,1},{10,18},{11,3},{16,24},{17,9... | collective-permute-start | bytes 368648 | tf_op jit(solution)/shard_map/ppermute | solution.py:91
  4.0 6.5 %collective-permute-start.16 = (bf16[96,640]{1,0:T(8,128)(2,1)S(1)}, bf16[96,640]{1,0:T(8,128)(2,1)S(1)}, u32[]{:S(2)}, u32[]{:S(2)}) collective-permute-start(bf16[96,640]{1,0:T(8,128)(2,1)S(1)} %get-tuple-element.11.refs_7_), channel_id=1, source_target_pairs={{0,4},{1,9},{2,6},{3,11},{8,0},{9,17},{10,2},{11,19},{16,8},{17,25... | collective-permute-start | bytes 368648 | tf_op jit(solution)/shard_map/ppermute | solution.py:91
  5.3 6.5 %collective-permute-start.7 = (bf16[96,640]{1,0:T(8,128)(2,1)S(1)}, bf16[96,640]{1,0:T(8,128)(2,1)S(1)}, u32[]{:S(2)}, u32[]{:S(2)}) collective-permute-start(bf16[96,640]{1,0:T(8,128)(2,1)S(1)} %get-tuple-element.10.refs_0_), channel_id=1, source_target_pairs={{0,8},{1,5},{2,10},{3,7},{8,16},{9,1},{10,18},{11,3},{16,24},{17,9... | collective-permute-start | bytes 368648 | tf_op jit(solution)/shard_map/ppermute | solution.py:91
  6.7 6.8 %collective-permute-start.1 = (bf16[96,640]{1,0:T(8,128)(2,1)S(1)}, bf16[96,640]{1,0:T(8,128)(2,1)S(1)}, u32[]{:S(2)}, u32[]{:S(2)}) collective-permute-start(bf16[96,640]{1,0:T(8,128)(2,1)S(1)} %collective-permute-done.refs_1_), channel_id=1, source_target_pairs={{0,8},{1,5},{2,10},{3,7},{8,16},{9,1},{10,18},{11,3},{16,24},{17,9... | collective-permute-start | bytes 368648 | tf_op jit(solution)/shard_map/ppermute | solution.py:91
  8.0 5.7 %collective-permute-start.5 = (bf16[96,640]{1,0:T(8,128)(2,1)S(1)}, bf16[96,640]{1,0:T(8,128)(2,1)S(1)}, u32[]{:S(2)}, u32[]{:S(2)}) collective-permute-start(bf16[96,640]{1,0:T(8,128)(2,1)S(1)} %collective-permute-done.4.refs_7_), channel_id=1, source_target_pairs={{0,4},{1,9},{2,6},{3,11},{8,0},{9,17},{10,2},{11,19},{16,8},{17,25... | collective-permute-start | bytes 368648 | tf_op jit(solution)/shard_map/ppermute | solution.py:91
  9.1 6.8 %collective-permute-start.11 = (bf16[96,640]{1,0:T(8,128)(2,1)S(1)}, bf16[96,640]{1,0:T(8,128)(2,1)S(1)}, u32[]{:S(2)}, u32[]{:S(2)}) collective-permute-start(bf16[96,640]{1,0:T(8,128)(2,1)S(1)} %collective-permute-done.10.refs_6_), channel_id=1, source_target_pairs={{0,4},{1,9},{2,6},{3,11},{8,0},{9,17},{10,2},{11,19},{16,8},{17,25... | collective-permute-start | bytes 368648 | tf_op jit(solution)/shard_map/ppermute | solution.py:91
  10.4 5.9 %collective-permute-start.14 = (bf16[96,640]{1,0:T(8,128)(2,1)S(1)}, bf16[96,640]{1,0:T(8,128)(2,1)S(1)}, u32[]{:S(2)}, u32[]{:S(2)}) collective-permute-start(bf16[96,640]{1,0:T(8,128)(2,1)S(1)} %collective-permute-done.13.refs_8_), channel_id=1, source_target_pairs={{0,8},{1,5},{2,10},{3,7},{8,16},{9,1},{10,18},{11,3},{16,24},{17,9... | collective-permute-start | bytes 368648 | tf_op jit(solution)/shard_map/ppermute | solution.py:91
  11.7 6.4 %collective-permute-start.17 = (bf16[96,640]{1,0:T(8,128)(2,1)S(1)}, bf16[96,640]{1,0:T(8,128)(2,1)S(1)}, u32[]{:S(2)}, u32[]{:S(2)}) collective-permute-start(bf16[96,640]{1,0:T(8,128)(2,1)S(1)} %collective-permute-done.16.refs_13_), channel_id=1, source_target_pairs={{0,4},{1,9},{2,6},{3,11},{8,0},{9,17},{10,2},{11,19},{16,8},{17,25... | collective-permute-start | bytes 368648 | tf_op jit(solution)/shard_map/ppermute | solution.py:91
  13.5 5.8 %collective-permute-start.2 = (bf16[96,640]{1,0:T(8,128)(2,1)S(1)}, bf16[96,640]{1,0:T(8,128)(2,1)S(1)}, u32[]{:S(2)}, u32[]{:S(2)}) collective-permute-start(bf16[96,640]{1,0:T(8,128)(2,1)S(1)} %collective-permute-done.1.refs_2_), channel_id=1, source_target_pairs={{0,8},{1,5},{2,10},{3,7},{8,16},{9,1},{10,18},{11,3},{16,24},{17,9... | collective-permute-start | bytes 368648 | tf_op jit(solution)/shard_map/ppermute | solution.py:91
  13.7 7.7 %collective-permute-start.8 = (bf16[96,640]{1,0:T(8,128)(2,1)S(1)}, bf16[96,640]{1,0:T(8,128)(2,1)S(1)}, u32[]{:S(2)}, u32[]{:S(2)}) collective-permute-start(bf16[96,640]{1,0:T(8,128)(2,1)S(1)} %collective-permute-done.7.refs_1_), channel_id=1, source_target_pairs={{0,8},{1,5},{2,10},{3,7},{8,16},{9,1},{10,18},{11,3},{16,24},{17,9... | collective-permute-start | bytes 368648 | tf_op jit(solution)/shard_map/ppermute | solution.py:91
  15.9 6.8 %collective-permute-start.6 = (bf16[96,640]{1,0:T(8,128)(2,1)S(1)}, bf16[96,640]{1,0:T(8,128)(2,1)S(1)}, u32[]{:S(2)}, u32[]{:S(2)}) collective-permute-start(bf16[96,640]{1,0:T(8,128)(2,1)S(1)} %collective-permute-done.5.refs_6_), channel_id=1, source_target_pairs={{0,4},{1,9},{2,6},{3,11},{8,0},{9,17},{10,2},{11,19},{16,8},{17,25... | collective-permute-start | bytes 368648 | tf_op jit(solution)/shard_map/ppermute | solution.py:91
  16.3 6.9 %collective-permute-start.12 = (bf16[96,640]{1,0:T(8,128)(2,1)S(1)}, bf16[96,640]{1,0:T(8,128)(2,1)S(1)}, u32[]{:S(2)}, u32[]{:S(2)}) collective-permute-start(bf16[96,640]{1,0:T(8,128)(2,1)S(1)} %collective-permute-done.11.refs_5_), channel_id=1, source_target_pairs={{0,4},{1,9},{2,6},{3,11},{8,0},{9,17},{10,2},{11,19},{16,8},{17,25... | collective-permute-start | bytes 368648 | tf_op jit(solution)/shard_map/ppermute | solution.py:91
  18.1 6.2 %collective-permute-start.15 = (bf16[96,640]{1,0:T(8,128)(2,1)S(1)}, bf16[96,640]{1,0:T(8,128)(2,1)S(1)}, u32[]{:S(2)}, u32[]{:S(2)}) collective-permute-start(bf16[96,640]{1,0:T(8,128)(2,1)S(1)} %collective-permute-done.14.refs_9_), channel_id=1, source_target_pairs={{0,8},{1,5},{2,10},{3,7},{8,16},{9,1},{10,18},{11,3},{16,24},{17,9... | collective-permute-start | bytes 368648 | tf_op jit(solution)/shard_map/ppermute | solution.py:91
  19.3 6.5 %collective-permute-start.3 = (bf16[96,640]{1,0:T(8,128)(2,1)S(1)}, bf16[96,640]{1,0:T(8,128)(2,1)S(1)}, u32[]{:S(2)}, u32[]{:S(2)}) collective-permute-start(bf16[96,640]{1,0:T(8,128)(2,1)S(1)} %collective-permute-done.2.refs_3_), channel_id=1, source_target_pairs={{0,8},{1,5},{2,10},{3,7},{8,16},{9,1},{10,18},{11,3},{16,24},{17,9... | collective-permute-start | bytes 368648 | tf_op jit(solution)/shard_map/ppermute | solution.py:91
  21.4 5.4 %collective-permute-start.18 = (bf16[96,640]{1,0:T(8,128)(2,1)S(1)}, bf16[96,640]{1,0:T(8,128)(2,1)S(1)}, u32[]{:S(2)}, u32[]{:S(2)}) collective-permute-start(bf16[96,640]{1,0:T(8,128)(2,1)S(1)} %collective-permute-done.17.refs_12_), channel_id=1, source_target_pairs={{0,4},{1,9},{2,6},{3,11},{8,0},{9,17},{10,2},{11,19},{16,8},{17,25... | collective-permute-start | bytes 368648 | tf_op jit(solution)/shard_map/ppermute | solution.py:91
  22.7 5.3 %collective-permute-start.9 = (bf16[96,640]{1,0:T(8,128)(2,1)S(1)}, bf16[96,640]{1,0:T(8,128)(2,1)S(1)}, u32[]{:S(2)}, u32[]{:S(2)}) collective-permute-start(bf16[96,640]{1,0:T(8,128)(2,1)S(1)} %collective-permute-done.8.refs_2_), channel_id=1, source_target_pairs={{0,8},{1,5},{2,10},{3,7},{8,16},{9,1},{10,18},{11,3},{16,24},{17,9... | collective-permute-start | bytes 368648 | tf_op jit(solution)/shard_map/ppermute | solution.py:91
  23.2 9.4 %collective-permute-start.19 = (bf16[96,640]{1,0:T(8,128)(2,1)S(1)}, bf16[96,640]{1,0:T(8,128)(2,1)S(1)}, u32[]{:S(2)}, u32[]{:S(2)}) collective-permute-start(bf16[96,640]{1,0:T(8,128)(2,1)S(1)} %collective-permute-done.12.refs_4_), channel_id=1, source_target_pairs={{0,4},{1,9},{2,6},{3,11},{8,0},{9,17},{10,2},{11,19},{16,8},{17,25... | collective-permute-start | bytes 368648 | tf_op jit(solution)/shard_map/ppermute | solution.py:91
  24.3 8.3 %collective-permute-start.20 = (bf16[96,640]{1,0:T(8,128)(2,1)S(1)}, bf16[96,640]{1,0:T(8,128)(2,1)S(1)}, u32[]{:S(2)}, u32[]{:S(2)}) collective-permute-start(bf16[96,640]{1,0:T(8,128)(2,1)S(1)} %collective-permute-done.15.refs_10_), channel_id=1, source_target_pairs={{0,8},{1,5},{2,10},{3,7},{8,16},{9,1},{10,18},{11,3},{16,24},{17,9... | collective-permute-start | bytes 368648 | tf_op jit(solution)/shard_map/ppermute | solution.py:91
  39.6 7.8 %collective-permute-start.22 = (bf16[96,640]{1,0:T(8,128)(2,1)S(1)}, bf16[96,640]{1,0:T(8,128)(2,1)S(1)}, u32[]{:S(2)}, u32[]{:S(2)}) collective-permute-start(bf16[96,640]{1,0:T(8,128)(2,1)S(1)} %get-tuple-element.16.refs_0_), channel_id=1, source_target_pairs={{0,2},{1,3},{2,0},{3,1},{4,6},{5,7},{6,4},{7,5},{8,10},{9,11},{10,... | collective-permute-start | bytes 368648 | tf_op jit(solution)/shard_map/ppermute | solution.py:292
  43.9 8.3 %collective-permute-start.25 = (bf16[96,640]{1,0:T(8,128)(2,1)S(1)}, bf16[96,640]{1,0:T(8,128)(2,1)S(1)}, u32[]{:S(2)}, u32[]{:S(2)}) collective-permute-start(bf16[96,640]{1,0:T(8,128)(2,1)S(1)} %shard_map.44), channel_id=1, source_target_pairs={{0,8},{1,12},{2,0},{3,4},{4,24},{5,28},{6,16},{7,20},{8,25},{9,29}... | collective-permute-start | bytes 368648 | tf_op jit(solution)/shard_map/ppermute | solution.py:304
  47.4 7.8 %collective-permute-start.23 = (bf16[96,640]{1,0:T(8,128)(2,1)S(1)}, bf16[96,640]{1,0:T(8,128)(2,1)S(1)}, u32[]{:S(2)}, u32[]{:S(2)}) collective-permute-start(bf16[96,640]{1,0:T(8,128)(2,1)S(1)} %shard_map.43), channel_id=1, source_target_pairs={{0,24},{1,28},{2,16},{3,20},{4,8},{5,12},{6,0},{7,4},{8,1},{9,5},{... | collective-permute-start | bytes 368648 | tf_op jit(solution)/shard_map/ppermute | solution.py:304
  (5 other events, 16.9 us)

commit v19 on v18

--- a/solution.py
+++ b/solution.py
@@ -143,7 +143,7 @@
         top = jnp.broadcast_to(top, (TPF, HD))
         if floor is not None:
             top = jnp.maximum(top, floor[r : r + TPF])
-        weights.append(jnp.concatenate([jnp.exp2((p - top) * SCALE).astype(jnp.bfloat16) for p in parts], axis=1))
+        weights.append(jnp.concatenate([jnp.exp2(((p - top) * SCALE).astype(jnp.bfloat16)) for p in parts], axis=1))
         tops.append(top)
     return jnp.concatenate(weights, axis=0), jnp.concatenate(tops, axis=0)
 
@@ -230,11 +230,13 @@
         mixed, total = mixed + of(mixed_ref, head) * kept, total + of(sum_ref, head) * kept
         attended.append((mixed / total).astype(jnp.bfloat16))
     rows = jnp.concatenate(attended, axis=1)
-    refs[-1][...] = jnp.dot(rows, w_ref[...], preferred_element_type=jnp.float32).astype(refs[-1].dtype)
+    result = jnp.dot(rows, w_ref[...], preferred_element_type=jnp.float32)
+    for i, out_ref in enumerate(refs[-len(flips) :]):
+        out_ref[...] = result[2 * i * ROWS : 2 * (i + 1) * ROWS].astype(out_ref.dtype)
 
 
 def sum_kernel(rows, kept_ref, from_core_ref, from_x_ref, total_ref):
-    total = kept_ref[rows] + from_core_ref[1, rows].astype(jnp.float32) + from_x_ref[...].astype(jnp.float32)
+    total = kept_ref[rows] + from_core_ref[rows].astype(jnp.float32) + from_x_ref[...].astype(jnp.float32)
     total_ref[...] = total.astype(total_ref.dtype)
 
 
@@ -274,21 +276,20 @@
     )
 
     def finish(flips, dtype, after=()):
-        (sums,) = call(
+        return call(
             functools.partial(finish_kernel, heads, n, flips),
             (where,),
             [rows, *state, keys[far], values[far], out_weight],
-            [((len(flips) * 2 * ROWS, cols), dtype)],
+            [((2 * ROWS, cols), dtype)] * len(flips),
             n * ROWS * width * cols,
             after,
         )
-        return sums.reshape(len(flips), 2 * ROWS, cols)
 
     given = finish([(1, 1), (0, 1)], bf16)
-    from_core = lax.ppermute(given, "heads", [(h, h ^ 1) for h in range(4)])
-    sums = finish([(1, 0)], f32, (given,))[0]
+    from_core = [lax.ppermute(block, "heads", [(h, h ^ 1) for h in range(4)]) for block in given]
+    sums = finish([(1, 0)], f32, given)[0]
     parts = [slice(slot * ROWS, (slot + 1) * ROWS) for slot in range(2)]
-    given = [(sums[part] + from_core[0, part].astype(f32)).astype(bf16) for part in parts]
+    given = [(sums[part] + from_core[0][part].astype(f32)).astype(bf16) for part in parts]
     from_x = [lax.ppermute(block, "heads", [(h, h ^ 2) for h in range(4)]) for block in given]
     kept = finish([(0, 0)], f32, given)[0]
     arrived = []
@@ -299,7 +300,7 @@
                 to = PATTERNS[(slot ^ (f & 1)) + 2 * (h >> 1)][f >> 1]
                 pairs.append((4 * f + h, 4 * (2 * to + (h & 1)) + (f >> 1)))
         (total,) = call(
-            functools.partial(sum_kernel, part), (), [kept, from_core, from_x[slot]], [((ROWS, cols), bf16)], 0
+            functools.partial(sum_kernel, part), (), [kept, from_core[1], from_x[slot]], [((ROWS, cols), bf16)], 0
         )
         arrived.append(lax.ppermute(total, ("frames", "heads"), pairs))
     patterns = [[p[source] for p in PATTERNS].index(to) for source in range(4) for to in range(4)]

time: 57 us -> 57.1 us (level)
    ppermute x1 -> x2, starting transfers between devices: 3.17 us -> 3.25 us  [on_device_ring(): lax.ppermute(block, 'heads', [(h, h ^ 1) for h in range(4)])]
  transfers between devices with their start and end apart: 26 -> 27, of which waited for: 15 -> 14; matrix products, arithmetic and copies ran while one was open for 0% -> 0% of each run, Pallas kernels for 13% -> 13%
where the time goes in v19:
time: 57.1 us; the launch traced here: 56.1 us
  starting transfers between devices  29.5 us (52%)
  waiting for transfers between devices  14.1 us (25%)
  Pallas kernels  9.53 us (17%)
  local copies, waits for them, and re-layouts  1.94 us (3%)
  other arithmetic  0.8 us (1%)
    ppermute x21, starting transfers between devices, hop(): return lax.ppermute(x, ('frames', 'heads'), pairs)  17.9 us
    pallas_call x8, Pallas kernels, call(): pl.pallas_call(kernel, out_shape=[jax.ShapeDtypeStruct(shape, dtype) for...  9.53 us
    ppermute x21, waiting for transfers between devices, hop(): return lax.ppermute(x, ('frames', 'heads'), pairs)  8.01 us
    ppermute x2, starting transfers between devices, on_device_ring(): arrived.append(lax.ppermute(total, ('frames', 'heads'), pairs))  6.81 us
    ppermute x2, waiting for transfers between devices, on_device_ring(): arrived.append(lax.ppermute(total, ('frames', 'heads'), pairs))  4.52 us
    ppermute x2, starting transfers between devices, on_device_ring(): lax.ppermute(block, 'heads', [(h, h ^ 1) for h in range(4)])  3.25 us
    unnamed x6, local copies, waits for them, and re-layouts  1.85 us
    ppermute x2, waiting for transfers between devices, on_device_ring(): lax.ppermute(block, 'heads', [(h, h ^ 2) for h in range(4)])  1.6 us
  transfers between devices with their start and end apart: 27, of which 14 were waited for; matrix products, arithmetic and copies ran while one was open for 0% of the time, Pallas kernels for 13%

profile of v19, /device:TPU:3, one launch (start us, length us, event | category | flops | bytes accessed | tf_op | source)
XLA Modules:
  0.0 56.1 jit_solution(14330608020117941132)
XLA Ops:
  0.0 1.2 %collective-permute-start = (bf16[96,640]{1,0:T(8,128)(2,1)}, bf16[96,640]{1,0:T(8,128)(2,1)S(1)}, u32[]{:S(2)}, u32[]{:S(2)}) collective-permute-start(bf16[96,640]{1,0:T(8,128)(2,1)} %refs_0_.1), channel_id=1, source_target_pairs={{0,8},{1,5},{2,10},{3,7},{8,16},{9,1},{10,18},{11,3},{16,24},{17,9... | collective-permute-start | bytes 368648 | tf_op jit(solution)/shard_map/ppermute | solution.py:91
  2.4 1.3 %collective-permute-start.10 = (bf16[96,640]{1,0:T(8,128)(2,1)S(1)}, bf16[96,640]{1,0:T(8,128)(2,1)S(1)}, u32[]{:S(2)}, u32[]{:S(2)}) collective-permute-start(bf16[96,640]{1,0:T(8,128)(2,1)S(1)} %get-tuple-element.12.refs_0_), channel_id=1, source_target_pairs={{0,4},{1,9},{2,6},{3,11},{8,0},{9,17},{10,2},{11,19},{16,8},{17,25... | collective-permute-start | bytes 368648 | tf_op jit(solution)/shard_map/ppermute | solution.py:91
  4.0 1.3 %collective-permute-start.16 = (bf16[96,640]{1,0:T(8,128)(2,1)S(1)}, bf16[96,640]{1,0:T(8,128)(2,1)S(1)}, u32[]{:S(2)}, u32[]{:S(2)}) collective-permute-start(bf16[96,640]{1,0:T(8,128)(2,1)S(1)} %get-tuple-element.13.refs_7_), channel_id=1, source_target_pairs={{0,4},{1,9},{2,6},{3,11},{8,0},{9,17},{10,2},{11,19},{16,8},{17,25... | collective-permute-start | bytes 368648 | tf_op jit(solution)/shard_map/ppermute | solution.py:91
  5.5 1.2 %collective-permute-done.4.refs_7_ = bf16[96,640]{1,0:T(8,128)(2,1)S(1)} collective-permute-done((bf16[96,640]{1,0:T(8,128)(2,1)}, bf16[96,640]{1,0:T(8,128)(2,1)S(1)}, u32[]{:S(2)}, u32[]{:S(2)}) %collective-permute-start.4) | collective-permute-done | bytes 122912 | tf_op jit(solution)/shard_map/ppermute | solution.py:91
  9.1 1.3 %collective-permute-start.11 = (bf16[96,640]{1,0:T(8,128)(2,1)S(1)}, bf16[96,640]{1,0:T(8,128)(2,1)S(1)}, u32[]{:S(2)}, u32[]{:S(2)}) collective-permute-start(bf16[96,640]{1,0:T(8,128)(2,1)S(1)} %collective-permute-done.10.refs_6_), channel_id=1, source_target_pairs={{0,4},{1,9},{2,6},{3,11},{8,0},{9,17},{10,2},{11,19},{16,8},{17,25... | collective-permute-start | bytes 368648 | tf_op jit(solution)/shard_map/ppermute | solution.py:91
  11.7 1.3 %collective-permute-start.17 = (bf16[96,640]{1,0:T(8,128)(2,1)S(1)}, bf16[96,640]{1,0:T(8,128)(2,1)S(1)}, u32[]{:S(2)}, u32[]{:S(2)}) collective-permute-start(bf16[96,640]{1,0:T(8,128)(2,1)S(1)} %collective-permute-done.16.refs_13_), channel_id=1, source_target_pairs={{0,4},{1,9},{2,6},{3,11},{8,0},{9,17},{10,2},{11,19},{16,8},{17,25... | collective-permute-start | bytes 368648 | tf_op jit(solution)/shard_map/ppermute | solution.py:91
  13.7 1.2 %collective-permute-start.8 = (bf16[96,640]{1,0:T(8,128)(2,1)S(1)}, bf16[96,640]{1,0:T(8,128)(2,1)S(1)}, u32[]{:S(2)}, u32[]{:S(2)}) collective-permute-start(bf16[96,640]{1,0:T(8,128)(2,1)S(1)} %collective-permute-done.7.refs_1_), channel_id=1, source_target_pairs={{0,8},{1,5},{2,10},{3,7},{8,16},{9,1},{10,18},{11,3},{16,24},{17,9... | collective-permute-start | bytes 368648 | tf_op jit(solution)/shard_map/ppermute | solution.py:91
  16.3 1.3 %collective-permute-start.12 = (bf16[96,640]{1,0:T(8,128)(2,1)S(1)}, bf16[96,640]{1,0:T(8,128)(2,1)S(1)}, u32[]{:S(2)}, u32[]{:S(2)}) collective-permute-start(bf16[96,640]{1,0:T(8,128)(2,1)S(1)} %collective-permute-done.11.refs_5_), channel_id=1, source_target_pairs={{0,4},{1,9},{2,6},{3,11},{8,0},{9,17},{10,2},{11,19},{16,8},{17,25... | collective-permute-start | bytes 368648 | tf_op jit(solution)/shard_map/ppermute | solution.py:91
  18.1 1.2 %collective-permute-start.15 = (bf16[96,640]{1,0:T(8,128)(2,1)S(1)}, bf16[96,640]{1,0:T(8,128)(2,1)S(1)}, u32[]{:S(2)}, u32[]{:S(2)}) collective-permute-start(bf16[96,640]{1,0:T(8,128)(2,1)S(1)} %collective-permute-done.14.refs_9_), channel_id=1, source_target_pairs={{0,8},{1,5},{2,10},{3,7},{8,16},{9,1},{10,18},{11,3},{16,24},{17,9... | collective-permute-start | bytes 368648 | tf_op jit(solution)/shard_map/ppermute | solution.py:91
  19.3 1.3 %collective-permute-start.3 = (bf16[96,640]{1,0:T(8,128)(2,1)S(1)}, bf16[96,640]{1,0:T(8,128)(2,1)S(1)}, u32[]{:S(2)}, u32[]{:S(2)}) collective-permute-start(bf16[96,640]{1,0:T(8,128)(2,1)S(1)} %collective-permute-done.2.refs_3_), channel_id=1, source_target_pairs={{0,8},{1,5},{2,10},{3,7},{8,16},{9,1},{10,18},{11,3},{16,24},{17,9... | collective-permute-start | bytes 368648 | tf_op jit(solution)/shard_map/ppermute | solution.py:91
  21.4 1.3 %collective-permute-start.18 = (bf16[96,640]{1,0:T(8,128)(2,1)S(1)}, bf16[96,640]{1,0:T(8,128)(2,1)S(1)}, u32[]{:S(2)}, u32[]{:S(2)}) collective-permute-start(bf16[96,640]{1,0:T(8,128)(2,1)S(1)} %collective-permute-done.17.refs_12_), channel_id=1, source_target_pairs={{0,4},{1,9},{2,6},{3,11},{8,0},{9,17},{10,2},{11,19},{16,8},{17,25... | collective-permute-start | bytes 368648 | tf_op jit(solution)/shard_map/ppermute | solution.py:91
  24.7 1.2 %collective-permute-done.3.refs_4_ = bf16[96,640]{1,0:T(8,128)(2,1)S(1)} collective-permute-done((bf16[96,640]{1,0:T(8,128)(2,1)S(1)}, bf16[96,640]{1,0:T(8,128)(2,1)S(1)}, u32[]{:S(2)}, u32[]{:S(2)}) %collective-permute-start.3) | collective-permute-done | bytes 122912 | tf_op jit(solution)/shard_map/ppermute | solution.py:91
  26.8 1.2 %collective-permute-done.9.refs_3_ = bf16[96,640]{1,0:T(8,128)(2,1)S(1)} collective-permute-done((bf16[96,640]{1,0:T(8,128)(2,1)S(1)}, bf16[96,640]{1,0:T(8,128)(2,1)S(1)}, u32[]{:S(2)}, u32[]{:S(2)}) %collective-permute-start.9) | collective-permute-done | bytes 122912 | tf_op jit(solution)/shard_map/ppermute | solution.py:91
  28.0 4.6 %shard_map.39 = (f32[5,8,96,128]{3,2,1,0:T(8,128)S(1)}, f32[5,8,96,128]{3,2,1,0:T(8,128)S(1)}, f32[5,8,96,128]{3,2,1,0:T(8,128)S(1)}) custom-call(s32[5]{0:T(128)S(1)} %stack.23.at_ref, bf16[8,96,640]{2,1,0:T(8,128)(2,1)S(1)} %shard_map.37.rows_ref, bf16[96,640]{1,0:T(8,128)(2,1)S(1)} %get-tuple-element.12.refs_0_, ...), custom_call_target="tpu_custom_call" | custom-call | flops 1321205760 | tf_op jit(solution)/shard_map/pallas_call | solution.py:245
  32.7 2.0 %shard_map.40 = (bf16[192,640]{1,0:T(8,128)(2,1)S(1)}, bf16[192,640]{1,0:T(8,128)(2,1)S(1)}) custom-call(s32[5]{0:T(128)S(1)} %stack.23.at_ref, bf16[8,96,640]{2,1,0:T(8,128)(2,1)S(1)} %shard_map.37.rows_ref, f32[5,8,96,128]{3,2,1,0:T(8,128)S(1)} %get-tuple-element.14.mixed_ref, f32[5,8,96,128]{3,2,1,0:T(8,128)S(1)} %get-tuple-element.15.sum_ref, ...), custom_call_target="tpu_custom_call" | custom-call | flops 314572800 | tf_op jit(solution)/shard_map/pallas_call | solution.py:245
  34.6 3.2 %collective-permute-start.21 = (bf16[192,640]{1,0:T(8,128)(2,1)S(1)}, bf16[192,640]{1,0:T(8,128)(2,1)S(1)}, u32[]{:S(2)}, u32[]{:S(2)}) collective-permute-start(bf16[192,640]{1,0:T(8,128)(2,1)S(1)} %get-tuple-element.17.refs_0_), channel_id=1, source_target_pairs={{0,1},{1,0},{2,3},{3,2},{4,5},{5,4},{6,7},{7,6},{8,9},{9,8},{10,11... | collective-permute-start | bytes 737288 | tf_op jit(solution)/shard_map/ppermute | solution.py:289
  37.9 1.4 %shard_map.41 = f32[192,640]{1,0:T(8,128)S(1)} custom-call(s32[5]{0:T(128)S(1)} %stack.23.at_ref, bf16[8,96,640]{2,1,0:T(8,128)(2,1)S(1)} %shard_map.37.rows_ref, f32[5,8,96,128]{3,2,1,0:T(8,128)S(1)} %get-tuple-element.14.mixed_ref, f32[5,8,96,128]{3,2,1,0:T(8,128)S(1)} %get-tuple-element.15.sum_ref, f32[5,8,96,128]{3,2,1,0:T(8,128)S(1)} %get-tuple-element.16.top_ref, ...), custom_call_target="tpu_custom_call" | custom-call | flops 314572800 | tf_op jit(solution)/shard_map/pallas_call | solution.py:245
  39.7 1.2 %collective-permute-start.23 = (bf16[96,640]{1,0:T(8,128)(2,1)S(1)}, bf16[96,640]{1,0:T(8,128)(2,1)S(1)}, u32[]{:S(2)}, u32[]{:S(2)}) collective-permute-start(bf16[96,640]{1,0:T(8,128)(2,1)S(1)} %get-tuple-element.20.refs_0_), channel_id=1, source_target_pairs={{0,2},{1,3},{2,0},{3,1},{4,6},{5,7},{6,4},{7,5},{8,10},{9,11},{10,... | collective-permute-start | bytes 368648 | tf_op jit(solution)/shard_map/ppermute | solution.py:293
  40.9 1.4 %shard_map.42.kept_ref = f32[192,640]{1,0:T(8,128)S(1)} custom-call(s32[5]{0:T(128)S(1)} %stack.23.at_ref, bf16[8,96,640]{2,1,0:T(8,128)(2,1)S(1)} %shard_map.37.rows_ref, f32[5,8,96,128]{3,2,1,0:T(8,128)S(1)} %get-tuple-element.14.mixed_ref, f32[5,8,96,128]{3,2,1,0:T(8,128)S(1)} %get-tuple-element.15.sum_ref, ...), custom_call_target="tpu_custom_call" | custom-call | flops 314572800 | tf_op jit(solution)/shard_map/pallas_call | solution.py:245
  42.3 1.6 %collective-permute-done.25.from_x_ref = bf16[96,640]{1,0:T(8,128)(2,1)S(1)} collective-permute-done((bf16[96,640]{1,0:T(8,128)(2,1)S(1)}, bf16[96,640]{1,0:T(8,128)(2,1)S(1)}, u32[]{:S(2)}, u32[]{:S(2)}) %collective-permute-start.25) | collective-permute-done | bytes 122912 | tf_op jit(solution)/shard_map/ppermute | solution.py:293
  43.9 3.6 %collective-permute-start.26 = (bf16[96,640]{1,0:T(8,128)(2,1)S(1)}, bf16[96,640]{1,0:T(8,128)(2,1)S(1)}, u32[]{:S(2)}, u32[]{:S(2)}) collective-permute-start(bf16[96,640]{1,0:T(8,128)(2,1)S(1)} %shard_map.44), channel_id=1, source_target_pairs={{0,8},{1,12},{2,0},{3,4},{4,24},{5,28},{6,16},{7,20},{8,25},{9,29}... | collective-permute-start | bytes 368648 | tf_op jit(solution)/shard_map/ppermute | solution.py:305
  47.6 3.2 %collective-permute-start.24 = (bf16[96,640]{1,0:T(8,128)(2,1)S(1)}, bf16[96,640]{1,0:T(8,128)(2,1)S(1)}, u32[]{:S(2)}, u32[]{:S(2)}) collective-permute-start(bf16[96,640]{1,0:T(8,128)(2,1)S(1)} %shard_map.43), channel_id=1, source_target_pairs={{0,24},{1,28},{2,16},{3,20},{4,8},{5,12},{6,0},{7,4},{8,1},{9,5},{... | collective-permute-start | bytes 368648 | tf_op jit(solution)/shard_map/ppermute | solution.py:305
  50.8 1.5 %collective-permute-done.26 = bf16[96,640]{1,0:T(8,128)(2,1)S(1)} collective-permute-done((bf16[96,640]{1,0:T(8,128)(2,1)S(1)}, bf16[96,640]{1,0:T(8,128)(2,1)S(1)}, u32[]{:S(2)}, u32[]{:S(2)}) %collective-permute-start.26) | collective-permute-done | bytes 122912 | tf_op jit(solution)/shard_map/ppermute | solution.py:305
  52.3 3.0 %collective-permute-done.24 = bf16[96,640]{1,0:T(8,128)(2,1)S(1)} collective-permute-done((bf16[96,640]{1,0:T(8,128)(2,1)S(1)}, bf16[96,640]{1,0:T(8,128)(2,1)S(1)}, u32[]{:S(2)}, u32[]{:S(2)}) %collective-permute-start.24) | collective-permute-done | bytes 122912 | tf_op jit(solution)/shard_map/ppermute | solution.py:305
  (48 shorter events, 12.9 us)
Async XLA Ops:
  0.0 5.3 %collective-permute-start = (bf16[96,640]{1,0:T(8,128)(2,1)}, bf16[96,640]{1,0:T(8,128)(2,1)S(1)}, u32[]{:S(2)}, u32[]{:S(2)}) collective-permute-start(bf16[96,640]{1,0:T(8,128)(2,1)} %refs_0_.1), channel_id=1, source_target_pairs={{0,8},{1,5},{2,10},{3,7},{8,16},{9,1},{10,18},{11,3},{16,24},{17,9... | collective-permute-start | bytes 368648 | tf_op jit(solution)/shard_map/ppermute | solution.py:91
  1.2 5.4 %collective-permute-start.4 = (bf16[96,640]{1,0:T(8,128)(2,1)}, bf16[96,640]{1,0:T(8,128)(2,1)S(1)}, u32[]{:S(2)}, u32[]{:S(2)}) collective-permute-start(bf16[96,640]{1,0:T(8,128)(2,1)} %refs_0_.1), channel_id=1, source_target_pairs={{0,4},{1,9},{2,6},{3,11},{8,0},{9,17},{10,2},{11,19},{16,8},{17,25... | collective-permute-start | bytes 368648 | tf_op jit(solution)/shard_map/ppermute | solution.py:91
  2.4 5.6 %collective-permute-start.10 = (bf16[96,640]{1,0:T(8,128)(2,1)S(1)}, bf16[96,640]{1,0:T(8,128)(2,1)S(1)}, u32[]{:S(2)}, u32[]{:S(2)}) collective-permute-start(bf16[96,640]{1,0:T(8,128)(2,1)S(1)} %get-tuple-element.12.refs_0_), channel_id=1, source_target_pairs={{0,4},{1,9},{2,6},{3,11},{8,0},{9,17},{10,2},{11,19},{16,8},{17,25... | collective-permute-start | bytes 368648 | tf_op jit(solution)/shard_map/ppermute | solution.py:91
  3.8 5.3 %collective-permute-start.13 = (bf16[96,640]{1,0:T(8,128)(2,1)S(1)}, bf16[96,640]{1,0:T(8,128)(2,1)S(1)}, u32[]{:S(2)}, u32[]{:S(2)}) collective-permute-start(bf16[96,640]{1,0:T(8,128)(2,1)S(1)} %get-tuple-element.13.refs_7_), channel_id=1, source_target_pairs={{0,8},{1,5},{2,10},{3,7},{8,16},{9,1},{10,18},{11,3},{16,24},{17,9... | collective-permute-start | bytes 368648 | tf_op jit(solution)/shard_map/ppermute | solution.py:91
  4.0 6.5 %collective-permute-start.16 = (bf16[96,640]{1,0:T(8,128)(2,1)S(1)}, bf16[96,640]{1,0:T(8,128)(2,1)S(1)}, u32[]{:S(2)}, u32[]{:S(2)}) collective-permute-start(bf16[96,640]{1,0:T(8,128)(2,1)S(1)} %get-tuple-element.13.refs_7_), channel_id=1, source_target_pairs={{0,4},{1,9},{2,6},{3,11},{8,0},{9,17},{10,2},{11,19},{16,8},{17,25... | collective-permute-start | bytes 368648 | tf_op jit(solution)/shard_map/ppermute | solution.py:91
  5.3 6.5 %collective-permute-start.7 = (bf16[96,640]{1,0:T(8,128)(2,1)S(1)}, bf16[96,640]{1,0:T(8,128)(2,1)S(1)}, u32[]{:S(2)}, u32[]{:S(2)}) collective-permute-start(bf16[96,640]{1,0:T(8,128)(2,1)S(1)} %get-tuple-element.12.refs_0_), channel_id=1, source_target_pairs={{0,8},{1,5},{2,10},{3,7},{8,16},{9,1},{10,18},{11,3},{16,24},{17,9... | collective-permute-start | bytes 368648 | tf_op jit(solution)/shard_map/ppermute | solution.py:91
  6.7 6.8 %collective-permute-start.1 = (bf16[96,640]{1,0:T(8,128)(2,1)S(1)}, bf16[96,640]{1,0:T(8,128)(2,1)S(1)}, u32[]{:S(2)}, u32[]{:S(2)}) collective-permute-start(bf16[96,640]{1,0:T(8,128)(2,1)S(1)} %collective-permute-done.refs_1_), channel_id=1, source_target_pairs={{0,8},{1,5},{2,10},{3,7},{8,16},{9,1},{10,18},{11,3},{16,24},{17,9... | collective-permute-start | bytes 368648 | tf_op jit(solution)/shard_map/ppermute | solution.py:91
  8.0 5.7 %collective-permute-start.5 = (bf16[96,640]{1,0:T(8,128)(2,1)S(1)}, bf16[96,640]{1,0:T(8,128)(2,1)S(1)}, u32[]{:S(2)}, u32[]{:S(2)}) collective-permute-start(bf16[96,640]{1,0:T(8,128)(2,1)S(1)} %collective-permute-done.4.refs_7_), channel_id=1, source_target_pairs={{0,4},{1,9},{2,6},{3,11},{8,0},{9,17},{10,2},{11,19},{16,8},{17,25... | collective-permute-start | bytes 368648 | tf_op jit(solution)/shard_map/ppermute | solution.py:91
  9.1 6.8 %collective-permute-start.11 = (bf16[96,640]{1,0:T(8,128)(2,1)S(1)}, bf16[96,640]{1,0:T(8,128)(2,1)S(1)}, u32[]{:S(2)}, u32[]{:S(2)}) collective-permute-start(bf16[96,640]{1,0:T(8,128)(2,1)S(1)} %collective-permute-done.10.refs_6_), channel_id=1, source_target_pairs={{0,4},{1,9},{2,6},{3,11},{8,0},{9,17},{10,2},{11,19},{16,8},{17,25... | collective-permute-start | bytes 368648 | tf_op jit(solution)/shard_map/ppermute | solution.py:91
  10.4 5.9 %collective-permute-start.14 = (bf16[96,640]{1,0:T(8,128)(2,1)S(1)}, bf16[96,640]{1,0:T(8,128)(2,1)S(1)}, u32[]{:S(2)}, u32[]{:S(2)}) collective-permute-start(bf16[96,640]{1,0:T(8,128)(2,1)S(1)} %collective-permute-done.13.refs_8_), channel_id=1, source_target_pairs={{0,8},{1,5},{2,10},{3,7},{8,16},{9,1},{10,18},{11,3},{16,24},{17,9... | collective-permute-start | bytes 368648 | tf_op jit(solution)/shard_map/ppermute | solution.py:91
  11.7 6.4 %collective-permute-start.17 = (bf16[96,640]{1,0:T(8,128)(2,1)S(1)}, bf16[96,640]{1,0:T(8,128)(2,1)S(1)}, u32[]{:S(2)}, u32[]{:S(2)}) collective-permute-start(bf16[96,640]{1,0:T(8,128)(2,1)S(1)} %collective-permute-done.16.refs_13_), channel_id=1, source_target_pairs={{0,4},{1,9},{2,6},{3,11},{8,0},{9,17},{10,2},{11,19},{16,8},{17,25... | collective-permute-start | bytes 368648 | tf_op jit(solution)/shard_map/ppermute | solution.py:91
  13.5 5.8 %collective-permute-start.2 = (bf16[96,640]{1,0:T(8,128)(2,1)S(1)}, bf16[96,640]{1,0:T(8,128)(2,1)S(1)}, u32[]{:S(2)}, u32[]{:S(2)}) collective-permute-start(bf16[96,640]{1,0:T(8,128)(2,1)S(1)} %collective-permute-done.1.refs_2_), channel_id=1, source_target_pairs={{0,8},{1,5},{2,10},{3,7},{8,16},{9,1},{10,18},{11,3},{16,24},{17,9... | collective-permute-start | bytes 368648 | tf_op jit(solution)/shard_map/ppermute | solution.py:91
  13.7 7.7 %collective-permute-start.8 = (bf16[96,640]{1,0:T(8,128)(2,1)S(1)}, bf16[96,640]{1,0:T(8,128)(2,1)S(1)}, u32[]{:S(2)}, u32[]{:S(2)}) collective-permute-start(bf16[96,640]{1,0:T(8,128)(2,1)S(1)} %collective-permute-done.7.refs_1_), channel_id=1, source_target_pairs={{0,8},{1,5},{2,10},{3,7},{8,16},{9,1},{10,18},{11,3},{16,24},{17,9... | collective-permute-start | bytes 368648 | tf_op jit(solution)/shard_map/ppermute | solution.py:91
  15.9 6.8 %collective-permute-start.6 = (bf16[96,640]{1,0:T(8,128)(2,1)S(1)}, bf16[96,640]{1,0:T(8,128)(2,1)S(1)}, u32[]{:S(2)}, u32[]{:S(2)}) collective-permute-start(bf16[96,640]{1,0:T(8,128)(2,1)S(1)} %collective-permute-done.5.refs_6_), channel_id=1, source_target_pairs={{0,4},{1,9},{2,6},{3,11},{8,0},{9,17},{10,2},{11,19},{16,8},{17,25... | collective-permute-start | bytes 368648 | tf_op jit(solution)/shard_map/ppermute | solution.py:91
  16.3 6.9 %collective-permute-start.12 = (bf16[96,640]{1,0:T(8,128)(2,1)S(1)}, bf16[96,640]{1,0:T(8,128)(2,1)S(1)}, u32[]{:S(2)}, u32[]{:S(2)}) collective-permute-start(bf16[96,640]{1,0:T(8,128)(2,1)S(1)} %collective-permute-done.11.refs_5_), channel_id=1, source_target_pairs={{0,4},{1,9},{2,6},{3,11},{8,0},{9,17},{10,2},{11,19},{16,8},{17,25... | collective-permute-start | bytes 368648 | tf_op jit(solution)/shard_map/ppermute | solution.py:91
  18.1 6.2 %collective-permute-start.15 = (bf16[96,640]{1,0:T(8,128)(2,1)S(1)}, bf16[96,640]{1,0:T(8,128)(2,1)S(1)}, u32[]{:S(2)}, u32[]{:S(2)}) collective-permute-start(bf16[96,640]{1,0:T(8,128)(2,1)S(1)} %collective-permute-done.14.refs_9_), channel_id=1, source_target_pairs={{0,8},{1,5},{2,10},{3,7},{8,16},{9,1},{10,18},{11,3},{16,24},{17,9... | collective-permute-start | bytes 368648 | tf_op jit(solution)/shard_map/ppermute | solution.py:91
  19.3 6.5 %collective-permute-start.3 = (bf16[96,640]{1,0:T(8,128)(2,1)S(1)}, bf16[96,640]{1,0:T(8,128)(2,1)S(1)}, u32[]{:S(2)}, u32[]{:S(2)}) collective-permute-start(bf16[96,640]{1,0:T(8,128)(2,1)S(1)} %collective-permute-done.2.refs_3_), channel_id=1, source_target_pairs={{0,8},{1,5},{2,10},{3,7},{8,16},{9,1},{10,18},{11,3},{16,24},{17,9... | collective-permute-start | bytes 368648 | tf_op jit(solution)/shard_map/ppermute | solution.py:91
  21.4 5.4 %collective-permute-start.18 = (bf16[96,640]{1,0:T(8,128)(2,1)S(1)}, bf16[96,640]{1,0:T(8,128)(2,1)S(1)}, u32[]{:S(2)}, u32[]{:S(2)}) collective-permute-start(bf16[96,640]{1,0:T(8,128)(2,1)S(1)} %collective-permute-done.17.refs_12_), channel_id=1, source_target_pairs={{0,4},{1,9},{2,6},{3,11},{8,0},{9,17},{10,2},{11,19},{16,8},{17,25... | collective-permute-start | bytes 368648 | tf_op jit(solution)/shard_map/ppermute | solution.py:91
  22.7 5.3 %collective-permute-start.9 = (bf16[96,640]{1,0:T(8,128)(2,1)S(1)}, bf16[96,640]{1,0:T(8,128)(2,1)S(1)}, u32[]{:S(2)}, u32[]{:S(2)}) collective-permute-start(bf16[96,640]{1,0:T(8,128)(2,1)S(1)} %collective-permute-done.8.refs_2_), channel_id=1, source_target_pairs={{0,8},{1,5},{2,10},{3,7},{8,16},{9,1},{10,18},{11,3},{16,24},{17,9... | collective-permute-start | bytes 368648 | tf_op jit(solution)/shard_map/ppermute | solution.py:91
  23.2 9.4 %collective-permute-start.19 = (bf16[96,640]{1,0:T(8,128)(2,1)S(1)}, bf16[96,640]{1,0:T(8,128)(2,1)S(1)}, u32[]{:S(2)}, u32[]{:S(2)}) collective-permute-start(bf16[96,640]{1,0:T(8,128)(2,1)S(1)} %collective-permute-done.12.refs_4_), channel_id=1, source_target_pairs={{0,4},{1,9},{2,6},{3,11},{8,0},{9,17},{10,2},{11,19},{16,8},{17,25... | collective-permute-start | bytes 368648 | tf_op jit(solution)/shard_map/ppermute | solution.py:91
  24.3 8.4 %collective-permute-start.20 = (bf16[96,640]{1,0:T(8,128)(2,1)S(1)}, bf16[96,640]{1,0:T(8,128)(2,1)S(1)}, u32[]{:S(2)}, u32[]{:S(2)}) collective-permute-start(bf16[96,640]{1,0:T(8,128)(2,1)S(1)} %collective-permute-done.15.refs_10_), channel_id=1, source_target_pairs={{0,8},{1,5},{2,10},{3,7},{8,16},{9,1},{10,18},{11,3},{16,24},{17,9... | collective-permute-start | bytes 368648 | tf_op jit(solution)/shard_map/ppermute | solution.py:91
  39.7 7.8 %collective-permute-start.23 = (bf16[96,640]{1,0:T(8,128)(2,1)S(1)}, bf16[96,640]{1,0:T(8,128)(2,1)S(1)}, u32[]{:S(2)}, u32[]{:S(2)}) collective-permute-start(bf16[96,640]{1,0:T(8,128)(2,1)S(1)} %get-tuple-element.20.refs_0_), channel_id=1, source_target_pairs={{0,2},{1,3},{2,0},{3,1},{4,6},{5,7},{6,4},{7,5},{8,10},{9,11},{10,... | collective-permute-start | bytes 368648 | tf_op jit(solution)/shard_map/ppermute | solution.py:293
  43.9 8.4 %collective-permute-start.26 = (bf16[96,640]{1,0:T(8,128)(2,1)S(1)}, bf16[96,640]{1,0:T(8,128)(2,1)S(1)}, u32[]{:S(2)}, u32[]{:S(2)}) collective-permute-start(bf16[96,640]{1,0:T(8,128)(2,1)S(1)} %shard_map.44), channel_id=1, source_target_pairs={{0,8},{1,12},{2,0},{3,4},{4,24},{5,28},{6,16},{7,20},{8,25},{9,29}... | collective-permute-start | bytes 368648 | tf_op jit(solution)/shard_map/ppermute | solution.py:305
  47.6 7.8 %collective-permute-start.24 = (bf16[96,640]{1,0:T(8,128)(2,1)S(1)}, bf16[96,640]{1,0:T(8,128)(2,1)S(1)}, u32[]{:S(2)}, u32[]{:S(2)}) collective-permute-start(bf16[96,640]{1,0:T(8,128)(2,1)S(1)} %shard_map.43), channel_id=1, source_target_pairs={{0,24},{1,28},{2,16},{3,20},{4,8},{5,12},{6,0},{7,4},{8,1},{9,5},{... | collective-permute-start | bytes 368648 | tf_op jit(solution)/shard_map/ppermute | solution.py:305
  (6 other events, 21.3 us)

commit v20 on v18

--- a/solution.py
+++ b/solution.py
@@ -154,7 +154,7 @@
     return mixed[:, :HD], mixed[:, HD:]
 
 
-PATTERNS = ((3, 0, 2, 1), (1, 3, 1, 3), (2, 1, 3, 0), (0, 2, 0, 2))
+PATTERNS = ((2, 0, 1, 3), (3, 1, 0, 2), (0, 2, 3, 1), (1, 3, 2, 0))
 
 
 def look_up(table, index):

time: 57 us -> 60.9 us (1.068); the launches traced: 56 us -> 60.7 us
  starting transfers between devices: 29.4 us -> 32.1 us
  waiting for transfers between devices: 14.3 us -> 16.2 us
    ppermute x2, starting transfers between devices: 6.79 us -> 9.47 us  [on_device_ring(): arrived.append(lax.ppermute(total, ('frames', 'heads'), pairs))]
    ppermute x2, waiting for transfers between devices: 4.52 us -> 6.42 us  [on_device_ring(): arrived.append(lax.ppermute(total, ('frames', 'heads'), pairs))]
  transfers between devices with their start and end apart: 26 -> 26, of which waited for: 15 -> 15; matrix products, arithmetic and copies ran while one was open for 0% -> 0% of each run, Pallas kernels for 13% -> 12%
where the time goes in v20:
time: 60.9 us; the launch traced here: 60.7 us
  starting transfers between devices  32.1 us (53%)
  waiting for transfers between devices  16.2 us (27%)
  Pallas kernels  9.43 us (15%)
  local copies, waits for them, and re-layouts  1.94 us (3%)
  other arithmetic  0.79 us (1%)
    ppermute x21, starting transfers between devices, hop(): return lax.ppermute(x, ('frames', 'heads'), pairs)  17.9 us
    ppermute x2, starting transfers between devices, on_device_ring(): arrived.append(lax.ppermute(total, ('frames', 'heads'), pairs))  9.47 us
    pallas_call x8, Pallas kernels, call(): pl.pallas_call(kernel, out_shape=[jax.ShapeDtypeStruct(shape, dtype) for...  9.43 us
    ppermute x21, waiting for transfers between devices, hop(): return lax.ppermute(x, ('frames', 'heads'), pairs)  8.01 us
    ppermute x2, waiting for transfers between devices, on_device_ring(): arrived.append(lax.ppermute(total, ('frames', 'heads'), pairs))  6.42 us
    ppermute x1, starting transfers between devices, on_device_ring(): from_core = lax.ppermute(given, 'heads', [(h, h ^ 1) for h in range(4)])  3.17 us
    unnamed x6, local copies, waits for them, and re-layouts  1.85 us
    ppermute x2, waiting for transfers between devices, on_device_ring(): lax.ppermute(block, 'heads', [(h, h ^ 2) for h in range(4)])  1.68 us
  transfers between devices with their start and end apart: 26, of which 15 were waited for; matrix products, arithmetic and copies ran while one was open for 0% of the time, Pallas kernels for 12%

profile of v20, /device:TPU:3, one launch (start us, length us, event | category | flops | bytes accessed | tf_op | source)
XLA Modules:
  0.0 60.7 jit_solution(9405431961094946554)
XLA Ops:
  0.0 1.2 %collective-permute-start = (bf16[96,640]{1,0:T(8,128)(2,1)}, bf16[96,640]{1,0:T(8,128)(2,1)S(1)}, u32[]{:S(2)}, u32[]{:S(2)}) collective-permute-start(bf16[96,640]{1,0:T(8,128)(2,1)} %refs_0_.1), channel_id=1, source_target_pairs={{0,8},{1,5},{2,10},{3,7},{8,16},{9,1},{10,18},{11,3},{16,24},{17,9... | collective-permute-start | bytes 368648 | tf_op jit(solution)/shard_map/ppermute | solution.py:91
  2.4 1.3 %collective-permute-start.10 = (bf16[96,640]{1,0:T(8,128)(2,1)S(1)}, bf16[96,640]{1,0:T(8,128)(2,1)S(1)}, u32[]{:S(2)}, u32[]{:S(2)}) collective-permute-start(bf16[96,640]{1,0:T(8,128)(2,1)S(1)} %get-tuple-element.10.refs_0_), channel_id=1, source_target_pairs={{0,4},{1,9},{2,6},{3,11},{8,0},{9,17},{10,2},{11,19},{16,8},{17,25... | collective-permute-start | bytes 368648 | tf_op jit(solution)/shard_map/ppermute | solution.py:91
  4.0 1.3 %collective-permute-start.16 = (bf16[96,640]{1,0:T(8,128)(2,1)S(1)}, bf16[96,640]{1,0:T(8,128)(2,1)S(1)}, u32[]{:S(2)}, u32[]{:S(2)}) collective-permute-start(bf16[96,640]{1,0:T(8,128)(2,1)S(1)} %get-tuple-element.11.refs_7_), channel_id=1, source_target_pairs={{0,4},{1,9},{2,6},{3,11},{8,0},{9,17},{10,2},{11,19},{16,8},{17,25... | collective-permute-start | bytes 368648 | tf_op jit(solution)/shard_map/ppermute | solution.py:91
  5.5 1.2 %collective-permute-done.4.refs_7_ = bf16[96,640]{1,0:T(8,128)(2,1)S(1)} collective-permute-done((bf16[96,640]{1,0:T(8,128)(2,1)}, bf16[96,640]{1,0:T(8,128)(2,1)S(1)}, u32[]{:S(2)}, u32[]{:S(2)}) %collective-permute-start.4) | collective-permute-done | bytes 122912 | tf_op jit(solution)/shard_map/ppermute | solution.py:91
  9.1 1.3 %collective-permute-start.11 = (bf16[96,640]{1,0:T(8,128)(2,1)S(1)}, bf16[96,640]{1,0:T(8,128)(2,1)S(1)}, u32[]{:S(2)}, u32[]{:S(2)}) collective-permute-start(bf16[96,640]{1,0:T(8,128)(2,1)S(1)} %collective-permute-done.10.refs_6_), channel_id=1, source_target_pairs={{0,4},{1,9},{2,6},{3,11},{8,0},{9,17},{10,2},{11,19},{16,8},{17,25... | collective-permute-start | bytes 368648 | tf_op jit(solution)/shard_map/ppermute | solution.py:91
  11.7 1.3 %collective-permute-start.17 = (bf16[96,640]{1,0:T(8,128)(2,1)S(1)}, bf16[96,640]{1,0:T(8,128)(2,1)S(1)}, u32[]{:S(2)}, u32[]{:S(2)}) collective-permute-start(bf16[96,640]{1,0:T(8,128)(2,1)S(1)} %collective-permute-done.16.refs_13_), channel_id=1, source_target_pairs={{0,4},{1,9},{2,6},{3,11},{8,0},{9,17},{10,2},{11,19},{16,8},{17,25... | collective-permute-start | bytes 368648 | tf_op jit(solution)/shard_map/ppermute | solution.py:91
  13.7 1.2 %collective-permute-start.8 = (bf16[96,640]{1,0:T(8,128)(2,1)S(1)}, bf16[96,640]{1,0:T(8,128)(2,1)S(1)}, u32[]{:S(2)}, u32[]{:S(2)}) collective-permute-start(bf16[96,640]{1,0:T(8,128)(2,1)S(1)} %collective-permute-done.7.refs_1_), channel_id=1, source_target_pairs={{0,8},{1,5},{2,10},{3,7},{8,16},{9,1},{10,18},{11,3},{16,24},{17,9... | collective-permute-start | bytes 368648 | tf_op jit(solution)/shard_map/ppermute | solution.py:91
  16.3 1.3 %collective-permute-start.12 = (bf16[96,640]{1,0:T(8,128)(2,1)S(1)}, bf16[96,640]{1,0:T(8,128)(2,1)S(1)}, u32[]{:S(2)}, u32[]{:S(2)}) collective-permute-start(bf16[96,640]{1,0:T(8,128)(2,1)S(1)} %collective-permute-done.11.refs_5_), channel_id=1, source_target_pairs={{0,4},{1,9},{2,6},{3,11},{8,0},{9,17},{10,2},{11,19},{16,8},{17,25... | collective-permute-start | bytes 368648 | tf_op jit(solution)/shard_map/ppermute | solution.py:91
  18.1 1.2 %collective-permute-start.15 = (bf16[96,640]{1,0:T(8,128)(2,1)S(1)}, bf16[96,640]{1,0:T(8,128)(2,1)S(1)}, u32[]{:S(2)}, u32[]{:S(2)}) collective-permute-start(bf16[96,640]{1,0:T(8,128)(2,1)S(1)} %collective-permute-done.14.refs_9_), channel_id=1, source_target_pairs={{0,8},{1,5},{2,10},{3,7},{8,16},{9,1},{10,18},{11,3},{16,24},{17,9... | collective-permute-start | bytes 368648 | tf_op jit(solution)/shard_map/ppermute | solution.py:91
  19.3 1.3 %collective-permute-start.3 = (bf16[96,640]{1,0:T(8,128)(2,1)S(1)}, bf16[96,640]{1,0:T(8,128)(2,1)S(1)}, u32[]{:S(2)}, u32[]{:S(2)}) collective-permute-start(bf16[96,640]{1,0:T(8,128)(2,1)S(1)} %collective-permute-done.2.refs_3_), channel_id=1, source_target_pairs={{0,8},{1,5},{2,10},{3,7},{8,16},{9,1},{10,18},{11,3},{16,24},{17,9... | collective-permute-start | bytes 368648 | tf_op jit(solution)/shard_map/ppermute | solution.py:91
  21.4 1.3 %collective-permute-start.18 = (bf16[96,640]{1,0:T(8,128)(2,1)S(1)}, bf16[96,640]{1,0:T(8,128)(2,1)S(1)}, u32[]{:S(2)}, u32[]{:S(2)}) collective-permute-start(bf16[96,640]{1,0:T(8,128)(2,1)S(1)} %collective-permute-done.17.refs_12_), channel_id=1, source_target_pairs={{0,4},{1,9},{2,6},{3,11},{8,0},{9,17},{10,2},{11,19},{16,8},{17,25... | collective-permute-start | bytes 368648 | tf_op jit(solution)/shard_map/ppermute | solution.py:91
  23.2 1.1 %collective-permute-start.19 = (bf16[96,640]{1,0:T(8,128)(2,1)S(1)}, bf16[96,640]{1,0:T(8,128)(2,1)S(1)}, u32[]{:S(2)}, u32[]{:S(2)}) collective-permute-start(bf16[96,640]{1,0:T(8,128)(2,1)S(1)} %collective-permute-done.12.refs_4_), channel_id=1, source_target_pairs={{0,4},{1,9},{2,6},{3,11},{8,0},{9,17},{10,2},{11,19},{16,8},{17,25... | collective-permute-start | bytes 368648 | tf_op jit(solution)/shard_map/ppermute | solution.py:91
  24.7 1.2 %collective-permute-done.3.refs_4_ = bf16[96,640]{1,0:T(8,128)(2,1)S(1)} collective-permute-done((bf16[96,640]{1,0:T(8,128)(2,1)S(1)}, bf16[96,640]{1,0:T(8,128)(2,1)S(1)}, u32[]{:S(2)}, u32[]{:S(2)}) %collective-permute-start.3) | collective-permute-done | bytes 122912 | tf_op jit(solution)/shard_map/ppermute | solution.py:91
  26.8 1.2 %collective-permute-done.9.refs_3_ = bf16[96,640]{1,0:T(8,128)(2,1)S(1)} collective-permute-done((bf16[96,640]{1,0:T(8,128)(2,1)S(1)}, bf16[96,640]{1,0:T(8,128)(2,1)S(1)}, u32[]{:S(2)}, u32[]{:S(2)}) %collective-permute-start.9) | collective-permute-done | bytes 122912 | tf_op jit(solution)/shard_map/ppermute | solution.py:91
  28.0 4.6 %shard_map.39 = (f32[5,8,96,128]{3,2,1,0:T(8,128)S(1)}, f32[5,8,96,128]{3,2,1,0:T(8,128)S(1)}, f32[5,8,96,128]{3,2,1,0:T(8,128)S(1)}) custom-call(s32[5]{0:T(128)S(1)} %stack.23.at_ref, bf16[8,96,640]{2,1,0:T(8,128)(2,1)S(1)} %shard_map.37.rows_ref, bf16[96,640]{1,0:T(8,128)(2,1)S(1)} %get-tuple-element.10.refs_0_, ...), custom_call_target="tpu_custom_call" | custom-call | flops 1321205760 | tf_op jit(solution)/shard_map/pallas_call | solution.py:243
  32.6 2.0 %shard_map.40 = bf16[384,640]{1,0:T(8,128)(2,1)S(1)} custom-call(s32[5]{0:T(128)S(1)} %stack.23.at_ref, bf16[8,96,640]{2,1,0:T(8,128)(2,1)S(1)} %shard_map.37.rows_ref, f32[5,8,96,128]{3,2,1,0:T(8,128)S(1)} %get-tuple-element.12.mixed_ref, f32[5,8,96,128]{3,2,1,0:T(8,128)S(1)} %get-tuple-element.13.sum_ref, f32[5,8,96,128]{3,2,1,0:T(8,128)S(1)} %get-tuple-element.14.top_ref, ...), custom_call_target="tpu_custom_call" | custom-call | flops 314572800 | tf_op jit(solution)/shard_map/pallas_call | solution.py:243
  34.6 3.2 %collective-permute-start.21 = (bf16[2,192,640]{2,1,0:T(8,128)(2,1)S(1)}, bf16[2,192,640]{2,1,0:T(8,128)(2,1)S(1)}, u32[]{:S(2)}, u32[]{:S(2)}) collective-permute-start(bf16[2,192,640]{2,1,0:T(8,128)(2,1)S(1)} %bitcast.16), channel_id=1, source_target_pairs={{0,1},{1,0},{2,3},{3,2},{4,5},{5,4},{6,7},{7,6},{8,9},{9,8},{10,11... | collective-permute-start | bytes 1474568 | tf_op jit(solution)/shard_map/ppermute | solution.py:288
  37.8 1.3 %shard_map.41 = f32[192,640]{1,0:T(8,128)S(1)} custom-call(s32[5]{0:T(128)S(1)} %stack.23.at_ref, bf16[8,96,640]{2,1,0:T(8,128)(2,1)S(1)} %shard_map.37.rows_ref, f32[5,8,96,128]{3,2,1,0:T(8,128)S(1)} %get-tuple-element.12.mixed_ref, f32[5,8,96,128]{3,2,1,0:T(8,128)S(1)} %get-tuple-element.13.sum_ref, f32[5,8,96,128]{3,2,1,0:T(8,128)S(1)} %get-tuple-element.14.top_ref, ...), custom_call_target="tpu_custom_call" | custom-call | flops 314572800 | tf_op jit(solution)/shard_map/pallas_call | solution.py:243
  39.6 1.2 %collective-permute-start.22 = (bf16[96,640]{1,0:T(8,128)(2,1)S(1)}, bf16[96,640]{1,0:T(8,128)(2,1)S(1)}, u32[]{:S(2)}, u32[]{:S(2)}) collective-permute-start(bf16[96,640]{1,0:T(8,128)(2,1)S(1)} %get-tuple-element.16.refs_0_), channel_id=1, source_target_pairs={{0,2},{1,3},{2,0},{3,1},{4,6},{5,7},{6,4},{7,5},{8,10},{9,11},{10,... | collective-permute-start | bytes 368648 | tf_op jit(solution)/shard_map/ppermute | solution.py:292
  40.9 1.4 %shard_map.42.kept_ref = f32[192,640]{1,0:T(8,128)S(1)} custom-call(s32[5]{0:T(128)S(1)} %stack.23.at_ref, bf16[8,96,640]{2,1,0:T(8,128)(2,1)S(1)} %shard_map.37.rows_ref, f32[5,8,96,128]{3,2,1,0:T(8,128)S(1)} %get-tuple-element.12.mixed_ref, f32[5,8,96,128]{3,2,1,0:T(8,128)S(1)} %get-tuple-element.13.sum_ref, ...), custom_call_target="tpu_custom_call" | custom-call | flops 314572800 | tf_op jit(solution)/shard_map/pallas_call | solution.py:243
  42.2 1.7 %collective-permute-done.24.from_x_ref = bf16[96,640]{1,0:T(8,128)(2,1)S(1)} collective-permute-done((bf16[96,640]{1,0:T(8,128)(2,1)S(1)}, bf16[96,640]{1,0:T(8,128)(2,1)S(1)}, u32[]{:S(2)}, u32[]{:S(2)}) %collective-permute-start.24) | collective-permute-done | bytes 122912 | tf_op jit(solution)/shard_map/ppermute | solution.py:292
  43.9 6.3 %collective-permute-start.25 = (bf16[96,640]{1,0:T(8,128)(2,1)S(1)}, bf16[96,640]{1,0:T(8,128)(2,1)S(1)}, u32[]{:S(2)}, u32[]{:S(2)}) collective-permute-start(bf16[96,640]{1,0:T(8,128)(2,1)S(1)} %shard_map.44), channel_id=1, source_target_pairs={{0,24},{1,28},{2,8},{3,12},{4,16},{5,20},{6,0},{7,4},{8,9},{9,13},... | collective-permute-start | bytes 368648 | tf_op jit(solution)/shard_map/ppermute | solution.py:304
  50.3 3.2 %collective-permute-start.23 = (bf16[96,640]{1,0:T(8,128)(2,1)S(1)}, bf16[96,640]{1,0:T(8,128)(2,1)S(1)}, u32[]{:S(2)}, u32[]{:S(2)}) collective-permute-start(bf16[96,640]{1,0:T(8,128)(2,1)S(1)} %shard_map.43), channel_id=1, source_target_pairs={{0,16},{1,20},{2,0},{3,4},{4,24},{5,28},{6,8},{7,12},{8,1},{9,5},{... | collective-permute-start | bytes 368648 | tf_op jit(solution)/shard_map/ppermute | solution.py:304
  54.2 5.7 %collective-permute-done.23 = bf16[96,640]{1,0:T(8,128)(2,1)S(1)} collective-permute-done((bf16[96,640]{1,0:T(8,128)(2,1)S(1)}, bf16[96,640]{1,0:T(8,128)(2,1)S(1)}, u32[]{:S(2)}, u32[]{:S(2)}) %collective-permute-start.23) | collective-permute-done | bytes 122912 | tf_op jit(solution)/shard_map/ppermute | solution.py:304
  (46 shorter events, 12.6 us)
Async XLA Ops:
  0.0 5.3 %collective-permute-start = (bf16[96,640]{1,0:T(8,128)(2,1)}, bf16[96,640]{1,0:T(8,128)(2,1)S(1)}, u32[]{:S(2)}, u32[]{:S(2)}) collective-permute-start(bf16[96,640]{1,0:T(8,128)(2,1)} %refs_0_.1), channel_id=1, source_target_pairs={{0,8},{1,5},{2,10},{3,7},{8,16},{9,1},{10,18},{11,3},{16,24},{17,9... | collective-permute-start | bytes 368648 | tf_op jit(solution)/shard_map/ppermute | solution.py:91
  1.2 5.4 %collective-permute-start.4 = (bf16[96,640]{1,0:T(8,128)(2,1)}, bf16[96,640]{1,0:T(8,128)(2,1)S(1)}, u32[]{:S(2)}, u32[]{:S(2)}) collective-permute-start(bf16[96,640]{1,0:T(8,128)(2,1)} %refs_0_.1), channel_id=1, source_target_pairs={{0,4},{1,9},{2,6},{3,11},{8,0},{9,17},{10,2},{11,19},{16,8},{17,25... | collective-permute-start | bytes 368648 | tf_op jit(solution)/shard_map/ppermute | solution.py:91
  2.4 5.6 %collective-permute-start.10 = (bf16[96,640]{1,0:T(8,128)(2,1)S(1)}, bf16[96,640]{1,0:T(8,128)(2,1)S(1)}, u32[]{:S(2)}, u32[]{:S(2)}) collective-permute-start(bf16[96,640]{1,0:T(8,128)(2,1)S(1)} %get-tuple-element.10.refs_0_), channel_id=1, source_target_pairs={{0,4},{1,9},{2,6},{3,11},{8,0},{9,17},{10,2},{11,19},{16,8},{17,25... | collective-permute-start | bytes 368648 | tf_op jit(solution)/shard_map/ppermute | solution.py:91
  3.8 5.3 %collective-permute-start.13 = (bf16[96,640]{1,0:T(8,128)(2,1)S(1)}, bf16[96,640]{1,0:T(8,128)(2,1)S(1)}, u32[]{:S(2)}, u32[]{:S(2)}) collective-permute-start(bf16[96,640]{1,0:T(8,128)(2,1)S(1)} %get-tuple-element.11.refs_7_), channel_id=1, source_target_pairs={{0,8},{1,5},{2,10},{3,7},{8,16},{9,1},{10,18},{11,3},{16,24},{17,9... | collective-permute-start | bytes 368648 | tf_op jit(solution)/shard_map/ppermute | solution.py:91
  4.0 6.5 %collective-permute-start.16 = (bf16[96,640]{1,0:T(8,128)(2,1)S(1)}, bf16[96,640]{1,0:T(8,128)(2,1)S(1)}, u32[]{:S(2)}, u32[]{:S(2)}) collective-permute-start(bf16[96,640]{1,0:T(8,128)(2,1)S(1)} %get-tuple-element.11.refs_7_), channel_id=1, source_target_pairs={{0,4},{1,9},{2,6},{3,11},{8,0},{9,17},{10,2},{11,19},{16,8},{17,25... | collective-permute-start | bytes 368648 | tf_op jit(solution)/shard_map/ppermute | solution.py:91
  5.3 6.5 %collective-permute-start.7 = (bf16[96,640]{1,0:T(8,128)(2,1)S(1)}, bf16[96,640]{1,0:T(8,128)(2,1)S(1)}, u32[]{:S(2)}, u32[]{:S(2)}) collective-permute-start(bf16[96,640]{1,0:T(8,128)(2,1)S(1)} %get-tuple-element.10.refs_0_), channel_id=1, source_target_pairs={{0,8},{1,5},{2,10},{3,7},{8,16},{9,1},{10,18},{11,3},{16,24},{17,9... | collective-permute-start | bytes 368648 | tf_op jit(solution)/shard_map/ppermute | solution.py:91
  6.7 6.8 %collective-permute-start.1 = (bf16[96,640]{1,0:T(8,128)(2,1)S(1)}, bf16[96,640]{1,0:T(8,128)(2,1)S(1)}, u32[]{:S(2)}, u32[]{:S(2)}) collective-permute-start(bf16[96,640]{1,0:T(8,128)(2,1)S(1)} %collective-permute-done.refs_1_), channel_id=1, source_target_pairs={{0,8},{1,5},{2,10},{3,7},{8,16},{9,1},{10,18},{11,3},{16,24},{17,9... | collective-permute-start | bytes 368648 | tf_op jit(solution)/shard_map/ppermute | solution.py:91
  8.0 5.7 %collective-permute-start.5 = (bf16[96,640]{1,0:T(8,128)(2,1)S(1)}, bf16[96,640]{1,0:T(8,128)(2,1)S(1)}, u32[]{:S(2)}, u32[]{:S(2)}) collective-permute-start(bf16[96,640]{1,0:T(8,128)(2,1)S(1)} %collective-permute-done.4.refs_7_), channel_id=1, source_target_pairs={{0,4},{1,9},{2,6},{3,11},{8,0},{9,17},{10,2},{11,19},{16,8},{17,25... | collective-permute-start | bytes 368648 | tf_op jit(solution)/shard_map/ppermute | solution.py:91
  9.1 6.8 %collective-permute-start.11 = (bf16[96,640]{1,0:T(8,128)(2,1)S(1)}, bf16[96,640]{1,0:T(8,128)(2,1)S(1)}, u32[]{:S(2)}, u32[]{:S(2)}) collective-permute-start(bf16[96,640]{1,0:T(8,128)(2,1)S(1)} %collective-permute-done.10.refs_6_), channel_id=1, source_target_pairs={{0,4},{1,9},{2,6},{3,11},{8,0},{9,17},{10,2},{11,19},{16,8},{17,25... | collective-permute-start | bytes 368648 | tf_op jit(solution)/shard_map/ppermute | solution.py:91
  10.4 5.9 %collective-permute-start.14 = (bf16[96,640]{1,0:T(8,128)(2,1)S(1)}, bf16[96,640]{1,0:T(8,128)(2,1)S(1)}, u32[]{:S(2)}, u32[]{:S(2)}) collective-permute-start(bf16[96,640]{1,0:T(8,128)(2,1)S(1)} %collective-permute-done.13.refs_8_), channel_id=1, source_target_pairs={{0,8},{1,5},{2,10},{3,7},{8,16},{9,1},{10,18},{11,3},{16,24},{17,9... | collective-permute-start | bytes 368648 | tf_op jit(solution)/shard_map/ppermute | solution.py:91
  11.7 6.4 %collective-permute-start.17 = (bf16[96,640]{1,0:T(8,128)(2,1)S(1)}, bf16[96,640]{1,0:T(8,128)(2,1)S(1)}, u32[]{:S(2)}, u32[]{:S(2)}) collective-permute-start(bf16[96,640]{1,0:T(8,128)(2,1)S(1)} %collective-permute-done.16.refs_13_), channel_id=1, source_target_pairs={{0,4},{1,9},{2,6},{3,11},{8,0},{9,17},{10,2},{11,19},{16,8},{17,25... | collective-permute-start | bytes 368648 | tf_op jit(solution)/shard_map/ppermute | solution.py:91
  13.5 5.8 %collective-permute-start.2 = (bf16[96,640]{1,0:T(8,128)(2,1)S(1)}, bf16[96,640]{1,0:T(8,128)(2,1)S(1)}, u32[]{:S(2)}, u32[]{:S(2)}) collective-permute-start(bf16[96,640]{1,0:T(8,128)(2,1)S(1)} %collective-permute-done.1.refs_2_), channel_id=1, source_target_pairs={{0,8},{1,5},{2,10},{3,7},{8,16},{9,1},{10,18},{11,3},{16,24},{17,9... | collective-permute-start | bytes 368648 | tf_op jit(solution)/shard_map/ppermute | solution.py:91
  13.7 7.7 %collective-permute-start.8 = (bf16[96,640]{1,0:T(8,128)(2,1)S(1)}, bf16[96,640]{1,0:T(8,128)(2,1)S(1)}, u32[]{:S(2)}, u32[]{:S(2)}) collective-permute-start(bf16[96,640]{1,0:T(8,128)(2,1)S(1)} %collective-permute-done.7.refs_1_), channel_id=1, source_target_pairs={{0,8},{1,5},{2,10},{3,7},{8,16},{9,1},{10,18},{11,3},{16,24},{17,9... | collective-permute-start | bytes 368648 | tf_op jit(solution)/shard_map/ppermute | solution.py:91
  15.9 6.8 %collective-permute-start.6 = (bf16[96,640]{1,0:T(8,128)(2,1)S(1)}, bf16[96,640]{1,0:T(8,128)(2,1)S(1)}, u32[]{:S(2)}, u32[]{:S(2)}) collective-permute-start(bf16[96,640]{1,0:T(8,128)(2,1)S(1)} %collective-permute-done.5.refs_6_), channel_id=1, source_target_pairs={{0,4},{1,9},{2,6},{3,11},{8,0},{9,17},{10,2},{11,19},{16,8},{17,25... | collective-permute-start | bytes 368648 | tf_op jit(solution)/shard_map/ppermute | solution.py:91
  16.3 6.9 %collective-permute-start.12 = (bf16[96,640]{1,0:T(8,128)(2,1)S(1)}, bf16[96,640]{1,0:T(8,128)(2,1)S(1)}, u32[]{:S(2)}, u32[]{:S(2)}) collective-permute-start(bf16[96,640]{1,0:T(8,128)(2,1)S(1)} %collective-permute-done.11.refs_5_), channel_id=1, source_target_pairs={{0,4},{1,9},{2,6},{3,11},{8,0},{9,17},{10,2},{11,19},{16,8},{17,25... | collective-permute-start | bytes 368648 | tf_op jit(solution)/shard_map/ppermute | solution.py:91
  18.1 6.2 %collective-permute-start.15 = (bf16[96,640]{1,0:T(8,128)(2,1)S(1)}, bf16[96,640]{1,0:T(8,128)(2,1)S(1)}, u32[]{:S(2)}, u32[]{:S(2)}) collective-permute-start(bf16[96,640]{1,0:T(8,128)(2,1)S(1)} %collective-permute-done.14.refs_9_), channel_id=1, source_target_pairs={{0,8},{1,5},{2,10},{3,7},{8,16},{9,1},{10,18},{11,3},{16,24},{17,9... | collective-permute-start | bytes 368648 | tf_op jit(solution)/shard_map/ppermute | solution.py:91
  19.3 6.5 %collective-permute-start.3 = (bf16[96,640]{1,0:T(8,128)(2,1)S(1)}, bf16[96,640]{1,0:T(8,128)(2,1)S(1)}, u32[]{:S(2)}, u32[]{:S(2)}) collective-permute-start(bf16[96,640]{1,0:T(8,128)(2,1)S(1)} %collective-permute-done.2.refs_3_), channel_id=1, source_target_pairs={{0,8},{1,5},{2,10},{3,7},{8,16},{9,1},{10,18},{11,3},{16,24},{17,9... | collective-permute-start | bytes 368648 | tf_op jit(solution)/shard_map/ppermute | solution.py:91
  21.4 5.4 %collective-permute-start.18 = (bf16[96,640]{1,0:T(8,128)(2,1)S(1)}, bf16[96,640]{1,0:T(8,128)(2,1)S(1)}, u32[]{:S(2)}, u32[]{:S(2)}) collective-permute-start(bf16[96,640]{1,0:T(8,128)(2,1)S(1)} %collective-permute-done.17.refs_12_), channel_id=1, source_target_pairs={{0,4},{1,9},{2,6},{3,11},{8,0},{9,17},{10,2},{11,19},{16,8},{17,25... | collective-permute-start | bytes 368648 | tf_op jit(solution)/shard_map/ppermute | solution.py:91
  22.7 5.3 %collective-permute-start.9 = (bf16[96,640]{1,0:T(8,128)(2,1)S(1)}, bf16[96,640]{1,0:T(8,128)(2,1)S(1)}, u32[]{:S(2)}, u32[]{:S(2)}) collective-permute-start(bf16[96,640]{1,0:T(8,128)(2,1)S(1)} %collective-permute-done.8.refs_2_), channel_id=1, source_target_pairs={{0,8},{1,5},{2,10},{3,7},{8,16},{9,1},{10,18},{11,3},{16,24},{17,9... | collective-permute-start | bytes 368648 | tf_op jit(solution)/shard_map/ppermute | solution.py:91
  23.2 9.4 %collective-permute-start.19 = (bf16[96,640]{1,0:T(8,128)(2,1)S(1)}, bf16[96,640]{1,0:T(8,128)(2,1)S(1)}, u32[]{:S(2)}, u32[]{:S(2)}) collective-permute-start(bf16[96,640]{1,0:T(8,128)(2,1)S(1)} %collective-permute-done.12.refs_4_), channel_id=1, source_target_pairs={{0,4},{1,9},{2,6},{3,11},{8,0},{9,17},{10,2},{11,19},{16,8},{17,25... | collective-permute-start | bytes 368648 | tf_op jit(solution)/shard_map/ppermute | solution.py:91
  24.3 8.3 %collective-permute-start.20 = (bf16[96,640]{1,0:T(8,128)(2,1)S(1)}, bf16[96,640]{1,0:T(8,128)(2,1)S(1)}, u32[]{:S(2)}, u32[]{:S(2)}) collective-permute-start(bf16[96,640]{1,0:T(8,128)(2,1)S(1)} %collective-permute-done.15.refs_10_), channel_id=1, source_target_pairs={{0,8},{1,5},{2,10},{3,7},{8,16},{9,1},{10,18},{11,3},{16,24},{17,9... | collective-permute-start | bytes 368648 | tf_op jit(solution)/shard_map/ppermute | solution.py:91
  39.6 10.6 %collective-permute-start.22 = (bf16[96,640]{1,0:T(8,128)(2,1)S(1)}, bf16[96,640]{1,0:T(8,128)(2,1)S(1)}, u32[]{:S(2)}, u32[]{:S(2)}) collective-permute-start(bf16[96,640]{1,0:T(8,128)(2,1)S(1)} %get-tuple-element.16.refs_0_), channel_id=1, source_target_pairs={{0,2},{1,3},{2,0},{3,1},{4,6},{5,7},{6,4},{7,5},{8,10},{9,11},{10,... | collective-permute-start | bytes 368648 | tf_op jit(solution)/shard_map/ppermute | solution.py:292
  43.9 10.3 %collective-permute-start.25 = (bf16[96,640]{1,0:T(8,128)(2,1)S(1)}, bf16[96,640]{1,0:T(8,128)(2,1)S(1)}, u32[]{:S(2)}, u32[]{:S(2)}) collective-permute-start(bf16[96,640]{1,0:T(8,128)(2,1)S(1)} %shard_map.44), channel_id=1, source_target_pairs={{0,24},{1,28},{2,8},{3,12},{4,16},{5,20},{6,0},{7,4},{8,9},{9,13},... | collective-permute-start | bytes 368648 | tf_op jit(solution)/shard_map/ppermute | solution.py:304
  50.3 9.6 %collective-permute-start.23 = (bf16[96,640]{1,0:T(8,128)(2,1)S(1)}, bf16[96,640]{1,0:T(8,128)(2,1)S(1)}, u32[]{:S(2)}, u32[]{:S(2)}) collective-permute-start(bf16[96,640]{1,0:T(8,128)(2,1)S(1)} %shard_map.43), channel_id=1, source_target_pairs={{0,16},{1,20},{2,0},{3,4},{4,24},{5,28},{6,8},{7,12},{8,1},{9,5},{... | collective-permute-start | bytes 368648 | tf_op jit(solution)/shard_map/ppermute | solution.py:304
  (5 other events, 16.9 us)

commit v21 on v15

--- a/solution.py
+++ b/solution.py
@@ -154,7 +154,7 @@
     return mixed[:, :HD], mixed[:, HD:]
 
 
-PATTERNS = ((2, 1, 2, 1), (0, 3, 0, 3), (3, 0, 1, 2), (1, 2, 3, 0))
+PATTERNS = ((3, 0, 2, 1), (1, 3, 1, 3), (2, 1, 3, 0), (0, 2, 0, 2))
 
 
 def look_up(table, index):
@@ -172,11 +172,9 @@
     return blocks
 
 
-def add_keys(mixed, total, before, scores, values):
-    weights, top = soften(scores, before)
-    more, more_total = mix(weights, values)
+def add_keys(mixed, total, before, top, more):
     kept = jnp.exp2((before - top) * SCALE)
-    return more + mixed * kept, more_total + total * kept, top
+    return more[0] + mixed * kept, more[1] + total * kept
 
 
 def ahead(scores, heads):
@@ -214,7 +212,8 @@
         values = rows_of(value_refs, cols, padding)
         if state:
             mixed, total, before = (ref[head].reshape(n * ROWS, HD) for ref in state)
-            mixed, total, top = add_keys(mixed, total, before, now, values)
+            weights, top = soften(now, before)
+            mixed, total = add_keys(mixed, total, before, top, mix(weights, values))
         else:
             weights, top = soften(now)
             mixed, total = mix(weights, values)
@@ -226,29 +225,29 @@
     blocks = [block for flip in flips for block in slot_blocks(at_ref, *flip, n)]
     marks = frame_marks(at_ref, blocks, n)
     keys_marks = key_marks([n // 2], TPF, n)
-    attended = []
 
     def of(ref, head):
         return jnp.concatenate([ref[head, block] for block in blocks], axis=0)
 
-    def scores(cols):
+    columns = [slice(head * HD, (head + 1) * HD) for head in range(heads)]
+    scores, attended = [], []
+    for cols in columns:
         queries = jnp.concatenate([rows_ref[block, :, cols] for block in blocks], axis=0)
         keys = jnp.concatenate([rows_of([keys_ref], cols, TPF), keys_marks], axis=1)
-        return scores_of(jnp.concatenate([queries, marks], axis=1), keys)
-
-    for head, cols, now in ahead(scores, heads):
-        values = rows_of([values_ref], cols, TPF)
-        mixed, total, _ = add_keys(of(mixed_ref, head), of(sum_ref, head), of(top_ref, head), now, values)
+        scores.append(scores_of(jnp.concatenate([queries, marks], axis=1), keys))
+    softened = [soften(now, of(top_ref, head)) for head, now in enumerate(scores)]
+    more = [mix(weights, rows_of([values_ref], cols, TPF)) for (weights, _), cols in zip(softened, columns)]
+    for head, ((_, top), (mixed, total)) in enumerate(zip(softened, more)):
+        now = mixed, total
+        mixed, total = add_keys(of(mixed_ref, head), of(sum_ref, head), of(top_ref, head), top, now)
         attended.append((mixed / total).astype(jnp.bfloat16))
     rows = jnp.concatenate(attended, axis=1)
     refs[-1][...] = jnp.dot(rows, w_ref[...], preferred_element_type=jnp.float32).astype(refs[-1].dtype)
 
 
-def sum_kernel(half, rows, others, own_ref, from_core_ref, *refs):
-    total = own_ref[rows] + from_core_ref[half, rows].astype(jnp.float32)
-    for ref in refs[:others]:
-        total += ref[...].astype(jnp.float32)
-    refs[-1][...] = total.astype(refs[-1].dtype)
+def sum_kernel(rows, kept_ref, from_core_ref, from_x_ref, total_ref):
+    total = kept_ref[rows] + from_core_ref[1, rows].astype(jnp.float32) + from_x_ref[...].astype(jnp.float32)
+    total_ref[...] = total.astype(total_ref.dtype)
 
 
 def call(kernel, scalars, operands, outs, flops, after=()):
@@ -303,16 +302,9 @@
     from_core = lax.ppermute(given, "heads", [(h, h ^ 1) for h in range(4)])
     sums = finish([(1, 0)], f32, (given,))[0]
     parts = [slice(slot * ROWS, (slot + 1) * ROWS) for slot in range(2)]
-
-    def add(half, part, own, others=(), after=()):
-        kernel = functools.partial(sum_kernel, half, part, len(others))
-        return call(kernel, (), [own, from_core, *others], [((ROWS, cols), bf16)], 0, after)[0]
-
-    to_x = [(h, h ^ 2) for h in range(4)]
-    given = add(0, parts[0], sums)
-    from_x = [lax.ppermute(given, "heads", to_x)]
-    kept = finish([(0, 0)], f32, (given,))[0]
-    from_x.append(lax.ppermute(add(0, parts[1], sums, (), (kept,)), "heads", to_x))
+    given = [(sums[part] + from_core[0, part].astype(f32)).astype(bf16) for part in parts]
+    from_x = [lax.ppermute(block, "heads", [(h, h ^ 2) for h in range(4)]) for block in given]
+    kept = finish([(0, 0)], f32, given)[0]
     arrived = []
     for slot, part in enumerate(parts):
         pairs = []
@@ -320,7 +312,9 @@
             for h in range(4):
                 to = PATTERNS[(slot ^ (f & 1)) + 2 * (h >> 1)][f >> 1]
                 pairs.append((4 * f + h, 4 * (2 * to + (h & 1)) + (f >> 1)))
-        total = add(1, part, kept, [from_x[slot]])
+        (total,) = call(
+            functools.partial(sum_kernel, part), (), [kept, from_core, from_x[slot]], [((ROWS, cols), bf16)], 0
+        )
         arrived.append(lax.ppermute(total, ("frames", "heads"), pairs))
     patterns = [[p[source] for p in PATTERNS].index(to) for source in range(4) for to in range(4)]
     straight = look_up(patterns, 4 * head + z) & 1 == 0

time: 61.3 us -> 57.2 us (0.933)
  waiting for transfers between devices: 17 us -> 14.4 us
  starting transfers between devices: 29.7 us -> 28.7 us
    ppermute x2, waiting for transfers between devices: 6.08 us -> 4.49 us  [on_device_ring(): arrived.append(lax.ppermute(total, ('frames', 'heads'), pairs))]
    ppermute x2, waiting for transfers between devices: 3.08 us -> 2.02 us  [on_device_ring(): lax.ppermute(block, 'heads', [(h, h ^ 2) for h in range(4)])]
    ppermute x2, starting transfers between devices: 7.42 us -> 6.4 us  [on_device_ring(): arrived.append(lax.ppermute(total, ('frames', 'heads'), pairs))]
    pallas_call x11 -> x9, Pallas kernels: 10.7 us -> 10.6 us  [call(): pl.pallas_call(kernel, out_shape=[jax.ShapeDtypeStruct(shape, dtype) for...]
  transfers between devices with their start and end apart: 26 -> 26, of which waited for: 13 -> 14; matrix products, arithmetic and copies ran while one was open for 0% -> 0% of each run, Pallas kernels for 12% -> 15%
where the time goes in v21:
time: 57.2 us; the launch traced here: 56.5 us
  starting transfers between devices  28.7 us (50%)
  waiting for transfers between devices  14.4 us (25%)
  Pallas kernels  10.6 us (19%)
  local copies, waits for them, and re-layouts  1.93 us (3%)
  other arithmetic  0.79 us (1%)
    ppermute x21, starting transfers between devices, hop(): return lax.ppermute(x, ('frames', 'heads'), pairs)  16.6 us
    pallas_call x9, Pallas kernels, call(): pl.pallas_call(kernel, out_shape=[jax.ShapeDtypeStruct(shape, dtype) for...  10.6 us
    ppermute x21, waiting for transfers between devices, hop(): return lax.ppermute(x, ('frames', 'heads'), pairs)  7.76 us
    ppermute x2, starting transfers between devices, on_device_ring(): arrived.append(lax.ppermute(total, ('frames', 'heads'), pairs))  6.4 us
    ppermute x2, waiting for transfers between devices, on_device_ring(): arrived.append(lax.ppermute(total, ('frames', 'heads'), pairs))  4.49 us
    ppermute x1, starting transfers between devices, on_device_ring(): from_core = lax.ppermute(given, 'heads', [(h, h ^ 1) for h in range(4)])  4.18 us
    ppermute x2, waiting for transfers between devices, on_device_ring(): lax.ppermute(block, 'heads', [(h, h ^ 2) for h in range(4)])  2.02 us
    unnamed x6, local copies, waits for them, and re-layouts  1.85 us
  transfers between devices with their start and end apart: 26, of which 14 were waited for; matrix products, arithmetic and copies ran while one was open for 0% of the time, Pallas kernels for 15%

profile of v21, /device:TPU:3, one launch (start us, length us, event | category | flops | bytes accessed | tf_op | source)
XLA Modules:
  0.0 56.5 jit_solution(9864005227099812036)
XLA Ops:
  0.0 1.2 %collective-permute-start = (bf16[96,640]{1,0:T(8,128)(2,1)}, bf16[96,640]{1,0:T(8,128)(2,1)S(1)}, u32[]{:S(2)}, u32[]{:S(2)}) collective-permute-start(bf16[96,640]{1,0:T(8,128)(2,1)} %queries_ref.1), channel_id=1, source_target_pairs={{0,8},{1,5},{2,10},{3,7},{8,16},{9,1},{10,18},{11,3},{16,24},{17,9... | collective-permute-start | bytes 368648 | tf_op jit(solution)/shard_map/ppermute | solution.py:91
  3.3 1.3 %collective-permute-start.10 = (bf16[96,640]{1,0:T(8,128)(2,1)S(1)}, bf16[96,640]{1,0:T(8,128)(2,1)S(1)}, u32[]{:S(2)}, u32[]{:S(2)}) collective-permute-start(bf16[96,640]{1,0:T(8,128)(2,1)S(1)} %get-tuple-element.15.refs_0_), channel_id=1, source_target_pairs={{0,4},{1,9},{2,6},{3,11},{8,0},{9,17},{10,2},{11,19},{16,8},{17,25... | collective-permute-start | bytes 368648 | tf_op jit(solution)/shard_map/ppermute | solution.py:91
  4.9 1.3 %collective-permute-start.16 = (bf16[96,640]{1,0:T(8,128)(2,1)S(1)}, bf16[96,640]{1,0:T(8,128)(2,1)S(1)}, u32[]{:S(2)}, u32[]{:S(2)}) collective-permute-start(bf16[96,640]{1,0:T(8,128)(2,1)S(1)} %get-tuple-element.16.refs_5_), channel_id=1, source_target_pairs={{0,4},{1,9},{2,6},{3,11},{8,0},{9,17},{10,2},{11,19},{16,8},{17,25... | collective-permute-start | bytes 368648 | tf_op jit(solution)/shard_map/ppermute | solution.py:91
  8.4 1.3 %collective-permute-done.13.refs_6_ = bf16[96,640]{1,0:T(8,128)(2,1)S(1)} collective-permute-done((bf16[96,640]{1,0:T(8,128)(2,1)S(1)}, bf16[96,640]{1,0:T(8,128)(2,1)S(1)}, u32[]{:S(2)}, u32[]{:S(2)}) %collective-permute-start.13) | collective-permute-done | bytes 122912 | tf_op jit(solution)/shard_map/ppermute | solution.py:91
  9.7 1.3 %collective-permute-start.11 = (bf16[96,640]{1,0:T(8,128)(2,1)S(1)}, bf16[96,640]{1,0:T(8,128)(2,1)S(1)}, u32[]{:S(2)}, u32[]{:S(2)}) collective-permute-start(bf16[96,640]{1,0:T(8,128)(2,1)S(1)} %collective-permute-done.10.refs_4_), channel_id=1, source_target_pairs={{0,4},{1,9},{2,6},{3,11},{8,0},{9,17},{10,2},{11,19},{16,8},{17,25... | collective-permute-start | bytes 368648 | tf_op jit(solution)/shard_map/ppermute | solution.py:91
  11.2 1.2 %collective-permute-done.7.refs_1_ = bf16[96,640]{1,0:T(8,128)(2,1)S(1)} collective-permute-done((bf16[96,640]{1,0:T(8,128)(2,1)S(1)}, bf16[96,640]{1,0:T(8,128)(2,1)S(1)}, u32[]{:S(2)}, u32[]{:S(2)}) %collective-permute-start.7) | collective-permute-done | bytes 122912 | tf_op jit(solution)/shard_map/ppermute | solution.py:91
  12.4 1.3 %collective-permute-start.17 = (bf16[96,640]{1,0:T(8,128)(2,1)S(1)}, bf16[96,640]{1,0:T(8,128)(2,1)S(1)}, u32[]{:S(2)}, u32[]{:S(2)}) collective-permute-start(bf16[96,640]{1,0:T(8,128)(2,1)S(1)} %collective-permute-done.16.refs_9_), channel_id=1, source_target_pairs={{0,4},{1,9},{2,6},{3,11},{8,0},{9,17},{10,2},{11,19},{16,8},{17,25... | collective-permute-start | bytes 368648 | tf_op jit(solution)/shard_map/ppermute | solution.py:91
  14.3 1.2 %collective-permute-start.8 = (bf16[96,640]{1,0:T(8,128)(2,1)S(1)}, bf16[96,640]{1,0:T(8,128)(2,1)S(1)}, u32[]{:S(2)}, u32[]{:S(2)}) collective-permute-start(bf16[96,640]{1,0:T(8,128)(2,1)S(1)} %collective-permute-done.7.refs_1_), channel_id=1, source_target_pairs={{0,8},{1,5},{2,10},{3,7},{8,16},{9,1},{10,18},{11,3},{16,24},{17,9... | collective-permute-start | bytes 368648 | tf_op jit(solution)/shard_map/ppermute | solution.py:91
  16.6 1.3 %collective-permute-start.12 = (bf16[96,640]{1,0:T(8,128)(2,1)S(1)}, bf16[96,640]{1,0:T(8,128)(2,1)S(1)}, u32[]{:S(2)}, u32[]{:S(2)}) collective-permute-start(bf16[96,640]{1,0:T(8,128)(2,1)S(1)} %collective-permute-done.11.refs_3_), channel_id=1, source_target_pairs={{0,4},{1,9},{2,6},{3,11},{8,0},{9,17},{10,2},{11,19},{16,8},{17,25... | collective-permute-start | bytes 368648 | tf_op jit(solution)/shard_map/ppermute | solution.py:91
  19.9 2.0 %collective-permute-done.8.refs_2_ = bf16[96,640]{1,0:T(8,128)(2,1)S(1)} collective-permute-done((bf16[96,640]{1,0:T(8,128)(2,1)S(1)}, bf16[96,640]{1,0:T(8,128)(2,1)S(1)}, u32[]{:S(2)}, u32[]{:S(2)}) %collective-permute-start.8) | collective-permute-done | bytes 122912 | tf_op jit(solution)/shard_map/ppermute | solution.py:91
  21.9 1.3 %collective-permute-start.18 = (bf16[96,640]{1,0:T(8,128)(2,1)S(1)}, bf16[96,640]{1,0:T(8,128)(2,1)S(1)}, u32[]{:S(2)}, u32[]{:S(2)}) collective-permute-start(bf16[96,640]{1,0:T(8,128)(2,1)S(1)} %collective-permute-done.17.refs_8_), channel_id=1, source_target_pairs={{0,4},{1,9},{2,6},{3,11},{8,0},{9,17},{10,2},{11,19},{16,8},{17,25... | collective-permute-start | bytes 368648 | tf_op jit(solution)/shard_map/ppermute | solution.py:91
  23.4 1.3 %collective-permute-start.19 = (bf16[96,640]{1,0:T(8,128)(2,1)S(1)}, bf16[96,640]{1,0:T(8,128)(2,1)S(1)}, u32[]{:S(2)}, u32[]{:S(2)}) collective-permute-start(bf16[96,640]{1,0:T(8,128)(2,1)S(1)} %collective-permute-done.12.refs_1_), channel_id=1, source_target_pairs={{0,4},{1,9},{2,6},{3,11},{8,0},{9,17},{10,2},{11,19},{16,8},{17,25... | collective-permute-start | bytes 368648 | tf_op jit(solution)/shard_map/ppermute | solution.py:91
  24.9 1.4 %collective-permute-done.3.refs_4_ = bf16[96,640]{1,0:T(8,128)(2,1)S(1)} collective-permute-done((bf16[96,640]{1,0:T(8,128)(2,1)S(1)}, bf16[96,640]{1,0:T(8,128)(2,1)S(1)}, u32[]{:S(2)}, u32[]{:S(2)}) %collective-permute-start.3) | collective-permute-done | bytes 122912 | tf_op jit(solution)/shard_map/ppermute | solution.py:91
  26.4 3.2 %shard_map.39 = (f32[5,8,96,128]{3,2,1,0:T(8,128)S(1)}, f32[5,8,96,128]{3,2,1,0:T(8,128)S(1)}, f32[5,8,96,128]{3,2,1,0:T(8,128)S(1)}) custom-call(s32[5]{0:T(128)S(1)} %stack.23.at_ref, bf16[8,96,640]{2,1,0:T(8,128)(2,1)S(1)} %shard_map.38.rows_ref, bf16[96,640]{1,0:T(8,128)(2,1)S(1)} %get-tuple-element.15.refs_0_, ...), custom_call_target="tpu_custom_call" | custom-call | flops 943718400 | tf_op jit(solution)/shard_map/pallas_call | solution.py:255
  29.6 2.5 %shard_map.40 = (f32[5,8,96,128]{3,2,1,0:T(8,128)S(1)}, f32[5,8,96,128]{3,2,1,0:T(8,128)S(1)}, f32[5,8,96,128]{3,2,1,0:T(8,128)S(1)}) custom-call(s32[5]{0:T(128)S(1)} %stack.23.at_ref, bf16[8,96,640]{2,1,0:T(8,128)(2,1)S(1)} %shard_map.38.rows_ref, bf16[96,640]{1,0:T(8,128)(2,1)S(1)} %collective-permute-done.9.refs_0_, ...), custom_call_target="tpu_custom_call" | custom-call | flops 377487360 | tf_op jit(solution)/shard_map/pallas_call | solution.py:255
  32.2 2.0 %shard_map.41 = bf16[384,640]{1,0:T(8,128)(2,1)S(1)} custom-call(s32[5]{0:T(128)S(1)} %stack.23.at_ref, bf16[8,96,640]{2,1,0:T(8,128)(2,1)S(1)} %shard_map.38.rows_ref, f32[5,8,96,128]{3,2,1,0:T(8,128)S(1)} %get-tuple-element.20.mixed_ref, f32[5,8,96,128]{3,2,1,0:T(8,128)S(1)} %get-tuple-element.21.sum_ref, f32[5,8,96,128]{3,2,1,0:T(8,128)S(1)} %get-tuple-element.22.top_ref, ...), custom_call_target="tpu_custom_call" | custom-call | flops 314572800 | tf_op jit(solution)/shard_map/pallas_call | solution.py:255
  34.1 4.2 %collective-permute-start.21 = (bf16[2,192,640]{2,1,0:T(8,128)(2,1)S(1)}, bf16[2,192,640]{2,1,0:T(8,128)(2,1)S(1)}, u32[]{:S(2)}, u32[]{:S(2)}) collective-permute-start(bf16[2,192,640]{2,1,0:T(8,128)(2,1)S(1)} %bitcast.16), channel_id=1, source_target_pairs={{0,1},{1,0},{2,3},{3,2},{4,5},{5,4},{6,7},{7,6},{8,9},{9,8},{10,11... | collective-permute-start | bytes 1474568 | tf_op jit(solution)/shard_map/ppermute | solution.py:302
  38.3 1.4 %shard_map.42 = f32[192,640]{1,0:T(8,128)S(1)} custom-call(s32[5]{0:T(128)S(1)} %stack.23.at_ref, bf16[8,96,640]{2,1,0:T(8,128)(2,1)S(1)} %shard_map.38.rows_ref, f32[5,8,96,128]{3,2,1,0:T(8,128)S(1)} %get-tuple-element.20.mixed_ref, f32[5,8,96,128]{3,2,1,0:T(8,128)S(1)} %get-tuple-element.21.sum_ref, f32[5,8,96,128]{3,2,1,0:T(8,128)S(1)} %get-tuple-element.22.top_ref, ...), custom_call_target="tpu_custom_call" | custom-call | flops 314572800 | tf_op jit(solution)/shard_map/pallas_call | solution.py:255
  40.0 1.4 %collective-permute-start.22 = (bf16[96,640]{1,0:T(8,128)(2,1)S(1)}, bf16[96,640]{1,0:T(8,128)(2,1)S(1)}, u32[]{:S(2)}, u32[]{:S(2)}) collective-permute-start(bf16[96,640]{1,0:T(8,128)(2,1)S(1)} %get-tuple-element.24.refs_0_), channel_id=1, source_target_pairs={{0,2},{1,3},{2,0},{3,1},{4,6},{5,7},{6,4},{7,5},{8,10},{9,11},{10,... | collective-permute-start | bytes 368648 | tf_op jit(solution)/shard_map/ppermute | solution.py:306
  41.4 1.4 %shard_map.43.kept_ref = f32[192,640]{1,0:T(8,128)S(1)} custom-call(s32[5]{0:T(128)S(1)} %stack.23.at_ref, bf16[8,96,640]{2,1,0:T(8,128)(2,1)S(1)} %shard_map.38.rows_ref, f32[5,8,96,128]{3,2,1,0:T(8,128)S(1)} %get-tuple-element.20.mixed_ref, f32[5,8,96,128]{3,2,1,0:T(8,128)S(1)} %get-tuple-element.21.sum_ref, ...), custom_call_target="tpu_custom_call" | custom-call | flops 314572800 | tf_op jit(solution)/shard_map/pallas_call | solution.py:255
  42.7 1.7 %collective-permute-done.24.from_x_ref = bf16[96,640]{1,0:T(8,128)(2,1)S(1)} collective-permute-done((bf16[96,640]{1,0:T(8,128)(2,1)S(1)}, bf16[96,640]{1,0:T(8,128)(2,1)S(1)}, u32[]{:S(2)}, u32[]{:S(2)}) %collective-permute-start.24) | collective-permute-done | bytes 122912 | tf_op jit(solution)/shard_map/ppermute | solution.py:306
  44.5 2.3 %collective-permute-start.25 = (bf16[96,640]{1,0:T(8,128)(2,1)S(1)}, bf16[96,640]{1,0:T(8,128)(2,1)S(1)}, u32[]{:S(2)}, u32[]{:S(2)}) collective-permute-start(bf16[96,640]{1,0:T(8,128)(2,1)S(1)} %shard_map.45), channel_id=1, source_target_pairs={{0,8},{1,12},{2,0},{3,4},{4,24},{5,28},{6,16},{7,20},{8,25},{9,29}... | collective-permute-start | bytes 368648 | tf_op jit(solution)/shard_map/ppermute | solution.py:318
  47.1 4.1 %collective-permute-start.23 = (bf16[96,640]{1,0:T(8,128)(2,1)S(1)}, bf16[96,640]{1,0:T(8,128)(2,1)S(1)}, u32[]{:S(2)}, u32[]{:S(2)}) collective-permute-start(bf16[96,640]{1,0:T(8,128)(2,1)S(1)} %shard_map.44), channel_id=1, source_target_pairs={{0,24},{1,28},{2,16},{3,20},{4,8},{5,12},{6,0},{7,4},{8,1},{9,5},{... | collective-permute-start | bytes 368648 | tf_op jit(solution)/shard_map/ppermute | solution.py:318
  52.4 3.3 %collective-permute-done.23 = bf16[96,640]{1,0:T(8,128)(2,1)S(1)} collective-permute-done((bf16[96,640]{1,0:T(8,128)(2,1)S(1)}, bf16[96,640]{1,0:T(8,128)(2,1)S(1)}, u32[]{:S(2)}, u32[]{:S(2)}) %collective-permute-start.23) | collective-permute-done | bytes 122912 | tf_op jit(solution)/shard_map/ppermute | solution.py:318
  (47 shorter events, 11.6 us)
Async XLA Ops:
  0.0 6.2 %collective-permute-start = (bf16[96,640]{1,0:T(8,128)(2,1)}, bf16[96,640]{1,0:T(8,128)(2,1)S(1)}, u32[]{:S(2)}, u32[]{:S(2)}) collective-permute-start(bf16[96,640]{1,0:T(8,128)(2,1)} %queries_ref.1), channel_id=1, source_target_pairs={{0,8},{1,5},{2,10},{3,7},{8,16},{9,1},{10,18},{11,3},{16,24},{17,9... | collective-permute-start | bytes 368648 | tf_op jit(solution)/shard_map/ppermute | solution.py:91
  1.2 5.4 %collective-permute-start.4 = (bf16[96,640]{1,0:T(8,128)(2,1)}, bf16[96,640]{1,0:T(8,128)(2,1)S(1)}, u32[]{:S(2)}, u32[]{:S(2)}) collective-permute-start(bf16[96,640]{1,0:T(8,128)(2,1)} %queries_ref.1), channel_id=1, source_target_pairs={{0,4},{1,9},{2,6},{3,11},{8,0},{9,17},{10,2},{11,19},{16,8},{17,25... | collective-permute-start | bytes 368648 | tf_op jit(solution)/shard_map/ppermute | solution.py:91
  4.7 5.0 %collective-permute-start.13 = (bf16[96,640]{1,0:T(8,128)(2,1)S(1)}, bf16[96,640]{1,0:T(8,128)(2,1)S(1)}, u32[]{:S(2)}, u32[]{:S(2)}) collective-permute-start(bf16[96,640]{1,0:T(8,128)(2,1)S(1)} %get-tuple-element.16.refs_5_), channel_id=1, source_target_pairs={{0,8},{1,5},{2,10},{3,7},{8,16},{9,1},{10,18},{11,3},{16,24},{17,9... | collective-permute-start | bytes 368648 | tf_op jit(solution)/shard_map/ppermute | solution.py:91
  4.9 6.2 %collective-permute-start.16 = (bf16[96,640]{1,0:T(8,128)(2,1)S(1)}, bf16[96,640]{1,0:T(8,128)(2,1)S(1)}, u32[]{:S(2)}, u32[]{:S(2)}) collective-permute-start(bf16[96,640]{1,0:T(8,128)(2,1)S(1)} %get-tuple-element.16.refs_5_), channel_id=1, source_target_pairs={{0,4},{1,9},{2,6},{3,11},{8,0},{9,17},{10,2},{11,19},{16,8},{17,25... | collective-permute-start | bytes 368648 | tf_op jit(solution)/shard_map/ppermute | solution.py:91
  6.2 6.2 %collective-permute-start.7 = (bf16[96,640]{1,0:T(8,128)(2,1)S(1)}, bf16[96,640]{1,0:T(8,128)(2,1)S(1)}, u32[]{:S(2)}, u32[]{:S(2)}) collective-permute-start(bf16[96,640]{1,0:T(8,128)(2,1)S(1)} %get-tuple-element.15.refs_0_), channel_id=1, source_target_pairs={{0,8},{1,5},{2,10},{3,7},{8,16},{9,1},{10,18},{11,3},{16,24},{17,9... | collective-permute-start | bytes 368648 | tf_op jit(solution)/shard_map/ppermute | solution.py:91
  6.7 7.3 %collective-permute-start.1 = (bf16[96,640]{1,0:T(8,128)(2,1)S(1)}, bf16[96,640]{1,0:T(8,128)(2,1)S(1)}, u32[]{:S(2)}, u32[]{:S(2)}) collective-permute-start(bf16[96,640]{1,0:T(8,128)(2,1)S(1)} %collective-permute-done.refs_1_), channel_id=1, source_target_pairs={{0,8},{1,5},{2,10},{3,7},{8,16},{9,1},{10,18},{11,3},{16,24},{17,9... | collective-permute-start | bytes 368648 | tf_op jit(solution)/shard_map/ppermute | solution.py:91
  8.0 6.3 %collective-permute-start.5 = (bf16[96,640]{1,0:T(8,128)(2,1)S(1)}, bf16[96,640]{1,0:T(8,128)(2,1)S(1)}, u32[]{:S(2)}, u32[]{:S(2)}) collective-permute-start(bf16[96,640]{1,0:T(8,128)(2,1)S(1)} %collective-permute-done.4.refs_7_), channel_id=1, source_target_pairs={{0,4},{1,9},{2,6},{3,11},{8,0},{9,17},{10,2},{11,19},{16,8},{17,25... | collective-permute-start | bytes 368648 | tf_op jit(solution)/shard_map/ppermute | solution.py:91
  9.7 5.8 %collective-permute-start.11 = (bf16[96,640]{1,0:T(8,128)(2,1)S(1)}, bf16[96,640]{1,0:T(8,128)(2,1)S(1)}, u32[]{:S(2)}, u32[]{:S(2)}) collective-permute-start(bf16[96,640]{1,0:T(8,128)(2,1)S(1)} %collective-permute-done.10.refs_4_), channel_id=1, source_target_pairs={{0,4},{1,9},{2,6},{3,11},{8,0},{9,17},{10,2},{11,19},{16,8},{17,25... | collective-permute-start | bytes 368648 | tf_op jit(solution)/shard_map/ppermute | solution.py:91
  11.0 5.6 %collective-permute-start.14 = (bf16[96,640]{1,0:T(8,128)(2,1)S(1)}, bf16[96,640]{1,0:T(8,128)(2,1)S(1)}, u32[]{:S(2)}, u32[]{:S(2)}) collective-permute-start(bf16[96,640]{1,0:T(8,128)(2,1)S(1)} %collective-permute-done.13.refs_6_), channel_id=1, source_target_pairs={{0,8},{1,5},{2,10},{3,7},{8,16},{9,1},{10,18},{11,3},{16,24},{17,9... | collective-permute-start | bytes 368648 | tf_op jit(solution)/shard_map/ppermute | solution.py:91
  12.4 5.6 %collective-permute-start.17 = (bf16[96,640]{1,0:T(8,128)(2,1)S(1)}, bf16[96,640]{1,0:T(8,128)(2,1)S(1)}, u32[]{:S(2)}, u32[]{:S(2)}) collective-permute-start(bf16[96,640]{1,0:T(8,128)(2,1)S(1)} %collective-permute-done.16.refs_9_), channel_id=1, source_target_pairs={{0,4},{1,9},{2,6},{3,11},{8,0},{9,17},{10,2},{11,19},{16,8},{17,25... | collective-permute-start | bytes 368648 | tf_op jit(solution)/shard_map/ppermute | solution.py:91
  14.0 5.4 %collective-permute-start.2 = (bf16[96,640]{1,0:T(8,128)(2,1)S(1)}, bf16[96,640]{1,0:T(8,128)(2,1)S(1)}, u32[]{:S(2)}, u32[]{:S(2)}) collective-permute-start(bf16[96,640]{1,0:T(8,128)(2,1)S(1)} %collective-permute-done.1.refs_2_), channel_id=1, source_target_pairs={{0,8},{1,5},{2,10},{3,7},{8,16},{9,1},{10,18},{11,3},{16,24},{17,9... | collective-permute-start | bytes 368648 | tf_op jit(solution)/shard_map/ppermute | solution.py:91
  14.3 7.6 %collective-permute-start.8 = (bf16[96,640]{1,0:T(8,128)(2,1)S(1)}, bf16[96,640]{1,0:T(8,128)(2,1)S(1)}, u32[]{:S(2)}, u32[]{:S(2)}) collective-permute-start(bf16[96,640]{1,0:T(8,128)(2,1)S(1)} %collective-permute-done.7.refs_1_), channel_id=1, source_target_pairs={{0,8},{1,5},{2,10},{3,7},{8,16},{9,1},{10,18},{11,3},{16,24},{17,9... | collective-permute-start | bytes 368648 | tf_op jit(solution)/shard_map/ppermute | solution.py:91
  15.5 7.7 %collective-permute-start.6 = (bf16[96,640]{1,0:T(8,128)(2,1)S(1)}, bf16[96,640]{1,0:T(8,128)(2,1)S(1)}, u32[]{:S(2)}, u32[]{:S(2)}) collective-permute-start(bf16[96,640]{1,0:T(8,128)(2,1)S(1)} %collective-permute-done.5.refs_6_), channel_id=1, source_target_pairs={{0,4},{1,9},{2,6},{3,11},{8,0},{9,17},{10,2},{11,19},{16,8},{17,25... | collective-permute-start | bytes 368648 | tf_op jit(solution)/shard_map/ppermute | solution.py:91
  16.6 6.8 %collective-permute-start.12 = (bf16[96,640]{1,0:T(8,128)(2,1)S(1)}, bf16[96,640]{1,0:T(8,128)(2,1)S(1)}, u32[]{:S(2)}, u32[]{:S(2)}) collective-permute-start(bf16[96,640]{1,0:T(8,128)(2,1)S(1)} %collective-permute-done.11.refs_3_), channel_id=1, source_target_pairs={{0,4},{1,9},{2,6},{3,11},{8,0},{9,17},{10,2},{11,19},{16,8},{17,25... | collective-permute-start | bytes 368648 | tf_op jit(solution)/shard_map/ppermute | solution.py:91
  17.9 6.8 %collective-permute-start.15 = (bf16[96,640]{1,0:T(8,128)(2,1)S(1)}, bf16[96,640]{1,0:T(8,128)(2,1)S(1)}, u32[]{:S(2)}, u32[]{:S(2)}) collective-permute-start(bf16[96,640]{1,0:T(8,128)(2,1)S(1)} %collective-permute-done.14.refs_7_), channel_id=1, source_target_pairs={{0,8},{1,5},{2,10},{3,7},{8,16},{9,1},{10,18},{11,3},{16,24},{17,9... | collective-permute-start | bytes 368648 | tf_op jit(solution)/shard_map/ppermute | solution.py:91
  19.4 6.9 %collective-permute-start.3 = (bf16[96,640]{1,0:T(8,128)(2,1)S(1)}, bf16[96,640]{1,0:T(8,128)(2,1)S(1)}, u32[]{:S(2)}, u32[]{:S(2)}) collective-permute-start(bf16[96,640]{1,0:T(8,128)(2,1)S(1)} %collective-permute-done.2.refs_3_), channel_id=1, source_target_pairs={{0,8},{1,5},{2,10},{3,7},{8,16},{9,1},{10,18},{11,3},{16,24},{17,9... | collective-permute-start | bytes 368648 | tf_op jit(solution)/shard_map/ppermute | solution.py:91
  21.9 7.7 %collective-permute-start.18 = (bf16[96,640]{1,0:T(8,128)(2,1)S(1)}, bf16[96,640]{1,0:T(8,128)(2,1)S(1)}, u32[]{:S(2)}, u32[]{:S(2)}) collective-permute-start(bf16[96,640]{1,0:T(8,128)(2,1)S(1)} %collective-permute-done.17.refs_8_), channel_id=1, source_target_pairs={{0,4},{1,9},{2,6},{3,11},{8,0},{9,17},{10,2},{11,19},{16,8},{17,25... | collective-permute-start | bytes 368648 | tf_op jit(solution)/shard_map/ppermute | solution.py:91
  23.2 6.4 %collective-permute-start.9 = (bf16[96,640]{1,0:T(8,128)(2,1)S(1)}, bf16[96,640]{1,0:T(8,128)(2,1)S(1)}, u32[]{:S(2)}, u32[]{:S(2)}) collective-permute-start(bf16[96,640]{1,0:T(8,128)(2,1)S(1)} %collective-permute-done.8.refs_2_), channel_id=1, source_target_pairs={{0,8},{1,5},{2,10},{3,7},{8,16},{9,1},{10,18},{11,3},{16,24},{17,9... | collective-permute-start | bytes 368648 | tf_op jit(solution)/shard_map/ppermute | solution.py:91
  23.4 8.7 %collective-permute-start.19 = (bf16[96,640]{1,0:T(8,128)(2,1)S(1)}, bf16[96,640]{1,0:T(8,128)(2,1)S(1)}, u32[]{:S(2)}, u32[]{:S(2)}) collective-permute-start(bf16[96,640]{1,0:T(8,128)(2,1)S(1)} %collective-permute-done.12.refs_1_), channel_id=1, source_target_pairs={{0,4},{1,9},{2,6},{3,11},{8,0},{9,17},{10,2},{11,19},{16,8},{17,25... | collective-permute-start | bytes 368648 | tf_op jit(solution)/shard_map/ppermute | solution.py:91
  24.7 7.4 %collective-permute-start.20 = (bf16[96,640]{1,0:T(8,128)(2,1)S(1)}, bf16[96,640]{1,0:T(8,128)(2,1)S(1)}, u32[]{:S(2)}, u32[]{:S(2)}) collective-permute-start(bf16[96,640]{1,0:T(8,128)(2,1)S(1)} %collective-permute-done.15.refs_2_), channel_id=1, source_target_pairs={{0,8},{1,5},{2,10},{3,7},{8,16},{9,1},{10,18},{11,3},{16,24},{17,9... | collective-permute-start | bytes 368648 | tf_op jit(solution)/shard_map/ppermute | solution.py:91
  34.1 5.7 %collective-permute-start.21 = (bf16[2,192,640]{2,1,0:T(8,128)(2,1)S(1)}, bf16[2,192,640]{2,1,0:T(8,128)(2,1)S(1)}, u32[]{:S(2)}, u32[]{:S(2)}) collective-permute-start(bf16[2,192,640]{2,1,0:T(8,128)(2,1)S(1)} %bitcast.16), channel_id=1, source_target_pairs={{0,1},{1,0},{2,3},{3,2},{4,5},{5,4},{6,7},{7,6},{8,9},{9,8},{10,11... | collective-permute-start | bytes 1474568 | tf_op jit(solution)/shard_map/ppermute | solution.py:302
  40.0 7.1 %collective-permute-start.22 = (bf16[96,640]{1,0:T(8,128)(2,1)S(1)}, bf16[96,640]{1,0:T(8,128)(2,1)S(1)}, u32[]{:S(2)}, u32[]{:S(2)}) collective-permute-start(bf16[96,640]{1,0:T(8,128)(2,1)S(1)} %get-tuple-element.24.refs_0_), channel_id=1, source_target_pairs={{0,2},{1,3},{2,0},{3,1},{4,6},{5,7},{6,4},{7,5},{8,10},{9,11},{10,... | collective-permute-start | bytes 368648 | tf_op jit(solution)/shard_map/ppermute | solution.py:306
  44.5 7.9 %collective-permute-start.25 = (bf16[96,640]{1,0:T(8,128)(2,1)S(1)}, bf16[96,640]{1,0:T(8,128)(2,1)S(1)}, u32[]{:S(2)}, u32[]{:S(2)}) collective-permute-start(bf16[96,640]{1,0:T(8,128)(2,1)S(1)} %shard_map.45), channel_id=1, source_target_pairs={{0,8},{1,12},{2,0},{3,4},{4,24},{5,28},{6,16},{7,20},{8,25},{9,29}... | collective-permute-start | bytes 368648 | tf_op jit(solution)/shard_map/ppermute | solution.py:318
  47.1 8.6 %collective-permute-start.23 = (bf16[96,640]{1,0:T(8,128)(2,1)S(1)}, bf16[96,640]{1,0:T(8,128)(2,1)S(1)}, u32[]{:S(2)}, u32[]{:S(2)}) collective-permute-start(bf16[96,640]{1,0:T(8,128)(2,1)S(1)} %shard_map.44), channel_id=1, source_target_pairs={{0,24},{1,28},{2,16},{3,20},{4,8},{5,12},{6,0},{7,4},{8,1},{9,5},{... | collective-permute-start | bytes 368648 | tf_op jit(solution)/shard_map/ppermute | solution.py:318
  (5 other events, 13.6 us)

commit v22 on v18

--- a/solution.py
+++ b/solution.py
@@ -93,11 +93,18 @@
 
 def gather_ring(streams, n):
     found = [[block] + [None] * (n - 1) for block in streams]
-    for step in range(1, n // 2 + 1):
+    far, half = n // 2, ROWS // 2
+    for step in range(1, far + 1):
         for j, blocks in enumerate(found):
-            for by in (1, -1):
-                if step < n // 2 or (j % 2 == 0) == (by == 1):
-                    blocks[by * step % n] = hop(blocks[by * (step - 1) % n], n, by)
+            before = {by: blocks[by * (step - 1) % n] for by in (1, -1)}
+            if step < far:
+                for by in (1, -1):
+                    blocks[by * step % n] = hop(before[by], n, by)
+            elif j == 0:
+                blocks[far] = hop(before[1][:half], n, 1), hop(before[-1][half:], n, -1)
+            else:
+                by = 1 if j % 2 == 0 else -1
+                blocks[far] = hop(before[by], n, by)
     return found
 
 
@@ -187,8 +194,12 @@
 
 
 def rows_kernel(n, *refs):
-    for d in range(n):
-        refs[n][d] = refs[d][...]
+    far, half = n // 2, ROWS // 2
+    *query_refs, top_ref, bottom_ref, rows_ref = refs
+    for d, ref in zip([d for d in range(n) if d != far], query_refs):
+        rows_ref[d] = ref[...]
+    rows_ref[far, :half] = top_ref[...]
+    rows_ref[far, half:] = bottom_ref[...]
 
 
 def near_kernel(heads, n, at_ref, rows_ref, *refs):
@@ -263,8 +274,9 @@
     block = (queries.shape, bf16)
     own = call(split_kernel, (), [keys_values], [block, block], 0)
     queries, keys, values = gather_ring([queries, *own], n)
+    far = n // 2
+    queries = [*queries[:far], *queries[far + 1 :], *queries[far]]
     (rows,) = call(functools.partial(rows_kernel, n), (), queries, [((n, ROWS, width), bf16)], 0)
-    far = n // 2
     state = call(
         functools.partial(near_kernel, heads, n),
         (where,),

time: 57 us -> 60 us (1.053)
  the two profiles are of different devices: /device:TPU:3 before, /device:TPU:16 now
where the time goes in v22:
time: 60 us; the launch traced here: 59.9 us
  starting transfers between devices  26 us (43%)
  waiting for transfers between devices  21.6 us (36%)
  Pallas kernels  9.45 us (16%)
  local copies, waits for them, and re-layouts  1.95 us (3%)
  other arithmetic  0.79 us (1%)
    ppermute x22, starting transfers between devices, hop(): return lax.ppermute(x, ('frames', 'heads'), pairs)  22.4 us
    pallas_call x8, Pallas kernels, call(): pl.pallas_call(kernel, out_shape=[jax.ShapeDtypeStruct(shape, dtype) for...  9.45 us
    ppermute x22, waiting for transfers between devices, hop(): return lax.ppermute(x, ('frames', 'heads'), pairs)  8.61 us
    ppermute x2, waiting for transfers between devices, on_device_ring(): arrived.append(lax.ppermute(total, ('frames', 'heads'), pairs))  6.65 us
    ppermute x2, waiting for transfers between devices, on_device_ring(): lax.ppermute(block, 'heads', [(h, h ^ 2) for h in range(4)])  5.83 us
    ppermute x2, starting transfers between devices, on_device_ring(): lax.ppermute(block, 'heads', [(h, h ^ 2) for h in range(4)])  2.09 us
    unnamed x6, local copies, waits for them, and re-layouts  1.85 us
    ppermute x2, starting transfers between devices, on_device_ring(): arrived.append(lax.ppermute(total, ('frames', 'heads'), pairs))  1.43 us
  transfers between devices with their start and end apart: 27, of which 13 were waited for; matrix products, arithmetic and copies ran while one was open for 0% of the time, Pallas kernels for 12%

profile of v22, /device:TPU:16, one launch (start us, length us, event | category | flops | bytes accessed | tf_op | source)
XLA Modules:
  0.0 59.9 jit_solution(8049596712075082593)
XLA Ops:
  0.0 1.6 %collective-permute-start = (bf16[96,640]{1,0:T(8,128)(2,1)}, bf16[96,640]{1,0:T(8,128)(2,1)S(1)}, u32[]{:S(2)}, u32[]{:S(2)}) collective-permute-start(bf16[96,640]{1,0:T(8,128)(2,1)} %refs_0_.1), channel_id=1, source_target_pairs={{0,8},{1,5},{2,10},{3,7},{8,16},{9,1},{10,18},{11,3},{16,24},{17,9... | collective-permute-start | bytes 368648 | tf_op jit(solution)/shard_map/ppermute | solution.py:91
  3.5 1.6 %collective-permute-start.14 = (bf16[96,640]{1,0:T(8,128)(2,1)S(1)}, bf16[96,640]{1,0:T(8,128)(2,1)S(1)}, u32[]{:S(2)}, u32[]{:S(2)}) collective-permute-start(bf16[96,640]{1,0:T(8,128)(2,1)S(1)} %get-tuple-element.11.refs_7_), channel_id=1, source_target_pairs={{0,8},{1,5},{2,10},{3,7},{8,16},{9,1},{10,18},{11,3},{16,24},{17,9... | collective-permute-start | bytes 368648 | tf_op jit(solution)/shard_map/ppermute | solution.py:91
  5.1 1.6 %collective-permute-start.8 = (bf16[96,640]{1,0:T(8,128)(2,1)S(1)}, bf16[96,640]{1,0:T(8,128)(2,1)S(1)}, u32[]{:S(2)}, u32[]{:S(2)}) collective-permute-start(bf16[96,640]{1,0:T(8,128)(2,1)S(1)} %get-tuple-element.10.refs_0_), channel_id=1, source_target_pairs={{0,8},{1,5},{2,10},{3,7},{8,16},{9,1},{10,18},{11,3},{16,24},{17,9... | collective-permute-start | bytes 368648 | tf_op jit(solution)/shard_map/ppermute | solution.py:91
  7.1 1.5 %collective-permute-start.1 = (bf16[96,640]{1,0:T(8,128)(2,1)S(1)}, bf16[96,640]{1,0:T(8,128)(2,1)S(1)}, u32[]{:S(2)}, u32[]{:S(2)}) collective-permute-start(bf16[96,640]{1,0:T(8,128)(2,1)S(1)} %collective-permute-done.refs_1_), channel_id=1, source_target_pairs={{0,8},{1,5},{2,10},{3,7},{8,16},{9,1},{10,18},{11,3},{16,24},{17,9... | collective-permute-start | bytes 368648 | tf_op jit(solution)/shard_map/ppermute | solution.py:91
  10.7 1.2 %collective-permute-done.8.refs_1_ = bf16[96,640]{1,0:T(8,128)(2,1)S(1)} collective-permute-done((bf16[96,640]{1,0:T(8,128)(2,1)S(1)}, bf16[96,640]{1,0:T(8,128)(2,1)S(1)}, u32[]{:S(2)}, u32[]{:S(2)}) %collective-permute-start.8) | collective-permute-done | bytes 122912 | tf_op jit(solution)/shard_map/ppermute | solution.py:91
  11.9 1.6 %collective-permute-start.15 = (bf16[96,640]{1,0:T(8,128)(2,1)S(1)}, bf16[96,640]{1,0:T(8,128)(2,1)S(1)}, u32[]{:S(2)}, u32[]{:S(2)}) collective-permute-start(bf16[96,640]{1,0:T(8,128)(2,1)S(1)} %collective-permute-done.14.refs_8_), channel_id=1, source_target_pairs={{0,8},{1,5},{2,10},{3,7},{8,16},{9,1},{10,18},{11,3},{16,24},{17,9... | collective-permute-start | bytes 368648 | tf_op jit(solution)/shard_map/ppermute | solution.py:91
  13.5 1.6 %collective-permute-start.9 = (bf16[96,640]{1,0:T(8,128)(2,1)S(1)}, bf16[96,640]{1,0:T(8,128)(2,1)S(1)}, u32[]{:S(2)}, u32[]{:S(2)}) collective-permute-start(bf16[96,640]{1,0:T(8,128)(2,1)S(1)} %collective-permute-done.8.refs_1_), channel_id=1, source_target_pairs={{0,8},{1,5},{2,10},{3,7},{8,16},{9,1},{10,18},{11,3},{16,24},{17,9... | collective-permute-start | bytes 368648 | tf_op jit(solution)/shard_map/ppermute | solution.py:91
  15.6 1.5 %collective-permute-start.2 = (bf16[96,640]{1,0:T(8,128)(2,1)S(1)}, bf16[96,640]{1,0:T(8,128)(2,1)S(1)}, u32[]{:S(2)}, u32[]{:S(2)}) collective-permute-start(bf16[96,640]{1,0:T(8,128)(2,1)S(1)} %collective-permute-done.1.refs_2_), channel_id=1, source_target_pairs={{0,8},{1,5},{2,10},{3,7},{8,16},{9,1},{10,18},{11,3},{16,24},{17,9... | collective-permute-start | bytes 368648 | tf_op jit(solution)/shard_map/ppermute | solution.py:91
  17.2 1.1 %collective-permute-done.12.refs_5_ = bf16[96,640]{1,0:T(8,128)(2,1)S(1)} collective-permute-done((bf16[96,640]{1,0:T(8,128)(2,1)S(1)}, bf16[96,640]{1,0:T(8,128)(2,1)S(1)}, u32[]{:S(2)}, u32[]{:S(2)}) %collective-permute-start.12) | collective-permute-done | bytes 122912 | tf_op jit(solution)/shard_map/ppermute | solution.py:91
  20.3 1.6 %collective-permute-start.16 = (bf16[96,640]{1,0:T(8,128)(2,1)S(1)}, bf16[96,640]{1,0:T(8,128)(2,1)S(1)}, u32[]{:S(2)}, u32[]{:S(2)}) collective-permute-start(bf16[96,640]{1,0:T(8,128)(2,1)S(1)} %collective-permute-done.15.refs_9_), channel_id=1, source_target_pairs={{0,8},{1,5},{2,10},{3,7},{8,16},{9,1},{10,18},{11,3},{16,24},{17,9... | collective-permute-start | bytes 368648 | tf_op jit(solution)/shard_map/ppermute | solution.py:91
  24.4 1.5 %collective-permute-start.6 = (bf16[48,640]{1,0:T(8,128)(2,1)S(1)}, bf16[48,640]{1,0:T(8,128)(2,1)S(1)}, u32[]{:S(2)}, u32[]{:S(2)}) collective-permute-start(bf16[48,640]{1,0:T(8,128)(2,1)S(1)} %slice.24), channel_id=1, source_target_pairs={{0,8},{1,5},{2,10},{3,7},{8,16},{9,1},{10,18},{11,3},{16,24},{17,9... | collective-permute-start | bytes 184328 | tf_op jit(solution)/shard_map/ppermute | solution.py:91
  25.9 1.1 %collective-permute-done.13.refs_4_ = bf16[96,640]{1,0:T(8,128)(2,1)S(1)} collective-permute-done((bf16[96,640]{1,0:T(8,128)(2,1)S(1)}, bf16[96,640]{1,0:T(8,128)(2,1)S(1)}, u32[]{:S(2)}, u32[]{:S(2)}) %collective-permute-start.13) | collective-permute-done | bytes 122912 | tf_op jit(solution)/shard_map/ppermute | solution.py:91
  28.0 2.3 %collective-permute-done.6.refs_7_ = bf16[48,640]{1,0:T(8,128)(2,1)S(1)} collective-permute-done((bf16[48,640]{1,0:T(8,128)(2,1)S(1)}, bf16[48,640]{1,0:T(8,128)(2,1)S(1)}, u32[]{:S(2)}, u32[]{:S(2)}) %collective-permute-start.6) | collective-permute-done | bytes 61472 | tf_op jit(solution)/shard_map/ppermute | solution.py:91
  30.4 1.7 %collective-permute-start.21 = (bf16[96,640]{1,0:T(8,128)(2,1)S(1)}, bf16[96,640]{1,0:T(8,128)(2,1)S(1)}, u32[]{:S(2)}, u32[]{:S(2)}) collective-permute-start(bf16[96,640]{1,0:T(8,128)(2,1)S(1)} %collective-permute-done.16.refs_10_), channel_id=1, source_target_pairs={{0,8},{1,5},{2,10},{3,7},{8,16},{9,1},{10,18},{11,3},{16,24},{17,9... | collective-permute-start | bytes 368648 | tf_op jit(solution)/shard_map/ppermute | solution.py:91
  33.1 4.6 %shard_map.39 = (f32[5,8,96,128]{3,2,1,0:T(8,128)S(1)}, f32[5,8,96,128]{3,2,1,0:T(8,128)S(1)}, f32[5,8,96,128]{3,2,1,0:T(8,128)S(1)}) custom-call(s32[5]{0:T(128)S(1)} %stack.23.at_ref, bf16[8,96,640]{2,1,0:T(8,128)(2,1)S(1)} %shard_map.37.rows_ref, bf16[96,640]{1,0:T(8,128)(2,1)S(1)} %get-tuple-element.10.refs_0_, ...), custom_call_target="tpu_custom_call" | custom-call | flops 1321205760 | tf_op jit(solution)/shard_map/pallas_call | solution.py:254
  37.7 2.0 %shard_map.40 = bf16[384,640]{1,0:T(8,128)(2,1)S(1)} custom-call(s32[5]{0:T(128)S(1)} %stack.23.at_ref, bf16[8,96,640]{2,1,0:T(8,128)(2,1)S(1)} %shard_map.37.rows_ref, f32[5,8,96,128]{3,2,1,0:T(8,128)S(1)} %get-tuple-element.12.mixed_ref, f32[5,8,96,128]{3,2,1,0:T(8,128)S(1)} %get-tuple-element.13.sum_ref, f32[5,8,96,128]{3,2,1,0:T(8,128)S(1)} %get-tuple-element.14.top_ref, ...), custom_call_target="tpu_custom_call" | custom-call | flops 314572800 | tf_op jit(solution)/shard_map/pallas_call | solution.py:254
  39.8 1.4 %shard_map.41 = f32[192,640]{1,0:T(8,128)S(1)} custom-call(s32[5]{0:T(128)S(1)} %stack.23.at_ref, bf16[8,96,640]{2,1,0:T(8,128)(2,1)S(1)} %shard_map.37.rows_ref, f32[5,8,96,128]{3,2,1,0:T(8,128)S(1)} %get-tuple-element.12.mixed_ref, f32[5,8,96,128]{3,2,1,0:T(8,128)S(1)} %get-tuple-element.13.sum_ref, f32[5,8,96,128]{3,2,1,0:T(8,128)S(1)} %get-tuple-element.14.top_ref, ...), custom_call_target="tpu_custom_call" | custom-call | flops 314572800 | tf_op jit(solution)/shard_map/pallas_call | solution.py:254
  41.6 1.6 %collective-permute-start.25 = (bf16[96,640]{1,0:T(8,128)(2,1)S(1)}, bf16[96,640]{1,0:T(8,128)(2,1)S(1)}, u32[]{:S(2)}, u32[]{:S(2)}) collective-permute-start(bf16[96,640]{1,0:T(8,128)(2,1)S(1)} %get-tuple-element.15.refs_1_), channel_id=1, source_target_pairs={{0,2},{1,3},{2,0},{3,1},{4,6},{5,7},{6,4},{7,5},{8,10},{9,11},{10,... | collective-permute-start | bytes 368648 | tf_op jit(solution)/shard_map/ppermute | solution.py:304
  43.7 1.4 %shard_map.42.kept_ref = f32[192,640]{1,0:T(8,128)S(1)} custom-call(s32[5]{0:T(128)S(1)} %stack.23.at_ref, bf16[8,96,640]{2,1,0:T(8,128)(2,1)S(1)} %shard_map.37.rows_ref, f32[5,8,96,128]{3,2,1,0:T(8,128)S(1)} %get-tuple-element.12.mixed_ref, f32[5,8,96,128]{3,2,1,0:T(8,128)S(1)} %get-tuple-element.13.sum_ref, ...), custom_call_target="tpu_custom_call" | custom-call | flops 314572800 | tf_op jit(solution)/shard_map/pallas_call | solution.py:254
  45.1 2.8 %collective-permute-done.25.from_x_ref = bf16[96,640]{1,0:T(8,128)(2,1)S(1)} collective-permute-done((bf16[96,640]{1,0:T(8,128)(2,1)S(1)}, bf16[96,640]{1,0:T(8,128)(2,1)S(1)}, u32[]{:S(2)}, u32[]{:S(2)}) %collective-permute-start.25) | collective-permute-done | bytes 122912 | tf_op jit(solution)/shard_map/ppermute | solution.py:304
  47.9 1.4 %collective-permute-start.26 = (bf16[96,640]{1,0:T(8,128)(2,1)S(1)}, bf16[96,640]{1,0:T(8,128)(2,1)S(1)}, u32[]{:S(2)}, u32[]{:S(2)}) collective-permute-start(bf16[96,640]{1,0:T(8,128)(2,1)S(1)} %shard_map.44), channel_id=1, source_target_pairs={{0,8},{1,12},{2,0},{3,4},{4,24},{5,28},{6,16},{7,20},{8,25},{9,29}... | collective-permute-start | bytes 368648 | tf_op jit(solution)/shard_map/ppermute | solution.py:316
  49.3 3.1 %collective-permute-done.23.from_x_ref = bf16[96,640]{1,0:T(8,128)(2,1)S(1)} collective-permute-done((bf16[96,640]{1,0:T(8,128)(2,1)S(1)}, bf16[96,640]{1,0:T(8,128)(2,1)S(1)}, u32[]{:S(2)}, u32[]{:S(2)}) %collective-permute-start.23) | collective-permute-done | bytes 122912 | tf_op jit(solution)/shard_map/ppermute | solution.py:304
  52.5 3.2 %collective-permute-done.26 = bf16[96,640]{1,0:T(8,128)(2,1)S(1)} collective-permute-done((bf16[96,640]{1,0:T(8,128)(2,1)S(1)}, bf16[96,640]{1,0:T(8,128)(2,1)S(1)}, u32[]{:S(2)}, u32[]{:S(2)}) %collective-permute-start.26) | collective-permute-done | bytes 122912 | tf_op jit(solution)/shard_map/ppermute | solution.py:316
  55.7 3.5 %collective-permute-done.24 = bf16[96,640]{1,0:T(8,128)(2,1)S(1)} collective-permute-done((bf16[96,640]{1,0:T(8,128)(2,1)S(1)}, bf16[96,640]{1,0:T(8,128)(2,1)S(1)}, u32[]{:S(2)}, u32[]{:S(2)}) %collective-permute-start.24) | collective-permute-done | bytes 122912 | tf_op jit(solution)/shard_map/ppermute | solution.py:316
  (50 shorter events, 13.5 us)
Async XLA Ops:
  0.0 6.7 %collective-permute-start = (bf16[96,640]{1,0:T(8,128)(2,1)}, bf16[96,640]{1,0:T(8,128)(2,1)S(1)}, u32[]{:S(2)}, u32[]{:S(2)}) collective-permute-start(bf16[96,640]{1,0:T(8,128)(2,1)} %refs_0_.1), channel_id=1, source_target_pairs={{0,8},{1,5},{2,10},{3,7},{8,16},{9,1},{10,18},{11,3},{16,24},{17,9... | collective-permute-start | bytes 368648 | tf_op jit(solution)/shard_map/ppermute | solution.py:91
  3.0 6.8 %collective-permute-start.11 = (bf16[96,640]{1,0:T(8,128)(2,1)S(1)}, bf16[96,640]{1,0:T(8,128)(2,1)S(1)}, u32[]{:S(2)}, u32[]{:S(2)}) collective-permute-start(bf16[96,640]{1,0:T(8,128)(2,1)S(1)} %get-tuple-element.10.refs_0_), channel_id=1, source_target_pairs={{0,4},{1,9},{2,6},{3,11},{8,0},{9,17},{10,2},{11,19},{16,8},{17,25... | collective-permute-start | bytes 368648 | tf_op jit(solution)/shard_map/ppermute | solution.py:91
  3.5 6.7 %collective-permute-start.14 = (bf16[96,640]{1,0:T(8,128)(2,1)S(1)}, bf16[96,640]{1,0:T(8,128)(2,1)S(1)}, u32[]{:S(2)}, u32[]{:S(2)}) collective-permute-start(bf16[96,640]{1,0:T(8,128)(2,1)S(1)} %get-tuple-element.11.refs_7_), channel_id=1, source_target_pairs={{0,8},{1,5},{2,10},{3,7},{8,16},{9,1},{10,18},{11,3},{16,24},{17,9... | collective-permute-start | bytes 368648 | tf_op jit(solution)/shard_map/ppermute | solution.py:91
  5.1 6.8 %collective-permute-start.8 = (bf16[96,640]{1,0:T(8,128)(2,1)S(1)}, bf16[96,640]{1,0:T(8,128)(2,1)S(1)}, u32[]{:S(2)}, u32[]{:S(2)}) collective-permute-start(bf16[96,640]{1,0:T(8,128)(2,1)S(1)} %get-tuple-element.10.refs_0_), channel_id=1, source_target_pairs={{0,8},{1,5},{2,10},{3,7},{8,16},{9,1},{10,18},{11,3},{16,24},{17,9... | collective-permute-start | bytes 368648 | tf_op jit(solution)/shard_map/ppermute | solution.py:91
  6.7 6.8 %collective-permute-start.17 = (bf16[96,640]{1,0:T(8,128)(2,1)S(1)}, bf16[96,640]{1,0:T(8,128)(2,1)S(1)}, u32[]{:S(2)}, u32[]{:S(2)}) collective-permute-start(bf16[96,640]{1,0:T(8,128)(2,1)S(1)} %get-tuple-element.11.refs_7_), channel_id=1, source_target_pairs={{0,4},{1,9},{2,6},{3,11},{8,0},{9,17},{10,2},{11,19},{16,8},{17,25... | collective-permute-start | bytes 368648 | tf_op jit(solution)/shard_map/ppermute | solution.py:91
  7.1 7.9 %collective-permute-start.1 = (bf16[96,640]{1,0:T(8,128)(2,1)S(1)}, bf16[96,640]{1,0:T(8,128)(2,1)S(1)}, u32[]{:S(2)}, u32[]{:S(2)}) collective-permute-start(bf16[96,640]{1,0:T(8,128)(2,1)S(1)} %collective-permute-done.refs_1_), channel_id=1, source_target_pairs={{0,8},{1,5},{2,10},{3,7},{8,16},{9,1},{10,18},{11,3},{16,24},{17,9... | collective-permute-start | bytes 368648 | tf_op jit(solution)/shard_map/ppermute | solution.py:91
  9.8 5.9 %collective-permute-start.4 = (bf16[96,640]{1,0:T(8,128)(2,1)S(1)}, bf16[96,640]{1,0:T(8,128)(2,1)S(1)}, u32[]{:S(2)}, u32[]{:S(2)}) collective-permute-start(bf16[96,640]{1,0:T(8,128)(2,1)S(1)} %collective-permute-done.3.refs_6_), channel_id=1, source_target_pairs={{0,4},{1,9},{2,6},{3,11},{8,0},{9,17},{10,2},{11,19},{16,8},{17,25... | collective-permute-start | bytes 368648 | tf_op jit(solution)/shard_map/ppermute | solution.py:91
  10.2 8.1 %collective-permute-start.12 = (bf16[96,640]{1,0:T(8,128)(2,1)S(1)}, bf16[96,640]{1,0:T(8,128)(2,1)S(1)}, u32[]{:S(2)}, u32[]{:S(2)}) collective-permute-start(bf16[96,640]{1,0:T(8,128)(2,1)S(1)} %collective-permute-done.11.refs_6_), channel_id=1, source_target_pairs={{0,4},{1,9},{2,6},{3,11},{8,0},{9,17},{10,2},{11,19},{16,8},{17,25... | collective-permute-start | bytes 368648 | tf_op jit(solution)/shard_map/ppermute | solution.py:91
  11.9 6.8 %collective-permute-start.15 = (bf16[96,640]{1,0:T(8,128)(2,1)S(1)}, bf16[96,640]{1,0:T(8,128)(2,1)S(1)}, u32[]{:S(2)}, u32[]{:S(2)}) collective-permute-start(bf16[96,640]{1,0:T(8,128)(2,1)S(1)} %collective-permute-done.14.refs_8_), channel_id=1, source_target_pairs={{0,8},{1,5},{2,10},{3,7},{8,16},{9,1},{10,18},{11,3},{16,24},{17,9... | collective-permute-start | bytes 368648 | tf_op jit(solution)/shard_map/ppermute | solution.py:91
  13.5 6.8 %collective-permute-start.9 = (bf16[96,640]{1,0:T(8,128)(2,1)S(1)}, bf16[96,640]{1,0:T(8,128)(2,1)S(1)}, u32[]{:S(2)}, u32[]{:S(2)}) collective-permute-start(bf16[96,640]{1,0:T(8,128)(2,1)S(1)} %collective-permute-done.8.refs_1_), channel_id=1, source_target_pairs={{0,8},{1,5},{2,10},{3,7},{8,16},{9,1},{10,18},{11,3},{16,24},{17,9... | collective-permute-start | bytes 368648 | tf_op jit(solution)/shard_map/ppermute | solution.py:91
  15.0 6.9 %collective-permute-start.18 = (bf16[96,640]{1,0:T(8,128)(2,1)S(1)}, bf16[96,640]{1,0:T(8,128)(2,1)S(1)}, u32[]{:S(2)}, u32[]{:S(2)}) collective-permute-start(bf16[96,640]{1,0:T(8,128)(2,1)S(1)} %collective-permute-done.17.refs_13_), channel_id=1, source_target_pairs={{0,4},{1,9},{2,6},{3,11},{8,0},{9,17},{10,2},{11,19},{16,8},{17,25... | collective-permute-start | bytes 368648 | tf_op jit(solution)/shard_map/ppermute | solution.py:91
  15.6 7.3 %collective-permute-start.2 = (bf16[96,640]{1,0:T(8,128)(2,1)S(1)}, bf16[96,640]{1,0:T(8,128)(2,1)S(1)}, u32[]{:S(2)}, u32[]{:S(2)}) collective-permute-start(bf16[96,640]{1,0:T(8,128)(2,1)S(1)} %collective-permute-done.1.refs_2_), channel_id=1, source_target_pairs={{0,8},{1,5},{2,10},{3,7},{8,16},{9,1},{10,18},{11,3},{16,24},{17,9... | collective-permute-start | bytes 368648 | tf_op jit(solution)/shard_map/ppermute | solution.py:91
  18.3 6.1 %collective-permute-start.5 = (bf16[96,640]{1,0:T(8,128)(2,1)S(1)}, bf16[96,640]{1,0:T(8,128)(2,1)S(1)}, u32[]{:S(2)}, u32[]{:S(2)}) collective-permute-start(bf16[96,640]{1,0:T(8,128)(2,1)S(1)} %collective-permute-done.4.refs_5_), channel_id=1, source_target_pairs={{0,4},{1,9},{2,6},{3,11},{8,0},{9,17},{10,2},{11,19},{16,8},{17,25... | collective-permute-start | bytes 368648 | tf_op jit(solution)/shard_map/ppermute | solution.py:91
  18.7 8.3 %collective-permute-start.13 = (bf16[96,640]{1,0:T(8,128)(2,1)S(1)}, bf16[96,640]{1,0:T(8,128)(2,1)S(1)}, u32[]{:S(2)}, u32[]{:S(2)}) collective-permute-start(bf16[96,640]{1,0:T(8,128)(2,1)S(1)} %collective-permute-done.12.refs_5_), channel_id=1, source_target_pairs={{0,4},{1,9},{2,6},{3,11},{8,0},{9,17},{10,2},{11,19},{16,8},{17,25... | collective-permute-start | bytes 368648 | tf_op jit(solution)/shard_map/ppermute | solution.py:91
  20.3 7.3 %collective-permute-start.16 = (bf16[96,640]{1,0:T(8,128)(2,1)S(1)}, bf16[96,640]{1,0:T(8,128)(2,1)S(1)}, u32[]{:S(2)}, u32[]{:S(2)}) collective-permute-start(bf16[96,640]{1,0:T(8,128)(2,1)S(1)} %collective-permute-done.15.refs_9_), channel_id=1, source_target_pairs={{0,8},{1,5},{2,10},{3,7},{8,16},{9,1},{10,18},{11,3},{16,24},{17,9... | collective-permute-start | bytes 368648 | tf_op jit(solution)/shard_map/ppermute | solution.py:91
  21.9 11.1 %collective-permute-start.10 = (bf16[96,640]{1,0:T(8,128)(2,1)S(1)}, bf16[96,640]{1,0:T(8,128)(2,1)S(1)}, u32[]{:S(2)}, u32[]{:S(2)}) collective-permute-start(bf16[96,640]{1,0:T(8,128)(2,1)S(1)} %collective-permute-done.9.refs_2_), channel_id=1, source_target_pairs={{0,8},{1,5},{2,10},{3,7},{8,16},{9,1},{10,18},{11,3},{16,24},{17,9... | collective-permute-start | bytes 368648 | tf_op jit(solution)/shard_map/ppermute | solution.py:91
  22.9 10.1 %collective-permute-start.19 = (bf16[96,640]{1,0:T(8,128)(2,1)S(1)}, bf16[96,640]{1,0:T(8,128)(2,1)S(1)}, u32[]{:S(2)}, u32[]{:S(2)}) collective-permute-start(bf16[96,640]{1,0:T(8,128)(2,1)S(1)} %collective-permute-done.18.refs_12_), channel_id=1, source_target_pairs={{0,4},{1,9},{2,6},{3,11},{8,0},{9,17},{10,2},{11,19},{16,8},{17,25... | collective-permute-start | bytes 368648 | tf_op jit(solution)/shard_map/ppermute | solution.py:91
  24.4 6.0 %collective-permute-start.6 = (bf16[48,640]{1,0:T(8,128)(2,1)S(1)}, bf16[48,640]{1,0:T(8,128)(2,1)S(1)}, u32[]{:S(2)}, u32[]{:S(2)}) collective-permute-start(bf16[48,640]{1,0:T(8,128)(2,1)S(1)} %slice.24), channel_id=1, source_target_pairs={{0,8},{1,5},{2,10},{3,7},{8,16},{9,1},{10,18},{11,3},{16,24},{17,9... | collective-permute-start | bytes 184328 | tf_op jit(solution)/shard_map/ppermute | solution.py:91
  27.6 10.1 %collective-permute-start.20 = (bf16[96,640]{1,0:T(8,128)(2,1)S(1)}, bf16[96,640]{1,0:T(8,128)(2,1)S(1)}, u32[]{:S(2)}, u32[]{:S(2)}) collective-permute-start(bf16[96,640]{1,0:T(8,128)(2,1)S(1)} %collective-permute-done.13.refs_4_), channel_id=1, source_target_pairs={{0,4},{1,9},{2,6},{3,11},{8,0},{9,17},{10,2},{11,19},{16,8},{17,25... | collective-permute-start | bytes 368648 | tf_op jit(solution)/shard_map/ppermute | solution.py:91
  30.4 7.3 %collective-permute-start.21 = (bf16[96,640]{1,0:T(8,128)(2,1)S(1)}, bf16[96,640]{1,0:T(8,128)(2,1)S(1)}, u32[]{:S(2)}, u32[]{:S(2)}) collective-permute-start(bf16[96,640]{1,0:T(8,128)(2,1)S(1)} %collective-permute-done.16.refs_10_), channel_id=1, source_target_pairs={{0,8},{1,5},{2,10},{3,7},{8,16},{9,1},{10,18},{11,3},{16,24},{17,9... | collective-permute-start | bytes 368648 | tf_op jit(solution)/shard_map/ppermute | solution.py:91
  41.6 6.2 %collective-permute-start.25 = (bf16[96,640]{1,0:T(8,128)(2,1)S(1)}, bf16[96,640]{1,0:T(8,128)(2,1)S(1)}, u32[]{:S(2)}, u32[]{:S(2)}) collective-permute-start(bf16[96,640]{1,0:T(8,128)(2,1)S(1)} %get-tuple-element.15.refs_1_), channel_id=1, source_target_pairs={{0,2},{1,3},{2,0},{3,1},{4,6},{5,7},{6,4},{7,5},{8,10},{9,11},{10,... | collective-permute-start | bytes 368648 | tf_op jit(solution)/shard_map/ppermute | solution.py:304
  43.2 9.1 %collective-permute-start.23 = (bf16[96,640]{1,0:T(8,128)(2,1)S(1)}, bf16[96,640]{1,0:T(8,128)(2,1)S(1)}, u32[]{:S(2)}, u32[]{:S(2)}) collective-permute-start(bf16[96,640]{1,0:T(8,128)(2,1)S(1)} %get-tuple-element.16.refs_0_), channel_id=1, source_target_pairs={{0,2},{1,3},{2,0},{3,1},{4,6},{5,7},{6,4},{7,5},{8,10},{9,11},{10,... | collective-permute-start | bytes 368648 | tf_op jit(solution)/shard_map/ppermute | solution.py:304
  47.9 7.7 %collective-permute-start.26 = (bf16[96,640]{1,0:T(8,128)(2,1)S(1)}, bf16[96,640]{1,0:T(8,128)(2,1)S(1)}, u32[]{:S(2)}, u32[]{:S(2)}) collective-permute-start(bf16[96,640]{1,0:T(8,128)(2,1)S(1)} %shard_map.44), channel_id=1, source_target_pairs={{0,8},{1,12},{2,0},{3,4},{4,24},{5,28},{6,16},{7,20},{8,25},{9,29}... | collective-permute-start | bytes 368648 | tf_op jit(solution)/shard_map/ppermute | solution.py:316
  52.4 6.7 %collective-permute-start.24 = (bf16[96,640]{1,0:T(8,128)(2,1)S(1)}, bf16[96,640]{1,0:T(8,128)(2,1)S(1)}, u32[]{:S(2)}, u32[]{:S(2)}) collective-permute-start(bf16[96,640]{1,0:T(8,128)(2,1)S(1)} %shard_map.43), channel_id=1, source_target_pairs={{0,24},{1,28},{2,16},{3,20},{4,8},{5,12},{6,0},{7,4},{8,1},{9,5},{... | collective-permute-start | bytes 368648 | tf_op jit(solution)/shard_map/ppermute | solution.py:316
  (6 other events, 19.0 us)

commit v23 on v18

--- a/solution.py
+++ b/solution.py
@@ -97,7 +97,11 @@
         for j, blocks in enumerate(found):
             for by in (1, -1):
                 if step < n // 2 or (j % 2 == 0) == (by == 1):
-                    blocks[by * step % n] = hop(blocks[by * (step - 1) % n], n, by)
+                    block = blocks[by * (step - 1) % n]
+                    if step == n // 2 and j > 0:
+                        other = blocks[-by * (step - 1) % n]
+                        (block,) = call(copy_kernel, (), [block], [(block.shape, block.dtype)], 0, (other,))
+                    blocks[by * step % n] = hop(block, n, by)
     return found
 
 
@@ -179,6 +183,10 @@
         later = scores(columns[head + 1]) if head + 1 < heads else None
         yield head, cols, now
         now = later
+
+
+def copy_kernel(from_ref, *refs):
+    refs[-1][...] = from_ref[...]
 
 
 def split_kernel(kv_ref, keys_ref, values_ref):

time: 57 us -> 57.9 us (1.016)
  the two profiles are of different devices: /device:TPU:3 before, /device:TPU:17 now
where the time goes in v23:
time: 57.9 us; the launch traced here: 57.7 us
  starting transfers between devices  25.3 us (44%)
  waiting for transfers between devices  20.2 us (35%)
  Pallas kernels  9.44 us (16%)
  local copies, waits for them, and re-layouts  1.94 us (3%)
  other arithmetic  0.79 us (1%)
    ppermute x21, starting transfers between devices, hop(): return lax.ppermute(x, ('frames', 'heads'), pairs)  14.8 us
    ppermute x21, waiting for transfers between devices, hop(): return lax.ppermute(x, ('frames', 'heads'), pairs)  11.9 us
    pallas_call x10, Pallas kernels, call(): pl.pallas_call(kernel, out_shape=[jax.ShapeDtypeStruct(shape, dtype) for...  9.44 us
    ppermute x2, waiting for transfers between devices, on_device_ring(): arrived.append(lax.ppermute(total, ('frames', 'heads'), pairs))  6.42 us
    ppermute x2, starting transfers between devices, on_device_ring(): arrived.append(lax.ppermute(total, ('frames', 'heads'), pairs))  5.76 us
    ppermute x1, starting transfers between devices, on_device_ring(): from_core = lax.ppermute(given, 'heads', [(h, h ^ 1) for h in range(4)])  3.17 us
    unnamed x6, local copies, waits for them, and re-layouts  1.85 us
    ppermute x2, waiting for transfers between devices, on_device_ring(): lax.ppermute(block, 'heads', [(h, h ^ 2) for h in range(4)])  1.71 us
  transfers between devices with their start and end apart: 26, of which 16 were waited for; matrix products, arithmetic and copies ran while one was open for 0% of the time, Pallas kernels for 13%

profile of v23, /device:TPU:17, one launch (start us, length us, event | category | flops | bytes accessed | tf_op | source)
XLA Modules:
  0.0 57.7 jit_solution(18314418961904307166)
XLA Ops:
  0.2 1.3 %collective-permute-start.4 = (bf16[96,640]{1,0:T(8,128)(2,1)}, bf16[96,640]{1,0:T(8,128)(2,1)S(1)}, u32[]{:S(2)}, u32[]{:S(2)}) collective-permute-start(bf16[96,640]{1,0:T(8,128)(2,1)} %refs_0_.1), channel_id=1, source_target_pairs={{0,4},{1,9},{2,6},{3,11},{8,0},{9,17},{10,2},{11,19},{16,8},{17,25... | collective-permute-start | bytes 368648 | tf_op jit(solution)/shard_map/ppermute | solution.py:91
  2.4 1.3 %collective-permute-start.10 = (bf16[96,640]{1,0:T(8,128)(2,1)S(1)}, bf16[96,640]{1,0:T(8,128)(2,1)S(1)}, u32[]{:S(2)}, u32[]{:S(2)}) collective-permute-start(bf16[96,640]{1,0:T(8,128)(2,1)S(1)} %get-tuple-element.10.refs_0_), channel_id=1, source_target_pairs={{0,4},{1,9},{2,6},{3,11},{8,0},{9,17},{10,2},{11,19},{16,8},{17,25... | collective-permute-start | bytes 368648 | tf_op jit(solution)/shard_map/ppermute | solution.py:91
  4.2 1.3 %collective-permute-start.16 = (bf16[96,640]{1,0:T(8,128)(2,1)S(1)}, bf16[96,640]{1,0:T(8,128)(2,1)S(1)}, u32[]{:S(2)}, u32[]{:S(2)}) collective-permute-start(bf16[96,640]{1,0:T(8,128)(2,1)S(1)} %get-tuple-element.11.refs_7_), channel_id=1, source_target_pairs={{0,4},{1,9},{2,6},{3,11},{8,0},{9,17},{10,2},{11,19},{16,8},{17,25... | collective-permute-start | bytes 368648 | tf_op jit(solution)/shard_map/ppermute | solution.py:91
  5.7 1.3 %collective-permute-done.10.refs_6_ = bf16[96,640]{1,0:T(8,128)(2,1)S(1)} collective-permute-done((bf16[96,640]{1,0:T(8,128)(2,1)S(1)}, bf16[96,640]{1,0:T(8,128)(2,1)S(1)}, u32[]{:S(2)}, u32[]{:S(2)}) %collective-permute-start.10) | collective-permute-done | bytes 122912 | tf_op jit(solution)/shard_map/ppermute | solution.py:91
  7.0 1.3 %collective-permute-start.5 = (bf16[96,640]{1,0:T(8,128)(2,1)S(1)}, bf16[96,640]{1,0:T(8,128)(2,1)S(1)}, u32[]{:S(2)}, u32[]{:S(2)}) collective-permute-start(bf16[96,640]{1,0:T(8,128)(2,1)S(1)} %collective-permute-done.4.refs_7_), channel_id=1, source_target_pairs={{0,4},{1,9},{2,6},{3,11},{8,0},{9,17},{10,2},{11,19},{16,8},{17,25... | collective-permute-start | bytes 368648 | tf_op jit(solution)/shard_map/ppermute | solution.py:91
  9.1 1.2 %collective-permute-start.11 = (bf16[96,640]{1,0:T(8,128)(2,1)S(1)}, bf16[96,640]{1,0:T(8,128)(2,1)S(1)}, u32[]{:S(2)}, u32[]{:S(2)}) collective-permute-start(bf16[96,640]{1,0:T(8,128)(2,1)S(1)} %collective-permute-done.10.refs_6_), channel_id=1, source_target_pairs={{0,4},{1,9},{2,6},{3,11},{8,0},{9,17},{10,2},{11,19},{16,8},{17,25... | collective-permute-start | bytes 368648 | tf_op jit(solution)/shard_map/ppermute | solution.py:91
  11.6 2.0 %collective-permute-done.1.refs_2_ = bf16[96,640]{1,0:T(8,128)(2,1)S(1)} collective-permute-done((bf16[96,640]{1,0:T(8,128)(2,1)S(1)}, bf16[96,640]{1,0:T(8,128)(2,1)S(1)}, u32[]{:S(2)}, u32[]{:S(2)}) %collective-permute-start.1) | collective-permute-done | bytes 122912 | tf_op jit(solution)/shard_map/ppermute | solution.py:91
  15.0 1.2 %collective-permute-start.12 = (bf16[96,640]{1,0:T(8,128)(2,1)S(1)}, bf16[96,640]{1,0:T(8,128)(2,1)S(1)}, u32[]{:S(2)}, u32[]{:S(2)}) collective-permute-start(bf16[96,640]{1,0:T(8,128)(2,1)S(1)} %collective-permute-done.11.refs_5_), channel_id=1, source_target_pairs={{0,4},{1,9},{2,6},{3,11},{8,0},{9,17},{10,2},{11,19},{16,8},{17,25... | collective-permute-start | bytes 368648 | tf_op jit(solution)/shard_map/ppermute | solution.py:91
  16.7 2.1 %collective-permute-done.14.refs_9_ = bf16[96,640]{1,0:T(8,128)(2,1)S(1)} collective-permute-done((bf16[96,640]{1,0:T(8,128)(2,1)S(1)}, bf16[96,640]{1,0:T(8,128)(2,1)S(1)}, u32[]{:S(2)}, u32[]{:S(2)}) %collective-permute-start.14) | collective-permute-done | bytes 122912 | tf_op jit(solution)/shard_map/ppermute | solution.py:91
  19.1 1.3 %collective-permute-start.18 = (bf16[96,640]{1,0:T(8,128)(2,1)S(1)}, bf16[96,640]{1,0:T(8,128)(2,1)S(1)}, u32[]{:S(2)}, u32[]{:S(2)}) collective-permute-start(bf16[96,640]{1,0:T(8,128)(2,1)S(1)} %collective-permute-done.17.refs_12_), channel_id=1, source_target_pairs={{0,4},{1,9},{2,6},{3,11},{8,0},{9,17},{10,2},{11,19},{16,8},{17,25... | collective-permute-start | bytes 368648 | tf_op jit(solution)/shard_map/ppermute | solution.py:91
  21.4 1.3 %collective-permute-start.6 = (bf16[96,640]{1,0:T(8,128)(2,1)S(1)}, bf16[96,640]{1,0:T(8,128)(2,1)S(1)}, u32[]{:S(2)}, u32[]{:S(2)}) collective-permute-start(bf16[96,640]{1,0:T(8,128)(2,1)S(1)} %collective-permute-done.5.refs_6_), channel_id=1, source_target_pairs={{0,4},{1,9},{2,6},{3,11},{8,0},{9,17},{10,2},{11,19},{16,8},{17,25... | collective-permute-start | bytes 368648 | tf_op jit(solution)/shard_map/ppermute | solution.py:91
  23.5 1.3 %collective-permute-start.19 = (bf16[96,640]{1,0:T(8,128)(2,1)S(1)}, bf16[96,640]{1,0:T(8,128)(2,1)S(1)}, u32[]{:S(2)}, u32[]{:S(2)}) collective-permute-start(bf16[96,640]{1,0:T(8,128)(2,1)S(1)} %shard_map.40), channel_id=1, source_target_pairs={{0,4},{1,9},{2,6},{3,11},{8,0},{9,17},{10,2},{11,19},{16,8},{17,25... | collective-permute-start | bytes 368648 | tf_op jit(solution)/shard_map/ppermute | solution.py:91
  25.7 1.4 %collective-permute-done.6.refs_5_ = bf16[96,640]{1,0:T(8,128)(2,1)S(1)} collective-permute-done((bf16[96,640]{1,0:T(8,128)(2,1)S(1)}, bf16[96,640]{1,0:T(8,128)(2,1)S(1)}, u32[]{:S(2)}, u32[]{:S(2)}) %collective-permute-start.6) | collective-permute-done | bytes 122912 | tf_op jit(solution)/shard_map/ppermute | solution.py:91
  28.8 4.6 %shard_map.39 = (f32[5,8,96,128]{3,2,1,0:T(8,128)S(1)}, f32[5,8,96,128]{3,2,1,0:T(8,128)S(1)}, f32[5,8,96,128]{3,2,1,0:T(8,128)S(1)}) custom-call(s32[5]{0:T(128)S(1)} %stack.23.at_ref, bf16[8,96,640]{2,1,0:T(8,128)(2,1)S(1)} %shard_map.37.rows_ref, bf16[96,640]{1,0:T(8,128)(2,1)S(1)} %get-tuple-element.10.refs_0_, ...), custom_call_target="tpu_custom_call" | custom-call | flops 1321205760 | tf_op jit(solution)/shard_map/pallas_call | solution.py:251
  33.4 2.0 %shard_map.42 = bf16[384,640]{1,0:T(8,128)(2,1)S(1)} custom-call(s32[5]{0:T(128)S(1)} %stack.23.at_ref, bf16[8,96,640]{2,1,0:T(8,128)(2,1)S(1)} %shard_map.37.rows_ref, f32[5,8,96,128]{3,2,1,0:T(8,128)S(1)} %get-tuple-element.12.mixed_ref, f32[5,8,96,128]{3,2,1,0:T(8,128)S(1)} %get-tuple-element.13.sum_ref, f32[5,8,96,128]{3,2,1,0:T(8,128)S(1)} %get-tuple-element.14.top_ref, ...), custom_call_target="tpu_custom_call" | custom-call | flops 314572800 | tf_op jit(solution)/shard_map/pallas_call | solution.py:251
  35.4 3.2 %collective-permute-start.21 = (bf16[2,192,640]{2,1,0:T(8,128)(2,1)S(1)}, bf16[2,192,640]{2,1,0:T(8,128)(2,1)S(1)}, u32[]{:S(2)}, u32[]{:S(2)}) collective-permute-start(bf16[2,192,640]{2,1,0:T(8,128)(2,1)S(1)} %bitcast.16), channel_id=1, source_target_pairs={{0,1},{1,0},{2,3},{3,2},{4,5},{5,4},{6,7},{7,6},{8,9},{9,8},{10,11... | collective-permute-start | bytes 1474568 | tf_op jit(solution)/shard_map/ppermute | solution.py:296
  38.6 1.4 %shard_map.43 = f32[192,640]{1,0:T(8,128)S(1)} custom-call(s32[5]{0:T(128)S(1)} %stack.23.at_ref, bf16[8,96,640]{2,1,0:T(8,128)(2,1)S(1)} %shard_map.37.rows_ref, f32[5,8,96,128]{3,2,1,0:T(8,128)S(1)} %get-tuple-element.12.mixed_ref, f32[5,8,96,128]{3,2,1,0:T(8,128)S(1)} %get-tuple-element.13.sum_ref, f32[5,8,96,128]{3,2,1,0:T(8,128)S(1)} %get-tuple-element.14.top_ref, ...), custom_call_target="tpu_custom_call" | custom-call | flops 314572800 | tf_op jit(solution)/shard_map/pallas_call | solution.py:251
  40.1 1.3 %collective-permute-start.24 = (bf16[96,640]{1,0:T(8,128)(2,1)S(1)}, bf16[96,640]{1,0:T(8,128)(2,1)S(1)}, u32[]{:S(2)}, u32[]{:S(2)}) collective-permute-start(bf16[96,640]{1,0:T(8,128)(2,1)S(1)} %get-tuple-element.15.refs_1_), channel_id=1, source_target_pairs={{0,2},{1,3},{2,0},{3,1},{4,6},{5,7},{6,4},{7,5},{8,10},{9,11},{10,... | collective-permute-start | bytes 368648 | tf_op jit(solution)/shard_map/ppermute | solution.py:300
  41.6 1.4 %shard_map.44.kept_ref = f32[192,640]{1,0:T(8,128)S(1)} custom-call(s32[5]{0:T(128)S(1)} %stack.23.at_ref, bf16[8,96,640]{2,1,0:T(8,128)(2,1)S(1)} %shard_map.37.rows_ref, f32[5,8,96,128]{3,2,1,0:T(8,128)S(1)} %get-tuple-element.12.mixed_ref, f32[5,8,96,128]{3,2,1,0:T(8,128)S(1)} %get-tuple-element.13.sum_ref, ...), custom_call_target="tpu_custom_call" | custom-call | flops 314572800 | tf_op jit(solution)/shard_map/pallas_call | solution.py:251
  43.0 1.7 %collective-permute-done.24.from_x_ref = bf16[96,640]{1,0:T(8,128)(2,1)S(1)} collective-permute-done((bf16[96,640]{1,0:T(8,128)(2,1)S(1)}, bf16[96,640]{1,0:T(8,128)(2,1)S(1)}, u32[]{:S(2)}, u32[]{:S(2)}) %collective-permute-start.24) | collective-permute-done | bytes 122912 | tf_op jit(solution)/shard_map/ppermute | solution.py:300
  44.7 3.9 %collective-permute-start.25 = (bf16[96,640]{1,0:T(8,128)(2,1)S(1)}, bf16[96,640]{1,0:T(8,128)(2,1)S(1)}, u32[]{:S(2)}, u32[]{:S(2)}) collective-permute-start(bf16[96,640]{1,0:T(8,128)(2,1)S(1)} %shard_map.46), channel_id=1, source_target_pairs={{0,8},{1,12},{2,0},{3,4},{4,24},{5,28},{6,16},{7,20},{8,25},{9,29}... | collective-permute-start | bytes 368648 | tf_op jit(solution)/shard_map/ppermute | solution.py:312
  48.7 1.9 %collective-permute-start.23 = (bf16[96,640]{1,0:T(8,128)(2,1)S(1)}, bf16[96,640]{1,0:T(8,128)(2,1)S(1)}, u32[]{:S(2)}, u32[]{:S(2)}) collective-permute-start(bf16[96,640]{1,0:T(8,128)(2,1)S(1)} %shard_map.45), channel_id=1, source_target_pairs={{0,24},{1,28},{2,16},{3,20},{4,8},{5,12},{6,0},{7,4},{8,1},{9,5},{... | collective-permute-start | bytes 368648 | tf_op jit(solution)/shard_map/ppermute | solution.py:312
  50.6 3.6 %collective-permute-done.25 = bf16[96,640]{1,0:T(8,128)(2,1)S(1)} collective-permute-done((bf16[96,640]{1,0:T(8,128)(2,1)S(1)}, bf16[96,640]{1,0:T(8,128)(2,1)S(1)}, u32[]{:S(2)}, u32[]{:S(2)}) %collective-permute-start.25) | collective-permute-done | bytes 122912 | tf_op jit(solution)/shard_map/ppermute | solution.py:312
  54.2 2.8 %collective-permute-done.23 = bf16[96,640]{1,0:T(8,128)(2,1)S(1)} collective-permute-done((bf16[96,640]{1,0:T(8,128)(2,1)S(1)}, bf16[96,640]{1,0:T(8,128)(2,1)S(1)}, u32[]{:S(2)}, u32[]{:S(2)}) %collective-permute-start.23) | collective-permute-done | bytes 122912 | tf_op jit(solution)/shard_map/ppermute | solution.py:312
  (48 shorter events, 11.6 us)
Async XLA Ops:
  0.2 5.4 %collective-permute-start.4 = (bf16[96,640]{1,0:T(8,128)(2,1)}, bf16[96,640]{1,0:T(8,128)(2,1)S(1)}, u32[]{:S(2)}, u32[]{:S(2)}) collective-permute-start(bf16[96,640]{1,0:T(8,128)(2,1)} %refs_0_.1), channel_id=1, source_target_pairs={{0,4},{1,9},{2,6},{3,11},{8,0},{9,17},{10,2},{11,19},{16,8},{17,25... | collective-permute-start | bytes 368648 | tf_op jit(solution)/shard_map/ppermute | solution.py:91
  2.4 4.6 %collective-permute-start.10 = (bf16[96,640]{1,0:T(8,128)(2,1)S(1)}, bf16[96,640]{1,0:T(8,128)(2,1)S(1)}, u32[]{:S(2)}, u32[]{:S(2)}) collective-permute-start(bf16[96,640]{1,0:T(8,128)(2,1)S(1)} %get-tuple-element.10.refs_0_), channel_id=1, source_target_pairs={{0,4},{1,9},{2,6},{3,11},{8,0},{9,17},{10,2},{11,19},{16,8},{17,25... | collective-permute-start | bytes 368648 | tf_op jit(solution)/shard_map/ppermute | solution.py:91
  3.8 5.3 %collective-permute-start.13 = (bf16[96,640]{1,0:T(8,128)(2,1)S(1)}, bf16[96,640]{1,0:T(8,128)(2,1)S(1)}, u32[]{:S(2)}, u32[]{:S(2)}) collective-permute-start(bf16[96,640]{1,0:T(8,128)(2,1)S(1)} %get-tuple-element.11.refs_7_), channel_id=1, source_target_pairs={{0,8},{1,5},{2,10},{3,7},{8,16},{9,1},{10,18},{11,3},{16,24},{17,9... | collective-permute-start | bytes 368648 | tf_op jit(solution)/shard_map/ppermute | solution.py:91
  4.0 7.3 %collective-permute-start.7 = (bf16[96,640]{1,0:T(8,128)(2,1)S(1)}, bf16[96,640]{1,0:T(8,128)(2,1)S(1)}, u32[]{:S(2)}, u32[]{:S(2)}) collective-permute-start(bf16[96,640]{1,0:T(8,128)(2,1)S(1)} %get-tuple-element.10.refs_0_), channel_id=1, source_target_pairs={{0,8},{1,5},{2,10},{3,7},{8,16},{9,1},{10,18},{11,3},{16,24},{17,9... | collective-permute-start | bytes 368648 | tf_op jit(solution)/shard_map/ppermute | solution.py:91
  4.2 7.2 %collective-permute-start.16 = (bf16[96,640]{1,0:T(8,128)(2,1)S(1)}, bf16[96,640]{1,0:T(8,128)(2,1)S(1)}, u32[]{:S(2)}, u32[]{:S(2)}) collective-permute-start(bf16[96,640]{1,0:T(8,128)(2,1)S(1)} %get-tuple-element.11.refs_7_), channel_id=1, source_target_pairs={{0,4},{1,9},{2,6},{3,11},{8,0},{9,17},{10,2},{11,19},{16,8},{17,25... | collective-permute-start | bytes 368648 | tf_op jit(solution)/shard_map/ppermute | solution.py:91
  5.5 8.0 %collective-permute-start.1 = (bf16[96,640]{1,0:T(8,128)(2,1)S(1)}, bf16[96,640]{1,0:T(8,128)(2,1)S(1)}, u32[]{:S(2)}, u32[]{:S(2)}) collective-permute-start(bf16[96,640]{1,0:T(8,128)(2,1)S(1)} %collective-permute-done.refs_1_), channel_id=1, source_target_pairs={{0,8},{1,5},{2,10},{3,7},{8,16},{9,1},{10,18},{11,3},{16,24},{17,9... | collective-permute-start | bytes 368648 | tf_op jit(solution)/shard_map/ppermute | solution.py:91
  7.0 7.7 %collective-permute-start.5 = (bf16[96,640]{1,0:T(8,128)(2,1)S(1)}, bf16[96,640]{1,0:T(8,128)(2,1)S(1)}, u32[]{:S(2)}, u32[]{:S(2)}) collective-permute-start(bf16[96,640]{1,0:T(8,128)(2,1)S(1)} %collective-permute-done.4.refs_7_), channel_id=1, source_target_pairs={{0,4},{1,9},{2,6},{3,11},{8,0},{9,17},{10,2},{11,19},{16,8},{17,25... | collective-permute-start | bytes 368648 | tf_op jit(solution)/shard_map/ppermute | solution.py:91
  9.1 5.9 %collective-permute-start.11 = (bf16[96,640]{1,0:T(8,128)(2,1)S(1)}, bf16[96,640]{1,0:T(8,128)(2,1)S(1)}, u32[]{:S(2)}, u32[]{:S(2)}) collective-permute-start(bf16[96,640]{1,0:T(8,128)(2,1)S(1)} %collective-permute-done.10.refs_6_), channel_id=1, source_target_pairs={{0,4},{1,9},{2,6},{3,11},{8,0},{9,17},{10,2},{11,19},{16,8},{17,25... | collective-permute-start | bytes 368648 | tf_op jit(solution)/shard_map/ppermute | solution.py:91
  11.2 5.3 %collective-permute-start.8 = (bf16[96,640]{1,0:T(8,128)(2,1)S(1)}, bf16[96,640]{1,0:T(8,128)(2,1)S(1)}, u32[]{:S(2)}, u32[]{:S(2)}) collective-permute-start(bf16[96,640]{1,0:T(8,128)(2,1)S(1)} %collective-permute-done.7.refs_1_), channel_id=1, source_target_pairs={{0,8},{1,5},{2,10},{3,7},{8,16},{9,1},{10,18},{11,3},{16,24},{17,9... | collective-permute-start | bytes 368648 | tf_op jit(solution)/shard_map/ppermute | solution.py:91
  11.4 7.5 %collective-permute-start.14 = (bf16[96,640]{1,0:T(8,128)(2,1)S(1)}, bf16[96,640]{1,0:T(8,128)(2,1)S(1)}, u32[]{:S(2)}, u32[]{:S(2)}) collective-permute-start(bf16[96,640]{1,0:T(8,128)(2,1)S(1)} %collective-permute-done.13.refs_8_), channel_id=1, source_target_pairs={{0,8},{1,5},{2,10},{3,7},{8,16},{9,1},{10,18},{11,3},{16,24},{17,9... | collective-permute-start | bytes 368648 | tf_op jit(solution)/shard_map/ppermute | solution.py:91
  13.5 5.5 %collective-permute-start.17 = (bf16[96,640]{1,0:T(8,128)(2,1)S(1)}, bf16[96,640]{1,0:T(8,128)(2,1)S(1)}, u32[]{:S(2)}, u32[]{:S(2)}) collective-permute-start(bf16[96,640]{1,0:T(8,128)(2,1)S(1)} %collective-permute-done.16.refs_13_), channel_id=1, source_target_pairs={{0,4},{1,9},{2,6},{3,11},{8,0},{9,17},{10,2},{11,19},{16,8},{17,25... | collective-permute-start | bytes 368648 | tf_op jit(solution)/shard_map/ppermute | solution.py:91
  14.8 6.7 %collective-permute-start.2 = (bf16[96,640]{1,0:T(8,128)(2,1)S(1)}, bf16[96,640]{1,0:T(8,128)(2,1)S(1)}, u32[]{:S(2)}, u32[]{:S(2)}) collective-permute-start(bf16[96,640]{1,0:T(8,128)(2,1)S(1)} %collective-permute-done.1.refs_2_), channel_id=1, source_target_pairs={{0,8},{1,5},{2,10},{3,7},{8,16},{9,1},{10,18},{11,3},{16,24},{17,9... | collective-permute-start | bytes 368648 | tf_op jit(solution)/shard_map/ppermute | solution.py:91
  15.0 7.8 %collective-permute-start.12 = (bf16[96,640]{1,0:T(8,128)(2,1)S(1)}, bf16[96,640]{1,0:T(8,128)(2,1)S(1)}, u32[]{:S(2)}, u32[]{:S(2)}) collective-permute-start(bf16[96,640]{1,0:T(8,128)(2,1)S(1)} %collective-permute-done.11.refs_5_), channel_id=1, source_target_pairs={{0,4},{1,9},{2,6},{3,11},{8,0},{9,17},{10,2},{11,19},{16,8},{17,25... | collective-permute-start | bytes 368648 | tf_op jit(solution)/shard_map/ppermute | solution.py:91
  16.6 6.9 %collective-permute-start.9 = (bf16[96,640]{1,0:T(8,128)(2,1)S(1)}, bf16[96,640]{1,0:T(8,128)(2,1)S(1)}, u32[]{:S(2)}, u32[]{:S(2)}) collective-permute-start(bf16[96,640]{1,0:T(8,128)(2,1)S(1)} %collective-permute-done.8.refs_2_), channel_id=1, source_target_pairs={{0,8},{1,5},{2,10},{3,7},{8,16},{9,1},{10,18},{11,3},{16,24},{17,9... | collective-permute-start | bytes 368648 | tf_op jit(solution)/shard_map/ppermute | solution.py:91
  18.9 6.6 %collective-permute-start.15 = (bf16[96,640]{1,0:T(8,128)(2,1)S(1)}, bf16[96,640]{1,0:T(8,128)(2,1)S(1)}, u32[]{:S(2)}, u32[]{:S(2)}) collective-permute-start(bf16[96,640]{1,0:T(8,128)(2,1)S(1)} %collective-permute-done.14.refs_9_), channel_id=1, source_target_pairs={{0,8},{1,5},{2,10},{3,7},{8,16},{9,1},{10,18},{11,3},{16,24},{17,9... | collective-permute-start | bytes 368648 | tf_op jit(solution)/shard_map/ppermute | solution.py:91
  19.1 6.4 %collective-permute-start.18 = (bf16[96,640]{1,0:T(8,128)(2,1)S(1)}, bf16[96,640]{1,0:T(8,128)(2,1)S(1)}, u32[]{:S(2)}, u32[]{:S(2)}) collective-permute-start(bf16[96,640]{1,0:T(8,128)(2,1)S(1)} %collective-permute-done.17.refs_12_), channel_id=1, source_target_pairs={{0,4},{1,9},{2,6},{3,11},{8,0},{9,17},{10,2},{11,19},{16,8},{17,25... | collective-permute-start | bytes 368648 | tf_op jit(solution)/shard_map/ppermute | solution.py:91
  21.4 5.6 %collective-permute-start.6 = (bf16[96,640]{1,0:T(8,128)(2,1)S(1)}, bf16[96,640]{1,0:T(8,128)(2,1)S(1)}, u32[]{:S(2)}, u32[]{:S(2)}) collective-permute-start(bf16[96,640]{1,0:T(8,128)(2,1)S(1)} %collective-permute-done.5.refs_6_), channel_id=1, source_target_pairs={{0,4},{1,9},{2,6},{3,11},{8,0},{9,17},{10,2},{11,19},{16,8},{17,25... | collective-permute-start | bytes 368648 | tf_op jit(solution)/shard_map/ppermute | solution.py:91
  22.8 5.1 %collective-permute-start.3 = (bf16[96,640]{1,0:T(8,128)(2,1)S(1)}, bf16[96,640]{1,0:T(8,128)(2,1)S(1)}, u32[]{:S(2)}, u32[]{:S(2)}) collective-permute-start(bf16[96,640]{1,0:T(8,128)(2,1)S(1)} %collective-permute-done.2.refs_3_), channel_id=1, source_target_pairs={{0,8},{1,5},{2,10},{3,7},{8,16},{9,1},{10,18},{11,3},{16,24},{17,9... | collective-permute-start | bytes 368648 | tf_op jit(solution)/shard_map/ppermute | solution.py:91
  23.5 9.9 %collective-permute-start.19 = (bf16[96,640]{1,0:T(8,128)(2,1)S(1)}, bf16[96,640]{1,0:T(8,128)(2,1)S(1)}, u32[]{:S(2)}, u32[]{:S(2)}) collective-permute-start(bf16[96,640]{1,0:T(8,128)(2,1)S(1)} %shard_map.40), channel_id=1, source_target_pairs={{0,4},{1,9},{2,6},{3,11},{8,0},{9,17},{10,2},{11,19},{16,8},{17,25... | collective-permute-start | bytes 368648 | tf_op jit(solution)/shard_map/ppermute | solution.py:91
  25.5 7.9 %collective-permute-start.20 = (bf16[96,640]{1,0:T(8,128)(2,1)S(1)}, bf16[96,640]{1,0:T(8,128)(2,1)S(1)}, u32[]{:S(2)}, u32[]{:S(2)}) collective-permute-start(bf16[96,640]{1,0:T(8,128)(2,1)S(1)} %shard_map.41), channel_id=1, source_target_pairs={{0,8},{1,5},{2,10},{3,7},{8,16},{9,1},{10,18},{11,3},{16,24},{17,9... | collective-permute-start | bytes 368648 | tf_op jit(solution)/shard_map/ppermute | solution.py:91
  35.4 4.7 %collective-permute-start.21 = (bf16[2,192,640]{2,1,0:T(8,128)(2,1)S(1)}, bf16[2,192,640]{2,1,0:T(8,128)(2,1)S(1)}, u32[]{:S(2)}, u32[]{:S(2)}) collective-permute-start(bf16[2,192,640]{2,1,0:T(8,128)(2,1)S(1)} %bitcast.16), channel_id=1, source_target_pairs={{0,1},{1,0},{2,3},{3,2},{4,5},{5,4},{6,7},{7,6},{8,9},{9,8},{10,11... | collective-permute-start | bytes 1474568 | tf_op jit(solution)/shard_map/ppermute | solution.py:296
  41.4 7.3 %collective-permute-start.22 = (bf16[96,640]{1,0:T(8,128)(2,1)S(1)}, bf16[96,640]{1,0:T(8,128)(2,1)S(1)}, u32[]{:S(2)}, u32[]{:S(2)}) collective-permute-start(bf16[96,640]{1,0:T(8,128)(2,1)S(1)} %get-tuple-element.16.refs_0_), channel_id=1, source_target_pairs={{0,2},{1,3},{2,0},{3,1},{4,6},{5,7},{6,4},{7,5},{8,10},{9,11},{10,... | collective-permute-start | bytes 368648 | tf_op jit(solution)/shard_map/ppermute | solution.py:300
  44.7 9.4 %collective-permute-start.25 = (bf16[96,640]{1,0:T(8,128)(2,1)S(1)}, bf16[96,640]{1,0:T(8,128)(2,1)S(1)}, u32[]{:S(2)}, u32[]{:S(2)}) collective-permute-start(bf16[96,640]{1,0:T(8,128)(2,1)S(1)} %shard_map.46), channel_id=1, source_target_pairs={{0,8},{1,12},{2,0},{3,4},{4,24},{5,28},{6,16},{7,20},{8,25},{9,29}... | collective-permute-start | bytes 368648 | tf_op jit(solution)/shard_map/ppermute | solution.py:312
  48.7 8.3 %collective-permute-start.23 = (bf16[96,640]{1,0:T(8,128)(2,1)S(1)}, bf16[96,640]{1,0:T(8,128)(2,1)S(1)}, u32[]{:S(2)}, u32[]{:S(2)}) collective-permute-start(bf16[96,640]{1,0:T(8,128)(2,1)S(1)} %shard_map.45), channel_id=1, source_target_pairs={{0,24},{1,28},{2,16},{3,20},{4,8},{5,12},{6,0},{7,4},{8,1},{9,5},{... | collective-permute-start | bytes 368648 | tf_op jit(solution)/shard_map/ppermute | solution.py:312
  (5 other events, 15.3 us)

commit v24 on v20

--- a/solution.py
+++ b/solution.py
@@ -154,7 +154,7 @@
     return mixed[:, :HD], mixed[:, HD:]
 
 
-PATTERNS = ((2, 0, 1, 3), (3, 1, 0, 2), (0, 2, 3, 1), (1, 3, 2, 0))
+PATTERNS = ((3, 1, 0, 2), (0, 2, 3, 1), (1, 3, 2, 0), (2, 0, 1, 3))
 
 
 def look_up(table, index):

time: 60.9 us -> 60.6 us (level)
  starting transfers between devices: 32.1 us -> 31.4 us
    ppermute x2, starting transfers between devices: 9.47 us -> 8.77 us  [on_device_ring(): arrived.append(lax.ppermute(total, ('frames', 'heads'), pairs))]
where the time goes in v24:
time: 60.6 us; the launch traced here: 60.1 us
  starting transfers between devices  31.4 us (52%)
  waiting for transfers between devices  16.3 us (27%)
  Pallas kernels  9.44 us (16%)
  local copies, waits for them, and re-layouts  1.94 us (3%)
  other arithmetic  0.79 us (1%)
    ppermute x21, starting transfers between devices, hop(): return lax.ppermute(x, ('frames', 'heads'), pairs)  17.9 us
    pallas_call x8, Pallas kernels, call(): pl.pallas_call(kernel, out_shape=[jax.ShapeDtypeStruct(shape, dtype) for...  9.44 us
    ppermute x2, starting transfers between devices, on_device_ring(): arrived.append(lax.ppermute(total, ('frames', 'heads'), pairs))  8.77 us
    ppermute x21, waiting for transfers between devices, hop(): return lax.ppermute(x, ('frames', 'heads'), pairs)  8.01 us
    ppermute x2, waiting for transfers between devices, on_device_ring(): arrived.append(lax.ppermute(total, ('frames', 'heads'), pairs))  6.51 us
    ppermute x1, starting transfers between devices, on_device_ring(): from_core = lax.ppermute(given, 'heads', [(h, h ^ 1) for h in range(4)])  3.17 us
    unnamed x6, local copies, waits for them, and re-layouts  1.85 us
    ppermute x2, waiting for transfers between devices, on_device_ring(): lax.ppermute(block, 'heads', [(h, h ^ 2) for h in range(4)])  1.68 us
  transfers between devices with their start and end apart: 26, of which 15 were waited for; matrix products, arithmetic and copies ran while one was open for 0% of the time, Pallas kernels for 12%

profile of v24, /device:TPU:3, one launch (start us, length us, event | category | flops | bytes accessed | tf_op | source)
XLA Modules:
  0.0 60.1 jit_solution(6995946746343177919)
XLA Ops:
  0.0 1.2 %collective-permute-start = (bf16[96,640]{1,0:T(8,128)(2,1)}, bf16[96,640]{1,0:T(8,128)(2,1)S(1)}, u32[]{:S(2)}, u32[]{:S(2)}) collective-permute-start(bf16[96,640]{1,0:T(8,128)(2,1)} %refs_0_.1), channel_id=1, source_target_pairs={{0,8},{1,5},{2,10},{3,7},{8,16},{9,1},{10,18},{11,3},{16,24},{17,9... | collective-permute-start | bytes 368648 | tf_op jit(solution)/shard_map/ppermute | solution.py:91
  2.4 1.3 %collective-permute-start.10 = (bf16[96,640]{1,0:T(8,128)(2,1)S(1)}, bf16[96,640]{1,0:T(8,128)(2,1)S(1)}, u32[]{:S(2)}, u32[]{:S(2)}) collective-permute-start(bf16[96,640]{1,0:T(8,128)(2,1)S(1)} %get-tuple-element.10.refs_0_), channel_id=1, source_target_pairs={{0,4},{1,9},{2,6},{3,11},{8,0},{9,17},{10,2},{11,19},{16,8},{17,25... | collective-permute-start | bytes 368648 | tf_op jit(solution)/shard_map/ppermute | solution.py:91
  4.0 1.3 %collective-permute-start.16 = (bf16[96,640]{1,0:T(8,128)(2,1)S(1)}, bf16[96,640]{1,0:T(8,128)(2,1)S(1)}, u32[]{:S(2)}, u32[]{:S(2)}) collective-permute-start(bf16[96,640]{1,0:T(8,128)(2,1)S(1)} %get-tuple-element.11.refs_7_), channel_id=1, source_target_pairs={{0,4},{1,9},{2,6},{3,11},{8,0},{9,17},{10,2},{11,19},{16,8},{17,25... | collective-permute-start | bytes 368648 | tf_op jit(solution)/shard_map/ppermute | solution.py:91
  5.5 1.2 %collective-permute-done.4.refs_7_ = bf16[96,640]{1,0:T(8,128)(2,1)S(1)} collective-permute-done((bf16[96,640]{1,0:T(8,128)(2,1)}, bf16[96,640]{1,0:T(8,128)(2,1)S(1)}, u32[]{:S(2)}, u32[]{:S(2)}) %collective-permute-start.4) | collective-permute-done | bytes 122912 | tf_op jit(solution)/shard_map/ppermute | solution.py:91
  9.1 1.3 %collective-permute-start.11 = (bf16[96,640]{1,0:T(8,128)(2,1)S(1)}, bf16[96,640]{1,0:T(8,128)(2,1)S(1)}, u32[]{:S(2)}, u32[]{:S(2)}) collective-permute-start(bf16[96,640]{1,0:T(8,128)(2,1)S(1)} %collective-permute-done.10.refs_6_), channel_id=1, source_target_pairs={{0,4},{1,9},{2,6},{3,11},{8,0},{9,17},{10,2},{11,19},{16,8},{17,25... | collective-permute-start | bytes 368648 | tf_op jit(solution)/shard_map/ppermute | solution.py:91
  11.7 1.3 %collective-permute-start.17 = (bf16[96,640]{1,0:T(8,128)(2,1)S(1)}, bf16[96,640]{1,0:T(8,128)(2,1)S(1)}, u32[]{:S(2)}, u32[]{:S(2)}) collective-permute-start(bf16[96,640]{1,0:T(8,128)(2,1)S(1)} %collective-permute-done.16.refs_13_), channel_id=1, source_target_pairs={{0,4},{1,9},{2,6},{3,11},{8,0},{9,17},{10,2},{11,19},{16,8},{17,25... | collective-permute-start | bytes 368648 | tf_op jit(solution)/shard_map/ppermute | solution.py:91
  13.7 1.2 %collective-permute-start.8 = (bf16[96,640]{1,0:T(8,128)(2,1)S(1)}, bf16[96,640]{1,0:T(8,128)(2,1)S(1)}, u32[]{:S(2)}, u32[]{:S(2)}) collective-permute-start(bf16[96,640]{1,0:T(8,128)(2,1)S(1)} %collective-permute-done.7.refs_1_), channel_id=1, source_target_pairs={{0,8},{1,5},{2,10},{3,7},{8,16},{9,1},{10,18},{11,3},{16,24},{17,9... | collective-permute-start | bytes 368648 | tf_op jit(solution)/shard_map/ppermute | solution.py:91
  16.3 1.3 %collective-permute-start.12 = (bf16[96,640]{1,0:T(8,128)(2,1)S(1)}, bf16[96,640]{1,0:T(8,128)(2,1)S(1)}, u32[]{:S(2)}, u32[]{:S(2)}) collective-permute-start(bf16[96,640]{1,0:T(8,128)(2,1)S(1)} %collective-permute-done.11.refs_5_), channel_id=1, source_target_pairs={{0,4},{1,9},{2,6},{3,11},{8,0},{9,17},{10,2},{11,19},{16,8},{17,25... | collective-permute-start | bytes 368648 | tf_op jit(solution)/shard_map/ppermute | solution.py:91
  18.1 1.2 %collective-permute-start.15 = (bf16[96,640]{1,0:T(8,128)(2,1)S(1)}, bf16[96,640]{1,0:T(8,128)(2,1)S(1)}, u32[]{:S(2)}, u32[]{:S(2)}) collective-permute-start(bf16[96,640]{1,0:T(8,128)(2,1)S(1)} %collective-permute-done.14.refs_9_), channel_id=1, source_target_pairs={{0,8},{1,5},{2,10},{3,7},{8,16},{9,1},{10,18},{11,3},{16,24},{17,9... | collective-permute-start | bytes 368648 | tf_op jit(solution)/shard_map/ppermute | solution.py:91
  19.3 1.3 %collective-permute-start.3 = (bf16[96,640]{1,0:T(8,128)(2,1)S(1)}, bf16[96,640]{1,0:T(8,128)(2,1)S(1)}, u32[]{:S(2)}, u32[]{:S(2)}) collective-permute-start(bf16[96,640]{1,0:T(8,128)(2,1)S(1)} %collective-permute-done.2.refs_3_), channel_id=1, source_target_pairs={{0,8},{1,5},{2,10},{3,7},{8,16},{9,1},{10,18},{11,3},{16,24},{17,9... | collective-permute-start | bytes 368648 | tf_op jit(solution)/shard_map/ppermute | solution.py:91
  21.4 1.3 %collective-permute-start.18 = (bf16[96,640]{1,0:T(8,128)(2,1)S(1)}, bf16[96,640]{1,0:T(8,128)(2,1)S(1)}, u32[]{:S(2)}, u32[]{:S(2)}) collective-permute-start(bf16[96,640]{1,0:T(8,128)(2,1)S(1)} %collective-permute-done.17.refs_12_), channel_id=1, source_target_pairs={{0,4},{1,9},{2,6},{3,11},{8,0},{9,17},{10,2},{11,19},{16,8},{17,25... | collective-permute-start | bytes 368648 | tf_op jit(solution)/shard_map/ppermute | solution.py:91
  24.7 1.2 %collective-permute-done.3.refs_4_ = bf16[96,640]{1,0:T(8,128)(2,1)S(1)} collective-permute-done((bf16[96,640]{1,0:T(8,128)(2,1)S(1)}, bf16[96,640]{1,0:T(8,128)(2,1)S(1)}, u32[]{:S(2)}, u32[]{:S(2)}) %collective-permute-start.3) | collective-permute-done | bytes 122912 | tf_op jit(solution)/shard_map/ppermute | solution.py:91
  26.8 1.2 %collective-permute-done.9.refs_3_ = bf16[96,640]{1,0:T(8,128)(2,1)S(1)} collective-permute-done((bf16[96,640]{1,0:T(8,128)(2,1)S(1)}, bf16[96,640]{1,0:T(8,128)(2,1)S(1)}, u32[]{:S(2)}, u32[]{:S(2)}) %collective-permute-start.9) | collective-permute-done | bytes 122912 | tf_op jit(solution)/shard_map/ppermute | solution.py:91
  28.0 4.6 %shard_map.39 = (f32[5,8,96,128]{3,2,1,0:T(8,128)S(1)}, f32[5,8,96,128]{3,2,1,0:T(8,128)S(1)}, f32[5,8,96,128]{3,2,1,0:T(8,128)S(1)}) custom-call(s32[5]{0:T(128)S(1)} %stack.23.at_ref, bf16[8,96,640]{2,1,0:T(8,128)(2,1)S(1)} %shard_map.37.rows_ref, bf16[96,640]{1,0:T(8,128)(2,1)S(1)} %get-tuple-element.10.refs_0_, ...), custom_call_target="tpu_custom_call" | custom-call | flops 1321205760 | tf_op jit(solution)/shard_map/pallas_call | solution.py:243
  32.6 2.0 %shard_map.40 = bf16[384,640]{1,0:T(8,128)(2,1)S(1)} custom-call(s32[5]{0:T(128)S(1)} %stack.23.at_ref, bf16[8,96,640]{2,1,0:T(8,128)(2,1)S(1)} %shard_map.37.rows_ref, f32[5,8,96,128]{3,2,1,0:T(8,128)S(1)} %get-tuple-element.12.mixed_ref, f32[5,8,96,128]{3,2,1,0:T(8,128)S(1)} %get-tuple-element.13.sum_ref, f32[5,8,96,128]{3,2,1,0:T(8,128)S(1)} %get-tuple-element.14.top_ref, ...), custom_call_target="tpu_custom_call" | custom-call | flops 314572800 | tf_op jit(solution)/shard_map/pallas_call | solution.py:243
  34.6 3.2 %collective-permute-start.21 = (bf16[2,192,640]{2,1,0:T(8,128)(2,1)S(1)}, bf16[2,192,640]{2,1,0:T(8,128)(2,1)S(1)}, u32[]{:S(2)}, u32[]{:S(2)}) collective-permute-start(bf16[2,192,640]{2,1,0:T(8,128)(2,1)S(1)} %bitcast.16), channel_id=1, source_target_pairs={{0,1},{1,0},{2,3},{3,2},{4,5},{5,4},{6,7},{7,6},{8,9},{9,8},{10,11... | collective-permute-start | bytes 1474568 | tf_op jit(solution)/shard_map/ppermute | solution.py:288
  37.8 1.4 %shard_map.41 = f32[192,640]{1,0:T(8,128)S(1)} custom-call(s32[5]{0:T(128)S(1)} %stack.23.at_ref, bf16[8,96,640]{2,1,0:T(8,128)(2,1)S(1)} %shard_map.37.rows_ref, f32[5,8,96,128]{3,2,1,0:T(8,128)S(1)} %get-tuple-element.12.mixed_ref, f32[5,8,96,128]{3,2,1,0:T(8,128)S(1)} %get-tuple-element.13.sum_ref, f32[5,8,96,128]{3,2,1,0:T(8,128)S(1)} %get-tuple-element.14.top_ref, ...), custom_call_target="tpu_custom_call" | custom-call | flops 314572800 | tf_op jit(solution)/shard_map/pallas_call | solution.py:243
  39.6 1.2 %collective-permute-start.22 = (bf16[96,640]{1,0:T(8,128)(2,1)S(1)}, bf16[96,640]{1,0:T(8,128)(2,1)S(1)}, u32[]{:S(2)}, u32[]{:S(2)}) collective-permute-start(bf16[96,640]{1,0:T(8,128)(2,1)S(1)} %get-tuple-element.16.refs_0_), channel_id=1, source_target_pairs={{0,2},{1,3},{2,0},{3,1},{4,6},{5,7},{6,4},{7,5},{8,10},{9,11},{10,... | collective-permute-start | bytes 368648 | tf_op jit(solution)/shard_map/ppermute | solution.py:292
  40.9 1.4 %shard_map.42.kept_ref = f32[192,640]{1,0:T(8,128)S(1)} custom-call(s32[5]{0:T(128)S(1)} %stack.23.at_ref, bf16[8,96,640]{2,1,0:T(8,128)(2,1)S(1)} %shard_map.37.rows_ref, f32[5,8,96,128]{3,2,1,0:T(8,128)S(1)} %get-tuple-element.12.mixed_ref, f32[5,8,96,128]{3,2,1,0:T(8,128)S(1)} %get-tuple-element.13.sum_ref, ...), custom_call_target="tpu_custom_call" | custom-call | flops 314572800 | tf_op jit(solution)/shard_map/pallas_call | solution.py:243
  42.2 1.7 %collective-permute-done.24.from_x_ref = bf16[96,640]{1,0:T(8,128)(2,1)S(1)} collective-permute-done((bf16[96,640]{1,0:T(8,128)(2,1)S(1)}, bf16[96,640]{1,0:T(8,128)(2,1)S(1)}, u32[]{:S(2)}, u32[]{:S(2)}) %collective-permute-start.24) | collective-permute-done | bytes 122912 | tf_op jit(solution)/shard_map/ppermute | solution.py:292
  43.9 6.8 %collective-permute-start.25 = (bf16[96,640]{1,0:T(8,128)(2,1)S(1)}, bf16[96,640]{1,0:T(8,128)(2,1)S(1)}, u32[]{:S(2)}, u32[]{:S(2)}) collective-permute-start(bf16[96,640]{1,0:T(8,128)(2,1)S(1)} %shard_map.44), channel_id=1, source_target_pairs={{0,0},{1,4},{2,16},{3,20},{4,24},{5,28},{6,8},{7,12},{8,17},{9,21}... | collective-permute-start | bytes 368648 | tf_op jit(solution)/shard_map/ppermute | solution.py:304
  50.9 1.9 %collective-permute-start.23 = (bf16[96,640]{1,0:T(8,128)(2,1)S(1)}, bf16[96,640]{1,0:T(8,128)(2,1)S(1)}, u32[]{:S(2)}, u32[]{:S(2)}) collective-permute-start(bf16[96,640]{1,0:T(8,128)(2,1)S(1)} %shard_map.43), channel_id=1, source_target_pairs={{0,24},{1,28},{2,8},{3,12},{4,0},{5,4},{6,16},{7,20},{8,9},{9,13},... | collective-permute-start | bytes 368648 | tf_op jit(solution)/shard_map/ppermute | solution.py:304
  52.8 1.4 %collective-permute-done.25 = bf16[96,640]{1,0:T(8,128)(2,1)S(1)} collective-permute-done((bf16[96,640]{1,0:T(8,128)(2,1)S(1)}, bf16[96,640]{1,0:T(8,128)(2,1)S(1)}, u32[]{:S(2)}, u32[]{:S(2)}) %collective-permute-start.25) | collective-permute-done | bytes 122912 | tf_op jit(solution)/shard_map/ppermute | solution.py:304
  54.2 5.1 %collective-permute-done.23 = bf16[96,640]{1,0:T(8,128)(2,1)S(1)} collective-permute-done((bf16[96,640]{1,0:T(8,128)(2,1)S(1)}, bf16[96,640]{1,0:T(8,128)(2,1)S(1)}, u32[]{:S(2)}, u32[]{:S(2)}) %collective-permute-start.23) | collective-permute-done | bytes 122912 | tf_op jit(solution)/shard_map/ppermute | solution.py:304
  (46 shorter events, 13.0 us)
Async XLA Ops:
  0.0 5.3 %collective-permute-start = (bf16[96,640]{1,0:T(8,128)(2,1)}, bf16[96,640]{1,0:T(8,128)(2,1)S(1)}, u32[]{:S(2)}, u32[]{:S(2)}) collective-permute-start(bf16[96,640]{1,0:T(8,128)(2,1)} %refs_0_.1), channel_id=1, source_target_pairs={{0,8},{1,5},{2,10},{3,7},{8,16},{9,1},{10,18},{11,3},{16,24},{17,9... | collective-permute-start | bytes 368648 | tf_op jit(solution)/shard_map/ppermute | solution.py:91
  1.2 5.4 %collective-permute-start.4 = (bf16[96,640]{1,0:T(8,128)(2,1)}, bf16[96,640]{1,0:T(8,128)(2,1)S(1)}, u32[]{:S(2)}, u32[]{:S(2)}) collective-permute-start(bf16[96,640]{1,0:T(8,128)(2,1)} %refs_0_.1), channel_id=1, source_target_pairs={{0,4},{1,9},{2,6},{3,11},{8,0},{9,17},{10,2},{11,19},{16,8},{17,25... | collective-permute-start | bytes 368648 | tf_op jit(solution)/shard_map/ppermute | solution.py:91
  2.4 5.6 %collective-permute-start.10 = (bf16[96,640]{1,0:T(8,128)(2,1)S(1)}, bf16[96,640]{1,0:T(8,128)(2,1)S(1)}, u32[]{:S(2)}, u32[]{:S(2)}) collective-permute-start(bf16[96,640]{1,0:T(8,128)(2,1)S(1)} %get-tuple-element.10.refs_0_), channel_id=1, source_target_pairs={{0,4},{1,9},{2,6},{3,11},{8,0},{9,17},{10,2},{11,19},{16,8},{17,25... | collective-permute-start | bytes 368648 | tf_op jit(solution)/shard_map/ppermute | solution.py:91
  3.8 5.3 %collective-permute-start.13 = (bf16[96,640]{1,0:T(8,128)(2,1)S(1)}, bf16[96,640]{1,0:T(8,128)(2,1)S(1)}, u32[]{:S(2)}, u32[]{:S(2)}) collective-permute-start(bf16[96,640]{1,0:T(8,128)(2,1)S(1)} %get-tuple-element.11.refs_7_), channel_id=1, source_target_pairs={{0,8},{1,5},{2,10},{3,7},{8,16},{9,1},{10,18},{11,3},{16,24},{17,9... | collective-permute-start | bytes 368648 | tf_op jit(solution)/shard_map/ppermute | solution.py:91
  4.0 6.5 %collective-permute-start.16 = (bf16[96,640]{1,0:T(8,128)(2,1)S(1)}, bf16[96,640]{1,0:T(8,128)(2,1)S(1)}, u32[]{:S(2)}, u32[]{:S(2)}) collective-permute-start(bf16[96,640]{1,0:T(8,128)(2,1)S(1)} %get-tuple-element.11.refs_7_), channel_id=1, source_target_pairs={{0,4},{1,9},{2,6},{3,11},{8,0},{9,17},{10,2},{11,19},{16,8},{17,25... | collective-permute-start | bytes 368648 | tf_op jit(solution)/shard_map/ppermute | solution.py:91
  5.3 6.5 %collective-permute-start.7 = (bf16[96,640]{1,0:T(8,128)(2,1)S(1)}, bf16[96,640]{1,0:T(8,128)(2,1)S(1)}, u32[]{:S(2)}, u32[]{:S(2)}) collective-permute-start(bf16[96,640]{1,0:T(8,128)(2,1)S(1)} %get-tuple-element.10.refs_0_), channel_id=1, source_target_pairs={{0,8},{1,5},{2,10},{3,7},{8,16},{9,1},{10,18},{11,3},{16,24},{17,9... | collective-permute-start | bytes 368648 | tf_op jit(solution)/shard_map/ppermute | solution.py:91
  6.7 6.8 %collective-permute-start.1 = (bf16[96,640]{1,0:T(8,128)(2,1)S(1)}, bf16[96,640]{1,0:T(8,128)(2,1)S(1)}, u32[]{:S(2)}, u32[]{:S(2)}) collective-permute-start(bf16[96,640]{1,0:T(8,128)(2,1)S(1)} %collective-permute-done.refs_1_), channel_id=1, source_target_pairs={{0,8},{1,5},{2,10},{3,7},{8,16},{9,1},{10,18},{11,3},{16,24},{17,9... | collective-permute-start | bytes 368648 | tf_op jit(solution)/shard_map/ppermute | solution.py:91
  8.0 5.7 %collective-permute-start.5 = (bf16[96,640]{1,0:T(8,128)(2,1)S(1)}, bf16[96,640]{1,0:T(8,128)(2,1)S(1)}, u32[]{:S(2)}, u32[]{:S(2)}) collective-permute-start(bf16[96,640]{1,0:T(8,128)(2,1)S(1)} %collective-permute-done.4.refs_7_), channel_id=1, source_target_pairs={{0,4},{1,9},{2,6},{3,11},{8,0},{9,17},{10,2},{11,19},{16,8},{17,25... | collective-permute-start | bytes 368648 | tf_op jit(solution)/shard_map/ppermute | solution.py:91
  9.1 6.8 %collective-permute-start.11 = (bf16[96,640]{1,0:T(8,128)(2,1)S(1)}, bf16[96,640]{1,0:T(8,128)(2,1)S(1)}, u32[]{:S(2)}, u32[]{:S(2)}) collective-permute-start(bf16[96,640]{1,0:T(8,128)(2,1)S(1)} %collective-permute-done.10.refs_6_), channel_id=1, source_target_pairs={{0,4},{1,9},{2,6},{3,11},{8,0},{9,17},{10,2},{11,19},{16,8},{17,25... | collective-permute-start | bytes 368648 | tf_op jit(solution)/shard_map/ppermute | solution.py:91
  10.4 5.9 %collective-permute-start.14 = (bf16[96,640]{1,0:T(8,128)(2,1)S(1)}, bf16[96,640]{1,0:T(8,128)(2,1)S(1)}, u32[]{:S(2)}, u32[]{:S(2)}) collective-permute-start(bf16[96,640]{1,0:T(8,128)(2,1)S(1)} %collective-permute-done.13.refs_8_), channel_id=1, source_target_pairs={{0,8},{1,5},{2,10},{3,7},{8,16},{9,1},{10,18},{11,3},{16,24},{17,9... | collective-permute-start | bytes 368648 | tf_op jit(solution)/shard_map/ppermute | solution.py:91
  11.7 6.4 %collective-permute-start.17 = (bf16[96,640]{1,0:T(8,128)(2,1)S(1)}, bf16[96,640]{1,0:T(8,128)(2,1)S(1)}, u32[]{:S(2)}, u32[]{:S(2)}) collective-permute-start(bf16[96,640]{1,0:T(8,128)(2,1)S(1)} %collective-permute-done.16.refs_13_), channel_id=1, source_target_pairs={{0,4},{1,9},{2,6},{3,11},{8,0},{9,17},{10,2},{11,19},{16,8},{17,25... | collective-permute-start | bytes 368648 | tf_op jit(solution)/shard_map/ppermute | solution.py:91
  13.5 5.8 %collective-permute-start.2 = (bf16[96,640]{1,0:T(8,128)(2,1)S(1)}, bf16[96,640]{1,0:T(8,128)(2,1)S(1)}, u32[]{:S(2)}, u32[]{:S(2)}) collective-permute-start(bf16[96,640]{1,0:T(8,128)(2,1)S(1)} %collective-permute-done.1.refs_2_), channel_id=1, source_target_pairs={{0,8},{1,5},{2,10},{3,7},{8,16},{9,1},{10,18},{11,3},{16,24},{17,9... | collective-permute-start | bytes 368648 | tf_op jit(solution)/shard_map/ppermute | solution.py:91
  13.7 7.7 %collective-permute-start.8 = (bf16[96,640]{1,0:T(8,128)(2,1)S(1)}, bf16[96,640]{1,0:T(8,128)(2,1)S(1)}, u32[]{:S(2)}, u32[]{:S(2)}) collective-permute-start(bf16[96,640]{1,0:T(8,128)(2,1)S(1)} %collective-permute-done.7.refs_1_), channel_id=1, source_target_pairs={{0,8},{1,5},{2,10},{3,7},{8,16},{9,1},{10,18},{11,3},{16,24},{17,9... | collective-permute-start | bytes 368648 | tf_op jit(solution)/shard_map/ppermute | solution.py:91
  15.9 6.8 %collective-permute-start.6 = (bf16[96,640]{1,0:T(8,128)(2,1)S(1)}, bf16[96,640]{1,0:T(8,128)(2,1)S(1)}, u32[]{:S(2)}, u32[]{:S(2)}) collective-permute-start(bf16[96,640]{1,0:T(8,128)(2,1)S(1)} %collective-permute-done.5.refs_6_), channel_id=1, source_target_pairs={{0,4},{1,9},{2,6},{3,11},{8,0},{9,17},{10,2},{11,19},{16,8},{17,25... | collective-permute-start | bytes 368648 | tf_op jit(solution)/shard_map/ppermute | solution.py:91
  16.3 6.9 %collective-permute-start.12 = (bf16[96,640]{1,0:T(8,128)(2,1)S(1)}, bf16[96,640]{1,0:T(8,128)(2,1)S(1)}, u32[]{:S(2)}, u32[]{:S(2)}) collective-permute-start(bf16[96,640]{1,0:T(8,128)(2,1)S(1)} %collective-permute-done.11.refs_5_), channel_id=1, source_target_pairs={{0,4},{1,9},{2,6},{3,11},{8,0},{9,17},{10,2},{11,19},{16,8},{17,25... | collective-permute-start | bytes 368648 | tf_op jit(solution)/shard_map/ppermute | solution.py:91
  18.1 6.2 %collective-permute-start.15 = (bf16[96,640]{1,0:T(8,128)(2,1)S(1)}, bf16[96,640]{1,0:T(8,128)(2,1)S(1)}, u32[]{:S(2)}, u32[]{:S(2)}) collective-permute-start(bf16[96,640]{1,0:T(8,128)(2,1)S(1)} %collective-permute-done.14.refs_9_), channel_id=1, source_target_pairs={{0,8},{1,5},{2,10},{3,7},{8,16},{9,1},{10,18},{11,3},{16,24},{17,9... | collective-permute-start | bytes 368648 | tf_op jit(solution)/shard_map/ppermute | solution.py:91
  19.3 6.5 %collective-permute-start.3 = (bf16[96,640]{1,0:T(8,128)(2,1)S(1)}, bf16[96,640]{1,0:T(8,128)(2,1)S(1)}, u32[]{:S(2)}, u32[]{:S(2)}) collective-permute-start(bf16[96,640]{1,0:T(8,128)(2,1)S(1)} %collective-permute-done.2.refs_3_), channel_id=1, source_target_pairs={{0,8},{1,5},{2,10},{3,7},{8,16},{9,1},{10,18},{11,3},{16,24},{17,9... | collective-permute-start | bytes 368648 | tf_op jit(solution)/shard_map/ppermute | solution.py:91
  21.4 5.4 %collective-permute-start.18 = (bf16[96,640]{1,0:T(8,128)(2,1)S(1)}, bf16[96,640]{1,0:T(8,128)(2,1)S(1)}, u32[]{:S(2)}, u32[]{:S(2)}) collective-permute-start(bf16[96,640]{1,0:T(8,128)(2,1)S(1)} %collective-permute-done.17.refs_12_), channel_id=1, source_target_pairs={{0,4},{1,9},{2,6},{3,11},{8,0},{9,17},{10,2},{11,19},{16,8},{17,25... | collective-permute-start | bytes 368648 | tf_op jit(solution)/shard_map/ppermute | solution.py:91
  22.7 5.3 %collective-permute-start.9 = (bf16[96,640]{1,0:T(8,128)(2,1)S(1)}, bf16[96,640]{1,0:T(8,128)(2,1)S(1)}, u32[]{:S(2)}, u32[]{:S(2)}) collective-permute-start(bf16[96,640]{1,0:T(8,128)(2,1)S(1)} %collective-permute-done.8.refs_2_), channel_id=1, source_target_pairs={{0,8},{1,5},{2,10},{3,7},{8,16},{9,1},{10,18},{11,3},{16,24},{17,9... | collective-permute-start | bytes 368648 | tf_op jit(solution)/shard_map/ppermute | solution.py:91
  23.2 9.4 %collective-permute-start.19 = (bf16[96,640]{1,0:T(8,128)(2,1)S(1)}, bf16[96,640]{1,0:T(8,128)(2,1)S(1)}, u32[]{:S(2)}, u32[]{:S(2)}) collective-permute-start(bf16[96,640]{1,0:T(8,128)(2,1)S(1)} %collective-permute-done.12.refs_4_), channel_id=1, source_target_pairs={{0,4},{1,9},{2,6},{3,11},{8,0},{9,17},{10,2},{11,19},{16,8},{17,25... | collective-permute-start | bytes 368648 | tf_op jit(solution)/shard_map/ppermute | solution.py:91
  24.3 8.3 %collective-permute-start.20 = (bf16[96,640]{1,0:T(8,128)(2,1)S(1)}, bf16[96,640]{1,0:T(8,128)(2,1)S(1)}, u32[]{:S(2)}, u32[]{:S(2)}) collective-permute-start(bf16[96,640]{1,0:T(8,128)(2,1)S(1)} %collective-permute-done.15.refs_10_), channel_id=1, source_target_pairs={{0,8},{1,5},{2,10},{3,7},{8,16},{9,1},{10,18},{11,3},{16,24},{17,9... | collective-permute-start | bytes 368648 | tf_op jit(solution)/shard_map/ppermute | solution.py:91
  39.6 11.2 %collective-permute-start.22 = (bf16[96,640]{1,0:T(8,128)(2,1)S(1)}, bf16[96,640]{1,0:T(8,128)(2,1)S(1)}, u32[]{:S(2)}, u32[]{:S(2)}) collective-permute-start(bf16[96,640]{1,0:T(8,128)(2,1)S(1)} %get-tuple-element.16.refs_0_), channel_id=1, source_target_pairs={{0,2},{1,3},{2,0},{3,1},{4,6},{5,7},{6,4},{7,5},{8,10},{9,11},{10,... | collective-permute-start | bytes 368648 | tf_op jit(solution)/shard_map/ppermute | solution.py:292
  43.9 10.3 %collective-permute-start.25 = (bf16[96,640]{1,0:T(8,128)(2,1)S(1)}, bf16[96,640]{1,0:T(8,128)(2,1)S(1)}, u32[]{:S(2)}, u32[]{:S(2)}) collective-permute-start(bf16[96,640]{1,0:T(8,128)(2,1)S(1)} %shard_map.44), channel_id=1, source_target_pairs={{0,0},{1,4},{2,16},{3,20},{4,24},{5,28},{6,8},{7,12},{8,17},{9,21}... | collective-permute-start | bytes 368648 | tf_op jit(solution)/shard_map/ppermute | solution.py:304
  50.9 8.5 %collective-permute-start.23 = (bf16[96,640]{1,0:T(8,128)(2,1)S(1)}, bf16[96,640]{1,0:T(8,128)(2,1)S(1)}, u32[]{:S(2)}, u32[]{:S(2)}) collective-permute-start(bf16[96,640]{1,0:T(8,128)(2,1)S(1)} %shard_map.43), channel_id=1, source_target_pairs={{0,24},{1,28},{2,8},{3,12},{4,0},{5,4},{6,16},{7,20},{8,9},{9,13},... | collective-permute-start | bytes 368648 | tf_op jit(solution)/shard_map/ppermute | solution.py:304
  (5 other events, 16.9 us)

commit v25 on v24

--- a/solution.py
+++ b/solution.py
@@ -154,7 +154,7 @@
     return mixed[:, :HD], mixed[:, HD:]
 
 
-PATTERNS = ((3, 1, 0, 2), (0, 2, 3, 1), (1, 3, 2, 0), (2, 0, 1, 3))
+PATTERNS = ((3, 0, 1, 3), (1, 3, 2, 1), (2, 1, 0, 2), (0, 2, 3, 0))
 
 
 def look_up(table, index):

time: 60.6 us -> 57 us (0.941)
  starting transfers between devices: 31.4 us -> 29.4 us
  waiting for transfers between devices: 16.3 us -> 14.8 us
    ppermute x2, starting transfers between devices: 8.77 us -> 6.79 us  [on_device_ring(): arrived.append(lax.ppermute(total, ('frames', 'heads'), pairs))]
    ppermute x2, waiting for transfers between devices: 6.51 us -> 5 us  [on_device_ring(): arrived.append(lax.ppermute(total, ('frames', 'heads'), pairs))]
  transfers between devices with their start and end apart: 26 -> 26, of which waited for: 15 -> 15; matrix products, arithmetic and copies ran while one was open for 0% -> 0% of each run, Pallas kernels for 12% -> 13%
where the time goes in v25:
time: 57 us; the launch traced here: 56.5 us
  starting transfers between devices  29.4 us (52%)
  waiting for transfers between devices  14.8 us (26%)
  Pallas kernels  9.43 us (17%)
  local copies, waits for them, and re-layouts  1.94 us (3%)
  other arithmetic  0.79 us (1%)
    ppermute x21, starting transfers between devices, hop(): return lax.ppermute(x, ('frames', 'heads'), pairs)  17.9 us
    pallas_call x8, Pallas kernels, call(): pl.pallas_call(kernel, out_shape=[jax.ShapeDtypeStruct(shape, dtype) for...  9.43 us
    ppermute x21, waiting for transfers between devices, hop(): return lax.ppermute(x, ('frames', 'heads'), pairs)  8.01 us
    ppermute x2, starting transfers between devices, on_device_ring(): arrived.append(lax.ppermute(total, ('frames', 'heads'), pairs))  6.79 us
    ppermute x2, waiting for transfers between devices, on_device_ring(): arrived.append(lax.ppermute(total, ('frames', 'heads'), pairs))  5 us
    ppermute x1, starting transfers between devices, on_device_ring(): from_core = lax.ppermute(given, 'heads', [(h, h ^ 1) for h in range(4)])  3.17 us
    unnamed x6, local copies, waits for them, and re-layouts  1.85 us
    ppermute x2, waiting for transfers between devices, on_device_ring(): lax.ppermute(block, 'heads', [(h, h ^ 2) for h in range(4)])  1.68 us
  transfers between devices with their start and end apart: 26, of which 15 were waited for; matrix products, arithmetic and copies ran while one was open for 0% of the time, Pallas kernels for 13%

profile of v25, /device:TPU:3, one launch (start us, length us, event | category | flops | bytes accessed | tf_op | source)
XLA Modules:
  0.0 56.5 jit_solution(4039113873618149774)
XLA Ops:
  0.0 1.2 %collective-permute-start = (bf16[96,640]{1,0:T(8,128)(2,1)}, bf16[96,640]{1,0:T(8,128)(2,1)S(1)}, u32[]{:S(2)}, u32[]{:S(2)}) collective-permute-start(bf16[96,640]{1,0:T(8,128)(2,1)} %refs_0_.1), channel_id=1, source_target_pairs={{0,8},{1,5},{2,10},{3,7},{8,16},{9,1},{10,18},{11,3},{16,24},{17,9... | collective-permute-start | bytes 368648 | tf_op jit(solution)/shard_map/ppermute | solution.py:91
  2.4 1.3 %collective-permute-start.10 = (bf16[96,640]{1,0:T(8,128)(2,1)S(1)}, bf16[96,640]{1,0:T(8,128)(2,1)S(1)}, u32[]{:S(2)}, u32[]{:S(2)}) collective-permute-start(bf16[96,640]{1,0:T(8,128)(2,1)S(1)} %get-tuple-element.10.refs_0_), channel_id=1, source_target_pairs={{0,4},{1,9},{2,6},{3,11},{8,0},{9,17},{10,2},{11,19},{16,8},{17,25... | collective-permute-start | bytes 368648 | tf_op jit(solution)/shard_map/ppermute | solution.py:91
  4.0 1.3 %collective-permute-start.16 = (bf16[96,640]{1,0:T(8,128)(2,1)S(1)}, bf16[96,640]{1,0:T(8,128)(2,1)S(1)}, u32[]{:S(2)}, u32[]{:S(2)}) collective-permute-start(bf16[96,640]{1,0:T(8,128)(2,1)S(1)} %get-tuple-element.11.refs_7_), channel_id=1, source_target_pairs={{0,4},{1,9},{2,6},{3,11},{8,0},{9,17},{10,2},{11,19},{16,8},{17,25... | collective-permute-start | bytes 368648 | tf_op jit(solution)/shard_map/ppermute | solution.py:91
  5.5 1.2 %collective-permute-done.4.refs_7_ = bf16[96,640]{1,0:T(8,128)(2,1)S(1)} collective-permute-done((bf16[96,640]{1,0:T(8,128)(2,1)}, bf16[96,640]{1,0:T(8,128)(2,1)S(1)}, u32[]{:S(2)}, u32[]{:S(2)}) %collective-permute-start.4) | collective-permute-done | bytes 122912 | tf_op jit(solution)/shard_map/ppermute | solution.py:91
  9.1 1.3 %collective-permute-start.11 = (bf16[96,640]{1,0:T(8,128)(2,1)S(1)}, bf16[96,640]{1,0:T(8,128)(2,1)S(1)}, u32[]{:S(2)}, u32[]{:S(2)}) collective-permute-start(bf16[96,640]{1,0:T(8,128)(2,1)S(1)} %collective-permute-done.10.refs_6_), channel_id=1, source_target_pairs={{0,4},{1,9},{2,6},{3,11},{8,0},{9,17},{10,2},{11,19},{16,8},{17,25... | collective-permute-start | bytes 368648 | tf_op jit(solution)/shard_map/ppermute | solution.py:91
  11.7 1.3 %collective-permute-start.17 = (bf16[96,640]{1,0:T(8,128)(2,1)S(1)}, bf16[96,640]{1,0:T(8,128)(2,1)S(1)}, u32[]{:S(2)}, u32[]{:S(2)}) collective-permute-start(bf16[96,640]{1,0:T(8,128)(2,1)S(1)} %collective-permute-done.16.refs_13_), channel_id=1, source_target_pairs={{0,4},{1,9},{2,6},{3,11},{8,0},{9,17},{10,2},{11,19},{16,8},{17,25... | collective-permute-start | bytes 368648 | tf_op jit(solution)/shard_map/ppermute | solution.py:91
  13.7 1.2 %collective-permute-start.8 = (bf16[96,640]{1,0:T(8,128)(2,1)S(1)}, bf16[96,640]{1,0:T(8,128)(2,1)S(1)}, u32[]{:S(2)}, u32[]{:S(2)}) collective-permute-start(bf16[96,640]{1,0:T(8,128)(2,1)S(1)} %collective-permute-done.7.refs_1_), channel_id=1, source_target_pairs={{0,8},{1,5},{2,10},{3,7},{8,16},{9,1},{10,18},{11,3},{16,24},{17,9... | collective-permute-start | bytes 368648 | tf_op jit(solution)/shard_map/ppermute | solution.py:91
  16.3 1.3 %collective-permute-start.12 = (bf16[96,640]{1,0:T(8,128)(2,1)S(1)}, bf16[96,640]{1,0:T(8,128)(2,1)S(1)}, u32[]{:S(2)}, u32[]{:S(2)}) collective-permute-start(bf16[96,640]{1,0:T(8,128)(2,1)S(1)} %collective-permute-done.11.refs_5_), channel_id=1, source_target_pairs={{0,4},{1,9},{2,6},{3,11},{8,0},{9,17},{10,2},{11,19},{16,8},{17,25... | collective-permute-start | bytes 368648 | tf_op jit(solution)/shard_map/ppermute | solution.py:91
  18.1 1.2 %collective-permute-start.15 = (bf16[96,640]{1,0:T(8,128)(2,1)S(1)}, bf16[96,640]{1,0:T(8,128)(2,1)S(1)}, u32[]{:S(2)}, u32[]{:S(2)}) collective-permute-start(bf16[96,640]{1,0:T(8,128)(2,1)S(1)} %collective-permute-done.14.refs_9_), channel_id=1, source_target_pairs={{0,8},{1,5},{2,10},{3,7},{8,16},{9,1},{10,18},{11,3},{16,24},{17,9... | collective-permute-start | bytes 368648 | tf_op jit(solution)/shard_map/ppermute | solution.py:91
  19.3 1.3 %collective-permute-start.3 = (bf16[96,640]{1,0:T(8,128)(2,1)S(1)}, bf16[96,640]{1,0:T(8,128)(2,1)S(1)}, u32[]{:S(2)}, u32[]{:S(2)}) collective-permute-start(bf16[96,640]{1,0:T(8,128)(2,1)S(1)} %collective-permute-done.2.refs_3_), channel_id=1, source_target_pairs={{0,8},{1,5},{2,10},{3,7},{8,16},{9,1},{10,18},{11,3},{16,24},{17,9... | collective-permute-start | bytes 368648 | tf_op jit(solution)/shard_map/ppermute | solution.py:91
  21.4 1.3 %collective-permute-start.18 = (bf16[96,640]{1,0:T(8,128)(2,1)S(1)}, bf16[96,640]{1,0:T(8,128)(2,1)S(1)}, u32[]{:S(2)}, u32[]{:S(2)}) collective-permute-start(bf16[96,640]{1,0:T(8,128)(2,1)S(1)} %collective-permute-done.17.refs_12_), channel_id=1, source_target_pairs={{0,4},{1,9},{2,6},{3,11},{8,0},{9,17},{10,2},{11,19},{16,8},{17,25... | collective-permute-start | bytes 368648 | tf_op jit(solution)/shard_map/ppermute | solution.py:91
  24.7 1.2 %collective-permute-done.3.refs_4_ = bf16[96,640]{1,0:T(8,128)(2,1)S(1)} collective-permute-done((bf16[96,640]{1,0:T(8,128)(2,1)S(1)}, bf16[96,640]{1,0:T(8,128)(2,1)S(1)}, u32[]{:S(2)}, u32[]{:S(2)}) %collective-permute-start.3) | collective-permute-done | bytes 122912 | tf_op jit(solution)/shard_map/ppermute | solution.py:91
  26.8 1.2 %collective-permute-done.9.refs_3_ = bf16[96,640]{1,0:T(8,128)(2,1)S(1)} collective-permute-done((bf16[96,640]{1,0:T(8,128)(2,1)S(1)}, bf16[96,640]{1,0:T(8,128)(2,1)S(1)}, u32[]{:S(2)}, u32[]{:S(2)}) %collective-permute-start.9) | collective-permute-done | bytes 122912 | tf_op jit(solution)/shard_map/ppermute | solution.py:91
  28.0 4.6 %shard_map.39 = (f32[5,8,96,128]{3,2,1,0:T(8,128)S(1)}, f32[5,8,96,128]{3,2,1,0:T(8,128)S(1)}, f32[5,8,96,128]{3,2,1,0:T(8,128)S(1)}) custom-call(s32[5]{0:T(128)S(1)} %stack.23.at_ref, bf16[8,96,640]{2,1,0:T(8,128)(2,1)S(1)} %shard_map.37.rows_ref, bf16[96,640]{1,0:T(8,128)(2,1)S(1)} %get-tuple-element.10.refs_0_, ...), custom_call_target="tpu_custom_call" | custom-call | flops 1321205760 | tf_op jit(solution)/shard_map/pallas_call | solution.py:243
  32.6 2.0 %shard_map.40 = bf16[384,640]{1,0:T(8,128)(2,1)S(1)} custom-call(s32[5]{0:T(128)S(1)} %stack.23.at_ref, bf16[8,96,640]{2,1,0:T(8,128)(2,1)S(1)} %shard_map.37.rows_ref, f32[5,8,96,128]{3,2,1,0:T(8,128)S(1)} %get-tuple-element.12.mixed_ref, f32[5,8,96,128]{3,2,1,0:T(8,128)S(1)} %get-tuple-element.13.sum_ref, f32[5,8,96,128]{3,2,1,0:T(8,128)S(1)} %get-tuple-element.14.top_ref, ...), custom_call_target="tpu_custom_call" | custom-call | flops 314572800 | tf_op jit(solution)/shard_map/pallas_call | solution.py:243
  34.6 3.2 %collective-permute-start.21 = (bf16[2,192,640]{2,1,0:T(8,128)(2,1)S(1)}, bf16[2,192,640]{2,1,0:T(8,128)(2,1)S(1)}, u32[]{:S(2)}, u32[]{:S(2)}) collective-permute-start(bf16[2,192,640]{2,1,0:T(8,128)(2,1)S(1)} %bitcast.16), channel_id=1, source_target_pairs={{0,1},{1,0},{2,3},{3,2},{4,5},{5,4},{6,7},{7,6},{8,9},{9,8},{10,11... | collective-permute-start | bytes 1474568 | tf_op jit(solution)/shard_map/ppermute | solution.py:288
  37.8 1.3 %shard_map.41 = f32[192,640]{1,0:T(8,128)S(1)} custom-call(s32[5]{0:T(128)S(1)} %stack.23.at_ref, bf16[8,96,640]{2,1,0:T(8,128)(2,1)S(1)} %shard_map.37.rows_ref, f32[5,8,96,128]{3,2,1,0:T(8,128)S(1)} %get-tuple-element.12.mixed_ref, f32[5,8,96,128]{3,2,1,0:T(8,128)S(1)} %get-tuple-element.13.sum_ref, f32[5,8,96,128]{3,2,1,0:T(8,128)S(1)} %get-tuple-element.14.top_ref, ...), custom_call_target="tpu_custom_call" | custom-call | flops 314572800 | tf_op jit(solution)/shard_map/pallas_call | solution.py:243
  39.6 1.2 %collective-permute-start.22 = (bf16[96,640]{1,0:T(8,128)(2,1)S(1)}, bf16[96,640]{1,0:T(8,128)(2,1)S(1)}, u32[]{:S(2)}, u32[]{:S(2)}) collective-permute-start(bf16[96,640]{1,0:T(8,128)(2,1)S(1)} %get-tuple-element.16.refs_0_), channel_id=1, source_target_pairs={{0,2},{1,3},{2,0},{3,1},{4,6},{5,7},{6,4},{7,5},{8,10},{9,11},{10,... | collective-permute-start | bytes 368648 | tf_op jit(solution)/shard_map/ppermute | solution.py:292
  40.8 1.4 %shard_map.42.kept_ref = f32[192,640]{1,0:T(8,128)S(1)} custom-call(s32[5]{0:T(128)S(1)} %stack.23.at_ref, bf16[8,96,640]{2,1,0:T(8,128)(2,1)S(1)} %shard_map.37.rows_ref, f32[5,8,96,128]{3,2,1,0:T(8,128)S(1)} %get-tuple-element.12.mixed_ref, f32[5,8,96,128]{3,2,1,0:T(8,128)S(1)} %get-tuple-element.13.sum_ref, ...), custom_call_target="tpu_custom_call" | custom-call | flops 314572800 | tf_op jit(solution)/shard_map/pallas_call | solution.py:243
  42.2 1.7 %collective-permute-done.24.from_x_ref = bf16[96,640]{1,0:T(8,128)(2,1)S(1)} collective-permute-done((bf16[96,640]{1,0:T(8,128)(2,1)S(1)}, bf16[96,640]{1,0:T(8,128)(2,1)S(1)}, u32[]{:S(2)}, u32[]{:S(2)}) %collective-permute-start.24) | collective-permute-done | bytes 122912 | tf_op jit(solution)/shard_map/ppermute | solution.py:292
  43.9 3.5 %collective-permute-start.25 = (bf16[96,640]{1,0:T(8,128)(2,1)S(1)}, bf16[96,640]{1,0:T(8,128)(2,1)S(1)}, u32[]{:S(2)}, u32[]{:S(2)}) collective-permute-start(bf16[96,640]{1,0:T(8,128)(2,1)S(1)} %shard_map.44), channel_id=1, source_target_pairs={{0,8},{1,12},{2,0},{3,4},{4,24},{5,28},{6,16},{7,20},{8,25},{9,29}... | collective-permute-start | bytes 368648 | tf_op jit(solution)/shard_map/ppermute | solution.py:304
  47.4 3.3 %collective-permute-start.23 = (bf16[96,640]{1,0:T(8,128)(2,1)S(1)}, bf16[96,640]{1,0:T(8,128)(2,1)S(1)}, u32[]{:S(2)}, u32[]{:S(2)}) collective-permute-start(bf16[96,640]{1,0:T(8,128)(2,1)S(1)} %shard_map.43), channel_id=1, source_target_pairs={{0,24},{1,28},{2,16},{3,20},{4,8},{5,12},{6,0},{7,4},{8,1},{9,5},{... | collective-permute-start | bytes 368648 | tf_op jit(solution)/shard_map/ppermute | solution.py:304
  50.8 1.8 %collective-permute-done.25 = bf16[96,640]{1,0:T(8,128)(2,1)S(1)} collective-permute-done((bf16[96,640]{1,0:T(8,128)(2,1)S(1)}, bf16[96,640]{1,0:T(8,128)(2,1)S(1)}, u32[]{:S(2)}, u32[]{:S(2)}) %collective-permute-start.25) | collective-permute-done | bytes 122912 | tf_op jit(solution)/shard_map/ppermute | solution.py:304
  52.6 3.2 %collective-permute-done.23 = bf16[96,640]{1,0:T(8,128)(2,1)S(1)} collective-permute-done((bf16[96,640]{1,0:T(8,128)(2,1)S(1)}, bf16[96,640]{1,0:T(8,128)(2,1)S(1)}, u32[]{:S(2)}, u32[]{:S(2)}) %collective-permute-start.23) | collective-permute-done | bytes 122912 | tf_op jit(solution)/shard_map/ppermute | solution.py:304
  (46 shorter events, 13.0 us)
Async XLA Ops:
  0.0 5.3 %collective-permute-start = (bf16[96,640]{1,0:T(8,128)(2,1)}, bf16[96,640]{1,0:T(8,128)(2,1)S(1)}, u32[]{:S(2)}, u32[]{:S(2)}) collective-permute-start(bf16[96,640]{1,0:T(8,128)(2,1)} %refs_0_.1), channel_id=1, source_target_pairs={{0,8},{1,5},{2,10},{3,7},{8,16},{9,1},{10,18},{11,3},{16,24},{17,9... | collective-permute-start | bytes 368648 | tf_op jit(solution)/shard_map/ppermute | solution.py:91
  1.2 5.4 %collective-permute-start.4 = (bf16[96,640]{1,0:T(8,128)(2,1)}, bf16[96,640]{1,0:T(8,128)(2,1)S(1)}, u32[]{:S(2)}, u32[]{:S(2)}) collective-permute-start(bf16[96,640]{1,0:T(8,128)(2,1)} %refs_0_.1), channel_id=1, source_target_pairs={{0,4},{1,9},{2,6},{3,11},{8,0},{9,17},{10,2},{11,19},{16,8},{17,25... | collective-permute-start | bytes 368648 | tf_op jit(solution)/shard_map/ppermute | solution.py:91
  2.4 5.6 %collective-permute-start.10 = (bf16[96,640]{1,0:T(8,128)(2,1)S(1)}, bf16[96,640]{1,0:T(8,128)(2,1)S(1)}, u32[]{:S(2)}, u32[]{:S(2)}) collective-permute-start(bf16[96,640]{1,0:T(8,128)(2,1)S(1)} %get-tuple-element.10.refs_0_), channel_id=1, source_target_pairs={{0,4},{1,9},{2,6},{3,11},{8,0},{9,17},{10,2},{11,19},{16,8},{17,25... | collective-permute-start | bytes 368648 | tf_op jit(solution)/shard_map/ppermute | solution.py:91
  3.8 5.3 %collective-permute-start.13 = (bf16[96,640]{1,0:T(8,128)(2,1)S(1)}, bf16[96,640]{1,0:T(8,128)(2,1)S(1)}, u32[]{:S(2)}, u32[]{:S(2)}) collective-permute-start(bf16[96,640]{1,0:T(8,128)(2,1)S(1)} %get-tuple-element.11.refs_7_), channel_id=1, source_target_pairs={{0,8},{1,5},{2,10},{3,7},{8,16},{9,1},{10,18},{11,3},{16,24},{17,9... | collective-permute-start | bytes 368648 | tf_op jit(solution)/shard_map/ppermute | solution.py:91
  4.0 6.5 %collective-permute-start.16 = (bf16[96,640]{1,0:T(8,128)(2,1)S(1)}, bf16[96,640]{1,0:T(8,128)(2,1)S(1)}, u32[]{:S(2)}, u32[]{:S(2)}) collective-permute-start(bf16[96,640]{1,0:T(8,128)(2,1)S(1)} %get-tuple-element.11.refs_7_), channel_id=1, source_target_pairs={{0,4},{1,9},{2,6},{3,11},{8,0},{9,17},{10,2},{11,19},{16,8},{17,25... | collective-permute-start | bytes 368648 | tf_op jit(solution)/shard_map/ppermute | solution.py:91
  5.3 6.5 %collective-permute-start.7 = (bf16[96,640]{1,0:T(8,128)(2,1)S(1)}, bf16[96,640]{1,0:T(8,128)(2,1)S(1)}, u32[]{:S(2)}, u32[]{:S(2)}) collective-permute-start(bf16[96,640]{1,0:T(8,128)(2,1)S(1)} %get-tuple-element.10.refs_0_), channel_id=1, source_target_pairs={{0,8},{1,5},{2,10},{3,7},{8,16},{9,1},{10,18},{11,3},{16,24},{17,9... | collective-permute-start | bytes 368648 | tf_op jit(solution)/shard_map/ppermute | solution.py:91
  6.7 6.8 %collective-permute-start.1 = (bf16[96,640]{1,0:T(8,128)(2,1)S(1)}, bf16[96,640]{1,0:T(8,128)(2,1)S(1)}, u32[]{:S(2)}, u32[]{:S(2)}) collective-permute-start(bf16[96,640]{1,0:T(8,128)(2,1)S(1)} %collective-permute-done.refs_1_), channel_id=1, source_target_pairs={{0,8},{1,5},{2,10},{3,7},{8,16},{9,1},{10,18},{11,3},{16,24},{17,9... | collective-permute-start | bytes 368648 | tf_op jit(solution)/shard_map/ppermute | solution.py:91
  8.0 5.7 %collective-permute-start.5 = (bf16[96,640]{1,0:T(8,128)(2,1)S(1)}, bf16[96,640]{1,0:T(8,128)(2,1)S(1)}, u32[]{:S(2)}, u32[]{:S(2)}) collective-permute-start(bf16[96,640]{1,0:T(8,128)(2,1)S(1)} %collective-permute-done.4.refs_7_), channel_id=1, source_target_pairs={{0,4},{1,9},{2,6},{3,11},{8,0},{9,17},{10,2},{11,19},{16,8},{17,25... | collective-permute-start | bytes 368648 | tf_op jit(solution)/shard_map/ppermute | solution.py:91
  9.1 6.8 %collective-permute-start.11 = (bf16[96,640]{1,0:T(8,128)(2,1)S(1)}, bf16[96,640]{1,0:T(8,128)(2,1)S(1)}, u32[]{:S(2)}, u32[]{:S(2)}) collective-permute-start(bf16[96,640]{1,0:T(8,128)(2,1)S(1)} %collective-permute-done.10.refs_6_), channel_id=1, source_target_pairs={{0,4},{1,9},{2,6},{3,11},{8,0},{9,17},{10,2},{11,19},{16,8},{17,25... | collective-permute-start | bytes 368648 | tf_op jit(solution)/shard_map/ppermute | solution.py:91
  10.4 5.9 %collective-permute-start.14 = (bf16[96,640]{1,0:T(8,128)(2,1)S(1)}, bf16[96,640]{1,0:T(8,128)(2,1)S(1)}, u32[]{:S(2)}, u32[]{:S(2)}) collective-permute-start(bf16[96,640]{1,0:T(8,128)(2,1)S(1)} %collective-permute-done.13.refs_8_), channel_id=1, source_target_pairs={{0,8},{1,5},{2,10},{3,7},{8,16},{9,1},{10,18},{11,3},{16,24},{17,9... | collective-permute-start | bytes 368648 | tf_op jit(solution)/shard_map/ppermute | solution.py:91
  11.7 6.4 %collective-permute-start.17 = (bf16[96,640]{1,0:T(8,128)(2,1)S(1)}, bf16[96,640]{1,0:T(8,128)(2,1)S(1)}, u32[]{:S(2)}, u32[]{:S(2)}) collective-permute-start(bf16[96,640]{1,0:T(8,128)(2,1)S(1)} %collective-permute-done.16.refs_13_), channel_id=1, source_target_pairs={{0,4},{1,9},{2,6},{3,11},{8,0},{9,17},{10,2},{11,19},{16,8},{17,25... | collective-permute-start | bytes 368648 | tf_op jit(solution)/shard_map/ppermute | solution.py:91
  13.5 5.8 %collective-permute-start.2 = (bf16[96,640]{1,0:T(8,128)(2,1)S(1)}, bf16[96,640]{1,0:T(8,128)(2,1)S(1)}, u32[]{:S(2)}, u32[]{:S(2)}) collective-permute-start(bf16[96,640]{1,0:T(8,128)(2,1)S(1)} %collective-permute-done.1.refs_2_), channel_id=1, source_target_pairs={{0,8},{1,5},{2,10},{3,7},{8,16},{9,1},{10,18},{11,3},{16,24},{17,9... | collective-permute-start | bytes 368648 | tf_op jit(solution)/shard_map/ppermute | solution.py:91
  13.7 7.7 %collective-permute-start.8 = (bf16[96,640]{1,0:T(8,128)(2,1)S(1)}, bf16[96,640]{1,0:T(8,128)(2,1)S(1)}, u32[]{:S(2)}, u32[]{:S(2)}) collective-permute-start(bf16[96,640]{1,0:T(8,128)(2,1)S(1)} %collective-permute-done.7.refs_1_), channel_id=1, source_target_pairs={{0,8},{1,5},{2,10},{3,7},{8,16},{9,1},{10,18},{11,3},{16,24},{17,9... | collective-permute-start | bytes 368648 | tf_op jit(solution)/shard_map/ppermute | solution.py:91
  15.9 6.8 %collective-permute-start.6 = (bf16[96,640]{1,0:T(8,128)(2,1)S(1)}, bf16[96,640]{1,0:T(8,128)(2,1)S(1)}, u32[]{:S(2)}, u32[]{:S(2)}) collective-permute-start(bf16[96,640]{1,0:T(8,128)(2,1)S(1)} %collective-permute-done.5.refs_6_), channel_id=1, source_target_pairs={{0,4},{1,9},{2,6},{3,11},{8,0},{9,17},{10,2},{11,19},{16,8},{17,25... | collective-permute-start | bytes 368648 | tf_op jit(solution)/shard_map/ppermute | solution.py:91
  16.3 6.9 %collective-permute-start.12 = (bf16[96,640]{1,0:T(8,128)(2,1)S(1)}, bf16[96,640]{1,0:T(8,128)(2,1)S(1)}, u32[]{:S(2)}, u32[]{:S(2)}) collective-permute-start(bf16[96,640]{1,0:T(8,128)(2,1)S(1)} %collective-permute-done.11.refs_5_), channel_id=1, source_target_pairs={{0,4},{1,9},{2,6},{3,11},{8,0},{9,17},{10,2},{11,19},{16,8},{17,25... | collective-permute-start | bytes 368648 | tf_op jit(solution)/shard_map/ppermute | solution.py:91
  18.1 6.2 %collective-permute-start.15 = (bf16[96,640]{1,0:T(8,128)(2,1)S(1)}, bf16[96,640]{1,0:T(8,128)(2,1)S(1)}, u32[]{:S(2)}, u32[]{:S(2)}) collective-permute-start(bf16[96,640]{1,0:T(8,128)(2,1)S(1)} %collective-permute-done.14.refs_9_), channel_id=1, source_target_pairs={{0,8},{1,5},{2,10},{3,7},{8,16},{9,1},{10,18},{11,3},{16,24},{17,9... | collective-permute-start | bytes 368648 | tf_op jit(solution)/shard_map/ppermute | solution.py:91
  19.3 6.5 %collective-permute-start.3 = (bf16[96,640]{1,0:T(8,128)(2,1)S(1)}, bf16[96,640]{1,0:T(8,128)(2,1)S(1)}, u32[]{:S(2)}, u32[]{:S(2)}) collective-permute-start(bf16[96,640]{1,0:T(8,128)(2,1)S(1)} %collective-permute-done.2.refs_3_), channel_id=1, source_target_pairs={{0,8},{1,5},{2,10},{3,7},{8,16},{9,1},{10,18},{11,3},{16,24},{17,9... | collective-permute-start | bytes 368648 | tf_op jit(solution)/shard_map/ppermute | solution.py:91
  21.4 5.4 %collective-permute-start.18 = (bf16[96,640]{1,0:T(8,128)(2,1)S(1)}, bf16[96,640]{1,0:T(8,128)(2,1)S(1)}, u32[]{:S(2)}, u32[]{:S(2)}) collective-permute-start(bf16[96,640]{1,0:T(8,128)(2,1)S(1)} %collective-permute-done.17.refs_12_), channel_id=1, source_target_pairs={{0,4},{1,9},{2,6},{3,11},{8,0},{9,17},{10,2},{11,19},{16,8},{17,25... | collective-permute-start | bytes 368648 | tf_op jit(solution)/shard_map/ppermute | solution.py:91
  22.7 5.3 %collective-permute-start.9 = (bf16[96,640]{1,0:T(8,128)(2,1)S(1)}, bf16[96,640]{1,0:T(8,128)(2,1)S(1)}, u32[]{:S(2)}, u32[]{:S(2)}) collective-permute-start(bf16[96,640]{1,0:T(8,128)(2,1)S(1)} %collective-permute-done.8.refs_2_), channel_id=1, source_target_pairs={{0,8},{1,5},{2,10},{3,7},{8,16},{9,1},{10,18},{11,3},{16,24},{17,9... | collective-permute-start | bytes 368648 | tf_op jit(solution)/shard_map/ppermute | solution.py:91
  23.2 9.4 %collective-permute-start.19 = (bf16[96,640]{1,0:T(8,128)(2,1)S(1)}, bf16[96,640]{1,0:T(8,128)(2,1)S(1)}, u32[]{:S(2)}, u32[]{:S(2)}) collective-permute-start(bf16[96,640]{1,0:T(8,128)(2,1)S(1)} %collective-permute-done.12.refs_4_), channel_id=1, source_target_pairs={{0,4},{1,9},{2,6},{3,11},{8,0},{9,17},{10,2},{11,19},{16,8},{17,25... | collective-permute-start | bytes 368648 | tf_op jit(solution)/shard_map/ppermute | solution.py:91
  24.3 8.3 %collective-permute-start.20 = (bf16[96,640]{1,0:T(8,128)(2,1)S(1)}, bf16[96,640]{1,0:T(8,128)(2,1)S(1)}, u32[]{:S(2)}, u32[]{:S(2)}) collective-permute-start(bf16[96,640]{1,0:T(8,128)(2,1)S(1)} %collective-permute-done.15.refs_10_), channel_id=1, source_target_pairs={{0,8},{1,5},{2,10},{3,7},{8,16},{9,1},{10,18},{11,3},{16,24},{17,9... | collective-permute-start | bytes 368648 | tf_op jit(solution)/shard_map/ppermute | solution.py:91
  39.6 7.8 %collective-permute-start.22 = (bf16[96,640]{1,0:T(8,128)(2,1)S(1)}, bf16[96,640]{1,0:T(8,128)(2,1)S(1)}, u32[]{:S(2)}, u32[]{:S(2)}) collective-permute-start(bf16[96,640]{1,0:T(8,128)(2,1)S(1)} %get-tuple-element.16.refs_0_), channel_id=1, source_target_pairs={{0,2},{1,3},{2,0},{3,1},{4,6},{5,7},{6,4},{7,5},{8,10},{9,11},{10,... | collective-permute-start | bytes 368648 | tf_op jit(solution)/shard_map/ppermute | solution.py:292
  43.9 8.6 %collective-permute-start.25 = (bf16[96,640]{1,0:T(8,128)(2,1)S(1)}, bf16[96,640]{1,0:T(8,128)(2,1)S(1)}, u32[]{:S(2)}, u32[]{:S(2)}) collective-permute-start(bf16[96,640]{1,0:T(8,128)(2,1)S(1)} %shard_map.44), channel_id=1, source_target_pairs={{0,8},{1,12},{2,0},{3,4},{4,24},{5,28},{6,16},{7,20},{8,25},{9,29}... | collective-permute-start | bytes 368648 | tf_op jit(solution)/shard_map/ppermute | solution.py:304
  47.4 8.3 %collective-permute-start.23 = (bf16[96,640]{1,0:T(8,128)(2,1)S(1)}, bf16[96,640]{1,0:T(8,128)(2,1)S(1)}, u32[]{:S(2)}, u32[]{:S(2)}) collective-permute-start(bf16[96,640]{1,0:T(8,128)(2,1)S(1)} %shard_map.43), channel_id=1, source_target_pairs={{0,24},{1,28},{2,16},{3,20},{4,8},{5,12},{6,0},{7,4},{8,1},{9,5},{... | collective-permute-start | bytes 368648 | tf_op jit(solution)/shard_map/ppermute | solution.py:304
  (5 other events, 16.9 us)

commit v26 on v25

--- a/solution.py
+++ b/solution.py
@@ -172,12 +172,11 @@
     return blocks
 
 
-def ahead(scores, heads):
-    columns = [slice(head * HD, (head + 1) * HD) for head in range(heads)]
-    now = scores(columns[0])
-    for head, cols in enumerate(columns):
-        later = scores(columns[head + 1]) if head + 1 < heads else None
-        yield head, cols, now
+def ahead(scores, units):
+    now = scores(units[0])
+    for unit, following in zip(units, [*units[1:], None]):
+        later = scores(following) if following else None
+        yield unit, now
         now = later
 
 
@@ -194,18 +193,24 @@
 def near_kernel(heads, n, at_ref, rows_ref, *refs):
     near = [d for d in range(n) if d != n // 2]
     key_refs, value_refs, (mixed_ref, sum_ref, top_ref) = refs[: n - 1], refs[n - 1 : -3], refs[-3:]
-    marks = frame_marks(at_ref, range(n), n)
     keys_marks = key_marks(near, ROWS, n)
-
-    def scores(cols):
-        queries = jnp.concatenate([rows_ref[:, :, cols].reshape(n * ROWS, HD), marks], axis=1)
-        return scores_of(queries, jnp.concatenate([rows_of(key_refs, cols, ROWS), keys_marks], axis=1))
-
-    for head, cols, now in ahead(scores, heads):
+    parts = [range(first, first + n // 2) for first in (0, n // 2)]
+    marks = [frame_marks(at_ref, part, n) for part in parts]
+    columns = [slice(head * HD, (head + 1) * HD) for head in range(heads)]
+    units = [(head, i) for head in range(heads) for i in range(2)]
+
+    def scores(unit):
+        head, i = unit
+        cols = columns[head]
+        queries = jnp.concatenate([rows_ref[d, :, cols] for d in parts[i]], axis=0)
+        keys = jnp.concatenate([rows_of(key_refs, cols, ROWS), keys_marks], axis=1)
+        return scores_of(jnp.concatenate([queries, marks[i]], axis=1), keys)
+
+    for (head, i), now in ahead(scores, units):
         weights, top = soften(now)
-        mixed, total = mix(weights, rows_of(value_refs, cols, ROWS))
-        for d in range(n):
-            rows = slice(d * ROWS, (d + 1) * ROWS)
+        mixed, total = mix(weights, rows_of(value_refs, columns[head], ROWS))
+        for r, d in enumerate(parts[i]):
+            rows = slice(r * ROWS, (r + 1) * ROWS)
             mixed_ref[head, d], sum_ref[head, d], top_ref[head, d] = mixed[rows], total[rows], top[rows]
 
 

time: 57 us -> 57 us (level)
  no operation moved by 1% of the time
where the time goes in v26:
time: 57 us; the launch traced here: 56.4 us
  starting transfers between devices  29.4 us (52%)
  waiting for transfers between devices  14.8 us (26%)
  Pallas kernels  9.37 us (16%)
  local copies, waits for them, and re-layouts  1.94 us (3%)
  other arithmetic  0.79 us (1%)
    ppermute x21, starting transfers between devices, hop(): return lax.ppermute(x, ('frames', 'heads'), pairs)  17.9 us
    pallas_call x8, Pallas kernels, call(): pl.pallas_call(kernel, out_shape=[jax.ShapeDtypeStruct(shape, dtype) for...  9.37 us
    ppermute x21, waiting for transfers between devices, hop(): return lax.ppermute(x, ('frames', 'heads'), pairs)  8.01 us
    ppermute x2, starting transfers between devices, on_device_ring(): arrived.append(lax.ppermute(total, ('frames', 'heads'), pairs))  6.8 us
    ppermute x2, waiting for transfers between devices, on_device_ring(): arrived.append(lax.ppermute(total, ('frames', 'heads'), pairs))  4.99 us
    ppermute x1, starting transfers between devices, on_device_ring(): from_core = lax.ppermute(given, 'heads', [(h, h ^ 1) for h in range(4)])  3.17 us
    unnamed x6, local copies, waits for them, and re-layouts  1.85 us
    ppermute x2, waiting for transfers between devices, on_device_ring(): lax.ppermute(block, 'heads', [(h, h ^ 2) for h in range(4)])  1.67 us
  transfers between devices with their start and end apart: 26, of which 15 were waited for; matrix products, arithmetic and copies ran while one was open for 0% of the time, Pallas kernels for 13%

profile of v26, /device:TPU:3, one launch (start us, length us, event | category | flops | bytes accessed | tf_op | source)
XLA Modules:
  0.0 56.4 jit_solution(12012712519987608043)
XLA Ops:
  0.0 1.2 %collective-permute-start = (bf16[96,640]{1,0:T(8,128)(2,1)}, bf16[96,640]{1,0:T(8,128)(2,1)S(1)}, u32[]{:S(2)}, u32[]{:S(2)}) collective-permute-start(bf16[96,640]{1,0:T(8,128)(2,1)} %refs_0_.1), channel_id=1, source_target_pairs={{0,8},{1,5},{2,10},{3,7},{8,16},{9,1},{10,18},{11,3},{16,24},{17,9... | collective-permute-start | bytes 368648 | tf_op jit(solution)/shard_map/ppermute | solution.py:91
  2.4 1.3 %collective-permute-start.10 = (bf16[96,640]{1,0:T(8,128)(2,1)S(1)}, bf16[96,640]{1,0:T(8,128)(2,1)S(1)}, u32[]{:S(2)}, u32[]{:S(2)}) collective-permute-start(bf16[96,640]{1,0:T(8,128)(2,1)S(1)} %get-tuple-element.10.refs_0_), channel_id=1, source_target_pairs={{0,4},{1,9},{2,6},{3,11},{8,0},{9,17},{10,2},{11,19},{16,8},{17,25... | collective-permute-start | bytes 368648 | tf_op jit(solution)/shard_map/ppermute | solution.py:91
  4.0 1.3 %collective-permute-start.16 = (bf16[96,640]{1,0:T(8,128)(2,1)S(1)}, bf16[96,640]{1,0:T(8,128)(2,1)S(1)}, u32[]{:S(2)}, u32[]{:S(2)}) collective-permute-start(bf16[96,640]{1,0:T(8,128)(2,1)S(1)} %get-tuple-element.11.refs_7_), channel_id=1, source_target_pairs={{0,4},{1,9},{2,6},{3,11},{8,0},{9,17},{10,2},{11,19},{16,8},{17,25... | collective-permute-start | bytes 368648 | tf_op jit(solution)/shard_map/ppermute | solution.py:91
  5.5 1.2 %collective-permute-done.4.refs_7_ = bf16[96,640]{1,0:T(8,128)(2,1)S(1)} collective-permute-done((bf16[96,640]{1,0:T(8,128)(2,1)}, bf16[96,640]{1,0:T(8,128)(2,1)S(1)}, u32[]{:S(2)}, u32[]{:S(2)}) %collective-permute-start.4) | collective-permute-done | bytes 122912 | tf_op jit(solution)/shard_map/ppermute | solution.py:91
  9.1 1.3 %collective-permute-start.11 = (bf16[96,640]{1,0:T(8,128)(2,1)S(1)}, bf16[96,640]{1,0:T(8,128)(2,1)S(1)}, u32[]{:S(2)}, u32[]{:S(2)}) collective-permute-start(bf16[96,640]{1,0:T(8,128)(2,1)S(1)} %collective-permute-done.10.refs_6_), channel_id=1, source_target_pairs={{0,4},{1,9},{2,6},{3,11},{8,0},{9,17},{10,2},{11,19},{16,8},{17,25... | collective-permute-start | bytes 368648 | tf_op jit(solution)/shard_map/ppermute | solution.py:91
  11.7 1.3 %collective-permute-start.17 = (bf16[96,640]{1,0:T(8,128)(2,1)S(1)}, bf16[96,640]{1,0:T(8,128)(2,1)S(1)}, u32[]{:S(2)}, u32[]{:S(2)}) collective-permute-start(bf16[96,640]{1,0:T(8,128)(2,1)S(1)} %collective-permute-done.16.refs_13_), channel_id=1, source_target_pairs={{0,4},{1,9},{2,6},{3,11},{8,0},{9,17},{10,2},{11,19},{16,8},{17,25... | collective-permute-start | bytes 368648 | tf_op jit(solution)/shard_map/ppermute | solution.py:91
  13.7 1.2 %collective-permute-start.8 = (bf16[96,640]{1,0:T(8,128)(2,1)S(1)}, bf16[96,640]{1,0:T(8,128)(2,1)S(1)}, u32[]{:S(2)}, u32[]{:S(2)}) collective-permute-start(bf16[96,640]{1,0:T(8,128)(2,1)S(1)} %collective-permute-done.7.refs_1_), channel_id=1, source_target_pairs={{0,8},{1,5},{2,10},{3,7},{8,16},{9,1},{10,18},{11,3},{16,24},{17,9... | collective-permute-start | bytes 368648 | tf_op jit(solution)/shard_map/ppermute | solution.py:91
  16.3 1.3 %collective-permute-start.12 = (bf16[96,640]{1,0:T(8,128)(2,1)S(1)}, bf16[96,640]{1,0:T(8,128)(2,1)S(1)}, u32[]{:S(2)}, u32[]{:S(2)}) collective-permute-start(bf16[96,640]{1,0:T(8,128)(2,1)S(1)} %collective-permute-done.11.refs_5_), channel_id=1, source_target_pairs={{0,4},{1,9},{2,6},{3,11},{8,0},{9,17},{10,2},{11,19},{16,8},{17,25... | collective-permute-start | bytes 368648 | tf_op jit(solution)/shard_map/ppermute | solution.py:91
  18.1 1.2 %collective-permute-start.15 = (bf16[96,640]{1,0:T(8,128)(2,1)S(1)}, bf16[96,640]{1,0:T(8,128)(2,1)S(1)}, u32[]{:S(2)}, u32[]{:S(2)}) collective-permute-start(bf16[96,640]{1,0:T(8,128)(2,1)S(1)} %collective-permute-done.14.refs_9_), channel_id=1, source_target_pairs={{0,8},{1,5},{2,10},{3,7},{8,16},{9,1},{10,18},{11,3},{16,24},{17,9... | collective-permute-start | bytes 368648 | tf_op jit(solution)/shard_map/ppermute | solution.py:91
  19.3 1.3 %collective-permute-start.3 = (bf16[96,640]{1,0:T(8,128)(2,1)S(1)}, bf16[96,640]{1,0:T(8,128)(2,1)S(1)}, u32[]{:S(2)}, u32[]{:S(2)}) collective-permute-start(bf16[96,640]{1,0:T(8,128)(2,1)S(1)} %collective-permute-done.2.refs_3_), channel_id=1, source_target_pairs={{0,8},{1,5},{2,10},{3,7},{8,16},{9,1},{10,18},{11,3},{16,24},{17,9... | collective-permute-start | bytes 368648 | tf_op jit(solution)/shard_map/ppermute | solution.py:91
  21.4 1.3 %collective-permute-start.18 = (bf16[96,640]{1,0:T(8,128)(2,1)S(1)}, bf16[96,640]{1,0:T(8,128)(2,1)S(1)}, u32[]{:S(2)}, u32[]{:S(2)}) collective-permute-start(bf16[96,640]{1,0:T(8,128)(2,1)S(1)} %collective-permute-done.17.refs_12_), channel_id=1, source_target_pairs={{0,4},{1,9},{2,6},{3,11},{8,0},{9,17},{10,2},{11,19},{16,8},{17,25... | collective-permute-start | bytes 368648 | tf_op jit(solution)/shard_map/ppermute | solution.py:91
  24.7 1.2 %collective-permute-done.3.refs_4_ = bf16[96,640]{1,0:T(8,128)(2,1)S(1)} collective-permute-done((bf16[96,640]{1,0:T(8,128)(2,1)S(1)}, bf16[96,640]{1,0:T(8,128)(2,1)S(1)}, u32[]{:S(2)}, u32[]{:S(2)}) %collective-permute-start.3) | collective-permute-done | bytes 122912 | tf_op jit(solution)/shard_map/ppermute | solution.py:91
  26.8 1.2 %collective-permute-done.9.refs_3_ = bf16[96,640]{1,0:T(8,128)(2,1)S(1)} collective-permute-done((bf16[96,640]{1,0:T(8,128)(2,1)S(1)}, bf16[96,640]{1,0:T(8,128)(2,1)S(1)}, u32[]{:S(2)}, u32[]{:S(2)}) %collective-permute-start.9) | collective-permute-done | bytes 122912 | tf_op jit(solution)/shard_map/ppermute | solution.py:91
  28.0 4.5 %shard_map.39 = (f32[5,8,96,128]{3,2,1,0:T(8,128)S(1)}, f32[5,8,96,128]{3,2,1,0:T(8,128)S(1)}, f32[5,8,96,128]{3,2,1,0:T(8,128)S(1)}) custom-call(s32[5]{0:T(128)S(1)} %stack.23.at_ref, bf16[8,96,640]{2,1,0:T(8,128)(2,1)S(1)} %shard_map.37.rows_ref, bf16[96,640]{1,0:T(8,128)(2,1)S(1)} %get-tuple-element.10.refs_0_, ...), custom_call_target="tpu_custom_call" | custom-call | flops 1321205760 | tf_op jit(solution)/shard_map/pallas_call | solution.py:248
  32.6 2.0 %shard_map.40 = bf16[384,640]{1,0:T(8,128)(2,1)S(1)} custom-call(s32[5]{0:T(128)S(1)} %stack.23.at_ref, bf16[8,96,640]{2,1,0:T(8,128)(2,1)S(1)} %shard_map.37.rows_ref, f32[5,8,96,128]{3,2,1,0:T(8,128)S(1)} %get-tuple-element.12.mixed_ref, f32[5,8,96,128]{3,2,1,0:T(8,128)S(1)} %get-tuple-element.13.sum_ref, f32[5,8,96,128]{3,2,1,0:T(8,128)S(1)} %get-tuple-element.14.top_ref, ...), custom_call_target="tpu_custom_call" | custom-call | flops 314572800 | tf_op jit(solution)/shard_map/pallas_call | solution.py:248
  34.5 3.2 %collective-permute-start.21 = (bf16[2,192,640]{2,1,0:T(8,128)(2,1)S(1)}, bf16[2,192,640]{2,1,0:T(8,128)(2,1)S(1)}, u32[]{:S(2)}, u32[]{:S(2)}) collective-permute-start(bf16[2,192,640]{2,1,0:T(8,128)(2,1)S(1)} %bitcast.16), channel_id=1, source_target_pairs={{0,1},{1,0},{2,3},{3,2},{4,5},{5,4},{6,7},{7,6},{8,9},{9,8},{10,11... | collective-permute-start | bytes 1474568 | tf_op jit(solution)/shard_map/ppermute | solution.py:293
  37.7 1.4 %shard_map.41 = f32[192,640]{1,0:T(8,128)S(1)} custom-call(s32[5]{0:T(128)S(1)} %stack.23.at_ref, bf16[8,96,640]{2,1,0:T(8,128)(2,1)S(1)} %shard_map.37.rows_ref, f32[5,8,96,128]{3,2,1,0:T(8,128)S(1)} %get-tuple-element.12.mixed_ref, f32[5,8,96,128]{3,2,1,0:T(8,128)S(1)} %get-tuple-element.13.sum_ref, f32[5,8,96,128]{3,2,1,0:T(8,128)S(1)} %get-tuple-element.14.top_ref, ...), custom_call_target="tpu_custom_call" | custom-call | flops 314572800 | tf_op jit(solution)/shard_map/pallas_call | solution.py:248
  39.6 1.2 %collective-permute-start.22 = (bf16[96,640]{1,0:T(8,128)(2,1)S(1)}, bf16[96,640]{1,0:T(8,128)(2,1)S(1)}, u32[]{:S(2)}, u32[]{:S(2)}) collective-permute-start(bf16[96,640]{1,0:T(8,128)(2,1)S(1)} %get-tuple-element.16.refs_0_), channel_id=1, source_target_pairs={{0,2},{1,3},{2,0},{3,1},{4,6},{5,7},{6,4},{7,5},{8,10},{9,11},{10,... | collective-permute-start | bytes 368648 | tf_op jit(solution)/shard_map/ppermute | solution.py:297
  40.8 1.4 %shard_map.42.kept_ref = f32[192,640]{1,0:T(8,128)S(1)} custom-call(s32[5]{0:T(128)S(1)} %stack.23.at_ref, bf16[8,96,640]{2,1,0:T(8,128)(2,1)S(1)} %shard_map.37.rows_ref, f32[5,8,96,128]{3,2,1,0:T(8,128)S(1)} %get-tuple-element.12.mixed_ref, f32[5,8,96,128]{3,2,1,0:T(8,128)S(1)} %get-tuple-element.13.sum_ref, ...), custom_call_target="tpu_custom_call" | custom-call | flops 314572800 | tf_op jit(solution)/shard_map/pallas_call | solution.py:248
  42.1 1.7 %collective-permute-done.24.from_x_ref = bf16[96,640]{1,0:T(8,128)(2,1)S(1)} collective-permute-done((bf16[96,640]{1,0:T(8,128)(2,1)S(1)}, bf16[96,640]{1,0:T(8,128)(2,1)S(1)}, u32[]{:S(2)}, u32[]{:S(2)}) %collective-permute-start.24) | collective-permute-done | bytes 122912 | tf_op jit(solution)/shard_map/ppermute | solution.py:297
  43.9 3.5 %collective-permute-start.25 = (bf16[96,640]{1,0:T(8,128)(2,1)S(1)}, bf16[96,640]{1,0:T(8,128)(2,1)S(1)}, u32[]{:S(2)}, u32[]{:S(2)}) collective-permute-start(bf16[96,640]{1,0:T(8,128)(2,1)S(1)} %shard_map.44), channel_id=1, source_target_pairs={{0,8},{1,12},{2,0},{3,4},{4,24},{5,28},{6,16},{7,20},{8,25},{9,29}... | collective-permute-start | bytes 368648 | tf_op jit(solution)/shard_map/ppermute | solution.py:309
  47.4 3.3 %collective-permute-start.23 = (bf16[96,640]{1,0:T(8,128)(2,1)S(1)}, bf16[96,640]{1,0:T(8,128)(2,1)S(1)}, u32[]{:S(2)}, u32[]{:S(2)}) collective-permute-start(bf16[96,640]{1,0:T(8,128)(2,1)S(1)} %shard_map.43), channel_id=1, source_target_pairs={{0,24},{1,28},{2,16},{3,20},{4,8},{5,12},{6,0},{7,4},{8,1},{9,5},{... | collective-permute-start | bytes 368648 | tf_op jit(solution)/shard_map/ppermute | solution.py:309
  50.7 1.8 %collective-permute-done.25 = bf16[96,640]{1,0:T(8,128)(2,1)S(1)} collective-permute-done((bf16[96,640]{1,0:T(8,128)(2,1)S(1)}, bf16[96,640]{1,0:T(8,128)(2,1)S(1)}, u32[]{:S(2)}, u32[]{:S(2)}) %collective-permute-start.25) | collective-permute-done | bytes 122912 | tf_op jit(solution)/shard_map/ppermute | solution.py:309
  52.5 3.2 %collective-permute-done.23 = bf16[96,640]{1,0:T(8,128)(2,1)S(1)} collective-permute-done((bf16[96,640]{1,0:T(8,128)(2,1)S(1)}, bf16[96,640]{1,0:T(8,128)(2,1)S(1)}, u32[]{:S(2)}, u32[]{:S(2)}) %collective-permute-start.23) | collective-permute-done | bytes 122912 | tf_op jit(solution)/shard_map/ppermute | solution.py:309
  (46 shorter events, 13.0 us)
Async XLA Ops:
  0.0 5.3 %collective-permute-start = (bf16[96,640]{1,0:T(8,128)(2,1)}, bf16[96,640]{1,0:T(8,128)(2,1)S(1)}, u32[]{:S(2)}, u32[]{:S(2)}) collective-permute-start(bf16[96,640]{1,0:T(8,128)(2,1)} %refs_0_.1), channel_id=1, source_target_pairs={{0,8},{1,5},{2,10},{3,7},{8,16},{9,1},{10,18},{11,3},{16,24},{17,9... | collective-permute-start | bytes 368648 | tf_op jit(solution)/shard_map/ppermute | solution.py:91
  1.2 5.4 %collective-permute-start.4 = (bf16[96,640]{1,0:T(8,128)(2,1)}, bf16[96,640]{1,0:T(8,128)(2,1)S(1)}, u32[]{:S(2)}, u32[]{:S(2)}) collective-permute-start(bf16[96,640]{1,0:T(8,128)(2,1)} %refs_0_.1), channel_id=1, source_target_pairs={{0,4},{1,9},{2,6},{3,11},{8,0},{9,17},{10,2},{11,19},{16,8},{17,25... | collective-permute-start | bytes 368648 | tf_op jit(solution)/shard_map/ppermute | solution.py:91
  2.4 5.6 %collective-permute-start.10 = (bf16[96,640]{1,0:T(8,128)(2,1)S(1)}, bf16[96,640]{1,0:T(8,128)(2,1)S(1)}, u32[]{:S(2)}, u32[]{:S(2)}) collective-permute-start(bf16[96,640]{1,0:T(8,128)(2,1)S(1)} %get-tuple-element.10.refs_0_), channel_id=1, source_target_pairs={{0,4},{1,9},{2,6},{3,11},{8,0},{9,17},{10,2},{11,19},{16,8},{17,25... | collective-permute-start | bytes 368648 | tf_op jit(solution)/shard_map/ppermute | solution.py:91
  3.8 5.3 %collective-permute-start.13 = (bf16[96,640]{1,0:T(8,128)(2,1)S(1)}, bf16[96,640]{1,0:T(8,128)(2,1)S(1)}, u32[]{:S(2)}, u32[]{:S(2)}) collective-permute-start(bf16[96,640]{1,0:T(8,128)(2,1)S(1)} %get-tuple-element.11.refs_7_), channel_id=1, source_target_pairs={{0,8},{1,5},{2,10},{3,7},{8,16},{9,1},{10,18},{11,3},{16,24},{17,9... | collective-permute-start | bytes 368648 | tf_op jit(solution)/shard_map/ppermute | solution.py:91
  4.0 6.5 %collective-permute-start.16 = (bf16[96,640]{1,0:T(8,128)(2,1)S(1)}, bf16[96,640]{1,0:T(8,128)(2,1)S(1)}, u32[]{:S(2)}, u32[]{:S(2)}) collective-permute-start(bf16[96,640]{1,0:T(8,128)(2,1)S(1)} %get-tuple-element.11.refs_7_), channel_id=1, source_target_pairs={{0,4},{1,9},{2,6},{3,11},{8,0},{9,17},{10,2},{11,19},{16,8},{17,25... | collective-permute-start | bytes 368648 | tf_op jit(solution)/shard_map/ppermute | solution.py:91
  5.3 6.5 %collective-permute-start.7 = (bf16[96,640]{1,0:T(8,128)(2,1)S(1)}, bf16[96,640]{1,0:T(8,128)(2,1)S(1)}, u32[]{:S(2)}, u32[]{:S(2)}) collective-permute-start(bf16[96,640]{1,0:T(8,128)(2,1)S(1)} %get-tuple-element.10.refs_0_), channel_id=1, source_target_pairs={{0,8},{1,5},{2,10},{3,7},{8,16},{9,1},{10,18},{11,3},{16,24},{17,9... | collective-permute-start | bytes 368648 | tf_op jit(solution)/shard_map/ppermute | solution.py:91
  6.7 6.8 %collective-permute-start.1 = (bf16[96,640]{1,0:T(8,128)(2,1)S(1)}, bf16[96,640]{1,0:T(8,128)(2,1)S(1)}, u32[]{:S(2)}, u32[]{:S(2)}) collective-permute-start(bf16[96,640]{1,0:T(8,128)(2,1)S(1)} %collective-permute-done.refs_1_), channel_id=1, source_target_pairs={{0,8},{1,5},{2,10},{3,7},{8,16},{9,1},{10,18},{11,3},{16,24},{17,9... | collective-permute-start | bytes 368648 | tf_op jit(solution)/shard_map/ppermute | solution.py:91
  8.0 5.7 %collective-permute-start.5 = (bf16[96,640]{1,0:T(8,128)(2,1)S(1)}, bf16[96,640]{1,0:T(8,128)(2,1)S(1)}, u32[]{:S(2)}, u32[]{:S(2)}) collective-permute-start(bf16[96,640]{1,0:T(8,128)(2,1)S(1)} %collective-permute-done.4.refs_7_), channel_id=1, source_target_pairs={{0,4},{1,9},{2,6},{3,11},{8,0},{9,17},{10,2},{11,19},{16,8},{17,25... | collective-permute-start | bytes 368648 | tf_op jit(solution)/shard_map/ppermute | solution.py:91
  9.1 6.8 %collective-permute-start.11 = (bf16[96,640]{1,0:T(8,128)(2,1)S(1)}, bf16[96,640]{1,0:T(8,128)(2,1)S(1)}, u32[]{:S(2)}, u32[]{:S(2)}) collective-permute-start(bf16[96,640]{1,0:T(8,128)(2,1)S(1)} %collective-permute-done.10.refs_6_), channel_id=1, source_target_pairs={{0,4},{1,9},{2,6},{3,11},{8,0},{9,17},{10,2},{11,19},{16,8},{17,25... | collective-permute-start | bytes 368648 | tf_op jit(solution)/shard_map/ppermute | solution.py:91
  10.4 5.9 %collective-permute-start.14 = (bf16[96,640]{1,0:T(8,128)(2,1)S(1)}, bf16[96,640]{1,0:T(8,128)(2,1)S(1)}, u32[]{:S(2)}, u32[]{:S(2)}) collective-permute-start(bf16[96,640]{1,0:T(8,128)(2,1)S(1)} %collective-permute-done.13.refs_8_), channel_id=1, source_target_pairs={{0,8},{1,5},{2,10},{3,7},{8,16},{9,1},{10,18},{11,3},{16,24},{17,9... | collective-permute-start | bytes 368648 | tf_op jit(solution)/shard_map/ppermute | solution.py:91
  11.7 6.4 %collective-permute-start.17 = (bf16[96,640]{1,0:T(8,128)(2,1)S(1)}, bf16[96,640]{1,0:T(8,128)(2,1)S(1)}, u32[]{:S(2)}, u32[]{:S(2)}) collective-permute-start(bf16[96,640]{1,0:T(8,128)(2,1)S(1)} %collective-permute-done.16.refs_13_), channel_id=1, source_target_pairs={{0,4},{1,9},{2,6},{3,11},{8,0},{9,17},{10,2},{11,19},{16,8},{17,25... | collective-permute-start | bytes 368648 | tf_op jit(solution)/shard_map/ppermute | solution.py:91
  13.5 5.8 %collective-permute-start.2 = (bf16[96,640]{1,0:T(8,128)(2,1)S(1)}, bf16[96,640]{1,0:T(8,128)(2,1)S(1)}, u32[]{:S(2)}, u32[]{:S(2)}) collective-permute-start(bf16[96,640]{1,0:T(8,128)(2,1)S(1)} %collective-permute-done.1.refs_2_), channel_id=1, source_target_pairs={{0,8},{1,5},{2,10},{3,7},{8,16},{9,1},{10,18},{11,3},{16,24},{17,9... | collective-permute-start | bytes 368648 | tf_op jit(solution)/shard_map/ppermute | solution.py:91
  13.7 7.7 %collective-permute-start.8 = (bf16[96,640]{1,0:T(8,128)(2,1)S(1)}, bf16[96,640]{1,0:T(8,128)(2,1)S(1)}, u32[]{:S(2)}, u32[]{:S(2)}) collective-permute-start(bf16[96,640]{1,0:T(8,128)(2,1)S(1)} %collective-permute-done.7.refs_1_), channel_id=1, source_target_pairs={{0,8},{1,5},{2,10},{3,7},{8,16},{9,1},{10,18},{11,3},{16,24},{17,9... | collective-permute-start | bytes 368648 | tf_op jit(solution)/shard_map/ppermute | solution.py:91
  15.9 6.8 %collective-permute-start.6 = (bf16[96,640]{1,0:T(8,128)(2,1)S(1)}, bf16[96,640]{1,0:T(8,128)(2,1)S(1)}, u32[]{:S(2)}, u32[]{:S(2)}) collective-permute-start(bf16[96,640]{1,0:T(8,128)(2,1)S(1)} %collective-permute-done.5.refs_6_), channel_id=1, source_target_pairs={{0,4},{1,9},{2,6},{3,11},{8,0},{9,17},{10,2},{11,19},{16,8},{17,25... | collective-permute-start | bytes 368648 | tf_op jit(solution)/shard_map/ppermute | solution.py:91
  16.3 6.9 %collective-permute-start.12 = (bf16[96,640]{1,0:T(8,128)(2,1)S(1)}, bf16[96,640]{1,0:T(8,128)(2,1)S(1)}, u32[]{:S(2)}, u32[]{:S(2)}) collective-permute-start(bf16[96,640]{1,0:T(8,128)(2,1)S(1)} %collective-permute-done.11.refs_5_), channel_id=1, source_target_pairs={{0,4},{1,9},{2,6},{3,11},{8,0},{9,17},{10,2},{11,19},{16,8},{17,25... | collective-permute-start | bytes 368648 | tf_op jit(solution)/shard_map/ppermute | solution.py:91
  18.1 6.2 %collective-permute-start.15 = (bf16[96,640]{1,0:T(8,128)(2,1)S(1)}, bf16[96,640]{1,0:T(8,128)(2,1)S(1)}, u32[]{:S(2)}, u32[]{:S(2)}) collective-permute-start(bf16[96,640]{1,0:T(8,128)(2,1)S(1)} %collective-permute-done.14.refs_9_), channel_id=1, source_target_pairs={{0,8},{1,5},{2,10},{3,7},{8,16},{9,1},{10,18},{11,3},{16,24},{17,9... | collective-permute-start | bytes 368648 | tf_op jit(solution)/shard_map/ppermute | solution.py:91
  19.3 6.5 %collective-permute-start.3 = (bf16[96,640]{1,0:T(8,128)(2,1)S(1)}, bf16[96,640]{1,0:T(8,128)(2,1)S(1)}, u32[]{:S(2)}, u32[]{:S(2)}) collective-permute-start(bf16[96,640]{1,0:T(8,128)(2,1)S(1)} %collective-permute-done.2.refs_3_), channel_id=1, source_target_pairs={{0,8},{1,5},{2,10},{3,7},{8,16},{9,1},{10,18},{11,3},{16,24},{17,9... | collective-permute-start | bytes 368648 | tf_op jit(solution)/shard_map/ppermute | solution.py:91
  21.4 5.4 %collective-permute-start.18 = (bf16[96,640]{1,0:T(8,128)(2,1)S(1)}, bf16[96,640]{1,0:T(8,128)(2,1)S(1)}, u32[]{:S(2)}, u32[]{:S(2)}) collective-permute-start(bf16[96,640]{1,0:T(8,128)(2,1)S(1)} %collective-permute-done.17.refs_12_), channel_id=1, source_target_pairs={{0,4},{1,9},{2,6},{3,11},{8,0},{9,17},{10,2},{11,19},{16,8},{17,25... | collective-permute-start | bytes 368648 | tf_op jit(solution)/shard_map/ppermute | solution.py:91
  22.7 5.3 %collective-permute-start.9 = (bf16[96,640]{1,0:T(8,128)(2,1)S(1)}, bf16[96,640]{1,0:T(8,128)(2,1)S(1)}, u32[]{:S(2)}, u32[]{:S(2)}) collective-permute-start(bf16[96,640]{1,0:T(8,128)(2,1)S(1)} %collective-permute-done.8.refs_2_), channel_id=1, source_target_pairs={{0,8},{1,5},{2,10},{3,7},{8,16},{9,1},{10,18},{11,3},{16,24},{17,9... | collective-permute-start | bytes 368648 | tf_op jit(solution)/shard_map/ppermute | solution.py:91
  23.2 9.3 %collective-permute-start.19 = (bf16[96,640]{1,0:T(8,128)(2,1)S(1)}, bf16[96,640]{1,0:T(8,128)(2,1)S(1)}, u32[]{:S(2)}, u32[]{:S(2)}) collective-permute-start(bf16[96,640]{1,0:T(8,128)(2,1)S(1)} %collective-permute-done.12.refs_4_), channel_id=1, source_target_pairs={{0,4},{1,9},{2,6},{3,11},{8,0},{9,17},{10,2},{11,19},{16,8},{17,25... | collective-permute-start | bytes 368648 | tf_op jit(solution)/shard_map/ppermute | solution.py:91
  24.3 8.3 %collective-permute-start.20 = (bf16[96,640]{1,0:T(8,128)(2,1)S(1)}, bf16[96,640]{1,0:T(8,128)(2,1)S(1)}, u32[]{:S(2)}, u32[]{:S(2)}) collective-permute-start(bf16[96,640]{1,0:T(8,128)(2,1)S(1)} %collective-permute-done.15.refs_10_), channel_id=1, source_target_pairs={{0,8},{1,5},{2,10},{3,7},{8,16},{9,1},{10,18},{11,3},{16,24},{17,9... | collective-permute-start | bytes 368648 | tf_op jit(solution)/shard_map/ppermute | solution.py:91
  39.6 7.8 %collective-permute-start.22 = (bf16[96,640]{1,0:T(8,128)(2,1)S(1)}, bf16[96,640]{1,0:T(8,128)(2,1)S(1)}, u32[]{:S(2)}, u32[]{:S(2)}) collective-permute-start(bf16[96,640]{1,0:T(8,128)(2,1)S(1)} %get-tuple-element.16.refs_0_), channel_id=1, source_target_pairs={{0,2},{1,3},{2,0},{3,1},{4,6},{5,7},{6,4},{7,5},{8,10},{9,11},{10,... | collective-permute-start | bytes 368648 | tf_op jit(solution)/shard_map/ppermute | solution.py:297
  43.9 8.6 %collective-permute-start.25 = (bf16[96,640]{1,0:T(8,128)(2,1)S(1)}, bf16[96,640]{1,0:T(8,128)(2,1)S(1)}, u32[]{:S(2)}, u32[]{:S(2)}) collective-permute-start(bf16[96,640]{1,0:T(8,128)(2,1)S(1)} %shard_map.44), channel_id=1, source_target_pairs={{0,8},{1,12},{2,0},{3,4},{4,24},{5,28},{6,16},{7,20},{8,25},{9,29}... | collective-permute-start | bytes 368648 | tf_op jit(solution)/shard_map/ppermute | solution.py:309
  47.4 8.3 %collective-permute-start.23 = (bf16[96,640]{1,0:T(8,128)(2,1)S(1)}, bf16[96,640]{1,0:T(8,128)(2,1)S(1)}, u32[]{:S(2)}, u32[]{:S(2)}) collective-permute-start(bf16[96,640]{1,0:T(8,128)(2,1)S(1)} %shard_map.43), channel_id=1, source_target_pairs={{0,24},{1,28},{2,16},{3,20},{4,8},{5,12},{6,0},{7,4},{8,1},{9,5},{... | collective-permute-start | bytes 368648 | tf_op jit(solution)/shard_map/ppermute | solution.py:309
  (5 other events, 16.8 us)

commit v27 on v25

--- a/solution.py
+++ b/solution.py
@@ -166,8 +166,9 @@
     z, y, x, core = (at_ref[i] for i in range(1, 5))
     blocks = []
     for slot in range(2):
-        to = look_up(sum(PATTERNS, ()), 4 * ((slot ^ y) + 2 * (x ^ flip_x)) + z)
-        owner = to + (core ^ flip_core) * (n - 1 - 2 * to)
+        row_y = core ^ flip_core
+        to = look_up(sum(PATTERNS, ()), 4 * ((slot ^ y ^ row_y) + 2 * (x ^ flip_x)) + z)
+        owner = to + row_y * (n - 1 - 2 * to)
         blocks.append(ring_distance(at_ref, owner, n))
     return blocks
 
@@ -296,14 +297,14 @@
         pairs = []
         for f in range(n):
             for h in range(4):
-                to = PATTERNS[(slot ^ (f & 1)) + 2 * (h >> 1)][f >> 1]
+                to = PATTERNS[(slot ^ (f & 1) ^ (h & 1)) + 2 * (h >> 1)][f >> 1]
                 pairs.append((4 * f + h, 4 * (2 * to + (h & 1)) + (f >> 1)))
         (total,) = call(
             functools.partial(sum_kernel, part), (), [kept, from_core, from_x[slot]], [((ROWS, cols), bf16)], 0
         )
         arrived.append(lax.ppermute(total, ("frames", "heads"), pairs))
     patterns = [[p[source] for p in PATTERNS].index(to) for source in range(4) for to in range(4)]
-    straight = look_up(patterns, 4 * head + z) & 1 == 0
+    straight = (look_up(patterns, 4 * head + z) ^ y) & 1 == 0
     low, high = arrived
     return jnp.concatenate([jnp.where(straight, low, high), jnp.where(straight, high, low)], axis=1)
 

time: 57 us -> 56.9 us (level)
  no operation moved by 1% of the time
where the time goes in v27:
time: 56.9 us; the launch traced here: 56.8 us
  starting transfers between devices  29.4 us (52%)
  waiting for transfers between devices  15.2 us (27%)
  Pallas kernels  9.42 us (17%)
  local copies, waits for them, and re-layouts  1.94 us (3%)
  other arithmetic  0.79 us (1%)
    ppermute x21, starting transfers between devices, hop(): return lax.ppermute(x, ('frames', 'heads'), pairs)  17.9 us
    pallas_call x8, Pallas kernels, call(): pl.pallas_call(kernel, out_shape=[jax.ShapeDtypeStruct(shape, dtype) for...  9.42 us
    ppermute x21, waiting for transfers between devices, hop(): return lax.ppermute(x, ('frames', 'heads'), pairs)  8.01 us
    ppermute x2, starting transfers between devices, on_device_ring(): arrived.append(lax.ppermute(total, ('frames', 'heads'), pairs))  6.73 us
    ppermute x2, waiting for transfers between devices, on_device_ring(): arrived.append(lax.ppermute(total, ('frames', 'heads'), pairs))  5.33 us
    ppermute x1, starting transfers between devices, on_device_ring(): from_core = lax.ppermute(given, 'heads', [(h, h ^ 1) for h in range(4)])  3.17 us
    unnamed x6, local copies, waits for them, and re-layouts  1.85 us
    ppermute x2, waiting for transfers between devices, on_device_ring(): lax.ppermute(block, 'heads', [(h, h ^ 2) for h in range(4)])  1.68 us
  transfers between devices with their start and end apart: 26, of which 15 were waited for; matrix products, arithmetic and copies ran while one was open for 0% of the time, Pallas kernels for 13%

profile of v27, /device:TPU:3, one launch (start us, length us, event | category | flops | bytes accessed | tf_op | source)
XLA Modules:
  0.0 56.8 jit_solution(6369208868772195045)
XLA Ops:
  0.0 1.2 %collective-permute-start = (bf16[96,640]{1,0:T(8,128)(2,1)}, bf16[96,640]{1,0:T(8,128)(2,1)S(1)}, u32[]{:S(2)}, u32[]{:S(2)}) collective-permute-start(bf16[96,640]{1,0:T(8,128)(2,1)} %refs_0_.1), channel_id=1, source_target_pairs={{0,8},{1,5},{2,10},{3,7},{8,16},{9,1},{10,18},{11,3},{16,24},{17,9... | collective-permute-start | bytes 368648 | tf_op jit(solution)/shard_map/ppermute | solution.py:91
  2.4 1.3 %collective-permute-start.10 = (bf16[96,640]{1,0:T(8,128)(2,1)S(1)}, bf16[96,640]{1,0:T(8,128)(2,1)S(1)}, u32[]{:S(2)}, u32[]{:S(2)}) collective-permute-start(bf16[96,640]{1,0:T(8,128)(2,1)S(1)} %get-tuple-element.10.refs_0_), channel_id=1, source_target_pairs={{0,4},{1,9},{2,6},{3,11},{8,0},{9,17},{10,2},{11,19},{16,8},{17,25... | collective-permute-start | bytes 368648 | tf_op jit(solution)/shard_map/ppermute | solution.py:91
  4.0 1.3 %collective-permute-start.16 = (bf16[96,640]{1,0:T(8,128)(2,1)S(1)}, bf16[96,640]{1,0:T(8,128)(2,1)S(1)}, u32[]{:S(2)}, u32[]{:S(2)}) collective-permute-start(bf16[96,640]{1,0:T(8,128)(2,1)S(1)} %get-tuple-element.11.refs_7_), channel_id=1, source_target_pairs={{0,4},{1,9},{2,6},{3,11},{8,0},{9,17},{10,2},{11,19},{16,8},{17,25... | collective-permute-start | bytes 368648 | tf_op jit(solution)/shard_map/ppermute | solution.py:91
  5.5 1.2 %collective-permute-done.4.refs_7_ = bf16[96,640]{1,0:T(8,128)(2,1)S(1)} collective-permute-done((bf16[96,640]{1,0:T(8,128)(2,1)}, bf16[96,640]{1,0:T(8,128)(2,1)S(1)}, u32[]{:S(2)}, u32[]{:S(2)}) %collective-permute-start.4) | collective-permute-done | bytes 122912 | tf_op jit(solution)/shard_map/ppermute | solution.py:91
  9.1 1.3 %collective-permute-start.11 = (bf16[96,640]{1,0:T(8,128)(2,1)S(1)}, bf16[96,640]{1,0:T(8,128)(2,1)S(1)}, u32[]{:S(2)}, u32[]{:S(2)}) collective-permute-start(bf16[96,640]{1,0:T(8,128)(2,1)S(1)} %collective-permute-done.10.refs_6_), channel_id=1, source_target_pairs={{0,4},{1,9},{2,6},{3,11},{8,0},{9,17},{10,2},{11,19},{16,8},{17,25... | collective-permute-start | bytes 368648 | tf_op jit(solution)/shard_map/ppermute | solution.py:91
  11.7 1.3 %collective-permute-start.17 = (bf16[96,640]{1,0:T(8,128)(2,1)S(1)}, bf16[96,640]{1,0:T(8,128)(2,1)S(1)}, u32[]{:S(2)}, u32[]{:S(2)}) collective-permute-start(bf16[96,640]{1,0:T(8,128)(2,1)S(1)} %collective-permute-done.16.refs_13_), channel_id=1, source_target_pairs={{0,4},{1,9},{2,6},{3,11},{8,0},{9,17},{10,2},{11,19},{16,8},{17,25... | collective-permute-start | bytes 368648 | tf_op jit(solution)/shard_map/ppermute | solution.py:91
  13.7 1.2 %collective-permute-start.8 = (bf16[96,640]{1,0:T(8,128)(2,1)S(1)}, bf16[96,640]{1,0:T(8,128)(2,1)S(1)}, u32[]{:S(2)}, u32[]{:S(2)}) collective-permute-start(bf16[96,640]{1,0:T(8,128)(2,1)S(1)} %collective-permute-done.7.refs_1_), channel_id=1, source_target_pairs={{0,8},{1,5},{2,10},{3,7},{8,16},{9,1},{10,18},{11,3},{16,24},{17,9... | collective-permute-start | bytes 368648 | tf_op jit(solution)/shard_map/ppermute | solution.py:91
  16.3 1.3 %collective-permute-start.12 = (bf16[96,640]{1,0:T(8,128)(2,1)S(1)}, bf16[96,640]{1,0:T(8,128)(2,1)S(1)}, u32[]{:S(2)}, u32[]{:S(2)}) collective-permute-start(bf16[96,640]{1,0:T(8,128)(2,1)S(1)} %collective-permute-done.11.refs_5_), channel_id=1, source_target_pairs={{0,4},{1,9},{2,6},{3,11},{8,0},{9,17},{10,2},{11,19},{16,8},{17,25... | collective-permute-start | bytes 368648 | tf_op jit(solution)/shard_map/ppermute | solution.py:91
  18.1 1.2 %collective-permute-start.15 = (bf16[96,640]{1,0:T(8,128)(2,1)S(1)}, bf16[96,640]{1,0:T(8,128)(2,1)S(1)}, u32[]{:S(2)}, u32[]{:S(2)}) collective-permute-start(bf16[96,640]{1,0:T(8,128)(2,1)S(1)} %collective-permute-done.14.refs_9_), channel_id=1, source_target_pairs={{0,8},{1,5},{2,10},{3,7},{8,16},{9,1},{10,18},{11,3},{16,24},{17,9... | collective-permute-start | bytes 368648 | tf_op jit(solution)/shard_map/ppermute | solution.py:91
  19.3 1.3 %collective-permute-start.3 = (bf16[96,640]{1,0:T(8,128)(2,1)S(1)}, bf16[96,640]{1,0:T(8,128)(2,1)S(1)}, u32[]{:S(2)}, u32[]{:S(2)}) collective-permute-start(bf16[96,640]{1,0:T(8,128)(2,1)S(1)} %collective-permute-done.2.refs_3_), channel_id=1, source_target_pairs={{0,8},{1,5},{2,10},{3,7},{8,16},{9,1},{10,18},{11,3},{16,24},{17,9... | collective-permute-start | bytes 368648 | tf_op jit(solution)/shard_map/ppermute | solution.py:91
  21.4 1.3 %collective-permute-start.18 = (bf16[96,640]{1,0:T(8,128)(2,1)S(1)}, bf16[96,640]{1,0:T(8,128)(2,1)S(1)}, u32[]{:S(2)}, u32[]{:S(2)}) collective-permute-start(bf16[96,640]{1,0:T(8,128)(2,1)S(1)} %collective-permute-done.17.refs_12_), channel_id=1, source_target_pairs={{0,4},{1,9},{2,6},{3,11},{8,0},{9,17},{10,2},{11,19},{16,8},{17,25... | collective-permute-start | bytes 368648 | tf_op jit(solution)/shard_map/ppermute | solution.py:91
  24.7 1.2 %collective-permute-done.3.refs_4_ = bf16[96,640]{1,0:T(8,128)(2,1)S(1)} collective-permute-done((bf16[96,640]{1,0:T(8,128)(2,1)S(1)}, bf16[96,640]{1,0:T(8,128)(2,1)S(1)}, u32[]{:S(2)}, u32[]{:S(2)}) %collective-permute-start.3) | collective-permute-done | bytes 122912 | tf_op jit(solution)/shard_map/ppermute | solution.py:91
  26.8 1.2 %collective-permute-done.9.refs_3_ = bf16[96,640]{1,0:T(8,128)(2,1)S(1)} collective-permute-done((bf16[96,640]{1,0:T(8,128)(2,1)S(1)}, bf16[96,640]{1,0:T(8,128)(2,1)S(1)}, u32[]{:S(2)}, u32[]{:S(2)}) %collective-permute-start.9) | collective-permute-done | bytes 122912 | tf_op jit(solution)/shard_map/ppermute | solution.py:91
  28.0 4.6 %shard_map.39 = (f32[5,8,96,128]{3,2,1,0:T(8,128)S(1)}, f32[5,8,96,128]{3,2,1,0:T(8,128)S(1)}, f32[5,8,96,128]{3,2,1,0:T(8,128)S(1)}) custom-call(s32[5]{0:T(128)S(1)} %stack.23.at_ref, bf16[8,96,640]{2,1,0:T(8,128)(2,1)S(1)} %shard_map.37.rows_ref, bf16[96,640]{1,0:T(8,128)(2,1)S(1)} %get-tuple-element.10.refs_0_, ...), custom_call_target="tpu_custom_call" | custom-call | flops 1321205760 | tf_op jit(solution)/shard_map/pallas_call | solution.py:244
  32.6 2.0 %shard_map.40 = bf16[384,640]{1,0:T(8,128)(2,1)S(1)} custom-call(s32[5]{0:T(128)S(1)} %stack.23.at_ref, bf16[8,96,640]{2,1,0:T(8,128)(2,1)S(1)} %shard_map.37.rows_ref, f32[5,8,96,128]{3,2,1,0:T(8,128)S(1)} %get-tuple-element.12.mixed_ref, f32[5,8,96,128]{3,2,1,0:T(8,128)S(1)} %get-tuple-element.13.sum_ref, f32[5,8,96,128]{3,2,1,0:T(8,128)S(1)} %get-tuple-element.14.top_ref, ...), custom_call_target="tpu_custom_call" | custom-call | flops 314572800 | tf_op jit(solution)/shard_map/pallas_call | solution.py:244
  34.6 3.2 %collective-permute-start.21 = (bf16[2,192,640]{2,1,0:T(8,128)(2,1)S(1)}, bf16[2,192,640]{2,1,0:T(8,128)(2,1)S(1)}, u32[]{:S(2)}, u32[]{:S(2)}) collective-permute-start(bf16[2,192,640]{2,1,0:T(8,128)(2,1)S(1)} %bitcast.16), channel_id=1, source_target_pairs={{0,1},{1,0},{2,3},{3,2},{4,5},{5,4},{6,7},{7,6},{8,9},{9,8},{10,11... | collective-permute-start | bytes 1474568 | tf_op jit(solution)/shard_map/ppermute | solution.py:289
  37.8 1.3 %shard_map.41 = f32[192,640]{1,0:T(8,128)S(1)} custom-call(s32[5]{0:T(128)S(1)} %stack.23.at_ref, bf16[8,96,640]{2,1,0:T(8,128)(2,1)S(1)} %shard_map.37.rows_ref, f32[5,8,96,128]{3,2,1,0:T(8,128)S(1)} %get-tuple-element.12.mixed_ref, f32[5,8,96,128]{3,2,1,0:T(8,128)S(1)} %get-tuple-element.13.sum_ref, f32[5,8,96,128]{3,2,1,0:T(8,128)S(1)} %get-tuple-element.14.top_ref, ...), custom_call_target="tpu_custom_call" | custom-call | flops 314572800 | tf_op jit(solution)/shard_map/pallas_call | solution.py:244
  39.6 1.2 %collective-permute-start.22 = (bf16[96,640]{1,0:T(8,128)(2,1)S(1)}, bf16[96,640]{1,0:T(8,128)(2,1)S(1)}, u32[]{:S(2)}, u32[]{:S(2)}) collective-permute-start(bf16[96,640]{1,0:T(8,128)(2,1)S(1)} %get-tuple-element.16.refs_0_), channel_id=1, source_target_pairs={{0,2},{1,3},{2,0},{3,1},{4,6},{5,7},{6,4},{7,5},{8,10},{9,11},{10,... | collective-permute-start | bytes 368648 | tf_op jit(solution)/shard_map/ppermute | solution.py:293
  40.8 1.3 %shard_map.42.kept_ref = f32[192,640]{1,0:T(8,128)S(1)} custom-call(s32[5]{0:T(128)S(1)} %stack.23.at_ref, bf16[8,96,640]{2,1,0:T(8,128)(2,1)S(1)} %shard_map.37.rows_ref, f32[5,8,96,128]{3,2,1,0:T(8,128)S(1)} %get-tuple-element.12.mixed_ref, f32[5,8,96,128]{3,2,1,0:T(8,128)S(1)} %get-tuple-element.13.sum_ref, ...), custom_call_target="tpu_custom_call" | custom-call | flops 314572800 | tf_op jit(solution)/shard_map/pallas_call | solution.py:244
  42.2 1.7 %collective-permute-done.24.from_x_ref = bf16[96,640]{1,0:T(8,128)(2,1)S(1)} collective-permute-done((bf16[96,640]{1,0:T(8,128)(2,1)S(1)}, bf16[96,640]{1,0:T(8,128)(2,1)S(1)}, u32[]{:S(2)}, u32[]{:S(2)}) %collective-permute-start.24) | collective-permute-done | bytes 122912 | tf_op jit(solution)/shard_map/ppermute | solution.py:293
  43.9 5.0 %collective-permute-start.25 = (bf16[96,640]{1,0:T(8,128)(2,1)S(1)}, bf16[96,640]{1,0:T(8,128)(2,1)S(1)}, u32[]{:S(2)}, u32[]{:S(2)}) collective-permute-start(bf16[96,640]{1,0:T(8,128)(2,1)S(1)} %shard_map.44), channel_id=1, source_target_pairs={{0,8},{1,28},{2,0},{3,20},{4,24},{5,12},{6,16},{7,4},{8,25},{9,5},... | collective-permute-start | bytes 368648 | tf_op jit(solution)/shard_map/ppermute | solution.py:305
  49.0 1.7 %collective-permute-start.23 = (bf16[96,640]{1,0:T(8,128)(2,1)S(1)}, bf16[96,640]{1,0:T(8,128)(2,1)S(1)}, u32[]{:S(2)}, u32[]{:S(2)}) collective-permute-start(bf16[96,640]{1,0:T(8,128)(2,1)S(1)} %shard_map.43), channel_id=1, source_target_pairs={{0,24},{1,12},{2,16},{3,4},{4,8},{5,28},{6,0},{7,20},{8,1},{9,29},... | collective-permute-start | bytes 368648 | tf_op jit(solution)/shard_map/ppermute | solution.py:305
  50.7 1.4 %collective-permute-done.25 = bf16[96,640]{1,0:T(8,128)(2,1)S(1)} collective-permute-done((bf16[96,640]{1,0:T(8,128)(2,1)S(1)}, bf16[96,640]{1,0:T(8,128)(2,1)S(1)}, u32[]{:S(2)}, u32[]{:S(2)}) %collective-permute-start.25) | collective-permute-done | bytes 122912 | tf_op jit(solution)/shard_map/ppermute | solution.py:305
  52.1 3.9 %collective-permute-done.23 = bf16[96,640]{1,0:T(8,128)(2,1)S(1)} collective-permute-done((bf16[96,640]{1,0:T(8,128)(2,1)S(1)}, bf16[96,640]{1,0:T(8,128)(2,1)S(1)}, u32[]{:S(2)}, u32[]{:S(2)}) %collective-permute-start.23) | collective-permute-done | bytes 122912 | tf_op jit(solution)/shard_map/ppermute | solution.py:305
  (46 shorter events, 13.0 us)
Async XLA Ops:
  0.0 5.3 %collective-permute-start = (bf16[96,640]{1,0:T(8,128)(2,1)}, bf16[96,640]{1,0:T(8,128)(2,1)S(1)}, u32[]{:S(2)}, u32[]{:S(2)}) collective-permute-start(bf16[96,640]{1,0:T(8,128)(2,1)} %refs_0_.1), channel_id=1, source_target_pairs={{0,8},{1,5},{2,10},{3,7},{8,16},{9,1},{10,18},{11,3},{16,24},{17,9... | collective-permute-start | bytes 368648 | tf_op jit(solution)/shard_map/ppermute | solution.py:91
  1.2 5.4 %collective-permute-start.4 = (bf16[96,640]{1,0:T(8,128)(2,1)}, bf16[96,640]{1,0:T(8,128)(2,1)S(1)}, u32[]{:S(2)}, u32[]{:S(2)}) collective-permute-start(bf16[96,640]{1,0:T(8,128)(2,1)} %refs_0_.1), channel_id=1, source_target_pairs={{0,4},{1,9},{2,6},{3,11},{8,0},{9,17},{10,2},{11,19},{16,8},{17,25... | collective-permute-start | bytes 368648 | tf_op jit(solution)/shard_map/ppermute | solution.py:91
  2.4 5.6 %collective-permute-start.10 = (bf16[96,640]{1,0:T(8,128)(2,1)S(1)}, bf16[96,640]{1,0:T(8,128)(2,1)S(1)}, u32[]{:S(2)}, u32[]{:S(2)}) collective-permute-start(bf16[96,640]{1,0:T(8,128)(2,1)S(1)} %get-tuple-element.10.refs_0_), channel_id=1, source_target_pairs={{0,4},{1,9},{2,6},{3,11},{8,0},{9,17},{10,2},{11,19},{16,8},{17,25... | collective-permute-start | bytes 368648 | tf_op jit(solution)/shard_map/ppermute | solution.py:91
  3.8 5.3 %collective-permute-start.13 = (bf16[96,640]{1,0:T(8,128)(2,1)S(1)}, bf16[96,640]{1,0:T(8,128)(2,1)S(1)}, u32[]{:S(2)}, u32[]{:S(2)}) collective-permute-start(bf16[96,640]{1,0:T(8,128)(2,1)S(1)} %get-tuple-element.11.refs_7_), channel_id=1, source_target_pairs={{0,8},{1,5},{2,10},{3,7},{8,16},{9,1},{10,18},{11,3},{16,24},{17,9... | collective-permute-start | bytes 368648 | tf_op jit(solution)/shard_map/ppermute | solution.py:91
  4.0 6.5 %collective-permute-start.16 = (bf16[96,640]{1,0:T(8,128)(2,1)S(1)}, bf16[96,640]{1,0:T(8,128)(2,1)S(1)}, u32[]{:S(2)}, u32[]{:S(2)}) collective-permute-start(bf16[96,640]{1,0:T(8,128)(2,1)S(1)} %get-tuple-element.11.refs_7_), channel_id=1, source_target_pairs={{0,4},{1,9},{2,6},{3,11},{8,0},{9,17},{10,2},{11,19},{16,8},{17,25... | collective-permute-start | bytes 368648 | tf_op jit(solution)/shard_map/ppermute | solution.py:91
  5.3 6.5 %collective-permute-start.7 = (bf16[96,640]{1,0:T(8,128)(2,1)S(1)}, bf16[96,640]{1,0:T(8,128)(2,1)S(1)}, u32[]{:S(2)}, u32[]{:S(2)}) collective-permute-start(bf16[96,640]{1,0:T(8,128)(2,1)S(1)} %get-tuple-element.10.refs_0_), channel_id=1, source_target_pairs={{0,8},{1,5},{2,10},{3,7},{8,16},{9,1},{10,18},{11,3},{16,24},{17,9... | collective-permute-start | bytes 368648 | tf_op jit(solution)/shard_map/ppermute | solution.py:91
  6.7 6.8 %collective-permute-start.1 = (bf16[96,640]{1,0:T(8,128)(2,1)S(1)}, bf16[96,640]{1,0:T(8,128)(2,1)S(1)}, u32[]{:S(2)}, u32[]{:S(2)}) collective-permute-start(bf16[96,640]{1,0:T(8,128)(2,1)S(1)} %collective-permute-done.refs_1_), channel_id=1, source_target_pairs={{0,8},{1,5},{2,10},{3,7},{8,16},{9,1},{10,18},{11,3},{16,24},{17,9... | collective-permute-start | bytes 368648 | tf_op jit(solution)/shard_map/ppermute | solution.py:91
  8.0 5.7 %collective-permute-start.5 = (bf16[96,640]{1,0:T(8,128)(2,1)S(1)}, bf16[96,640]{1,0:T(8,128)(2,1)S(1)}, u32[]{:S(2)}, u32[]{:S(2)}) collective-permute-start(bf16[96,640]{1,0:T(8,128)(2,1)S(1)} %collective-permute-done.4.refs_7_), channel_id=1, source_target_pairs={{0,4},{1,9},{2,6},{3,11},{8,0},{9,17},{10,2},{11,19},{16,8},{17,25... | collective-permute-start | bytes 368648 | tf_op jit(solution)/shard_map/ppermute | solution.py:91
  9.1 6.8 %collective-permute-start.11 = (bf16[96,640]{1,0:T(8,128)(2,1)S(1)}, bf16[96,640]{1,0:T(8,128)(2,1)S(1)}, u32[]{:S(2)}, u32[]{:S(2)}) collective-permute-start(bf16[96,640]{1,0:T(8,128)(2,1)S(1)} %collective-permute-done.10.refs_6_), channel_id=1, source_target_pairs={{0,4},{1,9},{2,6},{3,11},{8,0},{9,17},{10,2},{11,19},{16,8},{17,25... | collective-permute-start | bytes 368648 | tf_op jit(solution)/shard_map/ppermute | solution.py:91
  10.4 5.9 %collective-permute-start.14 = (bf16[96,640]{1,0:T(8,128)(2,1)S(1)}, bf16[96,640]{1,0:T(8,128)(2,1)S(1)}, u32[]{:S(2)}, u32[]{:S(2)}) collective-permute-start(bf16[96,640]{1,0:T(8,128)(2,1)S(1)} %collective-permute-done.13.refs_8_), channel_id=1, source_target_pairs={{0,8},{1,5},{2,10},{3,7},{8,16},{9,1},{10,18},{11,3},{16,24},{17,9... | collective-permute-start | bytes 368648 | tf_op jit(solution)/shard_map/ppermute | solution.py:91
  11.7 6.4 %collective-permute-start.17 = (bf16[96,640]{1,0:T(8,128)(2,1)S(1)}, bf16[96,640]{1,0:T(8,128)(2,1)S(1)}, u32[]{:S(2)}, u32[]{:S(2)}) collective-permute-start(bf16[96,640]{1,0:T(8,128)(2,1)S(1)} %collective-permute-done.16.refs_13_), channel_id=1, source_target_pairs={{0,4},{1,9},{2,6},{3,11},{8,0},{9,17},{10,2},{11,19},{16,8},{17,25... | collective-permute-start | bytes 368648 | tf_op jit(solution)/shard_map/ppermute | solution.py:91
  13.5 5.8 %collective-permute-start.2 = (bf16[96,640]{1,0:T(8,128)(2,1)S(1)}, bf16[96,640]{1,0:T(8,128)(2,1)S(1)}, u32[]{:S(2)}, u32[]{:S(2)}) collective-permute-start(bf16[96,640]{1,0:T(8,128)(2,1)S(1)} %collective-permute-done.1.refs_2_), channel_id=1, source_target_pairs={{0,8},{1,5},{2,10},{3,7},{8,16},{9,1},{10,18},{11,3},{16,24},{17,9... | collective-permute-start | bytes 368648 | tf_op jit(solution)/shard_map/ppermute | solution.py:91
  13.7 7.7 %collective-permute-start.8 = (bf16[96,640]{1,0:T(8,128)(2,1)S(1)}, bf16[96,640]{1,0:T(8,128)(2,1)S(1)}, u32[]{:S(2)}, u32[]{:S(2)}) collective-permute-start(bf16[96,640]{1,0:T(8,128)(2,1)S(1)} %collective-permute-done.7.refs_1_), channel_id=1, source_target_pairs={{0,8},{1,5},{2,10},{3,7},{8,16},{9,1},{10,18},{11,3},{16,24},{17,9... | collective-permute-start | bytes 368648 | tf_op jit(solution)/shard_map/ppermute | solution.py:91
  15.9 6.8 %collective-permute-start.6 = (bf16[96,640]{1,0:T(8,128)(2,1)S(1)}, bf16[96,640]{1,0:T(8,128)(2,1)S(1)}, u32[]{:S(2)}, u32[]{:S(2)}) collective-permute-start(bf16[96,640]{1,0:T(8,128)(2,1)S(1)} %collective-permute-done.5.refs_6_), channel_id=1, source_target_pairs={{0,4},{1,9},{2,6},{3,11},{8,0},{9,17},{10,2},{11,19},{16,8},{17,25... | collective-permute-start | bytes 368648 | tf_op jit(solution)/shard_map/ppermute | solution.py:91
  16.3 6.9 %collective-permute-start.12 = (bf16[96,640]{1,0:T(8,128)(2,1)S(1)}, bf16[96,640]{1,0:T(8,128)(2,1)S(1)}, u32[]{:S(2)}, u32[]{:S(2)}) collective-permute-start(bf16[96,640]{1,0:T(8,128)(2,1)S(1)} %collective-permute-done.11.refs_5_), channel_id=1, source_target_pairs={{0,4},{1,9},{2,6},{3,11},{8,0},{9,17},{10,2},{11,19},{16,8},{17,25... | collective-permute-start | bytes 368648 | tf_op jit(solution)/shard_map/ppermute | solution.py:91
  18.1 6.2 %collective-permute-start.15 = (bf16[96,640]{1,0:T(8,128)(2,1)S(1)}, bf16[96,640]{1,0:T(8,128)(2,1)S(1)}, u32[]{:S(2)}, u32[]{:S(2)}) collective-permute-start(bf16[96,640]{1,0:T(8,128)(2,1)S(1)} %collective-permute-done.14.refs_9_), channel_id=1, source_target_pairs={{0,8},{1,5},{2,10},{3,7},{8,16},{9,1},{10,18},{11,3},{16,24},{17,9... | collective-permute-start | bytes 368648 | tf_op jit(solution)/shard_map/ppermute | solution.py:91
  19.3 6.5 %collective-permute-start.3 = (bf16[96,640]{1,0:T(8,128)(2,1)S(1)}, bf16[96,640]{1,0:T(8,128)(2,1)S(1)}, u32[]{:S(2)}, u32[]{:S(2)}) collective-permute-start(bf16[96,640]{1,0:T(8,128)(2,1)S(1)} %collective-permute-done.2.refs_3_), channel_id=1, source_target_pairs={{0,8},{1,5},{2,10},{3,7},{8,16},{9,1},{10,18},{11,3},{16,24},{17,9... | collective-permute-start | bytes 368648 | tf_op jit(solution)/shard_map/ppermute | solution.py:91
  21.4 5.4 %collective-permute-start.18 = (bf16[96,640]{1,0:T(8,128)(2,1)S(1)}, bf16[96,640]{1,0:T(8,128)(2,1)S(1)}, u32[]{:S(2)}, u32[]{:S(2)}) collective-permute-start(bf16[96,640]{1,0:T(8,128)(2,1)S(1)} %collective-permute-done.17.refs_12_), channel_id=1, source_target_pairs={{0,4},{1,9},{2,6},{3,11},{8,0},{9,17},{10,2},{11,19},{16,8},{17,25... | collective-permute-start | bytes 368648 | tf_op jit(solution)/shard_map/ppermute | solution.py:91
  22.7 5.3 %collective-permute-start.9 = (bf16[96,640]{1,0:T(8,128)(2,1)S(1)}, bf16[96,640]{1,0:T(8,128)(2,1)S(1)}, u32[]{:S(2)}, u32[]{:S(2)}) collective-permute-start(bf16[96,640]{1,0:T(8,128)(2,1)S(1)} %collective-permute-done.8.refs_2_), channel_id=1, source_target_pairs={{0,8},{1,5},{2,10},{3,7},{8,16},{9,1},{10,18},{11,3},{16,24},{17,9... | collective-permute-start | bytes 368648 | tf_op jit(solution)/shard_map/ppermute | solution.py:91
  23.2 9.4 %collective-permute-start.19 = (bf16[96,640]{1,0:T(8,128)(2,1)S(1)}, bf16[96,640]{1,0:T(8,128)(2,1)S(1)}, u32[]{:S(2)}, u32[]{:S(2)}) collective-permute-start(bf16[96,640]{1,0:T(8,128)(2,1)S(1)} %collective-permute-done.12.refs_4_), channel_id=1, source_target_pairs={{0,4},{1,9},{2,6},{3,11},{8,0},{9,17},{10,2},{11,19},{16,8},{17,25... | collective-permute-start | bytes 368648 | tf_op jit(solution)/shard_map/ppermute | solution.py:91
  24.3 8.3 %collective-permute-start.20 = (bf16[96,640]{1,0:T(8,128)(2,1)S(1)}, bf16[96,640]{1,0:T(8,128)(2,1)S(1)}, u32[]{:S(2)}, u32[]{:S(2)}) collective-permute-start(bf16[96,640]{1,0:T(8,128)(2,1)S(1)} %collective-permute-done.15.refs_10_), channel_id=1, source_target_pairs={{0,8},{1,5},{2,10},{3,7},{8,16},{9,1},{10,18},{11,3},{16,24},{17,9... | collective-permute-start | bytes 368648 | tf_op jit(solution)/shard_map/ppermute | solution.py:91
  39.6 9.3 %collective-permute-start.22 = (bf16[96,640]{1,0:T(8,128)(2,1)S(1)}, bf16[96,640]{1,0:T(8,128)(2,1)S(1)}, u32[]{:S(2)}, u32[]{:S(2)}) collective-permute-start(bf16[96,640]{1,0:T(8,128)(2,1)S(1)} %get-tuple-element.16.refs_0_), channel_id=1, source_target_pairs={{0,2},{1,3},{2,0},{3,1},{4,6},{5,7},{6,4},{7,5},{8,10},{9,11},{10,... | collective-permute-start | bytes 368648 | tf_op jit(solution)/shard_map/ppermute | solution.py:293
  43.9 8.2 %collective-permute-start.25 = (bf16[96,640]{1,0:T(8,128)(2,1)S(1)}, bf16[96,640]{1,0:T(8,128)(2,1)S(1)}, u32[]{:S(2)}, u32[]{:S(2)}) collective-permute-start(bf16[96,640]{1,0:T(8,128)(2,1)S(1)} %shard_map.44), channel_id=1, source_target_pairs={{0,8},{1,28},{2,0},{3,20},{4,24},{5,12},{6,16},{7,4},{8,25},{9,5},... | collective-permute-start | bytes 368648 | tf_op jit(solution)/shard_map/ppermute | solution.py:305
  49.0 7.1 %collective-permute-start.23 = (bf16[96,640]{1,0:T(8,128)(2,1)S(1)}, bf16[96,640]{1,0:T(8,128)(2,1)S(1)}, u32[]{:S(2)}, u32[]{:S(2)}) collective-permute-start(bf16[96,640]{1,0:T(8,128)(2,1)S(1)} %shard_map.43), channel_id=1, source_target_pairs={{0,24},{1,12},{2,16},{3,4},{4,8},{5,28},{6,0},{7,20},{8,1},{9,29},... | collective-permute-start | bytes 368648 | tf_op jit(solution)/shard_map/ppermute | solution.py:305
  (5 other events, 16.9 us)

commit v28 on v26

--- a/solution.py
+++ b/solution.py
@@ -166,8 +166,9 @@
     z, y, x, core = (at_ref[i] for i in range(1, 5))
     blocks = []
     for slot in range(2):
-        to = look_up(sum(PATTERNS, ()), 4 * ((slot ^ y) + 2 * (x ^ flip_x)) + z)
-        owner = to + (core ^ flip_core) * (n - 1 - 2 * to)
+        row_y = core ^ flip_core
+        to = look_up(sum(PATTERNS, ()), 4 * ((slot ^ y ^ row_y) + 2 * (x ^ flip_x)) + z)
+        owner = to + row_y * (n - 1 - 2 * to)
         blocks.append(ring_distance(at_ref, owner, n))
     return blocks
 
@@ -180,7 +181,8 @@
         now = later
 
 
-def split_kernel(kv_ref, keys_ref, values_ref):
+def split_kernel(queries_ref, kv_ref, copy_ref, keys_ref, values_ref):
+    copy_ref[...] = queries_ref[...]
     keys_ref[...] = kv_ref[0]
     values_ref[...] = kv_ref[1]
 
@@ -266,8 +268,9 @@
     heads = width // HD
     f32, bf16 = jnp.float32, jnp.bfloat16
     block = (queries.shape, bf16)
-    own = call(split_kernel, (), [keys_values], [block, block], 0)
+    own_queries, *own = call(split_kernel, (), [queries, keys_values], [block] * 3, 0)
     queries, keys, values = gather_ring([queries, *own], n)
+    queries = [own_queries, *queries[1:]]
     (rows,) = call(functools.partial(rows_kernel, n), (), queries, [((n, ROWS, width), bf16)], 0)
     far = n // 2
     state = call(
@@ -301,14 +304,14 @@
         pairs = []
         for f in range(n):
             for h in range(4):
-                to = PATTERNS[(slot ^ (f & 1)) + 2 * (h >> 1)][f >> 1]
+                to = PATTERNS[(slot ^ (f & 1) ^ (h & 1)) + 2 * (h >> 1)][f >> 1]
                 pairs.append((4 * f + h, 4 * (2 * to + (h & 1)) + (f >> 1)))
         (total,) = call(
             functools.partial(sum_kernel, part), (), [kept, from_core, from_x[slot]], [((ROWS, cols), bf16)], 0
         )
         arrived.append(lax.ppermute(total, ("frames", "heads"), pairs))
     patterns = [[p[source] for p in PATTERNS].index(to) for source in range(4) for to in range(4)]
-    straight = look_up(patterns, 4 * head + z) & 1 == 0
+    straight = (look_up(patterns, 4 * head + z) ^ y) & 1 == 0
     low, high = arrived
     return jnp.concatenate([jnp.where(straight, low, high), jnp.where(straight, high, low)], axis=1)
 

time: 57 us -> 57.1 us (level)
  waiting for transfers between devices: 14.8 us -> 16.5 us
  starting transfers between devices: 29.4 us -> 28 us
    ppermute x21, waiting for transfers between devices: 8.01 us -> 9.83 us  [hop(): return lax.ppermute(x, ('frames', 'heads'), pairs)]
    ppermute x21, starting transfers between devices: 17.9 us -> 16.6 us  [hop(): return lax.ppermute(x, ('frames', 'heads'), pairs)]
where the time goes in v28:
time: 57.1 us; the launch traced here: 56.7 us
  starting transfers between devices  28 us (49%)
  waiting for transfers between devices  16.5 us (29%)
  Pallas kernels  9.4 us (16%)
  local copies, waits for them, and re-layouts  1.93 us (3%)
  other arithmetic  0.79 us (1%)
    ppermute x21, starting transfers between devices, hop(): return lax.ppermute(x, ('frames', 'heads'), pairs)  16.6 us
    ppermute x21, waiting for transfers between devices, hop(): return lax.ppermute(x, ('frames', 'heads'), pairs)  9.83 us
    pallas_call x8, Pallas kernels, call(): pl.pallas_call(kernel, out_shape=[jax.ShapeDtypeStruct(shape, dtype) for...  9.4 us
    ppermute x2, starting transfers between devices, on_device_ring(): arrived.append(lax.ppermute(total, ('frames', 'heads'), pairs))  6.71 us
    ppermute x2, waiting for transfers between devices, on_device_ring(): arrived.append(lax.ppermute(total, ('frames', 'heads'), pairs))  4.82 us
    ppermute x1, starting transfers between devices, on_device_ring(): from_core = lax.ppermute(given, 'heads', [(h, h ^ 1) for h in range(4)])  3.17 us
    unnamed x6, local copies, waits for them, and re-layouts  1.85 us
    ppermute x2, waiting for transfers between devices, on_device_ring(): lax.ppermute(block, 'heads', [(h, h ^ 2) for h in range(4)])  1.72 us
  transfers between devices with their start and end apart: 26, of which 15 were waited for; matrix products, arithmetic and copies ran while one was open for 0% of the time, Pallas kernels for 13%

profile of v28, /device:TPU:3, one launch (start us, length us, event | category | flops | bytes accessed | tf_op | source)
XLA Modules:
  0.0 56.7 jit_solution(6929549787693945574)
XLA Ops:
  0.0 1.2 %collective-permute-start = (bf16[96,640]{1,0:T(8,128)(2,1)}, bf16[96,640]{1,0:T(8,128)(2,1)S(1)}, u32[]{:S(2)}, u32[]{:S(2)}) collective-permute-start(bf16[96,640]{1,0:T(8,128)(2,1)} %queries_ref.1), channel_id=1, source_target_pairs={{0,8},{1,5},{2,10},{3,7},{8,16},{9,1},{10,18},{11,3},{16,24},{17,9... | collective-permute-start | bytes 368648 | tf_op jit(solution)/shard_map/ppermute | solution.py:91
  3.3 1.3 %collective-permute-start.10 = (bf16[96,640]{1,0:T(8,128)(2,1)S(1)}, bf16[96,640]{1,0:T(8,128)(2,1)S(1)}, u32[]{:S(2)}, u32[]{:S(2)}) collective-permute-start(bf16[96,640]{1,0:T(8,128)(2,1)S(1)} %get-tuple-element.12.refs_0_), channel_id=1, source_target_pairs={{0,4},{1,9},{2,6},{3,11},{8,0},{9,17},{10,2},{11,19},{16,8},{17,25... | collective-permute-start | bytes 368648 | tf_op jit(solution)/shard_map/ppermute | solution.py:91
  4.9 1.3 %collective-permute-start.16 = (bf16[96,640]{1,0:T(8,128)(2,1)S(1)}, bf16[96,640]{1,0:T(8,128)(2,1)S(1)}, u32[]{:S(2)}, u32[]{:S(2)}) collective-permute-start(bf16[96,640]{1,0:T(8,128)(2,1)S(1)} %get-tuple-element.13.refs_7_), channel_id=1, source_target_pairs={{0,4},{1,9},{2,6},{3,11},{8,0},{9,17},{10,2},{11,19},{16,8},{17,25... | collective-permute-start | bytes 368648 | tf_op jit(solution)/shard_map/ppermute | solution.py:91
  8.4 1.3 %collective-permute-done.13.refs_8_ = bf16[96,640]{1,0:T(8,128)(2,1)S(1)} collective-permute-done((bf16[96,640]{1,0:T(8,128)(2,1)S(1)}, bf16[96,640]{1,0:T(8,128)(2,1)S(1)}, u32[]{:S(2)}, u32[]{:S(2)}) %collective-permute-start.13) | collective-permute-done | bytes 122912 | tf_op jit(solution)/shard_map/ppermute | solution.py:91
  9.7 1.3 %collective-permute-start.11 = (bf16[96,640]{1,0:T(8,128)(2,1)S(1)}, bf16[96,640]{1,0:T(8,128)(2,1)S(1)}, u32[]{:S(2)}, u32[]{:S(2)}) collective-permute-start(bf16[96,640]{1,0:T(8,128)(2,1)S(1)} %collective-permute-done.10.refs_6_), channel_id=1, source_target_pairs={{0,4},{1,9},{2,6},{3,11},{8,0},{9,17},{10,2},{11,19},{16,8},{17,25... | collective-permute-start | bytes 368648 | tf_op jit(solution)/shard_map/ppermute | solution.py:91
  12.4 1.3 %collective-permute-start.17 = (bf16[96,640]{1,0:T(8,128)(2,1)S(1)}, bf16[96,640]{1,0:T(8,128)(2,1)S(1)}, u32[]{:S(2)}, u32[]{:S(2)}) collective-permute-start(bf16[96,640]{1,0:T(8,128)(2,1)S(1)} %collective-permute-done.16.refs_13_), channel_id=1, source_target_pairs={{0,4},{1,9},{2,6},{3,11},{8,0},{9,17},{10,2},{11,19},{16,8},{17,25... | collective-permute-start | bytes 368648 | tf_op jit(solution)/shard_map/ppermute | solution.py:91
  14.3 1.2 %collective-permute-start.8 = (bf16[96,640]{1,0:T(8,128)(2,1)S(1)}, bf16[96,640]{1,0:T(8,128)(2,1)S(1)}, u32[]{:S(2)}, u32[]{:S(2)}) collective-permute-start(bf16[96,640]{1,0:T(8,128)(2,1)S(1)} %collective-permute-done.7.refs_1_), channel_id=1, source_target_pairs={{0,8},{1,5},{2,10},{3,7},{8,16},{9,1},{10,18},{11,3},{16,24},{17,9... | collective-permute-start | bytes 368648 | tf_op jit(solution)/shard_map/ppermute | solution.py:91
  16.6 1.3 %collective-permute-start.12 = (bf16[96,640]{1,0:T(8,128)(2,1)S(1)}, bf16[96,640]{1,0:T(8,128)(2,1)S(1)}, u32[]{:S(2)}, u32[]{:S(2)}) collective-permute-start(bf16[96,640]{1,0:T(8,128)(2,1)S(1)} %collective-permute-done.11.refs_5_), channel_id=1, source_target_pairs={{0,4},{1,9},{2,6},{3,11},{8,0},{9,17},{10,2},{11,19},{16,8},{17,25... | collective-permute-start | bytes 368648 | tf_op jit(solution)/shard_map/ppermute | solution.py:91
  19.9 2.0 %collective-permute-done.8.refs_2_ = bf16[96,640]{1,0:T(8,128)(2,1)S(1)} collective-permute-done((bf16[96,640]{1,0:T(8,128)(2,1)S(1)}, bf16[96,640]{1,0:T(8,128)(2,1)S(1)}, u32[]{:S(2)}, u32[]{:S(2)}) %collective-permute-start.8) | collective-permute-done | bytes 122912 | tf_op jit(solution)/shard_map/ppermute | solution.py:91
  21.9 1.3 %collective-permute-start.18 = (bf16[96,640]{1,0:T(8,128)(2,1)S(1)}, bf16[96,640]{1,0:T(8,128)(2,1)S(1)}, u32[]{:S(2)}, u32[]{:S(2)}) collective-permute-start(bf16[96,640]{1,0:T(8,128)(2,1)S(1)} %collective-permute-done.17.refs_12_), channel_id=1, source_target_pairs={{0,4},{1,9},{2,6},{3,11},{8,0},{9,17},{10,2},{11,19},{16,8},{17,25... | collective-permute-start | bytes 368648 | tf_op jit(solution)/shard_map/ppermute | solution.py:91
  23.4 1.3 %collective-permute-start.19 = (bf16[96,640]{1,0:T(8,128)(2,1)S(1)}, bf16[96,640]{1,0:T(8,128)(2,1)S(1)}, u32[]{:S(2)}, u32[]{:S(2)}) collective-permute-start(bf16[96,640]{1,0:T(8,128)(2,1)S(1)} %collective-permute-done.12.refs_4_), channel_id=1, source_target_pairs={{0,4},{1,9},{2,6},{3,11},{8,0},{9,17},{10,2},{11,19},{16,8},{17,25... | collective-permute-start | bytes 368648 | tf_op jit(solution)/shard_map/ppermute | solution.py:91
  24.9 1.4 %collective-permute-done.3.refs_4_ = bf16[96,640]{1,0:T(8,128)(2,1)S(1)} collective-permute-done((bf16[96,640]{1,0:T(8,128)(2,1)S(1)}, bf16[96,640]{1,0:T(8,128)(2,1)S(1)}, u32[]{:S(2)}, u32[]{:S(2)}) %collective-permute-start.3) | collective-permute-done | bytes 122912 | tf_op jit(solution)/shard_map/ppermute | solution.py:91
  26.6 1.9 %collective-permute-done.9.refs_3_ = bf16[96,640]{1,0:T(8,128)(2,1)S(1)} collective-permute-done((bf16[96,640]{1,0:T(8,128)(2,1)S(1)}, bf16[96,640]{1,0:T(8,128)(2,1)S(1)}, u32[]{:S(2)}, u32[]{:S(2)}) %collective-permute-start.9) | collective-permute-done | bytes 122912 | tf_op jit(solution)/shard_map/ppermute | solution.py:91
  28.5 4.5 %shard_map.39 = (f32[5,8,96,128]{3,2,1,0:T(8,128)S(1)}, f32[5,8,96,128]{3,2,1,0:T(8,128)S(1)}, f32[5,8,96,128]{3,2,1,0:T(8,128)S(1)}) custom-call(s32[5]{0:T(128)S(1)} %stack.23.at_ref, bf16[8,96,640]{2,1,0:T(8,128)(2,1)S(1)} %shard_map.38.rows_ref, bf16[96,640]{1,0:T(8,128)(2,1)S(1)} %get-tuple-element.12.refs_0_, ...), custom_call_target="tpu_custom_call" | custom-call | flops 1321205760 | tf_op jit(solution)/shard_map/pallas_call | solution.py:250
  33.1 2.0 %shard_map.40 = bf16[384,640]{1,0:T(8,128)(2,1)S(1)} custom-call(s32[5]{0:T(128)S(1)} %stack.23.at_ref, bf16[8,96,640]{2,1,0:T(8,128)(2,1)S(1)} %shard_map.38.rows_ref, f32[5,8,96,128]{3,2,1,0:T(8,128)S(1)} %get-tuple-element.14.mixed_ref, f32[5,8,96,128]{3,2,1,0:T(8,128)S(1)} %get-tuple-element.15.sum_ref, f32[5,8,96,128]{3,2,1,0:T(8,128)S(1)} %get-tuple-element.16.top_ref, ...), custom_call_target="tpu_custom_call" | custom-call | flops 314572800 | tf_op jit(solution)/shard_map/pallas_call | solution.py:250
  35.0 3.2 %collective-permute-start.21 = (bf16[2,192,640]{2,1,0:T(8,128)(2,1)S(1)}, bf16[2,192,640]{2,1,0:T(8,128)(2,1)S(1)}, u32[]{:S(2)}, u32[]{:S(2)}) collective-permute-start(bf16[2,192,640]{2,1,0:T(8,128)(2,1)S(1)} %bitcast.16), channel_id=1, source_target_pairs={{0,1},{1,0},{2,3},{3,2},{4,5},{5,4},{6,7},{7,6},{8,9},{9,8},{10,11... | collective-permute-start | bytes 1474568 | tf_op jit(solution)/shard_map/ppermute | solution.py:296
  38.2 1.3 %shard_map.41 = f32[192,640]{1,0:T(8,128)S(1)} custom-call(s32[5]{0:T(128)S(1)} %stack.23.at_ref, bf16[8,96,640]{2,1,0:T(8,128)(2,1)S(1)} %shard_map.38.rows_ref, f32[5,8,96,128]{3,2,1,0:T(8,128)S(1)} %get-tuple-element.14.mixed_ref, f32[5,8,96,128]{3,2,1,0:T(8,128)S(1)} %get-tuple-element.15.sum_ref, f32[5,8,96,128]{3,2,1,0:T(8,128)S(1)} %get-tuple-element.16.top_ref, ...), custom_call_target="tpu_custom_call" | custom-call | flops 314572800 | tf_op jit(solution)/shard_map/pallas_call | solution.py:250
  40.0 1.3 %collective-permute-start.22 = (bf16[96,640]{1,0:T(8,128)(2,1)S(1)}, bf16[96,640]{1,0:T(8,128)(2,1)S(1)}, u32[]{:S(2)}, u32[]{:S(2)}) collective-permute-start(bf16[96,640]{1,0:T(8,128)(2,1)S(1)} %get-tuple-element.18.refs_0_), channel_id=1, source_target_pairs={{0,2},{1,3},{2,0},{3,1},{4,6},{5,7},{6,4},{7,5},{8,10},{9,11},{10,... | collective-permute-start | bytes 368648 | tf_op jit(solution)/shard_map/ppermute | solution.py:300
  41.3 1.3 %shard_map.42.kept_ref = f32[192,640]{1,0:T(8,128)S(1)} custom-call(s32[5]{0:T(128)S(1)} %stack.23.at_ref, bf16[8,96,640]{2,1,0:T(8,128)(2,1)S(1)} %shard_map.38.rows_ref, f32[5,8,96,128]{3,2,1,0:T(8,128)S(1)} %get-tuple-element.14.mixed_ref, f32[5,8,96,128]{3,2,1,0:T(8,128)S(1)} %get-tuple-element.15.sum_ref, ...), custom_call_target="tpu_custom_call" | custom-call | flops 314572800 | tf_op jit(solution)/shard_map/pallas_call | solution.py:250
  42.6 1.7 %collective-permute-done.24.from_x_ref = bf16[96,640]{1,0:T(8,128)(2,1)S(1)} collective-permute-done((bf16[96,640]{1,0:T(8,128)(2,1)S(1)}, bf16[96,640]{1,0:T(8,128)(2,1)S(1)}, u32[]{:S(2)}, u32[]{:S(2)}) %collective-permute-start.24) | collective-permute-done | bytes 122912 | tf_op jit(solution)/shard_map/ppermute | solution.py:300
  44.4 4.5 %collective-permute-start.25 = (bf16[96,640]{1,0:T(8,128)(2,1)S(1)}, bf16[96,640]{1,0:T(8,128)(2,1)S(1)}, u32[]{:S(2)}, u32[]{:S(2)}) collective-permute-start(bf16[96,640]{1,0:T(8,128)(2,1)S(1)} %shard_map.44), channel_id=1, source_target_pairs={{0,8},{1,28},{2,0},{3,20},{4,24},{5,12},{6,16},{7,4},{8,25},{9,5},... | collective-permute-start | bytes 368648 | tf_op jit(solution)/shard_map/ppermute | solution.py:312
  48.9 2.2 %collective-permute-start.23 = (bf16[96,640]{1,0:T(8,128)(2,1)S(1)}, bf16[96,640]{1,0:T(8,128)(2,1)S(1)}, u32[]{:S(2)}, u32[]{:S(2)}) collective-permute-start(bf16[96,640]{1,0:T(8,128)(2,1)S(1)} %shard_map.43), channel_id=1, source_target_pairs={{0,24},{1,12},{2,16},{3,4},{4,8},{5,28},{6,0},{7,20},{8,1},{9,29},... | collective-permute-start | bytes 368648 | tf_op jit(solution)/shard_map/ppermute | solution.py:312
  51.2 1.8 %collective-permute-done.25 = bf16[96,640]{1,0:T(8,128)(2,1)S(1)} collective-permute-done((bf16[96,640]{1,0:T(8,128)(2,1)S(1)}, bf16[96,640]{1,0:T(8,128)(2,1)S(1)}, u32[]{:S(2)}, u32[]{:S(2)}) %collective-permute-start.25) | collective-permute-done | bytes 122912 | tf_op jit(solution)/shard_map/ppermute | solution.py:312
  52.9 3.1 %collective-permute-done.23 = bf16[96,640]{1,0:T(8,128)(2,1)S(1)} collective-permute-done((bf16[96,640]{1,0:T(8,128)(2,1)S(1)}, bf16[96,640]{1,0:T(8,128)(2,1)S(1)}, u32[]{:S(2)}, u32[]{:S(2)}) %collective-permute-start.23) | collective-permute-done | bytes 122912 | tf_op jit(solution)/shard_map/ppermute | solution.py:312
  (46 shorter events, 11.6 us)
Async XLA Ops:
  0.0 6.2 %collective-permute-start = (bf16[96,640]{1,0:T(8,128)(2,1)}, bf16[96,640]{1,0:T(8,128)(2,1)S(1)}, u32[]{:S(2)}, u32[]{:S(2)}) collective-permute-start(bf16[96,640]{1,0:T(8,128)(2,1)} %queries_ref.1), channel_id=1, source_target_pairs={{0,8},{1,5},{2,10},{3,7},{8,16},{9,1},{10,18},{11,3},{16,24},{17,9... | collective-permute-start | bytes 368648 | tf_op jit(solution)/shard_map/ppermute | solution.py:91
  1.2 5.4 %collective-permute-start.4 = (bf16[96,640]{1,0:T(8,128)(2,1)}, bf16[96,640]{1,0:T(8,128)(2,1)S(1)}, u32[]{:S(2)}, u32[]{:S(2)}) collective-permute-start(bf16[96,640]{1,0:T(8,128)(2,1)} %queries_ref.1), channel_id=1, source_target_pairs={{0,4},{1,9},{2,6},{3,11},{8,0},{9,17},{10,2},{11,19},{16,8},{17,25... | collective-permute-start | bytes 368648 | tf_op jit(solution)/shard_map/ppermute | solution.py:91
  4.7 5.0 %collective-permute-start.13 = (bf16[96,640]{1,0:T(8,128)(2,1)S(1)}, bf16[96,640]{1,0:T(8,128)(2,1)S(1)}, u32[]{:S(2)}, u32[]{:S(2)}) collective-permute-start(bf16[96,640]{1,0:T(8,128)(2,1)S(1)} %get-tuple-element.13.refs_7_), channel_id=1, source_target_pairs={{0,8},{1,5},{2,10},{3,7},{8,16},{9,1},{10,18},{11,3},{16,24},{17,9... | collective-permute-start | bytes 368648 | tf_op jit(solution)/shard_map/ppermute | solution.py:91
  4.9 6.2 %collective-permute-start.16 = (bf16[96,640]{1,0:T(8,128)(2,1)S(1)}, bf16[96,640]{1,0:T(8,128)(2,1)S(1)}, u32[]{:S(2)}, u32[]{:S(2)}) collective-permute-start(bf16[96,640]{1,0:T(8,128)(2,1)S(1)} %get-tuple-element.13.refs_7_), channel_id=1, source_target_pairs={{0,4},{1,9},{2,6},{3,11},{8,0},{9,17},{10,2},{11,19},{16,8},{17,25... | collective-permute-start | bytes 368648 | tf_op jit(solution)/shard_map/ppermute | solution.py:91
  6.2 6.2 %collective-permute-start.7 = (bf16[96,640]{1,0:T(8,128)(2,1)S(1)}, bf16[96,640]{1,0:T(8,128)(2,1)S(1)}, u32[]{:S(2)}, u32[]{:S(2)}) collective-permute-start(bf16[96,640]{1,0:T(8,128)(2,1)S(1)} %get-tuple-element.12.refs_0_), channel_id=1, source_target_pairs={{0,8},{1,5},{2,10},{3,7},{8,16},{9,1},{10,18},{11,3},{16,24},{17,9... | collective-permute-start | bytes 368648 | tf_op jit(solution)/shard_map/ppermute | solution.py:91
  6.7 7.3 %collective-permute-start.1 = (bf16[96,640]{1,0:T(8,128)(2,1)S(1)}, bf16[96,640]{1,0:T(8,128)(2,1)S(1)}, u32[]{:S(2)}, u32[]{:S(2)}) collective-permute-start(bf16[96,640]{1,0:T(8,128)(2,1)S(1)} %collective-permute-done.refs_1_), channel_id=1, source_target_pairs={{0,8},{1,5},{2,10},{3,7},{8,16},{9,1},{10,18},{11,3},{16,24},{17,9... | collective-permute-start | bytes 368648 | tf_op jit(solution)/shard_map/ppermute | solution.py:91
  8.0 6.3 %collective-permute-start.5 = (bf16[96,640]{1,0:T(8,128)(2,1)S(1)}, bf16[96,640]{1,0:T(8,128)(2,1)S(1)}, u32[]{:S(2)}, u32[]{:S(2)}) collective-permute-start(bf16[96,640]{1,0:T(8,128)(2,1)S(1)} %collective-permute-done.4.refs_7_), channel_id=1, source_target_pairs={{0,4},{1,9},{2,6},{3,11},{8,0},{9,17},{10,2},{11,19},{16,8},{17,25... | collective-permute-start | bytes 368648 | tf_op jit(solution)/shard_map/ppermute | solution.py:91
  9.7 5.8 %collective-permute-start.11 = (bf16[96,640]{1,0:T(8,128)(2,1)S(1)}, bf16[96,640]{1,0:T(8,128)(2,1)S(1)}, u32[]{:S(2)}, u32[]{:S(2)}) collective-permute-start(bf16[96,640]{1,0:T(8,128)(2,1)S(1)} %collective-permute-done.10.refs_6_), channel_id=1, source_target_pairs={{0,4},{1,9},{2,6},{3,11},{8,0},{9,17},{10,2},{11,19},{16,8},{17,25... | collective-permute-start | bytes 368648 | tf_op jit(solution)/shard_map/ppermute | solution.py:91
  11.0 5.6 %collective-permute-start.14 = (bf16[96,640]{1,0:T(8,128)(2,1)S(1)}, bf16[96,640]{1,0:T(8,128)(2,1)S(1)}, u32[]{:S(2)}, u32[]{:S(2)}) collective-permute-start(bf16[96,640]{1,0:T(8,128)(2,1)S(1)} %collective-permute-done.13.refs_8_), channel_id=1, source_target_pairs={{0,8},{1,5},{2,10},{3,7},{8,16},{9,1},{10,18},{11,3},{16,24},{17,9... | collective-permute-start | bytes 368648 | tf_op jit(solution)/shard_map/ppermute | solution.py:91
  12.4 5.6 %collective-permute-start.17 = (bf16[96,640]{1,0:T(8,128)(2,1)S(1)}, bf16[96,640]{1,0:T(8,128)(2,1)S(1)}, u32[]{:S(2)}, u32[]{:S(2)}) collective-permute-start(bf16[96,640]{1,0:T(8,128)(2,1)S(1)} %collective-permute-done.16.refs_13_), channel_id=1, source_target_pairs={{0,4},{1,9},{2,6},{3,11},{8,0},{9,17},{10,2},{11,19},{16,8},{17,25... | collective-permute-start | bytes 368648 | tf_op jit(solution)/shard_map/ppermute | solution.py:91
  14.0 5.4 %collective-permute-start.2 = (bf16[96,640]{1,0:T(8,128)(2,1)S(1)}, bf16[96,640]{1,0:T(8,128)(2,1)S(1)}, u32[]{:S(2)}, u32[]{:S(2)}) collective-permute-start(bf16[96,640]{1,0:T(8,128)(2,1)S(1)} %collective-permute-done.1.refs_2_), channel_id=1, source_target_pairs={{0,8},{1,5},{2,10},{3,7},{8,16},{9,1},{10,18},{11,3},{16,24},{17,9... | collective-permute-start | bytes 368648 | tf_op jit(solution)/shard_map/ppermute | solution.py:91
  14.3 7.6 %collective-permute-start.8 = (bf16[96,640]{1,0:T(8,128)(2,1)S(1)}, bf16[96,640]{1,0:T(8,128)(2,1)S(1)}, u32[]{:S(2)}, u32[]{:S(2)}) collective-permute-start(bf16[96,640]{1,0:T(8,128)(2,1)S(1)} %collective-permute-done.7.refs_1_), channel_id=1, source_target_pairs={{0,8},{1,5},{2,10},{3,7},{8,16},{9,1},{10,18},{11,3},{16,24},{17,9... | collective-permute-start | bytes 368648 | tf_op jit(solution)/shard_map/ppermute | solution.py:91
  15.5 7.7 %collective-permute-start.6 = (bf16[96,640]{1,0:T(8,128)(2,1)S(1)}, bf16[96,640]{1,0:T(8,128)(2,1)S(1)}, u32[]{:S(2)}, u32[]{:S(2)}) collective-permute-start(bf16[96,640]{1,0:T(8,128)(2,1)S(1)} %collective-permute-done.5.refs_6_), channel_id=1, source_target_pairs={{0,4},{1,9},{2,6},{3,11},{8,0},{9,17},{10,2},{11,19},{16,8},{17,25... | collective-permute-start | bytes 368648 | tf_op jit(solution)/shard_map/ppermute | solution.py:91
  16.6 6.8 %collective-permute-start.12 = (bf16[96,640]{1,0:T(8,128)(2,1)S(1)}, bf16[96,640]{1,0:T(8,128)(2,1)S(1)}, u32[]{:S(2)}, u32[]{:S(2)}) collective-permute-start(bf16[96,640]{1,0:T(8,128)(2,1)S(1)} %collective-permute-done.11.refs_5_), channel_id=1, source_target_pairs={{0,4},{1,9},{2,6},{3,11},{8,0},{9,17},{10,2},{11,19},{16,8},{17,25... | collective-permute-start | bytes 368648 | tf_op jit(solution)/shard_map/ppermute | solution.py:91
  17.9 6.8 %collective-permute-start.15 = (bf16[96,640]{1,0:T(8,128)(2,1)S(1)}, bf16[96,640]{1,0:T(8,128)(2,1)S(1)}, u32[]{:S(2)}, u32[]{:S(2)}) collective-permute-start(bf16[96,640]{1,0:T(8,128)(2,1)S(1)} %collective-permute-done.14.refs_9_), channel_id=1, source_target_pairs={{0,8},{1,5},{2,10},{3,7},{8,16},{9,1},{10,18},{11,3},{16,24},{17,9... | collective-permute-start | bytes 368648 | tf_op jit(solution)/shard_map/ppermute | solution.py:91
  19.4 6.9 %collective-permute-start.3 = (bf16[96,640]{1,0:T(8,128)(2,1)S(1)}, bf16[96,640]{1,0:T(8,128)(2,1)S(1)}, u32[]{:S(2)}, u32[]{:S(2)}) collective-permute-start(bf16[96,640]{1,0:T(8,128)(2,1)S(1)} %collective-permute-done.2.refs_3_), channel_id=1, source_target_pairs={{0,8},{1,5},{2,10},{3,7},{8,16},{9,1},{10,18},{11,3},{16,24},{17,9... | collective-permute-start | bytes 368648 | tf_op jit(solution)/shard_map/ppermute | solution.py:91
  21.9 4.7 %collective-permute-start.18 = (bf16[96,640]{1,0:T(8,128)(2,1)S(1)}, bf16[96,640]{1,0:T(8,128)(2,1)S(1)}, u32[]{:S(2)}, u32[]{:S(2)}) collective-permute-start(bf16[96,640]{1,0:T(8,128)(2,1)S(1)} %collective-permute-done.17.refs_12_), channel_id=1, source_target_pairs={{0,4},{1,9},{2,6},{3,11},{8,0},{9,17},{10,2},{11,19},{16,8},{17,25... | collective-permute-start | bytes 368648 | tf_op jit(solution)/shard_map/ppermute | solution.py:91
  23.2 5.3 %collective-permute-start.9 = (bf16[96,640]{1,0:T(8,128)(2,1)S(1)}, bf16[96,640]{1,0:T(8,128)(2,1)S(1)}, u32[]{:S(2)}, u32[]{:S(2)}) collective-permute-start(bf16[96,640]{1,0:T(8,128)(2,1)S(1)} %collective-permute-done.8.refs_2_), channel_id=1, source_target_pairs={{0,8},{1,5},{2,10},{3,7},{8,16},{9,1},{10,18},{11,3},{16,24},{17,9... | collective-permute-start | bytes 368648 | tf_op jit(solution)/shard_map/ppermute | solution.py:91
  23.4 9.6 %collective-permute-start.19 = (bf16[96,640]{1,0:T(8,128)(2,1)S(1)}, bf16[96,640]{1,0:T(8,128)(2,1)S(1)}, u32[]{:S(2)}, u32[]{:S(2)}) collective-permute-start(bf16[96,640]{1,0:T(8,128)(2,1)S(1)} %collective-permute-done.12.refs_4_), channel_id=1, source_target_pairs={{0,4},{1,9},{2,6},{3,11},{8,0},{9,17},{10,2},{11,19},{16,8},{17,25... | collective-permute-start | bytes 368648 | tf_op jit(solution)/shard_map/ppermute | solution.py:91
  24.7 8.3 %collective-permute-start.20 = (bf16[96,640]{1,0:T(8,128)(2,1)S(1)}, bf16[96,640]{1,0:T(8,128)(2,1)S(1)}, u32[]{:S(2)}, u32[]{:S(2)}) collective-permute-start(bf16[96,640]{1,0:T(8,128)(2,1)S(1)} %collective-permute-done.15.refs_10_), channel_id=1, source_target_pairs={{0,8},{1,5},{2,10},{3,7},{8,16},{9,1},{10,18},{11,3},{16,24},{17,9... | collective-permute-start | bytes 368648 | tf_op jit(solution)/shard_map/ppermute | solution.py:91
  35.0 4.7 %collective-permute-start.21 = (bf16[2,192,640]{2,1,0:T(8,128)(2,1)S(1)}, bf16[2,192,640]{2,1,0:T(8,128)(2,1)S(1)}, u32[]{:S(2)}, u32[]{:S(2)}) collective-permute-start(bf16[2,192,640]{2,1,0:T(8,128)(2,1)S(1)} %bitcast.16), channel_id=1, source_target_pairs={{0,1},{1,0},{2,3},{3,2},{4,5},{5,4},{6,7},{7,6},{8,9},{9,8},{10,11... | collective-permute-start | bytes 1474568 | tf_op jit(solution)/shard_map/ppermute | solution.py:296
  40.0 8.9 %collective-permute-start.22 = (bf16[96,640]{1,0:T(8,128)(2,1)S(1)}, bf16[96,640]{1,0:T(8,128)(2,1)S(1)}, u32[]{:S(2)}, u32[]{:S(2)}) collective-permute-start(bf16[96,640]{1,0:T(8,128)(2,1)S(1)} %get-tuple-element.18.refs_0_), channel_id=1, source_target_pairs={{0,2},{1,3},{2,0},{3,1},{4,6},{5,7},{6,4},{7,5},{8,10},{9,11},{10,... | collective-permute-start | bytes 368648 | tf_op jit(solution)/shard_map/ppermute | solution.py:300
  44.4 8.5 %collective-permute-start.25 = (bf16[96,640]{1,0:T(8,128)(2,1)S(1)}, bf16[96,640]{1,0:T(8,128)(2,1)S(1)}, u32[]{:S(2)}, u32[]{:S(2)}) collective-permute-start(bf16[96,640]{1,0:T(8,128)(2,1)S(1)} %shard_map.44), channel_id=1, source_target_pairs={{0,8},{1,28},{2,0},{3,20},{4,24},{5,12},{6,16},{7,4},{8,25},{9,5},... | collective-permute-start | bytes 368648 | tf_op jit(solution)/shard_map/ppermute | solution.py:312
  48.9 7.1 %collective-permute-start.23 = (bf16[96,640]{1,0:T(8,128)(2,1)S(1)}, bf16[96,640]{1,0:T(8,128)(2,1)S(1)}, u32[]{:S(2)}, u32[]{:S(2)}) collective-permute-start(bf16[96,640]{1,0:T(8,128)(2,1)S(1)} %shard_map.43), channel_id=1, source_target_pairs={{0,24},{1,12},{2,16},{3,4},{4,8},{5,28},{6,0},{7,20},{8,1},{9,29},... | collective-permute-start | bytes 368648 | tf_op jit(solution)/shard_map/ppermute | solution.py:312
  (5 other events, 17.8 us)

commit v29 on v27

--- a/solution.py
+++ b/solution.py
@@ -154,7 +154,7 @@
     return mixed[:, :HD], mixed[:, HD:]
 
 
-PATTERNS = ((3, 0, 1, 3), (1, 3, 2, 1), (2, 1, 0, 2), (0, 2, 3, 0))
+PATTERNS = ((3, 0, 1, 1), (1, 3, 2, 3), (2, 2, 3, 0), (0, 1, 0, 2))
 
 
 def look_up(table, index):

time: 56.9 us -> 56.7 us (level)
  waiting for transfers between devices: 15.2 us -> 14.6 us
where the time goes in v29:
time: 56.7 us; the launch traced here: 56.2 us
  starting transfers between devices  29.4 us (52%)
  waiting for transfers between devices  14.6 us (26%)
  Pallas kernels  9.42 us (17%)
  local copies, waits for them, and re-layouts  1.94 us (3%)
  other arithmetic  0.79 us (1%)
    ppermute x21, starting transfers between devices, hop(): return lax.ppermute(x, ('frames', 'heads'), pairs)  17.9 us
    pallas_call x8, Pallas kernels, call(): pl.pallas_call(kernel, out_shape=[jax.ShapeDtypeStruct(shape, dtype) for...  9.42 us
    ppermute x21, waiting for transfers between devices, hop(): return lax.ppermute(x, ('frames', 'heads'), pairs)  8.01 us
    ppermute x2, starting transfers between devices, on_device_ring(): arrived.append(lax.ppermute(total, ('frames', 'heads'), pairs))  6.73 us
    ppermute x2, waiting for transfers between devices, on_device_ring(): arrived.append(lax.ppermute(total, ('frames', 'heads'), pairs))  4.77 us
    ppermute x1, starting transfers between devices, on_device_ring(): from_core = lax.ppermute(given, 'heads', [(h, h ^ 1) for h in range(4)])  3.17 us
    unnamed x6, local copies, waits for them, and re-layouts  1.85 us
    ppermute x2, waiting for transfers between devices, on_device_ring(): lax.ppermute(block, 'heads', [(h, h ^ 2) for h in range(4)])  1.68 us
  transfers between devices with their start and end apart: 26, of which 15 were waited for; matrix products, arithmetic and copies ran while one was open for 0% of the time, Pallas kernels for 13%

profile of v29, /device:TPU:3, one launch (start us, length us, event | category | flops | bytes accessed | tf_op | source)
XLA Modules:
  0.0 56.2 jit_solution(12527785551898505585)
XLA Ops:
  0.0 1.2 %collective-permute-start = (bf16[96,640]{1,0:T(8,128)(2,1)}, bf16[96,640]{1,0:T(8,128)(2,1)S(1)}, u32[]{:S(2)}, u32[]{:S(2)}) collective-permute-start(bf16[96,640]{1,0:T(8,128)(2,1)} %refs_0_.1), channel_id=1, source_target_pairs={{0,8},{1,5},{2,10},{3,7},{8,16},{9,1},{10,18},{11,3},{16,24},{17,9... | collective-permute-start | bytes 368648 | tf_op jit(solution)/shard_map/ppermute | solution.py:91
  2.4 1.3 %collective-permute-start.10 = (bf16[96,640]{1,0:T(8,128)(2,1)S(1)}, bf16[96,640]{1,0:T(8,128)(2,1)S(1)}, u32[]{:S(2)}, u32[]{:S(2)}) collective-permute-start(bf16[96,640]{1,0:T(8,128)(2,1)S(1)} %get-tuple-element.10.refs_0_), channel_id=1, source_target_pairs={{0,4},{1,9},{2,6},{3,11},{8,0},{9,17},{10,2},{11,19},{16,8},{17,25... | collective-permute-start | bytes 368648 | tf_op jit(solution)/shard_map/ppermute | solution.py:91
  4.0 1.3 %collective-permute-start.16 = (bf16[96,640]{1,0:T(8,128)(2,1)S(1)}, bf16[96,640]{1,0:T(8,128)(2,1)S(1)}, u32[]{:S(2)}, u32[]{:S(2)}) collective-permute-start(bf16[96,640]{1,0:T(8,128)(2,1)S(1)} %get-tuple-element.11.refs_7_), channel_id=1, source_target_pairs={{0,4},{1,9},{2,6},{3,11},{8,0},{9,17},{10,2},{11,19},{16,8},{17,25... | collective-permute-start | bytes 368648 | tf_op jit(solution)/shard_map/ppermute | solution.py:91
  5.5 1.2 %collective-permute-done.4.refs_7_ = bf16[96,640]{1,0:T(8,128)(2,1)S(1)} collective-permute-done((bf16[96,640]{1,0:T(8,128)(2,1)}, bf16[96,640]{1,0:T(8,128)(2,1)S(1)}, u32[]{:S(2)}, u32[]{:S(2)}) %collective-permute-start.4) | collective-permute-done | bytes 122912 | tf_op jit(solution)/shard_map/ppermute | solution.py:91
  9.1 1.3 %collective-permute-start.11 = (bf16[96,640]{1,0:T(8,128)(2,1)S(1)}, bf16[96,640]{1,0:T(8,128)(2,1)S(1)}, u32[]{:S(2)}, u32[]{:S(2)}) collective-permute-start(bf16[96,640]{1,0:T(8,128)(2,1)S(1)} %collective-permute-done.10.refs_6_), channel_id=1, source_target_pairs={{0,4},{1,9},{2,6},{3,11},{8,0},{9,17},{10,2},{11,19},{16,8},{17,25... | collective-permute-start | bytes 368648 | tf_op jit(solution)/shard_map/ppermute | solution.py:91
  11.7 1.3 %collective-permute-start.17 = (bf16[96,640]{1,0:T(8,128)(2,1)S(1)}, bf16[96,640]{1,0:T(8,128)(2,1)S(1)}, u32[]{:S(2)}, u32[]{:S(2)}) collective-permute-start(bf16[96,640]{1,0:T(8,128)(2,1)S(1)} %collective-permute-done.16.refs_13_), channel_id=1, source_target_pairs={{0,4},{1,9},{2,6},{3,11},{8,0},{9,17},{10,2},{11,19},{16,8},{17,25... | collective-permute-start | bytes 368648 | tf_op jit(solution)/shard_map/ppermute | solution.py:91
  13.7 1.2 %collective-permute-start.8 = (bf16[96,640]{1,0:T(8,128)(2,1)S(1)}, bf16[96,640]{1,0:T(8,128)(2,1)S(1)}, u32[]{:S(2)}, u32[]{:S(2)}) collective-permute-start(bf16[96,640]{1,0:T(8,128)(2,1)S(1)} %collective-permute-done.7.refs_1_), channel_id=1, source_target_pairs={{0,8},{1,5},{2,10},{3,7},{8,16},{9,1},{10,18},{11,3},{16,24},{17,9... | collective-permute-start | bytes 368648 | tf_op jit(solution)/shard_map/ppermute | solution.py:91
  16.3 1.3 %collective-permute-start.12 = (bf16[96,640]{1,0:T(8,128)(2,1)S(1)}, bf16[96,640]{1,0:T(8,128)(2,1)S(1)}, u32[]{:S(2)}, u32[]{:S(2)}) collective-permute-start(bf16[96,640]{1,0:T(8,128)(2,1)S(1)} %collective-permute-done.11.refs_5_), channel_id=1, source_target_pairs={{0,4},{1,9},{2,6},{3,11},{8,0},{9,17},{10,2},{11,19},{16,8},{17,25... | collective-permute-start | bytes 368648 | tf_op jit(solution)/shard_map/ppermute | solution.py:91
  18.1 1.2 %collective-permute-start.15 = (bf16[96,640]{1,0:T(8,128)(2,1)S(1)}, bf16[96,640]{1,0:T(8,128)(2,1)S(1)}, u32[]{:S(2)}, u32[]{:S(2)}) collective-permute-start(bf16[96,640]{1,0:T(8,128)(2,1)S(1)} %collective-permute-done.14.refs_9_), channel_id=1, source_target_pairs={{0,8},{1,5},{2,10},{3,7},{8,16},{9,1},{10,18},{11,3},{16,24},{17,9... | collective-permute-start | bytes 368648 | tf_op jit(solution)/shard_map/ppermute | solution.py:91
  19.3 1.3 %collective-permute-start.3 = (bf16[96,640]{1,0:T(8,128)(2,1)S(1)}, bf16[96,640]{1,0:T(8,128)(2,1)S(1)}, u32[]{:S(2)}, u32[]{:S(2)}) collective-permute-start(bf16[96,640]{1,0:T(8,128)(2,1)S(1)} %collective-permute-done.2.refs_3_), channel_id=1, source_target_pairs={{0,8},{1,5},{2,10},{3,7},{8,16},{9,1},{10,18},{11,3},{16,24},{17,9... | collective-permute-start | bytes 368648 | tf_op jit(solution)/shard_map/ppermute | solution.py:91
  21.4 1.3 %collective-permute-start.18 = (bf16[96,640]{1,0:T(8,128)(2,1)S(1)}, bf16[96,640]{1,0:T(8,128)(2,1)S(1)}, u32[]{:S(2)}, u32[]{:S(2)}) collective-permute-start(bf16[96,640]{1,0:T(8,128)(2,1)S(1)} %collective-permute-done.17.refs_12_), channel_id=1, source_target_pairs={{0,4},{1,9},{2,6},{3,11},{8,0},{9,17},{10,2},{11,19},{16,8},{17,25... | collective-permute-start | bytes 368648 | tf_op jit(solution)/shard_map/ppermute | solution.py:91
  24.7 1.2 %collective-permute-done.3.refs_4_ = bf16[96,640]{1,0:T(8,128)(2,1)S(1)} collective-permute-done((bf16[96,640]{1,0:T(8,128)(2,1)S(1)}, bf16[96,640]{1,0:T(8,128)(2,1)S(1)}, u32[]{:S(2)}, u32[]{:S(2)}) %collective-permute-start.3) | collective-permute-done | bytes 122912 | tf_op jit(solution)/shard_map/ppermute | solution.py:91
  26.8 1.2 %collective-permute-done.9.refs_3_ = bf16[96,640]{1,0:T(8,128)(2,1)S(1)} collective-permute-done((bf16[96,640]{1,0:T(8,128)(2,1)S(1)}, bf16[96,640]{1,0:T(8,128)(2,1)S(1)}, u32[]{:S(2)}, u32[]{:S(2)}) %collective-permute-start.9) | collective-permute-done | bytes 122912 | tf_op jit(solution)/shard_map/ppermute | solution.py:91
  28.0 4.6 %shard_map.39 = (f32[5,8,96,128]{3,2,1,0:T(8,128)S(1)}, f32[5,8,96,128]{3,2,1,0:T(8,128)S(1)}, f32[5,8,96,128]{3,2,1,0:T(8,128)S(1)}) custom-call(s32[5]{0:T(128)S(1)} %stack.23.at_ref, bf16[8,96,640]{2,1,0:T(8,128)(2,1)S(1)} %shard_map.37.rows_ref, bf16[96,640]{1,0:T(8,128)(2,1)S(1)} %get-tuple-element.10.refs_0_, ...), custom_call_target="tpu_custom_call" | custom-call | flops 1321205760 | tf_op jit(solution)/shard_map/pallas_call | solution.py:244
  32.6 2.0 %shard_map.40 = bf16[384,640]{1,0:T(8,128)(2,1)S(1)} custom-call(s32[5]{0:T(128)S(1)} %stack.23.at_ref, bf16[8,96,640]{2,1,0:T(8,128)(2,1)S(1)} %shard_map.37.rows_ref, f32[5,8,96,128]{3,2,1,0:T(8,128)S(1)} %get-tuple-element.12.mixed_ref, f32[5,8,96,128]{3,2,1,0:T(8,128)S(1)} %get-tuple-element.13.sum_ref, f32[5,8,96,128]{3,2,1,0:T(8,128)S(1)} %get-tuple-element.14.top_ref, ...), custom_call_target="tpu_custom_call" | custom-call | flops 314572800 | tf_op jit(solution)/shard_map/pallas_call | solution.py:244
  34.6 3.2 %collective-permute-start.21 = (bf16[2,192,640]{2,1,0:T(8,128)(2,1)S(1)}, bf16[2,192,640]{2,1,0:T(8,128)(2,1)S(1)}, u32[]{:S(2)}, u32[]{:S(2)}) collective-permute-start(bf16[2,192,640]{2,1,0:T(8,128)(2,1)S(1)} %bitcast.16), channel_id=1, source_target_pairs={{0,1},{1,0},{2,3},{3,2},{4,5},{5,4},{6,7},{7,6},{8,9},{9,8},{10,11... | collective-permute-start | bytes 1474568 | tf_op jit(solution)/shard_map/ppermute | solution.py:289
  37.8 1.3 %shard_map.41 = f32[192,640]{1,0:T(8,128)S(1)} custom-call(s32[5]{0:T(128)S(1)} %stack.23.at_ref, bf16[8,96,640]{2,1,0:T(8,128)(2,1)S(1)} %shard_map.37.rows_ref, f32[5,8,96,128]{3,2,1,0:T(8,128)S(1)} %get-tuple-element.12.mixed_ref, f32[5,8,96,128]{3,2,1,0:T(8,128)S(1)} %get-tuple-element.13.sum_ref, f32[5,8,96,128]{3,2,1,0:T(8,128)S(1)} %get-tuple-element.14.top_ref, ...), custom_call_target="tpu_custom_call" | custom-call | flops 314572800 | tf_op jit(solution)/shard_map/pallas_call | solution.py:244
  39.6 1.2 %collective-permute-start.22 = (bf16[96,640]{1,0:T(8,128)(2,1)S(1)}, bf16[96,640]{1,0:T(8,128)(2,1)S(1)}, u32[]{:S(2)}, u32[]{:S(2)}) collective-permute-start(bf16[96,640]{1,0:T(8,128)(2,1)S(1)} %get-tuple-element.16.refs_0_), channel_id=1, source_target_pairs={{0,2},{1,3},{2,0},{3,1},{4,6},{5,7},{6,4},{7,5},{8,10},{9,11},{10,... | collective-permute-start | bytes 368648 | tf_op jit(solution)/shard_map/ppermute | solution.py:293
  40.8 1.3 %shard_map.42.kept_ref = f32[192,640]{1,0:T(8,128)S(1)} custom-call(s32[5]{0:T(128)S(1)} %stack.23.at_ref, bf16[8,96,640]{2,1,0:T(8,128)(2,1)S(1)} %shard_map.37.rows_ref, f32[5,8,96,128]{3,2,1,0:T(8,128)S(1)} %get-tuple-element.12.mixed_ref, f32[5,8,96,128]{3,2,1,0:T(8,128)S(1)} %get-tuple-element.13.sum_ref, ...), custom_call_target="tpu_custom_call" | custom-call | flops 314572800 | tf_op jit(solution)/shard_map/pallas_call | solution.py:244
  42.2 1.7 %collective-permute-done.24.from_x_ref = bf16[96,640]{1,0:T(8,128)(2,1)S(1)} collective-permute-done((bf16[96,640]{1,0:T(8,128)(2,1)S(1)}, bf16[96,640]{1,0:T(8,128)(2,1)S(1)}, u32[]{:S(2)}, u32[]{:S(2)}) %collective-permute-start.24) | collective-permute-done | bytes 122912 | tf_op jit(solution)/shard_map/ppermute | solution.py:293
  43.9 5.0 %collective-permute-start.25 = (bf16[96,640]{1,0:T(8,128)(2,1)S(1)}, bf16[96,640]{1,0:T(8,128)(2,1)S(1)}, u32[]{:S(2)}, u32[]{:S(2)}) collective-permute-start(bf16[96,640]{1,0:T(8,128)(2,1)S(1)} %shard_map.44), channel_id=1, source_target_pairs={{0,8},{1,28},{2,0},{3,20},{4,24},{5,12},{6,16},{7,4},{8,25},{9,5},... | collective-permute-start | bytes 368648 | tf_op jit(solution)/shard_map/ppermute | solution.py:305
  49.0 1.7 %collective-permute-start.23 = (bf16[96,640]{1,0:T(8,128)(2,1)S(1)}, bf16[96,640]{1,0:T(8,128)(2,1)S(1)}, u32[]{:S(2)}, u32[]{:S(2)}) collective-permute-start(bf16[96,640]{1,0:T(8,128)(2,1)S(1)} %shard_map.43), channel_id=1, source_target_pairs={{0,24},{1,12},{2,16},{3,4},{4,8},{5,28},{6,0},{7,20},{8,1},{9,29},... | collective-permute-start | bytes 368648 | tf_op jit(solution)/shard_map/ppermute | solution.py:305
  50.7 1.2 %collective-permute-done.25 = bf16[96,640]{1,0:T(8,128)(2,1)S(1)} collective-permute-done((bf16[96,640]{1,0:T(8,128)(2,1)S(1)}, bf16[96,640]{1,0:T(8,128)(2,1)S(1)}, u32[]{:S(2)}, u32[]{:S(2)}) %collective-permute-start.25) | collective-permute-done | bytes 122912 | tf_op jit(solution)/shard_map/ppermute | solution.py:305
  51.9 3.6 %collective-permute-done.23 = bf16[96,640]{1,0:T(8,128)(2,1)S(1)} collective-permute-done((bf16[96,640]{1,0:T(8,128)(2,1)S(1)}, bf16[96,640]{1,0:T(8,128)(2,1)S(1)}, u32[]{:S(2)}, u32[]{:S(2)}) %collective-permute-start.23) | collective-permute-done | bytes 122912 | tf_op jit(solution)/shard_map/ppermute | solution.py:305
  (46 shorter events, 13.0 us)
Async XLA Ops:
  0.0 5.3 %collective-permute-start = (bf16[96,640]{1,0:T(8,128)(2,1)}, bf16[96,640]{1,0:T(8,128)(2,1)S(1)}, u32[]{:S(2)}, u32[]{:S(2)}) collective-permute-start(bf16[96,640]{1,0:T(8,128)(2,1)} %refs_0_.1), channel_id=1, source_target_pairs={{0,8},{1,5},{2,10},{3,7},{8,16},{9,1},{10,18},{11,3},{16,24},{17,9... | collective-permute-start | bytes 368648 | tf_op jit(solution)/shard_map/ppermute | solution.py:91
  1.2 5.4 %collective-permute-start.4 = (bf16[96,640]{1,0:T(8,128)(2,1)}, bf16[96,640]{1,0:T(8,128)(2,1)S(1)}, u32[]{:S(2)}, u32[]{:S(2)}) collective-permute-start(bf16[96,640]{1,0:T(8,128)(2,1)} %refs_0_.1), channel_id=1, source_target_pairs={{0,4},{1,9},{2,6},{3,11},{8,0},{9,17},{10,2},{11,19},{16,8},{17,25... | collective-permute-start | bytes 368648 | tf_op jit(solution)/shard_map/ppermute | solution.py:91
  2.4 5.6 %collective-permute-start.10 = (bf16[96,640]{1,0:T(8,128)(2,1)S(1)}, bf16[96,640]{1,0:T(8,128)(2,1)S(1)}, u32[]{:S(2)}, u32[]{:S(2)}) collective-permute-start(bf16[96,640]{1,0:T(8,128)(2,1)S(1)} %get-tuple-element.10.refs_0_), channel_id=1, source_target_pairs={{0,4},{1,9},{2,6},{3,11},{8,0},{9,17},{10,2},{11,19},{16,8},{17,25... | collective-permute-start | bytes 368648 | tf_op jit(solution)/shard_map/ppermute | solution.py:91
  3.8 5.3 %collective-permute-start.13 = (bf16[96,640]{1,0:T(8,128)(2,1)S(1)}, bf16[96,640]{1,0:T(8,128)(2,1)S(1)}, u32[]{:S(2)}, u32[]{:S(2)}) collective-permute-start(bf16[96,640]{1,0:T(8,128)(2,1)S(1)} %get-tuple-element.11.refs_7_), channel_id=1, source_target_pairs={{0,8},{1,5},{2,10},{3,7},{8,16},{9,1},{10,18},{11,3},{16,24},{17,9... | collective-permute-start | bytes 368648 | tf_op jit(solution)/shard_map/ppermute | solution.py:91
  4.0 6.5 %collective-permute-start.16 = (bf16[96,640]{1,0:T(8,128)(2,1)S(1)}, bf16[96,640]{1,0:T(8,128)(2,1)S(1)}, u32[]{:S(2)}, u32[]{:S(2)}) collective-permute-start(bf16[96,640]{1,0:T(8,128)(2,1)S(1)} %get-tuple-element.11.refs_7_), channel_id=1, source_target_pairs={{0,4},{1,9},{2,6},{3,11},{8,0},{9,17},{10,2},{11,19},{16,8},{17,25... | collective-permute-start | bytes 368648 | tf_op jit(solution)/shard_map/ppermute | solution.py:91
  5.3 6.5 %collective-permute-start.7 = (bf16[96,640]{1,0:T(8,128)(2,1)S(1)}, bf16[96,640]{1,0:T(8,128)(2,1)S(1)}, u32[]{:S(2)}, u32[]{:S(2)}) collective-permute-start(bf16[96,640]{1,0:T(8,128)(2,1)S(1)} %get-tuple-element.10.refs_0_), channel_id=1, source_target_pairs={{0,8},{1,5},{2,10},{3,7},{8,16},{9,1},{10,18},{11,3},{16,24},{17,9... | collective-permute-start | bytes 368648 | tf_op jit(solution)/shard_map/ppermute | solution.py:91
  6.7 6.8 %collective-permute-start.1 = (bf16[96,640]{1,0:T(8,128)(2,1)S(1)}, bf16[96,640]{1,0:T(8,128)(2,1)S(1)}, u32[]{:S(2)}, u32[]{:S(2)}) collective-permute-start(bf16[96,640]{1,0:T(8,128)(2,1)S(1)} %collective-permute-done.refs_1_), channel_id=1, source_target_pairs={{0,8},{1,5},{2,10},{3,7},{8,16},{9,1},{10,18},{11,3},{16,24},{17,9... | collective-permute-start | bytes 368648 | tf_op jit(solution)/shard_map/ppermute | solution.py:91
  8.0 5.7 %collective-permute-start.5 = (bf16[96,640]{1,0:T(8,128)(2,1)S(1)}, bf16[96,640]{1,0:T(8,128)(2,1)S(1)}, u32[]{:S(2)}, u32[]{:S(2)}) collective-permute-start(bf16[96,640]{1,0:T(8,128)(2,1)S(1)} %collective-permute-done.4.refs_7_), channel_id=1, source_target_pairs={{0,4},{1,9},{2,6},{3,11},{8,0},{9,17},{10,2},{11,19},{16,8},{17,25... | collective-permute-start | bytes 368648 | tf_op jit(solution)/shard_map/ppermute | solution.py:91
  9.1 6.8 %collective-permute-start.11 = (bf16[96,640]{1,0:T(8,128)(2,1)S(1)}, bf16[96,640]{1,0:T(8,128)(2,1)S(1)}, u32[]{:S(2)}, u32[]{:S(2)}) collective-permute-start(bf16[96,640]{1,0:T(8,128)(2,1)S(1)} %collective-permute-done.10.refs_6_), channel_id=1, source_target_pairs={{0,4},{1,9},{2,6},{3,11},{8,0},{9,17},{10,2},{11,19},{16,8},{17,25... | collective-permute-start | bytes 368648 | tf_op jit(solution)/shard_map/ppermute | solution.py:91
  10.4 5.9 %collective-permute-start.14 = (bf16[96,640]{1,0:T(8,128)(2,1)S(1)}, bf16[96,640]{1,0:T(8,128)(2,1)S(1)}, u32[]{:S(2)}, u32[]{:S(2)}) collective-permute-start(bf16[96,640]{1,0:T(8,128)(2,1)S(1)} %collective-permute-done.13.refs_8_), channel_id=1, source_target_pairs={{0,8},{1,5},{2,10},{3,7},{8,16},{9,1},{10,18},{11,3},{16,24},{17,9... | collective-permute-start | bytes 368648 | tf_op jit(solution)/shard_map/ppermute | solution.py:91
  11.7 6.4 %collective-permute-start.17 = (bf16[96,640]{1,0:T(8,128)(2,1)S(1)}, bf16[96,640]{1,0:T(8,128)(2,1)S(1)}, u32[]{:S(2)}, u32[]{:S(2)}) collective-permute-start(bf16[96,640]{1,0:T(8,128)(2,1)S(1)} %collective-permute-done.16.refs_13_), channel_id=1, source_target_pairs={{0,4},{1,9},{2,6},{3,11},{8,0},{9,17},{10,2},{11,19},{16,8},{17,25... | collective-permute-start | bytes 368648 | tf_op jit(solution)/shard_map/ppermute | solution.py:91
  13.5 5.8 %collective-permute-start.2 = (bf16[96,640]{1,0:T(8,128)(2,1)S(1)}, bf16[96,640]{1,0:T(8,128)(2,1)S(1)}, u32[]{:S(2)}, u32[]{:S(2)}) collective-permute-start(bf16[96,640]{1,0:T(8,128)(2,1)S(1)} %collective-permute-done.1.refs_2_), channel_id=1, source_target_pairs={{0,8},{1,5},{2,10},{3,7},{8,16},{9,1},{10,18},{11,3},{16,24},{17,9... | collective-permute-start | bytes 368648 | tf_op jit(solution)/shard_map/ppermute | solution.py:91
  13.7 7.7 %collective-permute-start.8 = (bf16[96,640]{1,0:T(8,128)(2,1)S(1)}, bf16[96,640]{1,0:T(8,128)(2,1)S(1)}, u32[]{:S(2)}, u32[]{:S(2)}) collective-permute-start(bf16[96,640]{1,0:T(8,128)(2,1)S(1)} %collective-permute-done.7.refs_1_), channel_id=1, source_target_pairs={{0,8},{1,5},{2,10},{3,7},{8,16},{9,1},{10,18},{11,3},{16,24},{17,9... | collective-permute-start | bytes 368648 | tf_op jit(solution)/shard_map/ppermute | solution.py:91
  15.9 6.8 %collective-permute-start.6 = (bf16[96,640]{1,0:T(8,128)(2,1)S(1)}, bf16[96,640]{1,0:T(8,128)(2,1)S(1)}, u32[]{:S(2)}, u32[]{:S(2)}) collective-permute-start(bf16[96,640]{1,0:T(8,128)(2,1)S(1)} %collective-permute-done.5.refs_6_), channel_id=1, source_target_pairs={{0,4},{1,9},{2,6},{3,11},{8,0},{9,17},{10,2},{11,19},{16,8},{17,25... | collective-permute-start | bytes 368648 | tf_op jit(solution)/shard_map/ppermute | solution.py:91
  16.3 6.9 %collective-permute-start.12 = (bf16[96,640]{1,0:T(8,128)(2,1)S(1)}, bf16[96,640]{1,0:T(8,128)(2,1)S(1)}, u32[]{:S(2)}, u32[]{:S(2)}) collective-permute-start(bf16[96,640]{1,0:T(8,128)(2,1)S(1)} %collective-permute-done.11.refs_5_), channel_id=1, source_target_pairs={{0,4},{1,9},{2,6},{3,11},{8,0},{9,17},{10,2},{11,19},{16,8},{17,25... | collective-permute-start | bytes 368648 | tf_op jit(solution)/shard_map/ppermute | solution.py:91
  18.1 6.2 %collective-permute-start.15 = (bf16[96,640]{1,0:T(8,128)(2,1)S(1)}, bf16[96,640]{1,0:T(8,128)(2,1)S(1)}, u32[]{:S(2)}, u32[]{:S(2)}) collective-permute-start(bf16[96,640]{1,0:T(8,128)(2,1)S(1)} %collective-permute-done.14.refs_9_), channel_id=1, source_target_pairs={{0,8},{1,5},{2,10},{3,7},{8,16},{9,1},{10,18},{11,3},{16,24},{17,9... | collective-permute-start | bytes 368648 | tf_op jit(solution)/shard_map/ppermute | solution.py:91
  19.3 6.5 %collective-permute-start.3 = (bf16[96,640]{1,0:T(8,128)(2,1)S(1)}, bf16[96,640]{1,0:T(8,128)(2,1)S(1)}, u32[]{:S(2)}, u32[]{:S(2)}) collective-permute-start(bf16[96,640]{1,0:T(8,128)(2,1)S(1)} %collective-permute-done.2.refs_3_), channel_id=1, source_target_pairs={{0,8},{1,5},{2,10},{3,7},{8,16},{9,1},{10,18},{11,3},{16,24},{17,9... | collective-permute-start | bytes 368648 | tf_op jit(solution)/shard_map/ppermute | solution.py:91
  21.4 5.4 %collective-permute-start.18 = (bf16[96,640]{1,0:T(8,128)(2,1)S(1)}, bf16[96,640]{1,0:T(8,128)(2,1)S(1)}, u32[]{:S(2)}, u32[]{:S(2)}) collective-permute-start(bf16[96,640]{1,0:T(8,128)(2,1)S(1)} %collective-permute-done.17.refs_12_), channel_id=1, source_target_pairs={{0,4},{1,9},{2,6},{3,11},{8,0},{9,17},{10,2},{11,19},{16,8},{17,25... | collective-permute-start | bytes 368648 | tf_op jit(solution)/shard_map/ppermute | solution.py:91
  22.7 5.3 %collective-permute-start.9 = (bf16[96,640]{1,0:T(8,128)(2,1)S(1)}, bf16[96,640]{1,0:T(8,128)(2,1)S(1)}, u32[]{:S(2)}, u32[]{:S(2)}) collective-permute-start(bf16[96,640]{1,0:T(8,128)(2,1)S(1)} %collective-permute-done.8.refs_2_), channel_id=1, source_target_pairs={{0,8},{1,5},{2,10},{3,7},{8,16},{9,1},{10,18},{11,3},{16,24},{17,9... | collective-permute-start | bytes 368648 | tf_op jit(solution)/shard_map/ppermute | solution.py:91
  23.2 9.4 %collective-permute-start.19 = (bf16[96,640]{1,0:T(8,128)(2,1)S(1)}, bf16[96,640]{1,0:T(8,128)(2,1)S(1)}, u32[]{:S(2)}, u32[]{:S(2)}) collective-permute-start(bf16[96,640]{1,0:T(8,128)(2,1)S(1)} %collective-permute-done.12.refs_4_), channel_id=1, source_target_pairs={{0,4},{1,9},{2,6},{3,11},{8,0},{9,17},{10,2},{11,19},{16,8},{17,25... | collective-permute-start | bytes 368648 | tf_op jit(solution)/shard_map/ppermute | solution.py:91
  24.3 8.3 %collective-permute-start.20 = (bf16[96,640]{1,0:T(8,128)(2,1)S(1)}, bf16[96,640]{1,0:T(8,128)(2,1)S(1)}, u32[]{:S(2)}, u32[]{:S(2)}) collective-permute-start(bf16[96,640]{1,0:T(8,128)(2,1)S(1)} %collective-permute-done.15.refs_10_), channel_id=1, source_target_pairs={{0,8},{1,5},{2,10},{3,7},{8,16},{9,1},{10,18},{11,3},{16,24},{17,9... | collective-permute-start | bytes 368648 | tf_op jit(solution)/shard_map/ppermute | solution.py:91
  39.6 9.3 %collective-permute-start.22 = (bf16[96,640]{1,0:T(8,128)(2,1)S(1)}, bf16[96,640]{1,0:T(8,128)(2,1)S(1)}, u32[]{:S(2)}, u32[]{:S(2)}) collective-permute-start(bf16[96,640]{1,0:T(8,128)(2,1)S(1)} %get-tuple-element.16.refs_0_), channel_id=1, source_target_pairs={{0,2},{1,3},{2,0},{3,1},{4,6},{5,7},{6,4},{7,5},{8,10},{9,11},{10,... | collective-permute-start | bytes 368648 | tf_op jit(solution)/shard_map/ppermute | solution.py:293
  43.9 8.0 %collective-permute-start.25 = (bf16[96,640]{1,0:T(8,128)(2,1)S(1)}, bf16[96,640]{1,0:T(8,128)(2,1)S(1)}, u32[]{:S(2)}, u32[]{:S(2)}) collective-permute-start(bf16[96,640]{1,0:T(8,128)(2,1)S(1)} %shard_map.44), channel_id=1, source_target_pairs={{0,8},{1,28},{2,0},{3,20},{4,24},{5,12},{6,16},{7,4},{8,25},{9,5},... | collective-permute-start | bytes 368648 | tf_op jit(solution)/shard_map/ppermute | solution.py:305
  49.0 6.5 %collective-permute-start.23 = (bf16[96,640]{1,0:T(8,128)(2,1)S(1)}, bf16[96,640]{1,0:T(8,128)(2,1)S(1)}, u32[]{:S(2)}, u32[]{:S(2)}) collective-permute-start(bf16[96,640]{1,0:T(8,128)(2,1)S(1)} %shard_map.43), channel_id=1, source_target_pairs={{0,24},{1,12},{2,16},{3,4},{4,8},{5,28},{6,0},{7,20},{8,1},{9,29},... | collective-permute-start | bytes 368648 | tf_op jit(solution)/shard_map/ppermute | solution.py:305
  (5 other events, 16.9 us)

commit v30 on v28

--- a/solution.py
+++ b/solution.py
@@ -181,8 +181,7 @@
         now = later
 
 
-def split_kernel(queries_ref, kv_ref, copy_ref, keys_ref, values_ref):
-    copy_ref[...] = queries_ref[...]
+def split_kernel(kv_ref, keys_ref, values_ref):
     keys_ref[...] = kv_ref[0]
     values_ref[...] = kv_ref[1]
 
@@ -268,9 +267,8 @@
     heads = width // HD
     f32, bf16 = jnp.float32, jnp.bfloat16
     block = (queries.shape, bf16)
-    own_queries, *own = call(split_kernel, (), [queries, keys_values], [block] * 3, 0)
+    own = call(split_kernel, (), [keys_values], [block, block], 0)
     queries, keys, values = gather_ring([queries, *own], n)
-    queries = [own_queries, *queries[1:]]
     (rows,) = call(functools.partial(rows_kernel, n), (), queries, [((n, ROWS, width), bf16)], 0)
     far = n // 2
     state = call(

time: 57.1 us -> 56.9 us (level)
  waiting for transfers between devices: 16.5 us -> 15.1 us
  starting transfers between devices: 28 us -> 29.4 us
    ppermute x21, waiting for transfers between devices: 9.83 us -> 8.01 us  [hop(): return lax.ppermute(x, ('frames', 'heads'), pairs)]
    ppermute x21, starting transfers between devices: 16.6 us -> 17.9 us  [hop(): return lax.ppermute(x, ('frames', 'heads'), pairs)]
where the time goes in v30:
time: 56.9 us; the launch traced here: 56.7 us
  starting transfers between devices  29.4 us (52%)
  waiting for transfers between devices  15.1 us (27%)
  Pallas kernels  9.37 us (16%)
  local copies, waits for them, and re-layouts  1.94 us (3%)
  other arithmetic  0.79 us (1%)
    ppermute x21, starting transfers between devices, hop(): return lax.ppermute(x, ('frames', 'heads'), pairs)  17.9 us
    pallas_call x8, Pallas kernels, call(): pl.pallas_call(kernel, out_shape=[jax.ShapeDtypeStruct(shape, dtype) for...  9.37 us
    ppermute x21, waiting for transfers between devices, hop(): return lax.ppermute(x, ('frames', 'heads'), pairs)  8.01 us
    ppermute x2, starting transfers between devices, on_device_ring(): arrived.append(lax.ppermute(total, ('frames', 'heads'), pairs))  6.75 us
    ppermute x2, waiting for transfers between devices, on_device_ring(): arrived.append(lax.ppermute(total, ('frames', 'heads'), pairs))  5.33 us
    ppermute x1, starting transfers between devices, on_device_ring(): from_core = lax.ppermute(given, 'heads', [(h, h ^ 1) for h in range(4)])  3.17 us
    unnamed x6, local copies, waits for them, and re-layouts  1.85 us
    ppermute x2, waiting for transfers between devices, on_device_ring(): lax.ppermute(block, 'heads', [(h, h ^ 2) for h in range(4)])  1.67 us
  transfers between devices with their start and end apart: 26, of which 15 were waited for; matrix products, arithmetic and copies ran while one was open for 0% of the time, Pallas kernels for 13%

profile of v30, /device:TPU:3, one launch (start us, length us, event | category | flops | bytes accessed | tf_op | source)
XLA Modules:
  0.0 56.7 jit_solution(13237997303984076902)
XLA Ops:
  0.0 1.2 %collective-permute-start = (bf16[96,640]{1,0:T(8,128)(2,1)}, bf16[96,640]{1,0:T(8,128)(2,1)S(1)}, u32[]{:S(2)}, u32[]{:S(2)}) collective-permute-start(bf16[96,640]{1,0:T(8,128)(2,1)} %refs_0_.1), channel_id=1, source_target_pairs={{0,8},{1,5},{2,10},{3,7},{8,16},{9,1},{10,18},{11,3},{16,24},{17,9... | collective-permute-start | bytes 368648 | tf_op jit(solution)/shard_map/ppermute | solution.py:91
  2.4 1.3 %collective-permute-start.10 = (bf16[96,640]{1,0:T(8,128)(2,1)S(1)}, bf16[96,640]{1,0:T(8,128)(2,1)S(1)}, u32[]{:S(2)}, u32[]{:S(2)}) collective-permute-start(bf16[96,640]{1,0:T(8,128)(2,1)S(1)} %get-tuple-element.10.refs_0_), channel_id=1, source_target_pairs={{0,4},{1,9},{2,6},{3,11},{8,0},{9,17},{10,2},{11,19},{16,8},{17,25... | collective-permute-start | bytes 368648 | tf_op jit(solution)/shard_map/ppermute | solution.py:91
  4.0 1.3 %collective-permute-start.16 = (bf16[96,640]{1,0:T(8,128)(2,1)S(1)}, bf16[96,640]{1,0:T(8,128)(2,1)S(1)}, u32[]{:S(2)}, u32[]{:S(2)}) collective-permute-start(bf16[96,640]{1,0:T(8,128)(2,1)S(1)} %get-tuple-element.11.refs_7_), channel_id=1, source_target_pairs={{0,4},{1,9},{2,6},{3,11},{8,0},{9,17},{10,2},{11,19},{16,8},{17,25... | collective-permute-start | bytes 368648 | tf_op jit(solution)/shard_map/ppermute | solution.py:91
  5.5 1.2 %collective-permute-done.4.refs_7_ = bf16[96,640]{1,0:T(8,128)(2,1)S(1)} collective-permute-done((bf16[96,640]{1,0:T(8,128)(2,1)}, bf16[96,640]{1,0:T(8,128)(2,1)S(1)}, u32[]{:S(2)}, u32[]{:S(2)}) %collective-permute-start.4) | collective-permute-done | bytes 122912 | tf_op jit(solution)/shard_map/ppermute | solution.py:91
  9.1 1.3 %collective-permute-start.11 = (bf16[96,640]{1,0:T(8,128)(2,1)S(1)}, bf16[96,640]{1,0:T(8,128)(2,1)S(1)}, u32[]{:S(2)}, u32[]{:S(2)}) collective-permute-start(bf16[96,640]{1,0:T(8,128)(2,1)S(1)} %collective-permute-done.10.refs_6_), channel_id=1, source_target_pairs={{0,4},{1,9},{2,6},{3,11},{8,0},{9,17},{10,2},{11,19},{16,8},{17,25... | collective-permute-start | bytes 368648 | tf_op jit(solution)/shard_map/ppermute | solution.py:91
  11.7 1.3 %collective-permute-start.17 = (bf16[96,640]{1,0:T(8,128)(2,1)S(1)}, bf16[96,640]{1,0:T(8,128)(2,1)S(1)}, u32[]{:S(2)}, u32[]{:S(2)}) collective-permute-start(bf16[96,640]{1,0:T(8,128)(2,1)S(1)} %collective-permute-done.16.refs_13_), channel_id=1, source_target_pairs={{0,4},{1,9},{2,6},{3,11},{8,0},{9,17},{10,2},{11,19},{16,8},{17,25... | collective-permute-start | bytes 368648 | tf_op jit(solution)/shard_map/ppermute | solution.py:91
  13.7 1.2 %collective-permute-start.8 = (bf16[96,640]{1,0:T(8,128)(2,1)S(1)}, bf16[96,640]{1,0:T(8,128)(2,1)S(1)}, u32[]{:S(2)}, u32[]{:S(2)}) collective-permute-start(bf16[96,640]{1,0:T(8,128)(2,1)S(1)} %collective-permute-done.7.refs_1_), channel_id=1, source_target_pairs={{0,8},{1,5},{2,10},{3,7},{8,16},{9,1},{10,18},{11,3},{16,24},{17,9... | collective-permute-start | bytes 368648 | tf_op jit(solution)/shard_map/ppermute | solution.py:91
  16.3 1.3 %collective-permute-start.12 = (bf16[96,640]{1,0:T(8,128)(2,1)S(1)}, bf16[96,640]{1,0:T(8,128)(2,1)S(1)}, u32[]{:S(2)}, u32[]{:S(2)}) collective-permute-start(bf16[96,640]{1,0:T(8,128)(2,1)S(1)} %collective-permute-done.11.refs_5_), channel_id=1, source_target_pairs={{0,4},{1,9},{2,6},{3,11},{8,0},{9,17},{10,2},{11,19},{16,8},{17,25... | collective-permute-start | bytes 368648 | tf_op jit(solution)/shard_map/ppermute | solution.py:91
  18.1 1.2 %collective-permute-start.15 = (bf16[96,640]{1,0:T(8,128)(2,1)S(1)}, bf16[96,640]{1,0:T(8,128)(2,1)S(1)}, u32[]{:S(2)}, u32[]{:S(2)}) collective-permute-start(bf16[96,640]{1,0:T(8,128)(2,1)S(1)} %collective-permute-done.14.refs_9_), channel_id=1, source_target_pairs={{0,8},{1,5},{2,10},{3,7},{8,16},{9,1},{10,18},{11,3},{16,24},{17,9... | collective-permute-start | bytes 368648 | tf_op jit(solution)/shard_map/ppermute | solution.py:91
  19.3 1.3 %collective-permute-start.3 = (bf16[96,640]{1,0:T(8,128)(2,1)S(1)}, bf16[96,640]{1,0:T(8,128)(2,1)S(1)}, u32[]{:S(2)}, u32[]{:S(2)}) collective-permute-start(bf16[96,640]{1,0:T(8,128)(2,1)S(1)} %collective-permute-done.2.refs_3_), channel_id=1, source_target_pairs={{0,8},{1,5},{2,10},{3,7},{8,16},{9,1},{10,18},{11,3},{16,24},{17,9... | collective-permute-start | bytes 368648 | tf_op jit(solution)/shard_map/ppermute | solution.py:91
  21.4 1.3 %collective-permute-start.18 = (bf16[96,640]{1,0:T(8,128)(2,1)S(1)}, bf16[96,640]{1,0:T(8,128)(2,1)S(1)}, u32[]{:S(2)}, u32[]{:S(2)}) collective-permute-start(bf16[96,640]{1,0:T(8,128)(2,1)S(1)} %collective-permute-done.17.refs_12_), channel_id=1, source_target_pairs={{0,4},{1,9},{2,6},{3,11},{8,0},{9,17},{10,2},{11,19},{16,8},{17,25... | collective-permute-start | bytes 368648 | tf_op jit(solution)/shard_map/ppermute | solution.py:91
  24.7 1.2 %collective-permute-done.3.refs_4_ = bf16[96,640]{1,0:T(8,128)(2,1)S(1)} collective-permute-done((bf16[96,640]{1,0:T(8,128)(2,1)S(1)}, bf16[96,640]{1,0:T(8,128)(2,1)S(1)}, u32[]{:S(2)}, u32[]{:S(2)}) %collective-permute-start.3) | collective-permute-done | bytes 122912 | tf_op jit(solution)/shard_map/ppermute | solution.py:91
  26.8 1.2 %collective-permute-done.9.refs_3_ = bf16[96,640]{1,0:T(8,128)(2,1)S(1)} collective-permute-done((bf16[96,640]{1,0:T(8,128)(2,1)S(1)}, bf16[96,640]{1,0:T(8,128)(2,1)S(1)}, u32[]{:S(2)}, u32[]{:S(2)}) %collective-permute-start.9) | collective-permute-done | bytes 122912 | tf_op jit(solution)/shard_map/ppermute | solution.py:91
  28.0 4.5 %shard_map.39 = (f32[5,8,96,128]{3,2,1,0:T(8,128)S(1)}, f32[5,8,96,128]{3,2,1,0:T(8,128)S(1)}, f32[5,8,96,128]{3,2,1,0:T(8,128)S(1)}) custom-call(s32[5]{0:T(128)S(1)} %stack.23.at_ref, bf16[8,96,640]{2,1,0:T(8,128)(2,1)S(1)} %shard_map.37.rows_ref, bf16[96,640]{1,0:T(8,128)(2,1)S(1)} %get-tuple-element.10.refs_0_, ...), custom_call_target="tpu_custom_call" | custom-call | flops 1321205760 | tf_op jit(solution)/shard_map/pallas_call | solution.py:249
  32.6 2.0 %shard_map.40 = bf16[384,640]{1,0:T(8,128)(2,1)S(1)} custom-call(s32[5]{0:T(128)S(1)} %stack.23.at_ref, bf16[8,96,640]{2,1,0:T(8,128)(2,1)S(1)} %shard_map.37.rows_ref, f32[5,8,96,128]{3,2,1,0:T(8,128)S(1)} %get-tuple-element.12.mixed_ref, f32[5,8,96,128]{3,2,1,0:T(8,128)S(1)} %get-tuple-element.13.sum_ref, f32[5,8,96,128]{3,2,1,0:T(8,128)S(1)} %get-tuple-element.14.top_ref, ...), custom_call_target="tpu_custom_call" | custom-call | flops 314572800 | tf_op jit(solution)/shard_map/pallas_call | solution.py:249
  34.5 3.2 %collective-permute-start.21 = (bf16[2,192,640]{2,1,0:T(8,128)(2,1)S(1)}, bf16[2,192,640]{2,1,0:T(8,128)(2,1)S(1)}, u32[]{:S(2)}, u32[]{:S(2)}) collective-permute-start(bf16[2,192,640]{2,1,0:T(8,128)(2,1)S(1)} %bitcast.16), channel_id=1, source_target_pairs={{0,1},{1,0},{2,3},{3,2},{4,5},{5,4},{6,7},{7,6},{8,9},{9,8},{10,11... | collective-permute-start | bytes 1474568 | tf_op jit(solution)/shard_map/ppermute | solution.py:294
  37.7 1.4 %shard_map.41 = f32[192,640]{1,0:T(8,128)S(1)} custom-call(s32[5]{0:T(128)S(1)} %stack.23.at_ref, bf16[8,96,640]{2,1,0:T(8,128)(2,1)S(1)} %shard_map.37.rows_ref, f32[5,8,96,128]{3,2,1,0:T(8,128)S(1)} %get-tuple-element.12.mixed_ref, f32[5,8,96,128]{3,2,1,0:T(8,128)S(1)} %get-tuple-element.13.sum_ref, f32[5,8,96,128]{3,2,1,0:T(8,128)S(1)} %get-tuple-element.14.top_ref, ...), custom_call_target="tpu_custom_call" | custom-call | flops 314572800 | tf_op jit(solution)/shard_map/pallas_call | solution.py:249
  39.6 1.2 %collective-permute-start.22 = (bf16[96,640]{1,0:T(8,128)(2,1)S(1)}, bf16[96,640]{1,0:T(8,128)(2,1)S(1)}, u32[]{:S(2)}, u32[]{:S(2)}) collective-permute-start(bf16[96,640]{1,0:T(8,128)(2,1)S(1)} %get-tuple-element.16.refs_0_), channel_id=1, source_target_pairs={{0,2},{1,3},{2,0},{3,1},{4,6},{5,7},{6,4},{7,5},{8,10},{9,11},{10,... | collective-permute-start | bytes 368648 | tf_op jit(solution)/shard_map/ppermute | solution.py:298
  40.8 1.4 %shard_map.42.kept_ref = f32[192,640]{1,0:T(8,128)S(1)} custom-call(s32[5]{0:T(128)S(1)} %stack.23.at_ref, bf16[8,96,640]{2,1,0:T(8,128)(2,1)S(1)} %shard_map.37.rows_ref, f32[5,8,96,128]{3,2,1,0:T(8,128)S(1)} %get-tuple-element.12.mixed_ref, f32[5,8,96,128]{3,2,1,0:T(8,128)S(1)} %get-tuple-element.13.sum_ref, ...), custom_call_target="tpu_custom_call" | custom-call | flops 314572800 | tf_op jit(solution)/shard_map/pallas_call | solution.py:249
  42.1 1.7 %collective-permute-done.24.from_x_ref = bf16[96,640]{1,0:T(8,128)(2,1)S(1)} collective-permute-done((bf16[96,640]{1,0:T(8,128)(2,1)S(1)}, bf16[96,640]{1,0:T(8,128)(2,1)S(1)}, u32[]{:S(2)}, u32[]{:S(2)}) %collective-permute-start.24) | collective-permute-done | bytes 122912 | tf_op jit(solution)/shard_map/ppermute | solution.py:298
  43.9 5.0 %collective-permute-start.25 = (bf16[96,640]{1,0:T(8,128)(2,1)S(1)}, bf16[96,640]{1,0:T(8,128)(2,1)S(1)}, u32[]{:S(2)}, u32[]{:S(2)}) collective-permute-start(bf16[96,640]{1,0:T(8,128)(2,1)S(1)} %shard_map.44), channel_id=1, source_target_pairs={{0,8},{1,28},{2,0},{3,20},{4,24},{5,12},{6,16},{7,4},{8,25},{9,5},... | collective-permute-start | bytes 368648 | tf_op jit(solution)/shard_map/ppermute | solution.py:310
  48.9 1.7 %collective-permute-start.23 = (bf16[96,640]{1,0:T(8,128)(2,1)S(1)}, bf16[96,640]{1,0:T(8,128)(2,1)S(1)}, u32[]{:S(2)}, u32[]{:S(2)}) collective-permute-start(bf16[96,640]{1,0:T(8,128)(2,1)S(1)} %shard_map.43), channel_id=1, source_target_pairs={{0,24},{1,12},{2,16},{3,4},{4,8},{5,28},{6,0},{7,20},{8,1},{9,29},... | collective-permute-start | bytes 368648 | tf_op jit(solution)/shard_map/ppermute | solution.py:310
  50.7 1.5 %collective-permute-done.25 = bf16[96,640]{1,0:T(8,128)(2,1)S(1)} collective-permute-done((bf16[96,640]{1,0:T(8,128)(2,1)S(1)}, bf16[96,640]{1,0:T(8,128)(2,1)S(1)}, u32[]{:S(2)}, u32[]{:S(2)}) %collective-permute-start.25) | collective-permute-done | bytes 122912 | tf_op jit(solution)/shard_map/ppermute | solution.py:310
  52.1 3.9 %collective-permute-done.23 = bf16[96,640]{1,0:T(8,128)(2,1)S(1)} collective-permute-done((bf16[96,640]{1,0:T(8,128)(2,1)S(1)}, bf16[96,640]{1,0:T(8,128)(2,1)S(1)}, u32[]{:S(2)}, u32[]{:S(2)}) %collective-permute-start.23) | collective-permute-done | bytes 122912 | tf_op jit(solution)/shard_map/ppermute | solution.py:310
  (46 shorter events, 13.0 us)
Async XLA Ops:
  0.0 5.3 %collective-permute-start = (bf16[96,640]{1,0:T(8,128)(2,1)}, bf16[96,640]{1,0:T(8,128)(2,1)S(1)}, u32[]{:S(2)}, u32[]{:S(2)}) collective-permute-start(bf16[96,640]{1,0:T(8,128)(2,1)} %refs_0_.1), channel_id=1, source_target_pairs={{0,8},{1,5},{2,10},{3,7},{8,16},{9,1},{10,18},{11,3},{16,24},{17,9... | collective-permute-start | bytes 368648 | tf_op jit(solution)/shard_map/ppermute | solution.py:91
  1.2 5.4 %collective-permute-start.4 = (bf16[96,640]{1,0:T(8,128)(2,1)}, bf16[96,640]{1,0:T(8,128)(2,1)S(1)}, u32[]{:S(2)}, u32[]{:S(2)}) collective-permute-start(bf16[96,640]{1,0:T(8,128)(2,1)} %refs_0_.1), channel_id=1, source_target_pairs={{0,4},{1,9},{2,6},{3,11},{8,0},{9,17},{10,2},{11,19},{16,8},{17,25... | collective-permute-start | bytes 368648 | tf_op jit(solution)/shard_map/ppermute | solution.py:91
  2.4 5.6 %collective-permute-start.10 = (bf16[96,640]{1,0:T(8,128)(2,1)S(1)}, bf16[96,640]{1,0:T(8,128)(2,1)S(1)}, u32[]{:S(2)}, u32[]{:S(2)}) collective-permute-start(bf16[96,640]{1,0:T(8,128)(2,1)S(1)} %get-tuple-element.10.refs_0_), channel_id=1, source_target_pairs={{0,4},{1,9},{2,6},{3,11},{8,0},{9,17},{10,2},{11,19},{16,8},{17,25... | collective-permute-start | bytes 368648 | tf_op jit(solution)/shard_map/ppermute | solution.py:91
  3.8 5.3 %collective-permute-start.13 = (bf16[96,640]{1,0:T(8,128)(2,1)S(1)}, bf16[96,640]{1,0:T(8,128)(2,1)S(1)}, u32[]{:S(2)}, u32[]{:S(2)}) collective-permute-start(bf16[96,640]{1,0:T(8,128)(2,1)S(1)} %get-tuple-element.11.refs_7_), channel_id=1, source_target_pairs={{0,8},{1,5},{2,10},{3,7},{8,16},{9,1},{10,18},{11,3},{16,24},{17,9... | collective-permute-start | bytes 368648 | tf_op jit(solution)/shard_map/ppermute | solution.py:91
  4.0 6.5 %collective-permute-start.16 = (bf16[96,640]{1,0:T(8,128)(2,1)S(1)}, bf16[96,640]{1,0:T(8,128)(2,1)S(1)}, u32[]{:S(2)}, u32[]{:S(2)}) collective-permute-start(bf16[96,640]{1,0:T(8,128)(2,1)S(1)} %get-tuple-element.11.refs_7_), channel_id=1, source_target_pairs={{0,4},{1,9},{2,6},{3,11},{8,0},{9,17},{10,2},{11,19},{16,8},{17,25... | collective-permute-start | bytes 368648 | tf_op jit(solution)/shard_map/ppermute | solution.py:91
  5.3 6.5 %collective-permute-start.7 = (bf16[96,640]{1,0:T(8,128)(2,1)S(1)}, bf16[96,640]{1,0:T(8,128)(2,1)S(1)}, u32[]{:S(2)}, u32[]{:S(2)}) collective-permute-start(bf16[96,640]{1,0:T(8,128)(2,1)S(1)} %get-tuple-element.10.refs_0_), channel_id=1, source_target_pairs={{0,8},{1,5},{2,10},{3,7},{8,16},{9,1},{10,18},{11,3},{16,24},{17,9... | collective-permute-start | bytes 368648 | tf_op jit(solution)/shard_map/ppermute | solution.py:91
  6.7 6.8 %collective-permute-start.1 = (bf16[96,640]{1,0:T(8,128)(2,1)S(1)}, bf16[96,640]{1,0:T(8,128)(2,1)S(1)}, u32[]{:S(2)}, u32[]{:S(2)}) collective-permute-start(bf16[96,640]{1,0:T(8,128)(2,1)S(1)} %collective-permute-done.refs_1_), channel_id=1, source_target_pairs={{0,8},{1,5},{2,10},{3,7},{8,16},{9,1},{10,18},{11,3},{16,24},{17,9... | collective-permute-start | bytes 368648 | tf_op jit(solution)/shard_map/ppermute | solution.py:91
  8.0 5.7 %collective-permute-start.5 = (bf16[96,640]{1,0:T(8,128)(2,1)S(1)}, bf16[96,640]{1,0:T(8,128)(2,1)S(1)}, u32[]{:S(2)}, u32[]{:S(2)}) collective-permute-start(bf16[96,640]{1,0:T(8,128)(2,1)S(1)} %collective-permute-done.4.refs_7_), channel_id=1, source_target_pairs={{0,4},{1,9},{2,6},{3,11},{8,0},{9,17},{10,2},{11,19},{16,8},{17,25... | collective-permute-start | bytes 368648 | tf_op jit(solution)/shard_map/ppermute | solution.py:91
  9.1 6.8 %collective-permute-start.11 = (bf16[96,640]{1,0:T(8,128)(2,1)S(1)}, bf16[96,640]{1,0:T(8,128)(2,1)S(1)}, u32[]{:S(2)}, u32[]{:S(2)}) collective-permute-start(bf16[96,640]{1,0:T(8,128)(2,1)S(1)} %collective-permute-done.10.refs_6_), channel_id=1, source_target_pairs={{0,4},{1,9},{2,6},{3,11},{8,0},{9,17},{10,2},{11,19},{16,8},{17,25... | collective-permute-start | bytes 368648 | tf_op jit(solution)/shard_map/ppermute | solution.py:91
  10.4 5.9 %collective-permute-start.14 = (bf16[96,640]{1,0:T(8,128)(2,1)S(1)}, bf16[96,640]{1,0:T(8,128)(2,1)S(1)}, u32[]{:S(2)}, u32[]{:S(2)}) collective-permute-start(bf16[96,640]{1,0:T(8,128)(2,1)S(1)} %collective-permute-done.13.refs_8_), channel_id=1, source_target_pairs={{0,8},{1,5},{2,10},{3,7},{8,16},{9,1},{10,18},{11,3},{16,24},{17,9... | collective-permute-start | bytes 368648 | tf_op jit(solution)/shard_map/ppermute | solution.py:91
  11.7 6.4 %collective-permute-start.17 = (bf16[96,640]{1,0:T(8,128)(2,1)S(1)}, bf16[96,640]{1,0:T(8,128)(2,1)S(1)}, u32[]{:S(2)}, u32[]{:S(2)}) collective-permute-start(bf16[96,640]{1,0:T(8,128)(2,1)S(1)} %collective-permute-done.16.refs_13_), channel_id=1, source_target_pairs={{0,4},{1,9},{2,6},{3,11},{8,0},{9,17},{10,2},{11,19},{16,8},{17,25... | collective-permute-start | bytes 368648 | tf_op jit(solution)/shard_map/ppermute | solution.py:91
  13.5 5.8 %collective-permute-start.2 = (bf16[96,640]{1,0:T(8,128)(2,1)S(1)}, bf16[96,640]{1,0:T(8,128)(2,1)S(1)}, u32[]{:S(2)}, u32[]{:S(2)}) collective-permute-start(bf16[96,640]{1,0:T(8,128)(2,1)S(1)} %collective-permute-done.1.refs_2_), channel_id=1, source_target_pairs={{0,8},{1,5},{2,10},{3,7},{8,16},{9,1},{10,18},{11,3},{16,24},{17,9... | collective-permute-start | bytes 368648 | tf_op jit(solution)/shard_map/ppermute | solution.py:91
  13.7 7.7 %collective-permute-start.8 = (bf16[96,640]{1,0:T(8,128)(2,1)S(1)}, bf16[96,640]{1,0:T(8,128)(2,1)S(1)}, u32[]{:S(2)}, u32[]{:S(2)}) collective-permute-start(bf16[96,640]{1,0:T(8,128)(2,1)S(1)} %collective-permute-done.7.refs_1_), channel_id=1, source_target_pairs={{0,8},{1,5},{2,10},{3,7},{8,16},{9,1},{10,18},{11,3},{16,24},{17,9... | collective-permute-start | bytes 368648 | tf_op jit(solution)/shard_map/ppermute | solution.py:91
  15.9 6.8 %collective-permute-start.6 = (bf16[96,640]{1,0:T(8,128)(2,1)S(1)}, bf16[96,640]{1,0:T(8,128)(2,1)S(1)}, u32[]{:S(2)}, u32[]{:S(2)}) collective-permute-start(bf16[96,640]{1,0:T(8,128)(2,1)S(1)} %collective-permute-done.5.refs_6_), channel_id=1, source_target_pairs={{0,4},{1,9},{2,6},{3,11},{8,0},{9,17},{10,2},{11,19},{16,8},{17,25... | collective-permute-start | bytes 368648 | tf_op jit(solution)/shard_map/ppermute | solution.py:91
  16.3 6.9 %collective-permute-start.12 = (bf16[96,640]{1,0:T(8,128)(2,1)S(1)}, bf16[96,640]{1,0:T(8,128)(2,1)S(1)}, u32[]{:S(2)}, u32[]{:S(2)}) collective-permute-start(bf16[96,640]{1,0:T(8,128)(2,1)S(1)} %collective-permute-done.11.refs_5_), channel_id=1, source_target_pairs={{0,4},{1,9},{2,6},{3,11},{8,0},{9,17},{10,2},{11,19},{16,8},{17,25... | collective-permute-start | bytes 368648 | tf_op jit(solution)/shard_map/ppermute | solution.py:91
  18.1 6.2 %collective-permute-start.15 = (bf16[96,640]{1,0:T(8,128)(2,1)S(1)}, bf16[96,640]{1,0:T(8,128)(2,1)S(1)}, u32[]{:S(2)}, u32[]{:S(2)}) collective-permute-start(bf16[96,640]{1,0:T(8,128)(2,1)S(1)} %collective-permute-done.14.refs_9_), channel_id=1, source_target_pairs={{0,8},{1,5},{2,10},{3,7},{8,16},{9,1},{10,18},{11,3},{16,24},{17,9... | collective-permute-start | bytes 368648 | tf_op jit(solution)/shard_map/ppermute | solution.py:91
  19.3 6.5 %collective-permute-start.3 = (bf16[96,640]{1,0:T(8,128)(2,1)S(1)}, bf16[96,640]{1,0:T(8,128)(2,1)S(1)}, u32[]{:S(2)}, u32[]{:S(2)}) collective-permute-start(bf16[96,640]{1,0:T(8,128)(2,1)S(1)} %collective-permute-done.2.refs_3_), channel_id=1, source_target_pairs={{0,8},{1,5},{2,10},{3,7},{8,16},{9,1},{10,18},{11,3},{16,24},{17,9... | collective-permute-start | bytes 368648 | tf_op jit(solution)/shard_map/ppermute | solution.py:91
  21.4 5.4 %collective-permute-start.18 = (bf16[96,640]{1,0:T(8,128)(2,1)S(1)}, bf16[96,640]{1,0:T(8,128)(2,1)S(1)}, u32[]{:S(2)}, u32[]{:S(2)}) collective-permute-start(bf16[96,640]{1,0:T(8,128)(2,1)S(1)} %collective-permute-done.17.refs_12_), channel_id=1, source_target_pairs={{0,4},{1,9},{2,6},{3,11},{8,0},{9,17},{10,2},{11,19},{16,8},{17,25... | collective-permute-start | bytes 368648 | tf_op jit(solution)/shard_map/ppermute | solution.py:91
  22.7 5.3 %collective-permute-start.9 = (bf16[96,640]{1,0:T(8,128)(2,1)S(1)}, bf16[96,640]{1,0:T(8,128)(2,1)S(1)}, u32[]{:S(2)}, u32[]{:S(2)}) collective-permute-start(bf16[96,640]{1,0:T(8,128)(2,1)S(1)} %collective-permute-done.8.refs_2_), channel_id=1, source_target_pairs={{0,8},{1,5},{2,10},{3,7},{8,16},{9,1},{10,18},{11,3},{16,24},{17,9... | collective-permute-start | bytes 368648 | tf_op jit(solution)/shard_map/ppermute | solution.py:91
  23.2 9.3 %collective-permute-start.19 = (bf16[96,640]{1,0:T(8,128)(2,1)S(1)}, bf16[96,640]{1,0:T(8,128)(2,1)S(1)}, u32[]{:S(2)}, u32[]{:S(2)}) collective-permute-start(bf16[96,640]{1,0:T(8,128)(2,1)S(1)} %collective-permute-done.12.refs_4_), channel_id=1, source_target_pairs={{0,4},{1,9},{2,6},{3,11},{8,0},{9,17},{10,2},{11,19},{16,8},{17,25... | collective-permute-start | bytes 368648 | tf_op jit(solution)/shard_map/ppermute | solution.py:91
  24.3 8.3 %collective-permute-start.20 = (bf16[96,640]{1,0:T(8,128)(2,1)S(1)}, bf16[96,640]{1,0:T(8,128)(2,1)S(1)}, u32[]{:S(2)}, u32[]{:S(2)}) collective-permute-start(bf16[96,640]{1,0:T(8,128)(2,1)S(1)} %collective-permute-done.15.refs_10_), channel_id=1, source_target_pairs={{0,8},{1,5},{2,10},{3,7},{8,16},{9,1},{10,18},{11,3},{16,24},{17,9... | collective-permute-start | bytes 368648 | tf_op jit(solution)/shard_map/ppermute | solution.py:91
  39.6 9.3 %collective-permute-start.22 = (bf16[96,640]{1,0:T(8,128)(2,1)S(1)}, bf16[96,640]{1,0:T(8,128)(2,1)S(1)}, u32[]{:S(2)}, u32[]{:S(2)}) collective-permute-start(bf16[96,640]{1,0:T(8,128)(2,1)S(1)} %get-tuple-element.16.refs_0_), channel_id=1, source_target_pairs={{0,2},{1,3},{2,0},{3,1},{4,6},{5,7},{6,4},{7,5},{8,10},{9,11},{10,... | collective-permute-start | bytes 368648 | tf_op jit(solution)/shard_map/ppermute | solution.py:298
  43.9 8.3 %collective-permute-start.25 = (bf16[96,640]{1,0:T(8,128)(2,1)S(1)}, bf16[96,640]{1,0:T(8,128)(2,1)S(1)}, u32[]{:S(2)}, u32[]{:S(2)}) collective-permute-start(bf16[96,640]{1,0:T(8,128)(2,1)S(1)} %shard_map.44), channel_id=1, source_target_pairs={{0,8},{1,28},{2,0},{3,20},{4,24},{5,12},{6,16},{7,4},{8,25},{9,5},... | collective-permute-start | bytes 368648 | tf_op jit(solution)/shard_map/ppermute | solution.py:310
  48.9 7.1 %collective-permute-start.23 = (bf16[96,640]{1,0:T(8,128)(2,1)S(1)}, bf16[96,640]{1,0:T(8,128)(2,1)S(1)}, u32[]{:S(2)}, u32[]{:S(2)}) collective-permute-start(bf16[96,640]{1,0:T(8,128)(2,1)S(1)} %shard_map.43), channel_id=1, source_target_pairs={{0,24},{1,12},{2,16},{3,4},{4,8},{5,28},{6,0},{7,20},{8,1},{9,29},... | collective-permute-start | bytes 368648 | tf_op jit(solution)/shard_map/ppermute | solution.py:310
  (5 other events, 16.8 us)

commit v31 on v27

--- a/solution.py
+++ b/solution.py
@@ -239,6 +239,19 @@
     total_ref[...] = total.astype(total_ref.dtype)
 
 
+def place_kernel(swapped_ref, first_ref, second_ref, out_ref, sems):
+    cols = first_ref.shape[1]
+    swapped = swapped_ref[0] & 1
+    copies = []
+    for i, (ref, at) in enumerate(((first_ref, swapped), (second_ref, 1 - swapped))):
+        columns = pl.ds(pl.multiple_of(at * cols, HD), cols)
+        copies.append(pltpu.make_async_copy(ref, out_ref.at[:, columns], sems.at[i]))
+    for copy in copies:
+        copy.start()
+    for copy in copies:
+        copy.wait()
+
+
 def call(kernel, scalars, operands, outs, flops, after=()):
     vmem = pl.BlockSpec(memory_space=pltpu.VMEM)
     return pl.pallas_call(
@@ -304,9 +317,15 @@
         )
         arrived.append(lax.ppermute(total, ("frames", "heads"), pairs))
     patterns = [[p[source] for p in PATTERNS].index(to) for source in range(4) for to in range(4)]
-    straight = (look_up(patterns, 4 * head + z) ^ y) & 1 == 0
-    low, high = arrived
-    return jnp.concatenate([jnp.where(straight, low, high), jnp.where(straight, high, low)], axis=1)
+    swapped = (look_up(patterns, 4 * head + z) ^ y) & 1
+    vmem = pl.BlockSpec(memory_space=pltpu.VMEM)
+    return pl.pallas_call(
+        place_kernel,
+        out_shape=jax.ShapeDtypeStruct((ROWS, 2 * cols), bf16),
+        in_specs=[pl.BlockSpec(memory_space=pltpu.SMEM), vmem, vmem],
+        out_specs=pl.BlockSpec(memory_space=pltpu.HBM),
+        scratch_shapes=[pltpu.SemaphoreType.DMA((2,))],
+    )(swapped.reshape(1).astype(jnp.int32), *arrived)
 
 
 def solution(mesh):

time: 56.9 us -> 58.5 us (1.028)
  Pallas kernels: 9.42 us -> 11.1 us
  other arithmetic: 0.79 us -> 0.04 us
  local copies, waits for them, and re-layouts: 1.94 us -> 2.59 us
    pallas_call x0 -> x1, Pallas kernels: none -> 1.66 us  [on_device_ring(): pl.pallas_call(place_kernel, out_shape=jax.ShapeDtypeStruct((ROWS, 2 * co...]
    concatenate x1 -> x0, other arithmetic: 0.71 us -> none  [on_device_ring(): jnp.concatenate([jnp.where(straight, low, high), jnp.where(straight, high...]
    unnamed x6 -> x10, local copies, waits for them, and re-layouts: 1.85 us -> 2.5 us
where the time goes in v31:
time: 58.5 us; the launch traced here: 58.4 us
  starting transfers between devices  29.4 us (50%)
  waiting for transfers between devices  15.2 us (26%)
  Pallas kernels  11.1 us (19%)
  local copies, waits for them, and re-layouts  2.59 us (4%)
    ppermute x21, starting transfers between devices, hop(): return lax.ppermute(x, ('frames', 'heads'), pairs)  17.9 us
    pallas_call x8, Pallas kernels, call(): pl.pallas_call(kernel, out_shape=[jax.ShapeDtypeStruct(shape, dtype) for...  9.42 us
    ppermute x21, waiting for transfers between devices, hop(): return lax.ppermute(x, ('frames', 'heads'), pairs)  8.01 us
    ppermute x2, starting transfers between devices, on_device_ring(): arrived.append(lax.ppermute(total, ('frames', 'heads'), pairs))  6.73 us
    ppermute x2, waiting for transfers between devices, on_device_ring(): arrived.append(lax.ppermute(total, ('frames', 'heads'), pairs))  5.32 us
    ppermute x1, starting transfers between devices, on_device_ring(): from_core = lax.ppermute(given, 'heads', [(h, h ^ 1) for h in range(4)])  3.17 us
    unnamed x10, local copies, waits for them, and re-layouts  2.5 us
    ppermute x2, waiting for transfers between devices, on_device_ring(): lax.ppermute(block, 'heads', [(h, h ^ 2) for h in range(4)])  1.68 us
  transfers between devices with their start and end apart: 26, of which 15 were waited for; matrix products, arithmetic and copies ran while one was open for 0% of the time, Pallas kernels for 13%

profile of v31, /device:TPU:3, one launch (start us, length us, event | category | flops | bytes accessed | tf_op | source)
XLA Modules:
  0.0 58.4 jit_solution(17607560542118230350)
XLA Ops:
  0.0 1.2 %collective-permute-start = (bf16[96,640]{1,0:T(8,128)(2,1)}, bf16[96,640]{1,0:T(8,128)(2,1)S(1)}, u32[]{:S(2)}, u32[]{:S(2)}) collective-permute-start(bf16[96,640]{1,0:T(8,128)(2,1)} %refs_0_.1), channel_id=1, source_target_pairs={{0,8},{1,5},{2,10},{3,7},{8,16},{9,1},{10,18},{11,3},{16,24},{17,9... | collective-permute-start | bytes 368648 | tf_op jit(solution)/shard_map/ppermute | solution.py:91
  2.4 1.3 %collective-permute-start.10 = (bf16[96,640]{1,0:T(8,128)(2,1)S(1)}, bf16[96,640]{1,0:T(8,128)(2,1)S(1)}, u32[]{:S(2)}, u32[]{:S(2)}) collective-permute-start(bf16[96,640]{1,0:T(8,128)(2,1)S(1)} %get-tuple-element.10.refs_0_), channel_id=1, source_target_pairs={{0,4},{1,9},{2,6},{3,11},{8,0},{9,17},{10,2},{11,19},{16,8},{17,25... | collective-permute-start | bytes 368648 | tf_op jit(solution)/shard_map/ppermute | solution.py:91
  4.0 1.3 %collective-permute-start.16 = (bf16[96,640]{1,0:T(8,128)(2,1)S(1)}, bf16[96,640]{1,0:T(8,128)(2,1)S(1)}, u32[]{:S(2)}, u32[]{:S(2)}) collective-permute-start(bf16[96,640]{1,0:T(8,128)(2,1)S(1)} %get-tuple-element.11.refs_7_), channel_id=1, source_target_pairs={{0,4},{1,9},{2,6},{3,11},{8,0},{9,17},{10,2},{11,19},{16,8},{17,25... | collective-permute-start | bytes 368648 | tf_op jit(solution)/shard_map/ppermute | solution.py:91
  5.5 1.2 %collective-permute-done.4.refs_7_ = bf16[96,640]{1,0:T(8,128)(2,1)S(1)} collective-permute-done((bf16[96,640]{1,0:T(8,128)(2,1)}, bf16[96,640]{1,0:T(8,128)(2,1)S(1)}, u32[]{:S(2)}, u32[]{:S(2)}) %collective-permute-start.4) | collective-permute-done | bytes 122912 | tf_op jit(solution)/shard_map/ppermute | solution.py:91
  9.1 1.3 %collective-permute-start.11 = (bf16[96,640]{1,0:T(8,128)(2,1)S(1)}, bf16[96,640]{1,0:T(8,128)(2,1)S(1)}, u32[]{:S(2)}, u32[]{:S(2)}) collective-permute-start(bf16[96,640]{1,0:T(8,128)(2,1)S(1)} %collective-permute-done.10.refs_6_), channel_id=1, source_target_pairs={{0,4},{1,9},{2,6},{3,11},{8,0},{9,17},{10,2},{11,19},{16,8},{17,25... | collective-permute-start | bytes 368648 | tf_op jit(solution)/shard_map/ppermute | solution.py:91
  11.7 1.3 %collective-permute-start.17 = (bf16[96,640]{1,0:T(8,128)(2,1)S(1)}, bf16[96,640]{1,0:T(8,128)(2,1)S(1)}, u32[]{:S(2)}, u32[]{:S(2)}) collective-permute-start(bf16[96,640]{1,0:T(8,128)(2,1)S(1)} %collective-permute-done.16.refs_13_), channel_id=1, source_target_pairs={{0,4},{1,9},{2,6},{3,11},{8,0},{9,17},{10,2},{11,19},{16,8},{17,25... | collective-permute-start | bytes 368648 | tf_op jit(solution)/shard_map/ppermute | solution.py:91
  13.7 1.2 %collective-permute-start.8 = (bf16[96,640]{1,0:T(8,128)(2,1)S(1)}, bf16[96,640]{1,0:T(8,128)(2,1)S(1)}, u32[]{:S(2)}, u32[]{:S(2)}) collective-permute-start(bf16[96,640]{1,0:T(8,128)(2,1)S(1)} %collective-permute-done.7.refs_1_), channel_id=1, source_target_pairs={{0,8},{1,5},{2,10},{3,7},{8,16},{9,1},{10,18},{11,3},{16,24},{17,9... | collective-permute-start | bytes 368648 | tf_op jit(solution)/shard_map/ppermute | solution.py:91
  16.3 1.3 %collective-permute-start.12 = (bf16[96,640]{1,0:T(8,128)(2,1)S(1)}, bf16[96,640]{1,0:T(8,128)(2,1)S(1)}, u32[]{:S(2)}, u32[]{:S(2)}) collective-permute-start(bf16[96,640]{1,0:T(8,128)(2,1)S(1)} %collective-permute-done.11.refs_5_), channel_id=1, source_target_pairs={{0,4},{1,9},{2,6},{3,11},{8,0},{9,17},{10,2},{11,19},{16,8},{17,25... | collective-permute-start | bytes 368648 | tf_op jit(solution)/shard_map/ppermute | solution.py:91
  18.1 1.2 %collective-permute-start.15 = (bf16[96,640]{1,0:T(8,128)(2,1)S(1)}, bf16[96,640]{1,0:T(8,128)(2,1)S(1)}, u32[]{:S(2)}, u32[]{:S(2)}) collective-permute-start(bf16[96,640]{1,0:T(8,128)(2,1)S(1)} %collective-permute-done.14.refs_9_), channel_id=1, source_target_pairs={{0,8},{1,5},{2,10},{3,7},{8,16},{9,1},{10,18},{11,3},{16,24},{17,9... | collective-permute-start | bytes 368648 | tf_op jit(solution)/shard_map/ppermute | solution.py:91
  19.3 1.3 %collective-permute-start.3 = (bf16[96,640]{1,0:T(8,128)(2,1)S(1)}, bf16[96,640]{1,0:T(8,128)(2,1)S(1)}, u32[]{:S(2)}, u32[]{:S(2)}) collective-permute-start(bf16[96,640]{1,0:T(8,128)(2,1)S(1)} %collective-permute-done.2.refs_3_), channel_id=1, source_target_pairs={{0,8},{1,5},{2,10},{3,7},{8,16},{9,1},{10,18},{11,3},{16,24},{17,9... | collective-permute-start | bytes 368648 | tf_op jit(solution)/shard_map/ppermute | solution.py:91
  21.4 1.3 %collective-permute-start.18 = (bf16[96,640]{1,0:T(8,128)(2,1)S(1)}, bf16[96,640]{1,0:T(8,128)(2,1)S(1)}, u32[]{:S(2)}, u32[]{:S(2)}) collective-permute-start(bf16[96,640]{1,0:T(8,128)(2,1)S(1)} %collective-permute-done.17.refs_12_), channel_id=1, source_target_pairs={{0,4},{1,9},{2,6},{3,11},{8,0},{9,17},{10,2},{11,19},{16,8},{17,25... | collective-permute-start | bytes 368648 | tf_op jit(solution)/shard_map/ppermute | solution.py:91
  26.8 1.2 %collective-permute-done.9.refs_3_ = bf16[96,640]{1,0:T(8,128)(2,1)S(1)} collective-permute-done((bf16[96,640]{1,0:T(8,128)(2,1)S(1)}, bf16[96,640]{1,0:T(8,128)(2,1)S(1)}, u32[]{:S(2)}, u32[]{:S(2)}) %collective-permute-start.9) | collective-permute-done | bytes 122912 | tf_op jit(solution)/shard_map/ppermute | solution.py:91
  28.0 4.6 %shard_map.39 = (f32[5,8,96,128]{3,2,1,0:T(8,128)S(1)}, f32[5,8,96,128]{3,2,1,0:T(8,128)S(1)}, f32[5,8,96,128]{3,2,1,0:T(8,128)S(1)}) custom-call(s32[5]{0:T(128)S(1)} %stack.23.at_ref, bf16[8,96,640]{2,1,0:T(8,128)(2,1)S(1)} %shard_map.37.rows_ref, bf16[96,640]{1,0:T(8,128)(2,1)S(1)} %get-tuple-element.10.refs_0_, ...), custom_call_target="tpu_custom_call" | custom-call | flops 1321205760 | tf_op jit(solution)/shard_map/pallas_call | solution.py:257
  32.6 2.0 %shard_map.40 = bf16[384,640]{1,0:T(8,128)(2,1)S(1)} custom-call(s32[5]{0:T(128)S(1)} %stack.23.at_ref, bf16[8,96,640]{2,1,0:T(8,128)(2,1)S(1)} %shard_map.37.rows_ref, f32[5,8,96,128]{3,2,1,0:T(8,128)S(1)} %get-tuple-element.12.mixed_ref, f32[5,8,96,128]{3,2,1,0:T(8,128)S(1)} %get-tuple-element.13.sum_ref, f32[5,8,96,128]{3,2,1,0:T(8,128)S(1)} %get-tuple-element.14.top_ref, ...), custom_call_target="tpu_custom_call" | custom-call | flops 314572800 | tf_op jit(solution)/shard_map/pallas_call | solution.py:257
  34.6 3.2 %collective-permute-start.21 = (bf16[2,192,640]{2,1,0:T(8,128)(2,1)S(1)}, bf16[2,192,640]{2,1,0:T(8,128)(2,1)S(1)}, u32[]{:S(2)}, u32[]{:S(2)}) collective-permute-start(bf16[2,192,640]{2,1,0:T(8,128)(2,1)S(1)} %bitcast.17), channel_id=1, source_target_pairs={{0,1},{1,0},{2,3},{3,2},{4,5},{5,4},{6,7},{7,6},{8,9},{9,8},{10,11... | collective-permute-start | bytes 1474568 | tf_op jit(solution)/shard_map/ppermute | solution.py:302
  37.8 1.3 %shard_map.41 = f32[192,640]{1,0:T(8,128)S(1)} custom-call(s32[5]{0:T(128)S(1)} %stack.23.at_ref, bf16[8,96,640]{2,1,0:T(8,128)(2,1)S(1)} %shard_map.37.rows_ref, f32[5,8,96,128]{3,2,1,0:T(8,128)S(1)} %get-tuple-element.12.mixed_ref, f32[5,8,96,128]{3,2,1,0:T(8,128)S(1)} %get-tuple-element.13.sum_ref, f32[5,8,96,128]{3,2,1,0:T(8,128)S(1)} %get-tuple-element.14.top_ref, ...), custom_call_target="tpu_custom_call" | custom-call | flops 314572800 | tf_op jit(solution)/shard_map/pallas_call | solution.py:257
  39.6 1.2 %collective-permute-start.22 = (bf16[96,640]{1,0:T(8,128)(2,1)S(1)}, bf16[96,640]{1,0:T(8,128)(2,1)S(1)}, u32[]{:S(2)}, u32[]{:S(2)}) collective-permute-start(bf16[96,640]{1,0:T(8,128)(2,1)S(1)} %get-tuple-element.16.refs_0_), channel_id=1, source_target_pairs={{0,2},{1,3},{2,0},{3,1},{4,6},{5,7},{6,4},{7,5},{8,10},{9,11},{10,... | collective-permute-start | bytes 368648 | tf_op jit(solution)/shard_map/ppermute | solution.py:306
  40.8 1.3 %shard_map.42.kept_ref = f32[192,640]{1,0:T(8,128)S(1)} custom-call(s32[5]{0:T(128)S(1)} %stack.23.at_ref, bf16[8,96,640]{2,1,0:T(8,128)(2,1)S(1)} %shard_map.37.rows_ref, f32[5,8,96,128]{3,2,1,0:T(8,128)S(1)} %get-tuple-element.12.mixed_ref, f32[5,8,96,128]{3,2,1,0:T(8,128)S(1)} %get-tuple-element.13.sum_ref, ...), custom_call_target="tpu_custom_call" | custom-call | flops 314572800 | tf_op jit(solution)/shard_map/pallas_call | solution.py:257
  42.2 1.7 %collective-permute-done.24.from_x_ref = bf16[96,640]{1,0:T(8,128)(2,1)S(1)} collective-permute-done((bf16[96,640]{1,0:T(8,128)(2,1)S(1)}, bf16[96,640]{1,0:T(8,128)(2,1)S(1)}, u32[]{:S(2)}, u32[]{:S(2)}) %collective-permute-start.24) | collective-permute-done | bytes 122912 | tf_op jit(solution)/shard_map/ppermute | solution.py:306
  43.9 5.0 %collective-permute-start.25 = (bf16[96,640]{1,0:T(8,128)(2,1)S(1)}, bf16[96,640]{1,0:T(8,128)(2,1)S(1)}, u32[]{:S(2)}, u32[]{:S(2)}) collective-permute-start(bf16[96,640]{1,0:T(8,128)(2,1)S(1)} %shard_map.44), channel_id=1, source_target_pairs={{0,8},{1,28},{2,0},{3,20},{4,24},{5,12},{6,16},{7,4},{8,25},{9,5},... | collective-permute-start | bytes 368648 | tf_op jit(solution)/shard_map/ppermute | solution.py:318
  49.0 1.7 %collective-permute-start.23 = (bf16[96,640]{1,0:T(8,128)(2,1)S(1)}, bf16[96,640]{1,0:T(8,128)(2,1)S(1)}, u32[]{:S(2)}, u32[]{:S(2)}) collective-permute-start(bf16[96,640]{1,0:T(8,128)(2,1)S(1)} %shard_map.43), channel_id=1, source_target_pairs={{0,24},{1,12},{2,16},{3,4},{4,8},{5,28},{6,0},{7,20},{8,1},{9,29},... | collective-permute-start | bytes 368648 | tf_op jit(solution)/shard_map/ppermute | solution.py:318
  50.7 1.4 %collective-permute-done.25.second_ref = bf16[96,640]{1,0:T(8,128)(2,1)S(1)} collective-permute-done((bf16[96,640]{1,0:T(8,128)(2,1)S(1)}, bf16[96,640]{1,0:T(8,128)(2,1)S(1)}, u32[]{:S(2)}, u32[]{:S(2)}) %collective-permute-start.25) | collective-permute-done | bytes 122912 | tf_op jit(solution)/shard_map/ppermute | solution.py:318
  52.1 3.9 %collective-permute-done.23.first_ref = bf16[96,640]{1,0:T(8,128)(2,1)S(1)} collective-permute-done((bf16[96,640]{1,0:T(8,128)(2,1)S(1)}, bf16[96,640]{1,0:T(8,128)(2,1)S(1)}, u32[]{:S(2)}, u32[]{:S(2)}) %collective-permute-start.23) | collective-permute-done | bytes 122912 | tf_op jit(solution)/shard_map/ppermute | solution.py:318
  56.7 1.7 %shard_map.45 = bf16[96,1280]{1,0:T(8,128)(2,1)} custom-call(s32[1]{0:T(128)} %bitcast.swapped_ref, bf16[96,640]{1,0:T(8,128)(2,1)} %copy-done.4, bf16[96,640]{1,0:T(8,128)(2,1)} %copy-done.3), custom_call_target="tpu_custom_call" | custom-call | tf_op jit(solution)/shard_map/pallas_call | solution.py:322
  (49 shorter events, 14.0 us)
Async XLA Ops:
  0.0 5.3 %collective-permute-start = (bf16[96,640]{1,0:T(8,128)(2,1)}, bf16[96,640]{1,0:T(8,128)(2,1)S(1)}, u32[]{:S(2)}, u32[]{:S(2)}) collective-permute-start(bf16[96,640]{1,0:T(8,128)(2,1)} %refs_0_.1), channel_id=1, source_target_pairs={{0,8},{1,5},{2,10},{3,7},{8,16},{9,1},{10,18},{11,3},{16,24},{17,9... | collective-permute-start | bytes 368648 | tf_op jit(solution)/shard_map/ppermute | solution.py:91
  1.2 5.4 %collective-permute-start.4 = (bf16[96,640]{1,0:T(8,128)(2,1)}, bf16[96,640]{1,0:T(8,128)(2,1)S(1)}, u32[]{:S(2)}, u32[]{:S(2)}) collective-permute-start(bf16[96,640]{1,0:T(8,128)(2,1)} %refs_0_.1), channel_id=1, source_target_pairs={{0,4},{1,9},{2,6},{3,11},{8,0},{9,17},{10,2},{11,19},{16,8},{17,25... | collective-permute-start | bytes 368648 | tf_op jit(solution)/shard_map/ppermute | solution.py:91
  2.4 5.6 %collective-permute-start.10 = (bf16[96,640]{1,0:T(8,128)(2,1)S(1)}, bf16[96,640]{1,0:T(8,128)(2,1)S(1)}, u32[]{:S(2)}, u32[]{:S(2)}) collective-permute-start(bf16[96,640]{1,0:T(8,128)(2,1)S(1)} %get-tuple-element.10.refs_0_), channel_id=1, source_target_pairs={{0,4},{1,9},{2,6},{3,11},{8,0},{9,17},{10,2},{11,19},{16,8},{17,25... | collective-permute-start | bytes 368648 | tf_op jit(solution)/shard_map/ppermute | solution.py:91
  3.8 5.3 %collective-permute-start.13 = (bf16[96,640]{1,0:T(8,128)(2,1)S(1)}, bf16[96,640]{1,0:T(8,128)(2,1)S(1)}, u32[]{:S(2)}, u32[]{:S(2)}) collective-permute-start(bf16[96,640]{1,0:T(8,128)(2,1)S(1)} %get-tuple-element.11.refs_7_), channel_id=1, source_target_pairs={{0,8},{1,5},{2,10},{3,7},{8,16},{9,1},{10,18},{11,3},{16,24},{17,9... | collective-permute-start | bytes 368648 | tf_op jit(solution)/shard_map/ppermute | solution.py:91
  4.0 6.5 %collective-permute-start.16 = (bf16[96,640]{1,0:T(8,128)(2,1)S(1)}, bf16[96,640]{1,0:T(8,128)(2,1)S(1)}, u32[]{:S(2)}, u32[]{:S(2)}) collective-permute-start(bf16[96,640]{1,0:T(8,128)(2,1)S(1)} %get-tuple-element.11.refs_7_), channel_id=1, source_target_pairs={{0,4},{1,9},{2,6},{3,11},{8,0},{9,17},{10,2},{11,19},{16,8},{17,25... | collective-permute-start | bytes 368648 | tf_op jit(solution)/shard_map/ppermute | solution.py:91
  5.3 6.5 %collective-permute-start.7 = (bf16[96,640]{1,0:T(8,128)(2,1)S(1)}, bf16[96,640]{1,0:T(8,128)(2,1)S(1)}, u32[]{:S(2)}, u32[]{:S(2)}) collective-permute-start(bf16[96,640]{1,0:T(8,128)(2,1)S(1)} %get-tuple-element.10.refs_0_), channel_id=1, source_target_pairs={{0,8},{1,5},{2,10},{3,7},{8,16},{9,1},{10,18},{11,3},{16,24},{17,9... | collective-permute-start | bytes 368648 | tf_op jit(solution)/shard_map/ppermute | solution.py:91
  6.7 6.8 %collective-permute-start.1 = (bf16[96,640]{1,0:T(8,128)(2,1)S(1)}, bf16[96,640]{1,0:T(8,128)(2,1)S(1)}, u32[]{:S(2)}, u32[]{:S(2)}) collective-permute-start(bf16[96,640]{1,0:T(8,128)(2,1)S(1)} %collective-permute-done.refs_1_), channel_id=1, source_target_pairs={{0,8},{1,5},{2,10},{3,7},{8,16},{9,1},{10,18},{11,3},{16,24},{17,9... | collective-permute-start | bytes 368648 | tf_op jit(solution)/shard_map/ppermute | solution.py:91
  8.0 5.7 %collective-permute-start.5 = (bf16[96,640]{1,0:T(8,128)(2,1)S(1)}, bf16[96,640]{1,0:T(8,128)(2,1)S(1)}, u32[]{:S(2)}, u32[]{:S(2)}) collective-permute-start(bf16[96,640]{1,0:T(8,128)(2,1)S(1)} %collective-permute-done.4.refs_7_), channel_id=1, source_target_pairs={{0,4},{1,9},{2,6},{3,11},{8,0},{9,17},{10,2},{11,19},{16,8},{17,25... | collective-permute-start | bytes 368648 | tf_op jit(solution)/shard_map/ppermute | solution.py:91
  9.1 6.8 %collective-permute-start.11 = (bf16[96,640]{1,0:T(8,128)(2,1)S(1)}, bf16[96,640]{1,0:T(8,128)(2,1)S(1)}, u32[]{:S(2)}, u32[]{:S(2)}) collective-permute-start(bf16[96,640]{1,0:T(8,128)(2,1)S(1)} %collective-permute-done.10.refs_6_), channel_id=1, source_target_pairs={{0,4},{1,9},{2,6},{3,11},{8,0},{9,17},{10,2},{11,19},{16,8},{17,25... | collective-permute-start | bytes 368648 | tf_op jit(solution)/shard_map/ppermute | solution.py:91
  10.4 5.9 %collective-permute-start.14 = (bf16[96,640]{1,0:T(8,128)(2,1)S(1)}, bf16[96,640]{1,0:T(8,128)(2,1)S(1)}, u32[]{:S(2)}, u32[]{:S(2)}) collective-permute-start(bf16[96,640]{1,0:T(8,128)(2,1)S(1)} %collective-permute-done.13.refs_8_), channel_id=1, source_target_pairs={{0,8},{1,5},{2,10},{3,7},{8,16},{9,1},{10,18},{11,3},{16,24},{17,9... | collective-permute-start | bytes 368648 | tf_op jit(solution)/shard_map/ppermute | solution.py:91
  11.7 6.4 %collective-permute-start.17 = (bf16[96,640]{1,0:T(8,128)(2,1)S(1)}, bf16[96,640]{1,0:T(8,128)(2,1)S(1)}, u32[]{:S(2)}, u32[]{:S(2)}) collective-permute-start(bf16[96,640]{1,0:T(8,128)(2,1)S(1)} %collective-permute-done.16.refs_13_), channel_id=1, source_target_pairs={{0,4},{1,9},{2,6},{3,11},{8,0},{9,17},{10,2},{11,19},{16,8},{17,25... | collective-permute-start | bytes 368648 | tf_op jit(solution)/shard_map/ppermute | solution.py:91
  13.5 5.8 %collective-permute-start.2 = (bf16[96,640]{1,0:T(8,128)(2,1)S(1)}, bf16[96,640]{1,0:T(8,128)(2,1)S(1)}, u32[]{:S(2)}, u32[]{:S(2)}) collective-permute-start(bf16[96,640]{1,0:T(8,128)(2,1)S(1)} %collective-permute-done.1.refs_2_), channel_id=1, source_target_pairs={{0,8},{1,5},{2,10},{3,7},{8,16},{9,1},{10,18},{11,3},{16,24},{17,9... | collective-permute-start | bytes 368648 | tf_op jit(solution)/shard_map/ppermute | solution.py:91
  13.7 7.7 %collective-permute-start.8 = (bf16[96,640]{1,0:T(8,128)(2,1)S(1)}, bf16[96,640]{1,0:T(8,128)(2,1)S(1)}, u32[]{:S(2)}, u32[]{:S(2)}) collective-permute-start(bf16[96,640]{1,0:T(8,128)(2,1)S(1)} %collective-permute-done.7.refs_1_), channel_id=1, source_target_pairs={{0,8},{1,5},{2,10},{3,7},{8,16},{9,1},{10,18},{11,3},{16,24},{17,9... | collective-permute-start | bytes 368648 | tf_op jit(solution)/shard_map/ppermute | solution.py:91
  15.9 6.8 %collective-permute-start.6 = (bf16[96,640]{1,0:T(8,128)(2,1)S(1)}, bf16[96,640]{1,0:T(8,128)(2,1)S(1)}, u32[]{:S(2)}, u32[]{:S(2)}) collective-permute-start(bf16[96,640]{1,0:T(8,128)(2,1)S(1)} %collective-permute-done.5.refs_6_), channel_id=1, source_target_pairs={{0,4},{1,9},{2,6},{3,11},{8,0},{9,17},{10,2},{11,19},{16,8},{17,25... | collective-permute-start | bytes 368648 | tf_op jit(solution)/shard_map/ppermute | solution.py:91
  16.3 6.9 %collective-permute-start.12 = (bf16[96,640]{1,0:T(8,128)(2,1)S(1)}, bf16[96,640]{1,0:T(8,128)(2,1)S(1)}, u32[]{:S(2)}, u32[]{:S(2)}) collective-permute-start(bf16[96,640]{1,0:T(8,128)(2,1)S(1)} %collective-permute-done.11.refs_5_), channel_id=1, source_target_pairs={{0,4},{1,9},{2,6},{3,11},{8,0},{9,17},{10,2},{11,19},{16,8},{17,25... | collective-permute-start | bytes 368648 | tf_op jit(solution)/shard_map/ppermute | solution.py:91
  18.1 6.2 %collective-permute-start.15 = (bf16[96,640]{1,0:T(8,128)(2,1)S(1)}, bf16[96,640]{1,0:T(8,128)(2,1)S(1)}, u32[]{:S(2)}, u32[]{:S(2)}) collective-permute-start(bf16[96,640]{1,0:T(8,128)(2,1)S(1)} %collective-permute-done.14.refs_9_), channel_id=1, source_target_pairs={{0,8},{1,5},{2,10},{3,7},{8,16},{9,1},{10,18},{11,3},{16,24},{17,9... | collective-permute-start | bytes 368648 | tf_op jit(solution)/shard_map/ppermute | solution.py:91
  19.3 6.5 %collective-permute-start.3 = (bf16[96,640]{1,0:T(8,128)(2,1)S(1)}, bf16[96,640]{1,0:T(8,128)(2,1)S(1)}, u32[]{:S(2)}, u32[]{:S(2)}) collective-permute-start(bf16[96,640]{1,0:T(8,128)(2,1)S(1)} %collective-permute-done.2.refs_3_), channel_id=1, source_target_pairs={{0,8},{1,5},{2,10},{3,7},{8,16},{9,1},{10,18},{11,3},{16,24},{17,9... | collective-permute-start | bytes 368648 | tf_op jit(solution)/shard_map/ppermute | solution.py:91
  21.4 5.4 %collective-permute-start.18 = (bf16[96,640]{1,0:T(8,128)(2,1)S(1)}, bf16[96,640]{1,0:T(8,128)(2,1)S(1)}, u32[]{:S(2)}, u32[]{:S(2)}) collective-permute-start(bf16[96,640]{1,0:T(8,128)(2,1)S(1)} %collective-permute-done.17.refs_12_), channel_id=1, source_target_pairs={{0,4},{1,9},{2,6},{3,11},{8,0},{9,17},{10,2},{11,19},{16,8},{17,25... | collective-permute-start | bytes 368648 | tf_op jit(solution)/shard_map/ppermute | solution.py:91
  22.7 5.3 %collective-permute-start.9 = (bf16[96,640]{1,0:T(8,128)(2,1)S(1)}, bf16[96,640]{1,0:T(8,128)(2,1)S(1)}, u32[]{:S(2)}, u32[]{:S(2)}) collective-permute-start(bf16[96,640]{1,0:T(8,128)(2,1)S(1)} %collective-permute-done.8.refs_2_), channel_id=1, source_target_pairs={{0,8},{1,5},{2,10},{3,7},{8,16},{9,1},{10,18},{11,3},{16,24},{17,9... | collective-permute-start | bytes 368648 | tf_op jit(solution)/shard_map/ppermute | solution.py:91
  23.2 9.4 %collective-permute-start.19 = (bf16[96,640]{1,0:T(8,128)(2,1)S(1)}, bf16[96,640]{1,0:T(8,128)(2,1)S(1)}, u32[]{:S(2)}, u32[]{:S(2)}) collective-permute-start(bf16[96,640]{1,0:T(8,128)(2,1)S(1)} %collective-permute-done.12.refs_4_), channel_id=1, source_target_pairs={{0,4},{1,9},{2,6},{3,11},{8,0},{9,17},{10,2},{11,19},{16,8},{17,25... | collective-permute-start | bytes 368648 | tf_op jit(solution)/shard_map/ppermute | solution.py:91
  24.3 8.3 %collective-permute-start.20 = (bf16[96,640]{1,0:T(8,128)(2,1)S(1)}, bf16[96,640]{1,0:T(8,128)(2,1)S(1)}, u32[]{:S(2)}, u32[]{:S(2)}) collective-permute-start(bf16[96,640]{1,0:T(8,128)(2,1)S(1)} %collective-permute-done.15.refs_10_), channel_id=1, source_target_pairs={{0,8},{1,5},{2,10},{3,7},{8,16},{9,1},{10,18},{11,3},{16,24},{17,9... | collective-permute-start | bytes 368648 | tf_op jit(solution)/shard_map/ppermute | solution.py:91
  39.6 9.3 %collective-permute-start.22 = (bf16[96,640]{1,0:T(8,128)(2,1)S(1)}, bf16[96,640]{1,0:T(8,128)(2,1)S(1)}, u32[]{:S(2)}, u32[]{:S(2)}) collective-permute-start(bf16[96,640]{1,0:T(8,128)(2,1)S(1)} %get-tuple-element.16.refs_0_), channel_id=1, source_target_pairs={{0,2},{1,3},{2,0},{3,1},{4,6},{5,7},{6,4},{7,5},{8,10},{9,11},{10,... | collective-permute-start | bytes 368648 | tf_op jit(solution)/shard_map/ppermute | solution.py:306
  43.9 8.2 %collective-permute-start.25 = (bf16[96,640]{1,0:T(8,128)(2,1)S(1)}, bf16[96,640]{1,0:T(8,128)(2,1)S(1)}, u32[]{:S(2)}, u32[]{:S(2)}) collective-permute-start(bf16[96,640]{1,0:T(8,128)(2,1)S(1)} %shard_map.44), channel_id=1, source_target_pairs={{0,8},{1,28},{2,0},{3,20},{4,24},{5,12},{6,16},{7,4},{8,25},{9,5},... | collective-permute-start | bytes 368648 | tf_op jit(solution)/shard_map/ppermute | solution.py:318
  49.0 7.1 %collective-permute-start.23 = (bf16[96,640]{1,0:T(8,128)(2,1)S(1)}, bf16[96,640]{1,0:T(8,128)(2,1)S(1)}, u32[]{:S(2)}, u32[]{:S(2)}) collective-permute-start(bf16[96,640]{1,0:T(8,128)(2,1)S(1)} %shard_map.43), channel_id=1, source_target_pairs={{0,24},{1,12},{2,16},{3,4},{4,8},{5,28},{6,0},{7,20},{8,1},{9,29},... | collective-permute-start | bytes 368648 | tf_op jit(solution)/shard_map/ppermute | solution.py:318
  (7 other events, 21.4 us)

commit v32 on v27

--- a/solution.py
+++ b/solution.py
@@ -87,7 +87,7 @@
     pairs = []
     for i in range(n):
         for h in range(4):
-            pairs.append((4 * order[i] + h, 4 * order[(i + by * (1 - 2 * (h & 1))) % n] + h))
+            pairs.append((4 * order[i] + h, 4 * order[(i + by * (2 * (h & 1) - 1)) % n] + h))
     return lax.ppermute(x, ("frames", "heads"), pairs)
 
 
@@ -103,7 +103,7 @@
 
 def ring_distance(at_ref, owner, n):
     place, core = at_ref[0], at_ref[4]
-    return (place - owner) * (1 - 2 * core) & (n - 1)
+    return (place - owner) * (2 * core - 1) & (n - 1)
 
 
 def frame_marks(at_ref, blocks, n):
@@ -111,7 +111,7 @@
     lane = lax.broadcasted_iota(jnp.int32, (TPF, HD), 1)
     marks = []
     for block in blocks:
-        owner = (place - block * (1 - 2 * core)) & (n - 1)
+        owner = (place - block * (2 * core - 1)) & (n - 1)
         frame = FR_DEV * ring_distance(at_ref, owner ^ 2, n)
         for g in range(FR_DEV):
             marks.append((lane == frame + g) | (lane >= n * FR_DEV))

time: 56.9 us -> 57.2 us (level)
  no operation moved by 1% of the time
where the time goes in v32:
time: 57.2 us; the launch traced here: 57 us
  starting transfers between devices  29.7 us (52%)
  waiting for transfers between devices  15 us (26%)
  Pallas kernels  9.42 us (16%)
  local copies, waits for them, and re-layouts  1.94 us (3%)
  other arithmetic  0.79 us (1%)
    ppermute x21, starting transfers between devices, hop(): return lax.ppermute(x, ('frames', 'heads'), pairs)  18.4 us
    pallas_call x8, Pallas kernels, call(): pl.pallas_call(kernel, out_shape=[jax.ShapeDtypeStruct(shape, dtype) for...  9.42 us
    ppermute x21, waiting for transfers between devices, hop(): return lax.ppermute(x, ('frames', 'heads'), pairs)  7.51 us
    ppermute x2, starting transfers between devices, on_device_ring(): arrived.append(lax.ppermute(total, ('frames', 'heads'), pairs))  6.64 us
    ppermute x2, waiting for transfers between devices, on_device_ring(): arrived.append(lax.ppermute(total, ('frames', 'heads'), pairs))  5.69 us
    ppermute x1, starting transfers between devices, on_device_ring(): from_core = lax.ppermute(given, 'heads', [(h, h ^ 1) for h in range(4)])  3.17 us
    unnamed x6, local copies, waits for them, and re-layouts  1.85 us
    ppermute x2, waiting for transfers between devices, on_device_ring(): lax.ppermute(block, 'heads', [(h, h ^ 2) for h in range(4)])  1.68 us
  transfers between devices with their start and end apart: 26, of which 15 were waited for; matrix products, arithmetic and copies ran while one was open for 0% of the time, Pallas kernels for 13%

profile of v32, /device:TPU:3, one launch (start us, length us, event | category | flops | bytes accessed | tf_op | source)
XLA Modules:
  0.0 57.0 jit_solution(3957945558298387063)
XLA Ops:
  0.0 1.3 %collective-permute-start = (bf16[96,640]{1,0:T(8,128)(2,1)}, bf16[96,640]{1,0:T(8,128)(2,1)S(1)}, u32[]{:S(2)}, u32[]{:S(2)}) collective-permute-start(bf16[96,640]{1,0:T(8,128)(2,1)} %refs_0_.1), channel_id=1, source_target_pairs={{0,4},{1,9},{2,6},{3,11},{8,0},{9,17},{10,2},{11,19},{16,8},{17,25... | collective-permute-start | bytes 368648 | tf_op jit(solution)/shard_map/ppermute | solution.py:91
  2.4 1.3 %collective-permute-start.10 = (bf16[96,640]{1,0:T(8,128)(2,1)S(1)}, bf16[96,640]{1,0:T(8,128)(2,1)S(1)}, u32[]{:S(2)}, u32[]{:S(2)}) collective-permute-start(bf16[96,640]{1,0:T(8,128)(2,1)S(1)} %get-tuple-element.10.refs_0_), channel_id=1, source_target_pairs={{0,8},{1,5},{2,10},{3,7},{8,16},{9,1},{10,18},{11,3},{16,24},{17,9... | collective-permute-start | bytes 368648 | tf_op jit(solution)/shard_map/ppermute | solution.py:91
  4.0 1.2 %collective-permute-start.16 = (bf16[96,640]{1,0:T(8,128)(2,1)S(1)}, bf16[96,640]{1,0:T(8,128)(2,1)S(1)}, u32[]{:S(2)}, u32[]{:S(2)}) collective-permute-start(bf16[96,640]{1,0:T(8,128)(2,1)S(1)} %get-tuple-element.11.refs_7_), channel_id=1, source_target_pairs={{0,8},{1,5},{2,10},{3,7},{8,16},{9,1},{10,18},{11,3},{16,24},{17,9... | collective-permute-start | bytes 368648 | tf_op jit(solution)/shard_map/ppermute | solution.py:91
  5.5 1.2 %collective-permute-done.4.refs_7_ = bf16[96,640]{1,0:T(8,128)(2,1)S(1)} collective-permute-done((bf16[96,640]{1,0:T(8,128)(2,1)}, bf16[96,640]{1,0:T(8,128)(2,1)S(1)}, u32[]{:S(2)}, u32[]{:S(2)}) %collective-permute-start.4) | collective-permute-done | bytes 122912 | tf_op jit(solution)/shard_map/ppermute | solution.py:91
  6.7 1.1 %collective-permute-start.1 = (bf16[96,640]{1,0:T(8,128)(2,1)S(1)}, bf16[96,640]{1,0:T(8,128)(2,1)S(1)}, u32[]{:S(2)}, u32[]{:S(2)}) collective-permute-start(bf16[96,640]{1,0:T(8,128)(2,1)S(1)} %collective-permute-done.refs_1_), channel_id=1, source_target_pairs={{0,4},{1,9},{2,6},{3,11},{8,0},{9,17},{10,2},{11,19},{16,8},{17,25... | collective-permute-start | bytes 368648 | tf_op jit(solution)/shard_map/ppermute | solution.py:91
  9.0 1.3 %collective-permute-start.11 = (bf16[96,640]{1,0:T(8,128)(2,1)S(1)}, bf16[96,640]{1,0:T(8,128)(2,1)S(1)}, u32[]{:S(2)}, u32[]{:S(2)}) collective-permute-start(bf16[96,640]{1,0:T(8,128)(2,1)S(1)} %collective-permute-done.10.refs_6_), channel_id=1, source_target_pairs={{0,8},{1,5},{2,10},{3,7},{8,16},{9,1},{10,18},{11,3},{16,24},{17,9... | collective-permute-start | bytes 368648 | tf_op jit(solution)/shard_map/ppermute | solution.py:91
  11.7 1.3 %collective-permute-start.17 = (bf16[96,640]{1,0:T(8,128)(2,1)S(1)}, bf16[96,640]{1,0:T(8,128)(2,1)S(1)}, u32[]{:S(2)}, u32[]{:S(2)}) collective-permute-start(bf16[96,640]{1,0:T(8,128)(2,1)S(1)} %collective-permute-done.16.refs_13_), channel_id=1, source_target_pairs={{0,8},{1,5},{2,10},{3,7},{8,16},{9,1},{10,18},{11,3},{16,24},{17,9... | collective-permute-start | bytes 368648 | tf_op jit(solution)/shard_map/ppermute | solution.py:91
  13.7 1.3 %collective-permute-start.8 = (bf16[96,640]{1,0:T(8,128)(2,1)S(1)}, bf16[96,640]{1,0:T(8,128)(2,1)S(1)}, u32[]{:S(2)}, u32[]{:S(2)}) collective-permute-start(bf16[96,640]{1,0:T(8,128)(2,1)S(1)} %collective-permute-done.7.refs_1_), channel_id=1, source_target_pairs={{0,4},{1,9},{2,6},{3,11},{8,0},{9,17},{10,2},{11,19},{16,8},{17,25... | collective-permute-start | bytes 368648 | tf_op jit(solution)/shard_map/ppermute | solution.py:91
  16.2 1.3 %collective-permute-start.12 = (bf16[96,640]{1,0:T(8,128)(2,1)S(1)}, bf16[96,640]{1,0:T(8,128)(2,1)S(1)}, u32[]{:S(2)}, u32[]{:S(2)}) collective-permute-start(bf16[96,640]{1,0:T(8,128)(2,1)S(1)} %collective-permute-done.11.refs_5_), channel_id=1, source_target_pairs={{0,8},{1,5},{2,10},{3,7},{8,16},{9,1},{10,18},{11,3},{16,24},{17,9... | collective-permute-start | bytes 368648 | tf_op jit(solution)/shard_map/ppermute | solution.py:91
  18.1 1.3 %collective-permute-start.15 = (bf16[96,640]{1,0:T(8,128)(2,1)S(1)}, bf16[96,640]{1,0:T(8,128)(2,1)S(1)}, u32[]{:S(2)}, u32[]{:S(2)}) collective-permute-start(bf16[96,640]{1,0:T(8,128)(2,1)S(1)} %collective-permute-done.14.refs_9_), channel_id=1, source_target_pairs={{0,4},{1,9},{2,6},{3,11},{8,0},{9,17},{10,2},{11,19},{16,8},{17,25... | collective-permute-start | bytes 368648 | tf_op jit(solution)/shard_map/ppermute | solution.py:91
  19.4 1.4 %collective-permute-start.3 = (bf16[96,640]{1,0:T(8,128)(2,1)S(1)}, bf16[96,640]{1,0:T(8,128)(2,1)S(1)}, u32[]{:S(2)}, u32[]{:S(2)}) collective-permute-start(bf16[96,640]{1,0:T(8,128)(2,1)S(1)} %collective-permute-done.2.refs_3_), channel_id=1, source_target_pairs={{0,4},{1,9},{2,6},{3,11},{8,0},{9,17},{10,2},{11,19},{16,8},{17,25... | collective-permute-start | bytes 368648 | tf_op jit(solution)/shard_map/ppermute | solution.py:91
  21.4 1.3 %collective-permute-start.18 = (bf16[96,640]{1,0:T(8,128)(2,1)S(1)}, bf16[96,640]{1,0:T(8,128)(2,1)S(1)}, u32[]{:S(2)}, u32[]{:S(2)}) collective-permute-start(bf16[96,640]{1,0:T(8,128)(2,1)S(1)} %collective-permute-done.17.refs_12_), channel_id=1, source_target_pairs={{0,8},{1,5},{2,10},{3,7},{8,16},{9,1},{10,18},{11,3},{16,24},{17,9... | collective-permute-start | bytes 368648 | tf_op jit(solution)/shard_map/ppermute | solution.py:91
  26.8 1.2 %collective-permute-done.9.refs_3_ = bf16[96,640]{1,0:T(8,128)(2,1)S(1)} collective-permute-done((bf16[96,640]{1,0:T(8,128)(2,1)S(1)}, bf16[96,640]{1,0:T(8,128)(2,1)S(1)}, u32[]{:S(2)}, u32[]{:S(2)}) %collective-permute-start.9) | collective-permute-done | bytes 122912 | tf_op jit(solution)/shard_map/ppermute | solution.py:91
  28.0 4.6 %shard_map.39 = (f32[5,8,96,128]{3,2,1,0:T(8,128)S(1)}, f32[5,8,96,128]{3,2,1,0:T(8,128)S(1)}, f32[5,8,96,128]{3,2,1,0:T(8,128)S(1)}) custom-call(s32[5]{0:T(128)S(1)} %stack.23.at_ref, bf16[8,96,640]{2,1,0:T(8,128)(2,1)S(1)} %shard_map.37.rows_ref, bf16[96,640]{1,0:T(8,128)(2,1)S(1)} %get-tuple-element.10.refs_0_, ...), custom_call_target="tpu_custom_call" | custom-call | flops 1321205760 | tf_op jit(solution)/shard_map/pallas_call | solution.py:244
  32.6 2.0 %shard_map.40 = bf16[384,640]{1,0:T(8,128)(2,1)S(1)} custom-call(s32[5]{0:T(128)S(1)} %stack.23.at_ref, bf16[8,96,640]{2,1,0:T(8,128)(2,1)S(1)} %shard_map.37.rows_ref, f32[5,8,96,128]{3,2,1,0:T(8,128)S(1)} %get-tuple-element.12.mixed_ref, f32[5,8,96,128]{3,2,1,0:T(8,128)S(1)} %get-tuple-element.13.sum_ref, f32[5,8,96,128]{3,2,1,0:T(8,128)S(1)} %get-tuple-element.14.top_ref, ...), custom_call_target="tpu_custom_call" | custom-call | flops 314572800 | tf_op jit(solution)/shard_map/pallas_call | solution.py:244
  34.5 3.2 %collective-permute-start.21 = (bf16[2,192,640]{2,1,0:T(8,128)(2,1)S(1)}, bf16[2,192,640]{2,1,0:T(8,128)(2,1)S(1)}, u32[]{:S(2)}, u32[]{:S(2)}) collective-permute-start(bf16[2,192,640]{2,1,0:T(8,128)(2,1)S(1)} %bitcast.16), channel_id=1, source_target_pairs={{0,1},{1,0},{2,3},{3,2},{4,5},{5,4},{6,7},{7,6},{8,9},{9,8},{10,11... | collective-permute-start | bytes 1474568 | tf_op jit(solution)/shard_map/ppermute | solution.py:289
  37.7 1.3 %shard_map.41 = f32[192,640]{1,0:T(8,128)S(1)} custom-call(s32[5]{0:T(128)S(1)} %stack.23.at_ref, bf16[8,96,640]{2,1,0:T(8,128)(2,1)S(1)} %shard_map.37.rows_ref, f32[5,8,96,128]{3,2,1,0:T(8,128)S(1)} %get-tuple-element.12.mixed_ref, f32[5,8,96,128]{3,2,1,0:T(8,128)S(1)} %get-tuple-element.13.sum_ref, f32[5,8,96,128]{3,2,1,0:T(8,128)S(1)} %get-tuple-element.14.top_ref, ...), custom_call_target="tpu_custom_call" | custom-call | flops 314572800 | tf_op jit(solution)/shard_map/pallas_call | solution.py:244
  39.6 1.2 %collective-permute-start.22 = (bf16[96,640]{1,0:T(8,128)(2,1)S(1)}, bf16[96,640]{1,0:T(8,128)(2,1)S(1)}, u32[]{:S(2)}, u32[]{:S(2)}) collective-permute-start(bf16[96,640]{1,0:T(8,128)(2,1)S(1)} %get-tuple-element.16.refs_0_), channel_id=1, source_target_pairs={{0,2},{1,3},{2,0},{3,1},{4,6},{5,7},{6,4},{7,5},{8,10},{9,11},{10,... | collective-permute-start | bytes 368648 | tf_op jit(solution)/shard_map/ppermute | solution.py:293
  40.8 1.3 %shard_map.42.kept_ref = f32[192,640]{1,0:T(8,128)S(1)} custom-call(s32[5]{0:T(128)S(1)} %stack.23.at_ref, bf16[8,96,640]{2,1,0:T(8,128)(2,1)S(1)} %shard_map.37.rows_ref, f32[5,8,96,128]{3,2,1,0:T(8,128)S(1)} %get-tuple-element.12.mixed_ref, f32[5,8,96,128]{3,2,1,0:T(8,128)S(1)} %get-tuple-element.13.sum_ref, ...), custom_call_target="tpu_custom_call" | custom-call | flops 314572800 | tf_op jit(solution)/shard_map/pallas_call | solution.py:244
  42.1 1.7 %collective-permute-done.24.from_x_ref = bf16[96,640]{1,0:T(8,128)(2,1)S(1)} collective-permute-done((bf16[96,640]{1,0:T(8,128)(2,1)S(1)}, bf16[96,640]{1,0:T(8,128)(2,1)S(1)}, u32[]{:S(2)}, u32[]{:S(2)}) %collective-permute-start.24) | collective-permute-done | bytes 122912 | tf_op jit(solution)/shard_map/ppermute | solution.py:293
  43.9 5.3 %collective-permute-start.25 = (bf16[96,640]{1,0:T(8,128)(2,1)S(1)}, bf16[96,640]{1,0:T(8,128)(2,1)S(1)}, u32[]{:S(2)}, u32[]{:S(2)}) collective-permute-start(bf16[96,640]{1,0:T(8,128)(2,1)S(1)} %shard_map.44), channel_id=1, source_target_pairs={{0,8},{1,28},{2,0},{3,20},{4,24},{5,12},{6,16},{7,4},{8,25},{9,5},... | collective-permute-start | bytes 368648 | tf_op jit(solution)/shard_map/ppermute | solution.py:305
  49.2 1.4 %collective-permute-start.23 = (bf16[96,640]{1,0:T(8,128)(2,1)S(1)}, bf16[96,640]{1,0:T(8,128)(2,1)S(1)}, u32[]{:S(2)}, u32[]{:S(2)}) collective-permute-start(bf16[96,640]{1,0:T(8,128)(2,1)S(1)} %shard_map.43), channel_id=1, source_target_pairs={{0,24},{1,12},{2,16},{3,4},{4,8},{5,28},{6,0},{7,20},{8,1},{9,29},... | collective-permute-start | bytes 368648 | tf_op jit(solution)/shard_map/ppermute | solution.py:305
  50.6 1.7 %collective-permute-done.25 = bf16[96,640]{1,0:T(8,128)(2,1)S(1)} collective-permute-done((bf16[96,640]{1,0:T(8,128)(2,1)S(1)}, bf16[96,640]{1,0:T(8,128)(2,1)S(1)}, u32[]{:S(2)}, u32[]{:S(2)}) %collective-permute-start.25) | collective-permute-done | bytes 122912 | tf_op jit(solution)/shard_map/ppermute | solution.py:305
  52.3 4.0 %collective-permute-done.23 = bf16[96,640]{1,0:T(8,128)(2,1)S(1)} collective-permute-done((bf16[96,640]{1,0:T(8,128)(2,1)S(1)}, bf16[96,640]{1,0:T(8,128)(2,1)S(1)}, u32[]{:S(2)}, u32[]{:S(2)}) %collective-permute-start.23) | collective-permute-done | bytes 122912 | tf_op jit(solution)/shard_map/ppermute | solution.py:305
  (46 shorter events, 12.8 us)
Async XLA Ops:
  0.0 5.2 %collective-permute-start = (bf16[96,640]{1,0:T(8,128)(2,1)}, bf16[96,640]{1,0:T(8,128)(2,1)S(1)}, u32[]{:S(2)}, u32[]{:S(2)}) collective-permute-start(bf16[96,640]{1,0:T(8,128)(2,1)} %refs_0_.1), channel_id=1, source_target_pairs={{0,4},{1,9},{2,6},{3,11},{8,0},{9,17},{10,2},{11,19},{16,8},{17,25... | collective-permute-start | bytes 368648 | tf_op jit(solution)/shard_map/ppermute | solution.py:91
  1.3 5.4 %collective-permute-start.4 = (bf16[96,640]{1,0:T(8,128)(2,1)}, bf16[96,640]{1,0:T(8,128)(2,1)S(1)}, u32[]{:S(2)}, u32[]{:S(2)}) collective-permute-start(bf16[96,640]{1,0:T(8,128)(2,1)} %refs_0_.1), channel_id=1, source_target_pairs={{0,8},{1,5},{2,10},{3,7},{8,16},{9,1},{10,18},{11,3},{16,24},{17,9... | collective-permute-start | bytes 368648 | tf_op jit(solution)/shard_map/ppermute | solution.py:91
  2.4 5.6 %collective-permute-start.10 = (bf16[96,640]{1,0:T(8,128)(2,1)S(1)}, bf16[96,640]{1,0:T(8,128)(2,1)S(1)}, u32[]{:S(2)}, u32[]{:S(2)}) collective-permute-start(bf16[96,640]{1,0:T(8,128)(2,1)S(1)} %get-tuple-element.10.refs_0_), channel_id=1, source_target_pairs={{0,8},{1,5},{2,10},{3,7},{8,16},{9,1},{10,18},{11,3},{16,24},{17,9... | collective-permute-start | bytes 368648 | tf_op jit(solution)/shard_map/ppermute | solution.py:91
  3.7 5.3 %collective-permute-start.13 = (bf16[96,640]{1,0:T(8,128)(2,1)S(1)}, bf16[96,640]{1,0:T(8,128)(2,1)S(1)}, u32[]{:S(2)}, u32[]{:S(2)}) collective-permute-start(bf16[96,640]{1,0:T(8,128)(2,1)S(1)} %get-tuple-element.11.refs_7_), channel_id=1, source_target_pairs={{0,4},{1,9},{2,6},{3,11},{8,0},{9,17},{10,2},{11,19},{16,8},{17,25... | collective-permute-start | bytes 368648 | tf_op jit(solution)/shard_map/ppermute | solution.py:91
  4.0 6.4 %collective-permute-start.16 = (bf16[96,640]{1,0:T(8,128)(2,1)S(1)}, bf16[96,640]{1,0:T(8,128)(2,1)S(1)}, u32[]{:S(2)}, u32[]{:S(2)}) collective-permute-start(bf16[96,640]{1,0:T(8,128)(2,1)S(1)} %get-tuple-element.11.refs_7_), channel_id=1, source_target_pairs={{0,8},{1,5},{2,10},{3,7},{8,16},{9,1},{10,18},{11,3},{16,24},{17,9... | collective-permute-start | bytes 368648 | tf_op jit(solution)/shard_map/ppermute | solution.py:91
  5.2 6.5 %collective-permute-start.7 = (bf16[96,640]{1,0:T(8,128)(2,1)S(1)}, bf16[96,640]{1,0:T(8,128)(2,1)S(1)}, u32[]{:S(2)}, u32[]{:S(2)}) collective-permute-start(bf16[96,640]{1,0:T(8,128)(2,1)S(1)} %get-tuple-element.10.refs_0_), channel_id=1, source_target_pairs={{0,4},{1,9},{2,6},{3,11},{8,0},{9,17},{10,2},{11,19},{16,8},{17,25... | collective-permute-start | bytes 368648 | tf_op jit(solution)/shard_map/ppermute | solution.py:91
  6.7 6.8 %collective-permute-start.1 = (bf16[96,640]{1,0:T(8,128)(2,1)S(1)}, bf16[96,640]{1,0:T(8,128)(2,1)S(1)}, u32[]{:S(2)}, u32[]{:S(2)}) collective-permute-start(bf16[96,640]{1,0:T(8,128)(2,1)S(1)} %collective-permute-done.refs_1_), channel_id=1, source_target_pairs={{0,4},{1,9},{2,6},{3,11},{8,0},{9,17},{10,2},{11,19},{16,8},{17,25... | collective-permute-start | bytes 368648 | tf_op jit(solution)/shard_map/ppermute | solution.py:91
  8.0 5.7 %collective-permute-start.5 = (bf16[96,640]{1,0:T(8,128)(2,1)S(1)}, bf16[96,640]{1,0:T(8,128)(2,1)S(1)}, u32[]{:S(2)}, u32[]{:S(2)}) collective-permute-start(bf16[96,640]{1,0:T(8,128)(2,1)S(1)} %collective-permute-done.4.refs_7_), channel_id=1, source_target_pairs={{0,8},{1,5},{2,10},{3,7},{8,16},{9,1},{10,18},{11,3},{16,24},{17,9... | collective-permute-start | bytes 368648 | tf_op jit(solution)/shard_map/ppermute | solution.py:91
  9.0 6.9 %collective-permute-start.11 = (bf16[96,640]{1,0:T(8,128)(2,1)S(1)}, bf16[96,640]{1,0:T(8,128)(2,1)S(1)}, u32[]{:S(2)}, u32[]{:S(2)}) collective-permute-start(bf16[96,640]{1,0:T(8,128)(2,1)S(1)} %collective-permute-done.10.refs_6_), channel_id=1, source_target_pairs={{0,8},{1,5},{2,10},{3,7},{8,16},{9,1},{10,18},{11,3},{16,24},{17,9... | collective-permute-start | bytes 368648 | tf_op jit(solution)/shard_map/ppermute | solution.py:91
  10.3 5.9 %collective-permute-start.14 = (bf16[96,640]{1,0:T(8,128)(2,1)S(1)}, bf16[96,640]{1,0:T(8,128)(2,1)S(1)}, u32[]{:S(2)}, u32[]{:S(2)}) collective-permute-start(bf16[96,640]{1,0:T(8,128)(2,1)S(1)} %collective-permute-done.13.refs_8_), channel_id=1, source_target_pairs={{0,4},{1,9},{2,6},{3,11},{8,0},{9,17},{10,2},{11,19},{16,8},{17,25... | collective-permute-start | bytes 368648 | tf_op jit(solution)/shard_map/ppermute | solution.py:91
  11.7 6.4 %collective-permute-start.17 = (bf16[96,640]{1,0:T(8,128)(2,1)S(1)}, bf16[96,640]{1,0:T(8,128)(2,1)S(1)}, u32[]{:S(2)}, u32[]{:S(2)}) collective-permute-start(bf16[96,640]{1,0:T(8,128)(2,1)S(1)} %collective-permute-done.16.refs_13_), channel_id=1, source_target_pairs={{0,8},{1,5},{2,10},{3,7},{8,16},{9,1},{10,18},{11,3},{16,24},{17,9... | collective-permute-start | bytes 368648 | tf_op jit(solution)/shard_map/ppermute | solution.py:91
  13.5 5.9 %collective-permute-start.2 = (bf16[96,640]{1,0:T(8,128)(2,1)S(1)}, bf16[96,640]{1,0:T(8,128)(2,1)S(1)}, u32[]{:S(2)}, u32[]{:S(2)}) collective-permute-start(bf16[96,640]{1,0:T(8,128)(2,1)S(1)} %collective-permute-done.1.refs_2_), channel_id=1, source_target_pairs={{0,4},{1,9},{2,6},{3,11},{8,0},{9,17},{10,2},{11,19},{16,8},{17,25... | collective-permute-start | bytes 368648 | tf_op jit(solution)/shard_map/ppermute | solution.py:91
  13.7 7.7 %collective-permute-start.8 = (bf16[96,640]{1,0:T(8,128)(2,1)S(1)}, bf16[96,640]{1,0:T(8,128)(2,1)S(1)}, u32[]{:S(2)}, u32[]{:S(2)}) collective-permute-start(bf16[96,640]{1,0:T(8,128)(2,1)S(1)} %collective-permute-done.7.refs_1_), channel_id=1, source_target_pairs={{0,4},{1,9},{2,6},{3,11},{8,0},{9,17},{10,2},{11,19},{16,8},{17,25... | collective-permute-start | bytes 368648 | tf_op jit(solution)/shard_map/ppermute | solution.py:91
  15.9 6.8 %collective-permute-start.6 = (bf16[96,640]{1,0:T(8,128)(2,1)S(1)}, bf16[96,640]{1,0:T(8,128)(2,1)S(1)}, u32[]{:S(2)}, u32[]{:S(2)}) collective-permute-start(bf16[96,640]{1,0:T(8,128)(2,1)S(1)} %collective-permute-done.5.refs_6_), channel_id=1, source_target_pairs={{0,8},{1,5},{2,10},{3,7},{8,16},{9,1},{10,18},{11,3},{16,24},{17,9... | collective-permute-start | bytes 368648 | tf_op jit(solution)/shard_map/ppermute | solution.py:91
  16.2 7.0 %collective-permute-start.12 = (bf16[96,640]{1,0:T(8,128)(2,1)S(1)}, bf16[96,640]{1,0:T(8,128)(2,1)S(1)}, u32[]{:S(2)}, u32[]{:S(2)}) collective-permute-start(bf16[96,640]{1,0:T(8,128)(2,1)S(1)} %collective-permute-done.11.refs_5_), channel_id=1, source_target_pairs={{0,8},{1,5},{2,10},{3,7},{8,16},{9,1},{10,18},{11,3},{16,24},{17,9... | collective-permute-start | bytes 368648 | tf_op jit(solution)/shard_map/ppermute | solution.py:91
  18.1 6.2 %collective-permute-start.15 = (bf16[96,640]{1,0:T(8,128)(2,1)S(1)}, bf16[96,640]{1,0:T(8,128)(2,1)S(1)}, u32[]{:S(2)}, u32[]{:S(2)}) collective-permute-start(bf16[96,640]{1,0:T(8,128)(2,1)S(1)} %collective-permute-done.14.refs_9_), channel_id=1, source_target_pairs={{0,4},{1,9},{2,6},{3,11},{8,0},{9,17},{10,2},{11,19},{16,8},{17,25... | collective-permute-start | bytes 368648 | tf_op jit(solution)/shard_map/ppermute | solution.py:91
  19.4 6.4 %collective-permute-start.3 = (bf16[96,640]{1,0:T(8,128)(2,1)S(1)}, bf16[96,640]{1,0:T(8,128)(2,1)S(1)}, u32[]{:S(2)}, u32[]{:S(2)}) collective-permute-start(bf16[96,640]{1,0:T(8,128)(2,1)S(1)} %collective-permute-done.2.refs_3_), channel_id=1, source_target_pairs={{0,4},{1,9},{2,6},{3,11},{8,0},{9,17},{10,2},{11,19},{16,8},{17,25... | collective-permute-start | bytes 368648 | tf_op jit(solution)/shard_map/ppermute | solution.py:91
  21.4 5.4 %collective-permute-start.18 = (bf16[96,640]{1,0:T(8,128)(2,1)S(1)}, bf16[96,640]{1,0:T(8,128)(2,1)S(1)}, u32[]{:S(2)}, u32[]{:S(2)}) collective-permute-start(bf16[96,640]{1,0:T(8,128)(2,1)S(1)} %collective-permute-done.17.refs_12_), channel_id=1, source_target_pairs={{0,8},{1,5},{2,10},{3,7},{8,16},{9,1},{10,18},{11,3},{16,24},{17,9... | collective-permute-start | bytes 368648 | tf_op jit(solution)/shard_map/ppermute | solution.py:91
  22.7 5.3 %collective-permute-start.9 = (bf16[96,640]{1,0:T(8,128)(2,1)S(1)}, bf16[96,640]{1,0:T(8,128)(2,1)S(1)}, u32[]{:S(2)}, u32[]{:S(2)}) collective-permute-start(bf16[96,640]{1,0:T(8,128)(2,1)S(1)} %collective-permute-done.8.refs_2_), channel_id=1, source_target_pairs={{0,4},{1,9},{2,6},{3,11},{8,0},{9,17},{10,2},{11,19},{16,8},{17,25... | collective-permute-start | bytes 368648 | tf_op jit(solution)/shard_map/ppermute | solution.py:91
  23.2 9.3 %collective-permute-start.19 = (bf16[96,640]{1,0:T(8,128)(2,1)S(1)}, bf16[96,640]{1,0:T(8,128)(2,1)S(1)}, u32[]{:S(2)}, u32[]{:S(2)}) collective-permute-start(bf16[96,640]{1,0:T(8,128)(2,1)S(1)} %collective-permute-done.12.refs_4_), channel_id=1, source_target_pairs={{0,8},{1,5},{2,10},{3,7},{8,16},{9,1},{10,18},{11,3},{16,24},{17,9... | collective-permute-start | bytes 368648 | tf_op jit(solution)/shard_map/ppermute | solution.py:91
  24.2 8.3 %collective-permute-start.20 = (bf16[96,640]{1,0:T(8,128)(2,1)S(1)}, bf16[96,640]{1,0:T(8,128)(2,1)S(1)}, u32[]{:S(2)}, u32[]{:S(2)}) collective-permute-start(bf16[96,640]{1,0:T(8,128)(2,1)S(1)} %collective-permute-done.15.refs_10_), channel_id=1, source_target_pairs={{0,4},{1,9},{2,6},{3,11},{8,0},{9,17},{10,2},{11,19},{16,8},{17,25... | collective-permute-start | bytes 368648 | tf_op jit(solution)/shard_map/ppermute | solution.py:91
  39.6 9.6 %collective-permute-start.22 = (bf16[96,640]{1,0:T(8,128)(2,1)S(1)}, bf16[96,640]{1,0:T(8,128)(2,1)S(1)}, u32[]{:S(2)}, u32[]{:S(2)}) collective-permute-start(bf16[96,640]{1,0:T(8,128)(2,1)S(1)} %get-tuple-element.16.refs_0_), channel_id=1, source_target_pairs={{0,2},{1,3},{2,0},{3,1},{4,6},{5,7},{6,4},{7,5},{8,10},{9,11},{10,... | collective-permute-start | bytes 368648 | tf_op jit(solution)/shard_map/ppermute | solution.py:293
  43.9 8.4 %collective-permute-start.25 = (bf16[96,640]{1,0:T(8,128)(2,1)S(1)}, bf16[96,640]{1,0:T(8,128)(2,1)S(1)}, u32[]{:S(2)}, u32[]{:S(2)}) collective-permute-start(bf16[96,640]{1,0:T(8,128)(2,1)S(1)} %shard_map.44), channel_id=1, source_target_pairs={{0,8},{1,28},{2,0},{3,20},{4,24},{5,12},{6,16},{7,4},{8,25},{9,5},... | collective-permute-start | bytes 368648 | tf_op jit(solution)/shard_map/ppermute | solution.py:305
  49.2 7.1 %collective-permute-start.23 = (bf16[96,640]{1,0:T(8,128)(2,1)S(1)}, bf16[96,640]{1,0:T(8,128)(2,1)S(1)}, u32[]{:S(2)}, u32[]{:S(2)}) collective-permute-start(bf16[96,640]{1,0:T(8,128)(2,1)S(1)} %shard_map.43), channel_id=1, source_target_pairs={{0,24},{1,12},{2,16},{3,4},{4,8},{5,28},{6,0},{7,20},{8,1},{9,29},... | collective-permute-start | bytes 368648 | tf_op jit(solution)/shard_map/ppermute | solution.py:305
  (5 other events, 16.9 us)

commit v33 on v27

--- a/solution.py
+++ b/solution.py
@@ -167,7 +167,7 @@
     blocks = []
     for slot in range(2):
         row_y = core ^ flip_core
-        to = look_up(sum(PATTERNS, ()), 4 * ((slot ^ y ^ row_y) + 2 * (x ^ flip_x)) + z)
+        to = look_up(sum(PATTERNS, ()), 4 * ((slot ^ y ^ row_y ^ x ^ flip_x) + 2 * (x ^ flip_x)) + z)
         owner = to + row_y * (n - 1 - 2 * to)
         blocks.append(ring_distance(at_ref, owner, n))
     return blocks
@@ -297,14 +297,15 @@
         pairs = []
         for f in range(n):
             for h in range(4):
-                to = PATTERNS[(slot ^ (f & 1) ^ (h & 1)) + 2 * (h >> 1)][f >> 1]
+                to = PATTERNS[(slot ^ (f & 1) ^ (h & 1) ^ (h >> 1)) + 2 * (h >> 1)][f >> 1]
                 pairs.append((4 * f + h, 4 * (2 * to + (h & 1)) + (f >> 1)))
         (total,) = call(
             functools.partial(sum_kernel, part), (), [kept, from_core, from_x[slot]], [((ROWS, cols), bf16)], 0
         )
         arrived.append(lax.ppermute(total, ("frames", "heads"), pairs))
     patterns = [[p[source] for p in PATTERNS].index(to) for source in range(4) for to in range(4)]
-    straight = (look_up(patterns, 4 * head + z) ^ y) & 1 == 0
+    pattern = look_up(patterns, 4 * head + z)
+    straight = (pattern ^ (pattern >> 1) ^ y) & 1 == 0
     low, high = arrived
     return jnp.concatenate([jnp.where(straight, low, high), jnp.where(straight, high, low)], axis=1)
 

time: 56.9 us -> 56.9 us (level); the launches traced: 56.8 us -> 55.8 us
  waiting for transfers between devices: 15.2 us -> 14.1 us
    ppermute x2, waiting for transfers between devices: 5.33 us -> 4.26 us  [on_device_ring(): arrived.append(lax.ppermute(total, ('frames', 'heads'), pairs))]
where the time goes in v33:
time: 56.9 us; the launch traced here: 55.8 us
  starting transfers between devices  29.4 us (52%)
  waiting for transfers between devices  14.1 us (25%)
  Pallas kernels  9.43 us (17%)
  local copies, waits for them, and re-layouts  1.94 us (3%)
  other arithmetic  0.79 us (1%)
    ppermute x21, starting transfers between devices, hop(): return lax.ppermute(x, ('frames', 'heads'), pairs)  17.9 us
    pallas_call x8, Pallas kernels, call(): pl.pallas_call(kernel, out_shape=[jax.ShapeDtypeStruct(shape, dtype) for...  9.43 us
    ppermute x21, waiting for transfers between devices, hop(): return lax.ppermute(x, ('frames', 'heads'), pairs)  8.01 us
    ppermute x2, starting transfers between devices, on_device_ring(): arrived.append(lax.ppermute(total, ('frames', 'heads'), pairs))  6.78 us
    ppermute x2, waiting for transfers between devices, on_device_ring(): arrived.append(lax.ppermute(total, ('frames', 'heads'), pairs))  4.26 us
    ppermute x1, starting transfers between devices, on_device_ring(): from_core = lax.ppermute(given, 'heads', [(h, h ^ 1) for h in range(4)])  3.17 us
    unnamed x6, local copies, waits for them, and re-layouts  1.85 us
    ppermute x2, waiting for transfers between devices, on_device_ring(): lax.ppermute(block, 'heads', [(h, h ^ 2) for h in range(4)])  1.68 us
  transfers between devices with their start and end apart: 26, of which 15 were waited for; matrix products, arithmetic and copies ran while one was open for 0% of the time, Pallas kernels for 13%

profile of v33, /device:TPU:3, one launch (start us, length us, event | category | flops | bytes accessed | tf_op | source)
XLA Modules:
  0.0 55.8 jit_solution(6021857009571951702)
XLA Ops:
  0.0 1.2 %collective-permute-start = (bf16[96,640]{1,0:T(8,128)(2,1)}, bf16[96,640]{1,0:T(8,128)(2,1)S(1)}, u32[]{:S(2)}, u32[]{:S(2)}) collective-permute-start(bf16[96,640]{1,0:T(8,128)(2,1)} %refs_0_.1), channel_id=1, source_target_pairs={{0,8},{1,5},{2,10},{3,7},{8,16},{9,1},{10,18},{11,3},{16,24},{17,9... | collective-permute-start | bytes 368648 | tf_op jit(solution)/shard_map/ppermute | solution.py:91
  2.4 1.3 %collective-permute-start.10 = (bf16[96,640]{1,0:T(8,128)(2,1)S(1)}, bf16[96,640]{1,0:T(8,128)(2,1)S(1)}, u32[]{:S(2)}, u32[]{:S(2)}) collective-permute-start(bf16[96,640]{1,0:T(8,128)(2,1)S(1)} %get-tuple-element.10.refs_0_), channel_id=1, source_target_pairs={{0,4},{1,9},{2,6},{3,11},{8,0},{9,17},{10,2},{11,19},{16,8},{17,25... | collective-permute-start | bytes 368648 | tf_op jit(solution)/shard_map/ppermute | solution.py:91
  4.0 1.3 %collective-permute-start.16 = (bf16[96,640]{1,0:T(8,128)(2,1)S(1)}, bf16[96,640]{1,0:T(8,128)(2,1)S(1)}, u32[]{:S(2)}, u32[]{:S(2)}) collective-permute-start(bf16[96,640]{1,0:T(8,128)(2,1)S(1)} %get-tuple-element.11.refs_7_), channel_id=1, source_target_pairs={{0,4},{1,9},{2,6},{3,11},{8,0},{9,17},{10,2},{11,19},{16,8},{17,25... | collective-permute-start | bytes 368648 | tf_op jit(solution)/shard_map/ppermute | solution.py:91
  5.5 1.2 %collective-permute-done.4.refs_7_ = bf16[96,640]{1,0:T(8,128)(2,1)S(1)} collective-permute-done((bf16[96,640]{1,0:T(8,128)(2,1)}, bf16[96,640]{1,0:T(8,128)(2,1)S(1)}, u32[]{:S(2)}, u32[]{:S(2)}) %collective-permute-start.4) | collective-permute-done | bytes 122912 | tf_op jit(solution)/shard_map/ppermute | solution.py:91
  9.1 1.3 %collective-permute-start.11 = (bf16[96,640]{1,0:T(8,128)(2,1)S(1)}, bf16[96,640]{1,0:T(8,128)(2,1)S(1)}, u32[]{:S(2)}, u32[]{:S(2)}) collective-permute-start(bf16[96,640]{1,0:T(8,128)(2,1)S(1)} %collective-permute-done.10.refs_6_), channel_id=1, source_target_pairs={{0,4},{1,9},{2,6},{3,11},{8,0},{9,17},{10,2},{11,19},{16,8},{17,25... | collective-permute-start | bytes 368648 | tf_op jit(solution)/shard_map/ppermute | solution.py:91
  11.7 1.3 %collective-permute-start.17 = (bf16[96,640]{1,0:T(8,128)(2,1)S(1)}, bf16[96,640]{1,0:T(8,128)(2,1)S(1)}, u32[]{:S(2)}, u32[]{:S(2)}) collective-permute-start(bf16[96,640]{1,0:T(8,128)(2,1)S(1)} %collective-permute-done.16.refs_13_), channel_id=1, source_target_pairs={{0,4},{1,9},{2,6},{3,11},{8,0},{9,17},{10,2},{11,19},{16,8},{17,25... | collective-permute-start | bytes 368648 | tf_op jit(solution)/shard_map/ppermute | solution.py:91
  13.7 1.2 %collective-permute-start.8 = (bf16[96,640]{1,0:T(8,128)(2,1)S(1)}, bf16[96,640]{1,0:T(8,128)(2,1)S(1)}, u32[]{:S(2)}, u32[]{:S(2)}) collective-permute-start(bf16[96,640]{1,0:T(8,128)(2,1)S(1)} %collective-permute-done.7.refs_1_), channel_id=1, source_target_pairs={{0,8},{1,5},{2,10},{3,7},{8,16},{9,1},{10,18},{11,3},{16,24},{17,9... | collective-permute-start | bytes 368648 | tf_op jit(solution)/shard_map/ppermute | solution.py:91
  16.3 1.3 %collective-permute-start.12 = (bf16[96,640]{1,0:T(8,128)(2,1)S(1)}, bf16[96,640]{1,0:T(8,128)(2,1)S(1)}, u32[]{:S(2)}, u32[]{:S(2)}) collective-permute-start(bf16[96,640]{1,0:T(8,128)(2,1)S(1)} %collective-permute-done.11.refs_5_), channel_id=1, source_target_pairs={{0,4},{1,9},{2,6},{3,11},{8,0},{9,17},{10,2},{11,19},{16,8},{17,25... | collective-permute-start | bytes 368648 | tf_op jit(solution)/shard_map/ppermute | solution.py:91
  18.1 1.2 %collective-permute-start.15 = (bf16[96,640]{1,0:T(8,128)(2,1)S(1)}, bf16[96,640]{1,0:T(8,128)(2,1)S(1)}, u32[]{:S(2)}, u32[]{:S(2)}) collective-permute-start(bf16[96,640]{1,0:T(8,128)(2,1)S(1)} %collective-permute-done.14.refs_9_), channel_id=1, source_target_pairs={{0,8},{1,5},{2,10},{3,7},{8,16},{9,1},{10,18},{11,3},{16,24},{17,9... | collective-permute-start | bytes 368648 | tf_op jit(solution)/shard_map/ppermute | solution.py:91
  19.3 1.3 %collective-permute-start.3 = (bf16[96,640]{1,0:T(8,128)(2,1)S(1)}, bf16[96,640]{1,0:T(8,128)(2,1)S(1)}, u32[]{:S(2)}, u32[]{:S(2)}) collective-permute-start(bf16[96,640]{1,0:T(8,128)(2,1)S(1)} %collective-permute-done.2.refs_3_), channel_id=1, source_target_pairs={{0,8},{1,5},{2,10},{3,7},{8,16},{9,1},{10,18},{11,3},{16,24},{17,9... | collective-permute-start | bytes 368648 | tf_op jit(solution)/shard_map/ppermute | solution.py:91
  21.4 1.3 %collective-permute-start.18 = (bf16[96,640]{1,0:T(8,128)(2,1)S(1)}, bf16[96,640]{1,0:T(8,128)(2,1)S(1)}, u32[]{:S(2)}, u32[]{:S(2)}) collective-permute-start(bf16[96,640]{1,0:T(8,128)(2,1)S(1)} %collective-permute-done.17.refs_12_), channel_id=1, source_target_pairs={{0,4},{1,9},{2,6},{3,11},{8,0},{9,17},{10,2},{11,19},{16,8},{17,25... | collective-permute-start | bytes 368648 | tf_op jit(solution)/shard_map/ppermute | solution.py:91
  24.7 1.2 %collective-permute-done.3.refs_4_ = bf16[96,640]{1,0:T(8,128)(2,1)S(1)} collective-permute-done((bf16[96,640]{1,0:T(8,128)(2,1)S(1)}, bf16[96,640]{1,0:T(8,128)(2,1)S(1)}, u32[]{:S(2)}, u32[]{:S(2)}) %collective-permute-start.3) | collective-permute-done | bytes 122912 | tf_op jit(solution)/shard_map/ppermute | solution.py:91
  26.8 1.2 %collective-permute-done.9.refs_3_ = bf16[96,640]{1,0:T(8,128)(2,1)S(1)} collective-permute-done((bf16[96,640]{1,0:T(8,128)(2,1)S(1)}, bf16[96,640]{1,0:T(8,128)(2,1)S(1)}, u32[]{:S(2)}, u32[]{:S(2)}) %collective-permute-start.9) | collective-permute-done | bytes 122912 | tf_op jit(solution)/shard_map/ppermute | solution.py:91
  28.0 4.6 %shard_map.39 = (f32[5,8,96,128]{3,2,1,0:T(8,128)S(1)}, f32[5,8,96,128]{3,2,1,0:T(8,128)S(1)}, f32[5,8,96,128]{3,2,1,0:T(8,128)S(1)}) custom-call(s32[5]{0:T(128)S(1)} %stack.23.at_ref, bf16[8,96,640]{2,1,0:T(8,128)(2,1)S(1)} %shard_map.37.rows_ref, bf16[96,640]{1,0:T(8,128)(2,1)S(1)} %get-tuple-element.10.refs_0_, ...), custom_call_target="tpu_custom_call" | custom-call | flops 1321205760 | tf_op jit(solution)/shard_map/pallas_call | solution.py:244
  32.6 2.0 %shard_map.40 = bf16[384,640]{1,0:T(8,128)(2,1)S(1)} custom-call(s32[5]{0:T(128)S(1)} %stack.23.at_ref, bf16[8,96,640]{2,1,0:T(8,128)(2,1)S(1)} %shard_map.37.rows_ref, f32[5,8,96,128]{3,2,1,0:T(8,128)S(1)} %get-tuple-element.12.mixed_ref, f32[5,8,96,128]{3,2,1,0:T(8,128)S(1)} %get-tuple-element.13.sum_ref, f32[5,8,96,128]{3,2,1,0:T(8,128)S(1)} %get-tuple-element.14.top_ref, ...), custom_call_target="tpu_custom_call" | custom-call | flops 314572800 | tf_op jit(solution)/shard_map/pallas_call | solution.py:244
  34.6 3.2 %collective-permute-start.21 = (bf16[2,192,640]{2,1,0:T(8,128)(2,1)S(1)}, bf16[2,192,640]{2,1,0:T(8,128)(2,1)S(1)}, u32[]{:S(2)}, u32[]{:S(2)}) collective-permute-start(bf16[2,192,640]{2,1,0:T(8,128)(2,1)S(1)} %bitcast.16), channel_id=1, source_target_pairs={{0,1},{1,0},{2,3},{3,2},{4,5},{5,4},{6,7},{7,6},{8,9},{9,8},{10,11... | collective-permute-start | bytes 1474568 | tf_op jit(solution)/shard_map/ppermute | solution.py:289
  37.8 1.3 %shard_map.41 = f32[192,640]{1,0:T(8,128)S(1)} custom-call(s32[5]{0:T(128)S(1)} %stack.23.at_ref, bf16[8,96,640]{2,1,0:T(8,128)(2,1)S(1)} %shard_map.37.rows_ref, f32[5,8,96,128]{3,2,1,0:T(8,128)S(1)} %get-tuple-element.12.mixed_ref, f32[5,8,96,128]{3,2,1,0:T(8,128)S(1)} %get-tuple-element.13.sum_ref, f32[5,8,96,128]{3,2,1,0:T(8,128)S(1)} %get-tuple-element.14.top_ref, ...), custom_call_target="tpu_custom_call" | custom-call | flops 314572800 | tf_op jit(solution)/shard_map/pallas_call | solution.py:244
  39.6 1.2 %collective-permute-start.22 = (bf16[96,640]{1,0:T(8,128)(2,1)S(1)}, bf16[96,640]{1,0:T(8,128)(2,1)S(1)}, u32[]{:S(2)}, u32[]{:S(2)}) collective-permute-start(bf16[96,640]{1,0:T(8,128)(2,1)S(1)} %get-tuple-element.16.refs_0_), channel_id=1, source_target_pairs={{0,2},{1,3},{2,0},{3,1},{4,6},{5,7},{6,4},{7,5},{8,10},{9,11},{10,... | collective-permute-start | bytes 368648 | tf_op jit(solution)/shard_map/ppermute | solution.py:293
  40.9 1.4 %shard_map.42.kept_ref = f32[192,640]{1,0:T(8,128)S(1)} custom-call(s32[5]{0:T(128)S(1)} %stack.23.at_ref, bf16[8,96,640]{2,1,0:T(8,128)(2,1)S(1)} %shard_map.37.rows_ref, f32[5,8,96,128]{3,2,1,0:T(8,128)S(1)} %get-tuple-element.12.mixed_ref, f32[5,8,96,128]{3,2,1,0:T(8,128)S(1)} %get-tuple-element.13.sum_ref, ...), custom_call_target="tpu_custom_call" | custom-call | flops 314572800 | tf_op jit(solution)/shard_map/pallas_call | solution.py:244
  42.2 1.7 %collective-permute-done.24.from_x_ref = bf16[96,640]{1,0:T(8,128)(2,1)S(1)} collective-permute-done((bf16[96,640]{1,0:T(8,128)(2,1)S(1)}, bf16[96,640]{1,0:T(8,128)(2,1)S(1)}, u32[]{:S(2)}, u32[]{:S(2)}) %collective-permute-start.24) | collective-permute-done | bytes 122912 | tf_op jit(solution)/shard_map/ppermute | solution.py:293
  43.9 3.5 %collective-permute-start.25 = (bf16[96,640]{1,0:T(8,128)(2,1)S(1)}, bf16[96,640]{1,0:T(8,128)(2,1)S(1)}, u32[]{:S(2)}, u32[]{:S(2)}) collective-permute-start(bf16[96,640]{1,0:T(8,128)(2,1)S(1)} %shard_map.44), channel_id=1, source_target_pairs={{0,8},{1,28},{2,16},{3,4},{4,24},{5,12},{6,0},{7,20},{8,25},{9,5},... | collective-permute-start | bytes 368648 | tf_op jit(solution)/shard_map/ppermute | solution.py:305
  47.5 3.3 %collective-permute-start.23 = (bf16[96,640]{1,0:T(8,128)(2,1)S(1)}, bf16[96,640]{1,0:T(8,128)(2,1)S(1)}, u32[]{:S(2)}, u32[]{:S(2)}) collective-permute-start(bf16[96,640]{1,0:T(8,128)(2,1)S(1)} %shard_map.43), channel_id=1, source_target_pairs={{0,24},{1,12},{2,0},{3,20},{4,8},{5,28},{6,16},{7,4},{8,1},{9,29},... | collective-permute-start | bytes 368648 | tf_op jit(solution)/shard_map/ppermute | solution.py:305
  50.8 1.1 %collective-permute-done.25 = bf16[96,640]{1,0:T(8,128)(2,1)S(1)} collective-permute-done((bf16[96,640]{1,0:T(8,128)(2,1)S(1)}, bf16[96,640]{1,0:T(8,128)(2,1)S(1)}, u32[]{:S(2)}, u32[]{:S(2)}) %collective-permute-start.25) | collective-permute-done | bytes 122912 | tf_op jit(solution)/shard_map/ppermute | solution.py:305
  51.9 3.1 %collective-permute-done.23 = bf16[96,640]{1,0:T(8,128)(2,1)S(1)} collective-permute-done((bf16[96,640]{1,0:T(8,128)(2,1)S(1)}, bf16[96,640]{1,0:T(8,128)(2,1)S(1)}, u32[]{:S(2)}, u32[]{:S(2)}) %collective-permute-start.23) | collective-permute-done | bytes 122912 | tf_op jit(solution)/shard_map/ppermute | solution.py:305
  (46 shorter events, 13.0 us)
Async XLA Ops:
  0.0 5.3 %collective-permute-start = (bf16[96,640]{1,0:T(8,128)(2,1)}, bf16[96,640]{1,0:T(8,128)(2,1)S(1)}, u32[]{:S(2)}, u32[]{:S(2)}) collective-permute-start(bf16[96,640]{1,0:T(8,128)(2,1)} %refs_0_.1), channel_id=1, source_target_pairs={{0,8},{1,5},{2,10},{3,7},{8,16},{9,1},{10,18},{11,3},{16,24},{17,9... | collective-permute-start | bytes 368648 | tf_op jit(solution)/shard_map/ppermute | solution.py:91
  1.2 5.4 %collective-permute-start.4 = (bf16[96,640]{1,0:T(8,128)(2,1)}, bf16[96,640]{1,0:T(8,128)(2,1)S(1)}, u32[]{:S(2)}, u32[]{:S(2)}) collective-permute-start(bf16[96,640]{1,0:T(8,128)(2,1)} %refs_0_.1), channel_id=1, source_target_pairs={{0,4},{1,9},{2,6},{3,11},{8,0},{9,17},{10,2},{11,19},{16,8},{17,25... | collective-permute-start | bytes 368648 | tf_op jit(solution)/shard_map/ppermute | solution.py:91
  2.4 5.6 %collective-permute-start.10 = (bf16[96,640]{1,0:T(8,128)(2,1)S(1)}, bf16[96,640]{1,0:T(8,128)(2,1)S(1)}, u32[]{:S(2)}, u32[]{:S(2)}) collective-permute-start(bf16[96,640]{1,0:T(8,128)(2,1)S(1)} %get-tuple-element.10.refs_0_), channel_id=1, source_target_pairs={{0,4},{1,9},{2,6},{3,11},{8,0},{9,17},{10,2},{11,19},{16,8},{17,25... | collective-permute-start | bytes 368648 | tf_op jit(solution)/shard_map/ppermute | solution.py:91
  3.8 5.3 %collective-permute-start.13 = (bf16[96,640]{1,0:T(8,128)(2,1)S(1)}, bf16[96,640]{1,0:T(8,128)(2,1)S(1)}, u32[]{:S(2)}, u32[]{:S(2)}) collective-permute-start(bf16[96,640]{1,0:T(8,128)(2,1)S(1)} %get-tuple-element.11.refs_7_), channel_id=1, source_target_pairs={{0,8},{1,5},{2,10},{3,7},{8,16},{9,1},{10,18},{11,3},{16,24},{17,9... | collective-permute-start | bytes 368648 | tf_op jit(solution)/shard_map/ppermute | solution.py:91
  4.0 6.5 %collective-permute-start.16 = (bf16[96,640]{1,0:T(8,128)(2,1)S(1)}, bf16[96,640]{1,0:T(8,128)(2,1)S(1)}, u32[]{:S(2)}, u32[]{:S(2)}) collective-permute-start(bf16[96,640]{1,0:T(8,128)(2,1)S(1)} %get-tuple-element.11.refs_7_), channel_id=1, source_target_pairs={{0,4},{1,9},{2,6},{3,11},{8,0},{9,17},{10,2},{11,19},{16,8},{17,25... | collective-permute-start | bytes 368648 | tf_op jit(solution)/shard_map/ppermute | solution.py:91
  5.3 6.5 %collective-permute-start.7 = (bf16[96,640]{1,0:T(8,128)(2,1)S(1)}, bf16[96,640]{1,0:T(8,128)(2,1)S(1)}, u32[]{:S(2)}, u32[]{:S(2)}) collective-permute-start(bf16[96,640]{1,0:T(8,128)(2,1)S(1)} %get-tuple-element.10.refs_0_), channel_id=1, source_target_pairs={{0,8},{1,5},{2,10},{3,7},{8,16},{9,1},{10,18},{11,3},{16,24},{17,9... | collective-permute-start | bytes 368648 | tf_op jit(solution)/shard_map/ppermute | solution.py:91
  6.7 6.8 %collective-permute-start.1 = (bf16[96,640]{1,0:T(8,128)(2,1)S(1)}, bf16[96,640]{1,0:T(8,128)(2,1)S(1)}, u32[]{:S(2)}, u32[]{:S(2)}) collective-permute-start(bf16[96,640]{1,0:T(8,128)(2,1)S(1)} %collective-permute-done.refs_1_), channel_id=1, source_target_pairs={{0,8},{1,5},{2,10},{3,7},{8,16},{9,1},{10,18},{11,3},{16,24},{17,9... | collective-permute-start | bytes 368648 | tf_op jit(solution)/shard_map/ppermute | solution.py:91
  8.0 5.7 %collective-permute-start.5 = (bf16[96,640]{1,0:T(8,128)(2,1)S(1)}, bf16[96,640]{1,0:T(8,128)(2,1)S(1)}, u32[]{:S(2)}, u32[]{:S(2)}) collective-permute-start(bf16[96,640]{1,0:T(8,128)(2,1)S(1)} %collective-permute-done.4.refs_7_), channel_id=1, source_target_pairs={{0,4},{1,9},{2,6},{3,11},{8,0},{9,17},{10,2},{11,19},{16,8},{17,25... | collective-permute-start | bytes 368648 | tf_op jit(solution)/shard_map/ppermute | solution.py:91
  9.1 6.8 %collective-permute-start.11 = (bf16[96,640]{1,0:T(8,128)(2,1)S(1)}, bf16[96,640]{1,0:T(8,128)(2,1)S(1)}, u32[]{:S(2)}, u32[]{:S(2)}) collective-permute-start(bf16[96,640]{1,0:T(8,128)(2,1)S(1)} %collective-permute-done.10.refs_6_), channel_id=1, source_target_pairs={{0,4},{1,9},{2,6},{3,11},{8,0},{9,17},{10,2},{11,19},{16,8},{17,25... | collective-permute-start | bytes 368648 | tf_op jit(solution)/shard_map/ppermute | solution.py:91
  10.4 5.9 %collective-permute-start.14 = (bf16[96,640]{1,0:T(8,128)(2,1)S(1)}, bf16[96,640]{1,0:T(8,128)(2,1)S(1)}, u32[]{:S(2)}, u32[]{:S(2)}) collective-permute-start(bf16[96,640]{1,0:T(8,128)(2,1)S(1)} %collective-permute-done.13.refs_8_), channel_id=1, source_target_pairs={{0,8},{1,5},{2,10},{3,7},{8,16},{9,1},{10,18},{11,3},{16,24},{17,9... | collective-permute-start | bytes 368648 | tf_op jit(solution)/shard_map/ppermute | solution.py:91
  11.7 6.4 %collective-permute-start.17 = (bf16[96,640]{1,0:T(8,128)(2,1)S(1)}, bf16[96,640]{1,0:T(8,128)(2,1)S(1)}, u32[]{:S(2)}, u32[]{:S(2)}) collective-permute-start(bf16[96,640]{1,0:T(8,128)(2,1)S(1)} %collective-permute-done.16.refs_13_), channel_id=1, source_target_pairs={{0,4},{1,9},{2,6},{3,11},{8,0},{9,17},{10,2},{11,19},{16,8},{17,25... | collective-permute-start | bytes 368648 | tf_op jit(solution)/shard_map/ppermute | solution.py:91
  13.5 5.8 %collective-permute-start.2 = (bf16[96,640]{1,0:T(8,128)(2,1)S(1)}, bf16[96,640]{1,0:T(8,128)(2,1)S(1)}, u32[]{:S(2)}, u32[]{:S(2)}) collective-permute-start(bf16[96,640]{1,0:T(8,128)(2,1)S(1)} %collective-permute-done.1.refs_2_), channel_id=1, source_target_pairs={{0,8},{1,5},{2,10},{3,7},{8,16},{9,1},{10,18},{11,3},{16,24},{17,9... | collective-permute-start | bytes 368648 | tf_op jit(solution)/shard_map/ppermute | solution.py:91
  13.7 7.7 %collective-permute-start.8 = (bf16[96,640]{1,0:T(8,128)(2,1)S(1)}, bf16[96,640]{1,0:T(8,128)(2,1)S(1)}, u32[]{:S(2)}, u32[]{:S(2)}) collective-permute-start(bf16[96,640]{1,0:T(8,128)(2,1)S(1)} %collective-permute-done.7.refs_1_), channel_id=1, source_target_pairs={{0,8},{1,5},{2,10},{3,7},{8,16},{9,1},{10,18},{11,3},{16,24},{17,9... | collective-permute-start | bytes 368648 | tf_op jit(solution)/shard_map/ppermute | solution.py:91
  15.9 6.8 %collective-permute-start.6 = (bf16[96,640]{1,0:T(8,128)(2,1)S(1)}, bf16[96,640]{1,0:T(8,128)(2,1)S(1)}, u32[]{:S(2)}, u32[]{:S(2)}) collective-permute-start(bf16[96,640]{1,0:T(8,128)(2,1)S(1)} %collective-permute-done.5.refs_6_), channel_id=1, source_target_pairs={{0,4},{1,9},{2,6},{3,11},{8,0},{9,17},{10,2},{11,19},{16,8},{17,25... | collective-permute-start | bytes 368648 | tf_op jit(solution)/shard_map/ppermute | solution.py:91
  16.3 6.9 %collective-permute-start.12 = (bf16[96,640]{1,0:T(8,128)(2,1)S(1)}, bf16[96,640]{1,0:T(8,128)(2,1)S(1)}, u32[]{:S(2)}, u32[]{:S(2)}) collective-permute-start(bf16[96,640]{1,0:T(8,128)(2,1)S(1)} %collective-permute-done.11.refs_5_), channel_id=1, source_target_pairs={{0,4},{1,9},{2,6},{3,11},{8,0},{9,17},{10,2},{11,19},{16,8},{17,25... | collective-permute-start | bytes 368648 | tf_op jit(solution)/shard_map/ppermute | solution.py:91
  18.1 6.2 %collective-permute-start.15 = (bf16[96,640]{1,0:T(8,128)(2,1)S(1)}, bf16[96,640]{1,0:T(8,128)(2,1)S(1)}, u32[]{:S(2)}, u32[]{:S(2)}) collective-permute-start(bf16[96,640]{1,0:T(8,128)(2,1)S(1)} %collective-permute-done.14.refs_9_), channel_id=1, source_target_pairs={{0,8},{1,5},{2,10},{3,7},{8,16},{9,1},{10,18},{11,3},{16,24},{17,9... | collective-permute-start | bytes 368648 | tf_op jit(solution)/shard_map/ppermute | solution.py:91
  19.3 6.5 %collective-permute-start.3 = (bf16[96,640]{1,0:T(8,128)(2,1)S(1)}, bf16[96,640]{1,0:T(8,128)(2,1)S(1)}, u32[]{:S(2)}, u32[]{:S(2)}) collective-permute-start(bf16[96,640]{1,0:T(8,128)(2,1)S(1)} %collective-permute-done.2.refs_3_), channel_id=1, source_target_pairs={{0,8},{1,5},{2,10},{3,7},{8,16},{9,1},{10,18},{11,3},{16,24},{17,9... | collective-permute-start | bytes 368648 | tf_op jit(solution)/shard_map/ppermute | solution.py:91
  21.4 5.4 %collective-permute-start.18 = (bf16[96,640]{1,0:T(8,128)(2,1)S(1)}, bf16[96,640]{1,0:T(8,128)(2,1)S(1)}, u32[]{:S(2)}, u32[]{:S(2)}) collective-permute-start(bf16[96,640]{1,0:T(8,128)(2,1)S(1)} %collective-permute-done.17.refs_12_), channel_id=1, source_target_pairs={{0,4},{1,9},{2,6},{3,11},{8,0},{9,17},{10,2},{11,19},{16,8},{17,25... | collective-permute-start | bytes 368648 | tf_op jit(solution)/shard_map/ppermute | solution.py:91
  22.7 5.3 %collective-permute-start.9 = (bf16[96,640]{1,0:T(8,128)(2,1)S(1)}, bf16[96,640]{1,0:T(8,128)(2,1)S(1)}, u32[]{:S(2)}, u32[]{:S(2)}) collective-permute-start(bf16[96,640]{1,0:T(8,128)(2,1)S(1)} %collective-permute-done.8.refs_2_), channel_id=1, source_target_pairs={{0,8},{1,5},{2,10},{3,7},{8,16},{9,1},{10,18},{11,3},{16,24},{17,9... | collective-permute-start | bytes 368648 | tf_op jit(solution)/shard_map/ppermute | solution.py:91
  23.2 9.4 %collective-permute-start.19 = (bf16[96,640]{1,0:T(8,128)(2,1)S(1)}, bf16[96,640]{1,0:T(8,128)(2,1)S(1)}, u32[]{:S(2)}, u32[]{:S(2)}) collective-permute-start(bf16[96,640]{1,0:T(8,128)(2,1)S(1)} %collective-permute-done.12.refs_4_), channel_id=1, source_target_pairs={{0,4},{1,9},{2,6},{3,11},{8,0},{9,17},{10,2},{11,19},{16,8},{17,25... | collective-permute-start | bytes 368648 | tf_op jit(solution)/shard_map/ppermute | solution.py:91
  24.3 8.3 %collective-permute-start.20 = (bf16[96,640]{1,0:T(8,128)(2,1)S(1)}, bf16[96,640]{1,0:T(8,128)(2,1)S(1)}, u32[]{:S(2)}, u32[]{:S(2)}) collective-permute-start(bf16[96,640]{1,0:T(8,128)(2,1)S(1)} %collective-permute-done.15.refs_10_), channel_id=1, source_target_pairs={{0,8},{1,5},{2,10},{3,7},{8,16},{9,1},{10,18},{11,3},{16,24},{17,9... | collective-permute-start | bytes 368648 | tf_op jit(solution)/shard_map/ppermute | solution.py:91
  39.6 7.8 %collective-permute-start.22 = (bf16[96,640]{1,0:T(8,128)(2,1)S(1)}, bf16[96,640]{1,0:T(8,128)(2,1)S(1)}, u32[]{:S(2)}, u32[]{:S(2)}) collective-permute-start(bf16[96,640]{1,0:T(8,128)(2,1)S(1)} %get-tuple-element.16.refs_0_), channel_id=1, source_target_pairs={{0,2},{1,3},{2,0},{3,1},{4,6},{5,7},{6,4},{7,5},{8,10},{9,11},{10,... | collective-permute-start | bytes 368648 | tf_op jit(solution)/shard_map/ppermute | solution.py:293
  43.9 8.0 %collective-permute-start.25 = (bf16[96,640]{1,0:T(8,128)(2,1)S(1)}, bf16[96,640]{1,0:T(8,128)(2,1)S(1)}, u32[]{:S(2)}, u32[]{:S(2)}) collective-permute-start(bf16[96,640]{1,0:T(8,128)(2,1)S(1)} %shard_map.44), channel_id=1, source_target_pairs={{0,8},{1,28},{2,16},{3,4},{4,24},{5,12},{6,0},{7,20},{8,25},{9,5},... | collective-permute-start | bytes 368648 | tf_op jit(solution)/shard_map/ppermute | solution.py:305
  47.5 7.6 %collective-permute-start.23 = (bf16[96,640]{1,0:T(8,128)(2,1)S(1)}, bf16[96,640]{1,0:T(8,128)(2,1)S(1)}, u32[]{:S(2)}, u32[]{:S(2)}) collective-permute-start(bf16[96,640]{1,0:T(8,128)(2,1)S(1)} %shard_map.43), channel_id=1, source_target_pairs={{0,24},{1,12},{2,0},{3,20},{4,8},{5,28},{6,16},{7,4},{8,1},{9,29},... | collective-permute-start | bytes 368648 | tf_op jit(solution)/shard_map/ppermute | solution.py:305
  (5 other events, 16.9 us)
